TPU v7x, 32 devices: a whole 2x2x4 slice. The times are simulated.
32 devices in a mesh: lat: 4 (over y, x), lon: 8 (over z, core).
Axes of the slice: x: 2, y: 2, z: 4, core: 2. Of those that a mesh axis runs over, the one named last changes fastest.
Arguments:
- inputs: bfloat16 [64, 1024, 64], P('lat', 'lon'), may hold values from -6 to 6
- pre_first: bfloat16 [64, 1024, 128], P('lat', 'lon'), may hold values from -6 to 6
- grad_out: bfloat16 [32, 512, 128], P('lat', 'lon'), may hold values from -6 to 6
- w_first: bfloat16 [3, 3, 64, 128], replicated, may hold values from -0.25 to 0.25
- w_second: bfloat16 [3, 3, 128, 128], replicated, may hold values from -0.1875 to 0.1875
Outputs:
- grad_inputs: bfloat16 [64, 1024, 64], P('lat', 'lon')
- grad_w_first: float32 [3, 3, 64, 128], replicated
- grad_w_second: float32 [3, 3, 128, 128], replicated
All inputs are finite; a program needn't handle non-finite values.
Results may differ from a plain program's by a relative error of at most 0.0049.
Values may be sent and summed in bfloat16 or wider, within the bound.
No kernel may reach another device: no remote copies, remote signals or barrier semaphores. Data moves between devices by JAX's collectives and lax.ppermute only.
A program may use at most 64 MiB of HBM per device.

v0:
```python
import jax
import jax.numpy as jnp
from jax import lax
from jax.sharding import PartitionSpec as P

inv_root = 0.7071067811865476
density = 0.3989422804014327


def passed_along(shard, axis, by):
    peers = lax.axis_size(axis)
    return lax.ppermute(shard, axis, [(i, (i + by) % peers) for i in range(peers)])


def extended(block, sides, width):
    for axis, dim in sides:
        count = lax.axis_size(axis)
        forward = [(i, i + 1) for i in range(count - 1)]
        forward.append((count - 1, 0))
        backward = [(target, source) for source, target in forward]
        low = lax.ppermute(
            lax.slice_in_dim(block, block.shape[dim] - width, None, axis=dim), axis, forward
        )
        high = lax.ppermute(lax.slice_in_dim(block, 0, width, axis=dim), axis, backward)
        block = jnp.concatenate([low, block, high], axis=dim)
    return block


def across_values(row):
    return passed_along(row, "lon", lax.axis_size("lon") // 2)


def across_grads(row):
    return passed_along(row, "lon", lax.axis_size("lon") // 2)


def pad_values(fields):
    band = lax.axis_index("lat")
    padded = extended(fields, (("lat", 0), ("lon", 1)), 1)
    opposite = across_values(padded[1])
    top = jnp.where(band == 0, opposite, padded[0])
    bottom = jnp.where(band == lax.axis_size("lat") - 1, jnp.zeros_like(padded[-1]), padded[-1])
    return jnp.concatenate([top[None], padded[1:-1], bottom[None]], 0)


def fold_grads(grid):
    band = lax.axis_index("lat")
    first = band == 0
    final = band == lax.axis_size("lat") - 1
    opposite = across_grads(grid[0])
    row_one = grid[1] + jnp.where(first, opposite, jnp.zeros_like(opposite))
    top = jnp.where(first, jnp.zeros_like(grid[0]), grid[0])
    bottom = jnp.where(final, jnp.zeros_like(grid[-1]), grid[-1])
    grid = jnp.concatenate([top[None], row_one[None], grid[2:-1], bottom[None]], 0)
    wide = extended(grid, (("lat", 0), ("lon", 1)), 1)
    inner = wide[2:-2]
    inner = inner.at[0].add(wide[0]).at[-1].add(wide[-1])
    core = inner[:, 2:-2]
    core = core.at[:, 0].add(inner[:, 0]).at[:, -1].add(inner[:, -1])
    return core


def taps_product(padded, grads):
    rows, cols = (grads.shape[0], grads.shape[1])
    flat = grads.reshape(rows * cols, grads.shape[2])
    result = []
    for a in range(3):
        line = []
        for b in range(3):
            piece = padded[a : a + rows, b : b + cols].reshape(rows * cols, padded.shape[2])
            line.append(
                lax.dot_general(
                    piece, flat, (((0,), (0,)), ((), ())), preferred_element_type=jnp.float32
                )
            )
        result.append(jnp.stack(line, 0))
    return jnp.stack(result, 0)


def spread(grads, weight):
    rows, cols, cout = grads.shape
    cin = weight.shape[2]
    every = jnp.transpose(weight, (3, 0, 1, 2)).reshape(cout, 9 * cin)
    terms = jnp.dot(grads.reshape(rows * cols, cout), every, preferred_element_type=jnp.float32)
    terms = terms.reshape(rows, cols, 3, 3, cin)
    grid = jnp.zeros((rows + 2, cols + 2, cin), jnp.float32)
    for a in range(3):
        for b in range(3):
            grid = grid.at[a : a + rows, b : b + cols].add(terms[:, :, a, b])
    return grid


def body(inputs, pre_first, grad_out, w_first, w_second):
    first_ch = inputs.shape[2]
    value = pre_first.astype(jnp.float32)
    cdf = 0.5 * (1.0 + lax.erf(value * inv_root))
    activated = (value * cdf).astype(jnp.bfloat16)
    slope = cdf + value * jnp.exp(-0.5 * value * value) * density
    padded = pad_values(jnp.concatenate([inputs, activated], 2))
    padded_in = padded[:, :, :first_ch]
    padded_act = padded[:, :, first_ch:]
    grad_pool = jnp.repeat(jnp.repeat(grad_out, 2, 0), 2, 1) * jnp.asarray(0.25, grad_out.dtype)
    local_second = taps_product(padded_act, grad_pool)
    grad_act = fold_grads(spread(grad_pool, w_second))
    grad_pre = (grad_act * slope).astype(jnp.bfloat16)
    local_first = taps_product(padded_in, grad_pre)
    grad_inputs = fold_grads(spread(grad_pre, w_first)).astype(jnp.bfloat16)
    grad_w_first, grad_w_second = lax.psum((local_first, local_second), ("lat", "lon"))
    return (grad_inputs, grad_w_first, grad_w_second)


def solution(mesh):
    in_specs = (P("lat", "lon", None), P("lat", "lon", None), P("lat", "lon", None), P(), P())
    out_specs = (P("lat", "lon", None), P(), P())
    return jax.shard_map(body, mesh=mesh, in_specs=in_specs, out_specs=out_specs, check_vma=False)
```

profile of v0, /device:TPU:0, one launch (start us, length us, event | category | flops | bytes accessed | tf_op | source)
XLA Modules:
  0.0 308.1 jit_solution(8142833253011935917)
XLA Ops:
  7.2 1.0 broadcast_multiply_fusion
  8.7 1.4 fusion.71
  10.9 1.1 fusion.104
  12.1 1.6 fusion.17
  14.5 3.4 %scatter-add.89 = f32[18,130,128]{2,1,0:T(8,128)S(1)} dynamic-update-slice(f32[18,130,128]{2,1,0:T(8,128)S(1)} %scatter-add.86, f32[16,128,128]{2,1,0:T(8,128)S(1)} %fusion.17, s32[]{:T(128)} %bitcast.10, s32[]{:T(128)} %bitcast.11, s32[]{:T(128)} %constant.654.clone.1) | dynamic-update-slice | bytes 2097156 | tf_op jit(solution)/shard_map/scatter-add | solution.py:89
  17.9 3.4 %add_select_fusion = f32[16,128,128]{2,1,0:T(8,128)S(1)} fusion(f32[16,128,3,3,128]{4,1,3,2,0:T(8,128)} %copy-done.1, f32[18,130,128]{2,1,0:T(8,128)S(1)} %scatter-add.89, s32[]{:T(128)} %bitcast.13, s32[]{:T(128)} %bitcast.14, pred[]{:T(512)} %and_reduce_fusion), kind=kLoop, calls=%fused_computation.15 | loop fusion | flops 524288 | bytes 3145737 | tf_op jit(solution)/shard_map/select.28
  21.3 3.5 %scatter-add.90 = f32[18,130,128]{2,1,0:T(8,128)S(1)} dynamic-update-slice(f32[18,130,128]{2,1,0:T(8,128)S(1)} %scatter-add.89, f32[16,128,128]{2,1,0:T(8,128)S(1)} %add_select_fusion, s32[]{:T(128)} %bitcast.13, s32[]{:T(128)} %bitcast.14, s32[]{:T(128)} %constant.654.clone.1) | dynamic-update-slice | bytes 2097156 | tf_op jit(solution)/shard_map/scatter-add | solution.py:89
  24.8 1.4 fusion.16
  26.2 1.3 fusion.14
  27.6 2.1 scatter-add.94
  29.7 1.3 fusion.13
  31.0 2.1 scatter-add.95
  33.2 1.4 fusion.12
  34.6 1.4 fusion.10
  36.0 2.1 scatter-add.99
  38.1 1.4 fusion.9
  39.4 2.1 scatter-add.100
  41.6 3.0 collective-permute-start
  44.6 3.2 %collective-permute-done = f32[1,130,128]{2,1,0:T(8,128)S(1)} collective-permute-done((f32[1,130,128]{2,1,0:T(8,128)S(1)}, f32[1,130,128]{2,1,0:T(8,128)S(1)}, u32[]{:S(2)}, u32[]{:S(2)}) %collective-permute-start) | collective-permute-done | bytes 66592 | tf_op jit(solution)/shard_map/ppermute | solution.py:21
  47.8 3.1 %collective-permute-start.1 = (f32[130,128]{1,0:T(8,128)S(1)}, f32[130,128]{1,0:T(8,128)S(1)}, u32[]{:S(2)}, u32[]{:S(2)}) collective-permute-start(f32[130,128]{1,0:T(8,128)S(1)} %get-tuple-element.325), channel_id=1, source_target_pairs={{0,4},{1,5},{2,6},{3,7},{4,0},{5,1},{6,2},{7,3},{8,12},{9,13},{10,... | collective-permute-start | bytes 199688 | tf_op jit(solution)/shard_map/ppermute | solution.py:12
  51.0 1.6 collective-permute-start.2
  53.4 1.9 collective-permute-done.2
  55.4 3.5 %collective-permute-start.4 = (f32[20,1,128]{2,1,0:T(1,128)S(1)}, f32[20,1,128]{2,1,0:T(1,128)S(1)}, u32[]{:S(2)}, u32[]{:S(2)}) collective-permute-start(f32[20,1,128]{2,1,0:T(1,128)S(1)} %get-tuple-element.322), channel_id=1, source_target_pairs={{1,0},{2,1},{3,2},{4,3},{5,4},{6,5},{7,6},{0,7},{9,8},{10,9},{11,1... | collective-permute-start | bytes 30728 | tf_op jit(solution)/shard_map/ppermute | solution.py:24
  59.2 1.1 collective-permute-done.3
  62.6 1.6 fusion.8
  65.1 3.0 fusion.69
  68.0 1.1 slice_bitcast_fusion.17
  69.1 3.3 %fusion.68 = f32[16,128,64]{1,2,0:T(8,128)} fusion(f32[16,128,3,3,64]{1,4,3,2,0:T(8,128)} %fusion.69, s32[]{:T(128)} %bitcast.10, s32[]{:T(128)} %bitcast.11, f32[16,128,64]{1,2,0:T(8,128)S(1)} %slice_bitcast_fusion.17), kind=kLoop, calls=%fused_computation.138 | loop fusion | flops 131072 | bytes 1572872 | tf_op jit(solution)/shard_map/add | solution.py:89
  72.7 1.5 collective-permute-start.10
  74.3 1.4 collective-permute-start.11
  75.7 6.0 %scatter-add.110 = f32[18,130,64]{1,2,0:T(8,128)S(1)} dynamic-update-slice(f32[18,130,64]{1,2,0:T(8,128)S(1)} %scatter-add.109, f32[16,128,64]{1,2,0:T(8,128)} %fusion.68, s32[]{:T(128)} %bitcast.10, s32[]{:T(128)} %bitcast.11, s32[]{:T(128)} %constant.654.clone.1) | dynamic-update-slice | bytes 1048580 | tf_op jit(solution)/shard_map/scatter-add | solution.py:89
  81.7 4.0 %add_select_fusion.1 = f32[16,128,64]{1,2,0:T(8,128)} fusion(f32[16,128,3,3,64]{1,4,3,2,0:T(8,128)} %fusion.69, f32[18,130,64]{1,2,0:T(8,128)S(1)} %scatter-add.110, s32[]{:T(128)} %bitcast.13, s32[]{:T(128)} %bitcast.14, pred[]{:T(512)} %and_reduce_fusion), kind=kLoop, calls=%fused_computation.66 | loop fusion | flops 262144 | bytes 1572873 | tf_op jit(solution)/shard_map/select.41
  85.7 6.0 %scatter-add.111 = f32[18,130,64]{1,2,0:T(8,128)S(1)} dynamic-update-slice(f32[18,130,64]{1,2,0:T(8,128)S(1)} %scatter-add.110, f32[16,128,64]{1,2,0:T(8,128)} %add_select_fusion.1, s32[]{:T(128)} %bitcast.13, s32[]{:T(128)} %bitcast.14, s32[]{:T(128)} %constant.654.clone.1) | dynamic-update-slice | bytes 1048580 | tf_op jit(solution)/shard_map/scatter-add | solution.py:89
  91.8 1.2 fusion.67
  92.9 2.0 fusion.65
  95.0 4.7 %scatter-add.115 = f32[18,130,64]{1,2,0:T(8,128)S(1)} dynamic-update-slice(f32[18,130,64]{1,2,0:T(8,128)S(1)} %fusion.67, f32[16,128,64]{1,2,0:T(8,128)} %fusion.65, s32[]{:T(128)} %constant.659.clone.1, s32[]{:T(128)} %constant.659.clone.1, s32[]{:T(128)} %constant.654.clone.1) | dynamic-update-slice | bytes 1048580 | tf_op jit(solution)/shard_map/scatter-add | solution.py:89
  99.7 2.0 fusion.64
  101.7 4.7 %scatter-add.116 = f32[18,130,64]{1,2,0:T(8,128)S(1)} dynamic-update-slice(f32[18,130,64]{1,2,0:T(8,128)S(1)} %scatter-add.115, f32[16,128,64]{1,2,0:T(8,128)} %fusion.64, s32[]{:T(128)} %constant.659.clone.1, s32[]{:T(128)} %constant.655.clone.1, s32[]{:T(128)} %constant.654.clone.1) | dynamic-update-slice | bytes 1048580 | tf_op jit(solution)/shard_map/scatter-add | solution.py:89
  106.4 1.2 fusion.63
  107.5 2.0 fusion.61
  109.6 4.7 %scatter-add.120 = f32[18,130,64]{1,2,0:T(8,128)S(1)} dynamic-update-slice(f32[18,130,64]{1,2,0:T(8,128)S(1)} %fusion.63, f32[16,128,64]{1,2,0:T(8,128)} %fusion.61, s32[]{:T(128)} %constant.655.clone.1, s32[]{:T(128)} %constant.659.clone.1, s32[]{:T(128)} %constant.654.clone.1) | dynamic-update-slice | bytes 1048580 | tf_op jit(solution)/shard_map/scatter-add | solution.py:89
  114.3 2.0 fusion.60
  116.3 4.7 %scatter-add.121 = f32[18,130,64]{1,2,0:T(8,128)S(1)} dynamic-update-slice(f32[18,130,64]{1,2,0:T(8,128)S(1)} %scatter-add.120, f32[16,128,64]{1,2,0:T(8,128)} %fusion.60, s32[]{:T(128)} %constant.655.clone.1, s32[]{:T(128)} %constant.655.clone.1, s32[]{:T(128)} %constant.654.clone.1) | dynamic-update-slice | bytes 1048580 | tf_op jit(solution)/shard_map/scatter-add | solution.py:89
  121.6 1.4 convolution_bitcast_fusion.4
  123.0 3.2 %collective-permute-done.5 = f32[1,130,64]{1,2,0:T(8,128)S(1)} collective-permute-done((f32[1,130,64]{1,2,0:T(8,128)S(1)}, f32[1,130,64]{1,2,0:T(8,128)S(1)}, u32[]{:S(2)}, u32[]{:S(2)}) %collective-permute-start.5) | collective-permute-done | bytes 33312 | tf_op jit(solution)/shard_map/ppermute | solution.py:21
  126.4 3.5 %collective-permute-start.13 = (bf16[18,1,192]{2,1,0:T(2,128)(2,1)S(1)}, bf16[18,1,192]{2,1,0:T(2,128)(2,1)S(1)}, u32[]{:S(2)}, u32[]{:S(2)}) collective-permute-start(bf16[18,1,192]{2,1,0:T(2,128)(2,1)S(1)} %get-tuple-element.329), channel_id=1, source_target_pairs={{1,0},{2,1},{3,2},{4,3},{5,4},{6,5},{7,6},{0,7},{9,8},{10,9},{11,1... | collective-permute-start | bytes 20744 | tf_op jit(solution)/shard_map/ppermute | solution.py:24
  132.4 0.9 copy-done.3
  134.2 1.2 convolution_bitcast_fusion.2
  135.4 1.3 convolution_bitcast_fusion.1
  139.3 0.9 convolution_bitcast_fusion.10
  140.2 2.2 collective-permute-start.14
  143.7 0.9 convolution_bitcast_fusion.14
  144.6 1.0 convolution_bitcast_fusion.13
  146.4 1.3 fusion.103
  148.0 2.0 copy.59
  150.0 3.4 %collective-permute-start.9 = (f32[20,1,64]{2,1,0:T(1,128)}, f32[20,1,64]{2,1,0:T(1,128)}, u32[]{:S(2)}, u32[]{:S(2)}) collective-permute-start(f32[20,1,64]{2,1,0:T(1,128)} %copy.59), channel_id=1, source_target_pairs={{1,0},{2,1},{3,2},{4,3},{5,4},{6,5},{7,6},{0,7},{9,8},{10,9},{11,1... | collective-permute-start | bytes 15368 | tf_op jit(solution)/shard_map/ppermute | solution.py:24
  154.3 1.8 copy.60
  156.1 1.8 copy.61
  158.0 1.9 pad_maximum_fusion.1
  159.9 1.0 copy-done.13
  170.2 1.9 scatter-add.129
  172.8 124.8 %all-reduce.5.cloned.1.call-done = (f32[3,3,64,128]{3,2,1,0:T(8,128)}, f32[3,3,128,128]{3,2,1,0:T(8,128)}) async-done(((f32[3,3,64,128]{3,2,1,0:T(8,128)}, f32[3,3,128,128]{3,2,1,0:T(8,128)}), (f32[3,3,64,128]{3,2,1,0:T(8,128)}, f32[3,3,128,128]{3,2,1,0:T(8,128)})) %all-reduce.5.cloned.1.call-update) | async-done | bytes 884752 | tf_op jit(solution)/shard_map/psum | solution.py:108
  297.6 1.7 copy.151
  299.3 1.9 copy.152
  (146 shorter events, 26.4 us)
Async XLA Ops:
  7.2 1.5 copy-start
  7.2 290.4 %all-reduce.5.cloned.1.call-start = ((), (), s32[]{:S(2)}) async-start(), calls=%async_computation | async-start | bytes 1769472 | tf_op jit(solution)/shard_map/psum | solution.py:108
  8.7 1.4 copy-start.10
  10.1 3.7 %copy-start.1 = (f32[16,128,3,3,128]{4,1,3,2,0:T(8,128)}, f32[16,128,3,3,128]{4,1,3,2,0:T(8,128)S(1)}, u32[]{:S(2)}) copy-start(f32[16,128,3,3,128]{4,1,3,2,0:T(8,128)S(1)} %fusion.71) | copy-start | bytes 28311556
  12.1 1.7 copy-start.30
  41.6 6.2 %collective-permute-start = (f32[1,130,128]{2,1,0:T(8,128)S(1)}, f32[1,130,128]{2,1,0:T(8,128)S(1)}, u32[]{:S(2)}, u32[]{:S(2)}) collective-permute-start(f32[1,130,128]{2,1,0:T(8,128)S(1)} %slice_select_fusion), channel_id=1, source_target_pairs={{0,8},{8,16},{16,24},{24,0},{1,9},{9,17},{17,25},{25,1},{2,10},{10... | collective-permute-start | bytes 199688 | tf_op jit(solution)/shard_map/ppermute | solution.py:21
  47.8 5.4 %collective-permute-start.1 = (f32[130,128]{1,0:T(8,128)S(1)}, f32[130,128]{1,0:T(8,128)S(1)}, u32[]{:S(2)}, u32[]{:S(2)}) collective-permute-start(f32[130,128]{1,0:T(8,128)S(1)} %get-tuple-element.325), channel_id=1, source_target_pairs={{0,4},{1,5},{2,6},{3,7},{4,0},{5,1},{6,2},{7,3},{8,12},{9,13},{10,... | collective-permute-start | bytes 199688 | tf_op jit(solution)/shard_map/ppermute | solution.py:12
  51.0 4.3 %collective-permute-start.2 = (f32[1,130,128]{2,1,0:T(8,128)S(1)}, f32[1,130,128]{2,1,0:T(8,128)S(1)}, u32[]{:S(2)}, u32[]{:S(2)}) collective-permute-start(f32[1,130,128]{2,1,0:T(8,128)S(1)} %get-tuple-element.320), channel_id=1, source_target_pairs={{8,0},{16,8},{24,16},{0,24},{9,1},{17,9},{25,17},{1,25},{10,2},{18... | collective-permute-start | bytes 199688 | tf_op jit(solution)/shard_map/ppermute | solution.py:24
  53.3 5.6 %copy-start.18 = (bf16[16,128,64]{1,2,0:T(8,128)(2,1)S(1)}, bf16[16,128,64]{1,2,0:T(8,128)(2,1)}, u32[]{:S(2)}) copy-start(bf16[16,128,64]{1,2,0:T(8,128)(2,1)} %param.57) | copy-start | bytes 786436
  55.3 4.9 %collective-permute-start.3 = (f32[20,1,128]{2,1,0:T(1,128)S(1)}, f32[20,1,128]{2,1,0:T(1,128)S(1)}, u32[]{:S(2)}, u32[]{:S(2)}) collective-permute-start(f32[20,1,128]{2,1,0:T(1,128)S(1)} %get-tuple-element.321), channel_id=1, source_target_pairs={{0,1},{1,2},{2,3},{3,4},{4,5},{5,6},{6,7},{7,0},{8,9},{9,10},{10,1... | collective-permute-start | bytes 30728 | tf_op jit(solution)/shard_map/ppermute | solution.py:21
  55.4 4.9 %collective-permute-start.4 = (f32[20,1,128]{2,1,0:T(1,128)S(1)}, f32[20,1,128]{2,1,0:T(1,128)S(1)}, u32[]{:S(2)}, u32[]{:S(2)}) collective-permute-start(f32[20,1,128]{2,1,0:T(1,128)S(1)} %get-tuple-element.322), channel_id=1, source_target_pairs={{1,0},{2,1},{3,2},{4,3},{5,4},{6,5},{7,6},{0,7},{9,8},{10,9},{11,1... | collective-permute-start | bytes 30728 | tf_op jit(solution)/shard_map/ppermute | solution.py:24
  59.2 72.3 %copy-start.7 = (bf16[16,128,64]{2,1,0:T(8,128)(2,1)}, bf16[16,128,64]{2,1,0:T(8,128)(2,1)S(1)}, u32[]{:S(2)}) copy-start(bf16[16,128,64]{2,1,0:T(8,128)(2,1)S(1)} %copy.62) | copy-start | bytes 786436
  60.5 1.0 copy-start.17
  62.6 2.5 copy-start.24
  64.2 67.2 %copy-start.2 = (bf16[16,128,128]{2,1,0:T(8,128)(2,1)}, bf16[16,128,128]{2,1,0:T(8,128)(2,1)S(1)}, u32[]{:S(2)}) copy-start(bf16[16,128,128]{2,1,0:T(8,128)(2,1)S(1)} %get-tuple-element.333) | copy-start | bytes 1572868
  72.7 53.5 %collective-permute-start.10 = (bf16[1,128,192]{2,1,0:T(8,128)(2,1)S(1)}, bf16[1,128,192]{2,1,0:T(8,128)(2,1)S(1)}, u32[]{:S(2)}, u32[]{:S(2)}) collective-permute-start(bf16[1,128,192]{2,1,0:T(8,128)(2,1)S(1)} %get-tuple-element.331), channel_id=1, source_target_pairs={{0,8},{8,16},{16,24},{24,0},{1,9},{9,17},{17,25},{25,1},{2,10},{10... | collective-permute-start | bytes 147464 | tf_op jit(solution)/shard_map/ppermute | solution.py:21
  74.3 52.0 %collective-permute-start.11 = (bf16[1,128,192]{2,1,0:T(8,128)(2,1)S(1)}, bf16[1,128,192]{2,1,0:T(8,128)(2,1)S(1)}, u32[]{:S(2)}, u32[]{:S(2)}) collective-permute-start(bf16[1,128,192]{2,1,0:T(8,128)(2,1)S(1)} %get-tuple-element.332), channel_id=1, source_target_pairs={{8,0},{16,8},{24,16},{0,24},{9,1},{17,9},{25,17},{1,25},{10,2},{18... | collective-permute-start | bytes 147464 | tf_op jit(solution)/shard_map/ppermute | solution.py:24
  121.0 5.2 %collective-permute-start.5 = (f32[1,130,64]{1,2,0:T(8,128)S(1)}, f32[1,130,64]{1,2,0:T(8,128)S(1)}, u32[]{:S(2)}, u32[]{:S(2)}) collective-permute-start(f32[1,130,64]{1,2,0:T(8,128)S(1)} %slice_select_fusion.1), channel_id=1, source_target_pairs={{0,8},{8,16},{16,24},{24,0},{1,9},{9,17},{17,25},{25,1},{2,10},{10... | collective-permute-start | bytes 99848 | tf_op jit(solution)/shard_map/ppermute | solution.py:21
  126.3 5.1 %collective-permute-start.12 = (bf16[18,1,192]{2,1,0:T(2,128)(2,1)S(1)}, bf16[18,1,192]{2,1,0:T(2,128)(2,1)S(1)}, u32[]{:S(2)}, u32[]{:S(2)}) collective-permute-start(bf16[18,1,192]{2,1,0:T(2,128)(2,1)S(1)} %get-tuple-element.328), channel_id=1, source_target_pairs={{0,1},{1,2},{2,3},{3,4},{4,5},{5,6},{6,7},{7,0},{8,9},{9,10},{10,1... | collective-permute-start | bytes 20744 | tf_op jit(solution)/shard_map/ppermute | solution.py:21
  126.4 5.0 %collective-permute-start.13 = (bf16[18,1,192]{2,1,0:T(2,128)(2,1)S(1)}, bf16[18,1,192]{2,1,0:T(2,128)(2,1)S(1)}, u32[]{:S(2)}, u32[]{:S(2)}) collective-permute-start(bf16[18,1,192]{2,1,0:T(2,128)(2,1)S(1)} %get-tuple-element.329), channel_id=1, source_target_pairs={{1,0},{2,1},{3,2},{4,3},{5,4},{6,5},{7,6},{0,7},{9,8},{10,9},{11,1... | collective-permute-start | bytes 20744 | tf_op jit(solution)/shard_map/ppermute | solution.py:24
  130.0 16.3 %collective-permute-start.6 = (f32[130,64]{0,1:T(8,128)S(1)}, f32[130,64]{0,1:T(8,128)S(1)}, u32[]{:S(2)}, u32[]{:S(2)}) collective-permute-start(f32[130,64]{0,1:T(8,128)S(1)} %get-tuple-element.330), channel_id=1, source_target_pairs={{0,4},{1,5},{2,6},{3,7},{4,0},{5,1},{6,2},{7,3},{8,12},{9,13},{10,... | collective-permute-start | bytes 99848 | tf_op jit(solution)/shard_map/ppermute | solution.py:12
  130.0 16.4 %collective-permute-start.7 = (f32[1,130,64]{1,2,0:T(8,128)S(1)}, f32[1,130,64]{1,2,0:T(8,128)S(1)}, u32[]{:S(2)}, u32[]{:S(2)}) collective-permute-start(f32[1,130,64]{1,2,0:T(8,128)S(1)} %get-tuple-element.318), channel_id=1, source_target_pairs={{8,0},{16,8},{24,16},{0,24},{9,1},{17,9},{25,17},{1,25},{10,2},{18... | collective-permute-start | bytes 99848 | tf_op jit(solution)/shard_map/ppermute | solution.py:24
  131.4 12.2 %copy-start.20 = (bf16[18,1,192]{2,1,0:T(2,128)(2,1)}, bf16[18,1,192]{2,1,0:T(2,128)(2,1)S(1)}, u32[]{:S(2)}) copy-start(bf16[18,1,192]{2,1,0:T(2,128)(2,1)S(1)} %collective-permute-done.12) | copy-start | bytes 20740
  131.5 13.2 %copy-start.22 = (bf16[18,1,192]{2,1,0:T(2,128)(2,1)}, bf16[18,1,192]{2,1,0:T(2,128)(2,1)S(1)}, u32[]{:S(2)}) copy-start(bf16[18,1,192]{2,1,0:T(2,128)(2,1)S(1)} %collective-permute-done.13) | copy-start | bytes 20740
  132.3 1.0 copy-start.3
  132.3 1.2 copy-start.8
  132.3 1.9 copy-start.11
  140.2 21.4 %collective-permute-start.14 = (bf16[130,192]{1,0:T(8,128)(2,1)}, bf16[130,192]{1,0:T(8,128)(2,1)}, u32[]{:S(2)}, u32[]{:S(2)}) collective-permute-start(bf16[130,192]{1,0:T(8,128)(2,1)} %get-tuple-element.326), channel_id=1, source_target_pairs={{0,4},{1,5},{2,6},{3,7},{4,0},{5,1},{6,2},{7,3},{8,12},{9,13},{10,... | collective-permute-start | bytes 149768 | tf_op jit(solution)/shard_map/ppermute | solution.py:12
  146.4 1.3 copy-start.5
  147.9 10.0 %copy-start.6 = (f32[20,130,64]{1,2,0:T(8,128)S(1)}, f32[20,130,64]{1,2,0:T(8,128)}, u32[]{:S(2)}) copy-start(f32[20,130,64]{1,2,0:T(8,128)} %copy-done.5) | copy-start | bytes 1996804
  147.9 6.3 %collective-permute-start.8 = (f32[20,1,64]{2,1,0:T(1,128)S(1)}, f32[20,1,64]{2,1,0:T(1,128)}, u32[]{:S(2)}, u32[]{:S(2)}) collective-permute-start(f32[20,1,64]{2,1,0:T(1,128)S(1)} %copy.58), channel_id=1, source_target_pairs={{0,1},{1,2},{2,3},{3,4},{4,5},{5,6},{6,7},{7,0},{8,9},{9,10},{10,1... | collective-permute-start | bytes 15368 | tf_op jit(solution)/shard_map/ppermute | solution.py:21
  150.0 6.1 %collective-permute-start.9 = (f32[20,1,64]{2,1,0:T(1,128)}, f32[20,1,64]{2,1,0:T(1,128)}, u32[]{:S(2)}, u32[]{:S(2)}) collective-permute-start(f32[20,1,64]{2,1,0:T(1,128)} %copy.59), channel_id=1, source_target_pairs={{1,0},{2,1},{3,2},{4,3},{5,4},{6,5},{7,6},{0,7},{9,8},{10,9},{11,1... | collective-permute-start | bytes 15368 | tf_op jit(solution)/shard_map/ppermute | solution.py:24
  159.8 1.1 copy-start.13
  159.8 1.3 copy-start.14
  161.2 1.0 copy-start.4
  161.2 1.6 copy-start.9
  161.2 1.6 copy-start.21
  161.3 1.6 copy-start.23
  161.4 3.0 copy-start.15
  161.4 2.4 copy-start.12
  166.3 0.8 copy-start.28
  166.3 0.9 copy-start.29
  166.4 1.0 copy-start.19
  167.2 1.0 copy-start.25
  167.2 1.0 copy-start.26
  167.2 1.0 copy-start.27
  167.3 1.7 copy-start.16
Sparse Core Ops, SparseCore 0:
  169.1 128.4 all-reduce.4
where the time goes:
time: 310 us; the launch traced here: 308 us
  waiting for transfers between devices  136 us (44%)
  local copies, waits for them, and re-layouts  69.2 us (22%)
  other arithmetic  44.8 us (14%)
  starting transfers between devices  24.9 us (8%)
  matrix products  18.6 us (6%)
  between operations  14.9 us (5%)
    psum x1, waiting for transfers between devices, body(): lax.psum((local_first, local_second), ('lat', 'lon'))  125 us
    scatter-add x14, local copies, waits for them, and re-layouts, spread(): grid = grid.at[a:a + rows, b:b + cols].add(terms[:, :, a, b])  46.2 us
    add x10, other arithmetic, spread(): grid = grid.at[a:a + rows, b:b + cols].add(terms[:, :, a, b])  18.6 us
    dot_general x18, matrix products, taps_product(): lax.dot_general(piece, flat, (((0,), (0,)), ((), ())), preferred_element_...  14.2 us
    ppermute x6, starting transfers between devices, extended(): lax.ppermute(lax.slice_in_dim(block, 0, width, axis=dim), axis, backward)  14.2 us
    unnamed x69, local copies, waits for them, and re-layouts  9.2 us
    ppermute x6, waiting for transfers between devices, extended(): lax.ppermute(lax.slice_in_dim(block, block.shape[dim] - width, None, axis...  8.2 us
    another operation x4, other arithmetic  8.09 us
  transfers between devices with their start and end apart: 16, of which 7 were waited for; matrix products, arithmetic and copies ran while one was open for 24% of the time, Pallas kernels for 0%

commit v1 on v0

v1 whole, which is shorter than its diff:
```python
import functools

import jax
import jax.numpy as jnp
from jax import lax
from jax.experimental import pallas as pl
from jax.experimental.pallas import tpu as pltpu
from jax.sharding import PartitionSpec as P

inv_root = 0.7071067811865476
density = 0.3989422804014327

F32 = jnp.float32
BF16 = jnp.bfloat16
EDGE = 16
AREA = ("lat", "lon")


def cdf_of(value):
    return 0.5 * (1.0 + lax.erf(value * inv_root))


def slope_of(value, cdf):
    return 0.25 * (cdf + value * jnp.exp(-0.5 * value * value) * density)


def dot(left, right):
    return jnp.dot(left, right, preferred_element_type=F32)


def dot_nt(left, right):
    return lax.dot_general(left, right, (((1,), (1,)), ((), ())), preferred_element_type=F32)


def local_kernel(pre, fields, w_first, w_second, slope, act_t, fields_t, taps_first, taps_second,
                 line, thin, act_s, fields_s):
    rows, cols, c1 = pre.shape
    c0 = fields.shape[2]
    half = cols // 2

    def one_row(r, carry):
        line[...] = pre[r].astype(F32)
        thin[...] = fields[r].astype(F32)
        for pc in range(2):
            value = line[pl.ds(pc, half, stride=2), :]
            cdf = cdf_of(value)
            act_s[r % 2, r // 2, :, pc * c1:(pc + 1) * c1] = (value * cdf).astype(BF16)
            slope[r, :, pc * c1:(pc + 1) * c1] = slope_of(value, cdf)
            fields_s[pc, r] = thin[pl.ds(pc, half, stride=2), :].astype(BF16)
        return carry

    lax.fori_loop(0, rows, one_row, 0)
    for pr in range(2):
        act_t[pr] = act_s[pr].reshape(rows // 2 * half, 2 * c1).T
        fields_t[pr * c0:(pr + 1) * c0, :] = fields_s[pr].reshape(rows * half, c0).T
    taps_second[...] = jnp.zeros_like(taps_second)
    taps_first[...] = jnp.zeros_like(taps_first)
    for a in range(3):
        for pc, blocks in ((0, (2, 1, None, 0)), (1, (None, 2, 0, 1))):
            for k, b in enumerate(blocks):
                if b is not None:
                    taps_second[a, pc * c1:(pc + 1) * c1, k * c1:(k + 1) * c1] = w_second[a, b]
        for pc, blocks in ((0, (2, 1, 0, None)), (1, (None, 2, 1, 0))):
            for k, b in enumerate(blocks):
                if b is not None:
                    low = (2 * a + pc) * c0
                    taps_first[low:low + c0, k * c1:(k + 1) * c1] = w_first[a, b]


def middle_kernel(flags, grad_out, top, bottom, left, right, slope, act_t, fields_t, taps,
                  spread, own, other,
                  grid, wide, prods, ends, line, side, sides, sums, corner, keep):
    first, last, core = flags[0], flags[1], flags[2]
    rows, half, c2 = slope.shape
    c1 = c2 // 2
    pooled = rows // 2
    c0 = fields_t.shape[0] // 2
    cells = pooled * half

    grid[:, half:, :] = jnp.zeros((pooled + 2, EDGE, c1), F32)
    grid[1:pooled + 1, :half, :] = grad_out[...].astype(F32)
    grid[0, :half, :] = top[2 * half:, :].astype(F32)
    grid[pooled + 1, :half, :] = bottom[2 * half:, :].astype(F32)
    side[0] = left[...].astype(F32)
    side[1] = right[...].astype(F32)
    for i in range(pooled + 2):
        grid[i, half:half + 1, :] = side[1, rows + 2 + i:rows + 3 + i, :]
        grid[i, half + EDGE - 1:half + EDGE, :] = side[0, rows + 2 + i:rows + 3 + i, :]
    for i in range(pooled + 2):
        here = grid[i]
        wide[i, :, :c1] = pltpu.roll(here, 1, 0).astype(BF16)
        wide[i, :, c1:2 * c1] = here.astype(BF16)
        wide[i, :, 2 * c1:3 * c1] = pltpu.roll(here, half + EDGE - 1, 0).astype(BF16)
        wide[i, :, 3 * c1:] = here.astype(BF16)

    flat = wide[1:pooled + 1].reshape(pooled * (half + EDGE), 4 * c1)
    for a in range(3):
        prods[a] = dot_nt(flat, taps[a]).reshape(pooled, half + EDGE, c2)
    fold = jnp.where(first == 1, taps[0], taps[2])
    ends[0] = dot_nt(wide[0], fold)
    ends[1] = dot_nt(wide[0], taps[1])
    ends[2] = dot_nt(wide[pooled + 1], taps[0])
    ends[3] = dot_nt(wide[pooled + 1], taps[1])

    for s in range(2):
        sides[s] = slope_of(side[s], cdf_of(side[s]))

    def place(r, total, incline):
        inner = total[:half] * incline
        rim = total[half:]
        after = rim[:1, :c1] * sides[1, pl.ds(r, 1), :]
        before = rim[EDGE - 1:, c1:] * sides[0, pl.ds(r, 1), :]
        even, odd = inner[:, :c1], inner[:, c1:]
        at = lax.broadcasted_iota(jnp.int32, (half, c1), 0)
        spread[r, :, :c1] = jnp.where(at == 0, before, pltpu.roll(odd, 1, 0)).astype(BF16)
        spread[r, :, c1:2 * c1] = even.astype(BF16)
        spread[r, :, 2 * c1:3 * c1] = odd.astype(BF16)
        spread[r, :, 3 * c1:] = jnp.where(at == half - 1, after, pltpu.roll(even, half - 1, 0)).astype(BF16)

    def halo_slope(message):
        line[...] = message[:2 * half, :].astype(F32)
        both = [line[pl.ds(pc, half, stride=2), :] for pc in range(2)]
        return jnp.concatenate([slope_of(v, cdf_of(v)) for v in both], axis=1)

    place(0, ends[0] + ends[1] + prods[0, 0], halo_slope(top))
    place(1, ends[0] + prods[1, 0] + prods[0, 0], slope[0])

    def pair(i, carry):
        middle = prods[2, i] + prods[1, i]
        place(2 * i + 2, middle + prods[0, i + 1], slope[2 * i + 1])
        place(2 * i + 3, prods[2, i] + prods[1, i + 1] + prods[0, i + 1], slope[2 * i + 2])
        return carry

    lax.fori_loop(0, pooled - 1, pair, 0)
    final = prods[2, pooled - 1]
    place(rows, final + prods[1, pooled - 1] + ends[2], slope[rows - 1])
    outside = jnp.where(last == 1, 0.0, 1.0)
    place(rows + 1, (final + ends[3] + ends[2]) * outside, halo_slope(bottom))

    is_first = jnp.where(first == 1, 1.0, 0.0).astype(BF16)
    not_first = jnp.where(first == 1, 0.0, 1.0).astype(BF16)
    above = wide[0, :half, :3 * c1]
    wide[0, :half, :3 * c1] = above * not_first
    for n, (pr, start) in enumerate(((0, 0), (0, 1), (1, 1), (1, 2))):
        around = wide[start:start + pooled, :half, :3 * c1].reshape(cells, 3 * c1)
        sums[n] = dot(act_t[pr], around)
    corner[...] = dot(act_t[0, :, :half], above * is_first)

    unit = c0
    per_tap = c1 // unit
    count = 9 * per_tap + 9
    split = (count + 1) // 2

    def put(k, value):
        keep[k // split, (k % split) * unit:(k % split + 1) * unit, :] = value

    pieces = {0: ((0, 1), (1, 3)), 1: ((0, 1), (1, 2)), 2: ((0, 0), (1, 2))}
    for a in range(3):
        for b in range(3):
            total = None
            for pr, n in pieces[a]:
                for pc in range(2):
                    k = (pc + 1 - b) // 2 + 1
                    term = sums[n, pc * c1:(pc + 1) * c1, k * c1:(k + 1) * c1]
                    total = term if total is None else total + term
            if a == 0:
                for pc in range(2):
                    k = (pc + 1 - b) // 2 + 1
                    total = total + corner[pc * c1:(pc + 1) * c1, k * c1:(k + 1) * c1]
            total = total * 0.25
            for part in range(per_tap):
                put((3 * a + b) * per_tap + part, total[part * unit:(part + 1) * unit])

    head = spread[0]
    spread[0] = head * not_first
    folded = dot(fields_t[:, :half], head * is_first)
    for a in range(3):
        around = spread[2 - a:2 - a + rows].reshape(rows * half, 4 * c1)
        got = dot(fields_t[...], around)
        if a == 0:
            got = got + folded
        for b in range(3):
            even = got[:c0, (2 - b) * c1:(3 - b) * c1]
            odd = got[c0:, (3 - b) * c1:(4 - b) * c1]
            put(9 * per_tap + 3 * a + b, even + odd)
    spread[0] = head
    for k in range(count, 2 * split):
        put(k, jnp.zeros((unit, c1), F32))
    if own.shape[0] > split * unit:
        rest = jnp.zeros((own.shape[0] - split * unit, c1), F32)
        own[split * unit:] = rest
        other[split * unit:] = rest
    own[:split * unit] = keep[core]
    other[:split * unit] = keep[1 - core]


def last_kernel(flags, spread, taps, out, prods, line):
    rows, cols, c0 = out.shape
    half = cols // 2
    c2 = 2 * c0
    prods[...] = dot_nt(spread[1:rows + 1].reshape(rows * half, spread.shape[2]), taps[...]).reshape(
        rows, half, 3 * c2)
    fold = jnp.where(flags[0] == 1, taps[:c2], taps[2 * c2:])
    above = dot_nt(spread[0], fold)
    below = dot_nt(spread[rows + 1], taps[:c2])

    def emit(r, total):
        line[pl.ds(0, half, stride=2), :] = total[:, :c0]
        line[pl.ds(1, half, stride=2), :] = total[:, c0:]
        out[r] = line[...].astype(BF16)

    emit(0, prods[1, :, :c2] + prods[0, :, c2:2 * c2] + above)

    def inner(r, carry):
        emit(r, prods[r + 1, :, :c2] + prods[r, :, c2:2 * c2] + prods[r - 1, :, 2 * c2:])
        return carry

    lax.fori_loop(1, rows - 1, inner, 0)
    emit(rows - 1, below + prods[rows - 1, :, c2:2 * c2] + prods[rows - 2, :, 2 * c2:])


def vmem(count):
    return [pl.BlockSpec(memory_space=pltpu.VMEM)] * count


def params():
    return pltpu.CompilerParams(vmem_limit_bytes=48 * 1024 * 1024)


def shape(dims, kind):
    return jax.ShapeDtypeStruct(dims, kind)


def body(inputs, pre_first, grad_out, w_first, w_second):
    rows, cols, c1 = pre_first.shape
    c0 = inputs.shape[2]
    half, pooled = cols // 2, rows // 2
    lats, lons = lax.axis_size("lat"), lax.axis_size("lon")
    band, place = lax.axis_index("lat"), lax.axis_index("lon")
    core = lax.rem(place, 2)
    flags = jnp.stack([band == 0, band == lats - 1, core]).astype(jnp.int32)

    head = jnp.concatenate([pre_first[0], grad_out[0]], 0)
    tail = jnp.concatenate([pre_first[-1], grad_out[-1]], 0)
    down = lax.ppermute(tail, "lat", [(i, i + 1) for i in range(lats - 1)])
    up = lax.ppermute(head, "lat", [(i + 1, i) for i in range(lats - 1)])
    over = lax.ppermute(head, AREA, [(i, (i + lons // 2) % lons) for i in range(lons)])
    top = jnp.where(band == 0, over, down)
    bottom = up

    slope, act_t, fields_t, taps_first, taps_second = pl.pallas_call(
        local_kernel,
        out_shape=(
            shape((rows, half, 2 * c1), F32),
            shape((2, 2 * c1, pooled * half), BF16),
            shape((2 * c0, rows * half), BF16),
            shape((6 * c0, 4 * c1), BF16),
            shape((3, 2 * c1, 4 * c1), BF16),
        ),
        in_specs=vmem(4),
        out_specs=tuple(vmem(5)),
        scratch_shapes=[
            pltpu.VMEM((cols, c1), F32),
            pltpu.VMEM((cols, c0), F32),
            pltpu.VMEM((2, pooled, half, 2 * c1), BF16),
            pltpu.VMEM((2, rows, half, c0), BF16),
        ],
        compiler_params=params(),
        cost_estimate=pl.CostEstimate(flops=60 * rows * cols * c1, bytes_accessed=6 << 20,
                                      transcendentals=2 * rows * cols * c1),
    )(pre_first, inputs, w_first, w_second)

    def column(at):
        p, g = at * (cols - 1), at * (half - 1)
        parts = [top[p:p + 1], pre_first[:, p], bottom[p:p + 1],
                 top[cols + g:cols + g + 1], grad_out[:, g], bottom[cols + g:cols + g + 1]]
        pad = -(rows + pooled + 4) % 16
        return jnp.concatenate(parts + [jnp.zeros((pad, c1), BF16)], 0)

    left = lax.ppermute(column(1), "lon", [(i, (i + 1) % lons) for i in range(lons)])
    right = lax.ppermute(column(0), "lon", [(i, (i - 1) % lons) for i in range(lons)])

    chips = lats * lons // 2
    unit = 8 * chips
    split = (9 * (c1 // c0) + 10) // 2 * c0
    held = -(-split // unit) * unit
    span = half + EDGE
    spread, own, other = pl.pallas_call(
        middle_kernel,
        out_shape=(
            shape((rows + 2, half, 4 * c1), BF16),
            shape((held, c1), F32),
            shape((held, c1), F32),
        ),
        in_specs=[pl.BlockSpec(memory_space=pltpu.SMEM)] + vmem(9),
        out_specs=tuple(vmem(3)),
        scratch_shapes=[
            pltpu.VMEM((pooled + 2, span, c1), F32),
            pltpu.VMEM((pooled + 2, span, 4 * c1), BF16),
            pltpu.VMEM((3, pooled, span, 2 * c1), F32),
            pltpu.VMEM((4, span, 2 * c1), F32),
            pltpu.VMEM((cols, c1), F32),
            pltpu.VMEM((2, left.shape[0], c1), F32),
            pltpu.VMEM((2, left.shape[0], c1), F32),
            pltpu.VMEM((4, 2 * c1, 3 * c1), F32),
            pltpu.VMEM((2 * c1, 3 * c1), F32),
            pltpu.VMEM((2, split, c1), F32),
        ],
        compiler_params=params(),
        cost_estimate=pl.CostEstimate(flops=2 * rows * cols * c1 * 9 * (2 * c1 + c0), bytes_accessed=8 << 20,
                                      transcendentals=0),
    )(flags, grad_out, top, bottom, left, right, slope, act_t, fields_t, taps_second)

    swap = [(i, i ^ 1) for i in range(lons)]
    mine = own + lax.ppermute(other, "lon", swap)
    groups = [[2 * i + k for i in range(chips)] for k in range(2)]
    parts = lax.all_to_all(mine.reshape(chips, held // chips, c1), AREA, 0, 0,
                           axis_index_groups=groups, tiled=True)
    total = jnp.sum(parts, 0)
    every = lax.all_to_all(jnp.broadcast_to(total[None], parts.shape), AREA, 0, 0,
                           axis_index_groups=groups, tiled=True)
    mine = every.reshape(held, c1)[:split]
    theirs = lax.ppermute(mine, "lon", swap)

    grad_inputs = pl.pallas_call(
        last_kernel,
        out_shape=shape((rows, cols, c0), BF16),
        in_specs=[pl.BlockSpec(memory_space=pltpu.SMEM)] + vmem(2),
        out_specs=vmem(1)[0],
        scratch_shapes=[
            pltpu.VMEM((rows, half, 6 * c0), F32),
            pltpu.VMEM((cols, c0), F32),
        ],
        compiler_params=params(),
        cost_estimate=pl.CostEstimate(flops=2 * rows * cols * c1 * 9 * c0, bytes_accessed=3 << 20, transcendentals=0),
    )(flags, spread, taps_first)

    low = jnp.where(core == 0, mine, theirs)
    high = jnp.where(core == 0, theirs, mine)
    both = jnp.concatenate([low, high], 0)
    size = 9 * c1
    grad_w_second = both[:size].reshape(3, 3, c1, c1)
    grad_w_first = both[size:size + 9 * c0].reshape(3, 3, c0, c1)
    return (grad_inputs, grad_w_first, grad_w_second)


def solution(mesh):
    in_specs = (P("lat", "lon", None), P("lat", "lon", None), P("lat", "lon", None), P(), P())
    out_specs = (P("lat", "lon", None), P(), P())
    return jax.shard_map(body, mesh=mesh, in_specs=in_specs, out_specs=out_specs, check_vma=False)
```

time: 310 us -> 70 us (0.23)
  waiting for transfers between devices: 136 us -> 1.94 us
  local copies, waits for them, and re-layouts: 69.2 us -> 6.61 us
  other arithmetic: 44.8 us -> 1.09 us
  blocking collectives: 0 us -> 39.5 us
  matrix products: 18.6 us -> 0 us
  between operations: 14.9 us -> 0.89 us
  starting transfers between devices: 24.9 us -> 12.2 us
  Pallas kernels: 0 us -> 7.28 us
    psum x1 -> x0, waiting for transfers between devices: 125 us -> none  [body(): lax.psum((local_first, local_second), ('lat', 'lon'))]
    scatter-add x18 -> x0, local copies, waits for them, and re-layouts: 48.8 us -> none  [the longest x14 46.2 us: spread(): grid = grid.at[a:a + rows, b:b + cols].add(terms[:, :, a, b])]
    all_to_all x0 -> x2, blocking collectives: none -> 39.5 us  [the longest x1 21.8 us: body(): lax.all_to_all(mine.reshape(chips, held // chips, c1), AREA, 0, 0, axis_i...]
    add x14 -> x1, other arithmetic: 20 us -> 0.05 us  [body(): mine = own + lax.ppermute(other, 'lon', swap)]
    dot_general x20 -> x0, matrix products: 18.6 us -> none  [the longest x18 14.2 us: taps_product(): lax.dot_general(piece, flat, (((0,), (0,)), ((), ())), preferred_element_...]
    ppermute x15 -> x7, starting transfers between devices: 24.9 us -> 12.2 us  [the longest x1 5.94 us: body(): lax.ppermute(head, AREA, [(i, (i + lons // 2) % lons) for i in range(lons)])]
    another operation x10 -> x1, other arithmetic: 11.2 us -> 0.08 us  [body(): flags = jnp.stack([band == 0, band == lats - 1, core]).astype(jnp.int32)]
    ppermute x15 -> x7, waiting for transfers between devices: 10.9 us -> 1.94 us  [the longest x1 1.8 us: body(): mine = own + lax.ppermute(other, 'lon', swap)]
  transfers between devices with their start and end apart: 16 -> 7, of which waited for: 7 -> 2; matrix products, arithmetic and copies ran while one was open for 24% -> 6% of each run, Pallas kernels for 0% -> 6%
where the time goes in v1:
time: 70 us; the launch traced here: 69.5 us
  blocking collectives  39.5 us (56%)
  starting transfers between devices  12.2 us (17%)
  Pallas kernels  7.28 us (10%)
  local copies, waits for them, and re-layouts  6.61 us (9%)
  waiting for transfers between devices  1.94 us (3%)
  other arithmetic  1.09 us (2%)
  between operations  0.89 us (1%)
    all_to_all x1, blocking collectives, body(): lax.all_to_all(mine.reshape(chips, held // chips, c1), AREA, 0, 0, axis_i...  21.8 us
    all_to_all x1, blocking collectives, body(): lax.all_to_all(jnp.broadcast_to(total[None], parts.shape), AREA, 0, 0, ax...  17.7 us
    ppermute x1, starting transfers between devices, body(): lax.ppermute(head, AREA, [(i, (i + lons // 2) % lons) for i in range(lons)])  5.94 us
    ppermute x1, starting transfers between devices, body(): lax.ppermute(column(0), 'lon', [(i, (i - 1) % lons) for i in range(lons)])  3.55 us
    pallas_call x1, Pallas kernels, body(): pl.pallas_call(middle_kernel, out_shape=(shape((rows + 2, half, 4 * c1),...  3.22 us
    pallas_call x1, Pallas kernels, body(): pl.pallas_call(last_kernel, out_shape=shape((rows, cols, c0), BF16), in_s...  2.83 us
    unnamed x14, local copies, waits for them, and re-layouts  2.17 us
    ppermute x1, waiting for transfers between devices, body(): mine = own + lax.ppermute(other, 'lon', swap)  1.8 us
  transfers between devices with their start and end apart: 7, of which 2 were waited for; matrix products, arithmetic and copies ran while one was open for 6% of the time, Pallas kernels for 6%

profile of v1, /device:TPU:0, one launch (start us, length us, event | category | flops | bytes accessed | tf_op | source)
XLA Modules:
  0.0 69.5 jit_solution(6262333720431073981)
XLA Ops:
  0.6 0.0 copy-start
  0.6 0.0 copy-start.1
  0.7 0.0 copy-start.2
  0.7 0.8 %slice_bitcast_fusion.2 = (bf16[64,128]{1,0:T(8,128)(2,1)S(1)}, bf16[64,128]{1,0:T(8,128)(2,1)S(1)}) fusion(bf16[8,64,128]{2,1,0:T(8,128)(2,1)} %grad_out.1), kind=kLoop, calls=%fused_computation.8 | loop fusion | bytes 65536 | tf_op jit(solution)/shard_map/squeeze | solution.py:244
  1.5 0.8 %slice_bitcast_fusion = (bf16[128,128]{1,0:T(8,128)(2,1)S(1)}, bf16[128,128]{1,0:T(8,128)(2,1)S(1)}) fusion(bf16[16,128,128]{2,1,0:T(8,128)(2,1)} %pre.1), kind=kLoop, calls=%fused_computation.6 | loop fusion | bytes 131072 | tf_op jit(solution)/shard_map/squeeze | solution.py:244
  2.3 1.3 %collective-permute-start.2 = (bf16[192,128]{1,0:T(8,128)(2,1)S(1)}, bf16[192,128]{1,0:T(8,128)(2,1)S(1)}, u32[]{:S(2)}, u32[]{:S(2)}) collective-permute-start(bf16[192,128]{1,0:T(8,128)(2,1)S(1)} %pad_maximum_fusion.1), channel_id=1, source_target_pairs={{8,0},{16,8},{24,16},{9,1},{17,9},{25,17},{10,2},{18,10},{26,18},{... | collective-permute-start | bytes 147464 | tf_op jit(solution)/shard_map/ppermute | solution.py:246
  3.6 5.9 %collective-permute-start = (bf16[192,128]{1,0:T(8,128)(2,1)S(1)}, bf16[192,128]{1,0:T(8,128)(2,1)S(1)}, u32[]{:S(2)}, u32[]{:S(2)}) collective-permute-start(bf16[192,128]{1,0:T(8,128)(2,1)S(1)} %pad_maximum_fusion.1), channel_id=1, source_target_pairs={{0,4},{1,5},{2,6},{3,7},{4,0},{5,1},{6,2},{7,3}} | collective-permute-start | bytes 147464 | tf_op jit(solution)/shard_map/ppermute | solution.py:247
  9.5 1.3 %collective-permute-start.1 = (bf16[192,128]{1,0:T(8,128)(2,1)S(1)}, bf16[192,128]{1,0:T(8,128)(2,1)S(1)}, u32[]{:S(2)}, u32[]{:S(2)}) collective-permute-start(bf16[192,128]{1,0:T(8,128)(2,1)S(1)} %pad_maximum_fusion.2), channel_id=1, source_target_pairs={{0,8},{8,16},{16,24},{1,9},{9,17},{17,25},{2,10},{10,18},{18,26},{... | collective-permute-start | bytes 147464 | tf_op jit(solution)/shard_map/ppermute | solution.py:245
  10.8 0.8 %fusion = (bf16[16,1,128]{2,1,0:T(2,128)(2,1)S(1)}, bf16[16,1,128]{2,1,0:T(2,128)(2,1)S(1)}) fusion(bf16[16,128,128]{2,1,0:T(8,128)(2,1)} %pre.1), kind=kLoop, calls=%fused_computation.15 | loop fusion | bytes 16384 | tf_op jit(solution)/shard_map/slice | solution.py:275
  11.6 0.7 %fusion.1 = (bf16[8,1,128]{2,1,0:T(2,128)(2,1)S(1)}, bf16[8,1,128]{2,1,0:T(2,128)(2,1)S(1)}) fusion(bf16[8,64,128]{2,1,0:T(8,128)(2,1)} %grad_out.1), kind=kLoop, calls=%fused_computation.16 | loop fusion | bytes 8192 | tf_op jit(solution)/shard_map/slice | solution.py:276
  12.4 0.0 collective-permute-done
  12.4 0.1 collective-permute-done.1
  12.6 0.0 copy-start.3
  12.6 0.0 collective-permute-done.2.bottom
  12.6 0.3 concatenate.17
  12.9 0.0 collective-permute-start.3
  13.0 0.3 concatenate.18
  13.2 3.6 %collective-permute-start.4 = (bf16[32,128]{1,0:T(8,128)(2,1)S(1)}, bf16[32,128]{1,0:T(8,128)(2,1)S(1)}, u32[]{:S(2)}, u32[]{:S(2)}) collective-permute-start(bf16[32,128]{1,0:T(8,128)(2,1)S(1)} %concatenate.18), channel_id=1, source_target_pairs={{0,7},{1,0},{2,1},{3,2},{4,3},{5,4},{6,5},{7,6},{8,15},{9,8},{10,9... | collective-permute-start | bytes 24584 | tf_op jit(solution)/shard_map/ppermute | solution.py:281
  16.8 0.1 pad_add_fusion.flags
  16.8 1.2 %copy.12.fields = bf16[16,128,64]{2,1,0:T(8,128)(2,1)S(1)} copy(bf16[16,128,64]{1,2,0:T(8,128)(2,1)} %param.5) | data formatting | bytes 524288 | tf_op args[0]
  18.1 0.0 copy-done
  18.1 0.0 copy-done.1
  18.1 0.0 copy-done.2
  18.1 1.2 %shard_map.76 = (f32[16,64,256]{2,1,0:T(8,128)S(1)}, bf16[2,256,512]{2,1,0:T(8,128)(2,1)S(1)}, bf16[128,1024]{1,0:T(8,128)(2,1)S(1)}, bf16[384,512]{1,0:T(8,128)(2,1)S(1)}, bf16[3,256,512]{2,1,0:T(8,128)(2,1)S(1)}) custom-call(bf16[16,128,128]{2,1,0:T(8,128)(2,1)S(1)} %copy-done, bf16[16,128,64]{2,1,0:T(8,128)(2,1)S(1)} %copy.12.fields, ...), custom_call_target="tpu_custom_call" | custom-call | flops 15728640 | bytes 6291456 | tf_op jit(solution)/shard_map/pallas_call | solution.py:251
  19.3 0.0 collective-permute-done.3.left
  19.4 0.0 collective-permute-done.4.right
  19.4 0.0 copy-done.3
  19.4 3.2 %shard_map.77 = (bf16[18,64,512]{2,1,0:T(8,128)(2,1)S(1)}, f32[896,128]{1,0:T(8,128)S(1)}, f32[896,128]{1,0:T(8,128)S(1)}) custom-call(s32[3]{0:T(128)S(1)} %pad_add_fusion.flags, bf16[8,64,128]{2,1,0:T(8,128)(2,1)S(1)} %copy-done.3, bf16[192,128]{1,0:T(8,128)(2,1)S(1)} %broadcast_select_fusion.2.top, bf16[192,128]{1,0:T(8,128)(2,1)S(1)} %collective-permute-done.2.bottom, ...), custom_call_target="tpu_custom_call" | custom-call | flops 1509949440 | bytes 8388608 | tf_op jit(solution)/shard_map/pallas_call | solution.py:288
  22.6 0.1 collective-permute-start.5
  22.7 1.8 %collective-permute-done.5 = f32[896,128]{1,0:T(8,128)S(1)} collective-permute-done((f32[896,128]{1,0:T(8,128)S(1)}, f32[896,128]{1,0:T(8,128)S(1)}, u32[]{:S(2)}, u32[]{:S(2)}) %collective-permute-start.5) | collective-permute-done | bytes 458784 | tf_op jit(solution)/shard_map/ppermute | solution.py:315
  24.5 21.8 %all_to_all.10 = f32[16,56,128]{2,1,0:T(8,128)S(1)} all-to-all(f32[16,56,128]{2,1,0:T(8,128)S(1)} %bitcast.30), channel_id=1, replica_groups={{0,2,4,6,8,10,12,14,16,18,20,22,24,26,28,30},{1,3,5,7,9,11,13,15,17,19,..., dimensions={0} | all-to-all | bytes 917504 | tf_op jit(solution)/shard_map/all_to_all | solution.py:317
  46.4 17.7 %all_to_all.11 = f32[16,56,128]{2,1,0:T(8,128)S(1)} all-to-all(f32[16,56,128]{2,1,0:T(8,128)S(1)} %broadcast_in_dim.2), channel_id=1, replica_groups={{0,2,4,6,8,10,12,14,16,18,20,22,24,26,28,30},{1,3,5,7,9,11,13,15,17,19,..., dimensions={0} | all-to-all | bytes 917504 | tf_op jit(solution)/shard_map/all_to_all | solution.py:320
  64.1 0.0 collective-permute-start.6
  64.1 2.8 %shard_map.78 = bf16[16,128,64]{2,1,0:T(8,128)(2,1)S(1)} custom-call(s32[3]{0:T(128)S(1)} %pad_add_fusion.flags, bf16[18,64,512]{2,1,0:T(8,128)(2,1)S(1)} %get-tuple-element.15.spread, bf16[384,512]{1,0:T(8,128)(2,1)S(1)} %get-tuple-element.16.taps), custom_call_target="tpu_custom_call" | custom-call | flops 301989888 | bytes 3145728 | tf_op jit(solution)/shard_map/pallas_call | solution.py:325
  66.9 0.9 %copy.13 = bf16[16,128,64]{1,2,0:T(8,128)(2,1)} copy(bf16[16,128,64]{2,1,0:T(8,128)(2,1)S(1)} %shard_map.78) | data formatting | bytes 524288
  67.8 0.0 collective-permute-done.6
  67.8 0.1 broadcast_select_fusion
  67.9 0.7 %slice.80 = f32[576,128]{1,0:T(8,128)} slice(f32[896,128]{1,0:T(8,128)S(1)} %get-tuple-element.23), slice={[256:832], [0:128]} | slice | bytes 589824 | tf_op jit(solution)/shard_map/slice | solution.py:343
  68.6 0.9 %pad_maximum_fusion = f32[1152,128]{1,0:T(8,128)} fusion(f32[896,128]{1,0:T(8,128)S(1)} %get-tuple-element.23, f32[896,128]{1,0:T(8,128)S(1)} %get-tuple-element.22), kind=kLoop, calls=%fused_computation | loop fusion | flops 147456 | bytes 1507328 | tf_op jit(solution)/shard_map/concatenate | solution.py:340
  (13 shorter events, 0.2 us)
Async XLA Ops:
  0.6 17.4 %copy-start = (bf16[16,128,128]{2,1,0:T(8,128)(2,1)S(1)}, bf16[16,128,128]{2,1,0:T(8,128)(2,1)}, u32[]{:S(2)}) copy-start(bf16[16,128,128]{2,1,0:T(8,128)(2,1)} %pre.1) | copy-start | bytes 1572868
  0.6 17.4 %copy-start.1 = (bf16[3,3,128,128]{3,2,1,0:T(8,128)(2,1)S(1)}, bf16[3,3,128,128]{3,2,1,0:T(8,128)(2,1)}, u32[]{:S(2)}) copy-start(bf16[3,3,128,128]{3,2,1,0:T(8,128)(2,1)} %w_second.1) | copy-start | bytes 884740
  0.7 17.4 %copy-start.2 = (bf16[3,3,64,128]{3,2,1,0:T(8,128)(2,1)S(1)}, bf16[3,3,64,128]{3,2,1,0:T(8,128)(2,1)}, u32[]{:S(2)}) copy-start(bf16[3,3,64,128]{3,2,1,0:T(8,128)(2,1)} %w_first.1) | copy-start | bytes 442372
  2.3 10.3 %collective-permute-start.2 = (bf16[192,128]{1,0:T(8,128)(2,1)S(1)}, bf16[192,128]{1,0:T(8,128)(2,1)S(1)}, u32[]{:S(2)}, u32[]{:S(2)}) collective-permute-start(bf16[192,128]{1,0:T(8,128)(2,1)S(1)} %pad_maximum_fusion.1), channel_id=1, source_target_pairs={{8,0},{16,8},{24,16},{9,1},{17,9},{25,17},{10,2},{18,10},{26,18},{... | collective-permute-start | bytes 147464 | tf_op jit(solution)/shard_map/ppermute | solution.py:246
  3.6 8.9 %collective-permute-start = (bf16[192,128]{1,0:T(8,128)(2,1)S(1)}, bf16[192,128]{1,0:T(8,128)(2,1)S(1)}, u32[]{:S(2)}, u32[]{:S(2)}) collective-permute-start(bf16[192,128]{1,0:T(8,128)(2,1)S(1)} %pad_maximum_fusion.1), channel_id=1, source_target_pairs={{0,4},{1,5},{2,6},{3,7},{4,0},{5,1},{6,2},{7,3}} | collective-permute-start | bytes 147464 | tf_op jit(solution)/shard_map/ppermute | solution.py:247
  9.5 3.0 %collective-permute-start.1 = (bf16[192,128]{1,0:T(8,128)(2,1)S(1)}, bf16[192,128]{1,0:T(8,128)(2,1)S(1)}, u32[]{:S(2)}, u32[]{:S(2)}) collective-permute-start(bf16[192,128]{1,0:T(8,128)(2,1)S(1)} %pad_maximum_fusion.2), channel_id=1, source_target_pairs={{0,8},{8,16},{16,24},{1,9},{9,17},{17,25},{2,10},{10,18},{18,26},{... | collective-permute-start | bytes 147464 | tf_op jit(solution)/shard_map/ppermute | solution.py:245
  12.6 6.8 %copy-start.3 = (bf16[8,64,128]{2,1,0:T(8,128)(2,1)S(1)}, bf16[8,64,128]{2,1,0:T(8,128)(2,1)}, u32[]{:S(2)}) copy-start(bf16[8,64,128]{2,1,0:T(8,128)(2,1)} %grad_out.1) | copy-start | bytes 393220
  12.9 6.4 %collective-permute-start.3 = (bf16[32,128]{1,0:T(8,128)(2,1)S(1)}, bf16[32,128]{1,0:T(8,128)(2,1)S(1)}, u32[]{:S(2)}, u32[]{:S(2)}) collective-permute-start(bf16[32,128]{1,0:T(8,128)(2,1)S(1)} %concatenate.17), channel_id=1, source_target_pairs={{0,1},{1,2},{2,3},{3,4},{4,5},{5,6},{6,7},{7,0},{8,9},{9,10},{10,1... | collective-permute-start | bytes 24584 | tf_op jit(solution)/shard_map/ppermute | solution.py:280
  13.2 6.1 %collective-permute-start.4 = (bf16[32,128]{1,0:T(8,128)(2,1)S(1)}, bf16[32,128]{1,0:T(8,128)(2,1)S(1)}, u32[]{:S(2)}, u32[]{:S(2)}) collective-permute-start(bf16[32,128]{1,0:T(8,128)(2,1)S(1)} %concatenate.18), channel_id=1, source_target_pairs={{0,7},{1,0},{2,1},{3,2},{4,3},{5,4},{6,5},{7,6},{8,15},{9,8},{10,9... | collective-permute-start | bytes 24584 | tf_op jit(solution)/shard_map/ppermute | solution.py:281
  22.6 1.9 %collective-permute-start.5 = (f32[896,128]{1,0:T(8,128)S(1)}, f32[896,128]{1,0:T(8,128)S(1)}, u32[]{:S(2)}, u32[]{:S(2)}) collective-permute-start(f32[896,128]{1,0:T(8,128)S(1)} %get-tuple-element.18), channel_id=1, source_target_pairs={{0,1},{1,0},{2,3},{3,2},{4,5},{5,4},{6,7},{7,6},{8,9},{9,8},{10,11... | collective-permute-start | bytes 1376264 | tf_op jit(solution)/shard_map/ppermute | solution.py:315
  64.1 3.7 %collective-permute-start.6 = (f32[896,128]{1,0:T(8,128)S(1)}, f32[896,128]{1,0:T(8,128)S(1)}, u32[]{:S(2)}, u32[]{:S(2)}) collective-permute-start(f32[896,128]{1,0:T(8,128)S(1)} %bitcast.29), channel_id=1, source_target_pairs={{0,1},{1,0},{2,3},{3,2},{4,5},{5,4},{6,7},{7,6},{8,9},{9,8},{10,11... | collective-permute-start | bytes 1376264 | tf_op jit(solution)/shard_map/ppermute | solution.py:323

commit v2 on v1

v2 whole, which is shorter than its diff:
```python
import jax
import jax.numpy as jnp
from jax import lax
from jax.experimental import pallas as pl
from jax.experimental.pallas import tpu as pltpu
from jax.sharding import PartitionSpec as P

inv_root = 0.7071067811865476
density = 0.3989422804014327

F32 = jnp.float32
BF16 = jnp.bfloat16
EDGE = 16
AREA = ("lat", "lon")


def cdf_of(value):
    return 0.5 * (1.0 + lax.erf(value * inv_root))


def slope_of(value, cdf):
    return 0.25 * (cdf + value * jnp.exp(-0.5 * value * value) * density)


def dot(left, right):
    return jnp.dot(left, right, preferred_element_type=F32)


def dot_nt(left, right):
    return lax.dot_general(left, right, (((1,), (1,)), ((), ())), preferred_element_type=F32)


def pack_kernel(pre, grad_out, head, tail, first_col, last_col, hold):
    rows, cols, c1 = pre.shape
    pooled, half = grad_out.shape[:2]
    head[:cols] = pre[0]
    head[cols:] = grad_out[0]
    tail[:cols] = pre[rows - 1]
    tail[cols:] = grad_out[pooled - 1]
    for message, p, g in ((first_col, 0, 0), (last_col, cols - 16, half - 16)):
        at = 0 if p == 0 else 15
        hold[rows + pooled:] = jnp.zeros((hold.shape[0] - rows - pooled, c1), F32)
        for r in range(rows):
            hold[r:r + 1] = pre[r, p:p + 16].astype(F32)[at:at + 1]
        for i in range(pooled):
            hold[rows + i:rows + i + 1] = grad_out[i, g:g + 16].astype(F32)[at:at + 1]
        message[...] = hold[...].astype(BF16)


def one_at(where):
    return jnp.where(where, 1.0, 0.0).astype(BF16)


def local_kernel(pre, fields, w_first, w_second, slope, act_t, fields_t, taps_first, taps_second,
                 line, act_s, turned):
    rows, cols, c1 = pre.shape
    c0 = fields.shape[1]
    half = cols // 2

    def one_row(r, carry):
        line[...] = pre[r].astype(F32)
        for pc in range(2):
            value = line[pl.ds(pc, half, stride=2), :]
            cdf = cdf_of(value)
            act_s[r % 2, r // 2, :, pc * c1:(pc + 1) * c1] = (value * cdf).astype(BF16)
            slope[r, :, pc * c1:(pc + 1) * c1] = slope_of(value, cdf)
        return carry

    lax.fori_loop(0, rows, one_row, 0)
    for pr in range(2):
        act_t[pr] = act_s[pr].reshape(rows // 2 * half, 2 * c1).T
    col = lax.broadcasted_iota(jnp.int32, (cols, 2 * cols), 0)
    lane = lax.broadcasted_iota(jnp.int32, (cols, 2 * cols), 1)
    turn = lane // cols
    parity = (lane % cols) // half
    parity = parity + turn - 2 * parity * turn
    order = one_at(col == 2 * (lane % half) + parity)
    turned[...] = dot(fields[...].reshape(rows * c0, cols), order).astype(BF16).reshape(rows, c0, 2 * cols)
    low = lax.broadcasted_iota(jnp.int32, (c0, cols), 1) < half
    for q in range(rows // 2):
        fields_t[:c0, q * cols:(q + 1) * cols] = jnp.where(low, turned[2 * q, :, :cols], turned[2 * q + 1, :, cols:])
        fields_t[c0:, q * cols:(q + 1) * cols] = jnp.where(low, turned[2 * q, :, cols:], turned[2 * q + 1, :, :cols])
    taps_second[...] = jnp.zeros_like(taps_second)
    taps_first[...] = jnp.zeros_like(taps_first)
    for a in range(3):
        for pc, blocks in ((0, (2, 1, None, 0)), (1, (None, 2, 0, 1))):
            for k, b in enumerate(blocks):
                if b is not None:
                    taps_second[a, pc * c1:(pc + 1) * c1, k * c1:(k + 1) * c1] = w_second[a, b]
        for pc, blocks in ((0, (2, 1, 0, None)), (1, (None, 2, 1, 0))):
            for k, b in enumerate(blocks):
                if b is not None:
                    start = (2 * a + pc) * c0
                    taps_first[start:start + c0, k * c1:(k + 1) * c1] = w_first[a, b]


def middle_kernel(flags, grad_out, top, bottom, left, right, slope, act_t, fields_t, taps,
                  spread, own, other,
                  grid, wide, prods, ends, line, side, sides, sums, corner, keep):
    first, last, core = flags[0], flags[1], flags[2]
    rows, half, c2 = slope.shape
    c1 = c2 // 2
    pooled = rows // 2
    c0 = fields_t.shape[0] // 2
    cells = pooled * half

    grid[:, half:, :] = jnp.zeros((pooled + 2, EDGE, c1), F32)
    grid[1:pooled + 1, :half, :] = grad_out[...].astype(F32)
    grid[0, :half, :] = top[2 * half:, :].astype(F32)
    grid[pooled + 1, :half, :] = bottom[2 * half:, :].astype(F32)
    side[0] = left[...].astype(F32)
    side[1] = right[...].astype(F32)
    for i in range(pooled + 2):
        at = rows + i - 1
        if i == 0:
            at = rows + pooled + 2
        if i == pooled + 1:
            at = rows + pooled + 3
        grid[i, half:half + 1, :] = side[1, at:at + 1, :]
        grid[i, half + EDGE - 1:half + EDGE, :] = side[0, at:at + 1, :]
    for i in range(pooled + 2):
        here = grid[i]
        wide[i, :, :c1] = pltpu.roll(here, 1, 0).astype(BF16)
        wide[i, :, c1:2 * c1] = here.astype(BF16)
        wide[i, :, 2 * c1:3 * c1] = pltpu.roll(here, half + EDGE - 1, 0).astype(BF16)
        wide[i, :, 3 * c1:] = here.astype(BF16)

    flat = wide[1:pooled + 1].reshape(pooled * (half + EDGE), 4 * c1)
    for a in range(3):
        prods[a] = dot_nt(flat, taps[a]).reshape(pooled, half + EDGE, c2)
    fold = jnp.where(first == 1, taps[0], taps[2])
    ends[0] = dot_nt(wide[0], fold)
    ends[1] = dot_nt(wide[0], taps[1])
    ends[2] = dot_nt(wide[pooled + 1], taps[0])
    ends[3] = dot_nt(wide[pooled + 1], taps[1])

    for s in range(2):
        sides[s] = slope_of(side[s], cdf_of(side[s]))

    def place(r, total, incline, edge):
        inner = total[:half] * incline
        rim = total[half:]
        after = rim[:1, :c1] * sides[1, pl.ds(edge, 1), :]
        before = rim[EDGE - 1:, c1:] * sides[0, pl.ds(edge, 1), :]
        even, odd = inner[:, :c1], inner[:, c1:]
        at = lax.broadcasted_iota(jnp.int32, (half, c1), 0)
        spread[r, :, :c1] = jnp.where(at == 0, before, pltpu.roll(odd, 1, 0)).astype(BF16)
        spread[r, :, c1:2 * c1] = even.astype(BF16)
        spread[r, :, 2 * c1:3 * c1] = odd.astype(BF16)
        spread[r, :, 3 * c1:] = jnp.where(at == half - 1, after, pltpu.roll(even, half - 1, 0)).astype(BF16)

    def halo_slope(message):
        line[...] = message[:2 * half, :].astype(F32)
        both = [line[pl.ds(pc, half, stride=2), :] for pc in range(2)]
        return jnp.concatenate([slope_of(v, cdf_of(v)) for v in both], axis=1)

    place(0, ends[0] + ends[1] + prods[0, 0], halo_slope(top), rows + pooled)
    place(1, ends[0] + prods[1, 0] + prods[0, 0], slope[0], 0)

    def pair(i, carry):
        middle = prods[2, i] + prods[1, i]
        place(2 * i + 2, middle + prods[0, i + 1], slope[2 * i + 1], 2 * i + 1)
        place(2 * i + 3, prods[2, i] + prods[1, i + 1] + prods[0, i + 1], slope[2 * i + 2], 2 * i + 2)
        return carry

    lax.fori_loop(0, pooled - 1, pair, 0)
    final = prods[2, pooled - 1]
    place(rows, final + prods[1, pooled - 1] + ends[2], slope[rows - 1], rows - 1)
    outside = jnp.where(last == 1, 0.0, 1.0)
    place(rows + 1, (final + ends[3] + ends[2]) * outside, halo_slope(bottom), rows + pooled + 1)

    is_first = jnp.where(first == 1, 1.0, 0.0).astype(BF16)
    not_first = jnp.where(first == 1, 0.0, 1.0).astype(BF16)
    above = wide[0, :half, :3 * c1]
    wide[0, :half, :3 * c1] = above * not_first
    for n, (pr, start) in enumerate(((0, 0), (0, 1), (1, 1), (1, 2))):
        around = wide[start:start + pooled, :half, :3 * c1].reshape(cells, 3 * c1)
        sums[n] = dot(act_t[pr], around)
    corner[...] = dot(act_t[0, :, :half], above * is_first)

    unit = c0
    per_tap = c1 // unit
    count = 9 * per_tap + 9
    held = own.shape[0]

    def put(k, value):
        keep[k * unit:(k + 1) * unit, :] = value

    pieces = {0: ((0, 1), (1, 3)), 1: ((0, 1), (1, 2)), 2: ((0, 0), (1, 2))}
    for a in range(3):
        for b in range(3):
            total = None
            for pr, n in pieces[a]:
                for pc in range(2):
                    k = (pc + 1 - b) // 2 + 1
                    term = sums[n, pc * c1:(pc + 1) * c1, k * c1:(k + 1) * c1]
                    total = term if total is None else total + term
            if a == 0:
                for pc in range(2):
                    k = (pc + 1 - b) // 2 + 1
                    total = total + corner[pc * c1:(pc + 1) * c1, k * c1:(k + 1) * c1]
            total = total * 0.25
            for part in range(per_tap):
                put((3 * a + b) * per_tap + part, total[part * unit:(part + 1) * unit])

    head = spread[0]
    spread[0] = head * not_first
    spread[rows + 2] = head * is_first
    folded = dot(fields_t[:, :half], spread[rows + 2])
    for a in range(3):
        around = spread[2 - a:2 - a + rows].reshape(rows * half, 4 * c1)
        got = dot(fields_t[...], around)
        if a == 0:
            got = got + folded
        for b in range(3):
            even = got[:c0, (2 - b) * c1:(3 - b) * c1]
            odd = got[c0:, (3 - b) * c1:(4 - b) * c1]
            put(9 * per_tap + 3 * a + b, even + odd)
    keep[count * unit:] = jnp.zeros((2 * held - count * unit, c1), F32)
    own[...] = keep[pl.ds(pl.multiple_of(core * held, held), held), :]
    other[...] = keep[pl.ds(pl.multiple_of((1 - core) * held, held), held), :]


def last_kernel(spread, taps, out, total, turned):
    rows, c0, cols = out.shape
    half = cols // 2
    c2 = 2 * c0
    depth = spread.shape[2]
    result = dot_nt(taps[:c2], spread[2:rows + 2].reshape(rows * half, depth))
    for a in (1, 2):
        result = result + dot_nt(taps[a * c2:(a + 1) * c2],
                                 spread[2 - a:2 - a + rows].reshape(rows * half, depth))
    total[...] = result
    total[:, :half] = total[:, :half] + dot_nt(taps[:c2], spread[rows + 2])
    for q in range(rows // 2):
        pair = total[:, q * cols:(q + 1) * cols].astype(BF16)
        turned[q, :, :cols] = pair[:c0]
        turned[q, :, cols:] = pair[c0:]
    k = lax.broadcasted_iota(jnp.int32, (2 * cols, 2 * cols), 0)
    n = lax.broadcasted_iota(jnp.int32, (2 * cols, 2 * cols), 1)
    order = one_at(n == ((k % cols) // half) * cols + 2 * (k % half) + k // cols)
    found = dot(turned[...].reshape(rows // 2 * c0, 2 * cols), order).astype(BF16)
    for q in range(rows // 2):
        for rp in range(2):
            out[2 * q + rp] = found[q * c0:(q + 1) * c0, rp * cols:(rp + 1) * cols]


def gather_kernel(flags, mine, theirs, out_first, out_second):
    band, core = flags[3], flags[2]
    lats, count, rows, c1 = mine.shape
    size = out_second.shape[0]
    total = size + out_first.shape[0]
    for h in range(2):
        for i in range(lats):
            for j in range(count):
                at = ((h * lats + i) * count + j) * rows
                if at < total:
                    source = i ^ band
                    piece = jnp.where(core == h, mine[source, j], theirs[source, j]).astype(F32)
                    for out, base, end in ((out_second, 0, size), (out_first, size, total)):
                        low, high = max(at, base), min(at + rows, end)
                        if low < high:
                            out[low - base:high - base] = piece[low - at:high - at]


def vmem(count):
    return [pl.BlockSpec(memory_space=pltpu.VMEM)] * count


def params():
    return pltpu.CompilerParams(vmem_limit_bytes=48 * 1024 * 1024)


def shape(dims, kind):
    return jax.ShapeDtypeStruct(dims, kind)


def body(inputs, pre_first, grad_out, w_first, w_second):
    rows, cols, c1 = pre_first.shape
    c0 = inputs.shape[2]
    half, pooled = cols // 2, rows // 2
    lats, lons = lax.axis_size("lat"), lax.axis_size("lon")
    depths = lons // 2
    band, place = lax.axis_index("lat"), lax.axis_index("lon")
    core = lax.rem(place, 2)
    flags = jnp.stack([(band == 0).astype(jnp.int32), (band == lats - 1).astype(jnp.int32), core, band])

    edge = -(-(rows + pooled + 4) // 16) * 16
    head, tail, first_col, last_col = pl.pallas_call(
        pack_kernel,
        out_shape=(
            shape((cols + half, c1), BF16),
            shape((cols + half, c1), BF16),
            shape((edge, c1), BF16),
            shape((edge, c1), BF16),
        ),
        in_specs=vmem(2),
        out_specs=tuple(vmem(4)),
        scratch_shapes=[pltpu.VMEM((edge, c1), F32)],
        compiler_params=params(),
        cost_estimate=pl.CostEstimate(flops=1000, bytes_accessed=1 << 18, transcendentals=0),
    )(pre_first, grad_out)
    down = lax.ppermute(tail, "lat", [(i, i + 1) for i in range(lats - 1)])
    over = lax.ppermute(head, AREA, [(i, (i + lons // 2) % lons) for i in range(lons)])
    bottom = lax.ppermute(head, "lat", [(i + 1, i) for i in range(lats - 1)])
    top = jnp.where(band == 0, over, down)

    slope, act_t, fields_t, taps_first, taps_second = pl.pallas_call(
        local_kernel,
        out_shape=(
            shape((rows, half, 2 * c1), F32),
            shape((2, 2 * c1, pooled * half), BF16),
            shape((2 * c0, rows * half), BF16),
            shape((6 * c0, 4 * c1), BF16),
            shape((3, 2 * c1, 4 * c1), BF16),
        ),
        in_specs=vmem(4),
        out_specs=tuple(vmem(5)),
        scratch_shapes=[
            pltpu.VMEM((cols, c1), F32),
            pltpu.VMEM((2, pooled, half, 2 * c1), BF16),
            pltpu.VMEM((rows, c0, 2 * cols), BF16),
        ],
        compiler_params=params(),
        cost_estimate=pl.CostEstimate(flops=60 * rows * cols * c1, bytes_accessed=6 << 20,
                                      transcendentals=2 * rows * cols * c1),
    )(pre_first, jnp.transpose(inputs, (0, 2, 1)), w_first, w_second)

    def column(own_part, at):
        p, g = at * (cols - 1), cols + at * (half - 1)
        parts = [own_part[:rows + pooled], top[p:p + 1], bottom[p:p + 1], top[g:g + 1], bottom[g:g + 1]]
        return jnp.concatenate(parts + [jnp.zeros((edge - rows - pooled - 4, c1), BF16)], 0)

    left = lax.ppermute(column(last_col, 1), "lon", [(i, (i + 1) % lons) for i in range(lons)])
    right = lax.ppermute(column(first_col, 0), "lon", [(i, (i - 1) % lons) for i in range(lons)])

    chips = lats * depths
    size = 9 * (c1 + c0)
    piece = -(-size // (2 * chips * 16)) * 16
    held = chips * piece
    span = half + EDGE
    spread, own, other = pl.pallas_call(
        middle_kernel,
        out_shape=(
            shape((rows + 3, half, 4 * c1), BF16),
            shape((held, c1), F32),
            shape((held, c1), F32),
        ),
        in_specs=[pl.BlockSpec(memory_space=pltpu.SMEM)] + vmem(9),
        out_specs=tuple(vmem(3)),
        scratch_shapes=[
            pltpu.VMEM((pooled + 2, span, c1), F32),
            pltpu.VMEM((pooled + 2, span, 4 * c1), BF16),
            pltpu.VMEM((3, pooled, span, 2 * c1), F32),
            pltpu.VMEM((4, span, 2 * c1), F32),
            pltpu.VMEM((cols, c1), F32),
            pltpu.VMEM((2, edge, c1), F32),
            pltpu.VMEM((2, edge, c1), F32),
            pltpu.VMEM((4, 2 * c1, 3 * c1), F32),
            pltpu.VMEM((2 * c1, 3 * c1), F32),
            pltpu.VMEM((2 * held, c1), F32),
        ],
        compiler_params=params(),
        cost_estimate=pl.CostEstimate(flops=2 * rows * cols * c1 * 9 * (2 * c1 + c0), bytes_accessed=8 << 20,
                                      transcendentals=0),
    )(flags, grad_out, top, bottom, left, right, slope, act_t, fields_t, taps_second)

    swap = [(i, i ^ 1) for i in range(lons)]
    parts = (own + lax.ppermute(other, "lon", swap)).reshape(lats, depths * piece, c1)
    total = lax.dynamic_index_in_dim(parts, band, 0, False)
    for k in range(1, lats):
        sent = lax.dynamic_index_in_dim(parts, band ^ k, 0, False).astype(BF16)
        total = total + lax.ppermute(sent, "lat", [(i, i ^ k) for i in range(lats)]).astype(F32)
    groups = [[2 * i + k for i in range(depths)] for k in range(2)]
    line = lax.all_to_all(total.reshape(depths, piece, c1).astype(BF16), "lon", 0, 0,
                          axis_index_groups=groups, tiled=True)
    total = jnp.sum(line.astype(F32), 0).astype(BF16)
    line = lax.all_to_all(jnp.broadcast_to(total[None], line.shape), "lon", 0, 0,
                          axis_index_groups=groups, tiled=True)
    every = [line] + [lax.ppermute(line, "lat", [(i, i ^ k) for i in range(lats)]) for k in range(1, lats)]
    mine = jnp.stack(every, 0)
    theirs = lax.ppermute(mine, "lon", swap)

    grad_inputs = pl.pallas_call(
        last_kernel,
        out_shape=shape((rows, c0, cols), BF16),
        in_specs=vmem(2),
        out_specs=vmem(1)[0],
        scratch_shapes=[
            pltpu.VMEM((2 * c0, rows * half), F32),
            pltpu.VMEM((pooled, c0, 2 * cols), BF16),
        ],
        compiler_params=params(),
        cost_estimate=pl.CostEstimate(flops=2 * rows * cols * c1 * 9 * c0, bytes_accessed=3 << 20, transcendentals=0),
    )(spread, taps_first)

    grad_w_first, grad_w_second = pl.pallas_call(
        gather_kernel,
        out_shape=(shape((9 * c0, c1), F32), shape((9 * c1, c1), F32)),
        in_specs=[pl.BlockSpec(memory_space=pltpu.SMEM)] + vmem(2),
        out_specs=tuple(vmem(2)),
        compiler_params=params(),
        cost_estimate=pl.CostEstimate(flops=1000, bytes_accessed=3 << 19, transcendentals=0),
    )(flags, mine, theirs)
    return (jnp.transpose(grad_inputs, (0, 2, 1)), grad_w_first.reshape(w_first.shape),
            grad_w_second.reshape(w_second.shape))


def solution(mesh):
    in_specs = (P("lat", "lon", None), P("lat", "lon", None), P("lat", "lon", None), P(), P())
    out_specs = (P("lat", "lon", None), P(), P())
    return jax.shard_map(body, mesh=mesh, in_specs=in_specs, out_specs=out_specs, check_vma=False)
```

time: 70 us -> 64.4 us (0.920)
  blocking collectives: 39.5 us -> 18.7 us
  waiting for transfers between devices: 1.94 us -> 12.3 us
  starting transfers between devices: 12.2 us -> 17.6 us
  Pallas kernels: 7.28 us -> 8.25 us
  other arithmetic: 1.09 us -> 0.25 us
    all_to_all x2, blocking collectives: 39.5 us -> 18.7 us  [the longest x1 10.6 us: body(): lax.all_to_all(total.reshape(depths, piece, c1).astype(BF16), 'lon', 0, 0...]
    ppermute x4 -> x10, waiting for transfers between devices: 1.81 us -> 12 us  [the longest x1 4.22 us: body(): bottom = lax.ppermute(head, 'lat', [(i + 1, i) for i in range(lats - 1)])]
    ppermute x4 -> x10, starting transfers between devices: 4.96 us -> 10.2 us  [the longest x3 3.57 us: body(): lax.ppermute(sent, 'lat', [(i, i ^ k) for i in range(lats)]).astype(F32)]
    unnamed x14, local copies, waits for them, and re-layouts: 2.17 us -> 5.81 us
    slice x5 -> x4, local copies, waits for them, and re-layouts: 2.29 us -> 0.02 us  [the longest x1 0.01 us: column(): top[g:g + 1]]
    squeeze x2 -> x0, local copies, waits for them, and re-layouts: 1.6 us -> none  [body(): tail = jnp.concatenate([pre_first[-1], grad_out[-1]], 0)]
    pallas_call x2 -> x4, Pallas kernels: 6.05 us -> 7.01 us  [the longest x1 3.24 us: body(): pl.pallas_call(middle_kernel, out_shape=(shape((rows + 3, half, 4 * c1),...]
    concatenate x3 -> x0, other arithmetic: 0.86 us -> none  [the longest x1 0.85 us: body(): both = jnp.concatenate([low, high], 0)]
  transfers between devices with their start and end apart: 7 -> 13, of which waited for: 2 -> 8; matrix products, arithmetic and copies ran while one was open for 6% -> 0% of each run, Pallas kernels for 6% -> 5%
where the time goes in v2:
time: 64.4 us; the launch traced here: 64 us
  blocking collectives  18.7 us (29%)
  starting transfers between devices  17.6 us (27%)
  waiting for transfers between devices  12.3 us (19%)
  Pallas kernels  8.25 us (13%)
  local copies, waits for them, and re-layouts  5.97 us (9%)
  between operations  0.82 us (1%)
    all_to_all x1, blocking collectives, body(): lax.all_to_all(total.reshape(depths, piece, c1).astype(BF16), 'lon', 0, 0...  10.6 us
    all_to_all x1, blocking collectives, body(): lax.all_to_all(jnp.broadcast_to(total[None], line.shape), 'lon', 0, 0, ax...  8.11 us
    ppermute x1, starting transfers between devices, body(): lax.ppermute(head, AREA, [(i, (i + lons // 2) % lons) for i in range(lons)])  6.07 us
    unnamed x14, local copies, waits for them, and re-layouts  5.81 us
    ppermute x1, waiting for transfers between devices, body(): bottom = lax.ppermute(head, 'lat', [(i + 1, i) for i in range(lats - 1)])  4.22 us
    ppermute x3, starting transfers between devices, body(): lax.ppermute(sent, 'lat', [(i, i ^ k) for i in range(lats)]).astype(F32)  3.57 us
    ppermute x3, starting transfers between devices, body(): lax.ppermute(line, 'lat', [(i, i ^ k) for i in range(lats)])  3.49 us
    ppermute x3, waiting for transfers between devices, body(): lax.ppermute(line, 'lat', [(i, i ^ k) for i in range(lats)])  3.27 us
  transfers between devices with their start and end apart: 13, of which 8 were waited for; matrix products, arithmetic and copies ran while one was open for 0% of the time, Pallas kernels for 5%

profile of v2, /device:TPU:0, one launch (start us, length us, event | category | flops | bytes accessed | tf_op | source)
XLA Modules:
  0.0 64.0 jit_solution(392795091317424804)
XLA Ops:
  0.6 0.0 copy-start
  0.6 1.0 %copy-done = bf16[16,128,128]{2,1,0:T(8,128)(2,1)S(1)} copy-done((bf16[16,128,128]{2,1,0:T(8,128)(2,1)S(1)}, bf16[16,128,128]{2,1,0:T(8,128)(2,1)}, u32[]{:S(2)}) %copy-start) | copy-done | bytes 524312
  1.7 0.0 copy-start.5
  1.7 0.9 %copy-done.5 = bf16[8,64,128]{2,1,0:T(8,128)(2,1)S(1)} copy-done((bf16[8,64,128]{2,1,0:T(8,128)(2,1)S(1)}, bf16[8,64,128]{2,1,0:T(8,128)(2,1)}, u32[]{:S(2)}) %copy-start.5) | copy-done | bytes 131096
  2.6 0.0 copy-start.6
  2.6 6.1 %collective-permute-start = (bf16[192,128]{1,0:T(8,128)(2,1)S(1)}, bf16[192,128]{1,0:T(8,128)(2,1)S(1)}, u32[]{:S(2)}, u32[]{:S(2)}) collective-permute-start(bf16[192,128]{1,0:T(8,128)(2,1)S(1)} %get-tuple-element.17), channel_id=1, source_target_pairs={{0,4},{1,5},{2,6},{3,7},{4,0},{5,1},{6,2},{7,3}} | collective-permute-start | bytes 147464 | tf_op jit(solution)/shard_map/ppermute | solution.py:304
  8.7 1.3 %collective-permute-start.1 = (bf16[192,128]{1,0:T(8,128)(2,1)S(1)}, bf16[192,128]{1,0:T(8,128)(2,1)S(1)}, u32[]{:S(2)}, u32[]{:S(2)}) collective-permute-start(bf16[192,128]{1,0:T(8,128)(2,1)S(1)} %get-tuple-element.18), channel_id=1, source_target_pairs={{0,8},{8,16},{16,24},{1,9},{9,17},{17,25},{2,10},{10,18},{18,26},{... | collective-permute-start | bytes 147464 | tf_op jit(solution)/shard_map/ppermute | solution.py:303
  10.0 1.3 %collective-permute-start.2 = (bf16[192,128]{1,0:T(8,128)(2,1)S(1)}, bf16[192,128]{1,0:T(8,128)(2,1)S(1)}, u32[]{:S(2)}, u32[]{:S(2)}) collective-permute-start(bf16[192,128]{1,0:T(8,128)(2,1)S(1)} %get-tuple-element.17), channel_id=1, source_target_pairs={{8,0},{16,8},{24,16},{9,1},{17,9},{25,17},{10,2},{18,10},{26,18},{... | collective-permute-start | bytes 147464 | tf_op jit(solution)/shard_map/ppermute | solution.py:305
  11.3 0.0 collective-permute-done
  11.3 0.4 collective-permute-done.1
  11.8 4.2 %collective-permute-done.2.bottom = bf16[192,128]{1,0:T(8,128)(2,1)S(1)} collective-permute-done((bf16[192,128]{1,0:T(8,128)(2,1)S(1)}, bf16[192,128]{1,0:T(8,128)(2,1)S(1)}, u32[]{:S(2)}, u32[]{:S(2)}) %collective-permute-start.2) | collective-permute-done | bytes 49184 | tf_op jit(solution)/shard_map/ppermute | solution.py:305
  16.0 0.0 collective-permute-start.4
  16.1 0.5 collective-permute-start.3
  16.7 0.1 pad_add_fusion.flags
  16.8 0.0 copy-start.1
  16.8 1.0 %copy-done.1 = bf16[16,128,128]{2,1,0:T(8,128)(2,1)S(1)} copy-done((bf16[16,128,128]{2,1,0:T(8,128)(2,1)S(1)}, bf16[16,128,128]{2,1,0:T(8,128)(2,1)}, u32[]{:S(2)}) %copy-start.1) | copy-done | bytes 524312
  17.8 0.0 copy-start.2
  17.8 1.0 %copy-done.2 = bf16[3,3,128,128]{3,2,1,0:T(8,128)(2,1)S(1)} copy-done((bf16[3,3,128,128]{3,2,1,0:T(8,128)(2,1)S(1)}, bf16[3,3,128,128]{3,2,1,0:T(8,128)(2,1)}, u32[]{:S(2)}) %copy-start.2) | copy-done | bytes 294936
  18.8 0.0 copy-start.3
  18.8 0.9 %copy-done.3 = bf16[16,128,64]{1,2,0:T(8,128)(2,1)S(1)} copy-done((bf16[16,128,64]{1,2,0:T(8,128)(2,1)S(1)}, bf16[16,128,64]{1,2,0:T(8,128)(2,1)}, u32[]{:S(2)}) %copy-start.3) | copy-done | bytes 262168
  19.7 0.0 copy-start.4
  19.7 0.9 %copy-done.4 = bf16[3,3,64,128]{3,2,1,0:T(8,128)(2,1)S(1)} copy-done((bf16[3,3,64,128]{3,2,1,0:T(8,128)(2,1)S(1)}, bf16[3,3,64,128]{3,2,1,0:T(8,128)(2,1)}, u32[]{:S(2)}) %copy-start.4) | copy-done | bytes 147480
  20.6 1.2 %shard_map.77 = (f32[16,64,256]{2,1,0:T(8,128)S(1)}, bf16[2,256,512]{2,1,0:T(8,128)(2,1)S(1)}, bf16[128,1024]{1,0:T(8,128)(2,1)S(1)}, bf16[384,512]{1,0:T(8,128)(2,1)S(1)}, bf16[3,256,512]{2,1,0:T(8,128)(2,1)S(1)}) custom-call(bf16[16,128,128]{2,1,0:T(8,128)(2,1)S(1)} %copy-done.1, bf16[16,64,128]{2,1,0:T(8,128)(2,1)S(1)} %bitcast.28, ...), custom_call_target="tpu_custom_call" | custom-call | flops 15728640 | bytes 6291456 | tf_op jit(solution)/shard_map/pallas_call | solution.py:308
  21.9 0.0 collective-permute-done.4.right
  21.9 0.0 collective-permute-done.3.left
  21.9 0.0 copy-done.6
  21.9 3.2 %shard_map.78 = (bf16[19,64,512]{2,1,0:T(8,128)(2,1)S(1)}, f32[1024,128]{1,0:T(8,128)S(1)}, f32[1024,128]{1,0:T(8,128)S(1)}) custom-call(s32[4]{0:T(128)S(1)} %pad_add_fusion.flags, bf16[8,64,128]{2,1,0:T(8,128)(2,1)S(1)} %copy-done.6, bf16[192,128]{1,0:T(8,128)(2,1)S(1)} %broadcast_select_fusion.top, bf16[192,128]{1,0:T(8,128)(2,1)S(1)} %collective-permute-done.2.bottom, ...), custom_call_target="tpu_custom_call" | custom-call | flops 1509949440 | bytes 8388608 | tf_op jit(solution)/shard_map/pallas_call | solution.py:342
  25.1 1.3 %collective-permute-start.5 = (f32[1024,128]{1,0:T(8,128)S(1)}, f32[1024,128]{1,0:T(8,128)S(1)}, u32[]{:S(2)}, u32[]{:S(2)}) collective-permute-start(f32[1024,128]{1,0:T(8,128)S(1)} %get-tuple-element.28), channel_id=1, source_target_pairs={{0,1},{1,0},{2,3},{3,2},{4,5},{5,4},{6,7},{7,6},{8,9},{9,8},{10,11... | collective-permute-start | bytes 1572872 | tf_op jit(solution)/shard_map/ppermute | solution.py:369
  26.4 1.5 %collective-permute-done.5 = f32[1024,128]{1,0:T(8,128)S(1)} collective-permute-done((f32[1024,128]{1,0:T(8,128)S(1)}, f32[1024,128]{1,0:T(8,128)S(1)}, u32[]{:S(2)}, u32[]{:S(2)}) %collective-permute-start.5) | collective-permute-done | bytes 524320 | tf_op jit(solution)/shard_map/ppermute | solution.py:369
  27.9 0.1 add.25
  28.1 1.0 %collective-permute-start.6 = (bf16[256,128]{1,0:T(8,128)(2,1)S(1)}, bf16[256,128]{1,0:T(8,128)(2,1)S(1)}, u32[]{:S(2)}, u32[]{:S(2)}) collective-permute-start(bf16[256,128]{1,0:T(8,128)(2,1)S(1)} %get-tuple-element.31), channel_id=1, source_target_pairs={{0,8},{8,0},{16,24},{24,16},{1,9},{9,1},{17,25},{25,17},{2,10},{10... | collective-permute-start | bytes 196616 | tf_op jit(solution)/shard_map/ppermute | solution.py:373
  29.1 0.0 collective-permute-start.7
  29.1 2.5 %collective-permute-start.8 = (bf16[256,128]{1,0:T(8,128)(2,1)S(1)}, bf16[256,128]{1,0:T(8,128)(2,1)S(1)}, u32[]{:S(2)}, u32[]{:S(2)}) collective-permute-start(bf16[256,128]{1,0:T(8,128)(2,1)S(1)} %get-tuple-element.32), channel_id=1, source_target_pairs={{0,24},{8,16},{16,8},{24,0},{1,25},{9,17},{17,9},{25,1},{2,26},{10... | collective-permute-start | bytes 196616 | tf_op jit(solution)/shard_map/ppermute | solution.py:373
  31.6 0.9 %collective-permute-done.6 = bf16[256,128]{1,0:T(8,128)(2,1)S(1)} collective-permute-done((bf16[256,128]{1,0:T(8,128)(2,1)S(1)}, bf16[256,128]{1,0:T(8,128)(2,1)S(1)}, u32[]{:S(2)}, u32[]{:S(2)}) %collective-permute-start.6) | collective-permute-done | bytes 65568 | tf_op jit(solution)/shard_map/ppermute | solution.py:373
  32.5 2.0 %collective-permute-done.7 = bf16[256,128]{1,0:T(8,128)(2,1)S(1)} collective-permute-done((bf16[256,128]{1,0:T(8,128)(2,1)S(1)}, bf16[256,128]{1,0:T(8,128)(2,1)S(1)}, u32[]{:S(2)}, u32[]{:S(2)}) %collective-permute-start.7) | collective-permute-done | bytes 65568 | tf_op jit(solution)/shard_map/ppermute | solution.py:373
  34.6 0.0 collective-permute-done.8
  34.6 10.6 %all_to_all.10 = bf16[4,64,128]{2,1,0:T(8,128)(2,1)S(1)} all-to-all(bf16[4,64,128]{2,1,0:T(8,128)(2,1)S(1)} %bitcast.31), channel_id=1, replica_groups={{0,2,4,6},{1,3,5,7},{8,10,12,14},{9,11,13,15},{16,18,20,22},{17,19,21,2..., dimensions={0} | all-to-all | bytes 131072 | tf_op jit(solution)/shard_map/all_to_all | solution.py:375
  45.2 8.1 %all_to_all.11 = bf16[4,64,128]{2,1,0:T(8,128)(2,1)S(1)} all-to-all(bf16[4,64,128]{2,1,0:T(8,128)(2,1)S(1)} %broadcast_in_dim.2), channel_id=1, replica_groups={{0,2,4,6},{1,3,5,7},{8,10,12,14},{9,11,13,15},{16,18,20,22},{17,19,21,2..., dimensions={0} | all-to-all | bytes 131072 | tf_op jit(solution)/shard_map/all_to_all | solution.py:378
  53.3 0.6 %collective-permute-start.9 = (bf16[4,64,128]{2,1,0:T(8,128)(2,1)S(1)}, bf16[4,64,128]{2,1,0:T(8,128)(2,1)S(1)}, u32[]{:S(2)}, u32[]{:S(2)}) collective-permute-start(bf16[4,64,128]{2,1,0:T(8,128)(2,1)S(1)} %all_to_all.11), channel_id=1, source_target_pairs={{0,8},{8,0},{16,24},{24,16},{1,9},{9,1},{17,25},{25,17},{2,10},{10... | collective-permute-start | bytes 196616 | tf_op jit(solution)/shard_map/ppermute | solution.py:380
  54.0 0.9 %collective-permute-start.10 = (bf16[4,64,128]{2,1,0:T(8,128)(2,1)S(1)}, bf16[4,64,128]{2,1,0:T(8,128)(2,1)S(1)}, u32[]{:S(2)}, u32[]{:S(2)}) collective-permute-start(bf16[4,64,128]{2,1,0:T(8,128)(2,1)S(1)} %all_to_all.11), channel_id=1, source_target_pairs={{0,16},{8,24},{16,0},{24,8},{1,17},{9,25},{17,1},{25,9},{2,18},{10... | collective-permute-start | bytes 196616 | tf_op jit(solution)/shard_map/ppermute | solution.py:380
  54.9 1.9 %collective-permute-start.11 = (bf16[4,64,128]{2,1,0:T(8,128)(2,1)S(1)}, bf16[4,64,128]{2,1,0:T(8,128)(2,1)S(1)}, u32[]{:S(2)}, u32[]{:S(2)}) collective-permute-start(bf16[4,64,128]{2,1,0:T(8,128)(2,1)S(1)} %all_to_all.11), channel_id=1, source_target_pairs={{0,24},{8,16},{16,8},{24,0},{1,25},{9,17},{17,9},{25,1},{2,26},{10... | collective-permute-start | bytes 196616 | tf_op jit(solution)/shard_map/ppermute | solution.py:380
  56.8 0.8 %collective-permute-done.9 = bf16[4,64,128]{2,1,0:T(8,128)(2,1)S(1)} collective-permute-done((bf16[4,64,128]{2,1,0:T(8,128)(2,1)S(1)}, bf16[4,64,128]{2,1,0:T(8,128)(2,1)S(1)}, u32[]{:S(2)}, u32[]{:S(2)}) %collective-permute-start.9) | collective-permute-done | bytes 65568 | tf_op jit(solution)/shard_map/ppermute | solution.py:380
  57.6 0.6 %collective-permute-done.10 = bf16[4,64,128]{2,1,0:T(8,128)(2,1)S(1)} collective-permute-done((bf16[4,64,128]{2,1,0:T(8,128)(2,1)S(1)}, bf16[4,64,128]{2,1,0:T(8,128)(2,1)S(1)}, u32[]{:S(2)}, u32[]{:S(2)}) %collective-permute-start.10) | collective-permute-done | bytes 65568 | tf_op jit(solution)/shard_map/ppermute | solution.py:380
  58.2 1.8 %collective-permute-done.11 = bf16[4,64,128]{2,1,0:T(8,128)(2,1)S(1)} collective-permute-done((bf16[4,64,128]{2,1,0:T(8,128)(2,1)S(1)}, bf16[4,64,128]{2,1,0:T(8,128)(2,1)S(1)}, u32[]{:S(2)}, u32[]{:S(2)}) %collective-permute-start.11) | collective-permute-done | bytes 65568 | tf_op jit(solution)/shard_map/ppermute | solution.py:380
  60.1 0.1 collective-permute-start.12
  60.2 2.2 %shard_map.79 = bf16[16,64,128]{2,1,0:T(8,128)(2,1)} custom-call(bf16[19,64,512]{2,1,0:T(8,128)(2,1)S(1)} %get-tuple-element.25.spread, bf16[384,512]{1,0:T(8,128)(2,1)S(1)} %get-tuple-element.26.taps), custom_call_target="tpu_custom_call" | custom-call | flops 301989888 | bytes 3145728 | tf_op jit(solution)/shard_map/pallas_call | solution.py:384
  62.4 0.0 collective-permute-done.12.theirs
  62.4 1.6 %shard_map.80 = (f32[576,128]{1,0:T(8,128)}, f32[1152,128]{1,0:T(8,128)}) custom-call(s32[4]{0:T(128)S(1)} %pad_add_fusion.flags, bf16[4,4,64,128]{3,2,1,0:T(8,128)(2,1)S(1)} %pad_maximum_fusion.mine, bf16[4,4,64,128]{3,2,1,0:T(8,128)(2,1)S(1)} %collective-permute-done.12.theirs), custom_call_target="tpu_custom_call" | custom-call | flops 1000 | bytes 1572864 | tf_op jit(solution)/shard_map/pallas_call | solution.py:397
  (14 shorter events, 0.3 us)
Async XLA Ops:
  0.6 1.0 %copy-start = (bf16[16,128,128]{2,1,0:T(8,128)(2,1)S(1)}, bf16[16,128,128]{2,1,0:T(8,128)(2,1)}, u32[]{:S(2)}) copy-start(bf16[16,128,128]{2,1,0:T(8,128)(2,1)} %pre.3) | copy-start | bytes 1572868
  1.7 0.9 %copy-start.5 = (bf16[8,64,128]{2,1,0:T(8,128)(2,1)S(1)}, bf16[8,64,128]{2,1,0:T(8,128)(2,1)}, u32[]{:S(2)}) copy-start(bf16[8,64,128]{2,1,0:T(8,128)(2,1)} %grad_out.3) | copy-start | bytes 393220
  2.6 19.3 %copy-start.6 = (bf16[8,64,128]{2,1,0:T(8,128)(2,1)S(1)}, bf16[8,64,128]{2,1,0:T(8,128)(2,1)}, u32[]{:S(2)}) copy-start(bf16[8,64,128]{2,1,0:T(8,128)(2,1)} %grad_out.3) | copy-start | bytes 393220
  2.6 8.7 %collective-permute-start = (bf16[192,128]{1,0:T(8,128)(2,1)S(1)}, bf16[192,128]{1,0:T(8,128)(2,1)S(1)}, u32[]{:S(2)}, u32[]{:S(2)}) collective-permute-start(bf16[192,128]{1,0:T(8,128)(2,1)S(1)} %get-tuple-element.17), channel_id=1, source_target_pairs={{0,4},{1,5},{2,6},{3,7},{4,0},{5,1},{6,2},{7,3}} | collective-permute-start | bytes 147464 | tf_op jit(solution)/shard_map/ppermute | solution.py:304
  8.7 3.0 %collective-permute-start.1 = (bf16[192,128]{1,0:T(8,128)(2,1)S(1)}, bf16[192,128]{1,0:T(8,128)(2,1)S(1)}, u32[]{:S(2)}, u32[]{:S(2)}) collective-permute-start(bf16[192,128]{1,0:T(8,128)(2,1)S(1)} %get-tuple-element.18), channel_id=1, source_target_pairs={{0,8},{8,16},{16,24},{1,9},{9,17},{17,25},{2,10},{10,18},{18,26},{... | collective-permute-start | bytes 147464 | tf_op jit(solution)/shard_map/ppermute | solution.py:303
  10.0 6.0 %collective-permute-start.2 = (bf16[192,128]{1,0:T(8,128)(2,1)S(1)}, bf16[192,128]{1,0:T(8,128)(2,1)S(1)}, u32[]{:S(2)}, u32[]{:S(2)}) collective-permute-start(bf16[192,128]{1,0:T(8,128)(2,1)S(1)} %get-tuple-element.17), channel_id=1, source_target_pairs={{8,0},{16,8},{24,16},{9,1},{17,9},{25,17},{10,2},{18,10},{26,18},{... | collective-permute-start | bytes 147464 | tf_op jit(solution)/shard_map/ppermute | solution.py:305
  16.0 5.8 %collective-permute-start.4 = (bf16[32,128]{1,0:T(8,128)(2,1)S(1)}, bf16[32,128]{1,0:T(8,128)(2,1)S(1)}, u32[]{:S(2)}, u32[]{:S(2)}) collective-permute-start(bf16[32,128]{1,0:T(8,128)(2,1)S(1)} %concatenate.7), channel_id=1, source_target_pairs={{0,7},{1,0},{2,1},{3,2},{4,3},{5,4},{6,5},{7,6},{8,15},{9,8},{10,9... | collective-permute-start | bytes 24584 | tf_op jit(solution)/shard_map/ppermute | solution.py:335
  16.1 5.7 %collective-permute-start.3 = (bf16[32,128]{1,0:T(8,128)(2,1)S(1)}, bf16[32,128]{1,0:T(8,128)(2,1)S(1)}, u32[]{:S(2)}, u32[]{:S(2)}) collective-permute-start(bf16[32,128]{1,0:T(8,128)(2,1)S(1)} %concatenate.6), channel_id=1, source_target_pairs={{0,1},{1,2},{2,3},{3,4},{4,5},{5,6},{6,7},{7,0},{8,9},{9,10},{10,1... | collective-permute-start | bytes 24584 | tf_op jit(solution)/shard_map/ppermute | solution.py:334
  16.8 1.0 %copy-start.1 = (bf16[16,128,128]{2,1,0:T(8,128)(2,1)S(1)}, bf16[16,128,128]{2,1,0:T(8,128)(2,1)}, u32[]{:S(2)}) copy-start(bf16[16,128,128]{2,1,0:T(8,128)(2,1)} %pre.3) | copy-start | bytes 1572868
  17.8 1.0 %copy-start.2 = (bf16[3,3,128,128]{3,2,1,0:T(8,128)(2,1)S(1)}, bf16[3,3,128,128]{3,2,1,0:T(8,128)(2,1)}, u32[]{:S(2)}) copy-start(bf16[3,3,128,128]{3,2,1,0:T(8,128)(2,1)} %w_second.1) | copy-start | bytes 884740
  18.8 0.9 %copy-start.3 = (bf16[16,128,64]{1,2,0:T(8,128)(2,1)S(1)}, bf16[16,128,64]{1,2,0:T(8,128)(2,1)}, u32[]{:S(2)}) copy-start(bf16[16,128,64]{1,2,0:T(8,128)(2,1)} %param.5) | copy-start | bytes 786436
  19.7 0.9 %copy-start.4 = (bf16[3,3,64,128]{3,2,1,0:T(8,128)(2,1)S(1)}, bf16[3,3,64,128]{3,2,1,0:T(8,128)(2,1)}, u32[]{:S(2)}) copy-start(bf16[3,3,64,128]{3,2,1,0:T(8,128)(2,1)} %w_first.1) | copy-start | bytes 442372
  25.1 2.8 %collective-permute-start.5 = (f32[1024,128]{1,0:T(8,128)S(1)}, f32[1024,128]{1,0:T(8,128)S(1)}, u32[]{:S(2)}, u32[]{:S(2)}) collective-permute-start(f32[1024,128]{1,0:T(8,128)S(1)} %get-tuple-element.28), channel_id=1, source_target_pairs={{0,1},{1,0},{2,3},{3,2},{4,5},{5,4},{6,7},{7,6},{8,9},{9,8},{10,11... | collective-permute-start | bytes 1572872 | tf_op jit(solution)/shard_map/ppermute | solution.py:369
  28.1 4.4 %collective-permute-start.6 = (bf16[256,128]{1,0:T(8,128)(2,1)S(1)}, bf16[256,128]{1,0:T(8,128)(2,1)S(1)}, u32[]{:S(2)}, u32[]{:S(2)}) collective-permute-start(bf16[256,128]{1,0:T(8,128)(2,1)S(1)} %get-tuple-element.31), channel_id=1, source_target_pairs={{0,8},{8,0},{16,24},{24,16},{1,9},{9,1},{17,25},{25,17},{2,10},{10... | collective-permute-start | bytes 196616 | tf_op jit(solution)/shard_map/ppermute | solution.py:373
  29.1 5.5 %collective-permute-start.7 = (bf16[256,128]{1,0:T(8,128)(2,1)S(1)}, bf16[256,128]{1,0:T(8,128)(2,1)S(1)}, u32[]{:S(2)}, u32[]{:S(2)}) collective-permute-start(bf16[256,128]{1,0:T(8,128)(2,1)S(1)} %get-tuple-element.33), channel_id=1, source_target_pairs={{0,16},{8,24},{16,0},{24,8},{1,17},{9,25},{17,1},{25,9},{2,18},{10... | collective-permute-start | bytes 196616 | tf_op jit(solution)/shard_map/ppermute | solution.py:373
  29.1 5.5 %collective-permute-start.8 = (bf16[256,128]{1,0:T(8,128)(2,1)S(1)}, bf16[256,128]{1,0:T(8,128)(2,1)S(1)}, u32[]{:S(2)}, u32[]{:S(2)}) collective-permute-start(bf16[256,128]{1,0:T(8,128)(2,1)S(1)} %get-tuple-element.32), channel_id=1, source_target_pairs={{0,24},{8,16},{16,8},{24,0},{1,25},{9,17},{17,9},{25,1},{2,26},{10... | collective-permute-start | bytes 196616 | tf_op jit(solution)/shard_map/ppermute | solution.py:373
  53.3 4.3 %collective-permute-start.9 = (bf16[4,64,128]{2,1,0:T(8,128)(2,1)S(1)}, bf16[4,64,128]{2,1,0:T(8,128)(2,1)S(1)}, u32[]{:S(2)}, u32[]{:S(2)}) collective-permute-start(bf16[4,64,128]{2,1,0:T(8,128)(2,1)S(1)} %all_to_all.11), channel_id=1, source_target_pairs={{0,8},{8,0},{16,24},{24,16},{1,9},{9,1},{17,25},{25,17},{2,10},{10... | collective-permute-start | bytes 196616 | tf_op jit(solution)/shard_map/ppermute | solution.py:380
  54.0 4.3 %collective-permute-start.10 = (bf16[4,64,128]{2,1,0:T(8,128)(2,1)S(1)}, bf16[4,64,128]{2,1,0:T(8,128)(2,1)S(1)}, u32[]{:S(2)}, u32[]{:S(2)}) collective-permute-start(bf16[4,64,128]{2,1,0:T(8,128)(2,1)S(1)} %all_to_all.11), channel_id=1, source_target_pairs={{0,16},{8,24},{16,0},{24,8},{1,17},{9,25},{17,1},{25,9},{2,18},{10... | collective-permute-start | bytes 196616 | tf_op jit(solution)/shard_map/ppermute | solution.py:380
  54.9 5.2 %collective-permute-start.11 = (bf16[4,64,128]{2,1,0:T(8,128)(2,1)S(1)}, bf16[4,64,128]{2,1,0:T(8,128)(2,1)S(1)}, u32[]{:S(2)}, u32[]{:S(2)}) collective-permute-start(bf16[4,64,128]{2,1,0:T(8,128)(2,1)S(1)} %all_to_all.11), channel_id=1, source_target_pairs={{0,24},{8,16},{16,8},{24,0},{1,25},{9,17},{17,9},{25,1},{2,26},{10... | collective-permute-start | bytes 196616 | tf_op jit(solution)/shard_map/ppermute | solution.py:380
  60.1 2.3 %collective-permute-start.12 = (bf16[4,4,64,128]{3,2,1,0:T(8,128)(2,1)S(1)}, bf16[4,4,64,128]{3,2,1,0:T(8,128)(2,1)S(1)}, u32[]{:S(2)}, u32[]{:S(2)}) collective-permute-start(bf16[4,4,64,128]{3,2,1,0:T(8,128)(2,1)S(1)} %pad_maximum_fusion.mine), channel_id=1, source_target_pairs={{0,1},{1,0},{2,3},{3,2},{4,5},{5,4},{6,7},{7,6},{8,9},{9,8},{10,11... | collective-permute-start | bytes 786440 | tf_op jit(solution)/shard_map/ppermute | solution.py:382

commit v3 on v2

--- a/solution.py
+++ b/solution.py
@@ -1,3 +1,5 @@
+import functools
+
 import jax
 import jax.numpy as jnp
 from jax import lax
@@ -51,10 +53,8 @@
     return jnp.where(where, 1.0, 0.0).astype(BF16)
 
 
-def local_kernel(pre, fields, w_first, w_second, slope, act_t, fields_t, taps_first, taps_second,
-                 line, act_s, turned):
+def local_kernel(pre, slope, act_t, line, act_s):
     rows, cols, c1 = pre.shape
-    c0 = fields.shape[1]
     half = cols // 2
 
     def one_row(r, carry):
@@ -69,6 +69,12 @@
     lax.fori_loop(0, rows, one_row, 0)
     for pr in range(2):
         act_t[pr] = act_s[pr].reshape(rows // 2 * half, 2 * c1).T
+
+
+def layout_kernel(fields, w_first, w_second, fields_t, taps_first, taps_second, turned):
+    rows, c0, cols = fields.shape
+    c1 = w_first.shape[3]
+    half = cols // 2
     col = lax.broadcasted_iota(jnp.int32, (cols, 2 * cols), 0)
     lane = lax.broadcasted_iota(jnp.int32, (cols, 2 * cols), 1)
     turn = lane // cols
@@ -94,7 +100,16 @@
                     taps_first[start:start + c0, k * c1:(k + 1) * c1] = w_first[a, b]
 
 
-def middle_kernel(flags, grad_out, top, bottom, left, right, slope, act_t, fields_t, taps,
+def steps(count, core):
+    bits = count.bit_length() - 1
+    return [1 << ((t + core) % bits) for t in range(bits)]
+
+
+def distance(index, masks):
+    return sum(m for t, m in enumerate(masks) if (index >> (len(masks) - 1 - t)) & 1)
+
+
+def middle_kernel(lats, flags, grad_out, top, bottom, left, right, slope, act_t, fields_t, taps,
                   spread, own, other,
                   grid, wide, prods, ends, line, side, sides, sums, corner, keep):
     first, last, core = flags[0], flags[1], flags[2]
@@ -107,7 +122,8 @@
     grid[:, half:, :] = jnp.zeros((pooled + 2, EDGE, c1), F32)
     grid[1:pooled + 1, :half, :] = grad_out[...].astype(F32)
     grid[0, :half, :] = top[2 * half:, :].astype(F32)
-    grid[pooled + 1, :half, :] = bottom[2 * half:, :].astype(F32)
+    outside = jnp.where(last == 1, 0.0, 1.0)
+    grid[pooled + 1, :half, :] = bottom[2 * half:, :].astype(F32) * outside
     side[0] = left[...].astype(F32)
     side[1] = right[...].astype(F32)
     for i in range(pooled + 2):
@@ -116,8 +132,9 @@
             at = rows + pooled + 2
         if i == pooled + 1:
             at = rows + pooled + 3
-        grid[i, half:half + 1, :] = side[1, at:at + 1, :]
-        grid[i, half + EDGE - 1:half + EDGE, :] = side[0, at:at + 1, :]
+        kept = outside if i == pooled + 1 else 1.0
+        grid[i, half:half + 1, :] = side[1, at:at + 1, :] * kept
+        grid[i, half + EDGE - 1:half + EDGE, :] = side[0, at:at + 1, :] * kept
     for i in range(pooled + 2):
         here = grid[i]
         wide[i, :, :c1] = pltpu.roll(here, 1, 0).astype(BF16)
@@ -166,7 +183,6 @@
     lax.fori_loop(0, pooled - 1, pair, 0)
     final = prods[2, pooled - 1]
     place(rows, final + prods[1, pooled - 1] + ends[2], slope[rows - 1], rows - 1)
-    outside = jnp.where(last == 1, 0.0, 1.0)
     place(rows + 1, (final + ends[3] + ends[2]) * outside, halo_slope(bottom), rows + pooled + 1)
 
     is_first = jnp.where(first == 1, 1.0, 0.0).astype(BF16)
@@ -217,8 +233,14 @@
             odd = got[c0:, (3 - b) * c1:(4 - b) * c1]
             put(9 * per_tap + 3 * a + b, even + odd)
     keep[count * unit:] = jnp.zeros((2 * held - count * unit, c1), F32)
-    own[...] = keep[pl.ds(pl.multiple_of(core * held, held), held), :]
-    other[...] = keep[pl.ds(pl.multiple_of((1 - core) * held, held), held), :]
+    band = flags[3]
+    block = held // lats
+    orders = [steps(lats, k) for k in range(2)]
+    for index in range(lats):
+        far = [distance(index, masks) for masks in orders]
+        for target, half_of in ((own, core), (other, 1 - core)):
+            piece_at = half_of * lats + (band ^ jnp.where(half_of == 0, far[0], far[1]))
+            target[index * block:(index + 1) * block] = keep[pl.ds(pl.multiple_of(piece_at * block, block), block), :]
 
 
 def last_kernel(spread, taps, out, total, turned):
@@ -247,28 +269,30 @@
 
 def gather_kernel(flags, mine, theirs, out_first, out_second):
     band, core = flags[3], flags[2]
-    lats, count, rows, c1 = mine.shape
+    lats, rows, c1 = mine.shape
     size = out_second.shape[0]
     total = size + out_first.shape[0]
     for h in range(2):
+        masks = steps(lats, h)
         for i in range(lats):
-            for j in range(count):
-                at = ((h * lats + i) * count + j) * rows
-                if at < total:
-                    source = i ^ band
-                    piece = jnp.where(core == h, mine[source, j], theirs[source, j]).astype(F32)
-                    for out, base, end in ((out_second, 0, size), (out_first, size, total)):
-                        low, high = max(at, base), min(at + rows, end)
-                        if low < high:
-                            out[low - base:high - base] = piece[low - at:high - at]
+            at = (h * lats + i) * rows
+            far = i ^ band
+            source = 0
+            for m in masks:
+                source = 2 * source + (far // m) % 2
+            for out, base, end in ((out_second, 0, size), (out_first, size, total)):
+                low, high = max(at, base), min(at + rows, end)
+                if low < high:
+                    here, there = (x[source, low - at:high - at] for x in (mine, theirs))
+                    out[low - base:high - base] = jnp.where(core == h, here, there).astype(F32)
 
 
 def vmem(count):
     return [pl.BlockSpec(memory_space=pltpu.VMEM)] * count
 
 
-def params():
-    return pltpu.CompilerParams(vmem_limit_bytes=48 * 1024 * 1024)
+def params(mib):
+    return pltpu.CompilerParams(vmem_limit_bytes=mib * 1024 * 1024)
 
 
 def shape(dims, kind):
@@ -296,43 +320,59 @@
         ),
         in_specs=vmem(2),
         out_specs=tuple(vmem(4)),
-        scratch_shapes=[pltpu.VMEM((edge, c1), F32)],
-        compiler_params=params(),
+        scratch_shapes=[
+            pltpu.VMEM((edge, c1), F32),
+        ],
+        compiler_params=params(50),
         cost_estimate=pl.CostEstimate(flops=1000, bytes_accessed=1 << 18, transcendentals=0),
     )(pre_first, grad_out)
-    down = lax.ppermute(tail, "lat", [(i, i + 1) for i in range(lats - 1)])
     over = lax.ppermute(head, AREA, [(i, (i + lons // 2) % lons) for i in range(lons)])
-    bottom = lax.ppermute(head, "lat", [(i + 1, i) for i in range(lats - 1)])
-    top = jnp.where(band == 0, over, down)
-
-    slope, act_t, fields_t, taps_first, taps_second = pl.pallas_call(
+    down = lax.ppermute(tail, "lat", [(i, (i + 1) % lats) for i in range(lats)])
+    bottom = lax.ppermute(head, "lat", [(i, (i - 1) % lats) for i in range(lats)])
+
+    slope, act_t = pl.pallas_call(
         local_kernel,
         out_shape=(
             shape((rows, half, 2 * c1), F32),
             shape((2, 2 * c1, pooled * half), BF16),
+        ),
+        in_specs=vmem(1),
+        out_specs=tuple(vmem(2)),
+        scratch_shapes=[
+            pltpu.VMEM((cols, c1), F32),
+            pltpu.VMEM((2, pooled, half, 2 * c1), BF16),
+        ],
+        compiler_params=params(16),
+        cost_estimate=pl.CostEstimate(flops=60 * rows * cols * c1, bytes_accessed=2 << 20,
+                                      transcendentals=2 * rows * cols * c1),
+    )(pre_first)
+
+    fields = jnp.transpose(inputs, (0, 2, 1))
+    over, down, bottom, slope, fields = lax.optimization_barrier((over, down, bottom, slope, fields))
+    top = jnp.where(band == 0, over, down)
+
+    def column(own_part, at):
+        p, g = at * (cols - 1), cols + at * (half - 1)
+        parts = [own_part[:rows + pooled], top[p:p + 1], bottom[p:p + 1], top[g:g + 1], bottom[g:g + 1]]
+        return jnp.concatenate(parts + [jnp.zeros((edge - rows - pooled - 4, c1), BF16)], 0)
+
+    left = lax.ppermute(column(last_col, 1), "lon", [(i, (i + 1) % lons) for i in range(lons)])
+    right = lax.ppermute(column(first_col, 0), "lon", [(i, (i - 1) % lons) for i in range(lons)])
+
+    fields_t, taps_first, taps_second = pl.pallas_call(
+        layout_kernel,
+        out_shape=(
             shape((2 * c0, rows * half), BF16),
             shape((6 * c0, 4 * c1), BF16),
             shape((3, 2 * c1, 4 * c1), BF16),
         ),
-        in_specs=vmem(4),
-        out_specs=tuple(vmem(5)),
-        scratch_shapes=[
-            pltpu.VMEM((cols, c1), F32),
-            pltpu.VMEM((2, pooled, half, 2 * c1), BF16),
-            pltpu.VMEM((rows, c0, 2 * cols), BF16),
-        ],
-        compiler_params=params(),
-        cost_estimate=pl.CostEstimate(flops=60 * rows * cols * c1, bytes_accessed=6 << 20,
-                                      transcendentals=2 * rows * cols * c1),
-    )(pre_first, jnp.transpose(inputs, (0, 2, 1)), w_first, w_second)
-
-    def column(own_part, at):
-        p, g = at * (cols - 1), cols + at * (half - 1)
-        parts = [own_part[:rows + pooled], top[p:p + 1], bottom[p:p + 1], top[g:g + 1], bottom[g:g + 1]]
-        return jnp.concatenate(parts + [jnp.zeros((edge - rows - pooled - 4, c1), BF16)], 0)
-
-    left = lax.ppermute(column(last_col, 1), "lon", [(i, (i + 1) % lons) for i in range(lons)])
-    right = lax.ppermute(column(first_col, 0), "lon", [(i, (i - 1) % lons) for i in range(lons)])
+        in_specs=vmem(3),
+        out_specs=tuple(vmem(3)),
+        scratch_shapes=[pltpu.VMEM((rows, c0, 2 * cols), BF16)],
+        compiler_params=params(16),
+        cost_estimate=pl.CostEstimate(flops=4 * rows * cols * c0 * cols, bytes_accessed=3 << 20, transcendentals=0),
+    )(fields, w_first, w_second)
+    left, right, fields_t = lax.optimization_barrier((left, right, fields_t))
 
     chips = lats * depths
     size = 9 * (c1 + c0)
@@ -340,7 +380,7 @@
     held = chips * piece
     span = half + EDGE
     spread, own, other = pl.pallas_call(
-        middle_kernel,
+        functools.partial(middle_kernel, lats),
         out_shape=(
             shape((rows + 3, half, 4 * c1), BF16),
             shape((held, c1), F32),
@@ -360,46 +400,57 @@
             pltpu.VMEM((2 * c1, 3 * c1), F32),
             pltpu.VMEM((2 * held, c1), F32),
         ],
-        compiler_params=params(),
+        compiler_params=params(16),
         cost_estimate=pl.CostEstimate(flops=2 * rows * cols * c1 * 9 * (2 * c1 + c0), bytes_accessed=8 << 20,
                                       transcendentals=0),
     )(flags, grad_out, top, bottom, left, right, slope, act_t, fields_t, taps_second)
 
     swap = [(i, i ^ 1) for i in range(lons)]
-    parts = (own + lax.ppermute(other, "lon", swap)).reshape(lats, depths * piece, c1)
-    total = lax.dynamic_index_in_dim(parts, band, 0, False)
-    for k in range(1, lats):
-        sent = lax.dynamic_index_in_dim(parts, band ^ k, 0, False).astype(BF16)
-        total = total + lax.ppermute(sent, "lat", [(i, i ^ k) for i in range(lats)]).astype(F32)
-    groups = [[2 * i + k for i in range(depths)] for k in range(2)]
-    line = lax.all_to_all(total.reshape(depths, piece, c1).astype(BF16), "lon", 0, 0,
-                          axis_index_groups=groups, tiled=True)
-    total = jnp.sum(line.astype(F32), 0).astype(BF16)
-    line = lax.all_to_all(jnp.broadcast_to(total[None], line.shape), "lon", 0, 0,
-                          axis_index_groups=groups, tiled=True)
-    every = [line] + [lax.ppermute(line, "lat", [(i, i ^ k) for i in range(lats)]) for k in range(1, lats)]
-    mine = jnp.stack(every, 0)
+    orders = [steps(lats, k) for k in range(2)]
+
+    def along_lat(t, block):
+        pairs = [(i * lons + j, (i ^ orders[j % 2][t]) * lons + j) for i in range(lats) for j in range(lons)]
+        return lax.ppermute(block, AREA, pairs)
+
+    total = (own + lax.ppermute(other, "lon", swap)).reshape(lats, held // lats, c1)
+    rounds = lats.bit_length() - 1
+    for t in range(rounds):
+        count = total.shape[0] // 2
+        sent = total[count:].astype(BF16)
+        if t == 0:
+            sent, spread = lax.optimization_barrier((sent, spread))
+        got = along_lat(t, sent)
+        if t == 0:
+            grad_inputs = pl.pallas_call(
+                last_kernel,
+                out_shape=shape((rows, c0, cols), BF16),
+                in_specs=vmem(2),
+                out_specs=vmem(1)[0],
+                scratch_shapes=[
+                    pltpu.VMEM((2 * c0, rows * half), F32),
+                    pltpu.VMEM((pooled, c0, 2 * cols), BF16),
+                ],
+                compiler_params=params(12),
+                cost_estimate=pl.CostEstimate(flops=2 * rows * cols * c1 * 9 * c0, bytes_accessed=3 << 20, transcendentals=0),
+            )(spread, taps_first)
+            got, grad_inputs = lax.optimization_barrier((got, grad_inputs))
+        total = total[:count] + got.astype(F32)
+    step = 2
+    while step < lons:
+        part = total.astype(BF16)
+        total = part.astype(F32) + lax.ppermute(part, "lon", [(i, i ^ step) for i in range(lons)]).astype(F32)
+        step *= 2
+    mine = total.astype(BF16)
+    for t in reversed(range(rounds)):
+        mine = jnp.concatenate([mine, along_lat(t, mine)], 0)
     theirs = lax.ppermute(mine, "lon", swap)
-
-    grad_inputs = pl.pallas_call(
-        last_kernel,
-        out_shape=shape((rows, c0, cols), BF16),
-        in_specs=vmem(2),
-        out_specs=vmem(1)[0],
-        scratch_shapes=[
-            pltpu.VMEM((2 * c0, rows * half), F32),
-            pltpu.VMEM((pooled, c0, 2 * cols), BF16),
-        ],
-        compiler_params=params(),
-        cost_estimate=pl.CostEstimate(flops=2 * rows * cols * c1 * 9 * c0, bytes_accessed=3 << 20, transcendentals=0),
-    )(spread, taps_first)
 
     grad_w_first, grad_w_second = pl.pallas_call(
         gather_kernel,
         out_shape=(shape((9 * c0, c1), F32), shape((9 * c1, c1), F32)),
         in_specs=[pl.BlockSpec(memory_space=pltpu.SMEM)] + vmem(2),
         out_specs=tuple(vmem(2)),
-        compiler_params=params(),
+        compiler_params=params(8),
         cost_estimate=pl.CostEstimate(flops=1000, bytes_accessed=3 << 19, transcendentals=0),
     )(flags, mine, theirs)
     return (jnp.transpose(grad_inputs, (0, 2, 1)), grad_w_first.reshape(w_first.shape),

time: 64.4 us -> 56.9 us (0.88)
  blocking collectives: 18.7 us -> 0 us
  waiting for transfers between devices: 12.3 us -> 26.5 us
  local copies, waits for them, and re-layouts: 5.97 us -> 3.15 us
    all_to_all x2 -> x0, blocking collectives: 18.7 us -> none  [the longest x1 10.6 us: body(): lax.all_to_all(total.reshape(depths, piece, c1).astype(BF16), 'lon', 0, 0...]
    ppermute x8, waiting for transfers between devices: 10.8 us -> 22.2 us  [the longest x4 16.2 us: along_lat(): return lax.ppermute(block, AREA, pairs)]
    ppermute x1, starting transfers between devices: 0.05 us -> 3.57 us  [body(): lax.ppermute(column(first_col, 0), 'lon', [(i, (i - 1) % lons) for i in r...]
    unnamed x14, local copies, waits for them, and re-layouts: 5.81 us -> 2.99 us
    ppermute x1, waiting for transfers between devices: 0.01 us -> 1.52 us  [body(): theirs = lax.ppermute(mine, 'lon', swap)]
    ppermute x1, starting transfers between devices: 1.26 us -> 0.08 us  [body(): lax.ppermute(other, 'lon', swap)]
    ppermute x1, starting transfers between devices: 6.07 us -> 4.9 us  [body(): lax.ppermute(head, AREA, [(i, (i + lons // 2) % lons) for i in range(lons)])]
    ppermute x8, starting transfers between devices: 9.64 us -> 8.72 us  [the longest x2 4.42 us: body(): lax.ppermute(part, 'lon', [(i, i ^ step) for i in range(lons)]).astype(F32)]
  transfers between devices with their start and end apart: 13 -> 13, of which waited for: 8 -> 11; matrix products, arithmetic and copies ran while one was open for 0% -> 0% of each run, Pallas kernels for 5% -> 6%
where the time goes in v3:
time: 56.9 us; the launch traced here: 56.7 us
  waiting for transfers between devices  26.5 us (47%)
  starting transfers between devices  17.4 us (31%)
  Pallas kernels  8.48 us (15%)
  local copies, waits for them, and re-layouts  3.15 us (6%)
  between operations  0.85 us (1%)
    ppermute x4, waiting for transfers between devices, along_lat(): return lax.ppermute(block, AREA, pairs)  16.2 us
    ppermute x2, waiting for transfers between devices, body(): lax.ppermute(part, 'lon', [(i, i ^ step) for i in range(lons)]).astype(F32)  5.95 us
    ppermute x1, starting transfers between devices, body(): lax.ppermute(head, AREA, [(i, (i + lons // 2) % lons) for i in range(lons)])  4.9 us
    ppermute x2, starting transfers between devices, body(): lax.ppermute(part, 'lon', [(i, i ^ step) for i in range(lons)]).astype(F32)  4.42 us
    ppermute x1, starting transfers between devices, body(): lax.ppermute(column(first_col, 0), 'lon', [(i, (i - 1) % lons) for i in r...  3.57 us
    pallas_call x1, Pallas kernels, body(): pl.pallas_call(functools.partial(middle_kernel, lats), out_shape=(shape((...  3.27 us
    unnamed x14, local copies, waits for them, and re-layouts  2.99 us
    ppermute x1, starting transfers between devices, body(): down = lax.ppermute(tail, 'lat', [(i, (i + 1) % lats) for i in range(lats)])  2.99 us
  transfers between devices with their start and end apart: 13, of which 11 were waited for; matrix products, arithmetic and copies ran while one was open for 0% of the time, Pallas kernels for 6%

profile of v3, /device:TPU:0, one launch (start us, length us, event | category | flops | bytes accessed | tf_op | source)
XLA Modules:
  0.0 56.7 jit_solution(8205215406781631007)
XLA Ops:
  0.6 0.0 copy-start
  0.6 1.0 %copy-done = bf16[16,128,128]{2,1,0:T(8,128)(2,1)S(1)} copy-done((bf16[16,128,128]{2,1,0:T(8,128)(2,1)S(1)}, bf16[16,128,128]{2,1,0:T(8,128)(2,1)}, u32[]{:S(2)}) %copy-start) | copy-done | bytes 524312
  1.7 0.0 copy-start.5
  1.7 0.9 %copy-done.5 = bf16[8,64,128]{2,1,0:T(8,128)(2,1)S(1)} copy-done((bf16[8,64,128]{2,1,0:T(8,128)(2,1)S(1)}, bf16[8,64,128]{2,1,0:T(8,128)(2,1)}, u32[]{:S(2)}) %copy-start.5) | copy-done | bytes 131096
  2.6 0.0 copy-start.2
  2.6 0.0 copy-start.3
  2.6 0.0 copy-start.4
  2.6 3.0 %collective-permute-start.1 = (bf16[192,128]{1,0:T(8,128)(2,1)S(1)}, bf16[192,128]{1,0:T(8,128)(2,1)S(1)}, u32[]{:S(2)}, u32[]{:S(2)}) collective-permute-start(bf16[192,128]{1,0:T(8,128)(2,1)S(1)} %get-tuple-element.30), channel_id=1, source_target_pairs={{0,8},{8,16},{16,24},{24,0},{1,9},{9,17},{17,25},{25,1},{2,10},{10... | collective-permute-start | bytes 147464 | tf_op jit(solution)/shard_map/ppermute | solution.py:330
  5.6 1.0 %collective-permute-start.2 = (bf16[192,128]{1,0:T(8,128)(2,1)S(1)}, bf16[192,128]{1,0:T(8,128)(2,1)S(1)}, u32[]{:S(2)}, u32[]{:S(2)}) collective-permute-start(bf16[192,128]{1,0:T(8,128)(2,1)S(1)} %get-tuple-element.29), channel_id=1, source_target_pairs={{0,24},{8,0},{16,8},{24,16},{1,25},{9,1},{17,9},{25,17},{2,26},{10... | collective-permute-start | bytes 147464 | tf_op jit(solution)/shard_map/ppermute | solution.py:331
  6.6 4.9 %collective-permute-start = (bf16[192,128]{1,0:T(8,128)(2,1)S(1)}, bf16[192,128]{1,0:T(8,128)(2,1)S(1)}, u32[]{:S(2)}, u32[]{:S(2)}) collective-permute-start(bf16[192,128]{1,0:T(8,128)(2,1)S(1)} %get-tuple-element.29), channel_id=1, source_target_pairs={{0,4},{1,5},{2,6},{3,7},{4,0},{5,1},{6,2},{7,3}} | collective-permute-start | bytes 147464 | tf_op jit(solution)/shard_map/ppermute | solution.py:329
  11.6 0.0 copy-start.1
  11.6 1.0 %copy-done.1 = bf16[16,128,128]{2,1,0:T(8,128)(2,1)S(1)} copy-done((bf16[16,128,128]{2,1,0:T(8,128)(2,1)S(1)}, bf16[16,128,128]{2,1,0:T(8,128)(2,1)}, u32[]{:S(2)}) %copy-start.1) | copy-done | bytes 524312
  12.6 0.0 copy-start.6
  12.6 0.9 %shard_map.77 = (f32[16,64,256]{2,1,0:T(8,128)S(1)}, bf16[2,256,512]{2,1,0:T(8,128)(2,1)S(1)}) custom-call(bf16[16,128,128]{2,1,0:T(8,128)(2,1)S(1)} %copy-done.1), custom_call_target="tpu_custom_call" | custom-call | flops 15728640 | bytes 2097152 | tf_op jit(solution)/shard_map/pallas_call | solution.py:333
  13.6 0.0 collective-permute-done.1
  13.6 0.0 collective-permute-done.2.bottom
  13.6 0.2 collective-permute-done
  13.8 0.0 collective-permute-start.3
  13.9 3.6 %collective-permute-start.4 = (bf16[32,128]{1,0:T(8,128)(2,1)S(1)}, bf16[32,128]{1,0:T(8,128)(2,1)S(1)}, u32[]{:S(2)}, u32[]{:S(2)}) collective-permute-start(bf16[32,128]{1,0:T(8,128)(2,1)S(1)} %concatenate.14), channel_id=1, source_target_pairs={{0,7},{1,0},{2,1},{3,2},{4,3},{5,4},{6,5},{7,6},{8,15},{9,8},{10,9... | collective-permute-start | bytes 24584 | tf_op jit(solution)/shard_map/ppermute | solution.py:360
  17.5 0.1 pad_add_fusion.flags
  17.6 0.0 copy-done.2
  17.6 0.0 copy-done.3
  17.6 0.0 copy-done.4
  17.6 0.5 shard_map.78
  18.1 0.7 %collective-permute-done.3.left = bf16[32,128]{1,0:T(8,128)(2,1)S(1)} collective-permute-done((bf16[32,128]{1,0:T(8,128)(2,1)S(1)}, bf16[32,128]{1,0:T(8,128)(2,1)S(1)}, u32[]{:S(2)}, u32[]{:S(2)}) %collective-permute-start.3) | collective-permute-done | bytes 8224 | tf_op jit(solution)/shard_map/ppermute | solution.py:359
  18.8 0.1 collective-permute-done.4.right
  18.9 0.0 copy-done.6
  18.9 3.3 %shard_map.79 = (bf16[19,64,512]{2,1,0:T(8,128)(2,1)S(1)}, f32[1024,128]{1,0:T(8,128)S(1)}, f32[1024,128]{1,0:T(8,128)S(1)}) custom-call(s32[4]{0:T(128)S(1)} %pad_add_fusion.flags, bf16[8,64,128]{2,1,0:T(8,128)(2,1)S(1)} %copy-done.6, bf16[192,128]{1,0:T(8,128)(2,1)S(1)} %broadcast_select_fusion.top, bf16[192,128]{1,0:T(8,128)(2,1)S(1)} %collective-permute-done.2.bottom, ...), custom_call_target="tpu_custom_call" | custom-call | flops 1509949440 | bytes 8388608 | tf_op jit(solution)/shard_map/pallas_call | solution.py:382
  22.2 0.1 collective-permute-start.5
  22.3 1.9 %collective-permute-done.5 = f32[1024,128]{1,0:T(8,128)S(1)} collective-permute-done((f32[1024,128]{1,0:T(8,128)S(1)}, f32[1024,128]{1,0:T(8,128)S(1)}, u32[]{:S(2)}, u32[]{:S(2)}) %collective-permute-start.5) | collective-permute-done | bytes 524320 | tf_op jit(solution)/shard_map/ppermute | solution.py:415
  24.1 0.1 add.15
  24.2 0.1 collective-permute-start.6
  24.3 2.2 %shard_map.80 = bf16[16,64,128]{2,1,0:T(8,128)(2,1)} custom-call(bf16[19,64,512]{2,1,0:T(8,128)(2,1)S(1)} %get-tuple-element.49.spread, bf16[384,512]{1,0:T(8,128)(2,1)S(1)} %get-tuple-element.50.taps), custom_call_target="tpu_custom_call" | custom-call | flops 301989888 | bytes 3145728 | tf_op jit(solution)/shard_map/pallas_call | solution.py:424
  26.5 2.7 %collective-permute-done.6 = bf16[2,256,128]{2,1,0:T(8,128)(2,1)S(1)} collective-permute-done((bf16[2,256,128]{2,1,0:T(8,128)(2,1)S(1)}, bf16[2,256,128]{2,1,0:T(8,128)(2,1)S(1)}, u32[]{:S(2)}, u32[]{:S(2)}) %collective-permute-start.6) | collective-permute-done | bytes 131104 | tf_op jit(solution)/shard_map/ppermute | solution.py:413
  29.3 0.1 collective-permute-start.7
  29.4 4.3 %collective-permute-done.7 = bf16[1,256,128]{2,1,0:T(8,128)(2,1)S(1)} collective-permute-done((bf16[1,256,128]{2,1,0:T(8,128)(2,1)S(1)}, bf16[1,256,128]{2,1,0:T(8,128)(2,1)S(1)}, u32[]{:S(2)}, u32[]{:S(2)}) %collective-permute-start.7) | collective-permute-done | bytes 65568 | tf_op jit(solution)/shard_map/ppermute | solution.py:413
  33.7 1.3 %collective-permute-start.8 = (bf16[1,256,128]{2,1,0:T(8,128)(2,1)S(1)}, bf16[1,256,128]{2,1,0:T(8,128)(2,1)S(1)}, u32[]{:S(2)}, u32[]{:S(2)}) collective-permute-start(bf16[1,256,128]{2,1,0:T(8,128)(2,1)S(1)} %fusion), channel_id=1, source_target_pairs={{0,2},{1,3},{2,0},{3,1},{4,6},{5,7},{6,4},{7,5},{8,10},{9,11},{10,... | collective-permute-start | bytes 196616 | tf_op jit(solution)/shard_map/ppermute | solution.py:441
  35.0 3.0 %collective-permute-done.8 = bf16[1,256,128]{2,1,0:T(8,128)(2,1)S(1)} collective-permute-done((bf16[1,256,128]{2,1,0:T(8,128)(2,1)S(1)}, bf16[1,256,128]{2,1,0:T(8,128)(2,1)S(1)}, u32[]{:S(2)}, u32[]{:S(2)}) %collective-permute-start.8) | collective-permute-done | bytes 65568 | tf_op jit(solution)/shard_map/ppermute | solution.py:441
  38.0 3.1 %collective-permute-start.9 = (bf16[1,256,128]{2,1,0:T(8,128)(2,1)S(1)}, bf16[1,256,128]{2,1,0:T(8,128)(2,1)S(1)}, u32[]{:S(2)}, u32[]{:S(2)}) collective-permute-start(bf16[1,256,128]{2,1,0:T(8,128)(2,1)S(1)} %add_convert_fusion.1), channel_id=1, source_target_pairs={{0,4},{1,5},{2,6},{3,7},{4,0},{5,1},{6,2},{7,3},{8,12},{9,13},{10,... | collective-permute-start | bytes 196616 | tf_op jit(solution)/shard_map/ppermute | solution.py:441
  41.1 2.9 %collective-permute-done.9 = bf16[1,256,128]{2,1,0:T(8,128)(2,1)S(1)} collective-permute-done((bf16[1,256,128]{2,1,0:T(8,128)(2,1)S(1)}, bf16[1,256,128]{2,1,0:T(8,128)(2,1)S(1)}, u32[]{:S(2)}, u32[]{:S(2)}) %collective-permute-start.9) | collective-permute-done | bytes 65568 | tf_op jit(solution)/shard_map/ppermute | solution.py:441
  44.1 0.1 collective-permute-start.10
  44.2 4.2 %collective-permute-done.10 = bf16[1,256,128]{2,1,0:T(8,128)(2,1)S(1)} collective-permute-done((bf16[1,256,128]{2,1,0:T(8,128)(2,1)S(1)}, bf16[1,256,128]{2,1,0:T(8,128)(2,1)S(1)}, u32[]{:S(2)}, u32[]{:S(2)}) %collective-permute-start.10) | collective-permute-done | bytes 65568 | tf_op jit(solution)/shard_map/ppermute | solution.py:413
  48.4 0.1 collective-permute-start.11
  48.5 5.0 %collective-permute-done.11 = bf16[2,256,128]{2,1,0:T(8,128)(2,1)S(1)} collective-permute-done((bf16[2,256,128]{2,1,0:T(8,128)(2,1)S(1)}, bf16[2,256,128]{2,1,0:T(8,128)(2,1)S(1)}, u32[]{:S(2)}, u32[]{:S(2)}) %collective-permute-start.11) | collective-permute-done | bytes 131104 | tf_op jit(solution)/shard_map/ppermute | solution.py:413
  53.5 0.1 collective-permute-start.12
  53.6 1.5 %collective-permute-done.12.theirs = bf16[4,256,128]{2,1,0:T(8,128)(2,1)S(1)} collective-permute-done((bf16[4,256,128]{2,1,0:T(8,128)(2,1)S(1)}, bf16[4,256,128]{2,1,0:T(8,128)(2,1)S(1)}, u32[]{:S(2)}, u32[]{:S(2)}) %collective-permute-start.12) | collective-permute-done | bytes 262176 | tf_op jit(solution)/shard_map/ppermute | solution.py:446
  55.1 1.6 %shard_map.81 = (f32[576,128]{1,0:T(8,128)}, f32[1152,128]{1,0:T(8,128)}) custom-call(s32[4]{0:T(128)S(1)} %pad_add_fusion.flags, bf16[4,256,128]{2,1,0:T(8,128)(2,1)S(1)} %pad_maximum_fusion.mine, bf16[4,256,128]{2,1,0:T(8,128)(2,1)S(1)} %collective-permute-done.12.theirs), custom_call_target="tpu_custom_call" | custom-call | flops 1000 | bytes 1572864 | tf_op jit(solution)/shard_map/pallas_call | solution.py:448
  (17 shorter events, 0.3 us)
Async XLA Ops:
  0.6 1.0 %copy-start = (bf16[16,128,128]{2,1,0:T(8,128)(2,1)S(1)}, bf16[16,128,128]{2,1,0:T(8,128)(2,1)}, u32[]{:S(2)}) copy-start(bf16[16,128,128]{2,1,0:T(8,128)(2,1)} %pre.3) | copy-start | bytes 1572868
  1.7 0.9 %copy-start.5 = (bf16[8,64,128]{2,1,0:T(8,128)(2,1)S(1)}, bf16[8,64,128]{2,1,0:T(8,128)(2,1)}, u32[]{:S(2)}) copy-start(bf16[8,64,128]{2,1,0:T(8,128)(2,1)} %grad_out.3) | copy-start | bytes 393220
  2.6 15.0 %copy-start.2 = (bf16[3,3,128,128]{3,2,1,0:T(8,128)(2,1)S(1)}, bf16[3,3,128,128]{3,2,1,0:T(8,128)(2,1)}, u32[]{:S(2)}) copy-start(bf16[3,3,128,128]{3,2,1,0:T(8,128)(2,1)} %w_second.1) | copy-start | bytes 884740
  2.6 15.0 %copy-start.3 = (bf16[16,128,64]{1,2,0:T(8,128)(2,1)S(1)}, bf16[16,128,64]{1,2,0:T(8,128)(2,1)}, u32[]{:S(2)}) copy-start(bf16[16,128,64]{1,2,0:T(8,128)(2,1)} %param.5) | copy-start | bytes 786436
  2.6 15.0 %copy-start.4 = (bf16[3,3,64,128]{3,2,1,0:T(8,128)(2,1)S(1)}, bf16[3,3,64,128]{3,2,1,0:T(8,128)(2,1)}, u32[]{:S(2)}) copy-start(bf16[3,3,64,128]{3,2,1,0:T(8,128)(2,1)} %w_first.1) | copy-start | bytes 442372
  2.6 10.9 %collective-permute-start.1 = (bf16[192,128]{1,0:T(8,128)(2,1)S(1)}, bf16[192,128]{1,0:T(8,128)(2,1)S(1)}, u32[]{:S(2)}, u32[]{:S(2)}) collective-permute-start(bf16[192,128]{1,0:T(8,128)(2,1)S(1)} %get-tuple-element.30), channel_id=1, source_target_pairs={{0,8},{8,16},{16,24},{24,0},{1,9},{9,17},{17,25},{25,1},{2,10},{10... | collective-permute-start | bytes 147464 | tf_op jit(solution)/shard_map/ppermute | solution.py:330
  5.6 8.0 %collective-permute-start.2 = (bf16[192,128]{1,0:T(8,128)(2,1)S(1)}, bf16[192,128]{1,0:T(8,128)(2,1)S(1)}, u32[]{:S(2)}, u32[]{:S(2)}) collective-permute-start(bf16[192,128]{1,0:T(8,128)(2,1)S(1)} %get-tuple-element.29), channel_id=1, source_target_pairs={{0,24},{8,0},{16,8},{24,16},{1,25},{9,1},{17,9},{25,17},{2,26},{10... | collective-permute-start | bytes 147464 | tf_op jit(solution)/shard_map/ppermute | solution.py:331
  6.6 7.1 %collective-permute-start = (bf16[192,128]{1,0:T(8,128)(2,1)S(1)}, bf16[192,128]{1,0:T(8,128)(2,1)S(1)}, u32[]{:S(2)}, u32[]{:S(2)}) collective-permute-start(bf16[192,128]{1,0:T(8,128)(2,1)S(1)} %get-tuple-element.29), channel_id=1, source_target_pairs={{0,4},{1,5},{2,6},{3,7},{4,0},{5,1},{6,2},{7,3}} | collective-permute-start | bytes 147464 | tf_op jit(solution)/shard_map/ppermute | solution.py:329
  11.6 1.0 %copy-start.1 = (bf16[16,128,128]{2,1,0:T(8,128)(2,1)S(1)}, bf16[16,128,128]{2,1,0:T(8,128)(2,1)}, u32[]{:S(2)}) copy-start(bf16[16,128,128]{2,1,0:T(8,128)(2,1)} %pre.3) | copy-start | bytes 1572868
  12.6 6.3 %copy-start.6 = (bf16[8,64,128]{2,1,0:T(8,128)(2,1)S(1)}, bf16[8,64,128]{2,1,0:T(8,128)(2,1)}, u32[]{:S(2)}) copy-start(bf16[8,64,128]{2,1,0:T(8,128)(2,1)} %grad_out.3) | copy-start | bytes 393220
  13.8 4.9 %collective-permute-start.3 = (bf16[32,128]{1,0:T(8,128)(2,1)S(1)}, bf16[32,128]{1,0:T(8,128)(2,1)S(1)}, u32[]{:S(2)}, u32[]{:S(2)}) collective-permute-start(bf16[32,128]{1,0:T(8,128)(2,1)S(1)} %concatenate.13), channel_id=1, source_target_pairs={{0,1},{1,2},{2,3},{3,4},{4,5},{5,6},{6,7},{7,0},{8,9},{9,10},{10,1... | collective-permute-start | bytes 24584 | tf_op jit(solution)/shard_map/ppermute | solution.py:359
  13.9 4.9 %collective-permute-start.4 = (bf16[32,128]{1,0:T(8,128)(2,1)S(1)}, bf16[32,128]{1,0:T(8,128)(2,1)S(1)}, u32[]{:S(2)}, u32[]{:S(2)}) collective-permute-start(bf16[32,128]{1,0:T(8,128)(2,1)S(1)} %concatenate.14), channel_id=1, source_target_pairs={{0,7},{1,0},{2,1},{3,2},{4,3},{5,4},{6,5},{7,6},{8,15},{9,8},{10,9... | collective-permute-start | bytes 24584 | tf_op jit(solution)/shard_map/ppermute | solution.py:360
  22.2 2.0 %collective-permute-start.5 = (f32[1024,128]{1,0:T(8,128)S(1)}, f32[1024,128]{1,0:T(8,128)S(1)}, u32[]{:S(2)}, u32[]{:S(2)}) collective-permute-start(f32[1024,128]{1,0:T(8,128)S(1)} %get-tuple-element.46), channel_id=1, source_target_pairs={{0,1},{1,0},{2,3},{3,2},{4,5},{5,4},{6,7},{7,6},{8,9},{9,8},{10,11... | collective-permute-start | bytes 1572872 | tf_op jit(solution)/shard_map/ppermute | solution.py:415
  24.2 5.0 %collective-permute-start.6 = (bf16[2,256,128]{2,1,0:T(8,128)(2,1)S(1)}, bf16[2,256,128]{2,1,0:T(8,128)(2,1)S(1)}, u32[]{:S(2)}, u32[]{:S(2)}) collective-permute-start(bf16[2,256,128]{2,1,0:T(8,128)(2,1)S(1)} %bitcast.13), channel_id=1, source_target_pairs={{0,8},{1,17},{2,10},{3,19},{4,12},{5,21},{6,14},{7,23},{8,0},{9,25... | collective-permute-start | bytes 393224 | tf_op jit(solution)/shard_map/ppermute | solution.py:413
  29.3 4.3 %collective-permute-start.7 = (bf16[1,256,128]{2,1,0:T(8,128)(2,1)S(1)}, bf16[1,256,128]{2,1,0:T(8,128)(2,1)S(1)}, u32[]{:S(2)}, u32[]{:S(2)}) collective-permute-start(bf16[1,256,128]{2,1,0:T(8,128)(2,1)S(1)} %slice.77), channel_id=1, source_target_pairs={{0,16},{1,9},{2,18},{3,11},{4,20},{5,13},{6,22},{7,15},{8,24},{9,1... | collective-permute-start | bytes 196616 | tf_op jit(solution)/shard_map/ppermute | solution.py:413
  33.7 4.3 %collective-permute-start.8 = (bf16[1,256,128]{2,1,0:T(8,128)(2,1)S(1)}, bf16[1,256,128]{2,1,0:T(8,128)(2,1)S(1)}, u32[]{:S(2)}, u32[]{:S(2)}) collective-permute-start(bf16[1,256,128]{2,1,0:T(8,128)(2,1)S(1)} %fusion), channel_id=1, source_target_pairs={{0,2},{1,3},{2,0},{3,1},{4,6},{5,7},{6,4},{7,5},{8,10},{9,11},{10,... | collective-permute-start | bytes 196616 | tf_op jit(solution)/shard_map/ppermute | solution.py:441
  38.0 6.0 %collective-permute-start.9 = (bf16[1,256,128]{2,1,0:T(8,128)(2,1)S(1)}, bf16[1,256,128]{2,1,0:T(8,128)(2,1)S(1)}, u32[]{:S(2)}, u32[]{:S(2)}) collective-permute-start(bf16[1,256,128]{2,1,0:T(8,128)(2,1)S(1)} %add_convert_fusion.1), channel_id=1, source_target_pairs={{0,4},{1,5},{2,6},{3,7},{4,0},{5,1},{6,2},{7,3},{8,12},{9,13},{10,... | collective-permute-start | bytes 196616 | tf_op jit(solution)/shard_map/ppermute | solution.py:441
  44.1 4.3 %collective-permute-start.10 = (bf16[1,256,128]{2,1,0:T(8,128)(2,1)S(1)}, bf16[1,256,128]{2,1,0:T(8,128)(2,1)S(1)}, u32[]{:S(2)}, u32[]{:S(2)}) collective-permute-start(bf16[1,256,128]{2,1,0:T(8,128)(2,1)S(1)} %add_convert_fusion), channel_id=1, source_target_pairs={{0,16},{1,9},{2,18},{3,11},{4,20},{5,13},{6,22},{7,15},{8,24},{9,1... | collective-permute-start | bytes 196616 | tf_op jit(solution)/shard_map/ppermute | solution.py:413
  48.4 5.0 %collective-permute-start.11 = (bf16[2,256,128]{2,1,0:T(8,128)(2,1)S(1)}, bf16[2,256,128]{2,1,0:T(8,128)(2,1)S(1)}, u32[]{:S(2)}, u32[]{:S(2)}) collective-permute-start(bf16[2,256,128]{2,1,0:T(8,128)(2,1)S(1)} %pad_maximum_fusion.1), channel_id=1, source_target_pairs={{0,8},{1,17},{2,10},{3,19},{4,12},{5,21},{6,14},{7,23},{8,0},{9,25... | collective-permute-start | bytes 393224 | tf_op jit(solution)/shard_map/ppermute | solution.py:413
  53.5 1.6 %collective-permute-start.12 = (bf16[4,256,128]{2,1,0:T(8,128)(2,1)S(1)}, bf16[4,256,128]{2,1,0:T(8,128)(2,1)S(1)}, u32[]{:S(2)}, u32[]{:S(2)}) collective-permute-start(bf16[4,256,128]{2,1,0:T(8,128)(2,1)S(1)} %pad_maximum_fusion.mine), channel_id=1, source_target_pairs={{0,1},{1,0},{2,3},{3,2},{4,5},{5,4},{6,7},{7,6},{8,9},{9,8},{10,11... | collective-permute-start | bytes 786440 | tf_op jit(solution)/shard_map/ppermute | solution.py:446

commit v4 on v3

--- a/solution.py
+++ b/solution.py
@@ -409,41 +409,39 @@
     orders = [steps(lats, k) for k in range(2)]
 
     def along_lat(t, block):
-        pairs = [(i * lons + j, (i ^ orders[j % 2][t]) * lons + j) for i in range(lats) for j in range(lons)]
+        far = [distance(t, masks) for masks in orders]
+        pairs = [(i * lons + j, (i ^ far[j % 2]) * lons + j) for i in range(lats) for j in range(lons)]
         return lax.ppermute(block, AREA, pairs)
 
-    total = (own + lax.ppermute(other, "lon", swap)).reshape(lats, held // lats, c1)
-    rounds = lats.bit_length() - 1
-    for t in range(rounds):
-        count = total.shape[0] // 2
-        sent = total[count:].astype(BF16)
-        if t == 0:
-            sent, spread = lax.optimization_barrier((sent, spread))
-        got = along_lat(t, sent)
-        if t == 0:
-            grad_inputs = pl.pallas_call(
-                last_kernel,
-                out_shape=shape((rows, c0, cols), BF16),
-                in_specs=vmem(2),
-                out_specs=vmem(1)[0],
-                scratch_shapes=[
-                    pltpu.VMEM((2 * c0, rows * half), F32),
-                    pltpu.VMEM((pooled, c0, 2 * cols), BF16),
-                ],
-                compiler_params=params(12),
-                cost_estimate=pl.CostEstimate(flops=2 * rows * cols * c1 * 9 * c0, bytes_accessed=3 << 20, transcendentals=0),
-            )(spread, taps_first)
-            got, grad_inputs = lax.optimization_barrier((got, grad_inputs))
-        total = total[:count] + got.astype(F32)
-    step = 2
-    while step < lons:
-        part = total.astype(BF16)
-        total = part.astype(F32) + lax.ppermute(part, "lon", [(i, i ^ step) for i in range(lons)]).astype(F32)
-        step *= 2
-    mine = total.astype(BF16)
-    for t in reversed(range(rounds)):
-        mine = jnp.concatenate([mine, along_lat(t, mine)], 0)
-    theirs = lax.ppermute(mine, "lon", swap)
+    parts = (own + lax.ppermute(other, "lon", swap)).reshape(lats, held // lats, c1)
+    sent = [parts[t].astype(BF16) for t in range(1, lats)]
+    *sent, spread = lax.optimization_barrier((*sent, spread))
+    got = [along_lat(t + 1, block) for t, block in enumerate(sent)]
+    grad_inputs = pl.pallas_call(
+        last_kernel,
+        out_shape=shape((rows, c0, cols), BF16),
+        in_specs=vmem(2),
+        out_specs=vmem(1)[0],
+        scratch_shapes=[
+            pltpu.VMEM((2 * c0, rows * half), F32),
+            pltpu.VMEM((pooled, c0, 2 * cols), BF16),
+        ],
+        compiler_params=params(12),
+        cost_estimate=pl.CostEstimate(flops=2 * rows * cols * c1 * 9 * c0, bytes_accessed=3 << 20, transcendentals=0),
+    )(spread, taps_first)
+    *got, grad_inputs = lax.optimization_barrier((*got, grad_inputs))
+    total = parts[0]
+    for block in got:
+        total = total + block.astype(F32)
+    part = total.astype(BF16)
+    blocks = [part] + [lax.ppermute(part, "lon", [(i, i ^ (2 * k)) for i in range(lons)]) for k in range(1, depths)]
+    blocks = [block.astype(F32) for block in blocks]
+    while len(blocks) > 1:
+        blocks = [blocks[k] + blocks[k + 1] for k in range(0, len(blocks), 2)]
+    block = blocks[0].astype(BF16)
+    mine = [block] + [along_lat(t, block) for t in range(1, lats)]
+    theirs = [lax.ppermute(block, "lon", swap) for block in mine]
+    mine, theirs = jnp.stack(mine, 0), jnp.stack(theirs, 0)
 
     grad_w_first, grad_w_second = pl.pallas_call(
         gather_kernel,

time: 56.9 us -> 49.5 us (0.87)
  waiting for transfers between devices: 26.5 us -> 12 us
  starting transfers between devices: 17.4 us -> 24.5 us
    ppermute x4 -> x6, waiting for transfers between devices: 16.2 us -> 3.81 us  [along_lat(): return lax.ppermute(block, AREA, pairs)]
    ppermute x4 -> x6, starting transfers between devices: 0.3 us -> 7.09 us  [along_lat(): return lax.ppermute(block, AREA, pairs)]
    ppermute x3 -> x7, waiting for transfers between devices: 7.47 us -> 5.33 us  [the longest x3 4.44 us: body(): lax.ppermute(part, 'lon', [(i, i ^ 2 * k) for i in range(lons)])]
    ppermute x3 -> x7, starting transfers between devices: 4.49 us -> 4.78 us  [the longest x3 4.45 us: body(): lax.ppermute(part, 'lon', [(i, i ^ 2 * k) for i in range(lons)])]
  transfers between devices with their start and end apart: 13 -> 19, of which waited for: 11 -> 12; matrix products, arithmetic and copies ran while one was open for 0% -> 0% of each run, Pallas kernels for 6% -> 7%
where the time goes in v4:
time: 49.5 us; the launch traced here: 49.2 us
  starting transfers between devices  24.5 us (49%)
  waiting for transfers between devices  12 us (24%)
  Pallas kernels  8.49 us (17%)
  local copies, waits for them, and re-layouts  3.12 us (6%)
  between operations  0.83 us (2%)
    ppermute x6, starting transfers between devices, along_lat(): return lax.ppermute(block, AREA, pairs)  7.09 us
    ppermute x1, starting transfers between devices, body(): lax.ppermute(head, AREA, [(i, (i + lons // 2) % lons) for i in range(lons)])  4.9 us
    ppermute x3, starting transfers between devices, body(): lax.ppermute(part, 'lon', [(i, i ^ 2 * k) for i in range(lons)])  4.45 us
    ppermute x3, waiting for transfers between devices, body(): lax.ppermute(part, 'lon', [(i, i ^ 2 * k) for i in range(lons)])  4.44 us
    ppermute x6, waiting for transfers between devices, along_lat(): return lax.ppermute(block, AREA, pairs)  3.81 us
    ppermute x1, starting transfers between devices, body(): lax.ppermute(column(first_col, 0), 'lon', [(i, (i - 1) % lons) for i in r...  3.57 us
    pallas_call x1, Pallas kernels, body(): pl.pallas_call(functools.partial(middle_kernel, lats), out_shape=(shape((...  3.27 us
    unnamed x14, local copies, waits for them, and re-layouts  2.99 us
  transfers between devices with their start and end apart: 19, of which 12 were waited for; matrix products, arithmetic and copies ran while one was open for 0% of the time, Pallas kernels for 7%

profile of v4, /device:TPU:0, one launch (start us, length us, event | category | flops | bytes accessed | tf_op | source)
XLA Modules:
  0.0 49.2 jit_solution(136976927922962343)
XLA Ops:
  0.6 0.0 copy-start
  0.6 1.0 %copy-done = bf16[16,128,128]{2,1,0:T(8,128)(2,1)S(1)} copy-done((bf16[16,128,128]{2,1,0:T(8,128)(2,1)S(1)}, bf16[16,128,128]{2,1,0:T(8,128)(2,1)}, u32[]{:S(2)}) %copy-start) | copy-done | bytes 524312
  1.7 0.0 copy-start.5
  1.7 0.9 %copy-done.5 = bf16[8,64,128]{2,1,0:T(8,128)(2,1)S(1)} copy-done((bf16[8,64,128]{2,1,0:T(8,128)(2,1)S(1)}, bf16[8,64,128]{2,1,0:T(8,128)(2,1)}, u32[]{:S(2)}) %copy-start.5) | copy-done | bytes 131096
  2.6 0.0 copy-start.2
  2.6 0.0 copy-start.3
  2.6 0.0 copy-start.4
  2.6 3.0 %collective-permute-start.1 = (bf16[192,128]{1,0:T(8,128)(2,1)S(1)}, bf16[192,128]{1,0:T(8,128)(2,1)S(1)}, u32[]{:S(2)}, u32[]{:S(2)}) collective-permute-start(bf16[192,128]{1,0:T(8,128)(2,1)S(1)} %get-tuple-element.34), channel_id=1, source_target_pairs={{0,8},{8,16},{16,24},{24,0},{1,9},{9,17},{17,25},{25,1},{2,10},{10... | collective-permute-start | bytes 147464 | tf_op jit(solution)/shard_map/ppermute | solution.py:330
  5.6 1.0 %collective-permute-start.2 = (bf16[192,128]{1,0:T(8,128)(2,1)S(1)}, bf16[192,128]{1,0:T(8,128)(2,1)S(1)}, u32[]{:S(2)}, u32[]{:S(2)}) collective-permute-start(bf16[192,128]{1,0:T(8,128)(2,1)S(1)} %get-tuple-element.33), channel_id=1, source_target_pairs={{0,24},{8,0},{16,8},{24,16},{1,25},{9,1},{17,9},{25,17},{2,26},{10... | collective-permute-start | bytes 147464 | tf_op jit(solution)/shard_map/ppermute | solution.py:331
  6.6 4.9 %collective-permute-start = (bf16[192,128]{1,0:T(8,128)(2,1)S(1)}, bf16[192,128]{1,0:T(8,128)(2,1)S(1)}, u32[]{:S(2)}, u32[]{:S(2)}) collective-permute-start(bf16[192,128]{1,0:T(8,128)(2,1)S(1)} %get-tuple-element.33), channel_id=1, source_target_pairs={{0,4},{1,5},{2,6},{3,7},{4,0},{5,1},{6,2},{7,3}} | collective-permute-start | bytes 147464 | tf_op jit(solution)/shard_map/ppermute | solution.py:329
  11.6 0.0 copy-start.1
  11.6 1.0 %copy-done.1 = bf16[16,128,128]{2,1,0:T(8,128)(2,1)S(1)} copy-done((bf16[16,128,128]{2,1,0:T(8,128)(2,1)S(1)}, bf16[16,128,128]{2,1,0:T(8,128)(2,1)}, u32[]{:S(2)}) %copy-start.1) | copy-done | bytes 524312
  12.6 0.0 copy-start.6
  12.6 0.9 %shard_map.77 = (f32[16,64,256]{2,1,0:T(8,128)S(1)}, bf16[2,256,512]{2,1,0:T(8,128)(2,1)S(1)}) custom-call(bf16[16,128,128]{2,1,0:T(8,128)(2,1)S(1)} %copy-done.1), custom_call_target="tpu_custom_call" | custom-call | flops 15728640 | bytes 2097152 | tf_op jit(solution)/shard_map/pallas_call | solution.py:333
  13.6 0.0 collective-permute-done.1
  13.6 0.0 collective-permute-done.2.bottom
  13.6 0.2 collective-permute-done
  13.8 0.0 collective-permute-start.3
  13.9 3.6 %collective-permute-start.4 = (bf16[32,128]{1,0:T(8,128)(2,1)S(1)}, bf16[32,128]{1,0:T(8,128)(2,1)S(1)}, u32[]{:S(2)}, u32[]{:S(2)}) collective-permute-start(bf16[32,128]{1,0:T(8,128)(2,1)S(1)} %concatenate.7), channel_id=1, source_target_pairs={{0,7},{1,0},{2,1},{3,2},{4,3},{5,4},{6,5},{7,6},{8,15},{9,8},{10,9... | collective-permute-start | bytes 24584 | tf_op jit(solution)/shard_map/ppermute | solution.py:360
  17.5 0.1 pad_add_fusion.flags
  17.6 0.0 copy-done.2
  17.6 0.0 copy-done.3
  17.6 0.0 copy-done.4
  17.6 0.5 shard_map.78
  18.1 0.7 %collective-permute-done.3.left = bf16[32,128]{1,0:T(8,128)(2,1)S(1)} collective-permute-done((bf16[32,128]{1,0:T(8,128)(2,1)S(1)}, bf16[32,128]{1,0:T(8,128)(2,1)S(1)}, u32[]{:S(2)}, u32[]{:S(2)}) %collective-permute-start.3) | collective-permute-done | bytes 8224 | tf_op jit(solution)/shard_map/ppermute | solution.py:359
  18.8 0.1 collective-permute-done.4.right
  18.9 0.0 copy-done.6
  18.9 3.3 %shard_map.79 = (bf16[19,64,512]{2,1,0:T(8,128)(2,1)S(1)}, f32[1024,128]{1,0:T(8,128)S(1)}, f32[1024,128]{1,0:T(8,128)S(1)}) custom-call(s32[4]{0:T(128)S(1)} %pad_add_fusion.flags, bf16[8,64,128]{2,1,0:T(8,128)(2,1)S(1)} %copy-done.6, bf16[192,128]{1,0:T(8,128)(2,1)S(1)} %broadcast_select_fusion.top, bf16[192,128]{1,0:T(8,128)(2,1)S(1)} %collective-permute-done.2.bottom, ...), custom_call_target="tpu_custom_call" | custom-call | flops 1509949440 | bytes 8388608 | tf_op jit(solution)/shard_map/pallas_call | solution.py:382
  22.2 0.1 collective-permute-start.5
  22.3 1.9 %collective-permute-done.5 = f32[1024,128]{1,0:T(8,128)S(1)} collective-permute-done((f32[1024,128]{1,0:T(8,128)S(1)}, f32[1024,128]{1,0:T(8,128)S(1)}, u32[]{:S(2)}, u32[]{:S(2)}) %collective-permute-start.5) | collective-permute-done | bytes 524320 | tf_op jit(solution)/shard_map/ppermute | solution.py:416
  24.1 0.1 fusion.3
  24.2 0.1 collective-permute-start.6
  24.3 0.1 collective-permute-start.7
  24.4 3.4 %collective-permute-start.8 = (bf16[256,128]{1,0:T(8,128)(2,1)S(1)}, bf16[256,128]{1,0:T(8,128)(2,1)S(1)}, u32[]{:S(2)}, u32[]{:S(2)}) collective-permute-start(bf16[256,128]{1,0:T(8,128)(2,1)S(1)} %get-tuple-element.54), channel_id=1, source_target_pairs={{0,24},{1,25},{2,26},{3,27},{4,28},{5,29},{6,30},{7,31},{8,16},{9,... | collective-permute-start | bytes 196616 | tf_op jit(solution)/shard_map/ppermute | solution.py:414
  27.8 2.2 %shard_map.80 = bf16[16,64,128]{2,1,0:T(8,128)(2,1)} custom-call(bf16[19,64,512]{2,1,0:T(8,128)(2,1)S(1)} %get-tuple-element.55.spread, bf16[384,512]{1,0:T(8,128)(2,1)S(1)} %get-tuple-element.56.taps), custom_call_target="tpu_custom_call" | custom-call | flops 301989888 | bytes 3145728 | tf_op jit(solution)/shard_map/pallas_call | solution.py:420
  30.0 0.0 collective-permute-done.6
  30.0 0.0 collective-permute-done.7
  30.0 0.7 %collective-permute-done.8 = bf16[256,128]{1,0:T(8,128)(2,1)S(1)} collective-permute-done((bf16[256,128]{1,0:T(8,128)(2,1)S(1)}, bf16[256,128]{1,0:T(8,128)(2,1)S(1)}, u32[]{:S(2)}, u32[]{:S(2)}) %collective-permute-start.8) | collective-permute-done | bytes 65568 | tf_op jit(solution)/shard_map/ppermute | solution.py:414
  30.8 3.6 %collective-permute-start.11 = (bf16[256,128]{1,0:T(8,128)(2,1)S(1)}, bf16[256,128]{1,0:T(8,128)(2,1)S(1)}, u32[]{:S(2)}, u32[]{:S(2)}) collective-permute-start(bf16[256,128]{1,0:T(8,128)(2,1)S(1)} %fusion.2), channel_id=1, source_target_pairs={{0,6},{1,7},{2,4},{3,5},{4,2},{5,3},{6,0},{7,1},{8,14},{9,15},{10,... | collective-permute-start | bytes 196616 | tf_op jit(solution)/shard_map/ppermute | solution.py:437
  34.4 0.0 collective-permute-start.10
  34.4 0.9 %collective-permute-start.9 = (bf16[256,128]{1,0:T(8,128)(2,1)S(1)}, bf16[256,128]{1,0:T(8,128)(2,1)S(1)}, u32[]{:S(2)}, u32[]{:S(2)}) collective-permute-start(bf16[256,128]{1,0:T(8,128)(2,1)S(1)} %fusion.2), channel_id=1, source_target_pairs={{0,2},{1,3},{2,0},{3,1},{4,6},{5,7},{6,4},{7,5},{8,10},{9,11},{10,... | collective-permute-start | bytes 196616 | tf_op jit(solution)/shard_map/ppermute | solution.py:437
  35.2 1.8 %collective-permute-done.11 = bf16[256,128]{1,0:T(8,128)(2,1)S(1)} collective-permute-done((bf16[256,128]{1,0:T(8,128)(2,1)S(1)}, bf16[256,128]{1,0:T(8,128)(2,1)S(1)}, u32[]{:S(2)}, u32[]{:S(2)}) %collective-permute-start.11) | collective-permute-done | bytes 65568 | tf_op jit(solution)/shard_map/ppermute | solution.py:437
  37.0 2.7 %collective-permute-done.10 = bf16[256,128]{1,0:T(8,128)(2,1)S(1)} collective-permute-done((bf16[256,128]{1,0:T(8,128)(2,1)S(1)}, bf16[256,128]{1,0:T(8,128)(2,1)S(1)}, u32[]{:S(2)}, u32[]{:S(2)}) %collective-permute-start.10) | collective-permute-done | bytes 65568 | tf_op jit(solution)/shard_map/ppermute | solution.py:437
  39.7 0.0 collective-permute-done.9
  39.7 2.2 %collective-permute-start.14 = (bf16[256,128]{1,0:T(8,128)(2,1)S(1)}, bf16[256,128]{1,0:T(8,128)(2,1)S(1)}, u32[]{:S(2)}, u32[]{:S(2)}) collective-permute-start(bf16[256,128]{1,0:T(8,128)(2,1)S(1)} %add_convert_fusion), channel_id=1, source_target_pairs={{0,24},{1,25},{2,26},{3,27},{4,28},{5,29},{6,30},{7,31},{8,16},{9,... | collective-permute-start | bytes 196616 | tf_op jit(solution)/shard_map/ppermute | solution.py:414
  41.9 0.2 collective-permute-start.13
  42.1 1.2 %collective-permute-start.12 = (bf16[256,128]{1,0:T(8,128)(2,1)S(1)}, bf16[256,128]{1,0:T(8,128)(2,1)S(1)}, u32[]{:S(2)}, u32[]{:S(2)}) collective-permute-start(bf16[256,128]{1,0:T(8,128)(2,1)S(1)} %add_convert_fusion), channel_id=1, source_target_pairs={{0,16},{1,9},{2,18},{3,11},{4,20},{5,13},{6,22},{7,15},{8,24},{9,1... | collective-permute-start | bytes 196616 | tf_op jit(solution)/shard_map/ppermute | solution.py:414
  43.3 0.0 collective-permute-start.15
  43.3 1.7 %collective-permute-done.14 = bf16[256,128]{1,0:T(8,128)(2,1)S(1)} collective-permute-done((bf16[256,128]{1,0:T(8,128)(2,1)S(1)}, bf16[256,128]{1,0:T(8,128)(2,1)S(1)}, u32[]{:S(2)}, u32[]{:S(2)}) %collective-permute-start.14) | collective-permute-done | bytes 65568 | tf_op jit(solution)/shard_map/ppermute | solution.py:414
  45.0 0.0 collective-permute-start.18
  45.0 1.2 %collective-permute-done.13 = bf16[256,128]{1,0:T(8,128)(2,1)S(1)} collective-permute-done((bf16[256,128]{1,0:T(8,128)(2,1)S(1)}, bf16[256,128]{1,0:T(8,128)(2,1)S(1)}, u32[]{:S(2)}, u32[]{:S(2)}) %collective-permute-start.13) | collective-permute-done | bytes 65568 | tf_op jit(solution)/shard_map/ppermute | solution.py:414
  46.1 0.0 collective-permute-start.17
  46.1 0.2 collective-permute-done.12
  46.3 0.3 collective-permute-start.16
  46.7 0.0 collective-permute-done.15
  46.7 0.0 collective-permute-done.18
  46.7 0.7 %collective-permute-done.17 = bf16[256,128]{1,0:T(8,128)(2,1)S(1)} collective-permute-done((bf16[256,128]{1,0:T(8,128)(2,1)S(1)}, bf16[256,128]{1,0:T(8,128)(2,1)S(1)}, u32[]{:S(2)}, u32[]{:S(2)}) %collective-permute-start.17) | collective-permute-done | bytes 65568 | tf_op jit(solution)/shard_map/ppermute | solution.py:443
  47.4 0.2 collective-permute-done.16
  47.6 1.6 %shard_map.81 = (f32[576,128]{1,0:T(8,128)}, f32[1152,128]{1,0:T(8,128)}) custom-call(s32[4]{0:T(128)S(1)} %pad_add_fusion.flags, bf16[4,256,128]{2,1,0:T(8,128)(2,1)S(1)} %pad_maximum_fusion.mine, bf16[4,256,128]{2,1,0:T(8,128)(2,1)S(1)} %pad_maximum_fusion.1.theirs), custom_call_target="tpu_custom_call" | custom-call | flops 1000 | bytes 1572864 | tf_op jit(solution)/shard_map/pallas_call | solution.py:446
  (13 shorter events, 0.3 us)
Async XLA Ops:
  0.6 1.0 %copy-start = (bf16[16,128,128]{2,1,0:T(8,128)(2,1)S(1)}, bf16[16,128,128]{2,1,0:T(8,128)(2,1)}, u32[]{:S(2)}) copy-start(bf16[16,128,128]{2,1,0:T(8,128)(2,1)} %pre.3) | copy-start | bytes 1572868
  1.7 0.9 %copy-start.5 = (bf16[8,64,128]{2,1,0:T(8,128)(2,1)S(1)}, bf16[8,64,128]{2,1,0:T(8,128)(2,1)}, u32[]{:S(2)}) copy-start(bf16[8,64,128]{2,1,0:T(8,128)(2,1)} %grad_out.3) | copy-start | bytes 393220
  2.6 15.0 %copy-start.2 = (bf16[3,3,128,128]{3,2,1,0:T(8,128)(2,1)S(1)}, bf16[3,3,128,128]{3,2,1,0:T(8,128)(2,1)}, u32[]{:S(2)}) copy-start(bf16[3,3,128,128]{3,2,1,0:T(8,128)(2,1)} %w_second.1) | copy-start | bytes 884740
  2.6 15.0 %copy-start.3 = (bf16[16,128,64]{1,2,0:T(8,128)(2,1)S(1)}, bf16[16,128,64]{1,2,0:T(8,128)(2,1)}, u32[]{:S(2)}) copy-start(bf16[16,128,64]{1,2,0:T(8,128)(2,1)} %param.5) | copy-start | bytes 786436
  2.6 15.0 %copy-start.4 = (bf16[3,3,64,128]{3,2,1,0:T(8,128)(2,1)S(1)}, bf16[3,3,64,128]{3,2,1,0:T(8,128)(2,1)}, u32[]{:S(2)}) copy-start(bf16[3,3,64,128]{3,2,1,0:T(8,128)(2,1)} %w_first.1) | copy-start | bytes 442372
  2.6 10.9 %collective-permute-start.1 = (bf16[192,128]{1,0:T(8,128)(2,1)S(1)}, bf16[192,128]{1,0:T(8,128)(2,1)S(1)}, u32[]{:S(2)}, u32[]{:S(2)}) collective-permute-start(bf16[192,128]{1,0:T(8,128)(2,1)S(1)} %get-tuple-element.34), channel_id=1, source_target_pairs={{0,8},{8,16},{16,24},{24,0},{1,9},{9,17},{17,25},{25,1},{2,10},{10... | collective-permute-start | bytes 147464 | tf_op jit(solution)/shard_map/ppermute | solution.py:330
  5.6 8.0 %collective-permute-start.2 = (bf16[192,128]{1,0:T(8,128)(2,1)S(1)}, bf16[192,128]{1,0:T(8,128)(2,1)S(1)}, u32[]{:S(2)}, u32[]{:S(2)}) collective-permute-start(bf16[192,128]{1,0:T(8,128)(2,1)S(1)} %get-tuple-element.33), channel_id=1, source_target_pairs={{0,24},{8,0},{16,8},{24,16},{1,25},{9,1},{17,9},{25,17},{2,26},{10... | collective-permute-start | bytes 147464 | tf_op jit(solution)/shard_map/ppermute | solution.py:331
  6.6 7.1 %collective-permute-start = (bf16[192,128]{1,0:T(8,128)(2,1)S(1)}, bf16[192,128]{1,0:T(8,128)(2,1)S(1)}, u32[]{:S(2)}, u32[]{:S(2)}) collective-permute-start(bf16[192,128]{1,0:T(8,128)(2,1)S(1)} %get-tuple-element.33), channel_id=1, source_target_pairs={{0,4},{1,5},{2,6},{3,7},{4,0},{5,1},{6,2},{7,3}} | collective-permute-start | bytes 147464 | tf_op jit(solution)/shard_map/ppermute | solution.py:329
  11.6 1.0 %copy-start.1 = (bf16[16,128,128]{2,1,0:T(8,128)(2,1)S(1)}, bf16[16,128,128]{2,1,0:T(8,128)(2,1)}, u32[]{:S(2)}) copy-start(bf16[16,128,128]{2,1,0:T(8,128)(2,1)} %pre.3) | copy-start | bytes 1572868
  12.6 6.3 %copy-start.6 = (bf16[8,64,128]{2,1,0:T(8,128)(2,1)S(1)}, bf16[8,64,128]{2,1,0:T(8,128)(2,1)}, u32[]{:S(2)}) copy-start(bf16[8,64,128]{2,1,0:T(8,128)(2,1)} %grad_out.3) | copy-start | bytes 393220
  13.8 4.9 %collective-permute-start.3 = (bf16[32,128]{1,0:T(8,128)(2,1)S(1)}, bf16[32,128]{1,0:T(8,128)(2,1)S(1)}, u32[]{:S(2)}, u32[]{:S(2)}) collective-permute-start(bf16[32,128]{1,0:T(8,128)(2,1)S(1)} %concatenate.6), channel_id=1, source_target_pairs={{0,1},{1,2},{2,3},{3,4},{4,5},{5,6},{6,7},{7,0},{8,9},{9,10},{10,1... | collective-permute-start | bytes 24584 | tf_op jit(solution)/shard_map/ppermute | solution.py:359
  13.9 4.9 %collective-permute-start.4 = (bf16[32,128]{1,0:T(8,128)(2,1)S(1)}, bf16[32,128]{1,0:T(8,128)(2,1)S(1)}, u32[]{:S(2)}, u32[]{:S(2)}) collective-permute-start(bf16[32,128]{1,0:T(8,128)(2,1)S(1)} %concatenate.7), channel_id=1, source_target_pairs={{0,7},{1,0},{2,1},{3,2},{4,3},{5,4},{6,5},{7,6},{8,15},{9,8},{10,9... | collective-permute-start | bytes 24584 | tf_op jit(solution)/shard_map/ppermute | solution.py:360
  22.2 2.0 %collective-permute-start.5 = (f32[1024,128]{1,0:T(8,128)S(1)}, f32[1024,128]{1,0:T(8,128)S(1)}, u32[]{:S(2)}, u32[]{:S(2)}) collective-permute-start(f32[1024,128]{1,0:T(8,128)S(1)} %get-tuple-element.50), channel_id=1, source_target_pairs={{0,1},{1,0},{2,3},{3,2},{4,5},{5,4},{6,7},{7,6},{8,9},{9,8},{10,11... | collective-permute-start | bytes 1572872 | tf_op jit(solution)/shard_map/ppermute | solution.py:416
  24.2 5.7 %collective-permute-start.6 = (bf16[256,128]{1,0:T(8,128)(2,1)S(1)}, bf16[256,128]{1,0:T(8,128)(2,1)S(1)}, u32[]{:S(2)}, u32[]{:S(2)}) collective-permute-start(bf16[256,128]{1,0:T(8,128)(2,1)S(1)} %get-tuple-element.52), channel_id=1, source_target_pairs={{0,16},{1,9},{2,18},{3,11},{4,20},{5,13},{6,22},{7,15},{8,24},{9,1... | collective-permute-start | bytes 196616 | tf_op jit(solution)/shard_map/ppermute | solution.py:414
  24.3 5.7 %collective-permute-start.7 = (bf16[256,128]{1,0:T(8,128)(2,1)S(1)}, bf16[256,128]{1,0:T(8,128)(2,1)S(1)}, u32[]{:S(2)}, u32[]{:S(2)}) collective-permute-start(bf16[256,128]{1,0:T(8,128)(2,1)S(1)} %get-tuple-element.53), channel_id=1, source_target_pairs={{0,8},{1,17},{2,10},{3,19},{4,12},{5,21},{6,14},{7,23},{8,0},{9,25... | collective-permute-start | bytes 196616 | tf_op jit(solution)/shard_map/ppermute | solution.py:414
  24.4 6.3 %collective-permute-start.8 = (bf16[256,128]{1,0:T(8,128)(2,1)S(1)}, bf16[256,128]{1,0:T(8,128)(2,1)S(1)}, u32[]{:S(2)}, u32[]{:S(2)}) collective-permute-start(bf16[256,128]{1,0:T(8,128)(2,1)S(1)} %get-tuple-element.54), channel_id=1, source_target_pairs={{0,24},{1,25},{2,26},{3,27},{4,28},{5,29},{6,30},{7,31},{8,16},{9,... | collective-permute-start | bytes 196616 | tf_op jit(solution)/shard_map/ppermute | solution.py:414
  30.8 6.2 %collective-permute-start.11 = (bf16[256,128]{1,0:T(8,128)(2,1)S(1)}, bf16[256,128]{1,0:T(8,128)(2,1)S(1)}, u32[]{:S(2)}, u32[]{:S(2)}) collective-permute-start(bf16[256,128]{1,0:T(8,128)(2,1)S(1)} %fusion.2), channel_id=1, source_target_pairs={{0,6},{1,7},{2,4},{3,5},{4,2},{5,3},{6,0},{7,1},{8,14},{9,15},{10,... | collective-permute-start | bytes 196616 | tf_op jit(solution)/shard_map/ppermute | solution.py:437
  34.4 5.3 %collective-permute-start.10 = (bf16[256,128]{1,0:T(8,128)(2,1)S(1)}, bf16[256,128]{1,0:T(8,128)(2,1)S(1)}, u32[]{:S(2)}, u32[]{:S(2)}) collective-permute-start(bf16[256,128]{1,0:T(8,128)(2,1)S(1)} %fusion.2), channel_id=1, source_target_pairs={{0,4},{1,5},{2,6},{3,7},{4,0},{5,1},{6,2},{7,3},{8,12},{9,13},{10,... | collective-permute-start | bytes 196616 | tf_op jit(solution)/shard_map/ppermute | solution.py:437
  34.4 5.3 %collective-permute-start.9 = (bf16[256,128]{1,0:T(8,128)(2,1)S(1)}, bf16[256,128]{1,0:T(8,128)(2,1)S(1)}, u32[]{:S(2)}, u32[]{:S(2)}) collective-permute-start(bf16[256,128]{1,0:T(8,128)(2,1)S(1)} %fusion.2), channel_id=1, source_target_pairs={{0,2},{1,3},{2,0},{3,1},{4,6},{5,7},{6,4},{7,5},{8,10},{9,11},{10,... | collective-permute-start | bytes 196616 | tf_op jit(solution)/shard_map/ppermute | solution.py:437
  39.7 5.2 %collective-permute-start.14 = (bf16[256,128]{1,0:T(8,128)(2,1)S(1)}, bf16[256,128]{1,0:T(8,128)(2,1)S(1)}, u32[]{:S(2)}, u32[]{:S(2)}) collective-permute-start(bf16[256,128]{1,0:T(8,128)(2,1)S(1)} %add_convert_fusion), channel_id=1, source_target_pairs={{0,24},{1,25},{2,26},{3,27},{4,28},{5,29},{6,30},{7,31},{8,16},{9,... | collective-permute-start | bytes 196616 | tf_op jit(solution)/shard_map/ppermute | solution.py:414
  41.9 4.3 %collective-permute-start.13 = (bf16[256,128]{1,0:T(8,128)(2,1)S(1)}, bf16[256,128]{1,0:T(8,128)(2,1)S(1)}, u32[]{:S(2)}, u32[]{:S(2)}) collective-permute-start(bf16[256,128]{1,0:T(8,128)(2,1)S(1)} %add_convert_fusion), channel_id=1, source_target_pairs={{0,8},{1,17},{2,10},{3,19},{4,12},{5,21},{6,14},{7,23},{8,0},{9,25... | collective-permute-start | bytes 196616 | tf_op jit(solution)/shard_map/ppermute | solution.py:414
  42.1 4.3 %collective-permute-start.12 = (bf16[256,128]{1,0:T(8,128)(2,1)S(1)}, bf16[256,128]{1,0:T(8,128)(2,1)S(1)}, u32[]{:S(2)}, u32[]{:S(2)}) collective-permute-start(bf16[256,128]{1,0:T(8,128)(2,1)S(1)} %add_convert_fusion), channel_id=1, source_target_pairs={{0,16},{1,9},{2,18},{3,11},{4,20},{5,13},{6,22},{7,15},{8,24},{9,1... | collective-permute-start | bytes 196616 | tf_op jit(solution)/shard_map/ppermute | solution.py:414
  43.3 3.4 %collective-permute-start.15 = (bf16[256,128]{1,0:T(8,128)(2,1)S(1)}, bf16[256,128]{1,0:T(8,128)(2,1)S(1)}, u32[]{:S(2)}, u32[]{:S(2)}) collective-permute-start(bf16[256,128]{1,0:T(8,128)(2,1)S(1)} %add_convert_fusion), channel_id=1, source_target_pairs={{0,1},{1,0},{2,3},{3,2},{4,5},{5,4},{6,7},{7,6},{8,9},{9,8},{10,11... | collective-permute-start | bytes 196616 | tf_op jit(solution)/shard_map/ppermute | solution.py:443
  45.0 1.7 %collective-permute-start.18 = (bf16[256,128]{1,0:T(8,128)(2,1)S(1)}, bf16[256,128]{1,0:T(8,128)(2,1)S(1)}, u32[]{:S(2)}, u32[]{:S(2)}) collective-permute-start(bf16[256,128]{1,0:T(8,128)(2,1)S(1)} %collective-permute-done.14), channel_id=1, source_target_pairs={{0,1},{1,0},{2,3},{3,2},{4,5},{5,4},{6,7},{7,6},{8,9},{9,8},{10,11... | collective-permute-start | bytes 196616 | tf_op jit(solution)/shard_map/ppermute | solution.py:443
  46.1 1.3 %collective-permute-start.17 = (bf16[256,128]{1,0:T(8,128)(2,1)S(1)}, bf16[256,128]{1,0:T(8,128)(2,1)S(1)}, u32[]{:S(2)}, u32[]{:S(2)}) collective-permute-start(bf16[256,128]{1,0:T(8,128)(2,1)S(1)} %collective-permute-done.13), channel_id=1, source_target_pairs={{0,1},{1,0},{2,3},{3,2},{4,5},{5,4},{6,7},{7,6},{8,9},{9,8},{10,11... | collective-permute-start | bytes 196616 | tf_op jit(solution)/shard_map/ppermute | solution.py:443
  46.3 1.3 %collective-permute-start.16 = (bf16[256,128]{1,0:T(8,128)(2,1)S(1)}, bf16[256,128]{1,0:T(8,128)(2,1)S(1)}, u32[]{:S(2)}, u32[]{:S(2)}) collective-permute-start(bf16[256,128]{1,0:T(8,128)(2,1)S(1)} %collective-permute-done.12), channel_id=1, source_target_pairs={{0,1},{1,0},{2,3},{3,2},{4,5},{5,4},{6,7},{7,6},{8,9},{9,8},{10,11... | collective-permute-start | bytes 196616 | tf_op jit(solution)/shard_map/ppermute | solution.py:443

commit v5 on v4

--- a/solution.py
+++ b/solution.py
@@ -32,21 +32,22 @@
     return lax.dot_general(left, right, (((1,), (1,)), ((), ())), preferred_element_type=F32)
 
 
-def pack_kernel(pre, grad_out, head, tail, first_col, last_col, hold):
+def pack_kernel(flags, pre, grad_out, row_a, row_b, col_a, col_b, hold):
     rows, cols, c1 = pre.shape
     pooled, half = grad_out.shape[:2]
-    head[:cols] = pre[0]
-    head[cols:] = grad_out[0]
-    tail[:cols] = pre[rows - 1]
-    tail[cols:] = grad_out[pooled - 1]
-    for message, p, g in ((first_col, 0, 0), (last_col, cols - 16, half - 16)):
-        at = 0 if p == 0 else 15
-        hold[rows + pooled:] = jnp.zeros((hold.shape[0] - rows - pooled, c1), F32)
+    core, even = flags[2], flags[4]
+    for message, low in ((row_a, even == 0), (row_b, even == 1)):
+        message[:cols] = pre[jnp.where(low, 0, rows - 1)]
+        message[cols:] = grad_out[jnp.where(low, 0, pooled - 1)]
+    hold[:, rows + pooled:] = jnp.zeros((2, hold.shape[1] - rows - pooled, c1), F32)
+    for side, (p, g) in enumerate(((0, 0), (cols - 16, half - 16))):
+        at = 15 * side
         for r in range(rows):
-            hold[r:r + 1] = pre[r, p:p + 16].astype(F32)[at:at + 1]
+            hold[side, r:r + 1] = pre[r, p:p + 16].astype(F32)[at:at + 1]
         for i in range(pooled):
-            hold[rows + i:rows + i + 1] = grad_out[i, g:g + 16].astype(F32)[at:at + 1]
-        message[...] = hold[...].astype(BF16)
+            hold[side, rows + i:rows + i + 1] = grad_out[i, g:g + 16].astype(F32)[at:at + 1]
+    col_a[...] = hold[1 - core].astype(BF16)
+    col_b[...] = hold[core].astype(BF16)
 
 
 def one_at(where):
@@ -109,10 +110,13 @@
     return sum(m for t, m in enumerate(masks) if (index >> (len(masks) - 1 - t)) & 1)
 
 
-def middle_kernel(lats, flags, grad_out, top, bottom, left, right, slope, act_t, fields_t, taps,
-                  spread, own, other,
-                  grid, wide, prods, ends, line, side, sides, sums, corner, keep):
-    first, last, core = flags[0], flags[1], flags[2]
+def middle_kernel(lats, flags, grad_out, row_a, row_b, col_a, col_b, slope, act_t, fields_t, taps,
+                  spread, own, *rest):
+    sends, scratch = rest[:lats - 1], rest[lats - 1:]
+    grid, wide, prods, ends, line, side, sides, sums, corner, keep = scratch
+    first, last, core, band, even = (flags[k] for k in range(5))
+    top = jnp.where(even == 1, row_b[...], row_a[...])
+    bottom = jnp.where(even == 1, row_a[...], row_b[...])
     rows, half, c2 = slope.shape
     c1 = c2 // 2
     pooled = rows // 2
@@ -124,8 +128,8 @@
     grid[0, :half, :] = top[2 * half:, :].astype(F32)
     outside = jnp.where(last == 1, 0.0, 1.0)
     grid[pooled + 1, :half, :] = bottom[2 * half:, :].astype(F32) * outside
-    side[0] = left[...].astype(F32)
-    side[1] = right[...].astype(F32)
+    side[1 - core] = col_a[...].astype(F32)
+    side[core] = col_b[...].astype(F32)
     for i in range(pooled + 2):
         at = rows + i - 1
         if i == 0:
@@ -197,7 +201,7 @@
     unit = c0
     per_tap = c1 // unit
     count = 9 * per_tap + 9
-    held = own.shape[0]
+    block = own.shape[0]
 
     def put(k, value):
         keep[k * unit:(k + 1) * unit, :] = value
@@ -232,15 +236,17 @@
             even = got[:c0, (2 - b) * c1:(3 - b) * c1]
             odd = got[c0:, (3 - b) * c1:(4 - b) * c1]
             put(9 * per_tap + 3 * a + b, even + odd)
-    keep[count * unit:] = jnp.zeros((2 * held - count * unit, c1), F32)
-    band = flags[3]
-    block = held // lats
+    if lats * block > count * unit:
+        keep[count * unit:] = jnp.zeros((lats * block - count * unit, c1), F32)
     orders = [steps(lats, k) for k in range(2)]
     for index in range(lats):
         far = [distance(index, masks) for masks in orders]
-        for target, half_of in ((own, core), (other, 1 - core)):
-            piece_at = half_of * lats + (band ^ jnp.where(half_of == 0, far[0], far[1]))
-            target[index * block:(index + 1) * block] = keep[pl.ds(pl.multiple_of(piece_at * block, block), block), :]
+        at = (band ^ jnp.where(core == 0, far[0], far[1])) * block
+        value = keep[pl.ds(pl.multiple_of(at, block), block), :]
+        if index == 0:
+            own[...] = value
+        else:
+            sends[index - 1][...] = value.astype(BF16)
 
 
 def last_kernel(spread, taps, out, total, turned):
@@ -267,24 +273,26 @@
             out[2 * q + rp] = found[q * c0:(q + 1) * c0, rp * cols:(rp + 1) * cols]
 
 
-def gather_kernel(flags, mine, theirs, out_first, out_second):
+def gather_kernel(flags, blocks, out_first, out_second):
     band, core = flags[3], flags[2]
-    lats, rows, c1 = mine.shape
+    lats, rows, c1 = blocks.shape
     size = out_second.shape[0]
     total = size + out_first.shape[0]
-    for h in range(2):
-        masks = steps(lats, h)
-        for i in range(lats):
-            at = (h * lats + i) * rows
-            far = i ^ band
-            source = 0
+    orders = [steps(lats, k) for k in range(2)]
+    for i in range(lats):
+        at = i * rows
+        far = i ^ band
+        places = []
+        for masks in orders:
+            place = 0
             for m in masks:
-                source = 2 * source + (far // m) % 2
-            for out, base, end in ((out_second, 0, size), (out_first, size, total)):
-                low, high = max(at, base), min(at + rows, end)
-                if low < high:
-                    here, there = (x[source, low - at:high - at] for x in (mine, theirs))
-                    out[low - base:high - base] = jnp.where(core == h, here, there).astype(F32)
+                place = 2 * place + (far // m) % 2
+            places.append(place)
+        source = jnp.where(core == 0, places[0], places[1])
+        for out, base, end in ((out_second, 0, size), (out_first, size, total)):
+            low, high = max(at, base), min(at + rows, end)
+            if low < high:
+                out[low - base:high - base] = blocks[source, low - at:high - at].astype(F32)
 
 
 def vmem(count):
@@ -307,10 +315,12 @@
     depths = lons // 2
     band, place = lax.axis_index("lat"), lax.axis_index("lon")
     core = lax.rem(place, 2)
-    flags = jnp.stack([(band == 0).astype(jnp.int32), (band == lats - 1).astype(jnp.int32), core, band])
+    even = lax.rem(band, 2) == 0
+    flags = jnp.stack([(band == 0).astype(jnp.int32), (band == lats - 1).astype(jnp.int32), core, band,
+                       even.astype(jnp.int32)])
 
     edge = -(-(rows + pooled + 4) // 16) * 16
-    head, tail, first_col, last_col = pl.pallas_call(
+    row_a, row_b, col_a, col_b = pl.pallas_call(
         pack_kernel,
         out_shape=(
             shape((cols + half, c1), BF16),
@@ -318,17 +328,20 @@
             shape((edge, c1), BF16),
             shape((edge, c1), BF16),
         ),
-        in_specs=vmem(2),
+        in_specs=[pl.BlockSpec(memory_space=pltpu.SMEM)] + vmem(2),
         out_specs=tuple(vmem(4)),
         scratch_shapes=[
-            pltpu.VMEM((edge, c1), F32),
+            pltpu.VMEM((2, edge, c1), F32),
         ],
         compiler_params=params(50),
         cost_estimate=pl.CostEstimate(flops=1000, bytes_accessed=1 << 18, transcendentals=0),
-    )(pre_first, grad_out)
-    over = lax.ppermute(head, AREA, [(i, (i + lons // 2) % lons) for i in range(lons)])
-    down = lax.ppermute(tail, "lat", [(i, (i + 1) % lats) for i in range(lats)])
-    bottom = lax.ppermute(head, "lat", [(i, (i - 1) % lats) for i in range(lats)])
+    )(flags, pre_first, grad_out)
+    pairs = [(j, (j + lons // 2) % lons) for j in range(lons)]
+    for i in range(1, lats - 1, 2):
+        for j in range(lons):
+            pairs += [(i * lons + j, (i + 1) * lons + j), ((i + 1) * lons + j, i * lons + j)]
+    row_b = lax.ppermute(row_b, AREA, pairs)
+    row_a = lax.ppermute(row_a, "lat", [(i, i ^ 1) for i in range(lats)])
 
     slope, act_t = pl.pallas_call(
         local_kernel,
@@ -348,16 +361,19 @@
     )(pre_first)
 
     fields = jnp.transpose(inputs, (0, 2, 1))
-    over, down, bottom, slope, fields = lax.optimization_barrier((over, down, bottom, slope, fields))
-    top = jnp.where(band == 0, over, down)
-
-    def column(own_part, at):
-        p, g = at * (cols - 1), cols + at * (half - 1)
-        parts = [own_part[:rows + pooled], top[p:p + 1], bottom[p:p + 1], top[g:g + 1], bottom[g:g + 1]]
-        return jnp.concatenate(parts + [jnp.zeros((edge - rows - pooled - 4, c1), BF16)], 0)
-
-    left = lax.ppermute(column(last_col, 1), "lon", [(i, (i + 1) % lons) for i in range(lons)])
-    right = lax.ppermute(column(first_col, 0), "lon", [(i, (i - 1) % lons) for i in range(lons)])
+    row_a, row_b, slope, fields = lax.optimization_barrier((row_a, row_b, slope, fields))
+
+    def corners(at):
+        places = (at * (cols - 1), cols + at * (half - 1))
+        above, below = (jnp.where(even, one, two) for one, two in ((row_b, row_a), (row_a, row_b)))
+        return jnp.concatenate([part[p:p + 1] for p in places for part in (above, below)], 0)
+
+    low, high = corners(0), corners(1)
+    pad = jnp.zeros((edge - rows - pooled - 4, c1), BF16)
+    col_a = jnp.concatenate([col_a[:rows + pooled], jnp.where(core == 0, high, low), pad], 0)
+    col_b = jnp.concatenate([col_b[:rows + pooled], jnp.where(core == 0, low, high), pad], 0)
+    col_b = lax.ppermute(col_b, "lon", [(i, (i + 2 * (i % 2) - 1) % lons) for i in range(lons)])
+    col_a = lax.ppermute(col_a, "lon", [(i, i ^ 1) for i in range(lons)])
 
     fields_t, taps_first, taps_second = pl.pallas_call(
         layout_kernel,
@@ -372,22 +388,18 @@
         compiler_params=params(16),
         cost_estimate=pl.CostEstimate(flops=4 * rows * cols * c0 * cols, bytes_accessed=3 << 20, transcendentals=0),
     )(fields, w_first, w_second)
-    left, right, fields_t = lax.optimization_barrier((left, right, fields_t))
-
-    chips = lats * depths
-    size = 9 * (c1 + c0)
-    piece = -(-size // (2 * chips * 16)) * 16
-    held = chips * piece
+    col_a, col_b, fields_t = lax.optimization_barrier((col_a, col_b, fields_t))
+
+    block = -(-9 * (c1 + c0) // (16 * lats)) * 16
     span = half + EDGE
-    spread, own, other = pl.pallas_call(
+    spread, own, *sends = pl.pallas_call(
         functools.partial(middle_kernel, lats),
         out_shape=(
             shape((rows + 3, half, 4 * c1), BF16),
-            shape((held, c1), F32),
-            shape((held, c1), F32),
-        ),
+            shape((block, c1), F32),
+        ) + (shape((block, c1), BF16),) * (lats - 1),
         in_specs=[pl.BlockSpec(memory_space=pltpu.SMEM)] + vmem(9),
-        out_specs=tuple(vmem(3)),
+        out_specs=tuple(vmem(lats + 1)),
         scratch_shapes=[
             pltpu.VMEM((pooled + 2, span, c1), F32),
             pltpu.VMEM((pooled + 2, span, 4 * c1), BF16),
@@ -398,25 +410,21 @@
             pltpu.VMEM((2, edge, c1), F32),
             pltpu.VMEM((4, 2 * c1, 3 * c1), F32),
             pltpu.VMEM((2 * c1, 3 * c1), F32),
-            pltpu.VMEM((2 * held, c1), F32),
+            pltpu.VMEM((lats * block, c1), F32),
         ],
         compiler_params=params(16),
         cost_estimate=pl.CostEstimate(flops=2 * rows * cols * c1 * 9 * (2 * c1 + c0), bytes_accessed=8 << 20,
                                       transcendentals=0),
-    )(flags, grad_out, top, bottom, left, right, slope, act_t, fields_t, taps_second)
-
-    swap = [(i, i ^ 1) for i in range(lons)]
+    )(flags, grad_out, row_a, row_b, col_a, col_b, slope, act_t, fields_t, taps_second)
+
     orders = [steps(lats, k) for k in range(2)]
 
-    def along_lat(t, block):
+    def along_lat(t, value):
         far = [distance(t, masks) for masks in orders]
-        pairs = [(i * lons + j, (i ^ far[j % 2]) * lons + j) for i in range(lats) for j in range(lons)]
-        return lax.ppermute(block, AREA, pairs)
-
-    parts = (own + lax.ppermute(other, "lon", swap)).reshape(lats, held // lats, c1)
-    sent = [parts[t].astype(BF16) for t in range(1, lats)]
-    *sent, spread = lax.optimization_barrier((*sent, spread))
-    got = [along_lat(t + 1, block) for t, block in enumerate(sent)]
+        return lax.ppermute(value, AREA, [
+            (i * lons + j, (i ^ far[j % 2]) * lons + j) for i in range(lats) for j in range(lons)])
+
+    got = [along_lat(t + 1, value) for t, value in enumerate(sends)]
     grad_inputs = pl.pallas_call(
         last_kernel,
         out_shape=shape((rows, c0, cols), BF16),
@@ -430,27 +438,30 @@
         cost_estimate=pl.CostEstimate(flops=2 * rows * cols * c1 * 9 * c0, bytes_accessed=3 << 20, transcendentals=0),
     )(spread, taps_first)
     *got, grad_inputs = lax.optimization_barrier((*got, grad_inputs))
-    total = parts[0]
-    for block in got:
-        total = total + block.astype(F32)
+    total = own
+    for value in got:
+        total = total + value.astype(F32)
+    swap = [(i, i ^ 1) for i in range(lons)]
+    low, high = total[:block // 2], total[block // 2:]
+    total = jnp.where(core == 0, low, high) + lax.ppermute(jnp.where(core == 0, high, low), "lon", swap)
     part = total.astype(BF16)
-    blocks = [part] + [lax.ppermute(part, "lon", [(i, i ^ (2 * k)) for i in range(lons)]) for k in range(1, depths)]
-    blocks = [block.astype(F32) for block in blocks]
-    while len(blocks) > 1:
-        blocks = [blocks[k] + blocks[k + 1] for k in range(0, len(blocks), 2)]
-    block = blocks[0].astype(BF16)
-    mine = [block] + [along_lat(t, block) for t in range(1, lats)]
-    theirs = [lax.ppermute(block, "lon", swap) for block in mine]
-    mine, theirs = jnp.stack(mine, 0), jnp.stack(theirs, 0)
+    terms = [part] + [lax.ppermute(part, "lon", [(i, i ^ (2 * k)) for i in range(lons)]) for k in range(1, depths)]
+    terms = [term.astype(F32) for term in terms]
+    while len(terms) > 1:
+        terms = [terms[k] + terms[k + 1] for k in range(0, len(terms), 2)]
+    mine = terms[0].astype(BF16)
+    theirs = lax.ppermute(mine, "lon", swap)
+    whole = jnp.concatenate([jnp.where(core == 0, mine, theirs), jnp.where(core == 0, theirs, mine)], 0)
+    blocks = jnp.stack([whole] + [along_lat(t, whole) for t in range(1, lats)], 0)
 
     grad_w_first, grad_w_second = pl.pallas_call(
         gather_kernel,
         out_shape=(shape((9 * c0, c1), F32), shape((9 * c1, c1), F32)),
-        in_specs=[pl.BlockSpec(memory_space=pltpu.SMEM)] + vmem(2),
+        in_specs=[pl.BlockSpec(memory_space=pltpu.SMEM)] + vmem(1),
         out_specs=tuple(vmem(2)),
         compiler_params=params(8),
         cost_estimate=pl.CostEstimate(flops=1000, bytes_accessed=3 << 19, transcendentals=0),
-    )(flags, mine, theirs)
+    )(flags, blocks)
     return (jnp.transpose(grad_inputs, (0, 2, 1)), grad_w_first.reshape(w_first.shape),
             grad_w_second.reshape(w_second.shape))
 

time: 49.5 us -> 50.8 us (1.026)
  waiting for transfers between devices: 12 us -> 16.2 us
  starting transfers between devices: 24.5 us -> 21.1 us
    ppermute x16 -> x12, waiting for transfers between devices: 7.56 us -> 12.3 us  [the longest x6 6.89 us: along_lat(): lax.ppermute(value, AREA, [(i * lons + j, (i ^ far[j % 2]) * lons + j) fo...]
    ppermute x16 -> x12, starting transfers between devices: 20 us -> 16.6 us  [the longest x6 7.11 us: along_lat(): lax.ppermute(value, AREA, [(i * lons + j, (i ^ far[j % 2]) * lons + j) fo...]
    ppermute x3, waiting for transfers between devices: 4.44 us -> 3.89 us  [body(): lax.ppermute(part, 'lon', [(i, i ^ 2 * k) for i in range(lons)])]
    pallas_call x1, Pallas kernels: 0.04 us -> 0.56 us  [body(): pl.pallas_call(pack_kernel, out_shape=(shape((cols + half, c1), BF16), sh...]
  transfers between devices with their start and end apart: 19 -> 15, of which waited for: 12 -> 12; matrix products, arithmetic and copies ran while one was open for 0% -> 0% of each run, Pallas kernels for 7% -> 7%
where the time goes in v5:
time: 50.8 us; the launch traced here: 50.5 us
  starting transfers between devices  21.1 us (42%)
  waiting for transfers between devices  16.2 us (32%)
  Pallas kernels  8.92 us (18%)
  local copies, waits for them, and re-layouts  3.18 us (6%)
  between operations  0.82 us (2%)
    ppermute x6, starting transfers between devices, along_lat(): lax.ppermute(value, AREA, [(i * lons + j, (i ^ far[j % 2]) * lons + j) fo...  7.11 us
    ppermute x6, waiting for transfers between devices, along_lat(): lax.ppermute(value, AREA, [(i * lons + j, (i ^ far[j % 2]) * lons + j) fo...  6.89 us
    ppermute x1, starting transfers between devices, body(): row_b = lax.ppermute(row_b, AREA, pairs)  4.49 us
    ppermute x3, starting transfers between devices, body(): lax.ppermute(part, 'lon', [(i, i ^ 2 * k) for i in range(lons)])  4.45 us
    ppermute x3, waiting for transfers between devices, body(): lax.ppermute(part, 'lon', [(i, i ^ 2 * k) for i in range(lons)])  3.89 us
    pallas_call x1, Pallas kernels, body(): pl.pallas_call(functools.partial(middle_kernel, lats), out_shape=(shape((...  3.24 us
    ppermute x1, starting transfers between devices, body(): row_a = lax.ppermute(row_a, 'lat', [(i, i ^ 1) for i in range(lats)])  3 us
    unnamed x14, local copies, waits for them, and re-layouts  3 us
  transfers between devices with their start and end apart: 15, of which 12 were waited for; matrix products, arithmetic and copies ran while one was open for 0% of the time, Pallas kernels for 7%

profile of v5, /device:TPU:0, one launch (start us, length us, event | category | flops | bytes accessed | tf_op | source)
XLA Modules:
  0.0 50.5 jit_solution(3492097768923086844)
XLA Ops:
  0.6 0.1 stack.50.flags
  0.7 0.0 copy-start
  0.7 1.0 %copy-done = bf16[16,128,128]{2,1,0:T(8,128)(2,1)S(1)} copy-done((bf16[16,128,128]{2,1,0:T(8,128)(2,1)S(1)}, bf16[16,128,128]{2,1,0:T(8,128)(2,1)}, u32[]{:S(2)}) %copy-start) | copy-done | bytes 524312
  1.8 0.0 copy-start.5
  1.8 0.9 %copy-done.5 = bf16[8,64,128]{2,1,0:T(8,128)(2,1)S(1)} copy-done((bf16[8,64,128]{2,1,0:T(8,128)(2,1)S(1)}, bf16[8,64,128]{2,1,0:T(8,128)(2,1)}, u32[]{:S(2)}) %copy-start.5) | copy-done | bytes 131096
  2.7 0.0 copy-start.2
  2.7 0.0 copy-start.3
  2.7 0.0 copy-start.6
  2.7 0.6 %shard_map.76 = (bf16[192,128]{1,0:T(8,128)(2,1)S(1)}, bf16[192,128]{1,0:T(8,128)(2,1)S(1)}, bf16[32,128]{1,0:T(8,128)(2,1)S(1)}, bf16[32,128]{1,0:T(8,128)(2,1)S(1)}) custom-call(s32[5]{0:T(128)S(1)} %stack.50.flags, bf16[16,128,128]{2,1,0:T(8,128)(2,1)S(1)} %copy-done, bf16[8,64,128]{2,1,0:T(8,128)(2,1)S(1)} %copy-done.5), custom_call_target="tpu_custom_call" | custom-call | flops 1000 | bytes 262144 | tf_op jit(solution)/shard_map/pallas_call | solution.py:323
  3.3 3.0 %collective-permute-start = (bf16[192,128]{1,0:T(8,128)(2,1)S(1)}, bf16[192,128]{1,0:T(8,128)(2,1)S(1)}, u32[]{:S(2)}, u32[]{:S(2)}) collective-permute-start(bf16[192,128]{1,0:T(8,128)(2,1)S(1)} %get-tuple-element.30), channel_id=1, source_target_pairs={{0,8},{8,0},{16,24},{24,16},{1,9},{9,1},{17,25},{25,17},{2,10},{10... | collective-permute-start | bytes 147464 | tf_op jit(solution)/shard_map/ppermute | solution.py:344
  6.3 4.5 %collective-permute-start.1 = (bf16[192,128]{1,0:T(8,128)(2,1)S(1)}, bf16[192,128]{1,0:T(8,128)(2,1)S(1)}, u32[]{:S(2)}, u32[]{:S(2)}) collective-permute-start(bf16[192,128]{1,0:T(8,128)(2,1)S(1)} %get-tuple-element.31), channel_id=1, source_target_pairs={{0,4},{1,5},{2,6},{3,7},{4,0},{5,1},{6,2},{7,3},{8,16},{16,8},{9,1... | collective-permute-start | bytes 147464 | tf_op jit(solution)/shard_map/ppermute | solution.py:343
  10.8 0.1 pad.11.clone
  10.9 0.0 copy-start.1
  10.9 1.0 %copy-done.1 = bf16[16,128,128]{2,1,0:T(8,128)(2,1)S(1)} copy-done((bf16[16,128,128]{2,1,0:T(8,128)(2,1)S(1)}, bf16[16,128,128]{2,1,0:T(8,128)(2,1)}, u32[]{:S(2)}) %copy-start.1) | copy-done | bytes 524312
  11.9 0.0 copy-start.4
  11.9 0.9 %shard_map.77 = (f32[16,64,256]{2,1,0:T(8,128)S(1)}, bf16[2,256,512]{2,1,0:T(8,128)(2,1)S(1)}) custom-call(bf16[16,128,128]{2,1,0:T(8,128)(2,1)S(1)} %copy-done.1), custom_call_target="tpu_custom_call" | custom-call | flops 15728640 | bytes 2097152 | tf_op jit(solution)/shard_map/pallas_call | solution.py:346
  12.9 0.0 collective-permute-done.row_a
  12.9 0.4 collective-permute-done.1.row_b
  13.3 0.1 maximum_maximum_fusion.1
  13.4 1.9 %collective-permute-start.3 = (bf16[32,128]{1,0:T(8,128)(2,1)S(1)}, bf16[32,128]{1,0:T(8,128)(2,1)S(1)}, u32[]{:S(2)}, u32[]{:S(2)}) collective-permute-start(bf16[32,128]{1,0:T(8,128)(2,1)S(1)} %get-tuple-element.73), channel_id=1, source_target_pairs={{0,7},{1,2},{2,1},{3,4},{4,3},{5,6},{6,5},{7,0},{8,15},{9,10},{10,... | collective-permute-start | bytes 24584 | tf_op jit(solution)/shard_map/ppermute | solution.py:375
  15.3 0.0 collective-permute-start.2
  15.3 0.0 copy-done.2
  15.3 0.0 copy-done.3
  15.3 0.0 copy-done.4
  15.3 0.5 shard_map.78
  15.8 2.5 %collective-permute-done.3.col_b = bf16[32,128]{1,0:T(8,128)(2,1)S(1)} collective-permute-done((bf16[32,128]{1,0:T(8,128)(2,1)S(1)}, bf16[32,128]{1,0:T(8,128)(2,1)S(1)}, u32[]{:S(2)}, u32[]{:S(2)}) %collective-permute-start.3) | collective-permute-done | bytes 8224 | tf_op jit(solution)/shard_map/ppermute | solution.py:375
  18.3 0.0 collective-permute-done.2.col_a
  18.3 0.0 copy-done.6
  18.3 3.2 %shard_map.79 = (bf16[19,64,512]{2,1,0:T(8,128)(2,1)S(1)}, f32[432,128]{1,0:T(8,128)S(1)}, bf16[432,128]{1,0:T(8,128)(2,1)S(1)}, bf16[432,128]{1,0:T(8,128)(2,1)S(1)}, bf16[432,128]{1,0:T(8,128)(2,1)S(1)}) custom-call(s32[5]{0:T(128)S(1)} %stack.50.flags, bf16[8,64,128]{2,1,0:T(8,128)(2,1)S(1)} %copy-done.6, ...), custom_call_target="tpu_custom_call" | custom-call | flops 1509949440 | bytes 8388608 | tf_op jit(solution)/shard_map/pallas_call | solution.py:395
  21.5 1.5 %collective-permute-start.4 = (bf16[432,128]{1,0:T(8,128)(2,1)S(1)}, bf16[432,128]{1,0:T(8,128)(2,1)S(1)}, u32[]{:S(2)}, u32[]{:S(2)}) collective-permute-start(bf16[432,128]{1,0:T(8,128)(2,1)S(1)} %get-tuple-element.45), channel_id=1, source_target_pairs={{0,16},{1,9},{2,18},{3,11},{4,20},{5,13},{6,22},{7,15},{8,24},{9,1... | collective-permute-start | bytes 331784 | tf_op jit(solution)/shard_map/ppermute | solution.py:424
  23.0 0.0 collective-permute-start.5
  23.0 2.1 %collective-permute-start.6 = (bf16[432,128]{1,0:T(8,128)(2,1)S(1)}, bf16[432,128]{1,0:T(8,128)(2,1)S(1)}, u32[]{:S(2)}, u32[]{:S(2)}) collective-permute-start(bf16[432,128]{1,0:T(8,128)(2,1)S(1)} %get-tuple-element.47), channel_id=1, source_target_pairs={{0,24},{1,25},{2,26},{3,27},{4,28},{5,29},{6,30},{7,31},{8,16},{9,... | collective-permute-start | bytes 331784 | tf_op jit(solution)/shard_map/ppermute | solution.py:424
  25.1 2.2 %shard_map.80 = bf16[16,64,128]{2,1,0:T(8,128)(2,1)} custom-call(bf16[19,64,512]{2,1,0:T(8,128)(2,1)S(1)} %get-tuple-element.48.spread, bf16[384,512]{1,0:T(8,128)(2,1)S(1)} %get-tuple-element.49.taps), custom_call_target="tpu_custom_call" | custom-call | flops 301989888 | bytes 3145728 | tf_op jit(solution)/shard_map/pallas_call | solution.py:428
  27.3 0.0 collective-permute-done.4
  27.3 0.5 collective-permute-done.5
  27.7 1.2 %collective-permute-done.6 = bf16[432,128]{1,0:T(8,128)(2,1)S(1)} collective-permute-done((bf16[432,128]{1,0:T(8,128)(2,1)S(1)}, bf16[432,128]{1,0:T(8,128)(2,1)S(1)}, u32[]{:S(2)}, u32[]{:S(2)}) %collective-permute-start.6) | collective-permute-done | bytes 110624 | tf_op jit(solution)/shard_map/ppermute | solution.py:424
  29.0 0.1 convert_add_fusion
  29.1 0.1 collective-permute-start.7
  29.1 1.3 %collective-permute-done.7 = f32[216,128]{1,0:T(8,128)S(1)} collective-permute-done((f32[216,128]{1,0:T(8,128)S(1)}, f32[216,128]{1,0:T(8,128)S(1)}, u32[]{:S(2)}, u32[]{:S(2)}) %collective-permute-start.7) | collective-permute-done | bytes 110624 | tf_op jit(solution)/shard_map/ppermute | solution.py:446
  30.5 2.9 %collective-permute-start.10 = (bf16[216,128]{1,0:T(8,128)(2,1)S(1)}, bf16[216,128]{1,0:T(8,128)(2,1)S(1)}, u32[]{:S(2)}, u32[]{:S(2)}) collective-permute-start(bf16[216,128]{1,0:T(8,128)(2,1)S(1)} %add_convert_fusion.1), channel_id=1, source_target_pairs={{0,6},{1,7},{2,4},{3,5},{4,2},{5,3},{6,0},{7,1},{8,14},{9,15},{10,... | collective-permute-start | bytes 165896 | tf_op jit(solution)/shard_map/ppermute | solution.py:448
  33.4 0.0 collective-permute-start.9
  33.4 1.5 %collective-permute-start.8 = (bf16[216,128]{1,0:T(8,128)(2,1)S(1)}, bf16[216,128]{1,0:T(8,128)(2,1)S(1)}, u32[]{:S(2)}, u32[]{:S(2)}) collective-permute-start(bf16[216,128]{1,0:T(8,128)(2,1)S(1)} %add_convert_fusion.1), channel_id=1, source_target_pairs={{0,2},{1,3},{2,0},{3,1},{4,6},{5,7},{6,4},{7,5},{8,10},{9,11},{10,... | collective-permute-start | bytes 165896 | tf_op jit(solution)/shard_map/ppermute | solution.py:448
  34.9 2.0 %collective-permute-done.10 = bf16[216,128]{1,0:T(8,128)(2,1)S(1)} collective-permute-done((bf16[216,128]{1,0:T(8,128)(2,1)S(1)}, bf16[216,128]{1,0:T(8,128)(2,1)S(1)}, u32[]{:S(2)}, u32[]{:S(2)}) %collective-permute-start.10) | collective-permute-done | bytes 55328 | tf_op jit(solution)/shard_map/ppermute | solution.py:448
  36.9 1.8 %collective-permute-done.9 = bf16[216,128]{1,0:T(8,128)(2,1)S(1)} collective-permute-done((bf16[216,128]{1,0:T(8,128)(2,1)S(1)}, bf16[216,128]{1,0:T(8,128)(2,1)S(1)}, u32[]{:S(2)}, u32[]{:S(2)}) %collective-permute-start.9) | collective-permute-done | bytes 55328 | tf_op jit(solution)/shard_map/ppermute | solution.py:448
  38.7 0.1 collective-permute-done.8
  38.9 0.1 collective-permute-start.11
  38.9 1.2 %collective-permute-done.11 = bf16[216,128]{1,0:T(8,128)(2,1)S(1)} collective-permute-done((bf16[216,128]{1,0:T(8,128)(2,1)S(1)}, bf16[216,128]{1,0:T(8,128)(2,1)S(1)}, u32[]{:S(2)}, u32[]{:S(2)}) %collective-permute-start.11) | collective-permute-done | bytes 55328 | tf_op jit(solution)/shard_map/ppermute | solution.py:453
  40.2 1.6 %collective-permute-start.13 = (bf16[432,128]{1,0:T(8,128)(2,1)S(1)}, bf16[432,128]{1,0:T(8,128)(2,1)S(1)}, u32[]{:S(2)}, u32[]{:S(2)}) collective-permute-start(bf16[432,128]{1,0:T(8,128)(2,1)S(1)} %get-tuple-element.58), channel_id=1, source_target_pairs={{0,8},{1,17},{2,10},{3,19},{4,12},{5,21},{6,14},{7,23},{8,0},{9,25... | collective-permute-start | bytes 331784 | tf_op jit(solution)/shard_map/ppermute | solution.py:424
  41.8 0.6 %collective-permute-start.12 = (bf16[432,128]{1,0:T(8,128)(2,1)S(1)}, bf16[432,128]{1,0:T(8,128)(2,1)S(1)}, u32[]{:S(2)}, u32[]{:S(2)}) collective-permute-start(bf16[432,128]{1,0:T(8,128)(2,1)S(1)} %get-tuple-element.58), channel_id=1, source_target_pairs={{0,16},{1,9},{2,18},{3,11},{4,20},{5,13},{6,22},{7,15},{8,24},{9,1... | collective-permute-start | bytes 331784 | tf_op jit(solution)/shard_map/ppermute | solution.py:424
  42.4 1.4 %collective-permute-start.14 = (bf16[432,128]{1,0:T(8,128)(2,1)S(1)}, bf16[432,128]{1,0:T(8,128)(2,1)S(1)}, u32[]{:S(2)}, u32[]{:S(2)}) collective-permute-start(bf16[432,128]{1,0:T(8,128)(2,1)S(1)} %get-tuple-element.58), channel_id=1, source_target_pairs={{0,24},{1,25},{2,26},{3,27},{4,28},{5,29},{6,30},{7,31},{8,16},{9,... | collective-permute-start | bytes 331784 | tf_op jit(solution)/shard_map/ppermute | solution.py:424
  43.8 2.3 %collective-permute-done.13 = bf16[432,128]{1,0:T(8,128)(2,1)S(1)} collective-permute-done((bf16[432,128]{1,0:T(8,128)(2,1)S(1)}, bf16[432,128]{1,0:T(8,128)(2,1)S(1)}, u32[]{:S(2)}, u32[]{:S(2)}) %collective-permute-start.13) | collective-permute-done | bytes 110624 | tf_op jit(solution)/shard_map/ppermute | solution.py:424
  46.1 0.6 %collective-permute-done.12 = bf16[432,128]{1,0:T(8,128)(2,1)S(1)} collective-permute-done((bf16[432,128]{1,0:T(8,128)(2,1)S(1)}, bf16[432,128]{1,0:T(8,128)(2,1)S(1)}, u32[]{:S(2)}, u32[]{:S(2)}) %collective-permute-start.12) | collective-permute-done | bytes 110624 | tf_op jit(solution)/shard_map/ppermute | solution.py:424
  46.7 2.2 %collective-permute-done.14 = bf16[432,128]{1,0:T(8,128)(2,1)S(1)} collective-permute-done((bf16[432,128]{1,0:T(8,128)(2,1)S(1)}, bf16[432,128]{1,0:T(8,128)(2,1)S(1)}, u32[]{:S(2)}, u32[]{:S(2)}) %collective-permute-start.14) | collective-permute-done | bytes 110624 | tf_op jit(solution)/shard_map/ppermute | solution.py:424
  49.0 0.1 pad_maximum_fusion.blocks
  49.0 1.5 %shard_map.81 = (f32[576,128]{1,0:T(8,128)}, f32[1152,128]{1,0:T(8,128)}) custom-call(s32[5]{0:T(128)S(1)} %stack.50.flags, bf16[4,432,128]{2,1,0:T(8,128)(2,1)S(1)} %pad_maximum_fusion.blocks), custom_call_target="tpu_custom_call" | custom-call | flops 1000 | bytes 1572864 | tf_op jit(solution)/shard_map/pallas_call | solution.py:457
  (11 shorter events, 0.2 us)
Async XLA Ops:
  0.7 1.0 %copy-start = (bf16[16,128,128]{2,1,0:T(8,128)(2,1)S(1)}, bf16[16,128,128]{2,1,0:T(8,128)(2,1)}, u32[]{:S(2)}) copy-start(bf16[16,128,128]{2,1,0:T(8,128)(2,1)} %pre.3) | copy-start | bytes 1572868
  1.8 0.9 %copy-start.5 = (bf16[8,64,128]{2,1,0:T(8,128)(2,1)S(1)}, bf16[8,64,128]{2,1,0:T(8,128)(2,1)}, u32[]{:S(2)}) copy-start(bf16[8,64,128]{2,1,0:T(8,128)(2,1)} %grad_out.3) | copy-start | bytes 393220
  2.7 12.6 %copy-start.2 = (bf16[3,3,128,128]{3,2,1,0:T(8,128)(2,1)S(1)}, bf16[3,3,128,128]{3,2,1,0:T(8,128)(2,1)}, u32[]{:S(2)}) copy-start(bf16[3,3,128,128]{3,2,1,0:T(8,128)(2,1)} %w_second.1) | copy-start | bytes 884740
  2.7 12.6 %copy-start.3 = (bf16[16,128,64]{1,2,0:T(8,128)(2,1)S(1)}, bf16[16,128,64]{1,2,0:T(8,128)(2,1)}, u32[]{:S(2)}) copy-start(bf16[16,128,64]{1,2,0:T(8,128)(2,1)} %param.5) | copy-start | bytes 786436
  2.7 15.6 %copy-start.6 = (bf16[8,64,128]{2,1,0:T(8,128)(2,1)S(1)}, bf16[8,64,128]{2,1,0:T(8,128)(2,1)}, u32[]{:S(2)}) copy-start(bf16[8,64,128]{2,1,0:T(8,128)(2,1)} %grad_out.3) | copy-start | bytes 393220
  3.3 9.6 %collective-permute-start = (bf16[192,128]{1,0:T(8,128)(2,1)S(1)}, bf16[192,128]{1,0:T(8,128)(2,1)S(1)}, u32[]{:S(2)}, u32[]{:S(2)}) collective-permute-start(bf16[192,128]{1,0:T(8,128)(2,1)S(1)} %get-tuple-element.30), channel_id=1, source_target_pairs={{0,8},{8,0},{16,24},{24,16},{1,9},{9,1},{17,25},{25,17},{2,10},{10... | collective-permute-start | bytes 147464 | tf_op jit(solution)/shard_map/ppermute | solution.py:344
  6.3 7.0 %collective-permute-start.1 = (bf16[192,128]{1,0:T(8,128)(2,1)S(1)}, bf16[192,128]{1,0:T(8,128)(2,1)S(1)}, u32[]{:S(2)}, u32[]{:S(2)}) collective-permute-start(bf16[192,128]{1,0:T(8,128)(2,1)S(1)} %get-tuple-element.31), channel_id=1, source_target_pairs={{0,4},{1,5},{2,6},{3,7},{4,0},{5,1},{6,2},{7,3},{8,16},{16,8},{9,1... | collective-permute-start | bytes 147464 | tf_op jit(solution)/shard_map/ppermute | solution.py:343
  10.9 1.0 %copy-start.1 = (bf16[16,128,128]{2,1,0:T(8,128)(2,1)S(1)}, bf16[16,128,128]{2,1,0:T(8,128)(2,1)}, u32[]{:S(2)}) copy-start(bf16[16,128,128]{2,1,0:T(8,128)(2,1)} %pre.3) | copy-start | bytes 1572868
  11.9 3.4 %copy-start.4 = (bf16[3,3,64,128]{3,2,1,0:T(8,128)(2,1)S(1)}, bf16[3,3,64,128]{3,2,1,0:T(8,128)(2,1)}, u32[]{:S(2)}) copy-start(bf16[3,3,64,128]{3,2,1,0:T(8,128)(2,1)} %w_first.1) | copy-start | bytes 442372
  13.4 4.9 %collective-permute-start.3 = (bf16[32,128]{1,0:T(8,128)(2,1)S(1)}, bf16[32,128]{1,0:T(8,128)(2,1)S(1)}, u32[]{:S(2)}, u32[]{:S(2)}) collective-permute-start(bf16[32,128]{1,0:T(8,128)(2,1)S(1)} %get-tuple-element.73), channel_id=1, source_target_pairs={{0,7},{1,2},{2,1},{3,4},{4,3},{5,6},{6,5},{7,0},{8,15},{9,10},{10,... | collective-permute-start | bytes 24584 | tf_op jit(solution)/shard_map/ppermute | solution.py:375
  15.3 3.0 %collective-permute-start.2 = (bf16[32,128]{1,0:T(8,128)(2,1)S(1)}, bf16[32,128]{1,0:T(8,128)(2,1)S(1)}, u32[]{:S(2)}, u32[]{:S(2)}) collective-permute-start(bf16[32,128]{1,0:T(8,128)(2,1)S(1)} %get-tuple-element.74), channel_id=1, source_target_pairs={{0,1},{1,0},{2,3},{3,2},{4,5},{5,4},{6,7},{7,6},{8,9},{9,8},{10,11... | collective-permute-start | bytes 24584 | tf_op jit(solution)/shard_map/ppermute | solution.py:376
  21.5 5.8 %collective-permute-start.4 = (bf16[432,128]{1,0:T(8,128)(2,1)S(1)}, bf16[432,128]{1,0:T(8,128)(2,1)S(1)}, u32[]{:S(2)}, u32[]{:S(2)}) collective-permute-start(bf16[432,128]{1,0:T(8,128)(2,1)S(1)} %get-tuple-element.45), channel_id=1, source_target_pairs={{0,16},{1,9},{2,18},{3,11},{4,20},{5,13},{6,22},{7,15},{8,24},{9,1... | collective-permute-start | bytes 331784 | tf_op jit(solution)/shard_map/ppermute | solution.py:424
  23.0 4.7 %collective-permute-start.5 = (bf16[432,128]{1,0:T(8,128)(2,1)S(1)}, bf16[432,128]{1,0:T(8,128)(2,1)S(1)}, u32[]{:S(2)}, u32[]{:S(2)}) collective-permute-start(bf16[432,128]{1,0:T(8,128)(2,1)S(1)} %get-tuple-element.46), channel_id=1, source_target_pairs={{0,8},{1,17},{2,10},{3,19},{4,12},{5,21},{6,14},{7,23},{8,0},{9,25... | collective-permute-start | bytes 331784 | tf_op jit(solution)/shard_map/ppermute | solution.py:424
  23.0 6.0 %collective-permute-start.6 = (bf16[432,128]{1,0:T(8,128)(2,1)S(1)}, bf16[432,128]{1,0:T(8,128)(2,1)S(1)}, u32[]{:S(2)}, u32[]{:S(2)}) collective-permute-start(bf16[432,128]{1,0:T(8,128)(2,1)S(1)} %get-tuple-element.47), channel_id=1, source_target_pairs={{0,24},{1,25},{2,26},{3,27},{4,28},{5,29},{6,30},{7,31},{8,16},{9,... | collective-permute-start | bytes 331784 | tf_op jit(solution)/shard_map/ppermute | solution.py:424
  29.1 1.4 %collective-permute-start.7 = (f32[216,128]{1,0:T(8,128)S(1)}, f32[216,128]{1,0:T(8,128)S(1)}, u32[]{:S(2)}, u32[]{:S(2)}) collective-permute-start(f32[216,128]{1,0:T(8,128)S(1)} %slice_select_fusion), channel_id=1, source_target_pairs={{0,1},{1,0},{2,3},{3,2},{4,5},{5,4},{6,7},{7,6},{8,9},{9,8},{10,11... | collective-permute-start | bytes 331784 | tf_op jit(solution)/shard_map/ppermute | solution.py:446
  30.5 6.4 %collective-permute-start.10 = (bf16[216,128]{1,0:T(8,128)(2,1)S(1)}, bf16[216,128]{1,0:T(8,128)(2,1)S(1)}, u32[]{:S(2)}, u32[]{:S(2)}) collective-permute-start(bf16[216,128]{1,0:T(8,128)(2,1)S(1)} %add_convert_fusion.1), channel_id=1, source_target_pairs={{0,6},{1,7},{2,4},{3,5},{4,2},{5,3},{6,0},{7,1},{8,14},{9,15},{10,... | collective-permute-start | bytes 165896 | tf_op jit(solution)/shard_map/ppermute | solution.py:448
  33.4 5.3 %collective-permute-start.9 = (bf16[216,128]{1,0:T(8,128)(2,1)S(1)}, bf16[216,128]{1,0:T(8,128)(2,1)S(1)}, u32[]{:S(2)}, u32[]{:S(2)}) collective-permute-start(bf16[216,128]{1,0:T(8,128)(2,1)S(1)} %add_convert_fusion.1), channel_id=1, source_target_pairs={{0,4},{1,5},{2,6},{3,7},{4,0},{5,1},{6,2},{7,3},{8,12},{9,13},{10,... | collective-permute-start | bytes 165896 | tf_op jit(solution)/shard_map/ppermute | solution.py:448
  33.4 5.4 %collective-permute-start.8 = (bf16[216,128]{1,0:T(8,128)(2,1)S(1)}, bf16[216,128]{1,0:T(8,128)(2,1)S(1)}, u32[]{:S(2)}, u32[]{:S(2)}) collective-permute-start(bf16[216,128]{1,0:T(8,128)(2,1)S(1)} %add_convert_fusion.1), channel_id=1, source_target_pairs={{0,2},{1,3},{2,0},{3,1},{4,6},{5,7},{6,4},{7,5},{8,10},{9,11},{10,... | collective-permute-start | bytes 165896 | tf_op jit(solution)/shard_map/ppermute | solution.py:448
  38.9 1.3 %collective-permute-start.11 = (bf16[216,128]{1,0:T(8,128)(2,1)S(1)}, bf16[216,128]{1,0:T(8,128)(2,1)S(1)}, u32[]{:S(2)}, u32[]{:S(2)}) collective-permute-start(bf16[216,128]{1,0:T(8,128)(2,1)S(1)} %add_convert_fusion), channel_id=1, source_target_pairs={{0,1},{1,0},{2,3},{3,2},{4,5},{5,4},{6,7},{7,6},{8,9},{9,8},{10,11... | collective-permute-start | bytes 165896 | tf_op jit(solution)/shard_map/ppermute | solution.py:453
  40.2 5.9 %collective-permute-start.13 = (bf16[432,128]{1,0:T(8,128)(2,1)S(1)}, bf16[432,128]{1,0:T(8,128)(2,1)S(1)}, u32[]{:S(2)}, u32[]{:S(2)}) collective-permute-start(bf16[432,128]{1,0:T(8,128)(2,1)S(1)} %get-tuple-element.58), channel_id=1, source_target_pairs={{0,8},{1,17},{2,10},{3,19},{4,12},{5,21},{6,14},{7,23},{8,0},{9,25... | collective-permute-start | bytes 331784 | tf_op jit(solution)/shard_map/ppermute | solution.py:424
  41.8 5.0 %collective-permute-start.12 = (bf16[432,128]{1,0:T(8,128)(2,1)S(1)}, bf16[432,128]{1,0:T(8,128)(2,1)S(1)}, u32[]{:S(2)}, u32[]{:S(2)}) collective-permute-start(bf16[432,128]{1,0:T(8,128)(2,1)S(1)} %get-tuple-element.58), channel_id=1, source_target_pairs={{0,16},{1,9},{2,18},{3,11},{4,20},{5,13},{6,22},{7,15},{8,24},{9,1... | collective-permute-start | bytes 331784 | tf_op jit(solution)/shard_map/ppermute | solution.py:424
  42.4 6.6 %collective-permute-start.14 = (bf16[432,128]{1,0:T(8,128)(2,1)S(1)}, bf16[432,128]{1,0:T(8,128)(2,1)S(1)}, u32[]{:S(2)}, u32[]{:S(2)}) collective-permute-start(bf16[432,128]{1,0:T(8,128)(2,1)S(1)} %get-tuple-element.58), channel_id=1, source_target_pairs={{0,24},{1,25},{2,26},{3,27},{4,28},{5,29},{6,30},{7,31},{8,16},{9,... | collective-permute-start | bytes 331784 | tf_op jit(solution)/shard_map/ppermute | solution.py:424

commit v6 on v5

--- a/solution.py
+++ b/solution.py
@@ -32,11 +32,16 @@
     return lax.dot_general(left, right, (((1,), (1,)), ((), ())), preferred_element_type=F32)
 
 
-def pack_kernel(flags, pre, grad_out, row_a, row_b, col_a, col_b, hold):
+def position(lats):
+    band, place = lax.axis_index("lat"), lax.axis_index("lon")
+    return band, band == 0, band == lats - 1, lax.rem(band, 2) == 0, lax.rem(place, 2)
+
+
+def pack_kernel(lats, pre, grad_out, row_a, row_b, col_a, col_b, hold):
     rows, cols, c1 = pre.shape
     pooled, half = grad_out.shape[:2]
-    core, even = flags[2], flags[4]
-    for message, low in ((row_a, even == 0), (row_b, even == 1)):
+    _, _, _, even, core = position(lats)
+    for message, low in ((row_a, ~even), (row_b, even)):
         message[:cols] = pre[jnp.where(low, 0, rows - 1)]
         message[cols:] = grad_out[jnp.where(low, 0, pooled - 1)]
     hold[:, rows + pooled:] = jnp.zeros((2, hold.shape[1] - rows - pooled, c1), F32)
@@ -101,22 +106,12 @@
                     taps_first[start:start + c0, k * c1:(k + 1) * c1] = w_first[a, b]
 
 
-def steps(count, core):
-    bits = count.bit_length() - 1
-    return [1 << ((t + core) % bits) for t in range(bits)]
-
-
-def distance(index, masks):
-    return sum(m for t, m in enumerate(masks) if (index >> (len(masks) - 1 - t)) & 1)
-
-
-def middle_kernel(lats, flags, grad_out, row_a, row_b, col_a, col_b, slope, act_t, fields_t, taps,
-                  spread, own, *rest):
-    sends, scratch = rest[:lats - 1], rest[lats - 1:]
-    grid, wide, prods, ends, line, side, sides, sums, corner, keep = scratch
-    first, last, core, band, even = (flags[k] for k in range(5))
-    top = jnp.where(even == 1, row_b[...], row_a[...])
-    bottom = jnp.where(even == 1, row_a[...], row_b[...])
+def middle_kernel(lats, grad_out, row_a, row_b, col_a, col_b, slope, act_t, fields_t, taps,
+                  spread, own, other,
+                  grid, wide, prods, ends, line, side, sides, sums, corner, keep):
+    band, first, last, even, core = position(lats)
+    top = jnp.where(even, row_b[...], row_a[...])
+    bottom = jnp.where(even, row_a[...], row_b[...])
     rows, half, c2 = slope.shape
     c1 = c2 // 2
     pooled = rows // 2
@@ -126,7 +121,7 @@
     grid[:, half:, :] = jnp.zeros((pooled + 2, EDGE, c1), F32)
     grid[1:pooled + 1, :half, :] = grad_out[...].astype(F32)
     grid[0, :half, :] = top[2 * half:, :].astype(F32)
-    outside = jnp.where(last == 1, 0.0, 1.0)
+    outside = jnp.where(last, 0.0, 1.0)
     grid[pooled + 1, :half, :] = bottom[2 * half:, :].astype(F32) * outside
     side[1 - core] = col_a[...].astype(F32)
     side[core] = col_b[...].astype(F32)
@@ -149,7 +144,7 @@
     flat = wide[1:pooled + 1].reshape(pooled * (half + EDGE), 4 * c1)
     for a in range(3):
         prods[a] = dot_nt(flat, taps[a]).reshape(pooled, half + EDGE, c2)
-    fold = jnp.where(first == 1, taps[0], taps[2])
+    fold = jnp.where(first, taps[0], taps[2])
     ends[0] = dot_nt(wide[0], fold)
     ends[1] = dot_nt(wide[0], taps[1])
     ends[2] = dot_nt(wide[pooled + 1], taps[0])
@@ -189,8 +184,8 @@
     place(rows, final + prods[1, pooled - 1] + ends[2], slope[rows - 1], rows - 1)
     place(rows + 1, (final + ends[3] + ends[2]) * outside, halo_slope(bottom), rows + pooled + 1)
 
-    is_first = jnp.where(first == 1, 1.0, 0.0).astype(BF16)
-    not_first = jnp.where(first == 1, 0.0, 1.0).astype(BF16)
+    is_first = jnp.where(first, 1.0, 0.0).astype(BF16)
+    not_first = jnp.where(first, 0.0, 1.0).astype(BF16)
     above = wide[0, :half, :3 * c1]
     wide[0, :half, :3 * c1] = above * not_first
     for n, (pr, start) in enumerate(((0, 0), (0, 1), (1, 1), (1, 2))):
@@ -201,7 +196,8 @@
     unit = c0
     per_tap = c1 // unit
     count = 9 * per_tap + 9
-    block = own.shape[0]
+    held = own.shape[0]
+    block = held // lats
 
     def put(k, value):
         keep[k * unit:(k + 1) * unit, :] = value
@@ -236,17 +232,12 @@
             even = got[:c0, (2 - b) * c1:(3 - b) * c1]
             odd = got[c0:, (3 - b) * c1:(4 - b) * c1]
             put(9 * per_tap + 3 * a + b, even + odd)
-    if lats * block > count * unit:
-        keep[count * unit:] = jnp.zeros((lats * block - count * unit, c1), F32)
-    orders = [steps(lats, k) for k in range(2)]
-    for index in range(lats):
-        far = [distance(index, masks) for masks in orders]
-        at = (band ^ jnp.where(core == 0, far[0], far[1])) * block
-        value = keep[pl.ds(pl.multiple_of(at, block), block), :]
-        if index == 0:
-            own[...] = value
-        else:
-            sends[index - 1][...] = value.astype(BF16)
+    if 2 * held > count * unit:
+        keep[count * unit:] = jnp.zeros((2 * held - count * unit, c1), F32)
+    for target, half_of in ((own, core), (other, 1 - core)):
+        for far in range(lats):
+            at = half_of * held + (band ^ far) * block
+            target[far * block:(far + 1) * block] = keep[pl.ds(pl.multiple_of(at, block), block), :]
 
 
 def last_kernel(spread, taps, out, total, turned):
@@ -273,26 +264,19 @@
             out[2 * q + rp] = found[q * c0:(q + 1) * c0, rp * cols:(rp + 1) * cols]
 
 
-def gather_kernel(flags, blocks, out_first, out_second):
-    band, core = flags[3], flags[2]
-    lats, rows, c1 = blocks.shape
+def gather_kernel(mine, theirs, out_first, out_second):
+    lats, rows, c1 = mine.shape
+    band, _, _, _, core = position(lats)
     size = out_second.shape[0]
     total = size + out_first.shape[0]
-    orders = [steps(lats, k) for k in range(2)]
-    for i in range(lats):
-        at = i * rows
-        far = i ^ band
-        places = []
-        for masks in orders:
-            place = 0
-            for m in masks:
-                place = 2 * place + (far // m) % 2
-            places.append(place)
-        source = jnp.where(core == 0, places[0], places[1])
-        for out, base, end in ((out_second, 0, size), (out_first, size, total)):
-            low, high = max(at, base), min(at + rows, end)
-            if low < high:
-                out[low - base:high - base] = blocks[source, low - at:high - at].astype(F32)
+    for h in range(2):
+        for i in range(lats):
+            at = (h * lats + i) * rows
+            for out, base, end in ((out_second, 0, size), (out_first, size, total)):
+                low, high = max(at, base), min(at + rows, end)
+                if low < high:
+                    here, there = (x[i ^ band, low - at:high - at] for x in (mine, theirs))
+                    out[low - base:high - base] = jnp.where(core == h, here, there).astype(F32)
 
 
 def vmem(count):
@@ -316,26 +300,24 @@
     band, place = lax.axis_index("lat"), lax.axis_index("lon")
     core = lax.rem(place, 2)
     even = lax.rem(band, 2) == 0
-    flags = jnp.stack([(band == 0).astype(jnp.int32), (band == lats - 1).astype(jnp.int32), core, band,
-                       even.astype(jnp.int32)])
 
     edge = -(-(rows + pooled + 4) // 16) * 16
     row_a, row_b, col_a, col_b = pl.pallas_call(
-        pack_kernel,
+        functools.partial(pack_kernel, lats),
         out_shape=(
             shape((cols + half, c1), BF16),
             shape((cols + half, c1), BF16),
             shape((edge, c1), BF16),
             shape((edge, c1), BF16),
         ),
-        in_specs=[pl.BlockSpec(memory_space=pltpu.SMEM)] + vmem(2),
+        in_specs=vmem(2),
         out_specs=tuple(vmem(4)),
         scratch_shapes=[
             pltpu.VMEM((2, edge, c1), F32),
         ],
         compiler_params=params(50),
         cost_estimate=pl.CostEstimate(flops=1000, bytes_accessed=1 << 18, transcendentals=0),
-    )(flags, pre_first, grad_out)
+    )(pre_first, grad_out)
     pairs = [(j, (j + lons // 2) % lons) for j in range(lons)]
     for i in range(1, lats - 1, 2):
         for j in range(lons):
@@ -390,16 +372,18 @@
     )(fields, w_first, w_second)
     col_a, col_b, fields_t = lax.optimization_barrier((col_a, col_b, fields_t))
 
-    block = -(-9 * (c1 + c0) // (16 * lats)) * 16
+    block = -(-9 * (c1 + c0) // (32 * lats)) * 16
+    held = lats * block
     span = half + EDGE
-    spread, own, *sends = pl.pallas_call(
+    spread, own, other = pl.pallas_call(
         functools.partial(middle_kernel, lats),
         out_shape=(
             shape((rows + 3, half, 4 * c1), BF16),
-            shape((block, c1), F32),
-        ) + (shape((block, c1), BF16),) * (lats - 1),
-        in_specs=[pl.BlockSpec(memory_space=pltpu.SMEM)] + vmem(9),
-        out_specs=tuple(vmem(lats + 1)),
+            shape((held, c1), F32),
+            shape((held, c1), F32),
+        ),
+        in_specs=vmem(9),
+        out_specs=tuple(vmem(3)),
         scratch_shapes=[
             pltpu.VMEM((pooled + 2, span, c1), F32),
             pltpu.VMEM((pooled + 2, span, 4 * c1), BF16),
@@ -410,21 +394,22 @@
             pltpu.VMEM((2, edge, c1), F32),
             pltpu.VMEM((4, 2 * c1, 3 * c1), F32),
             pltpu.VMEM((2 * c1, 3 * c1), F32),
-            pltpu.VMEM((lats * block, c1), F32),
+            pltpu.VMEM((2 * held, c1), F32),
         ],
         compiler_params=params(16),
         cost_estimate=pl.CostEstimate(flops=2 * rows * cols * c1 * 9 * (2 * c1 + c0), bytes_accessed=8 << 20,
                                       transcendentals=0),
-    )(flags, grad_out, row_a, row_b, col_a, col_b, slope, act_t, fields_t, taps_second)
-
-    orders = [steps(lats, k) for k in range(2)]
-
-    def along_lat(t, value):
-        far = [distance(t, masks) for masks in orders]
-        return lax.ppermute(value, AREA, [
-            (i * lons + j, (i ^ far[j % 2]) * lons + j) for i in range(lats) for j in range(lons)])
-
-    got = [along_lat(t + 1, value) for t, value in enumerate(sends)]
+    )(grad_out, row_a, row_b, col_a, col_b, slope, act_t, fields_t, taps_second)
+
+    swap = [(i, i ^ 1) for i in range(lons)]
+
+    def along_lat(far, value):
+        return lax.ppermute(value, "lat", [(i, i ^ far) for i in range(lats)])
+
+    parts = (own + lax.ppermute(other, "lon", swap)).reshape(lats, block, c1)
+    sent = [parts[far].astype(BF16) for far in range(1, lats)]
+    *sent, spread = lax.optimization_barrier((*sent, spread))
+    got = [along_lat(far + 1, value) for far, value in enumerate(sent)]
     grad_inputs = pl.pallas_call(
         last_kernel,
         out_shape=shape((rows, c0, cols), BF16),
@@ -438,30 +423,26 @@
         cost_estimate=pl.CostEstimate(flops=2 * rows * cols * c1 * 9 * c0, bytes_accessed=3 << 20, transcendentals=0),
     )(spread, taps_first)
     *got, grad_inputs = lax.optimization_barrier((*got, grad_inputs))
-    total = own
+    total = parts[0]
     for value in got:
         total = total + value.astype(F32)
-    swap = [(i, i ^ 1) for i in range(lons)]
-    low, high = total[:block // 2], total[block // 2:]
-    total = jnp.where(core == 0, low, high) + lax.ppermute(jnp.where(core == 0, high, low), "lon", swap)
     part = total.astype(BF16)
     terms = [part] + [lax.ppermute(part, "lon", [(i, i ^ (2 * k)) for i in range(lons)]) for k in range(1, depths)]
     terms = [term.astype(F32) for term in terms]
     while len(terms) > 1:
         terms = [terms[k] + terms[k + 1] for k in range(0, len(terms), 2)]
-    mine = terms[0].astype(BF16)
+    part = terms[0].astype(BF16)
+    mine = jnp.stack([part] + [along_lat(far, part) for far in range(1, lats)], 0)
     theirs = lax.ppermute(mine, "lon", swap)
-    whole = jnp.concatenate([jnp.where(core == 0, mine, theirs), jnp.where(core == 0, theirs, mine)], 0)
-    blocks = jnp.stack([whole] + [along_lat(t, whole) for t in range(1, lats)], 0)
 
     grad_w_first, grad_w_second = pl.pallas_call(
         gather_kernel,
         out_shape=(shape((9 * c0, c1), F32), shape((9 * c1, c1), F32)),
-        in_specs=[pl.BlockSpec(memory_space=pltpu.SMEM)] + vmem(1),
+        in_specs=vmem(2),
         out_specs=tuple(vmem(2)),
         compiler_params=params(8),
         cost_estimate=pl.CostEstimate(flops=1000, bytes_accessed=3 << 19, transcendentals=0),
-    )(flags, blocks)
+    )(mine, theirs)
     return (jnp.transpose(grad_inputs, (0, 2, 1)), grad_w_first.reshape(w_first.shape),
             grad_w_second.reshape(w_second.shape))
 

time: 50.8 us -> 46.8 us (0.921)
  waiting for transfers between devices: 16.2 us -> 13.9 us
  Pallas kernels: 8.92 us -> 7.29 us
    ppermute x7, waiting for transfers between devices: 8.19 us -> 6.43 us  [the longest x6 4.62 us: along_lat(): return lax.ppermute(value, 'lat', [(i, i ^ far) for i in range(lats)])]
    ppermute x3, waiting for transfers between devices: 3.89 us -> 3.16 us  [body(): lax.ppermute(part, 'lon', [(i, i ^ 2 * k) for i in range(lons)])]
    pallas_call x1, Pallas kernels: 3.24 us -> 2.66 us  [body(): pl.pallas_call(functools.partial(middle_kernel, lats), out_shape=(shape((...]
    pallas_call x1, Pallas kernels: 0.56 us -> 0.03 us  [body(): pl.pallas_call(functools.partial(pack_kernel, lats), out_shape=(shape((co...]
  transfers between devices with their start and end apart: 15 -> 15, of which waited for: 12 -> 10; matrix products, arithmetic and copies ran while one was open for 0% -> 0% of each run, Pallas kernels for 7% -> 8%
where the time goes in v6:
time: 46.8 us; the launch traced here: 46.5 us
  starting transfers between devices  21.1 us (45%)
  waiting for transfers between devices  13.9 us (30%)
  Pallas kernels  7.29 us (16%)
  local copies, waits for them, and re-layouts  3.11 us (7%)
  between operations  0.8 us (2%)
    ppermute x6, starting transfers between devices, along_lat(): return lax.ppermute(value, 'lat', [(i, i ^ far) for i in range(lats)])  7.11 us
    ppermute x6, waiting for transfers between devices, along_lat(): return lax.ppermute(value, 'lat', [(i, i ^ far) for i in range(lats)])  4.62 us
    ppermute x1, starting transfers between devices, body(): row_b = lax.ppermute(row_b, AREA, pairs)  4.49 us
    ppermute x3, starting transfers between devices, body(): lax.ppermute(part, 'lon', [(i, i ^ 2 * k) for i in range(lons)])  4.45 us
    ppermute x3, waiting for transfers between devices, body(): lax.ppermute(part, 'lon', [(i, i ^ 2 * k) for i in range(lons)])  3.16 us
    ppermute x1, starting transfers between devices, body(): row_a = lax.ppermute(row_a, 'lat', [(i, i ^ 1) for i in range(lats)])  3 us
    unnamed x14, local copies, waits for them, and re-layouts  3 us
    pallas_call x1, Pallas kernels, body(): pl.pallas_call(functools.partial(middle_kernel, lats), out_shape=(shape((...  2.66 us
  transfers between devices with their start and end apart: 15, of which 10 were waited for; matrix products, arithmetic and copies ran while one was open for 0% of the time, Pallas kernels for 8%

profile of v6, /device:TPU:0, one launch (start us, length us, event | category | flops | bytes accessed | tf_op | source)
XLA Modules:
  0.0 46.5 jit_solution(16904437250590741803)
XLA Ops:
  0.6 0.0 copy-start
  0.6 1.0 %copy-done = bf16[16,128,128]{2,1,0:T(8,128)(2,1)S(1)} copy-done((bf16[16,128,128]{2,1,0:T(8,128)(2,1)S(1)}, bf16[16,128,128]{2,1,0:T(8,128)(2,1)}, u32[]{:S(2)}) %copy-start) | copy-done | bytes 524312
  1.7 0.0 copy-start.5
  1.7 0.9 %copy-done.5 = bf16[8,64,128]{2,1,0:T(8,128)(2,1)S(1)} copy-done((bf16[8,64,128]{2,1,0:T(8,128)(2,1)S(1)}, bf16[8,64,128]{2,1,0:T(8,128)(2,1)}, u32[]{:S(2)}) %copy-start.5) | copy-done | bytes 131096
  2.6 0.0 copy-start.2
  2.6 0.0 copy-start.3
  2.6 0.0 copy-start.4
  2.6 3.0 %collective-permute-start = (bf16[192,128]{1,0:T(8,128)(2,1)S(1)}, bf16[192,128]{1,0:T(8,128)(2,1)S(1)}, u32[]{:S(2)}, u32[]{:S(2)}) collective-permute-start(bf16[192,128]{1,0:T(8,128)(2,1)S(1)} %get-tuple-element.32), channel_id=1, source_target_pairs={{0,8},{8,0},{16,24},{24,16},{1,9},{9,1},{17,25},{25,17},{2,10},{10... | collective-permute-start | bytes 147464 | tf_op jit(solution)/shard_map/ppermute | solution.py:326
  5.6 4.5 %collective-permute-start.1 = (bf16[192,128]{1,0:T(8,128)(2,1)S(1)}, bf16[192,128]{1,0:T(8,128)(2,1)S(1)}, u32[]{:S(2)}, u32[]{:S(2)}) collective-permute-start(bf16[192,128]{1,0:T(8,128)(2,1)S(1)} %get-tuple-element.33), channel_id=1, source_target_pairs={{0,4},{1,5},{2,6},{3,7},{4,0},{5,1},{6,2},{7,3},{8,16},{16,8},{9,1... | collective-permute-start | bytes 147464 | tf_op jit(solution)/shard_map/ppermute | solution.py:325
  10.2 0.1 pad.9.clone
  10.2 0.0 copy-start.1
  10.2 1.0 %copy-done.1 = bf16[16,128,128]{2,1,0:T(8,128)(2,1)S(1)} copy-done((bf16[16,128,128]{2,1,0:T(8,128)(2,1)S(1)}, bf16[16,128,128]{2,1,0:T(8,128)(2,1)}, u32[]{:S(2)}) %copy-start.1) | copy-done | bytes 524312
  11.3 0.0 copy-start.6
  11.3 0.9 %shard_map.77 = (f32[16,64,256]{2,1,0:T(8,128)S(1)}, bf16[2,256,512]{2,1,0:T(8,128)(2,1)S(1)}) custom-call(bf16[16,128,128]{2,1,0:T(8,128)(2,1)S(1)} %copy-done.1), custom_call_target="tpu_custom_call" | custom-call | flops 15728640 | bytes 2097152 | tf_op jit(solution)/shard_map/pallas_call | solution.py:328
  12.2 0.0 collective-permute-done.row_a
  12.2 0.4 collective-permute-done.1.row_b
  12.7 0.1 maximum_maximum_fusion.1
  12.8 1.9 %collective-permute-start.3 = (bf16[32,128]{1,0:T(8,128)(2,1)S(1)}, bf16[32,128]{1,0:T(8,128)(2,1)S(1)}, u32[]{:S(2)}, u32[]{:S(2)}) collective-permute-start(bf16[32,128]{1,0:T(8,128)(2,1)S(1)} %get-tuple-element.78), channel_id=1, source_target_pairs={{0,7},{1,2},{2,1},{3,4},{4,3},{5,6},{6,5},{7,0},{8,15},{9,10},{10,... | collective-permute-start | bytes 24584 | tf_op jit(solution)/shard_map/ppermute | solution.py:357
  14.7 0.0 collective-permute-start.2
  14.7 0.0 copy-done.2
  14.7 0.0 copy-done.3
  14.7 0.0 copy-done.4
  14.7 0.5 %shard_map.78 = (bf16[128,1024]{1,0:T(8,128)(2,1)S(1)}, bf16[384,512]{1,0:T(8,128)(2,1)S(1)}, bf16[3,256,512]{2,1,0:T(8,128)(2,1)S(1)}) custom-call(bf16[16,64,128]{2,1,0:T(8,128)(2,1)S(1)} %bitcast.8, bf16[3,3,64,128]{3,2,1,0:T(8,128)(2,1)S(1)} %copy-done.4, bf16[3,3,128,128]{3,2,1,0:T(8,128)(2,1)S(1)} %copy-done.2), custom_call_target="tpu_custom_call" | custom-call | flops 67108864 | bytes 3145728 | tf_op jit(solution)/shard_map/pallas_call | solution.py:360
  15.2 2.5 %collective-permute-done.3.col_b = bf16[32,128]{1,0:T(8,128)(2,1)S(1)} collective-permute-done((bf16[32,128]{1,0:T(8,128)(2,1)S(1)}, bf16[32,128]{1,0:T(8,128)(2,1)S(1)}, u32[]{:S(2)}, u32[]{:S(2)}) %collective-permute-start.3) | collective-permute-done | bytes 8224 | tf_op jit(solution)/shard_map/ppermute | solution.py:357
  17.6 0.0 collective-permute-done.2.col_a
  17.6 0.0 copy-done.6
  17.6 2.7 %shard_map.79 = (bf16[19,64,512]{2,1,0:T(8,128)(2,1)S(1)}, f32[896,128]{1,0:T(8,128)S(1)}, f32[896,128]{1,0:T(8,128)S(1)}) custom-call(bf16[8,64,128]{2,1,0:T(8,128)(2,1)S(1)} %copy-done.6, bf16[192,128]{1,0:T(8,128)(2,1)S(1)} %collective-permute-done.row_a, bf16[192,128]{1,0:T(8,128)(2,1)S(1)} %collective-permute-done.1.row_b, ...), custom_call_target="tpu_custom_call" | custom-call | flops 1509949440 | bytes 8388608 | tf_op jit(solution)/shard_map/pallas_call | solution.py:378
  20.3 0.1 collective-permute-start.4
  20.4 1.8 %collective-permute-done.4 = f32[896,128]{1,0:T(8,128)S(1)} collective-permute-done((f32[896,128]{1,0:T(8,128)S(1)}, f32[896,128]{1,0:T(8,128)S(1)}, u32[]{:S(2)}, u32[]{:S(2)}) %collective-permute-start.4) | collective-permute-done | bytes 458784 | tf_op jit(solution)/shard_map/ppermute | solution.py:409
  22.2 0.1 fusion.3
  22.3 0.1 collective-permute-start.5
  22.4 1.4 %collective-permute-start.6 = (bf16[224,128]{1,0:T(8,128)(2,1)S(1)}, bf16[224,128]{1,0:T(8,128)(2,1)S(1)}, u32[]{:S(2)}, u32[]{:S(2)}) collective-permute-start(bf16[224,128]{1,0:T(8,128)(2,1)S(1)} %get-tuple-element.51), channel_id=1, source_target_pairs={{0,16},{8,24},{16,0},{24,8},{1,17},{9,25},{17,1},{25,9},{2,18},{10... | collective-permute-start | bytes 172040 | tf_op jit(solution)/shard_map/ppermute | solution.py:407
  23.8 2.0 %collective-permute-start.7 = (bf16[224,128]{1,0:T(8,128)(2,1)S(1)}, bf16[224,128]{1,0:T(8,128)(2,1)S(1)}, u32[]{:S(2)}, u32[]{:S(2)}) collective-permute-start(bf16[224,128]{1,0:T(8,128)(2,1)S(1)} %get-tuple-element.52), channel_id=1, source_target_pairs={{0,24},{8,16},{16,8},{24,0},{1,25},{9,17},{17,9},{25,1},{2,26},{10... | collective-permute-start | bytes 172040 | tf_op jit(solution)/shard_map/ppermute | solution.py:407
  25.8 2.2 %shard_map.80 = bf16[16,64,128]{2,1,0:T(8,128)(2,1)} custom-call(bf16[19,64,512]{2,1,0:T(8,128)(2,1)S(1)} %get-tuple-element.53.spread, bf16[384,512]{1,0:T(8,128)(2,1)S(1)} %get-tuple-element.54.taps), custom_call_target="tpu_custom_call" | custom-call | flops 301989888 | bytes 3145728 | tf_op jit(solution)/shard_map/pallas_call | solution.py:413
  28.0 0.0 collective-permute-done.5
  28.0 0.0 collective-permute-done.6
  28.0 0.9 %collective-permute-done.7 = bf16[224,128]{1,0:T(8,128)(2,1)S(1)} collective-permute-done((bf16[224,128]{1,0:T(8,128)(2,1)S(1)}, bf16[224,128]{1,0:T(8,128)(2,1)S(1)}, u32[]{:S(2)}, u32[]{:S(2)}) %collective-permute-start.7) | collective-permute-done | bytes 57376 | tf_op jit(solution)/shard_map/ppermute | solution.py:407
  28.9 1.9 %collective-permute-start.10 = (bf16[224,128]{1,0:T(8,128)(2,1)S(1)}, bf16[224,128]{1,0:T(8,128)(2,1)S(1)}, u32[]{:S(2)}, u32[]{:S(2)}) collective-permute-start(bf16[224,128]{1,0:T(8,128)(2,1)S(1)} %fusion.2), channel_id=1, source_target_pairs={{0,6},{1,7},{2,4},{3,5},{4,2},{5,3},{6,0},{7,1},{8,14},{9,15},{10,... | collective-permute-start | bytes 172040 | tf_op jit(solution)/shard_map/ppermute | solution.py:430
  30.8 0.0 collective-permute-start.9
  30.8 2.6 %collective-permute-start.8 = (bf16[224,128]{1,0:T(8,128)(2,1)S(1)}, bf16[224,128]{1,0:T(8,128)(2,1)S(1)}, u32[]{:S(2)}, u32[]{:S(2)}) collective-permute-start(bf16[224,128]{1,0:T(8,128)(2,1)S(1)} %fusion.2), channel_id=1, source_target_pairs={{0,2},{1,3},{2,0},{3,1},{4,6},{5,7},{6,4},{7,5},{8,10},{9,11},{10,... | collective-permute-start | bytes 172040 | tf_op jit(solution)/shard_map/ppermute | solution.py:430
  33.4 2.0 %collective-permute-done.10 = bf16[224,128]{1,0:T(8,128)(2,1)S(1)} collective-permute-done((bf16[224,128]{1,0:T(8,128)(2,1)S(1)}, bf16[224,128]{1,0:T(8,128)(2,1)S(1)}, u32[]{:S(2)}, u32[]{:S(2)}) %collective-permute-start.10) | collective-permute-done | bytes 57376 | tf_op jit(solution)/shard_map/ppermute | solution.py:430
  35.4 1.1 %collective-permute-done.9 = bf16[224,128]{1,0:T(8,128)(2,1)S(1)} collective-permute-done((bf16[224,128]{1,0:T(8,128)(2,1)S(1)}, bf16[224,128]{1,0:T(8,128)(2,1)S(1)}, u32[]{:S(2)}, u32[]{:S(2)}) %collective-permute-start.9) | collective-permute-done | bytes 57376 | tf_op jit(solution)/shard_map/ppermute | solution.py:430
  36.6 0.0 collective-permute-done.8
  36.6 2.1 %collective-permute-start.13 = (bf16[224,128]{1,0:T(8,128)(2,1)S(1)}, bf16[224,128]{1,0:T(8,128)(2,1)S(1)}, u32[]{:S(2)}, u32[]{:S(2)}) collective-permute-start(bf16[224,128]{1,0:T(8,128)(2,1)S(1)} %add_convert_fusion), channel_id=1, source_target_pairs={{0,24},{8,16},{16,8},{24,0},{1,25},{9,17},{17,9},{25,1},{2,26},{10... | collective-permute-start | bytes 172040 | tf_op jit(solution)/shard_map/ppermute | solution.py:407
  38.7 1.1 %collective-permute-start.12 = (bf16[224,128]{1,0:T(8,128)(2,1)S(1)}, bf16[224,128]{1,0:T(8,128)(2,1)S(1)}, u32[]{:S(2)}, u32[]{:S(2)}) collective-permute-start(bf16[224,128]{1,0:T(8,128)(2,1)S(1)} %add_convert_fusion), channel_id=1, source_target_pairs={{0,16},{8,24},{16,0},{24,8},{1,17},{9,25},{17,1},{25,9},{2,18},{10... | collective-permute-start | bytes 172040 | tf_op jit(solution)/shard_map/ppermute | solution.py:407
  39.7 0.4 collective-permute-start.11
  40.1 1.6 %collective-permute-done.13 = bf16[224,128]{1,0:T(8,128)(2,1)S(1)} collective-permute-done((bf16[224,128]{1,0:T(8,128)(2,1)S(1)}, bf16[224,128]{1,0:T(8,128)(2,1)S(1)}, u32[]{:S(2)}, u32[]{:S(2)}) %collective-permute-start.13) | collective-permute-done | bytes 57376 | tf_op jit(solution)/shard_map/ppermute | solution.py:407
  41.7 1.1 %collective-permute-done.12 = bf16[224,128]{1,0:T(8,128)(2,1)S(1)} collective-permute-done((bf16[224,128]{1,0:T(8,128)(2,1)S(1)}, bf16[224,128]{1,0:T(8,128)(2,1)S(1)}, u32[]{:S(2)}, u32[]{:S(2)}) %collective-permute-start.12) | collective-permute-done | bytes 57376 | tf_op jit(solution)/shard_map/ppermute | solution.py:407
  42.8 1.1 %collective-permute-done.11 = bf16[224,128]{1,0:T(8,128)(2,1)S(1)} collective-permute-done((bf16[224,128]{1,0:T(8,128)(2,1)S(1)}, bf16[224,128]{1,0:T(8,128)(2,1)S(1)}, u32[]{:S(2)}, u32[]{:S(2)}) %collective-permute-start.11) | collective-permute-done | bytes 57376 | tf_op jit(solution)/shard_map/ppermute | solution.py:407
  43.9 0.1 collective-permute-start.14
  44.0 1.5 %collective-permute-done.14.theirs = bf16[4,224,128]{2,1,0:T(8,128)(2,1)S(1)} collective-permute-done((bf16[4,224,128]{2,1,0:T(8,128)(2,1)S(1)}, bf16[4,224,128]{2,1,0:T(8,128)(2,1)S(1)}, u32[]{:S(2)}, u32[]{:S(2)}) %collective-permute-start.14) | collective-permute-done | bytes 229408 | tf_op jit(solution)/shard_map/ppermute | solution.py:436
  45.5 1.0 %shard_map.81 = (f32[576,128]{1,0:T(8,128)}, f32[1152,128]{1,0:T(8,128)}) custom-call(bf16[4,224,128]{2,1,0:T(8,128)(2,1)S(1)} %pad_maximum_fusion.mine, bf16[4,224,128]{2,1,0:T(8,128)(2,1)S(1)} %collective-permute-done.14.theirs), custom_call_target="tpu_custom_call" | custom-call | flops 1000 | bytes 1572864 | tf_op jit(solution)/shard_map/pallas_call | solution.py:438
  (11 shorter events, 0.2 us)
Async XLA Ops:
  0.6 1.0 %copy-start = (bf16[16,128,128]{2,1,0:T(8,128)(2,1)S(1)}, bf16[16,128,128]{2,1,0:T(8,128)(2,1)}, u32[]{:S(2)}) copy-start(bf16[16,128,128]{2,1,0:T(8,128)(2,1)} %pre.3) | copy-start | bytes 1572868
  1.7 0.9 %copy-start.5 = (bf16[8,64,128]{2,1,0:T(8,128)(2,1)S(1)}, bf16[8,64,128]{2,1,0:T(8,128)(2,1)}, u32[]{:S(2)}) copy-start(bf16[8,64,128]{2,1,0:T(8,128)(2,1)} %grad_out.3) | copy-start | bytes 393220
  2.6 12.1 %copy-start.2 = (bf16[3,3,128,128]{3,2,1,0:T(8,128)(2,1)S(1)}, bf16[3,3,128,128]{3,2,1,0:T(8,128)(2,1)}, u32[]{:S(2)}) copy-start(bf16[3,3,128,128]{3,2,1,0:T(8,128)(2,1)} %w_second.1) | copy-start | bytes 884740
  2.6 12.1 %copy-start.3 = (bf16[16,128,64]{1,2,0:T(8,128)(2,1)S(1)}, bf16[16,128,64]{1,2,0:T(8,128)(2,1)}, u32[]{:S(2)}) copy-start(bf16[16,128,64]{1,2,0:T(8,128)(2,1)} %param.5) | copy-start | bytes 786436
  2.6 12.1 %copy-start.4 = (bf16[3,3,64,128]{3,2,1,0:T(8,128)(2,1)S(1)}, bf16[3,3,64,128]{3,2,1,0:T(8,128)(2,1)}, u32[]{:S(2)}) copy-start(bf16[3,3,64,128]{3,2,1,0:T(8,128)(2,1)} %w_first.1) | copy-start | bytes 442372
  2.6 9.6 %collective-permute-start = (bf16[192,128]{1,0:T(8,128)(2,1)S(1)}, bf16[192,128]{1,0:T(8,128)(2,1)S(1)}, u32[]{:S(2)}, u32[]{:S(2)}) collective-permute-start(bf16[192,128]{1,0:T(8,128)(2,1)S(1)} %get-tuple-element.32), channel_id=1, source_target_pairs={{0,8},{8,0},{16,24},{24,16},{1,9},{9,1},{17,25},{25,17},{2,10},{10... | collective-permute-start | bytes 147464 | tf_op jit(solution)/shard_map/ppermute | solution.py:326
  5.6 7.0 %collective-permute-start.1 = (bf16[192,128]{1,0:T(8,128)(2,1)S(1)}, bf16[192,128]{1,0:T(8,128)(2,1)S(1)}, u32[]{:S(2)}, u32[]{:S(2)}) collective-permute-start(bf16[192,128]{1,0:T(8,128)(2,1)S(1)} %get-tuple-element.33), channel_id=1, source_target_pairs={{0,4},{1,5},{2,6},{3,7},{4,0},{5,1},{6,2},{7,3},{8,16},{16,8},{9,1... | collective-permute-start | bytes 147464 | tf_op jit(solution)/shard_map/ppermute | solution.py:325
  10.2 1.0 %copy-start.1 = (bf16[16,128,128]{2,1,0:T(8,128)(2,1)S(1)}, bf16[16,128,128]{2,1,0:T(8,128)(2,1)}, u32[]{:S(2)}) copy-start(bf16[16,128,128]{2,1,0:T(8,128)(2,1)} %pre.3) | copy-start | bytes 1572868
  11.3 6.4 %copy-start.6 = (bf16[8,64,128]{2,1,0:T(8,128)(2,1)S(1)}, bf16[8,64,128]{2,1,0:T(8,128)(2,1)}, u32[]{:S(2)}) copy-start(bf16[8,64,128]{2,1,0:T(8,128)(2,1)} %grad_out.3) | copy-start | bytes 393220
  12.8 4.9 %collective-permute-start.3 = (bf16[32,128]{1,0:T(8,128)(2,1)S(1)}, bf16[32,128]{1,0:T(8,128)(2,1)S(1)}, u32[]{:S(2)}, u32[]{:S(2)}) collective-permute-start(bf16[32,128]{1,0:T(8,128)(2,1)S(1)} %get-tuple-element.78), channel_id=1, source_target_pairs={{0,7},{1,2},{2,1},{3,4},{4,3},{5,6},{6,5},{7,0},{8,15},{9,10},{10,... | collective-permute-start | bytes 24584 | tf_op jit(solution)/shard_map/ppermute | solution.py:357
  14.7 3.0 %collective-permute-start.2 = (bf16[32,128]{1,0:T(8,128)(2,1)S(1)}, bf16[32,128]{1,0:T(8,128)(2,1)S(1)}, u32[]{:S(2)}, u32[]{:S(2)}) collective-permute-start(bf16[32,128]{1,0:T(8,128)(2,1)S(1)} %get-tuple-element.79), channel_id=1, source_target_pairs={{0,1},{1,0},{2,3},{3,2},{4,5},{5,4},{6,7},{7,6},{8,9},{9,8},{10,11... | collective-permute-start | bytes 24584 | tf_op jit(solution)/shard_map/ppermute | solution.py:358
  20.3 1.9 %collective-permute-start.4 = (f32[896,128]{1,0:T(8,128)S(1)}, f32[896,128]{1,0:T(8,128)S(1)}, u32[]{:S(2)}, u32[]{:S(2)}) collective-permute-start(f32[896,128]{1,0:T(8,128)S(1)} %get-tuple-element.48), channel_id=1, source_target_pairs={{0,1},{1,0},{2,3},{3,2},{4,5},{5,4},{6,7},{7,6},{8,9},{9,8},{10,11... | collective-permute-start | bytes 1376264 | tf_op jit(solution)/shard_map/ppermute | solution.py:409
  22.3 5.7 %collective-permute-start.5 = (bf16[224,128]{1,0:T(8,128)(2,1)S(1)}, bf16[224,128]{1,0:T(8,128)(2,1)S(1)}, u32[]{:S(2)}, u32[]{:S(2)}) collective-permute-start(bf16[224,128]{1,0:T(8,128)(2,1)S(1)} %get-tuple-element.50), channel_id=1, source_target_pairs={{0,8},{8,0},{16,24},{24,16},{1,9},{9,1},{17,25},{25,17},{2,10},{10... | collective-permute-start | bytes 172040 | tf_op jit(solution)/shard_map/ppermute | solution.py:407
  22.4 5.6 %collective-permute-start.6 = (bf16[224,128]{1,0:T(8,128)(2,1)S(1)}, bf16[224,128]{1,0:T(8,128)(2,1)S(1)}, u32[]{:S(2)}, u32[]{:S(2)}) collective-permute-start(bf16[224,128]{1,0:T(8,128)(2,1)S(1)} %get-tuple-element.51), channel_id=1, source_target_pairs={{0,16},{8,24},{16,0},{24,8},{1,17},{9,25},{17,1},{25,9},{2,18},{10... | collective-permute-start | bytes 172040 | tf_op jit(solution)/shard_map/ppermute | solution.py:407
  23.8 5.1 %collective-permute-start.7 = (bf16[224,128]{1,0:T(8,128)(2,1)S(1)}, bf16[224,128]{1,0:T(8,128)(2,1)S(1)}, u32[]{:S(2)}, u32[]{:S(2)}) collective-permute-start(bf16[224,128]{1,0:T(8,128)(2,1)S(1)} %get-tuple-element.52), channel_id=1, source_target_pairs={{0,24},{8,16},{16,8},{24,0},{1,25},{9,17},{17,9},{25,1},{2,26},{10... | collective-permute-start | bytes 172040 | tf_op jit(solution)/shard_map/ppermute | solution.py:407
  28.9 6.5 %collective-permute-start.10 = (bf16[224,128]{1,0:T(8,128)(2,1)S(1)}, bf16[224,128]{1,0:T(8,128)(2,1)S(1)}, u32[]{:S(2)}, u32[]{:S(2)}) collective-permute-start(bf16[224,128]{1,0:T(8,128)(2,1)S(1)} %fusion.2), channel_id=1, source_target_pairs={{0,6},{1,7},{2,4},{3,5},{4,2},{5,3},{6,0},{7,1},{8,14},{9,15},{10,... | collective-permute-start | bytes 172040 | tf_op jit(solution)/shard_map/ppermute | solution.py:430
  30.8 5.7 %collective-permute-start.9 = (bf16[224,128]{1,0:T(8,128)(2,1)S(1)}, bf16[224,128]{1,0:T(8,128)(2,1)S(1)}, u32[]{:S(2)}, u32[]{:S(2)}) collective-permute-start(bf16[224,128]{1,0:T(8,128)(2,1)S(1)} %fusion.2), channel_id=1, source_target_pairs={{0,4},{1,5},{2,6},{3,7},{4,0},{5,1},{6,2},{7,3},{8,12},{9,13},{10,... | collective-permute-start | bytes 172040 | tf_op jit(solution)/shard_map/ppermute | solution.py:430
  30.8 5.7 %collective-permute-start.8 = (bf16[224,128]{1,0:T(8,128)(2,1)S(1)}, bf16[224,128]{1,0:T(8,128)(2,1)S(1)}, u32[]{:S(2)}, u32[]{:S(2)}) collective-permute-start(bf16[224,128]{1,0:T(8,128)(2,1)S(1)} %fusion.2), channel_id=1, source_target_pairs={{0,2},{1,3},{2,0},{3,1},{4,6},{5,7},{6,4},{7,5},{8,10},{9,11},{10,... | collective-permute-start | bytes 172040 | tf_op jit(solution)/shard_map/ppermute | solution.py:430
  36.6 5.1 %collective-permute-start.13 = (bf16[224,128]{1,0:T(8,128)(2,1)S(1)}, bf16[224,128]{1,0:T(8,128)(2,1)S(1)}, u32[]{:S(2)}, u32[]{:S(2)}) collective-permute-start(bf16[224,128]{1,0:T(8,128)(2,1)S(1)} %add_convert_fusion), channel_id=1, source_target_pairs={{0,24},{8,16},{16,8},{24,0},{1,25},{9,17},{17,9},{25,1},{2,26},{10... | collective-permute-start | bytes 172040 | tf_op jit(solution)/shard_map/ppermute | solution.py:407
  38.7 4.2 %collective-permute-start.12 = (bf16[224,128]{1,0:T(8,128)(2,1)S(1)}, bf16[224,128]{1,0:T(8,128)(2,1)S(1)}, u32[]{:S(2)}, u32[]{:S(2)}) collective-permute-start(bf16[224,128]{1,0:T(8,128)(2,1)S(1)} %add_convert_fusion), channel_id=1, source_target_pairs={{0,16},{8,24},{16,0},{24,8},{1,17},{9,25},{17,1},{25,9},{2,18},{10... | collective-permute-start | bytes 172040 | tf_op jit(solution)/shard_map/ppermute | solution.py:407
  39.7 4.2 %collective-permute-start.11 = (bf16[224,128]{1,0:T(8,128)(2,1)S(1)}, bf16[224,128]{1,0:T(8,128)(2,1)S(1)}, u32[]{:S(2)}, u32[]{:S(2)}) collective-permute-start(bf16[224,128]{1,0:T(8,128)(2,1)S(1)} %add_convert_fusion), channel_id=1, source_target_pairs={{0,8},{8,0},{16,24},{24,16},{1,9},{9,1},{17,25},{25,17},{2,10},{10... | collective-permute-start | bytes 172040 | tf_op jit(solution)/shard_map/ppermute | solution.py:407
  43.9 1.6 %collective-permute-start.14 = (bf16[4,224,128]{2,1,0:T(8,128)(2,1)S(1)}, bf16[4,224,128]{2,1,0:T(8,128)(2,1)S(1)}, u32[]{:S(2)}, u32[]{:S(2)}) collective-permute-start(bf16[4,224,128]{2,1,0:T(8,128)(2,1)S(1)} %pad_maximum_fusion.mine), channel_id=1, source_target_pairs={{0,1},{1,0},{2,3},{3,2},{4,5},{5,4},{6,7},{7,6},{8,9},{9,8},{10,11... | collective-permute-start | bytes 688136 | tf_op jit(solution)/shard_map/ppermute | solution.py:436

commit v7 on v6

--- a/solution.py
+++ b/solution.py
@@ -35,6 +35,11 @@
 def position(lats):
     band, place = lax.axis_index("lat"), lax.axis_index("lon")
     return band, band == 0, band == lats - 1, lax.rem(band, 2) == 0, lax.rem(place, 2)
+
+
+def bases(lats, depths):
+    band, depth = lax.axis_index("lat"), lax.axis_index("lon") // 2
+    return (band, depth if lats == depths else band)
 
 
 def pack_kernel(lats, pre, grad_out, row_a, row_b, col_a, col_b, hold):
@@ -106,10 +111,10 @@
                     taps_first[start:start + c0, k * c1:(k + 1) * c1] = w_first[a, b]
 
 
-def middle_kernel(lats, grad_out, row_a, row_b, col_a, col_b, slope, act_t, fields_t, taps,
+def middle_kernel(lats, depths, grad_out, row_a, row_b, col_a, col_b, slope, act_t, fields_t, taps,
                   spread, own, other,
                   grid, wide, prods, ends, line, side, sides, sums, corner, keep):
-    band, first, last, even, core = position(lats)
+    _, first, last, even, core = position(lats)
     top = jnp.where(even, row_b[...], row_a[...])
     bottom = jnp.where(even, row_a[...], row_b[...])
     rows, half, c2 = slope.shape
@@ -234,9 +239,10 @@
             put(9 * per_tap + 3 * a + b, even + odd)
     if 2 * held > count * unit:
         keep[count * unit:] = jnp.zeros((2 * held - count * unit, c1), F32)
+    base = bases(lats, depths)
     for target, half_of in ((own, core), (other, 1 - core)):
         for far in range(lats):
-            at = half_of * held + (band ^ far) * block
+            at = half_of * held + (jnp.where(half_of == 0, base[0], base[1]) ^ far) * block
             target[far * block:(far + 1) * block] = keep[pl.ds(pl.multiple_of(at, block), block), :]
 
 
@@ -264,9 +270,10 @@
             out[2 * q + rp] = found[q * c0:(q + 1) * c0, rp * cols:(rp + 1) * cols]
 
 
-def gather_kernel(mine, theirs, out_first, out_second):
+def gather_kernel(depths, mine, theirs, out_first, out_second):
     lats, rows, c1 = mine.shape
-    band, _, _, _, core = position(lats)
+    core = position(lats)[4]
+    places = bases(lats, depths)
     size = out_second.shape[0]
     total = size + out_first.shape[0]
     for h in range(2):
@@ -275,7 +282,7 @@
             for out, base, end in ((out_second, 0, size), (out_first, size, total)):
                 low, high = max(at, base), min(at + rows, end)
                 if low < high:
-                    here, there = (x[i ^ band, low - at:high - at] for x in (mine, theirs))
+                    here, there = (x[i ^ places[h], low - at:high - at] for x in (mine, theirs))
                     out[low - base:high - base] = jnp.where(core == h, here, there).astype(F32)
 
 
@@ -376,7 +383,7 @@
     held = lats * block
     span = half + EDGE
     spread, own, other = pl.pallas_call(
-        functools.partial(middle_kernel, lats),
+        functools.partial(middle_kernel, lats, depths),
         out_shape=(
             shape((rows + 3, half, 4 * c1), BF16),
             shape((held, c1), F32),
@@ -402,14 +409,21 @@
     )(grad_out, row_a, row_b, col_a, col_b, slope, act_t, fields_t, taps_second)
 
     swap = [(i, i ^ 1) for i in range(lons)]
-
-    def along_lat(far, value):
-        return lax.ppermute(value, "lat", [(i, i ^ far) for i in range(lats)])
+    crossed = lats == depths
+
+    def exchange(value, far, outer):
+        pairs = []
+        for i in range(lats):
+            for j in range(lons):
+                over_lat = outer != (crossed and j % 2 == 1)
+                target = (i ^ far, j) if over_lat else (i, j ^ (2 * far))
+                pairs.append((i * lons + j, target[0] * lons + target[1]))
+        return lax.ppermute(value, AREA, pairs)
 
     parts = (own + lax.ppermute(other, "lon", swap)).reshape(lats, block, c1)
     sent = [parts[far].astype(BF16) for far in range(1, lats)]
     *sent, spread = lax.optimization_barrier((*sent, spread))
-    got = [along_lat(far + 1, value) for far, value in enumerate(sent)]
+    got = [exchange(value, far + 1, True) for far, value in enumerate(sent)]
     grad_inputs = pl.pallas_call(
         last_kernel,
         out_shape=shape((rows, c0, cols), BF16),
@@ -427,16 +441,16 @@
     for value in got:
         total = total + value.astype(F32)
     part = total.astype(BF16)
-    terms = [part] + [lax.ppermute(part, "lon", [(i, i ^ (2 * k)) for i in range(lons)]) for k in range(1, depths)]
+    terms = [part] + [exchange(part, far, False) for far in range(1, depths)]
     terms = [term.astype(F32) for term in terms]
     while len(terms) > 1:
         terms = [terms[k] + terms[k + 1] for k in range(0, len(terms), 2)]
     part = terms[0].astype(BF16)
-    mine = jnp.stack([part] + [along_lat(far, part) for far in range(1, lats)], 0)
+    mine = jnp.stack([part] + [exchange(part, far, True) for far in range(1, lats)], 0)
     theirs = lax.ppermute(mine, "lon", swap)
 
     grad_w_first, grad_w_second = pl.pallas_call(
-        gather_kernel,
+        functools.partial(gather_kernel, depths),
         out_shape=(shape((9 * c0, c1), F32), shape((9 * c1, c1), F32)),
         in_specs=vmem(2),
         out_specs=tuple(vmem(2)),

time: 46.8 us -> 47.4 us (1.013)
  waiting for transfers between devices: 13.9 us -> 14.5 us
    ppermute x9, waiting for transfers between devices: 7.79 us -> 8.4 us  [exchange(): return lax.ppermute(value, AREA, pairs)]
where the time goes in v7:
time: 47.4 us; the launch traced here: 47.1 us
  starting transfers between devices  21.1 us (45%)
  waiting for transfers between devices  14.5 us (31%)
  Pallas kernels  7.29 us (15%)
  local copies, waits for them, and re-layouts  3.11 us (7%)
  between operations  0.8 us (2%)
    ppermute x9, starting transfers between devices, exchange(): return lax.ppermute(value, AREA, pairs)  11.6 us
    ppermute x9, waiting for transfers between devices, exchange(): return lax.ppermute(value, AREA, pairs)  8.4 us
    ppermute x1, starting transfers between devices, body(): row_b = lax.ppermute(row_b, AREA, pairs)  4.49 us
    ppermute x1, starting transfers between devices, body(): row_a = lax.ppermute(row_a, 'lat', [(i, i ^ 1) for i in range(lats)])  3 us
    unnamed x14, local copies, waits for them, and re-layouts  3 us
    pallas_call x1, Pallas kernels, body(): pl.pallas_call(functools.partial(middle_kernel, lats, depths), out_shape=...  2.66 us
    ppermute x1, waiting for transfers between devices, body(): lax.ppermute(col_b, 'lon', [(i, (i + 2 * (i % 2) - 1) % lons) for i in ra...  2.47 us
    pallas_call x1, Pallas kernels, body(): pl.pallas_call(last_kernel, out_shape=shape((rows, c0, cols), BF16), in_s...  2.19 us
  transfers between devices with their start and end apart: 15, of which 10 were waited for; matrix products, arithmetic and copies ran while one was open for 0% of the time, Pallas kernels for 8%

profile of v7, /device:TPU:0, one launch (start us, length us, event | category | flops | bytes accessed | tf_op | source)
XLA Modules:
  0.0 47.1 jit_solution(3614226088953240334)
XLA Ops:
  0.6 0.0 copy-start
  0.6 1.0 %copy-done = bf16[16,128,128]{2,1,0:T(8,128)(2,1)S(1)} copy-done((bf16[16,128,128]{2,1,0:T(8,128)(2,1)S(1)}, bf16[16,128,128]{2,1,0:T(8,128)(2,1)}, u32[]{:S(2)}) %copy-start) | copy-done | bytes 524312
  1.7 0.0 copy-start.5
  1.7 0.9 %copy-done.5 = bf16[8,64,128]{2,1,0:T(8,128)(2,1)S(1)} copy-done((bf16[8,64,128]{2,1,0:T(8,128)(2,1)S(1)}, bf16[8,64,128]{2,1,0:T(8,128)(2,1)}, u32[]{:S(2)}) %copy-start.5) | copy-done | bytes 131096
  2.6 0.0 copy-start.2
  2.6 0.0 copy-start.3
  2.6 0.0 copy-start.4
  2.6 3.0 %collective-permute-start = (bf16[192,128]{1,0:T(8,128)(2,1)S(1)}, bf16[192,128]{1,0:T(8,128)(2,1)S(1)}, u32[]{:S(2)}, u32[]{:S(2)}) collective-permute-start(bf16[192,128]{1,0:T(8,128)(2,1)S(1)} %get-tuple-element.32), channel_id=1, source_target_pairs={{0,8},{8,0},{16,24},{24,16},{1,9},{9,1},{17,25},{25,17},{2,10},{10... | collective-permute-start | bytes 147464 | tf_op jit(solution)/shard_map/ppermute | solution.py:333
  5.6 4.5 %collective-permute-start.1 = (bf16[192,128]{1,0:T(8,128)(2,1)S(1)}, bf16[192,128]{1,0:T(8,128)(2,1)S(1)}, u32[]{:S(2)}, u32[]{:S(2)}) collective-permute-start(bf16[192,128]{1,0:T(8,128)(2,1)S(1)} %get-tuple-element.33), channel_id=1, source_target_pairs={{0,4},{1,5},{2,6},{3,7},{4,0},{5,1},{6,2},{7,3},{8,16},{16,8},{9,1... | collective-permute-start | bytes 147464 | tf_op jit(solution)/shard_map/ppermute | solution.py:332
  10.2 0.1 pad.9.clone
  10.2 0.0 copy-start.1
  10.2 1.0 %copy-done.1 = bf16[16,128,128]{2,1,0:T(8,128)(2,1)S(1)} copy-done((bf16[16,128,128]{2,1,0:T(8,128)(2,1)S(1)}, bf16[16,128,128]{2,1,0:T(8,128)(2,1)}, u32[]{:S(2)}) %copy-start.1) | copy-done | bytes 524312
  11.3 0.0 copy-start.6
  11.3 0.9 %shard_map.77 = (f32[16,64,256]{2,1,0:T(8,128)S(1)}, bf16[2,256,512]{2,1,0:T(8,128)(2,1)S(1)}) custom-call(bf16[16,128,128]{2,1,0:T(8,128)(2,1)S(1)} %copy-done.1), custom_call_target="tpu_custom_call" | custom-call | flops 15728640 | bytes 2097152 | tf_op jit(solution)/shard_map/pallas_call | solution.py:335
  12.2 0.0 collective-permute-done.row_a
  12.2 0.4 collective-permute-done.1.row_b
  12.7 0.1 maximum_maximum_fusion.1
  12.8 1.9 %collective-permute-start.3 = (bf16[32,128]{1,0:T(8,128)(2,1)S(1)}, bf16[32,128]{1,0:T(8,128)(2,1)S(1)}, u32[]{:S(2)}, u32[]{:S(2)}) collective-permute-start(bf16[32,128]{1,0:T(8,128)(2,1)S(1)} %get-tuple-element.78), channel_id=1, source_target_pairs={{0,7},{1,2},{2,1},{3,4},{4,3},{5,6},{6,5},{7,0},{8,15},{9,10},{10,... | collective-permute-start | bytes 24584 | tf_op jit(solution)/shard_map/ppermute | solution.py:364
  14.7 0.0 collective-permute-start.2
  14.7 0.0 copy-done.2
  14.7 0.0 copy-done.3
  14.7 0.0 copy-done.4
  14.7 0.5 shard_map.78
  15.2 2.5 %collective-permute-done.3.col_b = bf16[32,128]{1,0:T(8,128)(2,1)S(1)} collective-permute-done((bf16[32,128]{1,0:T(8,128)(2,1)S(1)}, bf16[32,128]{1,0:T(8,128)(2,1)S(1)}, u32[]{:S(2)}, u32[]{:S(2)}) %collective-permute-start.3) | collective-permute-done | bytes 8224 | tf_op jit(solution)/shard_map/ppermute | solution.py:364
  17.6 0.0 collective-permute-done.2.col_a
  17.6 0.0 copy-done.6
  17.6 2.7 %shard_map.79 = (bf16[19,64,512]{2,1,0:T(8,128)(2,1)S(1)}, f32[896,128]{1,0:T(8,128)S(1)}, f32[896,128]{1,0:T(8,128)S(1)}) custom-call(bf16[8,64,128]{2,1,0:T(8,128)(2,1)S(1)} %copy-done.6, bf16[192,128]{1,0:T(8,128)(2,1)S(1)} %collective-permute-done.row_a, bf16[192,128]{1,0:T(8,128)(2,1)S(1)} %collective-permute-done.1.row_b, ...), custom_call_target="tpu_custom_call" | custom-call | flops 1509949440 | bytes 8388608 | tf_op jit(solution)/shard_map/pallas_call | solution.py:385
  20.3 0.1 collective-permute-start.4
  20.4 1.8 %collective-permute-done.4 = f32[896,128]{1,0:T(8,128)S(1)} collective-permute-done((f32[896,128]{1,0:T(8,128)S(1)}, f32[896,128]{1,0:T(8,128)S(1)}, u32[]{:S(2)}, u32[]{:S(2)}) %collective-permute-start.4) | collective-permute-done | bytes 458784 | tf_op jit(solution)/shard_map/ppermute | solution.py:423
  22.2 0.1 fusion.3
  22.3 0.1 collective-permute-start.5
  22.4 1.4 %collective-permute-start.6 = (bf16[224,128]{1,0:T(8,128)(2,1)S(1)}, bf16[224,128]{1,0:T(8,128)(2,1)S(1)}, u32[]{:S(2)}, u32[]{:S(2)}) collective-permute-start(bf16[224,128]{1,0:T(8,128)(2,1)S(1)} %get-tuple-element.51), channel_id=1, source_target_pairs={{0,16},{1,5},{2,18},{3,7},{4,20},{5,1},{6,22},{7,3},{8,24},{9,13},... | collective-permute-start | bytes 172040 | tf_op jit(solution)/shard_map/ppermute | solution.py:421
  23.8 2.0 %collective-permute-start.7 = (bf16[224,128]{1,0:T(8,128)(2,1)S(1)}, bf16[224,128]{1,0:T(8,128)(2,1)S(1)}, u32[]{:S(2)}, u32[]{:S(2)}) collective-permute-start(bf16[224,128]{1,0:T(8,128)(2,1)S(1)} %get-tuple-element.52), channel_id=1, source_target_pairs={{0,24},{1,7},{2,26},{3,5},{4,28},{5,3},{6,30},{7,1},{8,16},{9,15},... | collective-permute-start | bytes 172040 | tf_op jit(solution)/shard_map/ppermute | solution.py:421
  25.8 2.2 %shard_map.80 = bf16[16,64,128]{2,1,0:T(8,128)(2,1)} custom-call(bf16[19,64,512]{2,1,0:T(8,128)(2,1)S(1)} %get-tuple-element.53.spread, bf16[384,512]{1,0:T(8,128)(2,1)S(1)} %get-tuple-element.54.taps), custom_call_target="tpu_custom_call" | custom-call | flops 301989888 | bytes 3145728 | tf_op jit(solution)/shard_map/pallas_call | solution.py:427
  28.0 0.0 collective-permute-done.5
  28.0 0.0 collective-permute-done.6
  28.0 0.9 %collective-permute-done.7 = bf16[224,128]{1,0:T(8,128)(2,1)S(1)} collective-permute-done((bf16[224,128]{1,0:T(8,128)(2,1)S(1)}, bf16[224,128]{1,0:T(8,128)(2,1)S(1)}, u32[]{:S(2)}, u32[]{:S(2)}) %collective-permute-start.7) | collective-permute-done | bytes 57376 | tf_op jit(solution)/shard_map/ppermute | solution.py:421
  28.9 1.9 %collective-permute-start.10 = (bf16[224,128]{1,0:T(8,128)(2,1)S(1)}, bf16[224,128]{1,0:T(8,128)(2,1)S(1)}, u32[]{:S(2)}, u32[]{:S(2)}) collective-permute-start(bf16[224,128]{1,0:T(8,128)(2,1)S(1)} %fusion.2), channel_id=1, source_target_pairs={{0,6},{1,25},{2,4},{3,27},{4,2},{5,29},{6,0},{7,31},{8,14},{9,17},... | collective-permute-start | bytes 172040 | tf_op jit(solution)/shard_map/ppermute | solution.py:421
  30.8 0.0 collective-permute-start.9
  30.8 2.6 %collective-permute-start.8 = (bf16[224,128]{1,0:T(8,128)(2,1)S(1)}, bf16[224,128]{1,0:T(8,128)(2,1)S(1)}, u32[]{:S(2)}, u32[]{:S(2)}) collective-permute-start(bf16[224,128]{1,0:T(8,128)(2,1)S(1)} %fusion.2), channel_id=1, source_target_pairs={{0,2},{1,9},{2,0},{3,11},{4,6},{5,13},{6,4},{7,15},{8,10},{9,1},{1... | collective-permute-start | bytes 172040 | tf_op jit(solution)/shard_map/ppermute | solution.py:421
  33.4 1.6 %collective-permute-done.10 = bf16[224,128]{1,0:T(8,128)(2,1)S(1)} collective-permute-done((bf16[224,128]{1,0:T(8,128)(2,1)S(1)}, bf16[224,128]{1,0:T(8,128)(2,1)S(1)}, u32[]{:S(2)}, u32[]{:S(2)}) %collective-permute-start.10) | collective-permute-done | bytes 57376 | tf_op jit(solution)/shard_map/ppermute | solution.py:421
  35.0 1.8 %collective-permute-done.9 = bf16[224,128]{1,0:T(8,128)(2,1)S(1)} collective-permute-done((bf16[224,128]{1,0:T(8,128)(2,1)S(1)}, bf16[224,128]{1,0:T(8,128)(2,1)S(1)}, u32[]{:S(2)}, u32[]{:S(2)}) %collective-permute-start.9) | collective-permute-done | bytes 57376 | tf_op jit(solution)/shard_map/ppermute | solution.py:421
  36.8 0.0 collective-permute-done.8
  36.9 2.1 %collective-permute-start.13 = (bf16[224,128]{1,0:T(8,128)(2,1)S(1)}, bf16[224,128]{1,0:T(8,128)(2,1)S(1)}, u32[]{:S(2)}, u32[]{:S(2)}) collective-permute-start(bf16[224,128]{1,0:T(8,128)(2,1)S(1)} %add_convert_fusion), channel_id=1, source_target_pairs={{0,24},{1,7},{2,26},{3,5},{4,28},{5,3},{6,30},{7,1},{8,16},{9,15},... | collective-permute-start | bytes 172040 | tf_op jit(solution)/shard_map/ppermute | solution.py:421
  38.9 1.4 %collective-permute-start.12 = (bf16[224,128]{1,0:T(8,128)(2,1)S(1)}, bf16[224,128]{1,0:T(8,128)(2,1)S(1)}, u32[]{:S(2)}, u32[]{:S(2)}) collective-permute-start(bf16[224,128]{1,0:T(8,128)(2,1)S(1)} %add_convert_fusion), channel_id=1, source_target_pairs={{0,16},{1,5},{2,18},{3,7},{4,20},{5,1},{6,22},{7,3},{8,24},{9,13},... | collective-permute-start | bytes 172040 | tf_op jit(solution)/shard_map/ppermute | solution.py:421
  40.3 0.1 collective-permute-start.11
  40.4 1.6 %collective-permute-done.13 = bf16[224,128]{1,0:T(8,128)(2,1)S(1)} collective-permute-done((bf16[224,128]{1,0:T(8,128)(2,1)S(1)}, bf16[224,128]{1,0:T(8,128)(2,1)S(1)}, u32[]{:S(2)}, u32[]{:S(2)}) %collective-permute-start.13) | collective-permute-done | bytes 57376 | tf_op jit(solution)/shard_map/ppermute | solution.py:421
  42.0 1.1 %collective-permute-done.12 = bf16[224,128]{1,0:T(8,128)(2,1)S(1)} collective-permute-done((bf16[224,128]{1,0:T(8,128)(2,1)S(1)}, bf16[224,128]{1,0:T(8,128)(2,1)S(1)}, u32[]{:S(2)}, u32[]{:S(2)}) %collective-permute-start.12) | collective-permute-done | bytes 57376 | tf_op jit(solution)/shard_map/ppermute | solution.py:421
  43.1 1.4 %collective-permute-done.11 = bf16[224,128]{1,0:T(8,128)(2,1)S(1)} collective-permute-done((bf16[224,128]{1,0:T(8,128)(2,1)S(1)}, bf16[224,128]{1,0:T(8,128)(2,1)S(1)}, u32[]{:S(2)}, u32[]{:S(2)}) %collective-permute-start.11) | collective-permute-done | bytes 57376 | tf_op jit(solution)/shard_map/ppermute | solution.py:421
  44.5 0.1 collective-permute-start.14
  44.6 1.5 %collective-permute-done.14.theirs = bf16[4,224,128]{2,1,0:T(8,128)(2,1)S(1)} collective-permute-done((bf16[4,224,128]{2,1,0:T(8,128)(2,1)S(1)}, bf16[4,224,128]{2,1,0:T(8,128)(2,1)S(1)}, u32[]{:S(2)}, u32[]{:S(2)}) %collective-permute-start.14) | collective-permute-done | bytes 229408 | tf_op jit(solution)/shard_map/ppermute | solution.py:450
  46.1 1.0 %shard_map.81 = (f32[576,128]{1,0:T(8,128)}, f32[1152,128]{1,0:T(8,128)}) custom-call(bf16[4,224,128]{2,1,0:T(8,128)(2,1)S(1)} %pad_maximum_fusion.mine, bf16[4,224,128]{2,1,0:T(8,128)(2,1)S(1)} %collective-permute-done.14.theirs), custom_call_target="tpu_custom_call" | custom-call | flops 1000 | bytes 1572864 | tf_op jit(solution)/shard_map/pallas_call | solution.py:452
  (11 shorter events, 0.2 us)
Async XLA Ops:
  0.6 1.0 %copy-start = (bf16[16,128,128]{2,1,0:T(8,128)(2,1)S(1)}, bf16[16,128,128]{2,1,0:T(8,128)(2,1)}, u32[]{:S(2)}) copy-start(bf16[16,128,128]{2,1,0:T(8,128)(2,1)} %pre.3) | copy-start | bytes 1572868
  1.7 0.9 %copy-start.5 = (bf16[8,64,128]{2,1,0:T(8,128)(2,1)S(1)}, bf16[8,64,128]{2,1,0:T(8,128)(2,1)}, u32[]{:S(2)}) copy-start(bf16[8,64,128]{2,1,0:T(8,128)(2,1)} %grad_out.3) | copy-start | bytes 393220
  2.6 12.1 %copy-start.2 = (bf16[3,3,128,128]{3,2,1,0:T(8,128)(2,1)S(1)}, bf16[3,3,128,128]{3,2,1,0:T(8,128)(2,1)}, u32[]{:S(2)}) copy-start(bf16[3,3,128,128]{3,2,1,0:T(8,128)(2,1)} %w_second.1) | copy-start | bytes 884740
  2.6 12.1 %copy-start.3 = (bf16[16,128,64]{1,2,0:T(8,128)(2,1)S(1)}, bf16[16,128,64]{1,2,0:T(8,128)(2,1)}, u32[]{:S(2)}) copy-start(bf16[16,128,64]{1,2,0:T(8,128)(2,1)} %param.5) | copy-start | bytes 786436
  2.6 12.1 %copy-start.4 = (bf16[3,3,64,128]{3,2,1,0:T(8,128)(2,1)S(1)}, bf16[3,3,64,128]{3,2,1,0:T(8,128)(2,1)}, u32[]{:S(2)}) copy-start(bf16[3,3,64,128]{3,2,1,0:T(8,128)(2,1)} %w_first.1) | copy-start | bytes 442372
  2.6 9.6 %collective-permute-start = (bf16[192,128]{1,0:T(8,128)(2,1)S(1)}, bf16[192,128]{1,0:T(8,128)(2,1)S(1)}, u32[]{:S(2)}, u32[]{:S(2)}) collective-permute-start(bf16[192,128]{1,0:T(8,128)(2,1)S(1)} %get-tuple-element.32), channel_id=1, source_target_pairs={{0,8},{8,0},{16,24},{24,16},{1,9},{9,1},{17,25},{25,17},{2,10},{10... | collective-permute-start | bytes 147464 | tf_op jit(solution)/shard_map/ppermute | solution.py:333
  5.6 7.0 %collective-permute-start.1 = (bf16[192,128]{1,0:T(8,128)(2,1)S(1)}, bf16[192,128]{1,0:T(8,128)(2,1)S(1)}, u32[]{:S(2)}, u32[]{:S(2)}) collective-permute-start(bf16[192,128]{1,0:T(8,128)(2,1)S(1)} %get-tuple-element.33), channel_id=1, source_target_pairs={{0,4},{1,5},{2,6},{3,7},{4,0},{5,1},{6,2},{7,3},{8,16},{16,8},{9,1... | collective-permute-start | bytes 147464 | tf_op jit(solution)/shard_map/ppermute | solution.py:332
  10.2 1.0 %copy-start.1 = (bf16[16,128,128]{2,1,0:T(8,128)(2,1)S(1)}, bf16[16,128,128]{2,1,0:T(8,128)(2,1)}, u32[]{:S(2)}) copy-start(bf16[16,128,128]{2,1,0:T(8,128)(2,1)} %pre.3) | copy-start | bytes 1572868
  11.3 6.4 %copy-start.6 = (bf16[8,64,128]{2,1,0:T(8,128)(2,1)S(1)}, bf16[8,64,128]{2,1,0:T(8,128)(2,1)}, u32[]{:S(2)}) copy-start(bf16[8,64,128]{2,1,0:T(8,128)(2,1)} %grad_out.3) | copy-start | bytes 393220
  12.8 4.9 %collective-permute-start.3 = (bf16[32,128]{1,0:T(8,128)(2,1)S(1)}, bf16[32,128]{1,0:T(8,128)(2,1)S(1)}, u32[]{:S(2)}, u32[]{:S(2)}) collective-permute-start(bf16[32,128]{1,0:T(8,128)(2,1)S(1)} %get-tuple-element.78), channel_id=1, source_target_pairs={{0,7},{1,2},{2,1},{3,4},{4,3},{5,6},{6,5},{7,0},{8,15},{9,10},{10,... | collective-permute-start | bytes 24584 | tf_op jit(solution)/shard_map/ppermute | solution.py:364
  14.7 3.0 %collective-permute-start.2 = (bf16[32,128]{1,0:T(8,128)(2,1)S(1)}, bf16[32,128]{1,0:T(8,128)(2,1)S(1)}, u32[]{:S(2)}, u32[]{:S(2)}) collective-permute-start(bf16[32,128]{1,0:T(8,128)(2,1)S(1)} %get-tuple-element.79), channel_id=1, source_target_pairs={{0,1},{1,0},{2,3},{3,2},{4,5},{5,4},{6,7},{7,6},{8,9},{9,8},{10,11... | collective-permute-start | bytes 24584 | tf_op jit(solution)/shard_map/ppermute | solution.py:365
  20.3 1.9 %collective-permute-start.4 = (f32[896,128]{1,0:T(8,128)S(1)}, f32[896,128]{1,0:T(8,128)S(1)}, u32[]{:S(2)}, u32[]{:S(2)}) collective-permute-start(f32[896,128]{1,0:T(8,128)S(1)} %get-tuple-element.48), channel_id=1, source_target_pairs={{0,1},{1,0},{2,3},{3,2},{4,5},{5,4},{6,7},{7,6},{8,9},{9,8},{10,11... | collective-permute-start | bytes 1376264 | tf_op jit(solution)/shard_map/ppermute | solution.py:423
  22.3 5.7 %collective-permute-start.5 = (bf16[224,128]{1,0:T(8,128)(2,1)S(1)}, bf16[224,128]{1,0:T(8,128)(2,1)S(1)}, u32[]{:S(2)}, u32[]{:S(2)}) collective-permute-start(bf16[224,128]{1,0:T(8,128)(2,1)S(1)} %get-tuple-element.50), channel_id=1, source_target_pairs={{0,8},{1,3},{2,10},{3,1},{4,12},{5,7},{6,14},{7,5},{8,0},{9,11},{1... | collective-permute-start | bytes 172040 | tf_op jit(solution)/shard_map/ppermute | solution.py:421
  22.4 5.6 %collective-permute-start.6 = (bf16[224,128]{1,0:T(8,128)(2,1)S(1)}, bf16[224,128]{1,0:T(8,128)(2,1)S(1)}, u32[]{:S(2)}, u32[]{:S(2)}) collective-permute-start(bf16[224,128]{1,0:T(8,128)(2,1)S(1)} %get-tuple-element.51), channel_id=1, source_target_pairs={{0,16},{1,5},{2,18},{3,7},{4,20},{5,1},{6,22},{7,3},{8,24},{9,13},... | collective-permute-start | bytes 172040 | tf_op jit(solution)/shard_map/ppermute | solution.py:421
  23.8 5.1 %collective-permute-start.7 = (bf16[224,128]{1,0:T(8,128)(2,1)S(1)}, bf16[224,128]{1,0:T(8,128)(2,1)S(1)}, u32[]{:S(2)}, u32[]{:S(2)}) collective-permute-start(bf16[224,128]{1,0:T(8,128)(2,1)S(1)} %get-tuple-element.52), channel_id=1, source_target_pairs={{0,24},{1,7},{2,26},{3,5},{4,28},{5,3},{6,30},{7,1},{8,16},{9,15},... | collective-permute-start | bytes 172040 | tf_op jit(solution)/shard_map/ppermute | solution.py:421
  28.9 6.0 %collective-permute-start.10 = (bf16[224,128]{1,0:T(8,128)(2,1)S(1)}, bf16[224,128]{1,0:T(8,128)(2,1)S(1)}, u32[]{:S(2)}, u32[]{:S(2)}) collective-permute-start(bf16[224,128]{1,0:T(8,128)(2,1)S(1)} %fusion.2), channel_id=1, source_target_pairs={{0,6},{1,25},{2,4},{3,27},{4,2},{5,29},{6,0},{7,31},{8,14},{9,17},... | collective-permute-start | bytes 172040 | tf_op jit(solution)/shard_map/ppermute | solution.py:421
  30.8 6.0 %collective-permute-start.9 = (bf16[224,128]{1,0:T(8,128)(2,1)S(1)}, bf16[224,128]{1,0:T(8,128)(2,1)S(1)}, u32[]{:S(2)}, u32[]{:S(2)}) collective-permute-start(bf16[224,128]{1,0:T(8,128)(2,1)S(1)} %fusion.2), channel_id=1, source_target_pairs={{0,4},{1,17},{2,6},{3,19},{4,0},{5,21},{6,2},{7,23},{8,12},{9,25},... | collective-permute-start | bytes 172040 | tf_op jit(solution)/shard_map/ppermute | solution.py:421
  30.8 6.0 %collective-permute-start.8 = (bf16[224,128]{1,0:T(8,128)(2,1)S(1)}, bf16[224,128]{1,0:T(8,128)(2,1)S(1)}, u32[]{:S(2)}, u32[]{:S(2)}) collective-permute-start(bf16[224,128]{1,0:T(8,128)(2,1)S(1)} %fusion.2), channel_id=1, source_target_pairs={{0,2},{1,9},{2,0},{3,11},{4,6},{5,13},{6,4},{7,15},{8,10},{9,1},{1... | collective-permute-start | bytes 172040 | tf_op jit(solution)/shard_map/ppermute | solution.py:421
  36.9 5.1 %collective-permute-start.13 = (bf16[224,128]{1,0:T(8,128)(2,1)S(1)}, bf16[224,128]{1,0:T(8,128)(2,1)S(1)}, u32[]{:S(2)}, u32[]{:S(2)}) collective-permute-start(bf16[224,128]{1,0:T(8,128)(2,1)S(1)} %add_convert_fusion), channel_id=1, source_target_pairs={{0,24},{1,7},{2,26},{3,5},{4,28},{5,3},{6,30},{7,1},{8,16},{9,15},... | collective-permute-start | bytes 172040 | tf_op jit(solution)/shard_map/ppermute | solution.py:421
  38.9 4.2 %collective-permute-start.12 = (bf16[224,128]{1,0:T(8,128)(2,1)S(1)}, bf16[224,128]{1,0:T(8,128)(2,1)S(1)}, u32[]{:S(2)}, u32[]{:S(2)}) collective-permute-start(bf16[224,128]{1,0:T(8,128)(2,1)S(1)} %add_convert_fusion), channel_id=1, source_target_pairs={{0,16},{1,5},{2,18},{3,7},{4,20},{5,1},{6,22},{7,3},{8,24},{9,13},... | collective-permute-start | bytes 172040 | tf_op jit(solution)/shard_map/ppermute | solution.py:421
  40.3 4.2 %collective-permute-start.11 = (bf16[224,128]{1,0:T(8,128)(2,1)S(1)}, bf16[224,128]{1,0:T(8,128)(2,1)S(1)}, u32[]{:S(2)}, u32[]{:S(2)}) collective-permute-start(bf16[224,128]{1,0:T(8,128)(2,1)S(1)} %add_convert_fusion), channel_id=1, source_target_pairs={{0,8},{1,3},{2,10},{3,1},{4,12},{5,7},{6,14},{7,5},{8,0},{9,11},{1... | collective-permute-start | bytes 172040 | tf_op jit(solution)/shard_map/ppermute | solution.py:421
  44.5 1.6 %collective-permute-start.14 = (bf16[4,224,128]{2,1,0:T(8,128)(2,1)S(1)}, bf16[4,224,128]{2,1,0:T(8,128)(2,1)S(1)}, u32[]{:S(2)}, u32[]{:S(2)}) collective-permute-start(bf16[4,224,128]{2,1,0:T(8,128)(2,1)S(1)} %pad_maximum_fusion.mine), channel_id=1, source_target_pairs={{0,1},{1,0},{2,3},{3,2},{4,5},{5,4},{6,7},{7,6},{8,9},{9,8},{10,11... | collective-permute-start | bytes 688136 | tf_op jit(solution)/shard_map/ppermute | solution.py:450

commit v8 on v6

--- a/solution.py
+++ b/solution.py
@@ -37,7 +37,7 @@
     return band, band == 0, band == lats - 1, lax.rem(band, 2) == 0, lax.rem(place, 2)
 
 
-def pack_kernel(lats, pre, grad_out, row_a, row_b, col_a, col_b, hold):
+def pack_kernel(lats, pre, grad_out, row_a, row_b, col_a, col_b, held, hold):
     rows, cols, c1 = pre.shape
     pooled, half = grad_out.shape[:2]
     _, _, _, even, core = position(lats)
@@ -53,6 +53,7 @@
             hold[side, rows + i:rows + i + 1] = grad_out[i, g:g + 16].astype(F32)[at:at + 1]
     col_a[...] = hold[1 - core].astype(BF16)
     col_b[...] = hold[core].astype(BF16)
+    held[...] = pre[...]
 
 
 def one_at(where):
@@ -302,16 +303,17 @@
     even = lax.rem(band, 2) == 0
 
     edge = -(-(rows + pooled + 4) // 16) * 16
-    row_a, row_b, col_a, col_b = pl.pallas_call(
+    row_a, row_b, col_a, col_b, held_pre = pl.pallas_call(
         functools.partial(pack_kernel, lats),
         out_shape=(
             shape((cols + half, c1), BF16),
             shape((cols + half, c1), BF16),
             shape((edge, c1), BF16),
             shape((edge, c1), BF16),
+            shape(pre_first.shape, BF16),
         ),
         in_specs=vmem(2),
-        out_specs=tuple(vmem(4)),
+        out_specs=tuple(vmem(5)),
         scratch_shapes=[
             pltpu.VMEM((2, edge, c1), F32),
         ],
@@ -322,8 +324,9 @@
     for i in range(1, lats - 1, 2):
         for j in range(lons):
             pairs += [(i * lons + j, (i + 1) * lons + j), ((i + 1) * lons + j, i * lons + j)]
+    every = [(i * lons + j, (i ^ 1) * lons + j) for i in range(lats) for j in range(lons)]
     row_b = lax.ppermute(row_b, AREA, pairs)
-    row_a = lax.ppermute(row_a, "lat", [(i, i ^ 1) for i in range(lats)])
+    row_a = lax.ppermute(row_a, AREA, every)
 
     slope, act_t = pl.pallas_call(
         local_kernel,
@@ -340,10 +343,10 @@
         compiler_params=params(16),
         cost_estimate=pl.CostEstimate(flops=60 * rows * cols * c1, bytes_accessed=2 << 20,
                                       transcendentals=2 * rows * cols * c1),
-    )(pre_first)
+    )(held_pre)
 
     fields = jnp.transpose(inputs, (0, 2, 1))
-    row_a, row_b, slope, fields = lax.optimization_barrier((row_a, row_b, slope, fields))
+    row_b, row_a, slope, fields = lax.optimization_barrier((row_b, row_a, slope, fields))
 
     def corners(at):
         places = (at * (cols - 1), cols + at * (half - 1))

time: 46.8 us -> 46 us (0.983)
  waiting for transfers between devices: 13.9 us -> 15.4 us
  starting transfers between devices: 21.1 us -> 19.9 us
  local copies, waits for them, and re-layouts: 3.11 us -> 2.06 us
    ppermute x1, starting transfers between devices: 3 us -> 0.46 us  [body(): row_a = lax.ppermute(row_a, AREA, every)]
    ppermute x1, starting transfers between devices: 4.49 us -> 6.08 us  [body(): row_b = lax.ppermute(row_b, AREA, pairs)]
    ppermute x1, waiting for transfers between devices: 0.01 us -> 1.57 us  [body(): row_a = lax.ppermute(row_a, AREA, every)]
    ppermute x1, starting transfers between devices: 1.91 us -> 0.71 us  [body(): lax.ppermute(col_b, 'lon', [(i, (i + 2 * (i % 2) - 1) % lons) for i in ra...]
    unnamed x14 -> x12, local copies, waits for them, and re-layouts: 3 us -> 1.95 us
    ppermute x6, waiting for transfers between devices: 4.62 us -> 3.61 us  [along_lat(): return lax.ppermute(value, 'lat', [(i, i ^ far) for i in range(lats)])]
    ppermute x1, starting transfers between devices: 0.01 us -> 0.99 us  [body(): col_a = lax.ppermute(col_a, 'lon', [(i, i ^ 1) for i in range(lons)])]
    ppermute x1, waiting for transfers between devices: 0.38 us -> 1.09 us  [body(): row_b = lax.ppermute(row_b, AREA, pairs)]
  transfers between devices with their start and end apart: 15 -> 15, of which waited for: 10 -> 11; matrix products, arithmetic and copies ran while one was open for 0% -> 0% of each run, Pallas kernels for 8% -> 8%
where the time goes in v8:
time: 46 us; the launch traced here: 45.8 us
  starting transfers between devices  19.9 us (43%)
  waiting for transfers between devices  15.4 us (33%)
  Pallas kernels  7.34 us (16%)
  local copies, waits for them, and re-layouts  2.06 us (4%)
  between operations  0.76 us (2%)
    ppermute x6, starting transfers between devices, along_lat(): return lax.ppermute(value, 'lat', [(i, i ^ far) for i in range(lats)])  7.11 us
    ppermute x1, starting transfers between devices, body(): row_b = lax.ppermute(row_b, AREA, pairs)  6.08 us
    ppermute x3, starting transfers between devices, body(): lax.ppermute(part, 'lon', [(i, i ^ 2 * k) for i in range(lons)])  4.45 us
    ppermute x6, waiting for transfers between devices, along_lat(): return lax.ppermute(value, 'lat', [(i, i ^ far) for i in range(lats)])  3.61 us
    ppermute x3, waiting for transfers between devices, body(): lax.ppermute(part, 'lon', [(i, i ^ 2 * k) for i in range(lons)])  3.15 us
    ppermute x1, waiting for transfers between devices, body(): lax.ppermute(col_b, 'lon', [(i, (i + 2 * (i % 2) - 1) % lons) for i in ra...  2.69 us
    pallas_call x1, Pallas kernels, body(): pl.pallas_call(functools.partial(middle_kernel, lats), out_shape=(shape((...  2.66 us
    pallas_call x1, Pallas kernels, body(): pl.pallas_call(last_kernel, out_shape=shape((rows, c0, cols), BF16), in_s...  2.19 us
  transfers between devices with their start and end apart: 15, of which 11 were waited for; matrix products, arithmetic and copies ran while one was open for 0% of the time, Pallas kernels for 8%

profile of v8, /device:TPU:0, one launch (start us, length us, event | category | flops | bytes accessed | tf_op | source)
XLA Modules:
  0.0 45.8 jit_solution(10007011771363548969)
XLA Ops:
  0.6 0.0 copy-start
  0.6 1.0 %copy-done = bf16[16,128,128]{2,1,0:T(8,128)(2,1)S(1)} copy-done((bf16[16,128,128]{2,1,0:T(8,128)(2,1)S(1)}, bf16[16,128,128]{2,1,0:T(8,128)(2,1)}, u32[]{:S(2)}) %copy-start) | copy-done | bytes 524312
  1.7 0.0 copy-start.4
  1.7 0.9 %copy-done.4 = bf16[8,64,128]{2,1,0:T(8,128)(2,1)S(1)} copy-done((bf16[8,64,128]{2,1,0:T(8,128)(2,1)S(1)}, bf16[8,64,128]{2,1,0:T(8,128)(2,1)}, u32[]{:S(2)}) %copy-start.4) | copy-done | bytes 131096
  2.6 0.0 copy-start.1
  2.6 0.0 copy-start.2
  2.6 0.0 copy-start.3
  2.6 0.0 copy-start.5
  2.6 0.1 shard_map.76
  2.7 6.1 %collective-permute-start = (bf16[192,128]{1,0:T(8,128)(2,1)S(1)}, bf16[192,128]{1,0:T(8,128)(2,1)S(1)}, u32[]{:S(2)}, u32[]{:S(2)}) collective-permute-start(bf16[192,128]{1,0:T(8,128)(2,1)S(1)} %get-tuple-element.33), channel_id=1, source_target_pairs={{0,4},{1,5},{2,6},{3,7},{4,0},{5,1},{6,2},{7,3},{8,16},{16,8},{9,1... | collective-permute-start | bytes 147464 | tf_op jit(solution)/shard_map/ppermute | solution.py:328
  8.7 0.5 %collective-permute-start.1 = (bf16[192,128]{1,0:T(8,128)(2,1)S(1)}, bf16[192,128]{1,0:T(8,128)(2,1)S(1)}, u32[]{:S(2)}, u32[]{:S(2)}) collective-permute-start(bf16[192,128]{1,0:T(8,128)(2,1)S(1)} %get-tuple-element.34), channel_id=1, source_target_pairs={{0,8},{1,9},{2,10},{3,11},{4,12},{5,13},{6,14},{7,15},{8,0},{9,1},... | collective-permute-start | bytes 147464 | tf_op jit(solution)/shard_map/ppermute | solution.py:329
  9.2 0.1 pad.9.clone
  9.3 0.9 %shard_map.77 = (f32[16,64,256]{2,1,0:T(8,128)S(1)}, bf16[2,256,512]{2,1,0:T(8,128)(2,1)S(1)}) custom-call(bf16[16,128,128]{2,1,0:T(8,128)(2,1)S(1)} %get-tuple-element.35.pre), custom_call_target="tpu_custom_call" | custom-call | flops 15728640 | bytes 2097152 | tf_op jit(solution)/shard_map/pallas_call | solution.py:331
  10.2 1.1 %collective-permute-done.row_b = bf16[192,128]{1,0:T(8,128)(2,1)S(1)} collective-permute-done((bf16[192,128]{1,0:T(8,128)(2,1)S(1)}, bf16[192,128]{1,0:T(8,128)(2,1)S(1)}, u32[]{:S(2)}, u32[]{:S(2)}) %collective-permute-start) | collective-permute-done | bytes 49184 | tf_op jit(solution)/shard_map/ppermute | solution.py:328
  11.3 1.6 %collective-permute-done.1.row_a = bf16[192,128]{1,0:T(8,128)(2,1)S(1)} collective-permute-done((bf16[192,128]{1,0:T(8,128)(2,1)S(1)}, bf16[192,128]{1,0:T(8,128)(2,1)S(1)}, u32[]{:S(2)}, u32[]{:S(2)}) %collective-permute-start.1) | collective-permute-done | bytes 49184 | tf_op jit(solution)/shard_map/ppermute | solution.py:329
  13.0 0.1 maximum_maximum_fusion.1
  13.0 0.7 %collective-permute-start.3 = (bf16[32,128]{1,0:T(8,128)(2,1)S(1)}, bf16[32,128]{1,0:T(8,128)(2,1)S(1)}, u32[]{:S(2)}, u32[]{:S(2)}) collective-permute-start(bf16[32,128]{1,0:T(8,128)(2,1)S(1)} %get-tuple-element.80), channel_id=1, source_target_pairs={{0,7},{1,2},{2,1},{3,4},{4,3},{5,6},{6,5},{7,0},{8,15},{9,10},{10,... | collective-permute-start | bytes 24584 | tf_op jit(solution)/shard_map/ppermute | solution.py:360
  13.7 1.0 %collective-permute-start.2 = (bf16[32,128]{1,0:T(8,128)(2,1)S(1)}, bf16[32,128]{1,0:T(8,128)(2,1)S(1)}, u32[]{:S(2)}, u32[]{:S(2)}) collective-permute-start(bf16[32,128]{1,0:T(8,128)(2,1)S(1)} %get-tuple-element.81), channel_id=1, source_target_pairs={{0,1},{1,0},{2,3},{3,2},{4,5},{5,4},{6,7},{7,6},{8,9},{9,8},{10,11... | collective-permute-start | bytes 24584 | tf_op jit(solution)/shard_map/ppermute | solution.py:361
  14.7 0.0 copy-done.1
  14.7 0.0 copy-done.2
  14.7 0.0 copy-done.3
  14.7 0.5 %shard_map.78 = (bf16[128,1024]{1,0:T(8,128)(2,1)S(1)}, bf16[384,512]{1,0:T(8,128)(2,1)S(1)}, bf16[3,256,512]{2,1,0:T(8,128)(2,1)S(1)}) custom-call(bf16[16,64,128]{2,1,0:T(8,128)(2,1)S(1)} %bitcast.8, bf16[3,3,64,128]{3,2,1,0:T(8,128)(2,1)S(1)} %copy-done.3, bf16[3,3,128,128]{3,2,1,0:T(8,128)(2,1)S(1)} %copy-done.1), custom_call_target="tpu_custom_call" | custom-call | flops 67108864 | bytes 3145728 | tf_op jit(solution)/shard_map/pallas_call | solution.py:363
  15.2 2.7 %collective-permute-done.3.col_b = bf16[32,128]{1,0:T(8,128)(2,1)S(1)} collective-permute-done((bf16[32,128]{1,0:T(8,128)(2,1)S(1)}, bf16[32,128]{1,0:T(8,128)(2,1)S(1)}, u32[]{:S(2)}, u32[]{:S(2)}) %collective-permute-start.3) | collective-permute-done | bytes 8224 | tf_op jit(solution)/shard_map/ppermute | solution.py:360
  17.9 0.0 collective-permute-done.2.col_a
  17.9 0.0 copy-done.5
  17.9 2.7 %shard_map.79 = (bf16[19,64,512]{2,1,0:T(8,128)(2,1)S(1)}, f32[896,128]{1,0:T(8,128)S(1)}, f32[896,128]{1,0:T(8,128)S(1)}) custom-call(bf16[8,64,128]{2,1,0:T(8,128)(2,1)S(1)} %copy-done.5, bf16[192,128]{1,0:T(8,128)(2,1)S(1)} %collective-permute-done.1.row_a, bf16[192,128]{1,0:T(8,128)(2,1)S(1)} %collective-permute-done.row_b, ...), custom_call_target="tpu_custom_call" | custom-call | flops 1509949440 | bytes 8388608 | tf_op jit(solution)/shard_map/pallas_call | solution.py:381
  20.6 0.1 collective-permute-start.4
  20.7 1.8 %collective-permute-done.4 = f32[896,128]{1,0:T(8,128)S(1)} collective-permute-done((f32[896,128]{1,0:T(8,128)S(1)}, f32[896,128]{1,0:T(8,128)S(1)}, u32[]{:S(2)}, u32[]{:S(2)}) %collective-permute-start.4) | collective-permute-done | bytes 458784 | tf_op jit(solution)/shard_map/ppermute | solution.py:412
  22.5 0.1 fusion.3
  22.6 0.5 collective-permute-start.5
  23.0 0.4 collective-permute-start.6
  23.4 2.7 %collective-permute-start.7 = (bf16[224,128]{1,0:T(8,128)(2,1)S(1)}, bf16[224,128]{1,0:T(8,128)(2,1)S(1)}, u32[]{:S(2)}, u32[]{:S(2)}) collective-permute-start(bf16[224,128]{1,0:T(8,128)(2,1)S(1)} %get-tuple-element.54), channel_id=1, source_target_pairs={{0,24},{8,16},{16,8},{24,0},{1,25},{9,17},{17,9},{25,1},{2,26},{10... | collective-permute-start | bytes 172040 | tf_op jit(solution)/shard_map/ppermute | solution.py:410
  26.1 2.2 %shard_map.80 = bf16[16,64,128]{2,1,0:T(8,128)(2,1)} custom-call(bf16[19,64,512]{2,1,0:T(8,128)(2,1)S(1)} %get-tuple-element.55.spread, bf16[384,512]{1,0:T(8,128)(2,1)S(1)} %get-tuple-element.56.taps), custom_call_target="tpu_custom_call" | custom-call | flops 301989888 | bytes 3145728 | tf_op jit(solution)/shard_map/pallas_call | solution.py:416
  28.3 0.0 collective-permute-done.5
  28.3 0.0 collective-permute-done.6
  28.3 0.2 collective-permute-done.7
  28.5 2.0 %collective-permute-start.10 = (bf16[224,128]{1,0:T(8,128)(2,1)S(1)}, bf16[224,128]{1,0:T(8,128)(2,1)S(1)}, u32[]{:S(2)}, u32[]{:S(2)}) collective-permute-start(bf16[224,128]{1,0:T(8,128)(2,1)S(1)} %fusion.2), channel_id=1, source_target_pairs={{0,6},{1,7},{2,4},{3,5},{4,2},{5,3},{6,0},{7,1},{8,14},{9,15},{10,... | collective-permute-start | bytes 172040 | tf_op jit(solution)/shard_map/ppermute | solution.py:433
  30.5 0.0 collective-permute-start.9
  30.5 2.5 %collective-permute-start.8 = (bf16[224,128]{1,0:T(8,128)(2,1)S(1)}, bf16[224,128]{1,0:T(8,128)(2,1)S(1)}, u32[]{:S(2)}, u32[]{:S(2)}) collective-permute-start(bf16[224,128]{1,0:T(8,128)(2,1)S(1)} %fusion.2), channel_id=1, source_target_pairs={{0,2},{1,3},{2,0},{3,1},{4,6},{5,7},{6,4},{7,5},{8,10},{9,11},{10,... | collective-permute-start | bytes 172040 | tf_op jit(solution)/shard_map/ppermute | solution.py:433
  33.0 1.9 %collective-permute-done.10 = bf16[224,128]{1,0:T(8,128)(2,1)S(1)} collective-permute-done((bf16[224,128]{1,0:T(8,128)(2,1)S(1)}, bf16[224,128]{1,0:T(8,128)(2,1)S(1)}, u32[]{:S(2)}, u32[]{:S(2)}) %collective-permute-start.10) | collective-permute-done | bytes 57376 | tf_op jit(solution)/shard_map/ppermute | solution.py:433
  35.0 1.2 %collective-permute-done.9 = bf16[224,128]{1,0:T(8,128)(2,1)S(1)} collective-permute-done((bf16[224,128]{1,0:T(8,128)(2,1)S(1)}, bf16[224,128]{1,0:T(8,128)(2,1)S(1)}, u32[]{:S(2)}, u32[]{:S(2)}) %collective-permute-start.9) | collective-permute-done | bytes 57376 | tf_op jit(solution)/shard_map/ppermute | solution.py:433
  36.2 0.0 collective-permute-done.8
  36.2 2.3 %collective-permute-start.13 = (bf16[224,128]{1,0:T(8,128)(2,1)S(1)}, bf16[224,128]{1,0:T(8,128)(2,1)S(1)}, u32[]{:S(2)}, u32[]{:S(2)}) collective-permute-start(bf16[224,128]{1,0:T(8,128)(2,1)S(1)} %add_convert_fusion), channel_id=1, source_target_pairs={{0,24},{8,16},{16,8},{24,0},{1,25},{9,17},{17,9},{25,1},{2,26},{10... | collective-permute-start | bytes 172040 | tf_op jit(solution)/shard_map/ppermute | solution.py:410
  38.4 0.5 %collective-permute-start.12 = (bf16[224,128]{1,0:T(8,128)(2,1)S(1)}, bf16[224,128]{1,0:T(8,128)(2,1)S(1)}, u32[]{:S(2)}, u32[]{:S(2)}) collective-permute-start(bf16[224,128]{1,0:T(8,128)(2,1)S(1)} %add_convert_fusion), channel_id=1, source_target_pairs={{0,16},{8,24},{16,0},{24,8},{1,17},{9,25},{17,1},{25,9},{2,18},{10... | collective-permute-start | bytes 172040 | tf_op jit(solution)/shard_map/ppermute | solution.py:410
  39.0 0.8 %collective-permute-start.11 = (bf16[224,128]{1,0:T(8,128)(2,1)S(1)}, bf16[224,128]{1,0:T(8,128)(2,1)S(1)}, u32[]{:S(2)}, u32[]{:S(2)}) collective-permute-start(bf16[224,128]{1,0:T(8,128)(2,1)S(1)} %add_convert_fusion), channel_id=1, source_target_pairs={{0,8},{8,0},{16,24},{24,16},{1,9},{9,1},{17,25},{25,17},{2,10},{10... | collective-permute-start | bytes 172040 | tf_op jit(solution)/shard_map/ppermute | solution.py:410
  39.7 1.6 %collective-permute-done.13 = bf16[224,128]{1,0:T(8,128)(2,1)S(1)} collective-permute-done((bf16[224,128]{1,0:T(8,128)(2,1)S(1)}, bf16[224,128]{1,0:T(8,128)(2,1)S(1)}, u32[]{:S(2)}, u32[]{:S(2)}) %collective-permute-start.13) | collective-permute-done | bytes 57376 | tf_op jit(solution)/shard_map/ppermute | solution.py:410
  41.3 1.3 %collective-permute-done.12 = bf16[224,128]{1,0:T(8,128)(2,1)S(1)} collective-permute-done((bf16[224,128]{1,0:T(8,128)(2,1)S(1)}, bf16[224,128]{1,0:T(8,128)(2,1)S(1)}, u32[]{:S(2)}, u32[]{:S(2)}) %collective-permute-start.12) | collective-permute-done | bytes 57376 | tf_op jit(solution)/shard_map/ppermute | solution.py:410
  42.6 0.5 %collective-permute-done.11 = bf16[224,128]{1,0:T(8,128)(2,1)S(1)} collective-permute-done((bf16[224,128]{1,0:T(8,128)(2,1)S(1)}, bf16[224,128]{1,0:T(8,128)(2,1)S(1)}, u32[]{:S(2)}, u32[]{:S(2)}) %collective-permute-start.11) | collective-permute-done | bytes 57376 | tf_op jit(solution)/shard_map/ppermute | solution.py:410
  43.2 0.1 collective-permute-start.14
  43.3 1.5 %collective-permute-done.14.theirs = bf16[4,224,128]{2,1,0:T(8,128)(2,1)S(1)} collective-permute-done((bf16[4,224,128]{2,1,0:T(8,128)(2,1)S(1)}, bf16[4,224,128]{2,1,0:T(8,128)(2,1)S(1)}, u32[]{:S(2)}, u32[]{:S(2)}) %collective-permute-start.14) | collective-permute-done | bytes 229408 | tf_op jit(solution)/shard_map/ppermute | solution.py:439
  44.7 1.0 %shard_map.81 = (f32[576,128]{1,0:T(8,128)}, f32[1152,128]{1,0:T(8,128)}) custom-call(bf16[4,224,128]{2,1,0:T(8,128)(2,1)S(1)} %pad_maximum_fusion.mine, bf16[4,224,128]{2,1,0:T(8,128)(2,1)S(1)} %collective-permute-done.14.theirs), custom_call_target="tpu_custom_call" | custom-call | flops 1000 | bytes 1572864 | tf_op jit(solution)/shard_map/pallas_call | solution.py:441
  (10 shorter events, 0.2 us)
Async XLA Ops:
  0.6 1.0 %copy-start = (bf16[16,128,128]{2,1,0:T(8,128)(2,1)S(1)}, bf16[16,128,128]{2,1,0:T(8,128)(2,1)}, u32[]{:S(2)}) copy-start(bf16[16,128,128]{2,1,0:T(8,128)(2,1)} %pre.1) | copy-start | bytes 1572868
  1.7 0.9 %copy-start.4 = (bf16[8,64,128]{2,1,0:T(8,128)(2,1)S(1)}, bf16[8,64,128]{2,1,0:T(8,128)(2,1)}, u32[]{:S(2)}) copy-start(bf16[8,64,128]{2,1,0:T(8,128)(2,1)} %grad_out.3) | copy-start | bytes 393220
  2.6 12.2 %copy-start.1 = (bf16[3,3,128,128]{3,2,1,0:T(8,128)(2,1)S(1)}, bf16[3,3,128,128]{3,2,1,0:T(8,128)(2,1)}, u32[]{:S(2)}) copy-start(bf16[3,3,128,128]{3,2,1,0:T(8,128)(2,1)} %w_second.1) | copy-start | bytes 884740
  2.6 12.2 %copy-start.2 = (bf16[16,128,64]{1,2,0:T(8,128)(2,1)S(1)}, bf16[16,128,64]{1,2,0:T(8,128)(2,1)}, u32[]{:S(2)}) copy-start(bf16[16,128,64]{1,2,0:T(8,128)(2,1)} %param.5) | copy-start | bytes 786436
  2.6 12.2 %copy-start.3 = (bf16[3,3,64,128]{3,2,1,0:T(8,128)(2,1)S(1)}, bf16[3,3,64,128]{3,2,1,0:T(8,128)(2,1)}, u32[]{:S(2)}) copy-start(bf16[3,3,64,128]{3,2,1,0:T(8,128)(2,1)} %w_first.1) | copy-start | bytes 442372
  2.6 15.3 %copy-start.5 = (bf16[8,64,128]{2,1,0:T(8,128)(2,1)S(1)}, bf16[8,64,128]{2,1,0:T(8,128)(2,1)}, u32[]{:S(2)}) copy-start(bf16[8,64,128]{2,1,0:T(8,128)(2,1)} %grad_out.3) | copy-start | bytes 393220
  2.7 8.7 %collective-permute-start = (bf16[192,128]{1,0:T(8,128)(2,1)S(1)}, bf16[192,128]{1,0:T(8,128)(2,1)S(1)}, u32[]{:S(2)}, u32[]{:S(2)}) collective-permute-start(bf16[192,128]{1,0:T(8,128)(2,1)S(1)} %get-tuple-element.33), channel_id=1, source_target_pairs={{0,4},{1,5},{2,6},{3,7},{4,0},{5,1},{6,2},{7,3},{8,16},{16,8},{9,1... | collective-permute-start | bytes 147464 | tf_op jit(solution)/shard_map/ppermute | solution.py:328
  8.7 4.2 %collective-permute-start.1 = (bf16[192,128]{1,0:T(8,128)(2,1)S(1)}, bf16[192,128]{1,0:T(8,128)(2,1)S(1)}, u32[]{:S(2)}, u32[]{:S(2)}) collective-permute-start(bf16[192,128]{1,0:T(8,128)(2,1)S(1)} %get-tuple-element.34), channel_id=1, source_target_pairs={{0,8},{1,9},{2,10},{3,11},{4,12},{5,13},{6,14},{7,15},{8,0},{9,1},... | collective-permute-start | bytes 147464 | tf_op jit(solution)/shard_map/ppermute | solution.py:329
  13.0 4.9 %collective-permute-start.3 = (bf16[32,128]{1,0:T(8,128)(2,1)S(1)}, bf16[32,128]{1,0:T(8,128)(2,1)S(1)}, u32[]{:S(2)}, u32[]{:S(2)}) collective-permute-start(bf16[32,128]{1,0:T(8,128)(2,1)S(1)} %get-tuple-element.80), channel_id=1, source_target_pairs={{0,7},{1,2},{2,1},{3,4},{4,3},{5,6},{6,5},{7,0},{8,15},{9,10},{10,... | collective-permute-start | bytes 24584 | tf_op jit(solution)/shard_map/ppermute | solution.py:360
  13.7 4.2 %collective-permute-start.2 = (bf16[32,128]{1,0:T(8,128)(2,1)S(1)}, bf16[32,128]{1,0:T(8,128)(2,1)S(1)}, u32[]{:S(2)}, u32[]{:S(2)}) collective-permute-start(bf16[32,128]{1,0:T(8,128)(2,1)S(1)} %get-tuple-element.81), channel_id=1, source_target_pairs={{0,1},{1,0},{2,3},{3,2},{4,5},{5,4},{6,7},{7,6},{8,9},{9,8},{10,11... | collective-permute-start | bytes 24584 | tf_op jit(solution)/shard_map/ppermute | solution.py:361
  20.6 1.9 %collective-permute-start.4 = (f32[896,128]{1,0:T(8,128)S(1)}, f32[896,128]{1,0:T(8,128)S(1)}, u32[]{:S(2)}, u32[]{:S(2)}) collective-permute-start(f32[896,128]{1,0:T(8,128)S(1)} %get-tuple-element.50), channel_id=1, source_target_pairs={{0,1},{1,0},{2,3},{3,2},{4,5},{5,4},{6,7},{7,6},{8,9},{9,8},{10,11... | collective-permute-start | bytes 1376264 | tf_op jit(solution)/shard_map/ppermute | solution.py:412
  22.6 5.7 %collective-permute-start.5 = (bf16[224,128]{1,0:T(8,128)(2,1)S(1)}, bf16[224,128]{1,0:T(8,128)(2,1)S(1)}, u32[]{:S(2)}, u32[]{:S(2)}) collective-permute-start(bf16[224,128]{1,0:T(8,128)(2,1)S(1)} %get-tuple-element.52), channel_id=1, source_target_pairs={{0,8},{8,0},{16,24},{24,16},{1,9},{9,1},{17,25},{25,17},{2,10},{10... | collective-permute-start | bytes 172040 | tf_op jit(solution)/shard_map/ppermute | solution.py:410
  23.0 5.3 %collective-permute-start.6 = (bf16[224,128]{1,0:T(8,128)(2,1)S(1)}, bf16[224,128]{1,0:T(8,128)(2,1)S(1)}, u32[]{:S(2)}, u32[]{:S(2)}) collective-permute-start(bf16[224,128]{1,0:T(8,128)(2,1)S(1)} %get-tuple-element.53), channel_id=1, source_target_pairs={{0,16},{8,24},{16,0},{24,8},{1,17},{9,25},{17,1},{25,9},{2,18},{10... | collective-permute-start | bytes 172040 | tf_op jit(solution)/shard_map/ppermute | solution.py:410
  23.4 5.1 %collective-permute-start.7 = (bf16[224,128]{1,0:T(8,128)(2,1)S(1)}, bf16[224,128]{1,0:T(8,128)(2,1)S(1)}, u32[]{:S(2)}, u32[]{:S(2)}) collective-permute-start(bf16[224,128]{1,0:T(8,128)(2,1)S(1)} %get-tuple-element.54), channel_id=1, source_target_pairs={{0,24},{8,16},{16,8},{24,0},{1,25},{9,17},{17,9},{25,1},{2,26},{10... | collective-permute-start | bytes 172040 | tf_op jit(solution)/shard_map/ppermute | solution.py:410
  28.5 6.4 %collective-permute-start.10 = (bf16[224,128]{1,0:T(8,128)(2,1)S(1)}, bf16[224,128]{1,0:T(8,128)(2,1)S(1)}, u32[]{:S(2)}, u32[]{:S(2)}) collective-permute-start(bf16[224,128]{1,0:T(8,128)(2,1)S(1)} %fusion.2), channel_id=1, source_target_pairs={{0,6},{1,7},{2,4},{3,5},{4,2},{5,3},{6,0},{7,1},{8,14},{9,15},{10,... | collective-permute-start | bytes 172040 | tf_op jit(solution)/shard_map/ppermute | solution.py:433
  30.5 5.6 %collective-permute-start.9 = (bf16[224,128]{1,0:T(8,128)(2,1)S(1)}, bf16[224,128]{1,0:T(8,128)(2,1)S(1)}, u32[]{:S(2)}, u32[]{:S(2)}) collective-permute-start(bf16[224,128]{1,0:T(8,128)(2,1)S(1)} %fusion.2), channel_id=1, source_target_pairs={{0,4},{1,5},{2,6},{3,7},{4,0},{5,1},{6,2},{7,3},{8,12},{9,13},{10,... | collective-permute-start | bytes 172040 | tf_op jit(solution)/shard_map/ppermute | solution.py:433
  30.5 5.6 %collective-permute-start.8 = (bf16[224,128]{1,0:T(8,128)(2,1)S(1)}, bf16[224,128]{1,0:T(8,128)(2,1)S(1)}, u32[]{:S(2)}, u32[]{:S(2)}) collective-permute-start(bf16[224,128]{1,0:T(8,128)(2,1)S(1)} %fusion.2), channel_id=1, source_target_pairs={{0,2},{1,3},{2,0},{3,1},{4,6},{5,7},{6,4},{7,5},{8,10},{9,11},{10,... | collective-permute-start | bytes 172040 | tf_op jit(solution)/shard_map/ppermute | solution.py:433
  36.2 5.1 %collective-permute-start.13 = (bf16[224,128]{1,0:T(8,128)(2,1)S(1)}, bf16[224,128]{1,0:T(8,128)(2,1)S(1)}, u32[]{:S(2)}, u32[]{:S(2)}) collective-permute-start(bf16[224,128]{1,0:T(8,128)(2,1)S(1)} %add_convert_fusion), channel_id=1, source_target_pairs={{0,24},{8,16},{16,8},{24,0},{1,25},{9,17},{17,9},{25,1},{2,26},{10... | collective-permute-start | bytes 172040 | tf_op jit(solution)/shard_map/ppermute | solution.py:410
  38.4 4.2 %collective-permute-start.12 = (bf16[224,128]{1,0:T(8,128)(2,1)S(1)}, bf16[224,128]{1,0:T(8,128)(2,1)S(1)}, u32[]{:S(2)}, u32[]{:S(2)}) collective-permute-start(bf16[224,128]{1,0:T(8,128)(2,1)S(1)} %add_convert_fusion), channel_id=1, source_target_pairs={{0,16},{8,24},{16,0},{24,8},{1,17},{9,25},{17,1},{25,9},{2,18},{10... | collective-permute-start | bytes 172040 | tf_op jit(solution)/shard_map/ppermute | solution.py:410
  39.0 4.2 %collective-permute-start.11 = (bf16[224,128]{1,0:T(8,128)(2,1)S(1)}, bf16[224,128]{1,0:T(8,128)(2,1)S(1)}, u32[]{:S(2)}, u32[]{:S(2)}) collective-permute-start(bf16[224,128]{1,0:T(8,128)(2,1)S(1)} %add_convert_fusion), channel_id=1, source_target_pairs={{0,8},{8,0},{16,24},{24,16},{1,9},{9,1},{17,25},{25,17},{2,10},{10... | collective-permute-start | bytes 172040 | tf_op jit(solution)/shard_map/ppermute | solution.py:410
  43.2 1.6 %collective-permute-start.14 = (bf16[4,224,128]{2,1,0:T(8,128)(2,1)S(1)}, bf16[4,224,128]{2,1,0:T(8,128)(2,1)S(1)}, u32[]{:S(2)}, u32[]{:S(2)}) collective-permute-start(bf16[4,224,128]{2,1,0:T(8,128)(2,1)S(1)} %pad_maximum_fusion.mine), channel_id=1, source_target_pairs={{0,1},{1,0},{2,3},{3,2},{4,5},{5,4},{6,7},{7,6},{8,9},{9,8},{10,11... | collective-permute-start | bytes 688136 | tf_op jit(solution)/shard_map/ppermute | solution.py:439

commit v9 on v8

--- a/solution.py
+++ b/solution.py
@@ -320,7 +320,7 @@
         compiler_params=params(50),
         cost_estimate=pl.CostEstimate(flops=1000, bytes_accessed=1 << 18, transcendentals=0),
     )(pre_first, grad_out)
-    pairs = [(j, (j + lons // 2) % lons) for j in range(lons)]
+    pairs = [(i * lons + j, i * lons + (j + lons // 2) % lons) for i in (0, lats - 1) for j in range(lons)]
     for i in range(1, lats - 1, 2):
         for j in range(lons):
             pairs += [(i * lons + j, (i + 1) * lons + j), ((i + 1) * lons + j, i * lons + j)]

time: 46 us -> 44.6 us (0.970)
  starting transfers between devices: 19.9 us -> 17.9 us
  waiting for transfers between devices: 15.4 us -> 16.1 us
    ppermute x1, starting transfers between devices: 6.08 us -> 4.1 us  [body(): row_b = lax.ppermute(row_b, AREA, pairs)]
    ppermute x6, waiting for transfers between devices: 3.61 us -> 4.89 us  [along_lat(): return lax.ppermute(value, 'lat', [(i, i ^ far) for i in range(lats)])]
    ppermute x3, waiting for transfers between devices: 3.15 us -> 2.57 us  [body(): lax.ppermute(part, 'lon', [(i, i ^ 2 * k) for i in range(lons)])]
where the time goes in v9:
time: 44.6 us; the launch traced here: 44.4 us
  starting transfers between devices  17.9 us (40%)
  waiting for transfers between devices  16.1 us (36%)
  Pallas kernels  7.33 us (16%)
  local copies, waits for them, and re-layouts  2.06 us (5%)
  between operations  0.75 us (2%)
    ppermute x6, starting transfers between devices, along_lat(): return lax.ppermute(value, 'lat', [(i, i ^ far) for i in range(lats)])  7.11 us
    ppermute x6, waiting for transfers between devices, along_lat(): return lax.ppermute(value, 'lat', [(i, i ^ far) for i in range(lats)])  4.89 us
    ppermute x3, starting transfers between devices, body(): lax.ppermute(part, 'lon', [(i, i ^ 2 * k) for i in range(lons)])  4.45 us
    ppermute x1, starting transfers between devices, body(): row_b = lax.ppermute(row_b, AREA, pairs)  4.1 us
    ppermute x1, waiting for transfers between devices, body(): lax.ppermute(col_b, 'lon', [(i, (i + 2 * (i % 2) - 1) % lons) for i in ra...  2.69 us
    pallas_call x1, Pallas kernels, body(): pl.pallas_call(functools.partial(middle_kernel, lats), out_shape=(shape((...  2.66 us
    ppermute x3, waiting for transfers between devices, body(): lax.ppermute(part, 'lon', [(i, i ^ 2 * k) for i in range(lons)])  2.57 us
    pallas_call x1, Pallas kernels, body(): pl.pallas_call(last_kernel, out_shape=shape((rows, c0, cols), BF16), in_s...  2.18 us
  transfers between devices with their start and end apart: 15, of which 11 were waited for; matrix products, arithmetic and copies ran while one was open for 0% of the time, Pallas kernels for 8%

profile of v9, /device:TPU:0, one launch (start us, length us, event | category | flops | bytes accessed | tf_op | source)
XLA Modules:
  0.0 44.4 jit_solution(6012725855561045038)
XLA Ops:
  0.6 0.0 copy-start
  0.6 1.0 %copy-done = bf16[16,128,128]{2,1,0:T(8,128)(2,1)S(1)} copy-done((bf16[16,128,128]{2,1,0:T(8,128)(2,1)S(1)}, bf16[16,128,128]{2,1,0:T(8,128)(2,1)}, u32[]{:S(2)}) %copy-start) | copy-done | bytes 524312
  1.7 0.0 copy-start.4
  1.7 0.9 %copy-done.4 = bf16[8,64,128]{2,1,0:T(8,128)(2,1)S(1)} copy-done((bf16[8,64,128]{2,1,0:T(8,128)(2,1)S(1)}, bf16[8,64,128]{2,1,0:T(8,128)(2,1)}, u32[]{:S(2)}) %copy-start.4) | copy-done | bytes 131096
  2.6 0.0 copy-start.1
  2.6 0.0 copy-start.2
  2.6 0.0 copy-start.3
  2.6 0.0 copy-start.5
  2.6 0.1 shard_map.76
  2.7 4.1 %collective-permute-start = (bf16[192,128]{1,0:T(8,128)(2,1)S(1)}, bf16[192,128]{1,0:T(8,128)(2,1)S(1)}, u32[]{:S(2)}, u32[]{:S(2)}) collective-permute-start(bf16[192,128]{1,0:T(8,128)(2,1)S(1)} %get-tuple-element.33), channel_id=1, source_target_pairs={{0,4},{1,5},{2,6},{3,7},{4,0},{5,1},{6,2},{7,3},{24,28},{25,29},{2... | collective-permute-start | bytes 147464 | tf_op jit(solution)/shard_map/ppermute | solution.py:328
  6.8 0.4 collective-permute-start.1
  7.2 0.1 pad.9.clone
  7.2 0.9 %shard_map.77 = (f32[16,64,256]{2,1,0:T(8,128)S(1)}, bf16[2,256,512]{2,1,0:T(8,128)(2,1)S(1)}) custom-call(bf16[16,128,128]{2,1,0:T(8,128)(2,1)S(1)} %get-tuple-element.35.pre), custom_call_target="tpu_custom_call" | custom-call | flops 15728640 | bytes 2097152 | tf_op jit(solution)/shard_map/pallas_call | solution.py:331
  8.2 1.2 %collective-permute-done.row_b = bf16[192,128]{1,0:T(8,128)(2,1)S(1)} collective-permute-done((bf16[192,128]{1,0:T(8,128)(2,1)S(1)}, bf16[192,128]{1,0:T(8,128)(2,1)S(1)}, u32[]{:S(2)}, u32[]{:S(2)}) %collective-permute-start) | collective-permute-done | bytes 49184 | tf_op jit(solution)/shard_map/ppermute | solution.py:328
  9.4 1.5 %collective-permute-done.1.row_a = bf16[192,128]{1,0:T(8,128)(2,1)S(1)} collective-permute-done((bf16[192,128]{1,0:T(8,128)(2,1)S(1)}, bf16[192,128]{1,0:T(8,128)(2,1)S(1)}, u32[]{:S(2)}, u32[]{:S(2)}) %collective-permute-start.1) | collective-permute-done | bytes 49184 | tf_op jit(solution)/shard_map/ppermute | solution.py:329
  10.9 0.1 maximum_maximum_fusion.1
  11.0 0.8 %collective-permute-start.3 = (bf16[32,128]{1,0:T(8,128)(2,1)S(1)}, bf16[32,128]{1,0:T(8,128)(2,1)S(1)}, u32[]{:S(2)}, u32[]{:S(2)}) collective-permute-start(bf16[32,128]{1,0:T(8,128)(2,1)S(1)} %get-tuple-element.80), channel_id=1, source_target_pairs={{0,7},{1,2},{2,1},{3,4},{4,3},{5,6},{6,5},{7,0},{8,15},{9,10},{10,... | collective-permute-start | bytes 24584 | tf_op jit(solution)/shard_map/ppermute | solution.py:360
  11.8 0.9 %collective-permute-start.2 = (bf16[32,128]{1,0:T(8,128)(2,1)S(1)}, bf16[32,128]{1,0:T(8,128)(2,1)S(1)}, u32[]{:S(2)}, u32[]{:S(2)}) collective-permute-start(bf16[32,128]{1,0:T(8,128)(2,1)S(1)} %get-tuple-element.81), channel_id=1, source_target_pairs={{0,1},{1,0},{2,3},{3,2},{4,5},{5,4},{6,7},{7,6},{8,9},{9,8},{10,11... | collective-permute-start | bytes 24584 | tf_op jit(solution)/shard_map/ppermute | solution.py:361
  12.7 0.0 copy-done.1
  12.7 0.0 copy-done.2
  12.7 0.0 copy-done.3
  12.7 0.5 %shard_map.78 = (bf16[128,1024]{1,0:T(8,128)(2,1)S(1)}, bf16[384,512]{1,0:T(8,128)(2,1)S(1)}, bf16[3,256,512]{2,1,0:T(8,128)(2,1)S(1)}) custom-call(bf16[16,64,128]{2,1,0:T(8,128)(2,1)S(1)} %bitcast.8, bf16[3,3,64,128]{3,2,1,0:T(8,128)(2,1)S(1)} %copy-done.3, bf16[3,3,128,128]{3,2,1,0:T(8,128)(2,1)S(1)} %copy-done.1), custom_call_target="tpu_custom_call" | custom-call | flops 67108864 | bytes 3145728 | tf_op jit(solution)/shard_map/pallas_call | solution.py:363
  13.2 2.7 %collective-permute-done.3.col_b = bf16[32,128]{1,0:T(8,128)(2,1)S(1)} collective-permute-done((bf16[32,128]{1,0:T(8,128)(2,1)S(1)}, bf16[32,128]{1,0:T(8,128)(2,1)S(1)}, u32[]{:S(2)}, u32[]{:S(2)}) %collective-permute-start.3) | collective-permute-done | bytes 8224 | tf_op jit(solution)/shard_map/ppermute | solution.py:360
  15.9 0.0 collective-permute-done.2.col_a
  15.9 0.0 copy-done.5
  15.9 2.7 %shard_map.79 = (bf16[19,64,512]{2,1,0:T(8,128)(2,1)S(1)}, f32[896,128]{1,0:T(8,128)S(1)}, f32[896,128]{1,0:T(8,128)S(1)}) custom-call(bf16[8,64,128]{2,1,0:T(8,128)(2,1)S(1)} %copy-done.5, bf16[192,128]{1,0:T(8,128)(2,1)S(1)} %collective-permute-done.1.row_a, bf16[192,128]{1,0:T(8,128)(2,1)S(1)} %collective-permute-done.row_b, ...), custom_call_target="tpu_custom_call" | custom-call | flops 1509949440 | bytes 8388608 | tf_op jit(solution)/shard_map/pallas_call | solution.py:381
  18.5 0.1 collective-permute-start.4
  18.6 1.8 %collective-permute-done.4 = f32[896,128]{1,0:T(8,128)S(1)} collective-permute-done((f32[896,128]{1,0:T(8,128)S(1)}, f32[896,128]{1,0:T(8,128)S(1)}, u32[]{:S(2)}, u32[]{:S(2)}) %collective-permute-start.4) | collective-permute-done | bytes 458784 | tf_op jit(solution)/shard_map/ppermute | solution.py:412
  20.4 0.1 fusion.3
  20.5 0.5 %collective-permute-start.5 = (bf16[224,128]{1,0:T(8,128)(2,1)S(1)}, bf16[224,128]{1,0:T(8,128)(2,1)S(1)}, u32[]{:S(2)}, u32[]{:S(2)}) collective-permute-start(bf16[224,128]{1,0:T(8,128)(2,1)S(1)} %get-tuple-element.52), channel_id=1, source_target_pairs={{0,8},{8,0},{16,24},{24,16},{1,9},{9,1},{17,25},{25,17},{2,10},{10... | collective-permute-start | bytes 172040 | tf_op jit(solution)/shard_map/ppermute | solution.py:410
  21.0 2.6 %collective-permute-start.6 = (bf16[224,128]{1,0:T(8,128)(2,1)S(1)}, bf16[224,128]{1,0:T(8,128)(2,1)S(1)}, u32[]{:S(2)}, u32[]{:S(2)}) collective-permute-start(bf16[224,128]{1,0:T(8,128)(2,1)S(1)} %get-tuple-element.53), channel_id=1, source_target_pairs={{0,16},{8,24},{16,0},{24,8},{1,17},{9,25},{17,1},{25,9},{2,18},{10... | collective-permute-start | bytes 172040 | tf_op jit(solution)/shard_map/ppermute | solution.py:410
  23.6 0.5 %collective-permute-start.7 = (bf16[224,128]{1,0:T(8,128)(2,1)S(1)}, bf16[224,128]{1,0:T(8,128)(2,1)S(1)}, u32[]{:S(2)}, u32[]{:S(2)}) collective-permute-start(bf16[224,128]{1,0:T(8,128)(2,1)S(1)} %get-tuple-element.54), channel_id=1, source_target_pairs={{0,24},{8,16},{16,8},{24,0},{1,25},{9,17},{17,9},{25,1},{2,26},{10... | collective-permute-start | bytes 172040 | tf_op jit(solution)/shard_map/ppermute | solution.py:410
  24.1 2.2 %shard_map.80 = bf16[16,64,128]{2,1,0:T(8,128)(2,1)} custom-call(bf16[19,64,512]{2,1,0:T(8,128)(2,1)S(1)} %get-tuple-element.55.spread, bf16[384,512]{1,0:T(8,128)(2,1)S(1)} %get-tuple-element.56.taps), custom_call_target="tpu_custom_call" | custom-call | flops 301989888 | bytes 3145728 | tf_op jit(solution)/shard_map/pallas_call | solution.py:416
  26.3 0.0 collective-permute-done.5
  26.3 0.0 collective-permute-done.6
  26.3 2.4 %collective-permute-done.7 = bf16[224,128]{1,0:T(8,128)(2,1)S(1)} collective-permute-done((bf16[224,128]{1,0:T(8,128)(2,1)S(1)}, bf16[224,128]{1,0:T(8,128)(2,1)S(1)}, u32[]{:S(2)}, u32[]{:S(2)}) %collective-permute-start.7) | collective-permute-done | bytes 57376 | tf_op jit(solution)/shard_map/ppermute | solution.py:410
  28.7 0.7 %collective-permute-start.10 = (bf16[224,128]{1,0:T(8,128)(2,1)S(1)}, bf16[224,128]{1,0:T(8,128)(2,1)S(1)}, u32[]{:S(2)}, u32[]{:S(2)}) collective-permute-start(bf16[224,128]{1,0:T(8,128)(2,1)S(1)} %fusion.2), channel_id=1, source_target_pairs={{0,6},{1,7},{2,4},{3,5},{4,2},{5,3},{6,0},{7,1},{8,14},{9,15},{10,... | collective-permute-start | bytes 172040 | tf_op jit(solution)/shard_map/ppermute | solution.py:433
  29.4 0.6 %collective-permute-start.9 = (bf16[224,128]{1,0:T(8,128)(2,1)S(1)}, bf16[224,128]{1,0:T(8,128)(2,1)S(1)}, u32[]{:S(2)}, u32[]{:S(2)}) collective-permute-start(bf16[224,128]{1,0:T(8,128)(2,1)S(1)} %fusion.2), channel_id=1, source_target_pairs={{0,4},{1,5},{2,6},{3,7},{4,0},{5,1},{6,2},{7,3},{8,12},{9,13},{10,... | collective-permute-start | bytes 172040 | tf_op jit(solution)/shard_map/ppermute | solution.py:433
  30.0 3.1 %collective-permute-start.8 = (bf16[224,128]{1,0:T(8,128)(2,1)S(1)}, bf16[224,128]{1,0:T(8,128)(2,1)S(1)}, u32[]{:S(2)}, u32[]{:S(2)}) collective-permute-start(bf16[224,128]{1,0:T(8,128)(2,1)S(1)} %fusion.2), channel_id=1, source_target_pairs={{0,2},{1,3},{2,0},{3,1},{4,6},{5,7},{6,4},{7,5},{8,10},{9,11},{10,... | collective-permute-start | bytes 172040 | tf_op jit(solution)/shard_map/ppermute | solution.py:433
  33.2 1.7 %collective-permute-done.10 = bf16[224,128]{1,0:T(8,128)(2,1)S(1)} collective-permute-done((bf16[224,128]{1,0:T(8,128)(2,1)S(1)}, bf16[224,128]{1,0:T(8,128)(2,1)S(1)}, u32[]{:S(2)}, u32[]{:S(2)}) %collective-permute-start.10) | collective-permute-done | bytes 57376 | tf_op jit(solution)/shard_map/ppermute | solution.py:433
  34.9 0.9 %collective-permute-done.9 = bf16[224,128]{1,0:T(8,128)(2,1)S(1)} collective-permute-done((bf16[224,128]{1,0:T(8,128)(2,1)S(1)}, bf16[224,128]{1,0:T(8,128)(2,1)S(1)}, u32[]{:S(2)}, u32[]{:S(2)}) %collective-permute-start.9) | collective-permute-done | bytes 57376 | tf_op jit(solution)/shard_map/ppermute | solution.py:433
  35.7 0.0 collective-permute-done.8
  35.8 0.7 %collective-permute-start.13 = (bf16[224,128]{1,0:T(8,128)(2,1)S(1)}, bf16[224,128]{1,0:T(8,128)(2,1)S(1)}, u32[]{:S(2)}, u32[]{:S(2)}) collective-permute-start(bf16[224,128]{1,0:T(8,128)(2,1)S(1)} %add_convert_fusion), channel_id=1, source_target_pairs={{0,24},{8,16},{16,8},{24,0},{1,25},{9,17},{17,9},{25,1},{2,26},{10... | collective-permute-start | bytes 172040 | tf_op jit(solution)/shard_map/ppermute | solution.py:410
  36.5 1.1 %collective-permute-start.12 = (bf16[224,128]{1,0:T(8,128)(2,1)S(1)}, bf16[224,128]{1,0:T(8,128)(2,1)S(1)}, u32[]{:S(2)}, u32[]{:S(2)}) collective-permute-start(bf16[224,128]{1,0:T(8,128)(2,1)S(1)} %add_convert_fusion), channel_id=1, source_target_pairs={{0,16},{8,24},{16,0},{24,8},{1,17},{9,25},{17,1},{25,9},{2,18},{10... | collective-permute-start | bytes 172040 | tf_op jit(solution)/shard_map/ppermute | solution.py:410
  37.6 1.7 %collective-permute-start.11 = (bf16[224,128]{1,0:T(8,128)(2,1)S(1)}, bf16[224,128]{1,0:T(8,128)(2,1)S(1)}, u32[]{:S(2)}, u32[]{:S(2)}) collective-permute-start(bf16[224,128]{1,0:T(8,128)(2,1)S(1)} %add_convert_fusion), channel_id=1, source_target_pairs={{0,8},{8,0},{16,24},{24,16},{1,9},{9,1},{17,25},{25,17},{2,10},{10... | collective-permute-start | bytes 172040 | tf_op jit(solution)/shard_map/ppermute | solution.py:410
  39.3 1.7 %collective-permute-done.13 = bf16[224,128]{1,0:T(8,128)(2,1)S(1)} collective-permute-done((bf16[224,128]{1,0:T(8,128)(2,1)S(1)}, bf16[224,128]{1,0:T(8,128)(2,1)S(1)}, u32[]{:S(2)}, u32[]{:S(2)}) %collective-permute-start.13) | collective-permute-done | bytes 57376 | tf_op jit(solution)/shard_map/ppermute | solution.py:410
  41.0 0.3 collective-permute-done.12
  41.3 0.5 %collective-permute-done.11 = bf16[224,128]{1,0:T(8,128)(2,1)S(1)} collective-permute-done((bf16[224,128]{1,0:T(8,128)(2,1)S(1)}, bf16[224,128]{1,0:T(8,128)(2,1)S(1)}, u32[]{:S(2)}, u32[]{:S(2)}) %collective-permute-start.11) | collective-permute-done | bytes 57376 | tf_op jit(solution)/shard_map/ppermute | solution.py:410
  41.8 0.1 collective-permute-start.14
  41.9 1.5 %collective-permute-done.14.theirs = bf16[4,224,128]{2,1,0:T(8,128)(2,1)S(1)} collective-permute-done((bf16[4,224,128]{2,1,0:T(8,128)(2,1)S(1)}, bf16[4,224,128]{2,1,0:T(8,128)(2,1)S(1)}, u32[]{:S(2)}, u32[]{:S(2)}) %collective-permute-start.14) | collective-permute-done | bytes 229408 | tf_op jit(solution)/shard_map/ppermute | solution.py:439
  43.4 1.0 %shard_map.81 = (f32[576,128]{1,0:T(8,128)}, f32[1152,128]{1,0:T(8,128)}) custom-call(bf16[4,224,128]{2,1,0:T(8,128)(2,1)S(1)} %pad_maximum_fusion.mine, bf16[4,224,128]{2,1,0:T(8,128)(2,1)S(1)} %collective-permute-done.14.theirs), custom_call_target="tpu_custom_call" | custom-call | flops 1000 | bytes 1572864 | tf_op jit(solution)/shard_map/pallas_call | solution.py:441
  (10 shorter events, 0.2 us)
Async XLA Ops:
  0.6 1.0 %copy-start = (bf16[16,128,128]{2,1,0:T(8,128)(2,1)S(1)}, bf16[16,128,128]{2,1,0:T(8,128)(2,1)}, u32[]{:S(2)}) copy-start(bf16[16,128,128]{2,1,0:T(8,128)(2,1)} %pre.1) | copy-start | bytes 1572868
  1.7 0.9 %copy-start.4 = (bf16[8,64,128]{2,1,0:T(8,128)(2,1)S(1)}, bf16[8,64,128]{2,1,0:T(8,128)(2,1)}, u32[]{:S(2)}) copy-start(bf16[8,64,128]{2,1,0:T(8,128)(2,1)} %grad_out.3) | copy-start | bytes 393220
  2.6 10.1 %copy-start.1 = (bf16[3,3,128,128]{3,2,1,0:T(8,128)(2,1)S(1)}, bf16[3,3,128,128]{3,2,1,0:T(8,128)(2,1)}, u32[]{:S(2)}) copy-start(bf16[3,3,128,128]{3,2,1,0:T(8,128)(2,1)} %w_second.1) | copy-start | bytes 884740
  2.6 10.1 %copy-start.2 = (bf16[16,128,64]{1,2,0:T(8,128)(2,1)S(1)}, bf16[16,128,64]{1,2,0:T(8,128)(2,1)}, u32[]{:S(2)}) copy-start(bf16[16,128,64]{1,2,0:T(8,128)(2,1)} %param.5) | copy-start | bytes 786436
  2.6 10.1 %copy-start.3 = (bf16[3,3,64,128]{3,2,1,0:T(8,128)(2,1)S(1)}, bf16[3,3,64,128]{3,2,1,0:T(8,128)(2,1)}, u32[]{:S(2)}) copy-start(bf16[3,3,64,128]{3,2,1,0:T(8,128)(2,1)} %w_first.1) | copy-start | bytes 442372
  2.6 13.3 %copy-start.5 = (bf16[8,64,128]{2,1,0:T(8,128)(2,1)S(1)}, bf16[8,64,128]{2,1,0:T(8,128)(2,1)}, u32[]{:S(2)}) copy-start(bf16[8,64,128]{2,1,0:T(8,128)(2,1)} %grad_out.3) | copy-start | bytes 393220
  2.7 6.7 %collective-permute-start = (bf16[192,128]{1,0:T(8,128)(2,1)S(1)}, bf16[192,128]{1,0:T(8,128)(2,1)S(1)}, u32[]{:S(2)}, u32[]{:S(2)}) collective-permute-start(bf16[192,128]{1,0:T(8,128)(2,1)S(1)} %get-tuple-element.33), channel_id=1, source_target_pairs={{0,4},{1,5},{2,6},{3,7},{4,0},{5,1},{6,2},{7,3},{24,28},{25,29},{2... | collective-permute-start | bytes 147464 | tf_op jit(solution)/shard_map/ppermute | solution.py:328
  6.8 4.1 %collective-permute-start.1 = (bf16[192,128]{1,0:T(8,128)(2,1)S(1)}, bf16[192,128]{1,0:T(8,128)(2,1)S(1)}, u32[]{:S(2)}, u32[]{:S(2)}) collective-permute-start(bf16[192,128]{1,0:T(8,128)(2,1)S(1)} %get-tuple-element.34), channel_id=1, source_target_pairs={{0,8},{1,9},{2,10},{3,11},{4,12},{5,13},{6,14},{7,15},{8,0},{9,1},... | collective-permute-start | bytes 147464 | tf_op jit(solution)/shard_map/ppermute | solution.py:329
  11.0 4.9 %collective-permute-start.3 = (bf16[32,128]{1,0:T(8,128)(2,1)S(1)}, bf16[32,128]{1,0:T(8,128)(2,1)S(1)}, u32[]{:S(2)}, u32[]{:S(2)}) collective-permute-start(bf16[32,128]{1,0:T(8,128)(2,1)S(1)} %get-tuple-element.80), channel_id=1, source_target_pairs={{0,7},{1,2},{2,1},{3,4},{4,3},{5,6},{6,5},{7,0},{8,15},{9,10},{10,... | collective-permute-start | bytes 24584 | tf_op jit(solution)/shard_map/ppermute | solution.py:360
  11.8 4.1 %collective-permute-start.2 = (bf16[32,128]{1,0:T(8,128)(2,1)S(1)}, bf16[32,128]{1,0:T(8,128)(2,1)S(1)}, u32[]{:S(2)}, u32[]{:S(2)}) collective-permute-start(bf16[32,128]{1,0:T(8,128)(2,1)S(1)} %get-tuple-element.81), channel_id=1, source_target_pairs={{0,1},{1,0},{2,3},{3,2},{4,5},{5,4},{6,7},{7,6},{8,9},{9,8},{10,11... | collective-permute-start | bytes 24584 | tf_op jit(solution)/shard_map/ppermute | solution.py:361
  18.5 1.9 %collective-permute-start.4 = (f32[896,128]{1,0:T(8,128)S(1)}, f32[896,128]{1,0:T(8,128)S(1)}, u32[]{:S(2)}, u32[]{:S(2)}) collective-permute-start(f32[896,128]{1,0:T(8,128)S(1)} %get-tuple-element.50), channel_id=1, source_target_pairs={{0,1},{1,0},{2,3},{3,2},{4,5},{5,4},{6,7},{7,6},{8,9},{9,8},{10,11... | collective-permute-start | bytes 1376264 | tf_op jit(solution)/shard_map/ppermute | solution.py:412
  20.5 5.7 %collective-permute-start.5 = (bf16[224,128]{1,0:T(8,128)(2,1)S(1)}, bf16[224,128]{1,0:T(8,128)(2,1)S(1)}, u32[]{:S(2)}, u32[]{:S(2)}) collective-permute-start(bf16[224,128]{1,0:T(8,128)(2,1)S(1)} %get-tuple-element.52), channel_id=1, source_target_pairs={{0,8},{8,0},{16,24},{24,16},{1,9},{9,1},{17,25},{25,17},{2,10},{10... | collective-permute-start | bytes 172040 | tf_op jit(solution)/shard_map/ppermute | solution.py:410
  21.0 5.3 %collective-permute-start.6 = (bf16[224,128]{1,0:T(8,128)(2,1)S(1)}, bf16[224,128]{1,0:T(8,128)(2,1)S(1)}, u32[]{:S(2)}, u32[]{:S(2)}) collective-permute-start(bf16[224,128]{1,0:T(8,128)(2,1)S(1)} %get-tuple-element.53), channel_id=1, source_target_pairs={{0,16},{8,24},{16,0},{24,8},{1,17},{9,25},{17,1},{25,9},{2,18},{10... | collective-permute-start | bytes 172040 | tf_op jit(solution)/shard_map/ppermute | solution.py:410
  23.6 5.1 %collective-permute-start.7 = (bf16[224,128]{1,0:T(8,128)(2,1)S(1)}, bf16[224,128]{1,0:T(8,128)(2,1)S(1)}, u32[]{:S(2)}, u32[]{:S(2)}) collective-permute-start(bf16[224,128]{1,0:T(8,128)(2,1)S(1)} %get-tuple-element.54), channel_id=1, source_target_pairs={{0,24},{8,16},{16,8},{24,0},{1,25},{9,17},{17,9},{25,1},{2,26},{10... | collective-permute-start | bytes 172040 | tf_op jit(solution)/shard_map/ppermute | solution.py:410
  28.7 6.2 %collective-permute-start.10 = (bf16[224,128]{1,0:T(8,128)(2,1)S(1)}, bf16[224,128]{1,0:T(8,128)(2,1)S(1)}, u32[]{:S(2)}, u32[]{:S(2)}) collective-permute-start(bf16[224,128]{1,0:T(8,128)(2,1)S(1)} %fusion.2), channel_id=1, source_target_pairs={{0,6},{1,7},{2,4},{3,5},{4,2},{5,3},{6,0},{7,1},{8,14},{9,15},{10,... | collective-permute-start | bytes 172040 | tf_op jit(solution)/shard_map/ppermute | solution.py:433
  29.4 6.3 %collective-permute-start.9 = (bf16[224,128]{1,0:T(8,128)(2,1)S(1)}, bf16[224,128]{1,0:T(8,128)(2,1)S(1)}, u32[]{:S(2)}, u32[]{:S(2)}) collective-permute-start(bf16[224,128]{1,0:T(8,128)(2,1)S(1)} %fusion.2), channel_id=1, source_target_pairs={{0,4},{1,5},{2,6},{3,7},{4,0},{5,1},{6,2},{7,3},{8,12},{9,13},{10,... | collective-permute-start | bytes 172040 | tf_op jit(solution)/shard_map/ppermute | solution.py:433
  30.0 5.7 %collective-permute-start.8 = (bf16[224,128]{1,0:T(8,128)(2,1)S(1)}, bf16[224,128]{1,0:T(8,128)(2,1)S(1)}, u32[]{:S(2)}, u32[]{:S(2)}) collective-permute-start(bf16[224,128]{1,0:T(8,128)(2,1)S(1)} %fusion.2), channel_id=1, source_target_pairs={{0,2},{1,3},{2,0},{3,1},{4,6},{5,7},{6,4},{7,5},{8,10},{9,11},{10,... | collective-permute-start | bytes 172040 | tf_op jit(solution)/shard_map/ppermute | solution.py:433
  35.8 5.2 %collective-permute-start.13 = (bf16[224,128]{1,0:T(8,128)(2,1)S(1)}, bf16[224,128]{1,0:T(8,128)(2,1)S(1)}, u32[]{:S(2)}, u32[]{:S(2)}) collective-permute-start(bf16[224,128]{1,0:T(8,128)(2,1)S(1)} %add_convert_fusion), channel_id=1, source_target_pairs={{0,24},{8,16},{16,8},{24,0},{1,25},{9,17},{17,9},{25,1},{2,26},{10... | collective-permute-start | bytes 172040 | tf_op jit(solution)/shard_map/ppermute | solution.py:410
  36.5 4.8 %collective-permute-start.12 = (bf16[224,128]{1,0:T(8,128)(2,1)S(1)}, bf16[224,128]{1,0:T(8,128)(2,1)S(1)}, u32[]{:S(2)}, u32[]{:S(2)}) collective-permute-start(bf16[224,128]{1,0:T(8,128)(2,1)S(1)} %add_convert_fusion), channel_id=1, source_target_pairs={{0,16},{8,24},{16,0},{24,8},{1,17},{9,25},{17,1},{25,9},{2,18},{10... | collective-permute-start | bytes 172040 | tf_op jit(solution)/shard_map/ppermute | solution.py:410
  37.6 4.2 %collective-permute-start.11 = (bf16[224,128]{1,0:T(8,128)(2,1)S(1)}, bf16[224,128]{1,0:T(8,128)(2,1)S(1)}, u32[]{:S(2)}, u32[]{:S(2)}) collective-permute-start(bf16[224,128]{1,0:T(8,128)(2,1)S(1)} %add_convert_fusion), channel_id=1, source_target_pairs={{0,8},{8,0},{16,24},{24,16},{1,9},{9,1},{17,25},{25,17},{2,10},{10... | collective-permute-start | bytes 172040 | tf_op jit(solution)/shard_map/ppermute | solution.py:410
  41.8 1.6 %collective-permute-start.14 = (bf16[4,224,128]{2,1,0:T(8,128)(2,1)S(1)}, bf16[4,224,128]{2,1,0:T(8,128)(2,1)S(1)}, u32[]{:S(2)}, u32[]{:S(2)}) collective-permute-start(bf16[4,224,128]{2,1,0:T(8,128)(2,1)S(1)} %pad_maximum_fusion.mine), channel_id=1, source_target_pairs={{0,1},{1,0},{2,3},{3,2},{4,5},{5,4},{6,7},{7,6},{8,9},{9,8},{10,11... | collective-permute-start | bytes 688136 | tf_op jit(solution)/shard_map/ppermute | solution.py:439

commit v10 on v9

--- a/solution.py
+++ b/solution.py
@@ -108,8 +108,9 @@
 
 
 def middle_kernel(lats, grad_out, row_a, row_b, col_a, col_b, slope, act_t, fields_t, taps,
-                  spread, own, other,
-                  grid, wide, prods, ends, line, side, sides, sums, corner, keep):
+                  spread, *rest):
+    parts, scratch = rest[:lats], rest[lats:]
+    grid, wide, prods, ends, line, side, sides, sums, corner, keep = scratch
     band, first, last, even, core = position(lats)
     top = jnp.where(even, row_b[...], row_a[...])
     bottom = jnp.where(even, row_a[...], row_b[...])
@@ -197,8 +198,7 @@
     unit = c0
     per_tap = c1 // unit
     count = 9 * per_tap + 9
-    held = own.shape[0]
-    block = held // lats
+    block = parts[0].shape[0]
 
     def put(k, value):
         keep[k * unit:(k + 1) * unit, :] = value
@@ -233,12 +233,10 @@
             even = got[:c0, (2 - b) * c1:(3 - b) * c1]
             odd = got[c0:, (3 - b) * c1:(4 - b) * c1]
             put(9 * per_tap + 3 * a + b, even + odd)
-    if 2 * held > count * unit:
-        keep[count * unit:] = jnp.zeros((2 * held - count * unit, c1), F32)
-    for target, half_of in ((own, core), (other, 1 - core)):
-        for far in range(lats):
-            at = half_of * held + (band ^ far) * block
-            target[far * block:(far + 1) * block] = keep[pl.ds(pl.multiple_of(at, block), block), :]
+    if lats * block > count * unit:
+        keep[count * unit:] = jnp.zeros((lats * block - count * unit, c1), F32)
+    for far in range(lats):
+        parts[far][...] = keep[pl.ds(pl.multiple_of((band ^ far) * block, block), block), :]
 
 
 def last_kernel(spread, taps, out, total, turned):
@@ -270,14 +268,13 @@
     band, _, _, _, core = position(lats)
     size = out_second.shape[0]
     total = size + out_first.shape[0]
-    for h in range(2):
-        for i in range(lats):
-            at = (h * lats + i) * rows
-            for out, base, end in ((out_second, 0, size), (out_first, size, total)):
-                low, high = max(at, base), min(at + rows, end)
-                if low < high:
-                    here, there = (x[i ^ band, low - at:high - at] for x in (mine, theirs))
-                    out[low - base:high - base] = jnp.where(core == h, here, there).astype(F32)
+    for i in range(lats):
+        at = i * rows
+        for out, base, end in ((out_second, 0, size), (out_first, size, total)):
+            low, high = max(at, base), min(at + rows, end)
+            if low < high:
+                here, there = (x[i ^ band, low - at:high - at] for x in (mine, theirs))
+                out[low - base:high - base] = jnp.where(core == 1, here, there).astype(F32)
 
 
 def vmem(count):
@@ -375,18 +372,15 @@
     )(fields, w_first, w_second)
     col_a, col_b, fields_t = lax.optimization_barrier((col_a, col_b, fields_t))
 
-    block = -(-9 * (c1 + c0) // (32 * lats)) * 16
-    held = lats * block
+    block = -(-9 * (c1 + c0) // (16 * lats)) * 16
     span = half + EDGE
-    spread, own, other = pl.pallas_call(
+    spread, *parts = pl.pallas_call(
         functools.partial(middle_kernel, lats),
         out_shape=(
             shape((rows + 3, half, 4 * c1), BF16),
-            shape((held, c1), F32),
-            shape((held, c1), F32),
-        ),
+        ) + (shape((block, c1), F32),) * lats,
         in_specs=vmem(9),
-        out_specs=tuple(vmem(3)),
+        out_specs=tuple(vmem(lats + 1)),
         scratch_shapes=[
             pltpu.VMEM((pooled + 2, span, c1), F32),
             pltpu.VMEM((pooled + 2, span, 4 * c1), BF16),
@@ -397,22 +391,25 @@
             pltpu.VMEM((2, edge, c1), F32),
             pltpu.VMEM((4, 2 * c1, 3 * c1), F32),
             pltpu.VMEM((2 * c1, 3 * c1), F32),
-            pltpu.VMEM((2 * held, c1), F32),
+            pltpu.VMEM((lats * block, c1), F32),
         ],
         compiler_params=params(16),
         cost_estimate=pl.CostEstimate(flops=2 * rows * cols * c1 * 9 * (2 * c1 + c0), bytes_accessed=8 << 20,
                                       transcendentals=0),
     )(grad_out, row_a, row_b, col_a, col_b, slope, act_t, fields_t, taps_second)
 
-    swap = [(i, i ^ 1) for i in range(lons)]
-
-    def along_lat(far, value):
-        return lax.ppermute(value, "lat", [(i, i ^ far) for i in range(lats)])
-
-    parts = (own + lax.ppermute(other, "lon", swap)).reshape(lats, block, c1)
-    sent = [parts[far].astype(BF16) for far in range(1, lats)]
-    *sent, spread = lax.optimization_barrier((*sent, spread))
-    got = [along_lat(far + 1, value) for far, value in enumerate(sent)]
+    def swapped(value):
+        return lax.ppermute(value, "lon", [(i, i ^ 1) for i in range(lons)])
+
+    def between_chips(value, over_lat, over_lon):
+        return lax.ppermute(value, AREA, [
+            (i * lons + j, (i ^ over_lat * (j % 2)) * lons + (j ^ 2 * over_lon * (j % 2)))
+            for i in range(lats) for j in range(lons)])
+
+    order = [*range(1, lats), 0]
+    added = {far: swapped(parts[far]) for far in order}
+    added = {far: parts[far] + added[far] for far in order}
+    got = [between_chips(added[far].astype(BF16), far, 0) for far in range(1, lats)]
     grad_inputs = pl.pallas_call(
         last_kernel,
         out_shape=shape((rows, c0, cols), BF16),
@@ -426,17 +423,18 @@
         cost_estimate=pl.CostEstimate(flops=2 * rows * cols * c1 * 9 * c0, bytes_accessed=3 << 20, transcendentals=0),
     )(spread, taps_first)
     *got, grad_inputs = lax.optimization_barrier((*got, grad_inputs))
-    total = parts[0]
+    total = added[0]
     for value in got:
         total = total + value.astype(F32)
     part = total.astype(BF16)
-    terms = [part] + [lax.ppermute(part, "lon", [(i, i ^ (2 * k)) for i in range(lons)]) for k in range(1, depths)]
+    terms = [part] + [between_chips(part, 0, far) for far in range(1, depths)]
     terms = [term.astype(F32) for term in terms]
     while len(terms) > 1:
         terms = [terms[k] + terms[k + 1] for k in range(0, len(terms), 2)]
     part = terms[0].astype(BF16)
-    mine = jnp.stack([part] + [along_lat(far, part) for far in range(1, lats)], 0)
-    theirs = lax.ppermute(mine, "lon", swap)
+    mine = [part] + [between_chips(part, far, 0) for far in range(1, lats)]
+    theirs = [swapped(value) for value in mine]
+    mine, theirs = jnp.stack(mine, 0), jnp.stack(theirs, 0)
 
     grad_w_first, grad_w_second = pl.pallas_call(
         gather_kernel,

time: 44.6 us -> 57.5 us (1.29)
  starting transfers between devices: 17.9 us -> 39.7 us
  waiting for transfers between devices: 16.1 us -> 6.72 us
    ppermute x11 -> x17, starting transfers between devices: 11.7 us -> 33.5 us  [the longest x8 27.5 us: swapped(): return lax.ppermute(value, 'lon', [(i, i ^ 1) for i in range(lons)])]
    ppermute x11 -> x17, waiting for transfers between devices: 10.7 us -> 1.36 us  [the longest x8 1.34 us: swapped(): return lax.ppermute(value, 'lon', [(i, i ^ 1) for i in range(lons)])]
  transfers between devices with their start and end apart: 15 -> 21, of which waited for: 11 -> 5; matrix products, arithmetic and copies ran while one was open for 0% -> 0% of each run, Pallas kernels for 8% -> 6%
where the time goes in v10:
time: 57.5 us; the launch traced here: 57.2 us
  starting transfers between devices  39.7 us (69%)
  Pallas kernels  7.34 us (13%)
  waiting for transfers between devices  6.72 us (12%)
  local copies, waits for them, and re-layouts  2.05 us (4%)
  between operations  0.9 us (2%)
    ppermute x8, starting transfers between devices, swapped(): return lax.ppermute(value, 'lon', [(i, i ^ 1) for i in range(lons)])  27.5 us
    ppermute x9, starting transfers between devices, between_chips(): lax.ppermute(value, AREA, [(i * lons + j, (i ^ over_lat * (j % 2)) * lons...  6.01 us
    ppermute x1, starting transfers between devices, body(): row_b = lax.ppermute(row_b, AREA, pairs)  4.1 us
    ppermute x1, waiting for transfers between devices, body(): lax.ppermute(col_b, 'lon', [(i, (i + 2 * (i % 2) - 1) % lons) for i in ra...  2.69 us
    pallas_call x1, Pallas kernels, body(): pl.pallas_call(functools.partial(middle_kernel, lats), out_shape=(shape((...  2.65 us
    pallas_call x1, Pallas kernels, body(): pl.pallas_call(last_kernel, out_shape=shape((rows, c0, cols), BF16), in_s...  2.19 us
    unnamed x12, local copies, waits for them, and re-layouts  1.95 us
    ppermute x1, waiting for transfers between devices, body(): row_a = lax.ppermute(row_a, AREA, every)  1.49 us
  transfers between devices with their start and end apart: 21, of which 5 were waited for; matrix products, arithmetic and copies ran while one was open for 0% of the time, Pallas kernels for 6%

profile of v10, /device:TPU:0, one launch (start us, length us, event | category | flops | bytes accessed | tf_op | source)
XLA Modules:
  0.0 57.2 jit_solution(15590601747164628962)
XLA Ops:
  0.6 0.0 copy-start
  0.6 1.0 %copy-done = bf16[16,128,128]{2,1,0:T(8,128)(2,1)S(1)} copy-done((bf16[16,128,128]{2,1,0:T(8,128)(2,1)S(1)}, bf16[16,128,128]{2,1,0:T(8,128)(2,1)}, u32[]{:S(2)}) %copy-start) | copy-done | bytes 524312
  1.7 0.0 copy-start.4
  1.7 0.9 %copy-done.4 = bf16[8,64,128]{2,1,0:T(8,128)(2,1)S(1)} copy-done((bf16[8,64,128]{2,1,0:T(8,128)(2,1)S(1)}, bf16[8,64,128]{2,1,0:T(8,128)(2,1)}, u32[]{:S(2)}) %copy-start.4) | copy-done | bytes 131096
  2.6 0.0 copy-start.1
  2.6 0.0 copy-start.2
  2.6 0.1 shard_map.76
  2.7 4.1 %collective-permute-start = (bf16[192,128]{1,0:T(8,128)(2,1)S(1)}, bf16[192,128]{1,0:T(8,128)(2,1)S(1)}, u32[]{:S(2)}, u32[]{:S(2)}) collective-permute-start(bf16[192,128]{1,0:T(8,128)(2,1)S(1)} %get-tuple-element.31), channel_id=1, source_target_pairs={{0,4},{1,5},{2,6},{3,7},{4,0},{5,1},{6,2},{7,3},{24,28},{25,29},{2... | collective-permute-start | bytes 147464 | tf_op jit(solution)/shard_map/ppermute | solution.py:325
  6.8 0.4 collective-permute-start.1
  7.2 0.1 pad.13.clone
  7.2 0.9 %shard_map.77 = (f32[16,64,256]{2,1,0:T(8,128)S(1)}, bf16[2,256,512]{2,1,0:T(8,128)(2,1)S(1)}) custom-call(bf16[16,128,128]{2,1,0:T(8,128)(2,1)S(1)} %get-tuple-element.33.pre), custom_call_target="tpu_custom_call" | custom-call | flops 15728640 | bytes 2097152 | tf_op jit(solution)/shard_map/pallas_call | solution.py:328
  8.2 1.2 %collective-permute-done.row_b = bf16[192,128]{1,0:T(8,128)(2,1)S(1)} collective-permute-done((bf16[192,128]{1,0:T(8,128)(2,1)S(1)}, bf16[192,128]{1,0:T(8,128)(2,1)S(1)}, u32[]{:S(2)}, u32[]{:S(2)}) %collective-permute-start) | collective-permute-done | bytes 49184 | tf_op jit(solution)/shard_map/ppermute | solution.py:325
  9.4 1.5 %collective-permute-done.1.row_a = bf16[192,128]{1,0:T(8,128)(2,1)S(1)} collective-permute-done((bf16[192,128]{1,0:T(8,128)(2,1)S(1)}, bf16[192,128]{1,0:T(8,128)(2,1)S(1)}, u32[]{:S(2)}, u32[]{:S(2)}) %collective-permute-start.1) | collective-permute-done | bytes 49184 | tf_op jit(solution)/shard_map/ppermute | solution.py:326
  10.9 0.1 maximum_maximum_fusion.1
  11.0 0.8 %collective-permute-start.3 = (bf16[32,128]{1,0:T(8,128)(2,1)S(1)}, bf16[32,128]{1,0:T(8,128)(2,1)S(1)}, u32[]{:S(2)}, u32[]{:S(2)}) collective-permute-start(bf16[32,128]{1,0:T(8,128)(2,1)S(1)} %get-tuple-element.71), channel_id=1, source_target_pairs={{0,7},{1,2},{2,1},{3,4},{4,3},{5,6},{6,5},{7,0},{8,15},{9,10},{10,... | collective-permute-start | bytes 24584 | tf_op jit(solution)/shard_map/ppermute | solution.py:357
  11.8 0.9 %collective-permute-start.2 = (bf16[32,128]{1,0:T(8,128)(2,1)S(1)}, bf16[32,128]{1,0:T(8,128)(2,1)S(1)}, u32[]{:S(2)}, u32[]{:S(2)}) collective-permute-start(bf16[32,128]{1,0:T(8,128)(2,1)S(1)} %get-tuple-element.72), channel_id=1, source_target_pairs={{0,1},{1,0},{2,3},{3,2},{4,5},{5,4},{6,7},{7,6},{8,9},{9,8},{10,11... | collective-permute-start | bytes 24584 | tf_op jit(solution)/shard_map/ppermute | solution.py:358
  12.7 0.0 copy-done.1
  12.7 0.0 copy-done.2
  12.7 0.0 copy-done.3
  12.7 0.5 shard_map.78
  13.2 2.7 %collective-permute-done.3.col_b = bf16[32,128]{1,0:T(8,128)(2,1)S(1)} collective-permute-done((bf16[32,128]{1,0:T(8,128)(2,1)S(1)}, bf16[32,128]{1,0:T(8,128)(2,1)S(1)}, u32[]{:S(2)}, u32[]{:S(2)}) %collective-permute-start.3) | collective-permute-done | bytes 8224 | tf_op jit(solution)/shard_map/ppermute | solution.py:357
  15.9 0.0 collective-permute-done.2.col_a
  15.9 0.0 copy-done.5
  15.9 2.6 %shard_map.79 = (bf16[19,64,512]{2,1,0:T(8,128)(2,1)S(1)}, f32[432,128]{1,0:T(8,128)S(1)}, f32[432,128]{1,0:T(8,128)S(1)}, f32[432,128]{1,0:T(8,128)S(1)}, f32[432,128]{1,0:T(8,128)S(1)}) custom-call(bf16[8,64,128]{2,1,0:T(8,128)(2,1)S(1)} %copy-done.5, bf16[192,128]{1,0:T(8,128)(2,1)S(1)} %collective-permute-done.1.row_a, ...), custom_call_target="tpu_custom_call" | custom-call | flops 1509949440 | bytes 8388608 | tf_op jit(solution)/shard_map/pallas_call | solution.py:377
  18.5 0.1 collective-permute-start.4
  18.6 0.5 collective-permute-start.6
  19.1 0.1 collective-permute-start.8
  19.2 0.4 collective-permute-start.10
  19.6 0.5 collective-permute-done.4
  20.1 0.7 %collective-permute-start.5 = (bf16[432,128]{1,0:T(8,128)(2,1)S(1)}, bf16[432,128]{1,0:T(8,128)(2,1)S(1)}, u32[]{:S(2)}, u32[]{:S(2)}) collective-permute-start(bf16[432,128]{1,0:T(8,128)(2,1)S(1)} %add_convert_fusion.4), channel_id=1, source_target_pairs={{0,0},{1,9},{2,2},{3,11},{4,4},{5,13},{6,6},{7,15},{8,8},{9,1},{10... | collective-permute-start | bytes 331784 | tf_op jit(solution)/shard_map/ppermute | solution.py:405
  20.8 0.0 collective-permute-done.6
  20.8 0.7 %collective-permute-start.7 = (bf16[432,128]{1,0:T(8,128)(2,1)S(1)}, bf16[432,128]{1,0:T(8,128)(2,1)S(1)}, u32[]{:S(2)}, u32[]{:S(2)}) collective-permute-start(bf16[432,128]{1,0:T(8,128)(2,1)S(1)} %add_convert_fusion.3), channel_id=1, source_target_pairs={{0,0},{1,17},{2,2},{3,19},{4,4},{5,21},{6,6},{7,23},{8,8},{9,25},{... | collective-permute-start | bytes 331784 | tf_op jit(solution)/shard_map/ppermute | solution.py:405
  21.5 0.0 collective-permute-done.8
  21.5 0.7 %collective-permute-start.9 = (bf16[432,128]{1,0:T(8,128)(2,1)S(1)}, bf16[432,128]{1,0:T(8,128)(2,1)S(1)}, u32[]{:S(2)}, u32[]{:S(2)}) collective-permute-start(bf16[432,128]{1,0:T(8,128)(2,1)S(1)} %add_convert_fusion.2), channel_id=1, source_target_pairs={{0,0},{1,25},{2,2},{3,27},{4,4},{5,29},{6,6},{7,31},{8,8},{9,17},{... | collective-permute-start | bytes 331784 | tf_op jit(solution)/shard_map/ppermute | solution.py:405
  22.2 2.2 %shard_map.80 = bf16[16,64,128]{2,1,0:T(8,128)(2,1)} custom-call(bf16[19,64,512]{2,1,0:T(8,128)(2,1)S(1)} %get-tuple-element.50.spread, bf16[384,512]{1,0:T(8,128)(2,1)S(1)} %get-tuple-element.51.taps), custom_call_target="tpu_custom_call" | custom-call | flops 301989888 | bytes 3145728 | tf_op jit(solution)/shard_map/pallas_call | solution.py:413
  24.4 0.0 collective-permute-done.5
  24.4 0.0 collective-permute-done.7
  24.4 0.0 collective-permute-done.9
  24.4 0.0 collective-permute-done.10
  24.4 0.1 add_convert_fusion.1
  24.5 0.7 %collective-permute-start.13 = (bf16[432,128]{1,0:T(8,128)(2,1)S(1)}, bf16[432,128]{1,0:T(8,128)(2,1)S(1)}, u32[]{:S(2)}, u32[]{:S(2)}) collective-permute-start(bf16[432,128]{1,0:T(8,128)(2,1)S(1)} %add_convert_fusion.1), channel_id=1, source_target_pairs={{0,0},{1,7},{2,2},{3,5},{4,4},{5,3},{6,6},{7,1},{8,8},{9,15},{10,1... | collective-permute-start | bytes 331784 | tf_op jit(solution)/shard_map/ppermute | solution.py:405
  25.2 0.7 %collective-permute-start.12 = (bf16[432,128]{1,0:T(8,128)(2,1)S(1)}, bf16[432,128]{1,0:T(8,128)(2,1)S(1)}, u32[]{:S(2)}, u32[]{:S(2)}) collective-permute-start(bf16[432,128]{1,0:T(8,128)(2,1)S(1)} %add_convert_fusion.1), channel_id=1, source_target_pairs={{0,0},{1,5},{2,2},{3,7},{4,4},{5,1},{6,6},{7,3},{8,8},{9,13},{10,1... | collective-permute-start | bytes 331784 | tf_op jit(solution)/shard_map/ppermute | solution.py:405
  25.9 0.7 %collective-permute-start.11 = (bf16[432,128]{1,0:T(8,128)(2,1)S(1)}, bf16[432,128]{1,0:T(8,128)(2,1)S(1)}, u32[]{:S(2)}, u32[]{:S(2)}) collective-permute-start(bf16[432,128]{1,0:T(8,128)(2,1)S(1)} %add_convert_fusion.1), channel_id=1, source_target_pairs={{0,0},{1,3},{2,2},{3,1},{4,4},{5,7},{6,6},{7,5},{8,8},{9,11},{10,1... | collective-permute-start | bytes 331784 | tf_op jit(solution)/shard_map/ppermute | solution.py:405
  26.5 0.0 collective-permute-done.13
  26.6 0.0 collective-permute-done.12
  26.6 0.0 collective-permute-done.11
  26.6 0.1 add_convert_fusion
  26.6 0.7 %collective-permute-start.16 = (bf16[432,128]{1,0:T(8,128)(2,1)S(1)}, bf16[432,128]{1,0:T(8,128)(2,1)S(1)}, u32[]{:S(2)}, u32[]{:S(2)}) collective-permute-start(bf16[432,128]{1,0:T(8,128)(2,1)S(1)} %add_convert_fusion), channel_id=1, source_target_pairs={{0,0},{1,25},{2,2},{3,27},{4,4},{5,29},{6,6},{7,31},{8,8},{9,17},{... | collective-permute-start | bytes 331784 | tf_op jit(solution)/shard_map/ppermute | solution.py:405
  27.3 0.7 %collective-permute-start.15 = (bf16[432,128]{1,0:T(8,128)(2,1)S(1)}, bf16[432,128]{1,0:T(8,128)(2,1)S(1)}, u32[]{:S(2)}, u32[]{:S(2)}) collective-permute-start(bf16[432,128]{1,0:T(8,128)(2,1)S(1)} %add_convert_fusion), channel_id=1, source_target_pairs={{0,0},{1,17},{2,2},{3,19},{4,4},{5,21},{6,6},{7,23},{8,8},{9,25},{... | collective-permute-start | bytes 331784 | tf_op jit(solution)/shard_map/ppermute | solution.py:405
  28.0 0.7 %collective-permute-start.14 = (bf16[432,128]{1,0:T(8,128)(2,1)S(1)}, bf16[432,128]{1,0:T(8,128)(2,1)S(1)}, u32[]{:S(2)}, u32[]{:S(2)}) collective-permute-start(bf16[432,128]{1,0:T(8,128)(2,1)S(1)} %add_convert_fusion), channel_id=1, source_target_pairs={{0,0},{1,9},{2,2},{3,11},{4,4},{5,13},{6,6},{7,15},{8,8},{9,1},{10... | collective-permute-start | bytes 331784 | tf_op jit(solution)/shard_map/ppermute | solution.py:405
  28.7 24.4 %collective-permute-start.17 = (bf16[432,128]{1,0:T(8,128)(2,1)S(1)}, bf16[432,128]{1,0:T(8,128)(2,1)S(1)}, u32[]{:S(2)}, u32[]{:S(2)}) collective-permute-start(bf16[432,128]{1,0:T(8,128)(2,1)S(1)} %add_convert_fusion), channel_id=1, source_target_pairs={{0,1},{1,0},{2,3},{3,2},{4,5},{5,4},{6,7},{7,6},{8,9},{9,8},{10,11... | collective-permute-start | bytes 331784 | tf_op jit(solution)/shard_map/ppermute | solution.py:402
  53.1 0.0 collective-permute-done.16
  53.1 0.1 collective-permute-start.20
  53.1 0.0 collective-permute-done.15
  53.1 0.4 collective-permute-start.19
  53.6 0.0 collective-permute-done.14
  53.6 1.5 %collective-permute-start.18 = (bf16[432,128]{1,0:T(8,128)(2,1)S(1)}, bf16[432,128]{1,0:T(8,128)(2,1)S(1)}, u32[]{:S(2)}, u32[]{:S(2)}) collective-permute-start(bf16[432,128]{1,0:T(8,128)(2,1)S(1)} %collective-permute-done.14), channel_id=1, source_target_pairs={{0,1},{1,0},{2,3},{3,2},{4,5},{5,4},{6,7},{7,6},{8,9},{9,8},{10,11... | collective-permute-start | bytes 331784 | tf_op jit(solution)/shard_map/ppermute | solution.py:402
  55.1 0.1 pad_maximum_fusion.mine
  55.2 0.0 collective-permute-done.17
  55.2 0.0 collective-permute-done.20
  55.2 0.0 collective-permute-done.19
  55.2 0.9 %collective-permute-done.18 = bf16[432,128]{1,0:T(8,128)(2,1)S(1)} collective-permute-done((bf16[432,128]{1,0:T(8,128)(2,1)S(1)}, bf16[432,128]{1,0:T(8,128)(2,1)S(1)}, u32[]{:S(2)}, u32[]{:S(2)}) %collective-permute-start.18) | collective-permute-done | bytes 110624 | tf_op jit(solution)/shard_map/ppermute | solution.py:402
  56.1 0.1 pad_maximum_fusion.1.theirs
  56.1 1.0 %shard_map.81 = (f32[576,128]{1,0:T(8,128)}, f32[1152,128]{1,0:T(8,128)}) custom-call(bf16[4,432,128]{2,1,0:T(8,128)(2,1)S(1)} %pad_maximum_fusion.mine, bf16[4,432,128]{2,1,0:T(8,128)(2,1)S(1)} %pad_maximum_fusion.1.theirs), custom_call_target="tpu_custom_call" | custom-call | flops 1000 | bytes 1572864 | tf_op jit(solution)/shard_map/pallas_call | solution.py:439
  (11 shorter events, 0.1 us)
Async XLA Ops:
  0.6 1.0 %copy-start = (bf16[16,128,128]{2,1,0:T(8,128)(2,1)S(1)}, bf16[16,128,128]{2,1,0:T(8,128)(2,1)}, u32[]{:S(2)}) copy-start(bf16[16,128,128]{2,1,0:T(8,128)(2,1)} %pre.1) | copy-start | bytes 1572868
  1.7 0.9 %copy-start.4 = (bf16[8,64,128]{2,1,0:T(8,128)(2,1)S(1)}, bf16[8,64,128]{2,1,0:T(8,128)(2,1)}, u32[]{:S(2)}) copy-start(bf16[8,64,128]{2,1,0:T(8,128)(2,1)} %grad_out.3) | copy-start | bytes 393220
  2.6 10.1 %copy-start.1 = (bf16[3,3,128,128]{3,2,1,0:T(8,128)(2,1)S(1)}, bf16[3,3,128,128]{3,2,1,0:T(8,128)(2,1)}, u32[]{:S(2)}) copy-start(bf16[3,3,128,128]{3,2,1,0:T(8,128)(2,1)} %w_second.1) | copy-start | bytes 884740
  2.6 10.1 %copy-start.2 = (bf16[16,128,64]{1,2,0:T(8,128)(2,1)S(1)}, bf16[16,128,64]{1,2,0:T(8,128)(2,1)}, u32[]{:S(2)}) copy-start(bf16[16,128,64]{1,2,0:T(8,128)(2,1)} %param.5) | copy-start | bytes 786436
  2.6 10.1 %copy-start.3 = (bf16[3,3,64,128]{3,2,1,0:T(8,128)(2,1)S(1)}, bf16[3,3,64,128]{3,2,1,0:T(8,128)(2,1)}, u32[]{:S(2)}) copy-start(bf16[3,3,64,128]{3,2,1,0:T(8,128)(2,1)} %w_first.1) | copy-start | bytes 442372
  2.6 13.3 %copy-start.5 = (bf16[8,64,128]{2,1,0:T(8,128)(2,1)S(1)}, bf16[8,64,128]{2,1,0:T(8,128)(2,1)}, u32[]{:S(2)}) copy-start(bf16[8,64,128]{2,1,0:T(8,128)(2,1)} %grad_out.3) | copy-start | bytes 393220
  2.7 6.7 %collective-permute-start = (bf16[192,128]{1,0:T(8,128)(2,1)S(1)}, bf16[192,128]{1,0:T(8,128)(2,1)S(1)}, u32[]{:S(2)}, u32[]{:S(2)}) collective-permute-start(bf16[192,128]{1,0:T(8,128)(2,1)S(1)} %get-tuple-element.31), channel_id=1, source_target_pairs={{0,4},{1,5},{2,6},{3,7},{4,0},{5,1},{6,2},{7,3},{24,28},{25,29},{2... | collective-permute-start | bytes 147464 | tf_op jit(solution)/shard_map/ppermute | solution.py:325
  6.8 4.1 %collective-permute-start.1 = (bf16[192,128]{1,0:T(8,128)(2,1)S(1)}, bf16[192,128]{1,0:T(8,128)(2,1)S(1)}, u32[]{:S(2)}, u32[]{:S(2)}) collective-permute-start(bf16[192,128]{1,0:T(8,128)(2,1)S(1)} %get-tuple-element.32), channel_id=1, source_target_pairs={{0,8},{1,9},{2,10},{3,11},{4,12},{5,13},{6,14},{7,15},{8,0},{9,1},... | collective-permute-start | bytes 147464 | tf_op jit(solution)/shard_map/ppermute | solution.py:326
  11.0 4.9 %collective-permute-start.3 = (bf16[32,128]{1,0:T(8,128)(2,1)S(1)}, bf16[32,128]{1,0:T(8,128)(2,1)S(1)}, u32[]{:S(2)}, u32[]{:S(2)}) collective-permute-start(bf16[32,128]{1,0:T(8,128)(2,1)S(1)} %get-tuple-element.71), channel_id=1, source_target_pairs={{0,7},{1,2},{2,1},{3,4},{4,3},{5,6},{6,5},{7,0},{8,15},{9,10},{10,... | collective-permute-start | bytes 24584 | tf_op jit(solution)/shard_map/ppermute | solution.py:357
  11.8 4.1 %collective-permute-start.2 = (bf16[32,128]{1,0:T(8,128)(2,1)S(1)}, bf16[32,128]{1,0:T(8,128)(2,1)S(1)}, u32[]{:S(2)}, u32[]{:S(2)}) collective-permute-start(bf16[32,128]{1,0:T(8,128)(2,1)S(1)} %get-tuple-element.72), channel_id=1, source_target_pairs={{0,1},{1,0},{2,3},{3,2},{4,5},{5,4},{6,7},{7,6},{8,9},{9,8},{10,11... | collective-permute-start | bytes 24584 | tf_op jit(solution)/shard_map/ppermute | solution.py:358
  18.5 1.5 %collective-permute-start.4 = (f32[432,128]{1,0:T(8,128)S(1)}, f32[432,128]{1,0:T(8,128)S(1)}, u32[]{:S(2)}, u32[]{:S(2)}) collective-permute-start(f32[432,128]{1,0:T(8,128)S(1)} %get-tuple-element.47), channel_id=1, source_target_pairs={{0,1},{1,0},{2,3},{3,2},{4,5},{5,4},{6,7},{7,6},{8,9},{9,8},{10,11... | collective-permute-start | bytes 663560 | tf_op jit(solution)/shard_map/ppermute | solution.py:402
  18.6 2.2 %collective-permute-start.6 = (f32[432,128]{1,0:T(8,128)S(1)}, f32[432,128]{1,0:T(8,128)S(1)}, u32[]{:S(2)}, u32[]{:S(2)}) collective-permute-start(f32[432,128]{1,0:T(8,128)S(1)} %get-tuple-element.48), channel_id=1, source_target_pairs={{0,1},{1,0},{2,3},{3,2},{4,5},{5,4},{6,7},{7,6},{8,9},{9,8},{10,11... | collective-permute-start | bytes 663560 | tf_op jit(solution)/shard_map/ppermute | solution.py:402
  19.1 2.4 %collective-permute-start.8 = (f32[432,128]{1,0:T(8,128)S(1)}, f32[432,128]{1,0:T(8,128)S(1)}, u32[]{:S(2)}, u32[]{:S(2)}) collective-permute-start(f32[432,128]{1,0:T(8,128)S(1)} %get-tuple-element.49), channel_id=1, source_target_pairs={{0,1},{1,0},{2,3},{3,2},{4,5},{5,4},{6,7},{7,6},{8,9},{9,8},{10,11... | collective-permute-start | bytes 663560 | tf_op jit(solution)/shard_map/ppermute | solution.py:402
  19.2 5.2 %collective-permute-start.10 = (f32[432,128]{1,0:T(8,128)S(1)}, f32[432,128]{1,0:T(8,128)S(1)}, u32[]{:S(2)}, u32[]{:S(2)}) collective-permute-start(f32[432,128]{1,0:T(8,128)S(1)} %get-tuple-element.53), channel_id=1, source_target_pairs={{0,1},{1,0},{2,3},{3,2},{4,5},{5,4},{6,7},{7,6},{8,9},{9,8},{10,11... | collective-permute-start | bytes 663560 | tf_op jit(solution)/shard_map/ppermute | solution.py:402
  20.1 4.3 %collective-permute-start.5 = (bf16[432,128]{1,0:T(8,128)(2,1)S(1)}, bf16[432,128]{1,0:T(8,128)(2,1)S(1)}, u32[]{:S(2)}, u32[]{:S(2)}) collective-permute-start(bf16[432,128]{1,0:T(8,128)(2,1)S(1)} %add_convert_fusion.4), channel_id=1, source_target_pairs={{0,0},{1,9},{2,2},{3,11},{4,4},{5,13},{6,6},{7,15},{8,8},{9,1},{10... | collective-permute-start | bytes 331784 | tf_op jit(solution)/shard_map/ppermute | solution.py:405
  20.8 3.6 %collective-permute-start.7 = (bf16[432,128]{1,0:T(8,128)(2,1)S(1)}, bf16[432,128]{1,0:T(8,128)(2,1)S(1)}, u32[]{:S(2)}, u32[]{:S(2)}) collective-permute-start(bf16[432,128]{1,0:T(8,128)(2,1)S(1)} %add_convert_fusion.3), channel_id=1, source_target_pairs={{0,0},{1,17},{2,2},{3,19},{4,4},{5,21},{6,6},{7,23},{8,8},{9,25},{... | collective-permute-start | bytes 331784 | tf_op jit(solution)/shard_map/ppermute | solution.py:405
  21.5 2.9 %collective-permute-start.9 = (bf16[432,128]{1,0:T(8,128)(2,1)S(1)}, bf16[432,128]{1,0:T(8,128)(2,1)S(1)}, u32[]{:S(2)}, u32[]{:S(2)}) collective-permute-start(bf16[432,128]{1,0:T(8,128)(2,1)S(1)} %add_convert_fusion.2), channel_id=1, source_target_pairs={{0,0},{1,25},{2,2},{3,27},{4,4},{5,29},{6,6},{7,31},{8,8},{9,17},{... | collective-permute-start | bytes 331784 | tf_op jit(solution)/shard_map/ppermute | solution.py:405
  24.5 2.0 %collective-permute-start.13 = (bf16[432,128]{1,0:T(8,128)(2,1)S(1)}, bf16[432,128]{1,0:T(8,128)(2,1)S(1)}, u32[]{:S(2)}, u32[]{:S(2)}) collective-permute-start(bf16[432,128]{1,0:T(8,128)(2,1)S(1)} %add_convert_fusion.1), channel_id=1, source_target_pairs={{0,0},{1,7},{2,2},{3,5},{4,4},{5,3},{6,6},{7,1},{8,8},{9,15},{10,1... | collective-permute-start | bytes 331784 | tf_op jit(solution)/shard_map/ppermute | solution.py:405
  25.2 1.4 %collective-permute-start.12 = (bf16[432,128]{1,0:T(8,128)(2,1)S(1)}, bf16[432,128]{1,0:T(8,128)(2,1)S(1)}, u32[]{:S(2)}, u32[]{:S(2)}) collective-permute-start(bf16[432,128]{1,0:T(8,128)(2,1)S(1)} %add_convert_fusion.1), channel_id=1, source_target_pairs={{0,0},{1,5},{2,2},{3,7},{4,4},{5,1},{6,6},{7,3},{8,8},{9,13},{10,1... | collective-permute-start | bytes 331784 | tf_op jit(solution)/shard_map/ppermute | solution.py:405
  25.9 0.7 %collective-permute-start.11 = (bf16[432,128]{1,0:T(8,128)(2,1)S(1)}, bf16[432,128]{1,0:T(8,128)(2,1)S(1)}, u32[]{:S(2)}, u32[]{:S(2)}) collective-permute-start(bf16[432,128]{1,0:T(8,128)(2,1)S(1)} %add_convert_fusion.1), channel_id=1, source_target_pairs={{0,0},{1,3},{2,2},{3,1},{4,4},{5,7},{6,6},{7,5},{8,8},{9,11},{10,1... | collective-permute-start | bytes 331784 | tf_op jit(solution)/shard_map/ppermute | solution.py:405
  26.6 26.4 %collective-permute-start.16 = (bf16[432,128]{1,0:T(8,128)(2,1)S(1)}, bf16[432,128]{1,0:T(8,128)(2,1)S(1)}, u32[]{:S(2)}, u32[]{:S(2)}) collective-permute-start(bf16[432,128]{1,0:T(8,128)(2,1)S(1)} %add_convert_fusion), channel_id=1, source_target_pairs={{0,0},{1,25},{2,2},{3,27},{4,4},{5,29},{6,6},{7,31},{8,8},{9,17},{... | collective-permute-start | bytes 331784 | tf_op jit(solution)/shard_map/ppermute | solution.py:405
  27.3 25.8 %collective-permute-start.15 = (bf16[432,128]{1,0:T(8,128)(2,1)S(1)}, bf16[432,128]{1,0:T(8,128)(2,1)S(1)}, u32[]{:S(2)}, u32[]{:S(2)}) collective-permute-start(bf16[432,128]{1,0:T(8,128)(2,1)S(1)} %add_convert_fusion), channel_id=1, source_target_pairs={{0,0},{1,17},{2,2},{3,19},{4,4},{5,21},{6,6},{7,23},{8,8},{9,25},{... | collective-permute-start | bytes 331784 | tf_op jit(solution)/shard_map/ppermute | solution.py:405
  28.0 25.6 %collective-permute-start.14 = (bf16[432,128]{1,0:T(8,128)(2,1)S(1)}, bf16[432,128]{1,0:T(8,128)(2,1)S(1)}, u32[]{:S(2)}, u32[]{:S(2)}) collective-permute-start(bf16[432,128]{1,0:T(8,128)(2,1)S(1)} %add_convert_fusion), channel_id=1, source_target_pairs={{0,0},{1,9},{2,2},{3,11},{4,4},{5,13},{6,6},{7,15},{8,8},{9,1},{10... | collective-permute-start | bytes 331784 | tf_op jit(solution)/shard_map/ppermute | solution.py:405
  28.7 26.5 %collective-permute-start.17 = (bf16[432,128]{1,0:T(8,128)(2,1)S(1)}, bf16[432,128]{1,0:T(8,128)(2,1)S(1)}, u32[]{:S(2)}, u32[]{:S(2)}) collective-permute-start(bf16[432,128]{1,0:T(8,128)(2,1)S(1)} %add_convert_fusion), channel_id=1, source_target_pairs={{0,1},{1,0},{2,3},{3,2},{4,5},{5,4},{6,7},{7,6},{8,9},{9,8},{10,11... | collective-permute-start | bytes 331784 | tf_op jit(solution)/shard_map/ppermute | solution.py:402
  53.1 2.1 %collective-permute-start.20 = (bf16[432,128]{1,0:T(8,128)(2,1)S(1)}, bf16[432,128]{1,0:T(8,128)(2,1)S(1)}, u32[]{:S(2)}, u32[]{:S(2)}) collective-permute-start(bf16[432,128]{1,0:T(8,128)(2,1)S(1)} %collective-permute-done.16), channel_id=1, source_target_pairs={{0,1},{1,0},{2,3},{3,2},{4,5},{5,4},{6,7},{7,6},{8,9},{9,8},{10,11... | collective-permute-start | bytes 331784 | tf_op jit(solution)/shard_map/ppermute | solution.py:402
  53.1 2.0 %collective-permute-start.19 = (bf16[432,128]{1,0:T(8,128)(2,1)S(1)}, bf16[432,128]{1,0:T(8,128)(2,1)S(1)}, u32[]{:S(2)}, u32[]{:S(2)}) collective-permute-start(bf16[432,128]{1,0:T(8,128)(2,1)S(1)} %collective-permute-done.15), channel_id=1, source_target_pairs={{0,1},{1,0},{2,3},{3,2},{4,5},{5,4},{6,7},{7,6},{8,9},{9,8},{10,11... | collective-permute-start | bytes 331784 | tf_op jit(solution)/shard_map/ppermute | solution.py:402
  53.6 2.5 %collective-permute-start.18 = (bf16[432,128]{1,0:T(8,128)(2,1)S(1)}, bf16[432,128]{1,0:T(8,128)(2,1)S(1)}, u32[]{:S(2)}, u32[]{:S(2)}) collective-permute-start(bf16[432,128]{1,0:T(8,128)(2,1)S(1)} %collective-permute-done.14), channel_id=1, source_target_pairs={{0,1},{1,0},{2,3},{3,2},{4,5},{5,4},{6,7},{7,6},{8,9},{9,8},{10,11... | collective-permute-start | bytes 331784 | tf_op jit(solution)/shard_map/ppermute | solution.py:402

commit v11 on v9

--- a/solution.py
+++ b/solution.py
@@ -35,6 +35,17 @@
 def position(lats):
     band, place = lax.axis_index("lat"), lax.axis_index("lon")
     return band, band == 0, band == lats - 1, lax.rem(band, 2) == 0, lax.rem(place, 2)
+
+
+def odd(value):
+    for shift in (4, 2, 1):
+        value = value ^ (value >> shift)
+    return value & 1
+
+
+def half_held():
+    band, place = lax.axis_index("lat"), lax.axis_index("lon")
+    return odd(band) ^ odd(place // 2) ^ (place % 2)
 
 
 def pack_kernel(lats, pre, grad_out, row_a, row_b, col_a, col_b, held, hold):
@@ -235,7 +246,8 @@
             put(9 * per_tap + 3 * a + b, even + odd)
     if 2 * held > count * unit:
         keep[count * unit:] = jnp.zeros((2 * held - count * unit, c1), F32)
-    for target, half_of in ((own, core), (other, 1 - core)):
+    mine = half_held()
+    for target, half_of in ((own, mine), (other, 1 - mine)):
         for far in range(lats):
             at = half_of * held + (band ^ far) * block
             target[far * block:(far + 1) * block] = keep[pl.ds(pl.multiple_of(at, block), block), :]
@@ -267,7 +279,7 @@
 
 def gather_kernel(mine, theirs, out_first, out_second):
     lats, rows, c1 = mine.shape
-    band, _, _, _, core = position(lats)
+    band, held = lax.axis_index("lat"), half_held()
     size = out_second.shape[0]
     total = size + out_first.shape[0]
     for h in range(2):
@@ -277,7 +289,7 @@
                 low, high = max(at, base), min(at + rows, end)
                 if low < high:
                     here, there = (x[i ^ band, low - at:high - at] for x in (mine, theirs))
-                    out[low - base:high - base] = jnp.where(core == h, here, there).astype(F32)
+                    out[low - base:high - base] = jnp.where(held == h, here, there).astype(F32)
 
 
 def vmem(count):
@@ -406,13 +418,15 @@
 
     swap = [(i, i ^ 1) for i in range(lons)]
 
-    def along_lat(far, value):
-        return lax.ppermute(value, "lat", [(i, i ^ far) for i in range(lats)])
+    def between_chips(value, over_lat, over_lon):
+        turn = odd(over_lat) ^ odd(over_lon)
+        return lax.ppermute(value, AREA, [
+            (i * lons + j, (i ^ over_lat) * lons + (j ^ (2 * over_lon) ^ turn)) for i in range(lats) for j in range(lons)])
 
     parts = (own + lax.ppermute(other, "lon", swap)).reshape(lats, block, c1)
     sent = [parts[far].astype(BF16) for far in range(1, lats)]
     *sent, spread = lax.optimization_barrier((*sent, spread))
-    got = [along_lat(far + 1, value) for far, value in enumerate(sent)]
+    got = [between_chips(sent[far - 1], far, 0) for far in reversed(range(1, lats))]
     grad_inputs = pl.pallas_call(
         last_kernel,
         out_shape=shape((rows, c0, cols), BF16),
@@ -430,12 +444,12 @@
     for value in got:
         total = total + value.astype(F32)
     part = total.astype(BF16)
-    terms = [part] + [lax.ppermute(part, "lon", [(i, i ^ (2 * k)) for i in range(lons)]) for k in range(1, depths)]
+    terms = [part] + [between_chips(part, 0, far) for far in range(1, depths)]
     terms = [term.astype(F32) for term in terms]
     while len(terms) > 1:
         terms = [terms[k] + terms[k + 1] for k in range(0, len(terms), 2)]
     part = terms[0].astype(BF16)
-    mine = jnp.stack([part] + [along_lat(far, part) for far in range(1, lats)], 0)
+    mine = jnp.stack([part] + [between_chips(part, far, 0) for far in range(1, lats)], 0)
     theirs = lax.ppermute(mine, "lon", swap)
 
     grad_w_first, grad_w_second = pl.pallas_call(

time: 44.6 us -> 44.6 us (level)
  waiting for transfers between devices: 16.1 us -> 16.9 us
  starting transfers between devices: 17.9 us -> 17.2 us
    ppermute x9, waiting for transfers between devices: 7.46 us -> 8.33 us  [between_chips(): lax.ppermute(value, AREA, [(i * lons + j, (i ^ over_lat) * lons + (j ^ 2...]
    ppermute x9, starting transfers between devices: 11.6 us -> 10.7 us  [between_chips(): lax.ppermute(value, AREA, [(i * lons + j, (i ^ over_lat) * lons + (j ^ 2...]
where the time goes in v11:
time: 44.6 us; the launch traced here: 44.4 us
  starting transfers between devices  17.2 us (39%)
  waiting for transfers between devices  16.9 us (38%)
  Pallas kernels  7.33 us (16%)
  local copies, waits for them, and re-layouts  2.06 us (5%)
  between operations  0.75 us (2%)
    ppermute x9, starting transfers between devices, between_chips(): lax.ppermute(value, AREA, [(i * lons + j, (i ^ over_lat) * lons + (j ^ 2...  10.7 us
    ppermute x9, waiting for transfers between devices, between_chips(): lax.ppermute(value, AREA, [(i * lons + j, (i ^ over_lat) * lons + (j ^ 2...  8.33 us
    ppermute x1, starting transfers between devices, body(): row_b = lax.ppermute(row_b, AREA, pairs)  4.1 us
    ppermute x1, waiting for transfers between devices, body(): lax.ppermute(col_b, 'lon', [(i, (i + 2 * (i % 2) - 1) % lons) for i in ra...  2.69 us
    pallas_call x1, Pallas kernels, body(): pl.pallas_call(functools.partial(middle_kernel, lats), out_shape=(shape((...  2.66 us
    pallas_call x1, Pallas kernels, body(): pl.pallas_call(last_kernel, out_shape=shape((rows, c0, cols), BF16), in_s...  2.18 us
    unnamed x12, local copies, waits for them, and re-layouts  1.95 us
    ppermute x1, waiting for transfers between devices, body(): parts = (own + lax.ppermute(other, 'lon', swap)).reshape(lats, block, c1)  1.8 us
  transfers between devices with their start and end apart: 15, of which 11 were waited for; matrix products, arithmetic and copies ran while one was open for 0% of the time, Pallas kernels for 8%

profile of v11, /device:TPU:0, one launch (start us, length us, event | category | flops | bytes accessed | tf_op | source)
XLA Modules:
  0.0 44.4 jit_solution(10078493786238734813)
XLA Ops:
  0.6 0.0 copy-start
  0.6 1.0 %copy-done = bf16[16,128,128]{2,1,0:T(8,128)(2,1)S(1)} copy-done((bf16[16,128,128]{2,1,0:T(8,128)(2,1)S(1)}, bf16[16,128,128]{2,1,0:T(8,128)(2,1)}, u32[]{:S(2)}) %copy-start) | copy-done | bytes 524312
  1.7 0.0 copy-start.4
  1.7 0.9 %copy-done.4 = bf16[8,64,128]{2,1,0:T(8,128)(2,1)S(1)} copy-done((bf16[8,64,128]{2,1,0:T(8,128)(2,1)S(1)}, bf16[8,64,128]{2,1,0:T(8,128)(2,1)}, u32[]{:S(2)}) %copy-start.4) | copy-done | bytes 131096
  2.6 0.0 copy-start.1
  2.6 0.0 copy-start.2
  2.6 0.0 copy-start.3
  2.6 0.0 copy-start.5
  2.6 0.1 shard_map.76
  2.7 4.1 %collective-permute-start = (bf16[192,128]{1,0:T(8,128)(2,1)S(1)}, bf16[192,128]{1,0:T(8,128)(2,1)S(1)}, u32[]{:S(2)}, u32[]{:S(2)}) collective-permute-start(bf16[192,128]{1,0:T(8,128)(2,1)S(1)} %get-tuple-element.33), channel_id=1, source_target_pairs={{0,4},{1,5},{2,6},{3,7},{4,0},{5,1},{6,2},{7,3},{24,28},{25,29},{2... | collective-permute-start | bytes 147464 | tf_op jit(solution)/shard_map/ppermute | solution.py:340
  6.8 0.4 collective-permute-start.1
  7.2 0.1 pad.9.clone
  7.2 0.9 %shard_map.77 = (f32[16,64,256]{2,1,0:T(8,128)S(1)}, bf16[2,256,512]{2,1,0:T(8,128)(2,1)S(1)}) custom-call(bf16[16,128,128]{2,1,0:T(8,128)(2,1)S(1)} %get-tuple-element.35.pre), custom_call_target="tpu_custom_call" | custom-call | flops 15728640 | bytes 2097152 | tf_op jit(solution)/shard_map/pallas_call | solution.py:343
  8.2 1.2 %collective-permute-done.row_b = bf16[192,128]{1,0:T(8,128)(2,1)S(1)} collective-permute-done((bf16[192,128]{1,0:T(8,128)(2,1)S(1)}, bf16[192,128]{1,0:T(8,128)(2,1)S(1)}, u32[]{:S(2)}, u32[]{:S(2)}) %collective-permute-start) | collective-permute-done | bytes 49184 | tf_op jit(solution)/shard_map/ppermute | solution.py:340
  9.4 1.5 %collective-permute-done.1.row_a = bf16[192,128]{1,0:T(8,128)(2,1)S(1)} collective-permute-done((bf16[192,128]{1,0:T(8,128)(2,1)S(1)}, bf16[192,128]{1,0:T(8,128)(2,1)S(1)}, u32[]{:S(2)}, u32[]{:S(2)}) %collective-permute-start.1) | collective-permute-done | bytes 49184 | tf_op jit(solution)/shard_map/ppermute | solution.py:341
  10.9 0.1 maximum_maximum_fusion.1
  11.0 0.8 %collective-permute-start.3 = (bf16[32,128]{1,0:T(8,128)(2,1)S(1)}, bf16[32,128]{1,0:T(8,128)(2,1)S(1)}, u32[]{:S(2)}, u32[]{:S(2)}) collective-permute-start(bf16[32,128]{1,0:T(8,128)(2,1)S(1)} %get-tuple-element.80), channel_id=1, source_target_pairs={{0,7},{1,2},{2,1},{3,4},{4,3},{5,6},{6,5},{7,0},{8,15},{9,10},{10,... | collective-permute-start | bytes 24584 | tf_op jit(solution)/shard_map/ppermute | solution.py:372
  11.8 0.9 %collective-permute-start.2 = (bf16[32,128]{1,0:T(8,128)(2,1)S(1)}, bf16[32,128]{1,0:T(8,128)(2,1)S(1)}, u32[]{:S(2)}, u32[]{:S(2)}) collective-permute-start(bf16[32,128]{1,0:T(8,128)(2,1)S(1)} %get-tuple-element.81), channel_id=1, source_target_pairs={{0,1},{1,0},{2,3},{3,2},{4,5},{5,4},{6,7},{7,6},{8,9},{9,8},{10,11... | collective-permute-start | bytes 24584 | tf_op jit(solution)/shard_map/ppermute | solution.py:373
  12.7 0.0 copy-done.1
  12.7 0.0 copy-done.2
  12.7 0.0 copy-done.3
  12.7 0.5 %shard_map.78 = (bf16[128,1024]{1,0:T(8,128)(2,1)S(1)}, bf16[384,512]{1,0:T(8,128)(2,1)S(1)}, bf16[3,256,512]{2,1,0:T(8,128)(2,1)S(1)}) custom-call(bf16[16,64,128]{2,1,0:T(8,128)(2,1)S(1)} %bitcast.8, bf16[3,3,64,128]{3,2,1,0:T(8,128)(2,1)S(1)} %copy-done.3, bf16[3,3,128,128]{3,2,1,0:T(8,128)(2,1)S(1)} %copy-done.1), custom_call_target="tpu_custom_call" | custom-call | flops 67108864 | bytes 3145728 | tf_op jit(solution)/shard_map/pallas_call | solution.py:375
  13.2 2.7 %collective-permute-done.3.col_b = bf16[32,128]{1,0:T(8,128)(2,1)S(1)} collective-permute-done((bf16[32,128]{1,0:T(8,128)(2,1)S(1)}, bf16[32,128]{1,0:T(8,128)(2,1)S(1)}, u32[]{:S(2)}, u32[]{:S(2)}) %collective-permute-start.3) | collective-permute-done | bytes 8224 | tf_op jit(solution)/shard_map/ppermute | solution.py:372
  15.9 0.0 collective-permute-done.2.col_a
  15.9 0.0 copy-done.5
  15.9 2.7 %shard_map.79 = (bf16[19,64,512]{2,1,0:T(8,128)(2,1)S(1)}, f32[896,128]{1,0:T(8,128)S(1)}, f32[896,128]{1,0:T(8,128)S(1)}) custom-call(bf16[8,64,128]{2,1,0:T(8,128)(2,1)S(1)} %copy-done.5, bf16[192,128]{1,0:T(8,128)(2,1)S(1)} %collective-permute-done.1.row_a, bf16[192,128]{1,0:T(8,128)(2,1)S(1)} %collective-permute-done.row_b, ...), custom_call_target="tpu_custom_call" | custom-call | flops 1509949440 | bytes 8388608 | tf_op jit(solution)/shard_map/pallas_call | solution.py:393
  18.5 0.1 collective-permute-start.4
  18.6 1.8 %collective-permute-done.4 = f32[896,128]{1,0:T(8,128)S(1)} collective-permute-done((f32[896,128]{1,0:T(8,128)S(1)}, f32[896,128]{1,0:T(8,128)S(1)}, u32[]{:S(2)}, u32[]{:S(2)}) %collective-permute-start.4) | collective-permute-done | bytes 458784 | tf_op jit(solution)/shard_map/ppermute | solution.py:426
  20.4 0.1 fusion.3
  20.5 2.5 %collective-permute-start.5 = (bf16[224,128]{1,0:T(8,128)(2,1)S(1)}, bf16[224,128]{1,0:T(8,128)(2,1)S(1)}, u32[]{:S(2)}, u32[]{:S(2)}) collective-permute-start(bf16[224,128]{1,0:T(8,128)(2,1)S(1)} %get-tuple-element.52), channel_id=1, source_target_pairs={{0,24},{1,25},{2,26},{3,27},{4,28},{5,29},{6,30},{7,31},{8,16},{9,... | collective-permute-start | bytes 172040 | tf_op jit(solution)/shard_map/ppermute | solution.py:423
  23.0 0.0 collective-permute-start.6
  23.0 0.8 %collective-permute-start.7 = (bf16[224,128]{1,0:T(8,128)(2,1)S(1)}, bf16[224,128]{1,0:T(8,128)(2,1)S(1)}, u32[]{:S(2)}, u32[]{:S(2)}) collective-permute-start(bf16[224,128]{1,0:T(8,128)(2,1)S(1)} %get-tuple-element.54), channel_id=1, source_target_pairs={{0,9},{1,8},{2,11},{3,10},{4,13},{5,12},{6,15},{7,14},{8,1},{9,0},... | collective-permute-start | bytes 172040 | tf_op jit(solution)/shard_map/ppermute | solution.py:423
  23.8 2.2 %shard_map.80 = bf16[16,64,128]{2,1,0:T(8,128)(2,1)} custom-call(bf16[19,64,512]{2,1,0:T(8,128)(2,1)S(1)} %get-tuple-element.55.spread, bf16[384,512]{1,0:T(8,128)(2,1)S(1)} %get-tuple-element.56.taps), custom_call_target="tpu_custom_call" | custom-call | flops 301989888 | bytes 3145728 | tf_op jit(solution)/shard_map/pallas_call | solution.py:430
  26.0 0.0 collective-permute-done.5
  26.0 1.2 %collective-permute-done.6 = bf16[224,128]{1,0:T(8,128)(2,1)S(1)} collective-permute-done((bf16[224,128]{1,0:T(8,128)(2,1)S(1)}, bf16[224,128]{1,0:T(8,128)(2,1)S(1)}, u32[]{:S(2)}, u32[]{:S(2)}) %collective-permute-start.6) | collective-permute-done | bytes 57376 | tf_op jit(solution)/shard_map/ppermute | solution.py:423
  27.2 0.0 collective-permute-done.7
  27.3 0.5 %collective-permute-start.10 = (bf16[224,128]{1,0:T(8,128)(2,1)S(1)}, bf16[224,128]{1,0:T(8,128)(2,1)S(1)}, u32[]{:S(2)}, u32[]{:S(2)}) collective-permute-start(bf16[224,128]{1,0:T(8,128)(2,1)S(1)} %fusion.2), channel_id=1, source_target_pairs={{0,6},{1,7},{2,4},{3,5},{4,2},{5,3},{6,0},{7,1},{8,14},{9,15},{10,... | collective-permute-start | bytes 172040 | tf_op jit(solution)/shard_map/ppermute | solution.py:423
  27.7 0.3 collective-permute-start.9
  28.0 3.4 %collective-permute-start.8 = (bf16[224,128]{1,0:T(8,128)(2,1)S(1)}, bf16[224,128]{1,0:T(8,128)(2,1)S(1)}, u32[]{:S(2)}, u32[]{:S(2)}) collective-permute-start(bf16[224,128]{1,0:T(8,128)(2,1)S(1)} %fusion.2), channel_id=1, source_target_pairs={{0,3},{1,2},{2,1},{3,0},{4,7},{5,6},{6,5},{7,4},{8,11},{9,10},{10,... | collective-permute-start | bytes 172040 | tf_op jit(solution)/shard_map/ppermute | solution.py:423
  31.4 2.6 %collective-permute-done.10 = bf16[224,128]{1,0:T(8,128)(2,1)S(1)} collective-permute-done((bf16[224,128]{1,0:T(8,128)(2,1)S(1)}, bf16[224,128]{1,0:T(8,128)(2,1)S(1)}, u32[]{:S(2)}, u32[]{:S(2)}) %collective-permute-start.10) | collective-permute-done | bytes 57376 | tf_op jit(solution)/shard_map/ppermute | solution.py:423
  34.0 1.2 %collective-permute-done.9 = bf16[224,128]{1,0:T(8,128)(2,1)S(1)} collective-permute-done((bf16[224,128]{1,0:T(8,128)(2,1)S(1)}, bf16[224,128]{1,0:T(8,128)(2,1)S(1)}, u32[]{:S(2)}, u32[]{:S(2)}) %collective-permute-start.9) | collective-permute-done | bytes 57376 | tf_op jit(solution)/shard_map/ppermute | solution.py:423
  35.1 0.3 collective-permute-done.8
  35.5 2.0 %collective-permute-start.13 = (bf16[224,128]{1,0:T(8,128)(2,1)S(1)}, bf16[224,128]{1,0:T(8,128)(2,1)S(1)}, u32[]{:S(2)}, u32[]{:S(2)}) collective-permute-start(bf16[224,128]{1,0:T(8,128)(2,1)S(1)} %add_convert_fusion), channel_id=1, source_target_pairs={{0,24},{1,25},{2,26},{3,27},{4,28},{5,29},{6,30},{7,31},{8,16},{9,... | collective-permute-start | bytes 172040 | tf_op jit(solution)/shard_map/ppermute | solution.py:423
  37.4 0.0 collective-permute-start.12
  37.4 1.3 %collective-permute-start.11 = (bf16[224,128]{1,0:T(8,128)(2,1)S(1)}, bf16[224,128]{1,0:T(8,128)(2,1)S(1)}, u32[]{:S(2)}, u32[]{:S(2)}) collective-permute-start(bf16[224,128]{1,0:T(8,128)(2,1)S(1)} %add_convert_fusion), channel_id=1, source_target_pairs={{0,9},{1,8},{2,11},{3,10},{4,13},{5,12},{6,15},{7,14},{8,1},{9,0},... | collective-permute-start | bytes 172040 | tf_op jit(solution)/shard_map/ppermute | solution.py:423
  38.7 1.9 %collective-permute-done.13 = bf16[224,128]{1,0:T(8,128)(2,1)S(1)} collective-permute-done((bf16[224,128]{1,0:T(8,128)(2,1)S(1)}, bf16[224,128]{1,0:T(8,128)(2,1)S(1)}, u32[]{:S(2)}, u32[]{:S(2)}) %collective-permute-start.13) | collective-permute-done | bytes 57376 | tf_op jit(solution)/shard_map/ppermute | solution.py:423
  40.6 1.2 %collective-permute-done.12 = bf16[224,128]{1,0:T(8,128)(2,1)S(1)} collective-permute-done((bf16[224,128]{1,0:T(8,128)(2,1)S(1)}, bf16[224,128]{1,0:T(8,128)(2,1)S(1)}, u32[]{:S(2)}, u32[]{:S(2)}) %collective-permute-start.12) | collective-permute-done | bytes 57376 | tf_op jit(solution)/shard_map/ppermute | solution.py:423
  41.8 0.0 collective-permute-done.11
  41.9 0.2 collective-permute-start.14
  42.0 1.4 %collective-permute-done.14.theirs = bf16[4,224,128]{2,1,0:T(8,128)(2,1)S(1)} collective-permute-done((bf16[4,224,128]{2,1,0:T(8,128)(2,1)S(1)}, bf16[4,224,128]{2,1,0:T(8,128)(2,1)S(1)}, u32[]{:S(2)}, u32[]{:S(2)}) %collective-permute-start.14) | collective-permute-done | bytes 229408 | tf_op jit(solution)/shard_map/ppermute | solution.py:453
  43.4 1.0 %shard_map.81 = (f32[576,128]{1,0:T(8,128)}, f32[1152,128]{1,0:T(8,128)}) custom-call(bf16[4,224,128]{2,1,0:T(8,128)(2,1)S(1)} %pad_maximum_fusion.mine, bf16[4,224,128]{2,1,0:T(8,128)(2,1)S(1)} %collective-permute-done.14.theirs), custom_call_target="tpu_custom_call" | custom-call | flops 1000 | bytes 1572864 | tf_op jit(solution)/shard_map/pallas_call | solution.py:455
  (10 shorter events, 0.2 us)
Async XLA Ops:
  0.6 1.0 %copy-start = (bf16[16,128,128]{2,1,0:T(8,128)(2,1)S(1)}, bf16[16,128,128]{2,1,0:T(8,128)(2,1)}, u32[]{:S(2)}) copy-start(bf16[16,128,128]{2,1,0:T(8,128)(2,1)} %pre.1) | copy-start | bytes 1572868
  1.7 0.9 %copy-start.4 = (bf16[8,64,128]{2,1,0:T(8,128)(2,1)S(1)}, bf16[8,64,128]{2,1,0:T(8,128)(2,1)}, u32[]{:S(2)}) copy-start(bf16[8,64,128]{2,1,0:T(8,128)(2,1)} %grad_out.3) | copy-start | bytes 393220
  2.6 10.1 %copy-start.1 = (bf16[3,3,128,128]{3,2,1,0:T(8,128)(2,1)S(1)}, bf16[3,3,128,128]{3,2,1,0:T(8,128)(2,1)}, u32[]{:S(2)}) copy-start(bf16[3,3,128,128]{3,2,1,0:T(8,128)(2,1)} %w_second.1) | copy-start | bytes 884740
  2.6 10.1 %copy-start.2 = (bf16[16,128,64]{1,2,0:T(8,128)(2,1)S(1)}, bf16[16,128,64]{1,2,0:T(8,128)(2,1)}, u32[]{:S(2)}) copy-start(bf16[16,128,64]{1,2,0:T(8,128)(2,1)} %param.5) | copy-start | bytes 786436
  2.6 10.1 %copy-start.3 = (bf16[3,3,64,128]{3,2,1,0:T(8,128)(2,1)S(1)}, bf16[3,3,64,128]{3,2,1,0:T(8,128)(2,1)}, u32[]{:S(2)}) copy-start(bf16[3,3,64,128]{3,2,1,0:T(8,128)(2,1)} %w_first.1) | copy-start | bytes 442372
  2.6 13.3 %copy-start.5 = (bf16[8,64,128]{2,1,0:T(8,128)(2,1)S(1)}, bf16[8,64,128]{2,1,0:T(8,128)(2,1)}, u32[]{:S(2)}) copy-start(bf16[8,64,128]{2,1,0:T(8,128)(2,1)} %grad_out.3) | copy-start | bytes 393220
  2.7 6.7 %collective-permute-start = (bf16[192,128]{1,0:T(8,128)(2,1)S(1)}, bf16[192,128]{1,0:T(8,128)(2,1)S(1)}, u32[]{:S(2)}, u32[]{:S(2)}) collective-permute-start(bf16[192,128]{1,0:T(8,128)(2,1)S(1)} %get-tuple-element.33), channel_id=1, source_target_pairs={{0,4},{1,5},{2,6},{3,7},{4,0},{5,1},{6,2},{7,3},{24,28},{25,29},{2... | collective-permute-start | bytes 147464 | tf_op jit(solution)/shard_map/ppermute | solution.py:340
  6.8 4.1 %collective-permute-start.1 = (bf16[192,128]{1,0:T(8,128)(2,1)S(1)}, bf16[192,128]{1,0:T(8,128)(2,1)S(1)}, u32[]{:S(2)}, u32[]{:S(2)}) collective-permute-start(bf16[192,128]{1,0:T(8,128)(2,1)S(1)} %get-tuple-element.34), channel_id=1, source_target_pairs={{0,8},{1,9},{2,10},{3,11},{4,12},{5,13},{6,14},{7,15},{8,0},{9,1},... | collective-permute-start | bytes 147464 | tf_op jit(solution)/shard_map/ppermute | solution.py:341
  11.0 4.9 %collective-permute-start.3 = (bf16[32,128]{1,0:T(8,128)(2,1)S(1)}, bf16[32,128]{1,0:T(8,128)(2,1)S(1)}, u32[]{:S(2)}, u32[]{:S(2)}) collective-permute-start(bf16[32,128]{1,0:T(8,128)(2,1)S(1)} %get-tuple-element.80), channel_id=1, source_target_pairs={{0,7},{1,2},{2,1},{3,4},{4,3},{5,6},{6,5},{7,0},{8,15},{9,10},{10,... | collective-permute-start | bytes 24584 | tf_op jit(solution)/shard_map/ppermute | solution.py:372
  11.8 4.1 %collective-permute-start.2 = (bf16[32,128]{1,0:T(8,128)(2,1)S(1)}, bf16[32,128]{1,0:T(8,128)(2,1)S(1)}, u32[]{:S(2)}, u32[]{:S(2)}) collective-permute-start(bf16[32,128]{1,0:T(8,128)(2,1)S(1)} %get-tuple-element.81), channel_id=1, source_target_pairs={{0,1},{1,0},{2,3},{3,2},{4,5},{5,4},{6,7},{7,6},{8,9},{9,8},{10,11... | collective-permute-start | bytes 24584 | tf_op jit(solution)/shard_map/ppermute | solution.py:373
  18.5 1.9 %collective-permute-start.4 = (f32[896,128]{1,0:T(8,128)S(1)}, f32[896,128]{1,0:T(8,128)S(1)}, u32[]{:S(2)}, u32[]{:S(2)}) collective-permute-start(f32[896,128]{1,0:T(8,128)S(1)} %get-tuple-element.50), channel_id=1, source_target_pairs={{0,1},{1,0},{2,3},{3,2},{4,5},{5,4},{6,7},{7,6},{8,9},{9,8},{10,11... | collective-permute-start | bytes 1376264 | tf_op jit(solution)/shard_map/ppermute | solution.py:426
  20.5 5.5 %collective-permute-start.5 = (bf16[224,128]{1,0:T(8,128)(2,1)S(1)}, bf16[224,128]{1,0:T(8,128)(2,1)S(1)}, u32[]{:S(2)}, u32[]{:S(2)}) collective-permute-start(bf16[224,128]{1,0:T(8,128)(2,1)S(1)} %get-tuple-element.52), channel_id=1, source_target_pairs={{0,24},{1,25},{2,26},{3,27},{4,28},{5,29},{6,30},{7,31},{8,16},{9,... | collective-permute-start | bytes 172040 | tf_op jit(solution)/shard_map/ppermute | solution.py:423
  23.0 4.2 %collective-permute-start.6 = (bf16[224,128]{1,0:T(8,128)(2,1)S(1)}, bf16[224,128]{1,0:T(8,128)(2,1)S(1)}, u32[]{:S(2)}, u32[]{:S(2)}) collective-permute-start(bf16[224,128]{1,0:T(8,128)(2,1)S(1)} %get-tuple-element.53), channel_id=1, source_target_pairs={{0,17},{1,16},{2,19},{3,18},{4,21},{5,20},{6,23},{7,22},{8,25},{9,... | collective-permute-start | bytes 172040 | tf_op jit(solution)/shard_map/ppermute | solution.py:423
  23.0 4.2 %collective-permute-start.7 = (bf16[224,128]{1,0:T(8,128)(2,1)S(1)}, bf16[224,128]{1,0:T(8,128)(2,1)S(1)}, u32[]{:S(2)}, u32[]{:S(2)}) collective-permute-start(bf16[224,128]{1,0:T(8,128)(2,1)S(1)} %get-tuple-element.54), channel_id=1, source_target_pairs={{0,9},{1,8},{2,11},{3,10},{4,13},{5,12},{6,15},{7,14},{8,1},{9,0},... | collective-permute-start | bytes 172040 | tf_op jit(solution)/shard_map/ppermute | solution.py:423
  27.3 6.7 %collective-permute-start.10 = (bf16[224,128]{1,0:T(8,128)(2,1)S(1)}, bf16[224,128]{1,0:T(8,128)(2,1)S(1)}, u32[]{:S(2)}, u32[]{:S(2)}) collective-permute-start(bf16[224,128]{1,0:T(8,128)(2,1)S(1)} %fusion.2), channel_id=1, source_target_pairs={{0,6},{1,7},{2,4},{3,5},{4,2},{5,3},{6,0},{7,1},{8,14},{9,15},{10,... | collective-permute-start | bytes 172040 | tf_op jit(solution)/shard_map/ppermute | solution.py:423
  27.7 7.4 %collective-permute-start.9 = (bf16[224,128]{1,0:T(8,128)(2,1)S(1)}, bf16[224,128]{1,0:T(8,128)(2,1)S(1)}, u32[]{:S(2)}, u32[]{:S(2)}) collective-permute-start(bf16[224,128]{1,0:T(8,128)(2,1)S(1)} %fusion.2), channel_id=1, source_target_pairs={{0,5},{1,4},{2,7},{3,6},{4,1},{5,0},{6,3},{7,2},{8,13},{9,12},{10,... | collective-permute-start | bytes 172040 | tf_op jit(solution)/shard_map/ppermute | solution.py:423
  28.0 7.4 %collective-permute-start.8 = (bf16[224,128]{1,0:T(8,128)(2,1)S(1)}, bf16[224,128]{1,0:T(8,128)(2,1)S(1)}, u32[]{:S(2)}, u32[]{:S(2)}) collective-permute-start(bf16[224,128]{1,0:T(8,128)(2,1)S(1)} %fusion.2), channel_id=1, source_target_pairs={{0,3},{1,2},{2,1},{3,0},{4,7},{5,6},{6,5},{7,4},{8,11},{9,10},{10,... | collective-permute-start | bytes 172040 | tf_op jit(solution)/shard_map/ppermute | solution.py:423
  35.5 5.2 %collective-permute-start.13 = (bf16[224,128]{1,0:T(8,128)(2,1)S(1)}, bf16[224,128]{1,0:T(8,128)(2,1)S(1)}, u32[]{:S(2)}, u32[]{:S(2)}) collective-permute-start(bf16[224,128]{1,0:T(8,128)(2,1)S(1)} %add_convert_fusion), channel_id=1, source_target_pairs={{0,24},{1,25},{2,26},{3,27},{4,28},{5,29},{6,30},{7,31},{8,16},{9,... | collective-permute-start | bytes 172040 | tf_op jit(solution)/shard_map/ppermute | solution.py:423
  37.4 4.4 %collective-permute-start.12 = (bf16[224,128]{1,0:T(8,128)(2,1)S(1)}, bf16[224,128]{1,0:T(8,128)(2,1)S(1)}, u32[]{:S(2)}, u32[]{:S(2)}) collective-permute-start(bf16[224,128]{1,0:T(8,128)(2,1)S(1)} %add_convert_fusion), channel_id=1, source_target_pairs={{0,17},{1,16},{2,19},{3,18},{4,21},{5,20},{6,23},{7,22},{8,25},{9,... | collective-permute-start | bytes 172040 | tf_op jit(solution)/shard_map/ppermute | solution.py:423
  37.4 4.4 %collective-permute-start.11 = (bf16[224,128]{1,0:T(8,128)(2,1)S(1)}, bf16[224,128]{1,0:T(8,128)(2,1)S(1)}, u32[]{:S(2)}, u32[]{:S(2)}) collective-permute-start(bf16[224,128]{1,0:T(8,128)(2,1)S(1)} %add_convert_fusion), channel_id=1, source_target_pairs={{0,9},{1,8},{2,11},{3,10},{4,13},{5,12},{6,15},{7,14},{8,1},{9,0},... | collective-permute-start | bytes 172040 | tf_op jit(solution)/shard_map/ppermute | solution.py:423
  41.9 1.6 %collective-permute-start.14 = (bf16[4,224,128]{2,1,0:T(8,128)(2,1)S(1)}, bf16[4,224,128]{2,1,0:T(8,128)(2,1)S(1)}, u32[]{:S(2)}, u32[]{:S(2)}) collective-permute-start(bf16[4,224,128]{2,1,0:T(8,128)(2,1)S(1)} %pad_maximum_fusion.mine), channel_id=1, source_target_pairs={{0,1},{1,0},{2,3},{3,2},{4,5},{5,4},{6,7},{7,6},{8,9},{9,8},{10,11... | collective-permute-start | bytes 688136 | tf_op jit(solution)/shard_map/ppermute | solution.py:453

commit v12 on v11

--- a/solution.py
+++ b/solution.py
@@ -48,7 +48,12 @@
     return odd(band) ^ odd(place // 2) ^ (place % 2)
 
 
-def pack_kernel(lats, pre, grad_out, row_a, row_b, col_a, col_b, held, hold):
+def pack_kernel(lats, pre_far, grad_far, row_a, row_b, col_a, col_b, pre, hold, grad_out, sems):
+    copies = [pltpu.make_async_copy(pre_far, pre, sems.at[0]), pltpu.make_async_copy(grad_far, grad_out, sems.at[1])]
+    for copy in copies:
+        copy.start()
+    for copy in copies:
+        copy.wait()
     rows, cols, c1 = pre.shape
     pooled, half = grad_out.shape[:2]
     _, _, _, even, core = position(lats)
@@ -64,7 +69,6 @@
             hold[side, rows + i:rows + i + 1] = grad_out[i, g:g + 16].astype(F32)[at:at + 1]
     col_a[...] = hold[1 - core].astype(BF16)
     col_b[...] = hold[core].astype(BF16)
-    held[...] = pre[...]
 
 
 def one_at(where):
@@ -296,6 +300,10 @@
     return [pl.BlockSpec(memory_space=pltpu.VMEM)] * count
 
 
+def far(count):
+    return [pl.BlockSpec(memory_space=pl.ANY)] * count
+
+
 def params(mib):
     return pltpu.CompilerParams(vmem_limit_bytes=mib * 1024 * 1024)
 
@@ -318,18 +326,20 @@
     row_a, row_b, col_a, col_b, held_pre = pl.pallas_call(
         functools.partial(pack_kernel, lats),
         out_shape=(
-            shape((cols + half, c1), BF16),
-            shape((cols + half, c1), BF16),
-            shape((edge, c1), BF16),
-            shape((edge, c1), BF16),
-            shape(pre_first.shape, BF16),
+            pltpu.VMEM((cols + half, c1), BF16),
+            pltpu.VMEM((cols + half, c1), BF16),
+            pltpu.VMEM((edge, c1), BF16),
+            pltpu.VMEM((edge, c1), BF16),
+            pltpu.VMEM(pre_first.shape, BF16),
         ),
-        in_specs=vmem(2),
+        in_specs=far(2),
         out_specs=tuple(vmem(5)),
         scratch_shapes=[
             pltpu.VMEM((2, edge, c1), F32),
+            pltpu.VMEM(grad_out.shape, BF16),
+            pltpu.SemaphoreType.DMA((2,)),
         ],
-        compiler_params=params(50),
+        compiler_params=params(58),
         cost_estimate=pl.CostEstimate(flops=1000, bytes_accessed=1 << 18, transcendentals=0),
     )(pre_first, grad_out)
     pairs = [(i * lons + j, i * lons + (j + lons // 2) % lons) for i in (0, lats - 1) for j in range(lons)]

time: 44.6 us -> 43.8 us (0.982)
  local copies, waits for them, and re-layouts: 2.06 us -> 0.12 us
  Pallas kernels: 7.33 us -> 8.44 us
    unnamed x12 -> x8, local copies, waits for them, and re-layouts: 1.95 us -> 0.02 us
    pallas_call x1, Pallas kernels: 0.06 us -> 1.18 us  [body(): pl.pallas_call(functools.partial(pack_kernel, lats), out_shape=(pltpu.VME...]
where the time goes in v12:
time: 43.8 us; the launch traced here: 43.6 us
  starting transfers between devices  17.2 us (39%)
  waiting for transfers between devices  16.9 us (39%)
  Pallas kernels  8.44 us (19%)
  between operations  0.76 us (2%)
    ppermute x9, starting transfers between devices, between_chips(): lax.ppermute(value, AREA, [(i * lons + j, (i ^ over_lat) * lons + (j ^ 2...  10.7 us
    ppermute x9, waiting for transfers between devices, between_chips(): lax.ppermute(value, AREA, [(i * lons + j, (i ^ over_lat) * lons + (j ^ 2...  8.33 us
    ppermute x1, starting transfers between devices, body(): row_b = lax.ppermute(row_b, AREA, pairs)  4.1 us
    ppermute x1, waiting for transfers between devices, body(): lax.ppermute(col_b, 'lon', [(i, (i + 2 * (i % 2) - 1) % lons) for i in ra...  2.7 us
    pallas_call x1, Pallas kernels, body(): pl.pallas_call(functools.partial(middle_kernel, lats), out_shape=(shape((...  2.66 us
    pallas_call x1, Pallas kernels, body(): pl.pallas_call(last_kernel, out_shape=shape((rows, c0, cols), BF16), in_s...  2.19 us
    ppermute x1, waiting for transfers between devices, body(): parts = (own + lax.ppermute(other, 'lon', swap)).reshape(lats, block, c1)  1.8 us
    ppermute x1, waiting for transfers between devices, body(): row_a = lax.ppermute(row_a, AREA, every)  1.49 us
  transfers between devices with their start and end apart: 15, of which 11 were waited for; matrix products, arithmetic and copies ran while one was open for 0% of the time, Pallas kernels for 8%

profile of v12, /device:TPU:0, one launch (start us, length us, event | category | flops | bytes accessed | tf_op | source)
XLA Modules:
  0.0 43.6 jit_solution(6415187061575121538)
XLA Ops:
  0.6 0.0 copy-start.3
  0.6 0.0 copy-start.1
  0.7 0.0 copy-start
  0.7 0.0 copy-start.2
  0.7 1.2 %shard_map.76 = (bf16[192,128]{1,0:T(8,128)(2,1)S(1)}, bf16[192,128]{1,0:T(8,128)(2,1)S(1)}, bf16[32,128]{1,0:T(8,128)(2,1)S(1)}, bf16[32,128]{1,0:T(8,128)(2,1)S(1)}, bf16[16,128,128]{2,1,0:T(8,128)(2,1)S(1)}) custom-call(bf16[16,128,128]{2,1,0:T(8,128)(2,1)} %pre_far.1, bf16[8,64,128]{2,1,0:T(8,128)(2,1)} %grad_out.1), custom_call_target="tpu_custom_call" | custom-call | flops 1000 | bytes 262144 | tf_op jit(solution)/shard_map/pallas_call | solution.py:326
  1.9 4.1 %collective-permute-start = (bf16[192,128]{1,0:T(8,128)(2,1)S(1)}, bf16[192,128]{1,0:T(8,128)(2,1)S(1)}, u32[]{:S(2)}, u32[]{:S(2)}) collective-permute-start(bf16[192,128]{1,0:T(8,128)(2,1)S(1)} %get-tuple-element.33), channel_id=1, source_target_pairs={{0,4},{1,5},{2,6},{3,7},{4,0},{5,1},{6,2},{7,3},{24,28},{25,29},{2... | collective-permute-start | bytes 147464 | tf_op jit(solution)/shard_map/ppermute | solution.py:350
  6.0 0.4 collective-permute-start.1
  6.4 0.1 pad.9.clone
  6.4 0.9 %shard_map.77 = (f32[16,64,256]{2,1,0:T(8,128)S(1)}, bf16[2,256,512]{2,1,0:T(8,128)(2,1)S(1)}) custom-call(bf16[16,128,128]{2,1,0:T(8,128)(2,1)S(1)} %get-tuple-element.35.pre), custom_call_target="tpu_custom_call" | custom-call | flops 15728640 | bytes 2097152 | tf_op jit(solution)/shard_map/pallas_call | solution.py:353
  7.4 1.2 %collective-permute-done.row_b = bf16[192,128]{1,0:T(8,128)(2,1)S(1)} collective-permute-done((bf16[192,128]{1,0:T(8,128)(2,1)S(1)}, bf16[192,128]{1,0:T(8,128)(2,1)S(1)}, u32[]{:S(2)}, u32[]{:S(2)}) %collective-permute-start) | collective-permute-done | bytes 49184 | tf_op jit(solution)/shard_map/ppermute | solution.py:350
  8.6 1.5 %collective-permute-done.1.row_a = bf16[192,128]{1,0:T(8,128)(2,1)S(1)} collective-permute-done((bf16[192,128]{1,0:T(8,128)(2,1)S(1)}, bf16[192,128]{1,0:T(8,128)(2,1)S(1)}, u32[]{:S(2)}, u32[]{:S(2)}) %collective-permute-start.1) | collective-permute-done | bytes 49184 | tf_op jit(solution)/shard_map/ppermute | solution.py:351
  10.1 0.1 maximum_maximum_fusion.1
  10.2 0.8 %collective-permute-start.3 = (bf16[32,128]{1,0:T(8,128)(2,1)S(1)}, bf16[32,128]{1,0:T(8,128)(2,1)S(1)}, u32[]{:S(2)}, u32[]{:S(2)}) collective-permute-start(bf16[32,128]{1,0:T(8,128)(2,1)S(1)} %get-tuple-element.80), channel_id=1, source_target_pairs={{0,7},{1,2},{2,1},{3,4},{4,3},{5,6},{6,5},{7,0},{8,15},{9,10},{10,... | collective-permute-start | bytes 24584 | tf_op jit(solution)/shard_map/ppermute | solution.py:382
  11.0 0.9 %collective-permute-start.2 = (bf16[32,128]{1,0:T(8,128)(2,1)S(1)}, bf16[32,128]{1,0:T(8,128)(2,1)S(1)}, u32[]{:S(2)}, u32[]{:S(2)}) collective-permute-start(bf16[32,128]{1,0:T(8,128)(2,1)S(1)} %get-tuple-element.81), channel_id=1, source_target_pairs={{0,1},{1,0},{2,3},{3,2},{4,5},{5,4},{6,7},{7,6},{8,9},{9,8},{10,11... | collective-permute-start | bytes 24584 | tf_op jit(solution)/shard_map/ppermute | solution.py:383
  11.9 0.0 copy-done.1
  11.9 0.0 copy-done
  11.9 0.0 copy-done.2
  11.9 0.5 %shard_map.78 = (bf16[128,1024]{1,0:T(8,128)(2,1)S(1)}, bf16[384,512]{1,0:T(8,128)(2,1)S(1)}, bf16[3,256,512]{2,1,0:T(8,128)(2,1)S(1)}) custom-call(bf16[16,64,128]{2,1,0:T(8,128)(2,1)S(1)} %bitcast.8, bf16[3,3,64,128]{3,2,1,0:T(8,128)(2,1)S(1)} %copy-done.2, bf16[3,3,128,128]{3,2,1,0:T(8,128)(2,1)S(1)} %copy-done), custom_call_target="tpu_custom_call" | custom-call | flops 67108864 | bytes 3145728 | tf_op jit(solution)/shard_map/pallas_call | solution.py:385
  12.4 2.7 %collective-permute-done.3.col_b = bf16[32,128]{1,0:T(8,128)(2,1)S(1)} collective-permute-done((bf16[32,128]{1,0:T(8,128)(2,1)S(1)}, bf16[32,128]{1,0:T(8,128)(2,1)S(1)}, u32[]{:S(2)}, u32[]{:S(2)}) %collective-permute-start.3) | collective-permute-done | bytes 8224 | tf_op jit(solution)/shard_map/ppermute | solution.py:382
  15.1 0.0 collective-permute-done.2.col_a
  15.1 0.0 copy-done.3
  15.1 2.7 %shard_map.79 = (bf16[19,64,512]{2,1,0:T(8,128)(2,1)S(1)}, f32[896,128]{1,0:T(8,128)S(1)}, f32[896,128]{1,0:T(8,128)S(1)}) custom-call(bf16[8,64,128]{2,1,0:T(8,128)(2,1)S(1)} %copy-done.3, bf16[192,128]{1,0:T(8,128)(2,1)S(1)} %collective-permute-done.1.row_a, bf16[192,128]{1,0:T(8,128)(2,1)S(1)} %collective-permute-done.row_b, ...), custom_call_target="tpu_custom_call" | custom-call | flops 1509949440 | bytes 8388608 | tf_op jit(solution)/shard_map/pallas_call | solution.py:403
  17.7 0.1 collective-permute-start.4
  17.8 1.8 %collective-permute-done.4 = f32[896,128]{1,0:T(8,128)S(1)} collective-permute-done((f32[896,128]{1,0:T(8,128)S(1)}, f32[896,128]{1,0:T(8,128)S(1)}, u32[]{:S(2)}, u32[]{:S(2)}) %collective-permute-start.4) | collective-permute-done | bytes 458784 | tf_op jit(solution)/shard_map/ppermute | solution.py:436
  19.6 0.1 fusion.3
  19.7 2.5 %collective-permute-start.5 = (bf16[224,128]{1,0:T(8,128)(2,1)S(1)}, bf16[224,128]{1,0:T(8,128)(2,1)S(1)}, u32[]{:S(2)}, u32[]{:S(2)}) collective-permute-start(bf16[224,128]{1,0:T(8,128)(2,1)S(1)} %get-tuple-element.52), channel_id=1, source_target_pairs={{0,24},{1,25},{2,26},{3,27},{4,28},{5,29},{6,30},{7,31},{8,16},{9,... | collective-permute-start | bytes 172040 | tf_op jit(solution)/shard_map/ppermute | solution.py:433
  22.2 0.0 collective-permute-start.6
  22.2 0.8 %collective-permute-start.7 = (bf16[224,128]{1,0:T(8,128)(2,1)S(1)}, bf16[224,128]{1,0:T(8,128)(2,1)S(1)}, u32[]{:S(2)}, u32[]{:S(2)}) collective-permute-start(bf16[224,128]{1,0:T(8,128)(2,1)S(1)} %get-tuple-element.54), channel_id=1, source_target_pairs={{0,9},{1,8},{2,11},{3,10},{4,13},{5,12},{6,15},{7,14},{8,1},{9,0},... | collective-permute-start | bytes 172040 | tf_op jit(solution)/shard_map/ppermute | solution.py:433
  23.0 2.2 %shard_map.80 = bf16[16,64,128]{2,1,0:T(8,128)(2,1)} custom-call(bf16[19,64,512]{2,1,0:T(8,128)(2,1)S(1)} %get-tuple-element.55.spread, bf16[384,512]{1,0:T(8,128)(2,1)S(1)} %get-tuple-element.56.taps), custom_call_target="tpu_custom_call" | custom-call | flops 301989888 | bytes 3145728 | tf_op jit(solution)/shard_map/pallas_call | solution.py:440
  25.2 0.0 collective-permute-done.5
  25.2 1.2 %collective-permute-done.6 = bf16[224,128]{1,0:T(8,128)(2,1)S(1)} collective-permute-done((bf16[224,128]{1,0:T(8,128)(2,1)S(1)}, bf16[224,128]{1,0:T(8,128)(2,1)S(1)}, u32[]{:S(2)}, u32[]{:S(2)}) %collective-permute-start.6) | collective-permute-done | bytes 57376 | tf_op jit(solution)/shard_map/ppermute | solution.py:433
  26.4 0.0 collective-permute-done.7
  26.4 0.5 %collective-permute-start.10 = (bf16[224,128]{1,0:T(8,128)(2,1)S(1)}, bf16[224,128]{1,0:T(8,128)(2,1)S(1)}, u32[]{:S(2)}, u32[]{:S(2)}) collective-permute-start(bf16[224,128]{1,0:T(8,128)(2,1)S(1)} %fusion.2), channel_id=1, source_target_pairs={{0,6},{1,7},{2,4},{3,5},{4,2},{5,3},{6,0},{7,1},{8,14},{9,15},{10,... | collective-permute-start | bytes 172040 | tf_op jit(solution)/shard_map/ppermute | solution.py:433
  26.9 0.3 collective-permute-start.9
  27.2 3.4 %collective-permute-start.8 = (bf16[224,128]{1,0:T(8,128)(2,1)S(1)}, bf16[224,128]{1,0:T(8,128)(2,1)S(1)}, u32[]{:S(2)}, u32[]{:S(2)}) collective-permute-start(bf16[224,128]{1,0:T(8,128)(2,1)S(1)} %fusion.2), channel_id=1, source_target_pairs={{0,3},{1,2},{2,1},{3,0},{4,7},{5,6},{6,5},{7,4},{8,11},{9,10},{10,... | collective-permute-start | bytes 172040 | tf_op jit(solution)/shard_map/ppermute | solution.py:433
  30.6 2.5 %collective-permute-done.10 = bf16[224,128]{1,0:T(8,128)(2,1)S(1)} collective-permute-done((bf16[224,128]{1,0:T(8,128)(2,1)S(1)}, bf16[224,128]{1,0:T(8,128)(2,1)S(1)}, u32[]{:S(2)}, u32[]{:S(2)}) %collective-permute-start.10) | collective-permute-done | bytes 57376 | tf_op jit(solution)/shard_map/ppermute | solution.py:433
  33.2 1.2 %collective-permute-done.9 = bf16[224,128]{1,0:T(8,128)(2,1)S(1)} collective-permute-done((bf16[224,128]{1,0:T(8,128)(2,1)S(1)}, bf16[224,128]{1,0:T(8,128)(2,1)S(1)}, u32[]{:S(2)}, u32[]{:S(2)}) %collective-permute-start.9) | collective-permute-done | bytes 57376 | tf_op jit(solution)/shard_map/ppermute | solution.py:433
  34.3 0.3 collective-permute-done.8
  34.7 2.0 %collective-permute-start.13 = (bf16[224,128]{1,0:T(8,128)(2,1)S(1)}, bf16[224,128]{1,0:T(8,128)(2,1)S(1)}, u32[]{:S(2)}, u32[]{:S(2)}) collective-permute-start(bf16[224,128]{1,0:T(8,128)(2,1)S(1)} %add_convert_fusion), channel_id=1, source_target_pairs={{0,24},{1,25},{2,26},{3,27},{4,28},{5,29},{6,30},{7,31},{8,16},{9,... | collective-permute-start | bytes 172040 | tf_op jit(solution)/shard_map/ppermute | solution.py:433
  36.6 0.0 collective-permute-start.12
  36.6 1.3 %collective-permute-start.11 = (bf16[224,128]{1,0:T(8,128)(2,1)S(1)}, bf16[224,128]{1,0:T(8,128)(2,1)S(1)}, u32[]{:S(2)}, u32[]{:S(2)}) collective-permute-start(bf16[224,128]{1,0:T(8,128)(2,1)S(1)} %add_convert_fusion), channel_id=1, source_target_pairs={{0,9},{1,8},{2,11},{3,10},{4,13},{5,12},{6,15},{7,14},{8,1},{9,0},... | collective-permute-start | bytes 172040 | tf_op jit(solution)/shard_map/ppermute | solution.py:433
  37.9 1.9 %collective-permute-done.13 = bf16[224,128]{1,0:T(8,128)(2,1)S(1)} collective-permute-done((bf16[224,128]{1,0:T(8,128)(2,1)S(1)}, bf16[224,128]{1,0:T(8,128)(2,1)S(1)}, u32[]{:S(2)}, u32[]{:S(2)}) %collective-permute-start.13) | collective-permute-done | bytes 57376 | tf_op jit(solution)/shard_map/ppermute | solution.py:433
  39.8 1.2 %collective-permute-done.12 = bf16[224,128]{1,0:T(8,128)(2,1)S(1)} collective-permute-done((bf16[224,128]{1,0:T(8,128)(2,1)S(1)}, bf16[224,128]{1,0:T(8,128)(2,1)S(1)}, u32[]{:S(2)}, u32[]{:S(2)}) %collective-permute-start.12) | collective-permute-done | bytes 57376 | tf_op jit(solution)/shard_map/ppermute | solution.py:433
  41.0 0.0 collective-permute-done.11
  41.1 0.2 collective-permute-start.14
  41.2 1.4 %collective-permute-done.14.theirs = bf16[4,224,128]{2,1,0:T(8,128)(2,1)S(1)} collective-permute-done((bf16[4,224,128]{2,1,0:T(8,128)(2,1)S(1)}, bf16[4,224,128]{2,1,0:T(8,128)(2,1)S(1)}, u32[]{:S(2)}, u32[]{:S(2)}) %collective-permute-start.14) | collective-permute-done | bytes 229408 | tf_op jit(solution)/shard_map/ppermute | solution.py:463
  42.6 1.0 %shard_map.81 = (f32[576,128]{1,0:T(8,128)}, f32[1152,128]{1,0:T(8,128)}) custom-call(bf16[4,224,128]{2,1,0:T(8,128)(2,1)S(1)} %pad_maximum_fusion.mine, bf16[4,224,128]{2,1,0:T(8,128)(2,1)S(1)} %collective-permute-done.14.theirs), custom_call_target="tpu_custom_call" | custom-call | flops 1000 | bytes 1572864 | tf_op jit(solution)/shard_map/pallas_call | solution.py:465
  (10 shorter events, 0.2 us)
Async XLA Ops:
  0.6 14.4 %copy-start.3 = (bf16[8,64,128]{2,1,0:T(8,128)(2,1)S(1)}, bf16[8,64,128]{2,1,0:T(8,128)(2,1)}, u32[]{:S(2)}) copy-start(bf16[8,64,128]{2,1,0:T(8,128)(2,1)} %grad_out.1) | copy-start | bytes 393220
  0.6 11.2 %copy-start.1 = (bf16[16,128,64]{1,2,0:T(8,128)(2,1)S(1)}, bf16[16,128,64]{1,2,0:T(8,128)(2,1)}, u32[]{:S(2)}) copy-start(bf16[16,128,64]{1,2,0:T(8,128)(2,1)} %param.5) | copy-start | bytes 786436
  0.7 11.2 %copy-start = (bf16[3,3,128,128]{3,2,1,0:T(8,128)(2,1)S(1)}, bf16[3,3,128,128]{3,2,1,0:T(8,128)(2,1)}, u32[]{:S(2)}) copy-start(bf16[3,3,128,128]{3,2,1,0:T(8,128)(2,1)} %w_second.1) | copy-start | bytes 884740
  0.7 11.2 %copy-start.2 = (bf16[3,3,64,128]{3,2,1,0:T(8,128)(2,1)S(1)}, bf16[3,3,64,128]{3,2,1,0:T(8,128)(2,1)}, u32[]{:S(2)}) copy-start(bf16[3,3,64,128]{3,2,1,0:T(8,128)(2,1)} %w_first.1) | copy-start | bytes 442372
  1.9 6.7 %collective-permute-start = (bf16[192,128]{1,0:T(8,128)(2,1)S(1)}, bf16[192,128]{1,0:T(8,128)(2,1)S(1)}, u32[]{:S(2)}, u32[]{:S(2)}) collective-permute-start(bf16[192,128]{1,0:T(8,128)(2,1)S(1)} %get-tuple-element.33), channel_id=1, source_target_pairs={{0,4},{1,5},{2,6},{3,7},{4,0},{5,1},{6,2},{7,3},{24,28},{25,29},{2... | collective-permute-start | bytes 147464 | tf_op jit(solution)/shard_map/ppermute | solution.py:350
  6.0 4.1 %collective-permute-start.1 = (bf16[192,128]{1,0:T(8,128)(2,1)S(1)}, bf16[192,128]{1,0:T(8,128)(2,1)S(1)}, u32[]{:S(2)}, u32[]{:S(2)}) collective-permute-start(bf16[192,128]{1,0:T(8,128)(2,1)S(1)} %get-tuple-element.34), channel_id=1, source_target_pairs={{0,8},{1,9},{2,10},{3,11},{4,12},{5,13},{6,14},{7,15},{8,0},{9,1},... | collective-permute-start | bytes 147464 | tf_op jit(solution)/shard_map/ppermute | solution.py:351
  10.2 4.9 %collective-permute-start.3 = (bf16[32,128]{1,0:T(8,128)(2,1)S(1)}, bf16[32,128]{1,0:T(8,128)(2,1)S(1)}, u32[]{:S(2)}, u32[]{:S(2)}) collective-permute-start(bf16[32,128]{1,0:T(8,128)(2,1)S(1)} %get-tuple-element.80), channel_id=1, source_target_pairs={{0,7},{1,2},{2,1},{3,4},{4,3},{5,6},{6,5},{7,0},{8,15},{9,10},{10,... | collective-permute-start | bytes 24584 | tf_op jit(solution)/shard_map/ppermute | solution.py:382
  11.0 4.1 %collective-permute-start.2 = (bf16[32,128]{1,0:T(8,128)(2,1)S(1)}, bf16[32,128]{1,0:T(8,128)(2,1)S(1)}, u32[]{:S(2)}, u32[]{:S(2)}) collective-permute-start(bf16[32,128]{1,0:T(8,128)(2,1)S(1)} %get-tuple-element.81), channel_id=1, source_target_pairs={{0,1},{1,0},{2,3},{3,2},{4,5},{5,4},{6,7},{7,6},{8,9},{9,8},{10,11... | collective-permute-start | bytes 24584 | tf_op jit(solution)/shard_map/ppermute | solution.py:383
  17.7 1.9 %collective-permute-start.4 = (f32[896,128]{1,0:T(8,128)S(1)}, f32[896,128]{1,0:T(8,128)S(1)}, u32[]{:S(2)}, u32[]{:S(2)}) collective-permute-start(f32[896,128]{1,0:T(8,128)S(1)} %get-tuple-element.50), channel_id=1, source_target_pairs={{0,1},{1,0},{2,3},{3,2},{4,5},{5,4},{6,7},{7,6},{8,9},{9,8},{10,11... | collective-permute-start | bytes 1376264 | tf_op jit(solution)/shard_map/ppermute | solution.py:436
  19.7 5.5 %collective-permute-start.5 = (bf16[224,128]{1,0:T(8,128)(2,1)S(1)}, bf16[224,128]{1,0:T(8,128)(2,1)S(1)}, u32[]{:S(2)}, u32[]{:S(2)}) collective-permute-start(bf16[224,128]{1,0:T(8,128)(2,1)S(1)} %get-tuple-element.52), channel_id=1, source_target_pairs={{0,24},{1,25},{2,26},{3,27},{4,28},{5,29},{6,30},{7,31},{8,16},{9,... | collective-permute-start | bytes 172040 | tf_op jit(solution)/shard_map/ppermute | solution.py:433
  22.2 4.2 %collective-permute-start.6 = (bf16[224,128]{1,0:T(8,128)(2,1)S(1)}, bf16[224,128]{1,0:T(8,128)(2,1)S(1)}, u32[]{:S(2)}, u32[]{:S(2)}) collective-permute-start(bf16[224,128]{1,0:T(8,128)(2,1)S(1)} %get-tuple-element.53), channel_id=1, source_target_pairs={{0,17},{1,16},{2,19},{3,18},{4,21},{5,20},{6,23},{7,22},{8,25},{9,... | collective-permute-start | bytes 172040 | tf_op jit(solution)/shard_map/ppermute | solution.py:433
  22.2 4.2 %collective-permute-start.7 = (bf16[224,128]{1,0:T(8,128)(2,1)S(1)}, bf16[224,128]{1,0:T(8,128)(2,1)S(1)}, u32[]{:S(2)}, u32[]{:S(2)}) collective-permute-start(bf16[224,128]{1,0:T(8,128)(2,1)S(1)} %get-tuple-element.54), channel_id=1, source_target_pairs={{0,9},{1,8},{2,11},{3,10},{4,13},{5,12},{6,15},{7,14},{8,1},{9,0},... | collective-permute-start | bytes 172040 | tf_op jit(solution)/shard_map/ppermute | solution.py:433
  26.4 6.7 %collective-permute-start.10 = (bf16[224,128]{1,0:T(8,128)(2,1)S(1)}, bf16[224,128]{1,0:T(8,128)(2,1)S(1)}, u32[]{:S(2)}, u32[]{:S(2)}) collective-permute-start(bf16[224,128]{1,0:T(8,128)(2,1)S(1)} %fusion.2), channel_id=1, source_target_pairs={{0,6},{1,7},{2,4},{3,5},{4,2},{5,3},{6,0},{7,1},{8,14},{9,15},{10,... | collective-permute-start | bytes 172040 | tf_op jit(solution)/shard_map/ppermute | solution.py:433
  26.9 7.4 %collective-permute-start.9 = (bf16[224,128]{1,0:T(8,128)(2,1)S(1)}, bf16[224,128]{1,0:T(8,128)(2,1)S(1)}, u32[]{:S(2)}, u32[]{:S(2)}) collective-permute-start(bf16[224,128]{1,0:T(8,128)(2,1)S(1)} %fusion.2), channel_id=1, source_target_pairs={{0,5},{1,4},{2,7},{3,6},{4,1},{5,0},{6,3},{7,2},{8,13},{9,12},{10,... | collective-permute-start | bytes 172040 | tf_op jit(solution)/shard_map/ppermute | solution.py:433
  27.2 7.4 %collective-permute-start.8 = (bf16[224,128]{1,0:T(8,128)(2,1)S(1)}, bf16[224,128]{1,0:T(8,128)(2,1)S(1)}, u32[]{:S(2)}, u32[]{:S(2)}) collective-permute-start(bf16[224,128]{1,0:T(8,128)(2,1)S(1)} %fusion.2), channel_id=1, source_target_pairs={{0,3},{1,2},{2,1},{3,0},{4,7},{5,6},{6,5},{7,4},{8,11},{9,10},{10,... | collective-permute-start | bytes 172040 | tf_op jit(solution)/shard_map/ppermute | solution.py:433
  34.7 5.2 %collective-permute-start.13 = (bf16[224,128]{1,0:T(8,128)(2,1)S(1)}, bf16[224,128]{1,0:T(8,128)(2,1)S(1)}, u32[]{:S(2)}, u32[]{:S(2)}) collective-permute-start(bf16[224,128]{1,0:T(8,128)(2,1)S(1)} %add_convert_fusion), channel_id=1, source_target_pairs={{0,24},{1,25},{2,26},{3,27},{4,28},{5,29},{6,30},{7,31},{8,16},{9,... | collective-permute-start | bytes 172040 | tf_op jit(solution)/shard_map/ppermute | solution.py:433
  36.6 4.4 %collective-permute-start.12 = (bf16[224,128]{1,0:T(8,128)(2,1)S(1)}, bf16[224,128]{1,0:T(8,128)(2,1)S(1)}, u32[]{:S(2)}, u32[]{:S(2)}) collective-permute-start(bf16[224,128]{1,0:T(8,128)(2,1)S(1)} %add_convert_fusion), channel_id=1, source_target_pairs={{0,17},{1,16},{2,19},{3,18},{4,21},{5,20},{6,23},{7,22},{8,25},{9,... | collective-permute-start | bytes 172040 | tf_op jit(solution)/shard_map/ppermute | solution.py:433
  36.6 4.4 %collective-permute-start.11 = (bf16[224,128]{1,0:T(8,128)(2,1)S(1)}, bf16[224,128]{1,0:T(8,128)(2,1)S(1)}, u32[]{:S(2)}, u32[]{:S(2)}) collective-permute-start(bf16[224,128]{1,0:T(8,128)(2,1)S(1)} %add_convert_fusion), channel_id=1, source_target_pairs={{0,9},{1,8},{2,11},{3,10},{4,13},{5,12},{6,15},{7,14},{8,1},{9,0},... | collective-permute-start | bytes 172040 | tf_op jit(solution)/shard_map/ppermute | solution.py:433
  41.1 1.6 %collective-permute-start.14 = (bf16[4,224,128]{2,1,0:T(8,128)(2,1)S(1)}, bf16[4,224,128]{2,1,0:T(8,128)(2,1)S(1)}, u32[]{:S(2)}, u32[]{:S(2)}) collective-permute-start(bf16[4,224,128]{2,1,0:T(8,128)(2,1)S(1)} %pad_maximum_fusion.mine), channel_id=1, source_target_pairs={{0,1},{1,0},{2,3},{3,2},{4,5},{5,4},{6,7},{7,6},{8,9},{9,8},{10,11... | collective-permute-start | bytes 688136 | tf_op jit(solution)/shard_map/ppermute | solution.py:463

commit v13 on v12

--- a/solution.py
+++ b/solution.py
@@ -12,7 +12,6 @@
 
 F32 = jnp.float32
 BF16 = jnp.bfloat16
-EDGE = 16
 AREA = ("lat", "lon")
 
 
@@ -75,7 +74,7 @@
     return jnp.where(where, 1.0, 0.0).astype(BF16)
 
 
-def local_kernel(pre, slope, act_t, line, act_s):
+def local_kernel(pre, slope, act_t, act_ends, line, act_s):
     rows, cols, c1 = pre.shape
     half = cols // 2
 
@@ -84,7 +83,9 @@
         for pc in range(2):
             value = line[pl.ds(pc, half, stride=2), :]
             cdf = cdf_of(value)
-            act_s[r % 2, r // 2, :, pc * c1:(pc + 1) * c1] = (value * cdf).astype(BF16)
+            act = value * cdf
+            act_s[r % 2, r // 2, :, pc * c1:(pc + 1) * c1] = act.astype(BF16)
+            act_ends[pc, pl.ds(r, 1), :] = act[pc * (half - 1):pc * (half - 1) + 1]
             slope[r, :, pc * c1:(pc + 1) * c1] = slope_of(value, cdf)
         return carry
 
@@ -93,7 +94,7 @@
         act_t[pr] = act_s[pr].reshape(rows // 2 * half, 2 * c1).T
 
 
-def layout_kernel(fields, w_first, w_second, fields_t, taps_first, taps_second, turned):
+def layout_kernel(fields, w_first, w_second, fields_t, field_ends, taps_first, taps_second, turned):
     rows, c0, cols = fields.shape
     c1 = w_first.shape[3]
     half = cols // 2
@@ -108,6 +109,10 @@
     for q in range(rows // 2):
         fields_t[:c0, q * cols:(q + 1) * cols] = jnp.where(low, turned[2 * q, :, :cols], turned[2 * q + 1, :, cols:])
         fields_t[c0:, q * cols:(q + 1) * cols] = jnp.where(low, turned[2 * q, :, cols:], turned[2 * q + 1, :, :cols])
+    cell = lax.broadcasted_iota(jnp.int32, (rows * half, 2 * rows), 0)
+    n = lax.broadcasted_iota(jnp.int32, (rows * half, 2 * rows), 1)
+    pick = one_at(cell == (n % rows) * half + (n // rows) * (half - 1))
+    field_ends[...] = dot(fields_t[...], pick).astype(BF16)
     taps_second[...] = jnp.zeros_like(taps_second)
     taps_first[...] = jnp.zeros_like(taps_first)
     for a in range(3):
@@ -122,10 +127,10 @@
                     taps_first[start:start + c0, k * c1:(k + 1) * c1] = w_first[a, b]
 
 
-def middle_kernel(lats, grad_out, row_a, row_b, col_a, col_b, slope, act_t, fields_t, taps,
-                  spread, own, other,
-                  grid, wide, prods, ends, line, side, sides, sums, corner, keep):
-    band, first, last, even, core = position(lats)
+def middle_kernel(lats, grad_out, row_a, row_b, slope, act_t, fields_t, taps,
+                  spread, keep, raw_ends, slope_ends, out_ends,
+                  grid, wide, prods, ends, line, sums, corner):
+    _, first, last, even, _ = position(lats)
     top = jnp.where(even, row_b[...], row_a[...])
     bottom = jnp.where(even, row_a[...], row_b[...])
     rows, half, c2 = slope.shape
@@ -133,87 +138,76 @@
     pooled = rows // 2
     c0 = fields_t.shape[0] // 2
     cells = pooled * half
-
-    grid[:, half:, :] = jnp.zeros((pooled + 2, EDGE, c1), F32)
-    grid[1:pooled + 1, :half, :] = grad_out[...].astype(F32)
-    grid[0, :half, :] = top[2 * half:, :].astype(F32)
+    raw_ends[...] = jnp.zeros_like(raw_ends)
+    slope_ends[...] = jnp.zeros_like(slope_ends)
+    out_ends[...] = jnp.zeros_like(out_ends)
+
+    grid[1:pooled + 1] = grad_out[...].astype(F32)
+    grid[0] = top[2 * half:, :].astype(F32)
     outside = jnp.where(last, 0.0, 1.0)
-    grid[pooled + 1, :half, :] = bottom[2 * half:, :].astype(F32) * outside
-    side[1 - core] = col_a[...].astype(F32)
-    side[core] = col_b[...].astype(F32)
-    for i in range(pooled + 2):
-        at = rows + i - 1
-        if i == 0:
-            at = rows + pooled + 2
-        if i == pooled + 1:
-            at = rows + pooled + 3
-        kept = outside if i == pooled + 1 else 1.0
-        grid[i, half:half + 1, :] = side[1, at:at + 1, :] * kept
-        grid[i, half + EDGE - 1:half + EDGE, :] = side[0, at:at + 1, :] * kept
+    grid[pooled + 1] = bottom[2 * half:, :].astype(F32) * outside
+    at = lax.broadcasted_iota(jnp.int32, (half, c1), 0)
     for i in range(pooled + 2):
         here = grid[i]
-        wide[i, :, :c1] = pltpu.roll(here, 1, 0).astype(BF16)
+        out_ends[0, i:i + 1] = here[:1]
+        out_ends[1, i:i + 1] = here[half - 1:]
+        wide[i, :, :c1] = jnp.where(at == 0, 0.0, pltpu.roll(here, 1, 0)).astype(BF16)
         wide[i, :, c1:2 * c1] = here.astype(BF16)
-        wide[i, :, 2 * c1:3 * c1] = pltpu.roll(here, half + EDGE - 1, 0).astype(BF16)
+        wide[i, :, 2 * c1:3 * c1] = jnp.where(at == half - 1, 0.0, pltpu.roll(here, half - 1, 0)).astype(BF16)
         wide[i, :, 3 * c1:] = here.astype(BF16)
 
-    flat = wide[1:pooled + 1].reshape(pooled * (half + EDGE), 4 * c1)
+    flat = wide[1:pooled + 1].reshape(cells, 4 * c1)
     for a in range(3):
-        prods[a] = dot_nt(flat, taps[a]).reshape(pooled, half + EDGE, c2)
+        prods[a] = dot_nt(flat, taps[a]).reshape(pooled, half, c2)
     fold = jnp.where(first, taps[0], taps[2])
     ends[0] = dot_nt(wide[0], fold)
     ends[1] = dot_nt(wide[0], taps[1])
     ends[2] = dot_nt(wide[pooled + 1], taps[0])
     ends[3] = dot_nt(wide[pooled + 1], taps[1])
 
-    for s in range(2):
-        sides[s] = slope_of(side[s], cdf_of(side[s]))
-
-    def place(r, total, incline, edge):
-        inner = total[:half] * incline
-        rim = total[half:]
-        after = rim[:1, :c1] * sides[1, pl.ds(edge, 1), :]
-        before = rim[EDGE - 1:, c1:] * sides[0, pl.ds(edge, 1), :]
+    def place(r, total, incline):
+        inner = total * incline
+        raw_ends[0, pl.ds(r, 1), :] = total[:1, :c1]
+        raw_ends[1, pl.ds(r, 1), :] = total[half - 1:, c1:]
+        slope_ends[0, pl.ds(r, 1), :] = incline[:1, :c1]
+        slope_ends[1, pl.ds(r, 1), :] = incline[half - 1:, c1:]
         even, odd = inner[:, :c1], inner[:, c1:]
-        at = lax.broadcasted_iota(jnp.int32, (half, c1), 0)
-        spread[r, :, :c1] = jnp.where(at == 0, before, pltpu.roll(odd, 1, 0)).astype(BF16)
-        spread[r, :, c1:2 * c1] = even.astype(BF16)
-        spread[r, :, 2 * c1:3 * c1] = odd.astype(BF16)
-        spread[r, :, 3 * c1:] = jnp.where(at == half - 1, after, pltpu.roll(even, half - 1, 0)).astype(BF16)
+        spread[r, :, :c1] = jnp.where(at == 0, 0.0, pltpu.roll(odd, 1, 0)).astype(BF16)
+        spread[r, :, c1:2 * c1] = jnp.where(at == 0, 0.0, even).astype(BF16)
+        spread[r, :, 2 * c1:3 * c1] = jnp.where(at == half - 1, 0.0, odd).astype(BF16)
+        spread[r, :, 3 * c1:] = jnp.where(at == half - 1, 0.0, pltpu.roll(even, half - 1, 0)).astype(BF16)
 
     def halo_slope(message):
         line[...] = message[:2 * half, :].astype(F32)
         both = [line[pl.ds(pc, half, stride=2), :] for pc in range(2)]
         return jnp.concatenate([slope_of(v, cdf_of(v)) for v in both], axis=1)
 
-    place(0, ends[0] + ends[1] + prods[0, 0], halo_slope(top), rows + pooled)
-    place(1, ends[0] + prods[1, 0] + prods[0, 0], slope[0], 0)
+    place(0, ends[0] + ends[1] + prods[0, 0], halo_slope(top))
+    place(1, ends[0] + prods[1, 0] + prods[0, 0], slope[0])
 
     def pair(i, carry):
         middle = prods[2, i] + prods[1, i]
-        place(2 * i + 2, middle + prods[0, i + 1], slope[2 * i + 1], 2 * i + 1)
-        place(2 * i + 3, prods[2, i] + prods[1, i + 1] + prods[0, i + 1], slope[2 * i + 2], 2 * i + 2)
+        place(2 * i + 2, middle + prods[0, i + 1], slope[2 * i + 1])
+        place(2 * i + 3, prods[2, i] + prods[1, i + 1] + prods[0, i + 1], slope[2 * i + 2])
         return carry
 
     lax.fori_loop(0, pooled - 1, pair, 0)
     final = prods[2, pooled - 1]
-    place(rows, final + prods[1, pooled - 1] + ends[2], slope[rows - 1], rows - 1)
-    place(rows + 1, (final + ends[3] + ends[2]) * outside, halo_slope(bottom), rows + pooled + 1)
+    place(rows, final + prods[1, pooled - 1] + ends[2], slope[rows - 1])
+    place(rows + 1, (final + ends[3] + ends[2]) * outside, halo_slope(bottom))
 
     is_first = jnp.where(first, 1.0, 0.0).astype(BF16)
     not_first = jnp.where(first, 0.0, 1.0).astype(BF16)
-    above = wide[0, :half, :3 * c1]
-    wide[0, :half, :3 * c1] = above * not_first
+    above = wide[0, :, :3 * c1]
+    wide[0, :, :3 * c1] = above * not_first
     for n, (pr, start) in enumerate(((0, 0), (0, 1), (1, 1), (1, 2))):
-        around = wide[start:start + pooled, :half, :3 * c1].reshape(cells, 3 * c1)
+        around = wide[start:start + pooled, :, :3 * c1].reshape(cells, 3 * c1)
         sums[n] = dot(act_t[pr], around)
     corner[...] = dot(act_t[0, :, :half], above * is_first)
 
     unit = c0
     per_tap = c1 // unit
     count = 9 * per_tap + 9
-    held = own.shape[0]
-    block = held // lats
 
     def put(k, value):
         keep[k * unit:(k + 1) * unit, :] = value
@@ -248,20 +242,132 @@
             even = got[:c0, (2 - b) * c1:(3 - b) * c1]
             odd = got[c0:, (3 - b) * c1:(4 - b) * c1]
             put(9 * per_tap + 3 * a + b, even + odd)
-    if 2 * held > count * unit:
-        keep[count * unit:] = jnp.zeros((2 * held - count * unit, c1), F32)
+    if keep.shape[0] > count * unit:
+        keep[count * unit:] = jnp.zeros((keep.shape[0] - count * unit, c1), F32)
+
+
+def columns_kernel(lats, col_a, col_b, act_ends, field_ends, taps, keep, raw_ends, slope_ends, out_ends,
+                   ends, own, other, lhs, values, right_hand, total):
+    band, first, last, _, core = position(lats)
+    c1 = act_ends.shape[2]
+    rows = act_ends.shape[1]
+    pooled = rows // 2
+    c0 = field_ends.shape[0] // 2
+    span, size = raw_ends.shape[1], col_a.shape[0]
+    got_a, got_b = col_a[...].astype(F32), col_b[...].astype(F32)
+    message = jnp.concatenate([jnp.where(core == 0, got_b, got_a), jnp.where(core == 0, got_a, got_b)], 1)
+    at = lax.broadcasted_iota(jnp.int32, (size, 2 * c1), 0)
+    message = jnp.where(jnp.logical_and(at == rows + pooled + 3, last), 0.0, message).astype(BF16)
+
+    n = lax.broadcasted_iota(jnp.int32, (3 * span, size), 0)
+    k = lax.broadcasted_iota(jnp.int32, (3 * span, size), 1)
+    row = n % span
+    want = (row - n // span + 2) // 2 - 1
+    place = jnp.where(want < 0, rows + pooled + 2, jnp.where(want == pooled, rows + pooled + 3, rows + want))
+    beside = dot(one_at(jnp.logical_and(k == place, row < rows + 2)), message)
+    n = lax.broadcasted_iota(jnp.int32, (3 * span, out_ends.shape[1]), 0)
+    k = lax.broadcasted_iota(jnp.int32, (3 * span, out_ends.shape[1]), 1)
+    row = n % span
+    want = (row - n // span + 2) // 2
+    pick = one_at(jnp.logical_and(k == want, row < rows + 2))
+    within = dot(pick, jnp.concatenate([out_ends[0], out_ends[1]], 1).astype(BF16))
+    n = lax.broadcasted_iota(jnp.int32, (span, size), 0)
+    k = lax.broadcasted_iota(jnp.int32, (span, size), 1)
+    place = jnp.where(n == 0, rows + pooled, jnp.where(n == rows + 1, rows + pooled + 1, n - 1))
+    saved = dot(one_at(jnp.logical_and(k == place, n < rows + 2)), message)
+    incline = slope_of(saved, cdf_of(saved))
+
+    head = lax.broadcasted_iota(jnp.int32, (span, 2 * c1), 0) < 2
+    turned = jnp.logical_and(head, first)
+    lhs[...] = jnp.zeros_like(lhs)
+    rights = []
+    for a in range(4):
+        sides, inner = (x[min(a, 2) * span:(min(a, 2) + 1) * span] for x in (beside, within))
+        if a == 2:
+            sides, inner = jnp.where(turned, 0.0, sides), jnp.where(turned, 0.0, inner)
+        if a == 3:
+            sides, inner = jnp.where(turned, sides, 0.0), jnp.where(turned, inner, 0.0)
+        rights.append(sides)
+        sides, inner = sides.astype(BF16), inner.astype(BF16)
+        left, right = sides[:, :c1], sides[:, c1:]
+        lhs[a, :span, c1:2 * c1] = left
+        lhs[a, :span, 2 * c1:3 * c1] = inner[:, :c1]
+        lhs[a, :span, 3 * c1:] = left
+        lhs[a, span:2 * span, :c1] = left
+        lhs[a, 2 * span:3 * span, :c1] = inner[:, c1:]
+        lhs[a, 2 * span:3 * span, c1:2 * c1] = right
+        lhs[a, 2 * span:3 * span, 3 * c1:] = right
+        lhs[a, 3 * span:, 2 * c1:3 * c1] = right
+    found = dot_nt(lhs[0], taps[0]) + dot_nt(lhs[1], taps[1]) + dot_nt(lhs[2], taps[2]) + dot_nt(lhs[3], taps[0])
+    row = lax.broadcasted_iota(jnp.int32, (span, c1), 0)
+    inside = jnp.where(jnp.logical_or(row > rows + 1, jnp.logical_and(row == rows + 1, last)), 0.0, 1.0)
+    values[0] = found[:span, c1:] * incline[:, :c1] * inside
+    values[1] = (raw_ends[0] + found[span:2 * span, :c1]) * slope_ends[0] * inside
+    values[2] = (raw_ends[1] + found[3 * span:, c1:]) * slope_ends[1] * inside
+    values[3] = found[2 * span:3 * span, :c1] * incline[:, c1:] * inside
+    ends[...] = values[...].astype(BF16)
+
+    total[...] = keep[...]
+    for side, b in ((0, 2), (1, 0)):
+        around = jnp.concatenate([x[1:rows + 1, side * c1:(side + 1) * c1] for x in rights], 1).astype(BF16)
+        terms = lax.dot_general(act_ends[side].astype(BF16), around, (((0,), (0,)), ((), ())),
+                                preferred_element_type=F32) * 0.25
+        for a in range(3):
+            term = terms[:, a * c1:(a + 1) * c1]
+            if a == 0:
+                term = term + terms[:, 3 * c1:]
+            low = (3 * a + b) * c1
+            total[low:low + c1] = total[low:low + c1] + term
+    right_hand[...] = jnp.zeros_like(right_hand)
+    top = lax.broadcasted_iota(jnp.int32, (rows, c1), 0) == 0
+    over = jnp.logical_and(top, first)
+    for a in range(4):
+        for j in range(4):
+            value = values[j, 2 - min(a, 2):2 - min(a, 2) + rows]
+            if a == 2:
+                value = jnp.where(over, 0.0, value)
+            if a == 3:
+                value = jnp.where(over, value, 0.0)
+            right_hand[a, j // 2 * rows:(j // 2 + 1) * rows, j * c1:(j + 1) * c1] = value.astype(BF16)
+    for a in range(3):
+        got = dot(field_ends[...], right_hand[a])
+        if a == 0:
+            got = got + dot(field_ends[...], right_hand[3])
+        for b in range(3):
+            even = got[:c0, (2 - b) * c1:(3 - b) * c1]
+            odd = got[c0:, (3 - b) * c1:(4 - b) * c1]
+            low = 9 * c1 + (3 * a + b) * c0
+            total[low:low + c0] = total[low:low + c0] + even + odd
+
+    held = own.shape[0]
+    block = held // lats
     mine = half_held()
     for target, half_of in ((own, mine), (other, 1 - mine)):
         for far in range(lats):
-            at = half_of * held + (band ^ far) * block
-            target[far * block:(far + 1) * block] = keep[pl.ds(pl.multiple_of(at, block), block), :]
-
-
-def last_kernel(spread, taps, out, total, turned):
+            start = half_of * held + (band ^ far) * block
+            target[far * block:(far + 1) * block] = total[pl.ds(pl.multiple_of(start, block), block), :]
+
+
+def last_kernel(lats, part, ends, taps, out, spread, values, total, turned):
     rows, c0, cols = out.shape
     half = cols // 2
     c2 = 2 * c0
     depth = spread.shape[2]
+    first = position(lats)[1]
+    spread[...] = part[...]
+    c1 = depth // 4
+    for j in range(4):
+        values[:, j * c1:(j + 1) * c1] = ends[j].astype(F32)
+    at = lax.broadcasted_iota(jnp.int32, (16, 2 * c1), 0)
+    for r in range(rows + 3):
+        n = 0 if r == rows + 2 else r
+        for side, (low, spot) in enumerate(((0, 0), (half - 16, 15))):
+            lanes = slice(2 * side * c1, 2 * (side + 1) * c1)
+            new = values[n:n + 1, lanes]
+            if n == 0:
+                new = jnp.where(first == (r != 0), new, 0.0)
+            tile = spread[r, low:low + 16, lanes].astype(F32)
+            spread[r, low:low + 16, lanes] = jnp.where(at == spot, new, tile).astype(BF16)
     result = dot_nt(taps[:c2], spread[2:rows + 2].reshape(rows * half, depth))
     for a in (1, 2):
         result = result + dot_nt(taps[a * c2:(a + 1) * c2],
@@ -350,14 +456,15 @@
     row_b = lax.ppermute(row_b, AREA, pairs)
     row_a = lax.ppermute(row_a, AREA, every)
 
-    slope, act_t = pl.pallas_call(
+    slope, act_t, act_ends = pl.pallas_call(
         local_kernel,
         out_shape=(
             shape((rows, half, 2 * c1), F32),
             shape((2, 2 * c1, pooled * half), BF16),
+            shape((2, rows, c1), F32),
         ),
         in_specs=vmem(1),
-        out_specs=tuple(vmem(2)),
+        out_specs=tuple(vmem(3)),
         scratch_shapes=[
             pltpu.VMEM((cols, c1), F32),
             pltpu.VMEM((2, pooled, half, 2 * c1), BF16),
@@ -367,8 +474,21 @@
                                       transcendentals=2 * rows * cols * c1),
     )(held_pre)
 
-    fields = jnp.transpose(inputs, (0, 2, 1))
-    row_b, row_a, slope, fields = lax.optimization_barrier((row_b, row_a, slope, fields))
+    fields_t, field_ends, taps_first, taps_second = pl.pallas_call(
+        layout_kernel,
+        out_shape=(
+            shape((2 * c0, rows * half), BF16),
+            shape((2 * c0, 2 * rows), BF16),
+            shape((6 * c0, 4 * c1), BF16),
+            shape((3, 2 * c1, 4 * c1), BF16),
+        ),
+        in_specs=vmem(3),
+        out_specs=tuple(vmem(4)),
+        scratch_shapes=[pltpu.VMEM((rows, c0, 2 * cols), BF16)],
+        compiler_params=params(16),
+        cost_estimate=pl.CostEstimate(flops=4 * rows * cols * c0 * cols, bytes_accessed=3 << 20, transcendentals=0),
+    )(jnp.transpose(inputs, (0, 2, 1)), w_first, w_second)
+    row_b, row_a, slope, fields_t = lax.optimization_barrier((row_b, row_a, slope, fields_t))
 
     def corners(at):
         places = (at * (cols - 1), cols + at * (half - 1))
@@ -382,49 +502,53 @@
     col_b = lax.ppermute(col_b, "lon", [(i, (i + 2 * (i % 2) - 1) % lons) for i in range(lons)])
     col_a = lax.ppermute(col_a, "lon", [(i, i ^ 1) for i in range(lons)])
 
-    fields_t, taps_first, taps_second = pl.pallas_call(
-        layout_kernel,
-        out_shape=(
-            shape((2 * c0, rows * half), BF16),
-            shape((6 * c0, 4 * c1), BF16),
-            shape((3, 2 * c1, 4 * c1), BF16),
-        ),
-        in_specs=vmem(3),
-        out_specs=tuple(vmem(3)),
-        scratch_shapes=[pltpu.VMEM((rows, c0, 2 * cols), BF16)],
-        compiler_params=params(16),
-        cost_estimate=pl.CostEstimate(flops=4 * rows * cols * c0 * cols, bytes_accessed=3 << 20, transcendentals=0),
-    )(fields, w_first, w_second)
-    col_a, col_b, fields_t = lax.optimization_barrier((col_a, col_b, fields_t))
-
     block = -(-9 * (c1 + c0) // (32 * lats)) * 16
     held = lats * block
-    span = half + EDGE
-    spread, own, other = pl.pallas_call(
+    reach = -(-(rows + 2) // 16) * 16
+    spread, keep, raw_ends, slope_ends, out_ends = pl.pallas_call(
         functools.partial(middle_kernel, lats),
         out_shape=(
             shape((rows + 3, half, 4 * c1), BF16),
+            shape((2 * held, c1), F32),
+            shape((2, reach, c1), F32),
+            shape((2, reach, c1), F32),
+            shape((2, -(-(pooled + 2) // 16) * 16, c1), F32),
+        ),
+        in_specs=vmem(7),
+        out_specs=tuple(vmem(5)),
+        scratch_shapes=[
+            pltpu.VMEM((pooled + 2, half, c1), F32),
+            pltpu.VMEM((pooled + 2, half, 4 * c1), BF16),
+            pltpu.VMEM((3, pooled, half, 2 * c1), F32),
+            pltpu.VMEM((4, half, 2 * c1), F32),
+            pltpu.VMEM((cols, c1), F32),
+            pltpu.VMEM((4, 2 * c1, 3 * c1), F32),
+            pltpu.VMEM((2 * c1, 3 * c1), F32),
+        ],
+        compiler_params=params(16),
+        cost_estimate=pl.CostEstimate(flops=2 * rows * cols * c1 * 9 * (2 * c1 + c0), bytes_accessed=8 << 20,
+                                      transcendentals=0),
+    )(grad_out, row_a, row_b, slope, act_t, fields_t, taps_second)
+    col_a, col_b, keep = lax.optimization_barrier((col_a, col_b, keep))
+
+    ends, own, other = pl.pallas_call(
+        functools.partial(columns_kernel, lats),
+        out_shape=(
+            shape((4, reach, c1), BF16),
             shape((held, c1), F32),
             shape((held, c1), F32),
         ),
         in_specs=vmem(9),
         out_specs=tuple(vmem(3)),
         scratch_shapes=[
-            pltpu.VMEM((pooled + 2, span, c1), F32),
-            pltpu.VMEM((pooled + 2, span, 4 * c1), BF16),
-            pltpu.VMEM((3, pooled, span, 2 * c1), F32),
-            pltpu.VMEM((4, span, 2 * c1), F32),
-            pltpu.VMEM((cols, c1), F32),
-            pltpu.VMEM((2, edge, c1), F32),
-            pltpu.VMEM((2, edge, c1), F32),
-            pltpu.VMEM((4, 2 * c1, 3 * c1), F32),
-            pltpu.VMEM((2 * c1, 3 * c1), F32),
+            pltpu.VMEM((4, 4 * reach, 4 * c1), BF16),
+            pltpu.VMEM((4, reach, c1), F32),
+            pltpu.VMEM((4, 2 * rows, 4 * c1), BF16),
             pltpu.VMEM((2 * held, c1), F32),
         ],
         compiler_params=params(16),
-        cost_estimate=pl.CostEstimate(flops=2 * rows * cols * c1 * 9 * (2 * c1 + c0), bytes_accessed=8 << 20,
-                                      transcendentals=0),
-    )(grad_out, row_a, row_b, col_a, col_b, slope, act_t, fields_t, taps_second)
+        cost_estimate=pl.CostEstimate(flops=1 << 28, bytes_accessed=3 << 20, transcendentals=0),
+    )(col_a, col_b, act_ends, field_ends, taps_second, keep, raw_ends, slope_ends, out_ends)
 
     swap = [(i, i ^ 1) for i in range(lons)]
 
@@ -435,20 +559,22 @@
 
     parts = (own + lax.ppermute(other, "lon", swap)).reshape(lats, block, c1)
     sent = [parts[far].astype(BF16) for far in range(1, lats)]
-    *sent, spread = lax.optimization_barrier((*sent, spread))
+    *sent, ends = lax.optimization_barrier((*sent, ends))
     got = [between_chips(sent[far - 1], far, 0) for far in reversed(range(1, lats))]
     grad_inputs = pl.pallas_call(
-        last_kernel,
+        functools.partial(last_kernel, lats),
         out_shape=shape((rows, c0, cols), BF16),
-        in_specs=vmem(2),
+        in_specs=vmem(3),
         out_specs=vmem(1)[0],
         scratch_shapes=[
+            pltpu.VMEM((rows + 3, half, 4 * c1), BF16),
+            pltpu.VMEM((reach, 4 * c1), F32),
             pltpu.VMEM((2 * c0, rows * half), F32),
             pltpu.VMEM((pooled, c0, 2 * cols), BF16),
         ],
         compiler_params=params(12),
         cost_estimate=pl.CostEstimate(flops=2 * rows * cols * c1 * 9 * c0, bytes_accessed=3 << 20, transcendentals=0),
-    )(spread, taps_first)
+    )(spread, ends, taps_first)
     *got, grad_inputs = lax.optimization_barrier((*got, grad_inputs))
     total = parts[0]
     for value in got:

time: 43.8 us -> 42.6 us (0.973)
  waiting for transfers between devices: 16.9 us -> 14.6 us
  Pallas kernels: 8.44 us -> 9.56 us
    ppermute x1, waiting for transfers between devices: 2.7 us -> 0.78 us  [body(): lax.ppermute(col_b, 'lon', [(i, (i + 2 * (i % 2) - 1) % lons) for i in ra...]
    pallas_call x1 -> x2, Pallas kernels: 2.19 us -> 3.34 us  [the longest x1 2.16 us: body(): pl.pallas_call(functools.partial(last_kernel, lats), out_shape=shape((row...]
    ppermute x1, waiting for transfers between devices: 1.17 us -> 0.44 us  [body(): row_b = lax.ppermute(row_b, AREA, pairs)]
  transfers between devices with their start and end apart: 15 -> 15, of which waited for: 11 -> 11; matrix products, arithmetic and copies ran while one was open for 0% -> 0% of each run, Pallas kernels for 8% -> 15%
where the time goes in v13:
time: 42.6 us; the launch traced here: 42.5 us
  starting transfers between devices  17.2 us (40%)
  waiting for transfers between devices  14.6 us (34%)
  Pallas kernels  9.56 us (22%)
  between operations  0.79 us (2%)
    ppermute x9, starting transfers between devices, between_chips(): lax.ppermute(value, AREA, [(i * lons + j, (i ^ over_lat) * lons + (j ^ 2...  10.7 us
    ppermute x9, waiting for transfers between devices, between_chips(): lax.ppermute(value, AREA, [(i * lons + j, (i ^ over_lat) * lons + (j ^ 2...  8.66 us
    ppermute x1, starting transfers between devices, body(): row_b = lax.ppermute(row_b, AREA, pairs)  4.1 us
    pallas_call x1, Pallas kernels, body(): pl.pallas_call(functools.partial(middle_kernel, lats), out_shape=(shape((...  2.4 us
    pallas_call x1, Pallas kernels, body(): pl.pallas_call(functools.partial(last_kernel, lats), out_shape=shape((row...  2.16 us
    ppermute x1, waiting for transfers between devices, body(): parts = (own + lax.ppermute(other, 'lon', swap)).reshape(lats, block, c1)  1.8 us
    ppermute x1, waiting for transfers between devices, body(): row_a = lax.ppermute(row_a, AREA, every)  1.49 us
    ppermute x1, waiting for transfers between devices, body(): theirs = lax.ppermute(mine, 'lon', swap)  1.38 us
  transfers between devices with their start and end apart: 15, of which 11 were waited for; matrix products, arithmetic and copies ran while one was open for 0% of the time, Pallas kernels for 15%

profile of v13, /device:TPU:0, one launch (start us, length us, event | category | flops | bytes accessed | tf_op | source)
XLA Modules:
  0.0 42.5 jit_solution(13324632619188398893)
XLA Ops:
  0.6 0.0 copy-start.3
  0.6 0.0 copy-start
  0.7 0.0 copy-start.2
  0.7 0.0 copy-start.1
  0.7 1.2 %shard_map.76 = (bf16[192,128]{1,0:T(8,128)(2,1)S(1)}, bf16[192,128]{1,0:T(8,128)(2,1)S(1)}, bf16[32,128]{1,0:T(8,128)(2,1)S(1)}, bf16[32,128]{1,0:T(8,128)(2,1)S(1)}, bf16[16,128,128]{2,1,0:T(8,128)(2,1)S(1)}) custom-call(bf16[16,128,128]{2,1,0:T(8,128)(2,1)} %pre_far.1, bf16[8,64,128]{2,1,0:T(8,128)(2,1)} %grad_out.1), custom_call_target="tpu_custom_call" | custom-call | flops 1000 | bytes 262144 | tf_op jit(solution)/shard_map/pallas_call | solution.py:432
  1.9 4.1 %collective-permute-start = (bf16[192,128]{1,0:T(8,128)(2,1)S(1)}, bf16[192,128]{1,0:T(8,128)(2,1)S(1)}, u32[]{:S(2)}, u32[]{:S(2)}) collective-permute-start(bf16[192,128]{1,0:T(8,128)(2,1)S(1)} %get-tuple-element.41), channel_id=1, source_target_pairs={{0,4},{1,5},{2,6},{3,7},{4,0},{5,1},{6,2},{7,3},{24,28},{25,29},{2... | collective-permute-start | bytes 147464 | tf_op jit(solution)/shard_map/ppermute | solution.py:456
  6.0 0.4 collective-permute-start.1
  6.4 0.1 pad.9.clone
  6.4 0.9 %shard_map.77 = (f32[16,64,256]{2,1,0:T(8,128)S(1)}, bf16[2,256,512]{2,1,0:T(8,128)(2,1)S(1)}, f32[2,16,128]{2,1,0:T(8,128)S(1)}) custom-call(bf16[16,128,128]{2,1,0:T(8,128)(2,1)S(1)} %get-tuple-element.43.pre), custom_call_target="tpu_custom_call" | custom-call | flops 15728640 | bytes 2097152 | tf_op jit(solution)/shard_map/pallas_call | solution.py:459
  7.4 0.0 copy-done
  7.4 0.0 copy-done.2
  7.4 0.0 copy-done.1
  7.4 0.7 %shard_map.78 = (bf16[128,1024]{1,0:T(8,128)(2,1)S(1)}, bf16[128,32]{1,0:T(8,128)(2,1)S(1)}, bf16[384,512]{1,0:T(8,128)(2,1)S(1)}, bf16[3,256,512]{2,1,0:T(8,128)(2,1)S(1)}) custom-call(bf16[16,64,128]{2,1,0:T(8,128)(2,1)S(1)} %bitcast.8, bf16[3,3,64,128]{3,2,1,0:T(8,128)(2,1)S(1)} %copy-done.2, bf16[3,3,128,128]{3,2,1,0:T(8,128)(2,1)S(1)} %copy-done), custom_call_target="tpu_custom_call" | custom-call | flops 67108864 | bytes 3145728 | tf_op jit(solution)/shard_map/pallas_call | solution.py:477
  8.1 0.4 %collective-permute-done.row_b = bf16[192,128]{1,0:T(8,128)(2,1)S(1)} collective-permute-done((bf16[192,128]{1,0:T(8,128)(2,1)S(1)}, bf16[192,128]{1,0:T(8,128)(2,1)S(1)}, u32[]{:S(2)}, u32[]{:S(2)}) %collective-permute-start) | collective-permute-done | bytes 49184 | tf_op jit(solution)/shard_map/ppermute | solution.py:456
  8.6 1.5 %collective-permute-done.1.row_a = bf16[192,128]{1,0:T(8,128)(2,1)S(1)} collective-permute-done((bf16[192,128]{1,0:T(8,128)(2,1)S(1)}, bf16[192,128]{1,0:T(8,128)(2,1)S(1)}, u32[]{:S(2)}, u32[]{:S(2)}) %collective-permute-start.1) | collective-permute-done | bytes 49184 | tf_op jit(solution)/shard_map/ppermute | solution.py:457
  10.1 0.1 maximum_maximum_fusion.1
  10.2 0.8 %collective-permute-start.3 = (bf16[32,128]{1,0:T(8,128)(2,1)S(1)}, bf16[32,128]{1,0:T(8,128)(2,1)S(1)}, u32[]{:S(2)}, u32[]{:S(2)}) collective-permute-start(bf16[32,128]{1,0:T(8,128)(2,1)S(1)} %get-tuple-element.94), channel_id=1, source_target_pairs={{0,7},{1,2},{2,1},{3,4},{4,3},{5,6},{6,5},{7,0},{8,15},{9,10},{10,... | collective-permute-start | bytes 24584 | tf_op jit(solution)/shard_map/ppermute | solution.py:502
  11.0 0.9 %collective-permute-start.2 = (bf16[32,128]{1,0:T(8,128)(2,1)S(1)}, bf16[32,128]{1,0:T(8,128)(2,1)S(1)}, u32[]{:S(2)}, u32[]{:S(2)}) collective-permute-start(bf16[32,128]{1,0:T(8,128)(2,1)S(1)} %get-tuple-element.95), channel_id=1, source_target_pairs={{0,1},{1,0},{2,3},{3,2},{4,5},{5,4},{6,7},{7,6},{8,9},{9,8},{10,11... | collective-permute-start | bytes 24584 | tf_op jit(solution)/shard_map/ppermute | solution.py:503
  11.9 0.0 copy-done.3
  11.9 2.4 %shard_map.79 = (bf16[19,64,512]{2,1,0:T(8,128)(2,1)S(1)}, f32[1792,128]{1,0:T(8,128)S(1)}, f32[2,32,128]{2,1,0:T(8,128)S(1)}, f32[2,32,128]{2,1,0:T(8,128)S(1)}, f32[2,16,128]{2,1,0:T(8,128)S(1)}) custom-call(bf16[8,64,128]{2,1,0:T(8,128)(2,1)S(1)} %copy-done.3, bf16[192,128]{1,0:T(8,128)(2,1)S(1)} %collective-permute-done.1.row_a, ...), custom_call_target="tpu_custom_call" | custom-call | flops 1509949440 | bytes 8388608 | tf_op jit(solution)/shard_map/pallas_call | solution.py:508
  14.3 0.8 %collective-permute-done.3.col_b = bf16[32,128]{1,0:T(8,128)(2,1)S(1)} collective-permute-done((bf16[32,128]{1,0:T(8,128)(2,1)S(1)}, bf16[32,128]{1,0:T(8,128)(2,1)S(1)}, u32[]{:S(2)}, u32[]{:S(2)}) %collective-permute-start.3) | collective-permute-done | bytes 8224 | tf_op jit(solution)/shard_map/ppermute | solution.py:502
  15.1 0.0 collective-permute-done.2.col_a
  15.1 1.2 %shard_map.80 = (bf16[4,32,128]{2,1,0:T(8,128)(2,1)S(1)}, f32[896,128]{1,0:T(8,128)S(1)}, f32[896,128]{1,0:T(8,128)S(1)}) custom-call(bf16[32,128]{1,0:T(8,128)(2,1)S(1)} %collective-permute-done.2.col_a, bf16[32,128]{1,0:T(8,128)(2,1)S(1)} %collective-permute-done.3.col_b, f32[2,16,128]{2,1,0:T(8,128)S(1)} %get-tuple-element.56.act_ends, ...), custom_call_target="tpu_custom_call" | custom-call | flops 268435456 | bytes 3145728 | tf_op jit(solution)/shard_map/pallas_call | solution.py:534
  16.3 0.1 collective-permute-start.4
  16.3 1.8 %collective-permute-done.4 = f32[896,128]{1,0:T(8,128)S(1)} collective-permute-done((f32[896,128]{1,0:T(8,128)S(1)}, f32[896,128]{1,0:T(8,128)S(1)}, u32[]{:S(2)}, u32[]{:S(2)}) %collective-permute-start.4) | collective-permute-done | bytes 458784 | tf_op jit(solution)/shard_map/ppermute | solution.py:560
  18.1 0.1 fusion.3
  18.2 2.5 %collective-permute-start.5 = (bf16[224,128]{1,0:T(8,128)(2,1)S(1)}, bf16[224,128]{1,0:T(8,128)(2,1)S(1)}, u32[]{:S(2)}, u32[]{:S(2)}) collective-permute-start(bf16[224,128]{1,0:T(8,128)(2,1)S(1)} %get-tuple-element.65), channel_id=1, source_target_pairs={{0,24},{1,25},{2,26},{3,27},{4,28},{5,29},{6,30},{7,31},{8,16},{9,... | collective-permute-start | bytes 172040 | tf_op jit(solution)/shard_map/ppermute | solution.py:557
  20.7 0.0 collective-permute-start.6
  20.8 0.8 %collective-permute-start.7 = (bf16[224,128]{1,0:T(8,128)(2,1)S(1)}, bf16[224,128]{1,0:T(8,128)(2,1)S(1)}, u32[]{:S(2)}, u32[]{:S(2)}) collective-permute-start(bf16[224,128]{1,0:T(8,128)(2,1)S(1)} %get-tuple-element.67), channel_id=1, source_target_pairs={{0,9},{1,8},{2,11},{3,10},{4,13},{5,12},{6,15},{7,14},{8,1},{9,0},... | collective-permute-start | bytes 172040 | tf_op jit(solution)/shard_map/ppermute | solution.py:557
  21.5 2.2 %shard_map.81 = bf16[16,64,128]{2,1,0:T(8,128)(2,1)} custom-call(bf16[19,64,512]{2,1,0:T(8,128)(2,1)S(1)} %get-tuple-element.68.part, bf16[4,32,128]{2,1,0:T(8,128)(2,1)S(1)} %get-tuple-element.69.ends, bf16[384,512]{1,0:T(8,128)(2,1)S(1)} %get-tuple-element.70.taps), custom_call_target="tpu_custom_call" | custom-call | flops 301989888 | bytes 3145728 | tf_op jit(solution)/shard_map/pallas_call | solution.py:564
  23.7 0.0 collective-permute-done.5
  23.7 1.3 %collective-permute-done.6 = bf16[224,128]{1,0:T(8,128)(2,1)S(1)} collective-permute-done((bf16[224,128]{1,0:T(8,128)(2,1)S(1)}, bf16[224,128]{1,0:T(8,128)(2,1)S(1)}, u32[]{:S(2)}, u32[]{:S(2)}) %collective-permute-start.6) | collective-permute-done | bytes 57376 | tf_op jit(solution)/shard_map/ppermute | solution.py:557
  24.9 0.0 collective-permute-done.7
  25.0 1.6 %collective-permute-start.10 = (bf16[224,128]{1,0:T(8,128)(2,1)S(1)}, bf16[224,128]{1,0:T(8,128)(2,1)S(1)}, u32[]{:S(2)}, u32[]{:S(2)}) collective-permute-start(bf16[224,128]{1,0:T(8,128)(2,1)S(1)} %fusion.2), channel_id=1, source_target_pairs={{0,6},{1,7},{2,4},{3,5},{4,2},{5,3},{6,0},{7,1},{8,14},{9,15},{10,... | collective-permute-start | bytes 172040 | tf_op jit(solution)/shard_map/ppermute | solution.py:557
  26.5 0.0 collective-permute-start.9
  26.5 2.6 %collective-permute-start.8 = (bf16[224,128]{1,0:T(8,128)(2,1)S(1)}, bf16[224,128]{1,0:T(8,128)(2,1)S(1)}, u32[]{:S(2)}, u32[]{:S(2)}) collective-permute-start(bf16[224,128]{1,0:T(8,128)(2,1)S(1)} %fusion.2), channel_id=1, source_target_pairs={{0,3},{1,2},{2,1},{3,0},{4,7},{5,6},{6,5},{7,4},{8,11},{9,10},{10,... | collective-permute-start | bytes 172040 | tf_op jit(solution)/shard_map/ppermute | solution.py:557
  29.1 2.4 %collective-permute-done.10 = bf16[224,128]{1,0:T(8,128)(2,1)S(1)} collective-permute-done((bf16[224,128]{1,0:T(8,128)(2,1)S(1)}, bf16[224,128]{1,0:T(8,128)(2,1)S(1)}, u32[]{:S(2)}, u32[]{:S(2)}) %collective-permute-start.10) | collective-permute-done | bytes 57376 | tf_op jit(solution)/shard_map/ppermute | solution.py:557
  31.5 1.8 %collective-permute-done.9 = bf16[224,128]{1,0:T(8,128)(2,1)S(1)} collective-permute-done((bf16[224,128]{1,0:T(8,128)(2,1)S(1)}, bf16[224,128]{1,0:T(8,128)(2,1)S(1)}, u32[]{:S(2)}, u32[]{:S(2)}) %collective-permute-start.9) | collective-permute-done | bytes 57376 | tf_op jit(solution)/shard_map/ppermute | solution.py:557
  33.3 0.2 collective-permute-done.8
  33.5 1.8 %collective-permute-start.13 = (bf16[224,128]{1,0:T(8,128)(2,1)S(1)}, bf16[224,128]{1,0:T(8,128)(2,1)S(1)}, u32[]{:S(2)}, u32[]{:S(2)}) collective-permute-start(bf16[224,128]{1,0:T(8,128)(2,1)S(1)} %add_convert_fusion), channel_id=1, source_target_pairs={{0,24},{1,25},{2,26},{3,27},{4,28},{5,29},{6,30},{7,31},{8,16},{9,... | collective-permute-start | bytes 172040 | tf_op jit(solution)/shard_map/ppermute | solution.py:557
  35.3 0.0 collective-permute-start.12
  35.3 1.5 %collective-permute-start.11 = (bf16[224,128]{1,0:T(8,128)(2,1)S(1)}, bf16[224,128]{1,0:T(8,128)(2,1)S(1)}, u32[]{:S(2)}, u32[]{:S(2)}) collective-permute-start(bf16[224,128]{1,0:T(8,128)(2,1)S(1)} %add_convert_fusion), channel_id=1, source_target_pairs={{0,9},{1,8},{2,11},{3,10},{4,13},{5,12},{6,15},{7,14},{8,1},{9,0},... | collective-permute-start | bytes 172040 | tf_op jit(solution)/shard_map/ppermute | solution.py:557
  36.8 1.9 %collective-permute-done.13 = bf16[224,128]{1,0:T(8,128)(2,1)S(1)} collective-permute-done((bf16[224,128]{1,0:T(8,128)(2,1)S(1)}, bf16[224,128]{1,0:T(8,128)(2,1)S(1)}, u32[]{:S(2)}, u32[]{:S(2)}) %collective-permute-start.13) | collective-permute-done | bytes 57376 | tf_op jit(solution)/shard_map/ppermute | solution.py:557
  38.7 1.2 %collective-permute-done.12 = bf16[224,128]{1,0:T(8,128)(2,1)S(1)} collective-permute-done((bf16[224,128]{1,0:T(8,128)(2,1)S(1)}, bf16[224,128]{1,0:T(8,128)(2,1)S(1)}, u32[]{:S(2)}, u32[]{:S(2)}) %collective-permute-start.12) | collective-permute-done | bytes 57376 | tf_op jit(solution)/shard_map/ppermute | solution.py:557
  39.9 0.0 collective-permute-done.11
  39.9 0.2 collective-permute-start.14
  40.1 1.4 %collective-permute-done.14.theirs = bf16[4,224,128]{2,1,0:T(8,128)(2,1)S(1)} collective-permute-done((bf16[4,224,128]{2,1,0:T(8,128)(2,1)S(1)}, bf16[4,224,128]{2,1,0:T(8,128)(2,1)S(1)}, u32[]{:S(2)}, u32[]{:S(2)}) %collective-permute-start.14) | collective-permute-done | bytes 229408 | tf_op jit(solution)/shard_map/ppermute | solution.py:589
  41.5 1.0 %shard_map.82 = (f32[576,128]{1,0:T(8,128)}, f32[1152,128]{1,0:T(8,128)}) custom-call(bf16[4,224,128]{2,1,0:T(8,128)(2,1)S(1)} %pad_maximum_fusion.mine, bf16[4,224,128]{2,1,0:T(8,128)(2,1)S(1)} %collective-permute-done.14.theirs), custom_call_target="tpu_custom_call" | custom-call | flops 1000 | bytes 1572864 | tf_op jit(solution)/shard_map/pallas_call | solution.py:591
  (10 shorter events, 0.2 us)
Async XLA Ops:
  0.6 11.3 %copy-start.3 = (bf16[8,64,128]{2,1,0:T(8,128)(2,1)S(1)}, bf16[8,64,128]{2,1,0:T(8,128)(2,1)}, u32[]{:S(2)}) copy-start(bf16[8,64,128]{2,1,0:T(8,128)(2,1)} %grad_out.1) | copy-start | bytes 393220
  0.6 6.7 %copy-start = (bf16[3,3,128,128]{3,2,1,0:T(8,128)(2,1)S(1)}, bf16[3,3,128,128]{3,2,1,0:T(8,128)(2,1)}, u32[]{:S(2)}) copy-start(bf16[3,3,128,128]{3,2,1,0:T(8,128)(2,1)} %w_second.1) | copy-start | bytes 884740
  0.7 6.7 %copy-start.2 = (bf16[3,3,64,128]{3,2,1,0:T(8,128)(2,1)S(1)}, bf16[3,3,64,128]{3,2,1,0:T(8,128)(2,1)}, u32[]{:S(2)}) copy-start(bf16[3,3,64,128]{3,2,1,0:T(8,128)(2,1)} %w_first.1) | copy-start | bytes 442372
  0.7 6.7 %copy-start.1 = (bf16[16,128,64]{1,2,0:T(8,128)(2,1)S(1)}, bf16[16,128,64]{1,2,0:T(8,128)(2,1)}, u32[]{:S(2)}) copy-start(bf16[16,128,64]{1,2,0:T(8,128)(2,1)} %param.5) | copy-start | bytes 786436
  1.9 6.7 %collective-permute-start = (bf16[192,128]{1,0:T(8,128)(2,1)S(1)}, bf16[192,128]{1,0:T(8,128)(2,1)S(1)}, u32[]{:S(2)}, u32[]{:S(2)}) collective-permute-start(bf16[192,128]{1,0:T(8,128)(2,1)S(1)} %get-tuple-element.41), channel_id=1, source_target_pairs={{0,4},{1,5},{2,6},{3,7},{4,0},{5,1},{6,2},{7,3},{24,28},{25,29},{2... | collective-permute-start | bytes 147464 | tf_op jit(solution)/shard_map/ppermute | solution.py:456
  6.0 4.1 %collective-permute-start.1 = (bf16[192,128]{1,0:T(8,128)(2,1)S(1)}, bf16[192,128]{1,0:T(8,128)(2,1)S(1)}, u32[]{:S(2)}, u32[]{:S(2)}) collective-permute-start(bf16[192,128]{1,0:T(8,128)(2,1)S(1)} %get-tuple-element.42), channel_id=1, source_target_pairs={{0,8},{1,9},{2,10},{3,11},{4,12},{5,13},{6,14},{7,15},{8,0},{9,1},... | collective-permute-start | bytes 147464 | tf_op jit(solution)/shard_map/ppermute | solution.py:457
  10.2 4.9 %collective-permute-start.3 = (bf16[32,128]{1,0:T(8,128)(2,1)S(1)}, bf16[32,128]{1,0:T(8,128)(2,1)S(1)}, u32[]{:S(2)}, u32[]{:S(2)}) collective-permute-start(bf16[32,128]{1,0:T(8,128)(2,1)S(1)} %get-tuple-element.94), channel_id=1, source_target_pairs={{0,7},{1,2},{2,1},{3,4},{4,3},{5,6},{6,5},{7,0},{8,15},{9,10},{10,... | collective-permute-start | bytes 24584 | tf_op jit(solution)/shard_map/ppermute | solution.py:502
  11.0 4.1 %collective-permute-start.2 = (bf16[32,128]{1,0:T(8,128)(2,1)S(1)}, bf16[32,128]{1,0:T(8,128)(2,1)S(1)}, u32[]{:S(2)}, u32[]{:S(2)}) collective-permute-start(bf16[32,128]{1,0:T(8,128)(2,1)S(1)} %get-tuple-element.95), channel_id=1, source_target_pairs={{0,1},{1,0},{2,3},{3,2},{4,5},{5,4},{6,7},{7,6},{8,9},{9,8},{10,11... | collective-permute-start | bytes 24584 | tf_op jit(solution)/shard_map/ppermute | solution.py:503
  16.3 1.9 %collective-permute-start.4 = (f32[896,128]{1,0:T(8,128)S(1)}, f32[896,128]{1,0:T(8,128)S(1)}, u32[]{:S(2)}, u32[]{:S(2)}) collective-permute-start(f32[896,128]{1,0:T(8,128)S(1)} %get-tuple-element.63), channel_id=1, source_target_pairs={{0,1},{1,0},{2,3},{3,2},{4,5},{5,4},{6,7},{7,6},{8,9},{9,8},{10,11... | collective-permute-start | bytes 1376264 | tf_op jit(solution)/shard_map/ppermute | solution.py:560
  18.2 5.4 %collective-permute-start.5 = (bf16[224,128]{1,0:T(8,128)(2,1)S(1)}, bf16[224,128]{1,0:T(8,128)(2,1)S(1)}, u32[]{:S(2)}, u32[]{:S(2)}) collective-permute-start(bf16[224,128]{1,0:T(8,128)(2,1)S(1)} %get-tuple-element.65), channel_id=1, source_target_pairs={{0,24},{1,25},{2,26},{3,27},{4,28},{5,29},{6,30},{7,31},{8,16},{9,... | collective-permute-start | bytes 172040 | tf_op jit(solution)/shard_map/ppermute | solution.py:557
  20.7 4.2 %collective-permute-start.6 = (bf16[224,128]{1,0:T(8,128)(2,1)S(1)}, bf16[224,128]{1,0:T(8,128)(2,1)S(1)}, u32[]{:S(2)}, u32[]{:S(2)}) collective-permute-start(bf16[224,128]{1,0:T(8,128)(2,1)S(1)} %get-tuple-element.66), channel_id=1, source_target_pairs={{0,17},{1,16},{2,19},{3,18},{4,21},{5,20},{6,23},{7,22},{8,25},{9,... | collective-permute-start | bytes 172040 | tf_op jit(solution)/shard_map/ppermute | solution.py:557
  20.8 4.2 %collective-permute-start.7 = (bf16[224,128]{1,0:T(8,128)(2,1)S(1)}, bf16[224,128]{1,0:T(8,128)(2,1)S(1)}, u32[]{:S(2)}, u32[]{:S(2)}) collective-permute-start(bf16[224,128]{1,0:T(8,128)(2,1)S(1)} %get-tuple-element.67), channel_id=1, source_target_pairs={{0,9},{1,8},{2,11},{3,10},{4,13},{5,12},{6,15},{7,14},{8,1},{9,0},... | collective-permute-start | bytes 172040 | tf_op jit(solution)/shard_map/ppermute | solution.py:557
  25.0 6.5 %collective-permute-start.10 = (bf16[224,128]{1,0:T(8,128)(2,1)S(1)}, bf16[224,128]{1,0:T(8,128)(2,1)S(1)}, u32[]{:S(2)}, u32[]{:S(2)}) collective-permute-start(bf16[224,128]{1,0:T(8,128)(2,1)S(1)} %fusion.2), channel_id=1, source_target_pairs={{0,6},{1,7},{2,4},{3,5},{4,2},{5,3},{6,0},{7,1},{8,14},{9,15},{10,... | collective-permute-start | bytes 172040 | tf_op jit(solution)/shard_map/ppermute | solution.py:557
  26.5 6.8 %collective-permute-start.9 = (bf16[224,128]{1,0:T(8,128)(2,1)S(1)}, bf16[224,128]{1,0:T(8,128)(2,1)S(1)}, u32[]{:S(2)}, u32[]{:S(2)}) collective-permute-start(bf16[224,128]{1,0:T(8,128)(2,1)S(1)} %fusion.2), channel_id=1, source_target_pairs={{0,5},{1,4},{2,7},{3,6},{4,1},{5,0},{6,3},{7,2},{8,13},{9,12},{10,... | collective-permute-start | bytes 172040 | tf_op jit(solution)/shard_map/ppermute | solution.py:557
  26.5 6.9 %collective-permute-start.8 = (bf16[224,128]{1,0:T(8,128)(2,1)S(1)}, bf16[224,128]{1,0:T(8,128)(2,1)S(1)}, u32[]{:S(2)}, u32[]{:S(2)}) collective-permute-start(bf16[224,128]{1,0:T(8,128)(2,1)S(1)} %fusion.2), channel_id=1, source_target_pairs={{0,3},{1,2},{2,1},{3,0},{4,7},{5,6},{6,5},{7,4},{8,11},{9,10},{10,... | collective-permute-start | bytes 172040 | tf_op jit(solution)/shard_map/ppermute | solution.py:557
  33.5 5.2 %collective-permute-start.13 = (bf16[224,128]{1,0:T(8,128)(2,1)S(1)}, bf16[224,128]{1,0:T(8,128)(2,1)S(1)}, u32[]{:S(2)}, u32[]{:S(2)}) collective-permute-start(bf16[224,128]{1,0:T(8,128)(2,1)S(1)} %add_convert_fusion), channel_id=1, source_target_pairs={{0,24},{1,25},{2,26},{3,27},{4,28},{5,29},{6,30},{7,31},{8,16},{9,... | collective-permute-start | bytes 172040 | tf_op jit(solution)/shard_map/ppermute | solution.py:557
  35.3 4.6 %collective-permute-start.12 = (bf16[224,128]{1,0:T(8,128)(2,1)S(1)}, bf16[224,128]{1,0:T(8,128)(2,1)S(1)}, u32[]{:S(2)}, u32[]{:S(2)}) collective-permute-start(bf16[224,128]{1,0:T(8,128)(2,1)S(1)} %add_convert_fusion), channel_id=1, source_target_pairs={{0,17},{1,16},{2,19},{3,18},{4,21},{5,20},{6,23},{7,22},{8,25},{9,... | collective-permute-start | bytes 172040 | tf_op jit(solution)/shard_map/ppermute | solution.py:557
  35.3 4.6 %collective-permute-start.11 = (bf16[224,128]{1,0:T(8,128)(2,1)S(1)}, bf16[224,128]{1,0:T(8,128)(2,1)S(1)}, u32[]{:S(2)}, u32[]{:S(2)}) collective-permute-start(bf16[224,128]{1,0:T(8,128)(2,1)S(1)} %add_convert_fusion), channel_id=1, source_target_pairs={{0,9},{1,8},{2,11},{3,10},{4,13},{5,12},{6,15},{7,14},{8,1},{9,0},... | collective-permute-start | bytes 172040 | tf_op jit(solution)/shard_map/ppermute | solution.py:557
  39.9 1.6 %collective-permute-start.14 = (bf16[4,224,128]{2,1,0:T(8,128)(2,1)S(1)}, bf16[4,224,128]{2,1,0:T(8,128)(2,1)S(1)}, u32[]{:S(2)}, u32[]{:S(2)}) collective-permute-start(bf16[4,224,128]{2,1,0:T(8,128)(2,1)S(1)} %pad_maximum_fusion.mine), channel_id=1, source_target_pairs={{0,1},{1,0},{2,3},{3,2},{4,5},{5,4},{6,7},{7,6},{8,9},{9,8},{10,11... | collective-permute-start | bytes 688136 | tf_op jit(solution)/shard_map/ppermute | solution.py:589

commit v14 on v13

--- a/solution.py
+++ b/solution.py
@@ -387,19 +387,25 @@
             out[2 * q + rp] = found[q * c0:(q + 1) * c0, rp * cols:(rp + 1) * cols]
 
 
-def gather_kernel(mine, theirs, out_first, out_second):
+def gather_kernel(mine, theirs, out_first, out_second, whole, sems):
     lats, rows, c1 = mine.shape
     band, held = lax.axis_index("lat"), half_held()
     size = out_second.shape[0]
     total = size + out_first.shape[0]
+    copies = []
     for h in range(2):
         for i in range(lats):
             at = (h * lats + i) * rows
+            here, there = (x[i ^ band].astype(F32) for x in (mine, theirs))
+            whole[at:at + rows] = jnp.where(held == h, here, there)
             for out, base, end in ((out_second, 0, size), (out_first, size, total)):
                 low, high = max(at, base), min(at + rows, end)
                 if low < high:
-                    here, there = (x[i ^ band, low - at:high - at] for x in (mine, theirs))
-                    out[low - base:high - base] = jnp.where(held == h, here, there).astype(F32)
+                    copies.append(pltpu.make_async_copy(whole.at[pl.ds(low, high - low)],
+                                                        out.at[pl.ds(low - base, high - low)], sems.at[len(copies)]))
+                    copies[-1].start()
+    for copy in copies:
+        copy.wait()
 
 
 def vmem(count):
@@ -585,14 +591,16 @@
     while len(terms) > 1:
         terms = [terms[k] + terms[k + 1] for k in range(0, len(terms), 2)]
     part = terms[0].astype(BF16)
-    mine = jnp.stack([part] + [between_chips(part, far, 0) for far in range(1, lats)], 0)
-    theirs = lax.ppermute(mine, "lon", swap)
+    mine = [part] + [between_chips(part, far, 0) for far in range(1, lats)]
+    theirs = [lax.ppermute(value, "lon", swap) for value in mine]
+    mine, theirs = jnp.stack(mine, 0), jnp.stack(theirs, 0)
 
     grad_w_first, grad_w_second = pl.pallas_call(
         gather_kernel,
         out_shape=(shape((9 * c0, c1), F32), shape((9 * c1, c1), F32)),
         in_specs=vmem(2),
-        out_specs=tuple(vmem(2)),
+        out_specs=tuple(far(2)),
+        scratch_shapes=[pltpu.VMEM((2 * held, c1), F32), pltpu.SemaphoreType.DMA((2 * lats + 2,))],
         compiler_params=params(8),
         cost_estimate=pl.CostEstimate(flops=1000, bytes_accessed=3 << 19, transcendentals=0),
     )(mine, theirs)

time: 42.6 us -> 42.5 us (level)
  waiting for transfers between devices: 14.6 us -> 14 us
    ppermute x1 -> x4, waiting for transfers between devices: 1.38 us -> 0.84 us  [body(): theirs = [lax.ppermute(value, 'lon', swap) for value in mine]]
  transfers between devices with their start and end apart: 15 -> 18, of which waited for: 11 -> 12; matrix products, arithmetic and copies ran while one was open for 0% -> 0% of each run, Pallas kernels for 15% -> 15%
where the time goes in v14:
time: 42.5 us; the launch traced here: 42.3 us
  starting transfers between devices  17.5 us (41%)
  waiting for transfers between devices  14 us (33%)
  Pallas kernels  9.57 us (23%)
  between operations  0.81 us (2%)
    ppermute x9, starting transfers between devices, between_chips(): lax.ppermute(value, AREA, [(i * lons + j, (i ^ over_lat) * lons + (j ^ 2...  10.7 us
    ppermute x9, waiting for transfers between devices, between_chips(): lax.ppermute(value, AREA, [(i * lons + j, (i ^ over_lat) * lons + (j ^ 2...  8.65 us
    ppermute x1, starting transfers between devices, body(): row_b = lax.ppermute(row_b, AREA, pairs)  4.1 us
    pallas_call x1, Pallas kernels, body(): pl.pallas_call(functools.partial(middle_kernel, lats), out_shape=(shape((...  2.4 us
    pallas_call x1, Pallas kernels, body(): pl.pallas_call(functools.partial(last_kernel, lats), out_shape=shape((row...  2.16 us
    ppermute x1, waiting for transfers between devices, body(): parts = (own + lax.ppermute(other, 'lon', swap)).reshape(lats, block, c1)  1.8 us
    ppermute x1, waiting for transfers between devices, body(): row_a = lax.ppermute(row_a, AREA, every)  1.49 us
    pallas_call x1, Pallas kernels, body(): pl.pallas_call(functools.partial(columns_kernel, lats), out_shape=(shape(...  1.18 us
  transfers between devices with their start and end apart: 18, of which 12 were waited for; matrix products, arithmetic and copies ran while one was open for 0% of the time, Pallas kernels for 15%

profile of v14, /device:TPU:0, one launch (start us, length us, event | category | flops | bytes accessed | tf_op | source)
XLA Modules:
  0.0 42.3 jit_solution(8178726716915743061)
XLA Ops:
  0.6 0.0 copy-start.3
  0.6 0.0 copy-start
  0.7 0.0 copy-start.2
  0.7 0.0 copy-start.1
  0.7 1.2 %shard_map.76 = (bf16[192,128]{1,0:T(8,128)(2,1)S(1)}, bf16[192,128]{1,0:T(8,128)(2,1)S(1)}, bf16[32,128]{1,0:T(8,128)(2,1)S(1)}, bf16[32,128]{1,0:T(8,128)(2,1)S(1)}, bf16[16,128,128]{2,1,0:T(8,128)(2,1)S(1)}) custom-call(bf16[16,128,128]{2,1,0:T(8,128)(2,1)} %pre_far.1, bf16[8,64,128]{2,1,0:T(8,128)(2,1)} %grad_out.1), custom_call_target="tpu_custom_call" | custom-call | flops 1000 | bytes 262144 | tf_op jit(solution)/shard_map/pallas_call | solution.py:438
  1.9 4.1 %collective-permute-start = (bf16[192,128]{1,0:T(8,128)(2,1)S(1)}, bf16[192,128]{1,0:T(8,128)(2,1)S(1)}, u32[]{:S(2)}, u32[]{:S(2)}) collective-permute-start(bf16[192,128]{1,0:T(8,128)(2,1)S(1)} %get-tuple-element.41), channel_id=1, source_target_pairs={{0,4},{1,5},{2,6},{3,7},{4,0},{5,1},{6,2},{7,3},{24,28},{25,29},{2... | collective-permute-start | bytes 147464 | tf_op jit(solution)/shard_map/ppermute | solution.py:462
  6.0 0.4 collective-permute-start.1
  6.4 0.1 pad.13.clone
  6.4 0.9 %shard_map.77 = (f32[16,64,256]{2,1,0:T(8,128)S(1)}, bf16[2,256,512]{2,1,0:T(8,128)(2,1)S(1)}, f32[2,16,128]{2,1,0:T(8,128)S(1)}) custom-call(bf16[16,128,128]{2,1,0:T(8,128)(2,1)S(1)} %get-tuple-element.43.pre), custom_call_target="tpu_custom_call" | custom-call | flops 15728640 | bytes 2097152 | tf_op jit(solution)/shard_map/pallas_call | solution.py:465
  7.4 0.0 copy-done
  7.4 0.0 copy-done.2
  7.4 0.0 copy-done.1
  7.4 0.7 %shard_map.78 = (bf16[128,1024]{1,0:T(8,128)(2,1)S(1)}, bf16[128,32]{1,0:T(8,128)(2,1)S(1)}, bf16[384,512]{1,0:T(8,128)(2,1)S(1)}, bf16[3,256,512]{2,1,0:T(8,128)(2,1)S(1)}) custom-call(bf16[16,64,128]{2,1,0:T(8,128)(2,1)S(1)} %bitcast.12, bf16[3,3,64,128]{3,2,1,0:T(8,128)(2,1)S(1)} %copy-done.2, bf16[3,3,128,128]{3,2,1,0:T(8,128)(2,1)S(1)} %copy-done), custom_call_target="tpu_custom_call" | custom-call | flops 67108864 | bytes 3145728 | tf_op jit(solution)/shard_map/pallas_call | solution.py:483
  8.1 0.4 %collective-permute-done.row_b = bf16[192,128]{1,0:T(8,128)(2,1)S(1)} collective-permute-done((bf16[192,128]{1,0:T(8,128)(2,1)S(1)}, bf16[192,128]{1,0:T(8,128)(2,1)S(1)}, u32[]{:S(2)}, u32[]{:S(2)}) %collective-permute-start) | collective-permute-done | bytes 49184 | tf_op jit(solution)/shard_map/ppermute | solution.py:462
  8.6 1.5 %collective-permute-done.1.row_a = bf16[192,128]{1,0:T(8,128)(2,1)S(1)} collective-permute-done((bf16[192,128]{1,0:T(8,128)(2,1)S(1)}, bf16[192,128]{1,0:T(8,128)(2,1)S(1)}, u32[]{:S(2)}, u32[]{:S(2)}) %collective-permute-start.1) | collective-permute-done | bytes 49184 | tf_op jit(solution)/shard_map/ppermute | solution.py:463
  10.1 0.1 maximum_maximum_fusion.1
  10.2 0.8 %collective-permute-start.3 = (bf16[32,128]{1,0:T(8,128)(2,1)S(1)}, bf16[32,128]{1,0:T(8,128)(2,1)S(1)}, u32[]{:S(2)}, u32[]{:S(2)}) collective-permute-start(bf16[32,128]{1,0:T(8,128)(2,1)S(1)} %get-tuple-element.94), channel_id=1, source_target_pairs={{0,7},{1,2},{2,1},{3,4},{4,3},{5,6},{6,5},{7,0},{8,15},{9,10},{10,... | collective-permute-start | bytes 24584 | tf_op jit(solution)/shard_map/ppermute | solution.py:508
  11.0 0.9 %collective-permute-start.2 = (bf16[32,128]{1,0:T(8,128)(2,1)S(1)}, bf16[32,128]{1,0:T(8,128)(2,1)S(1)}, u32[]{:S(2)}, u32[]{:S(2)}) collective-permute-start(bf16[32,128]{1,0:T(8,128)(2,1)S(1)} %get-tuple-element.95), channel_id=1, source_target_pairs={{0,1},{1,0},{2,3},{3,2},{4,5},{5,4},{6,7},{7,6},{8,9},{9,8},{10,11... | collective-permute-start | bytes 24584 | tf_op jit(solution)/shard_map/ppermute | solution.py:509
  11.9 0.0 copy-done.3
  11.9 2.4 %shard_map.79 = (bf16[19,64,512]{2,1,0:T(8,128)(2,1)S(1)}, f32[1792,128]{1,0:T(8,128)S(1)}, f32[2,32,128]{2,1,0:T(8,128)S(1)}, f32[2,32,128]{2,1,0:T(8,128)S(1)}, f32[2,16,128]{2,1,0:T(8,128)S(1)}) custom-call(bf16[8,64,128]{2,1,0:T(8,128)(2,1)S(1)} %copy-done.3, bf16[192,128]{1,0:T(8,128)(2,1)S(1)} %collective-permute-done.1.row_a, ...), custom_call_target="tpu_custom_call" | custom-call | flops 1509949440 | bytes 8388608 | tf_op jit(solution)/shard_map/pallas_call | solution.py:514
  14.3 0.8 %collective-permute-done.3.col_b = bf16[32,128]{1,0:T(8,128)(2,1)S(1)} collective-permute-done((bf16[32,128]{1,0:T(8,128)(2,1)S(1)}, bf16[32,128]{1,0:T(8,128)(2,1)S(1)}, u32[]{:S(2)}, u32[]{:S(2)}) %collective-permute-start.3) | collective-permute-done | bytes 8224 | tf_op jit(solution)/shard_map/ppermute | solution.py:508
  15.1 0.0 collective-permute-done.2.col_a
  15.1 1.2 %shard_map.80 = (bf16[4,32,128]{2,1,0:T(8,128)(2,1)S(1)}, f32[896,128]{1,0:T(8,128)S(1)}, f32[896,128]{1,0:T(8,128)S(1)}) custom-call(bf16[32,128]{1,0:T(8,128)(2,1)S(1)} %collective-permute-done.2.col_a, bf16[32,128]{1,0:T(8,128)(2,1)S(1)} %collective-permute-done.3.col_b, f32[2,16,128]{2,1,0:T(8,128)S(1)} %get-tuple-element.56.act_ends, ...), custom_call_target="tpu_custom_call" | custom-call | flops 268435456 | bytes 3145728 | tf_op jit(solution)/shard_map/pallas_call | solution.py:540
  16.3 0.1 collective-permute-start.4
  16.3 1.8 %collective-permute-done.4 = f32[896,128]{1,0:T(8,128)S(1)} collective-permute-done((f32[896,128]{1,0:T(8,128)S(1)}, f32[896,128]{1,0:T(8,128)S(1)}, u32[]{:S(2)}, u32[]{:S(2)}) %collective-permute-start.4) | collective-permute-done | bytes 458784 | tf_op jit(solution)/shard_map/ppermute | solution.py:566
  18.1 0.1 fusion.3
  18.2 2.5 %collective-permute-start.5 = (bf16[224,128]{1,0:T(8,128)(2,1)S(1)}, bf16[224,128]{1,0:T(8,128)(2,1)S(1)}, u32[]{:S(2)}, u32[]{:S(2)}) collective-permute-start(bf16[224,128]{1,0:T(8,128)(2,1)S(1)} %get-tuple-element.65), channel_id=1, source_target_pairs={{0,24},{1,25},{2,26},{3,27},{4,28},{5,29},{6,30},{7,31},{8,16},{9,... | collective-permute-start | bytes 172040 | tf_op jit(solution)/shard_map/ppermute | solution.py:563
  20.7 0.0 collective-permute-start.6
  20.8 0.8 %collective-permute-start.7 = (bf16[224,128]{1,0:T(8,128)(2,1)S(1)}, bf16[224,128]{1,0:T(8,128)(2,1)S(1)}, u32[]{:S(2)}, u32[]{:S(2)}) collective-permute-start(bf16[224,128]{1,0:T(8,128)(2,1)S(1)} %get-tuple-element.67), channel_id=1, source_target_pairs={{0,9},{1,8},{2,11},{3,10},{4,13},{5,12},{6,15},{7,14},{8,1},{9,0},... | collective-permute-start | bytes 172040 | tf_op jit(solution)/shard_map/ppermute | solution.py:563
  21.5 2.2 %shard_map.81 = bf16[16,64,128]{2,1,0:T(8,128)(2,1)} custom-call(bf16[19,64,512]{2,1,0:T(8,128)(2,1)S(1)} %get-tuple-element.68.part, bf16[4,32,128]{2,1,0:T(8,128)(2,1)S(1)} %get-tuple-element.69.ends, bf16[384,512]{1,0:T(8,128)(2,1)S(1)} %get-tuple-element.70.taps), custom_call_target="tpu_custom_call" | custom-call | flops 301989888 | bytes 3145728 | tf_op jit(solution)/shard_map/pallas_call | solution.py:570
  23.7 0.0 collective-permute-done.5
  23.7 1.3 %collective-permute-done.6 = bf16[224,128]{1,0:T(8,128)(2,1)S(1)} collective-permute-done((bf16[224,128]{1,0:T(8,128)(2,1)S(1)}, bf16[224,128]{1,0:T(8,128)(2,1)S(1)}, u32[]{:S(2)}, u32[]{:S(2)}) %collective-permute-start.6) | collective-permute-done | bytes 57376 | tf_op jit(solution)/shard_map/ppermute | solution.py:563
  24.9 0.0 collective-permute-done.7
  25.0 1.6 %collective-permute-start.10 = (bf16[224,128]{1,0:T(8,128)(2,1)S(1)}, bf16[224,128]{1,0:T(8,128)(2,1)S(1)}, u32[]{:S(2)}, u32[]{:S(2)}) collective-permute-start(bf16[224,128]{1,0:T(8,128)(2,1)S(1)} %fusion.2), channel_id=1, source_target_pairs={{0,6},{1,7},{2,4},{3,5},{4,2},{5,3},{6,0},{7,1},{8,14},{9,15},{10,... | collective-permute-start | bytes 172040 | tf_op jit(solution)/shard_map/ppermute | solution.py:563
  26.5 0.0 collective-permute-start.9
  26.5 2.6 %collective-permute-start.8 = (bf16[224,128]{1,0:T(8,128)(2,1)S(1)}, bf16[224,128]{1,0:T(8,128)(2,1)S(1)}, u32[]{:S(2)}, u32[]{:S(2)}) collective-permute-start(bf16[224,128]{1,0:T(8,128)(2,1)S(1)} %fusion.2), channel_id=1, source_target_pairs={{0,3},{1,2},{2,1},{3,0},{4,7},{5,6},{6,5},{7,4},{8,11},{9,10},{10,... | collective-permute-start | bytes 172040 | tf_op jit(solution)/shard_map/ppermute | solution.py:563
  29.1 2.4 %collective-permute-done.10 = bf16[224,128]{1,0:T(8,128)(2,1)S(1)} collective-permute-done((bf16[224,128]{1,0:T(8,128)(2,1)S(1)}, bf16[224,128]{1,0:T(8,128)(2,1)S(1)}, u32[]{:S(2)}, u32[]{:S(2)}) %collective-permute-start.10) | collective-permute-done | bytes 57376 | tf_op jit(solution)/shard_map/ppermute | solution.py:563
  31.5 1.8 %collective-permute-done.9 = bf16[224,128]{1,0:T(8,128)(2,1)S(1)} collective-permute-done((bf16[224,128]{1,0:T(8,128)(2,1)S(1)}, bf16[224,128]{1,0:T(8,128)(2,1)S(1)}, u32[]{:S(2)}, u32[]{:S(2)}) %collective-permute-start.9) | collective-permute-done | bytes 57376 | tf_op jit(solution)/shard_map/ppermute | solution.py:563
  33.3 0.2 collective-permute-done.8
  33.5 1.8 %collective-permute-start.13 = (bf16[224,128]{1,0:T(8,128)(2,1)S(1)}, bf16[224,128]{1,0:T(8,128)(2,1)S(1)}, u32[]{:S(2)}, u32[]{:S(2)}) collective-permute-start(bf16[224,128]{1,0:T(8,128)(2,1)S(1)} %add_convert_fusion), channel_id=1, source_target_pairs={{0,24},{1,25},{2,26},{3,27},{4,28},{5,29},{6,30},{7,31},{8,16},{9,... | collective-permute-start | bytes 172040 | tf_op jit(solution)/shard_map/ppermute | solution.py:563
  35.3 0.0 collective-permute-start.12
  35.3 1.5 %collective-permute-start.11 = (bf16[224,128]{1,0:T(8,128)(2,1)S(1)}, bf16[224,128]{1,0:T(8,128)(2,1)S(1)}, u32[]{:S(2)}, u32[]{:S(2)}) collective-permute-start(bf16[224,128]{1,0:T(8,128)(2,1)S(1)} %add_convert_fusion), channel_id=1, source_target_pairs={{0,9},{1,8},{2,11},{3,10},{4,13},{5,12},{6,15},{7,14},{8,1},{9,0},... | collective-permute-start | bytes 172040 | tf_op jit(solution)/shard_map/ppermute | solution.py:563
  36.8 0.0 collective-permute-start.14
  36.8 1.9 %collective-permute-done.13 = bf16[224,128]{1,0:T(8,128)(2,1)S(1)} collective-permute-done((bf16[224,128]{1,0:T(8,128)(2,1)S(1)}, bf16[224,128]{1,0:T(8,128)(2,1)S(1)}, u32[]{:S(2)}, u32[]{:S(2)}) %collective-permute-start.13) | collective-permute-done | bytes 57376 | tf_op jit(solution)/shard_map/ppermute | solution.py:563
  38.7 0.0 collective-permute-start.17
  38.7 1.2 %collective-permute-done.12 = bf16[224,128]{1,0:T(8,128)(2,1)S(1)} collective-permute-done((bf16[224,128]{1,0:T(8,128)(2,1)S(1)}, bf16[224,128]{1,0:T(8,128)(2,1)S(1)}, u32[]{:S(2)}, u32[]{:S(2)}) %collective-permute-start.12) | collective-permute-done | bytes 57376 | tf_op jit(solution)/shard_map/ppermute | solution.py:563
  39.9 0.1 collective-permute-start.16
  40.0 0.0 collective-permute-done.11
  40.0 0.4 collective-permute-start.15
  40.4 0.0 collective-permute-done.14
  40.4 0.0 collective-permute-done.17
  40.4 0.7 %collective-permute-done.16 = bf16[224,128]{1,0:T(8,128)(2,1)S(1)} collective-permute-done((bf16[224,128]{1,0:T(8,128)(2,1)S(1)}, bf16[224,128]{1,0:T(8,128)(2,1)S(1)}, u32[]{:S(2)}, u32[]{:S(2)}) %collective-permute-start.16) | collective-permute-done | bytes 57376 | tf_op jit(solution)/shard_map/ppermute | solution.py:595
  41.1 0.2 collective-permute-done.15
  41.3 1.0 %shard_map.82 = (f32[576,128]{1,0:T(8,128)}, f32[1152,128]{1,0:T(8,128)}) custom-call(bf16[4,224,128]{2,1,0:T(8,128)(2,1)S(1)} %pad_maximum_fusion.mine, bf16[4,224,128]{2,1,0:T(8,128)(2,1)S(1)} %pad_maximum_fusion.1.theirs), custom_call_target="tpu_custom_call" | custom-call | flops 1000 | bytes 1572864 | tf_op jit(solution)/shard_map/pallas_call | solution.py:598
  (11 shorter events, 0.2 us)
Async XLA Ops:
  0.6 11.3 %copy-start.3 = (bf16[8,64,128]{2,1,0:T(8,128)(2,1)S(1)}, bf16[8,64,128]{2,1,0:T(8,128)(2,1)}, u32[]{:S(2)}) copy-start(bf16[8,64,128]{2,1,0:T(8,128)(2,1)} %grad_out.1) | copy-start | bytes 393220
  0.6 6.7 %copy-start = (bf16[3,3,128,128]{3,2,1,0:T(8,128)(2,1)S(1)}, bf16[3,3,128,128]{3,2,1,0:T(8,128)(2,1)}, u32[]{:S(2)}) copy-start(bf16[3,3,128,128]{3,2,1,0:T(8,128)(2,1)} %w_second.1) | copy-start | bytes 884740
  0.7 6.7 %copy-start.2 = (bf16[3,3,64,128]{3,2,1,0:T(8,128)(2,1)S(1)}, bf16[3,3,64,128]{3,2,1,0:T(8,128)(2,1)}, u32[]{:S(2)}) copy-start(bf16[3,3,64,128]{3,2,1,0:T(8,128)(2,1)} %w_first.1) | copy-start | bytes 442372
  0.7 6.7 %copy-start.1 = (bf16[16,128,64]{1,2,0:T(8,128)(2,1)S(1)}, bf16[16,128,64]{1,2,0:T(8,128)(2,1)}, u32[]{:S(2)}) copy-start(bf16[16,128,64]{1,2,0:T(8,128)(2,1)} %param.5) | copy-start | bytes 786436
  1.9 6.7 %collective-permute-start = (bf16[192,128]{1,0:T(8,128)(2,1)S(1)}, bf16[192,128]{1,0:T(8,128)(2,1)S(1)}, u32[]{:S(2)}, u32[]{:S(2)}) collective-permute-start(bf16[192,128]{1,0:T(8,128)(2,1)S(1)} %get-tuple-element.41), channel_id=1, source_target_pairs={{0,4},{1,5},{2,6},{3,7},{4,0},{5,1},{6,2},{7,3},{24,28},{25,29},{2... | collective-permute-start | bytes 147464 | tf_op jit(solution)/shard_map/ppermute | solution.py:462
  6.0 4.1 %collective-permute-start.1 = (bf16[192,128]{1,0:T(8,128)(2,1)S(1)}, bf16[192,128]{1,0:T(8,128)(2,1)S(1)}, u32[]{:S(2)}, u32[]{:S(2)}) collective-permute-start(bf16[192,128]{1,0:T(8,128)(2,1)S(1)} %get-tuple-element.42), channel_id=1, source_target_pairs={{0,8},{1,9},{2,10},{3,11},{4,12},{5,13},{6,14},{7,15},{8,0},{9,1},... | collective-permute-start | bytes 147464 | tf_op jit(solution)/shard_map/ppermute | solution.py:463
  10.2 4.9 %collective-permute-start.3 = (bf16[32,128]{1,0:T(8,128)(2,1)S(1)}, bf16[32,128]{1,0:T(8,128)(2,1)S(1)}, u32[]{:S(2)}, u32[]{:S(2)}) collective-permute-start(bf16[32,128]{1,0:T(8,128)(2,1)S(1)} %get-tuple-element.94), channel_id=1, source_target_pairs={{0,7},{1,2},{2,1},{3,4},{4,3},{5,6},{6,5},{7,0},{8,15},{9,10},{10,... | collective-permute-start | bytes 24584 | tf_op jit(solution)/shard_map/ppermute | solution.py:508
  11.0 4.1 %collective-permute-start.2 = (bf16[32,128]{1,0:T(8,128)(2,1)S(1)}, bf16[32,128]{1,0:T(8,128)(2,1)S(1)}, u32[]{:S(2)}, u32[]{:S(2)}) collective-permute-start(bf16[32,128]{1,0:T(8,128)(2,1)S(1)} %get-tuple-element.95), channel_id=1, source_target_pairs={{0,1},{1,0},{2,3},{3,2},{4,5},{5,4},{6,7},{7,6},{8,9},{9,8},{10,11... | collective-permute-start | bytes 24584 | tf_op jit(solution)/shard_map/ppermute | solution.py:509
  16.3 1.9 %collective-permute-start.4 = (f32[896,128]{1,0:T(8,128)S(1)}, f32[896,128]{1,0:T(8,128)S(1)}, u32[]{:S(2)}, u32[]{:S(2)}) collective-permute-start(f32[896,128]{1,0:T(8,128)S(1)} %get-tuple-element.63), channel_id=1, source_target_pairs={{0,1},{1,0},{2,3},{3,2},{4,5},{5,4},{6,7},{7,6},{8,9},{9,8},{10,11... | collective-permute-start | bytes 1376264 | tf_op jit(solution)/shard_map/ppermute | solution.py:566
  18.2 5.4 %collective-permute-start.5 = (bf16[224,128]{1,0:T(8,128)(2,1)S(1)}, bf16[224,128]{1,0:T(8,128)(2,1)S(1)}, u32[]{:S(2)}, u32[]{:S(2)}) collective-permute-start(bf16[224,128]{1,0:T(8,128)(2,1)S(1)} %get-tuple-element.65), channel_id=1, source_target_pairs={{0,24},{1,25},{2,26},{3,27},{4,28},{5,29},{6,30},{7,31},{8,16},{9,... | collective-permute-start | bytes 172040 | tf_op jit(solution)/shard_map/ppermute | solution.py:563
  20.7 4.2 %collective-permute-start.6 = (bf16[224,128]{1,0:T(8,128)(2,1)S(1)}, bf16[224,128]{1,0:T(8,128)(2,1)S(1)}, u32[]{:S(2)}, u32[]{:S(2)}) collective-permute-start(bf16[224,128]{1,0:T(8,128)(2,1)S(1)} %get-tuple-element.66), channel_id=1, source_target_pairs={{0,17},{1,16},{2,19},{3,18},{4,21},{5,20},{6,23},{7,22},{8,25},{9,... | collective-permute-start | bytes 172040 | tf_op jit(solution)/shard_map/ppermute | solution.py:563
  20.8 4.2 %collective-permute-start.7 = (bf16[224,128]{1,0:T(8,128)(2,1)S(1)}, bf16[224,128]{1,0:T(8,128)(2,1)S(1)}, u32[]{:S(2)}, u32[]{:S(2)}) collective-permute-start(bf16[224,128]{1,0:T(8,128)(2,1)S(1)} %get-tuple-element.67), channel_id=1, source_target_pairs={{0,9},{1,8},{2,11},{3,10},{4,13},{5,12},{6,15},{7,14},{8,1},{9,0},... | collective-permute-start | bytes 172040 | tf_op jit(solution)/shard_map/ppermute | solution.py:563
  25.0 6.5 %collective-permute-start.10 = (bf16[224,128]{1,0:T(8,128)(2,1)S(1)}, bf16[224,128]{1,0:T(8,128)(2,1)S(1)}, u32[]{:S(2)}, u32[]{:S(2)}) collective-permute-start(bf16[224,128]{1,0:T(8,128)(2,1)S(1)} %fusion.2), channel_id=1, source_target_pairs={{0,6},{1,7},{2,4},{3,5},{4,2},{5,3},{6,0},{7,1},{8,14},{9,15},{10,... | collective-permute-start | bytes 172040 | tf_op jit(solution)/shard_map/ppermute | solution.py:563
  26.5 6.8 %collective-permute-start.9 = (bf16[224,128]{1,0:T(8,128)(2,1)S(1)}, bf16[224,128]{1,0:T(8,128)(2,1)S(1)}, u32[]{:S(2)}, u32[]{:S(2)}) collective-permute-start(bf16[224,128]{1,0:T(8,128)(2,1)S(1)} %fusion.2), channel_id=1, source_target_pairs={{0,5},{1,4},{2,7},{3,6},{4,1},{5,0},{6,3},{7,2},{8,13},{9,12},{10,... | collective-permute-start | bytes 172040 | tf_op jit(solution)/shard_map/ppermute | solution.py:563
  26.5 6.9 %collective-permute-start.8 = (bf16[224,128]{1,0:T(8,128)(2,1)S(1)}, bf16[224,128]{1,0:T(8,128)(2,1)S(1)}, u32[]{:S(2)}, u32[]{:S(2)}) collective-permute-start(bf16[224,128]{1,0:T(8,128)(2,1)S(1)} %fusion.2), channel_id=1, source_target_pairs={{0,3},{1,2},{2,1},{3,0},{4,7},{5,6},{6,5},{7,4},{8,11},{9,10},{10,... | collective-permute-start | bytes 172040 | tf_op jit(solution)/shard_map/ppermute | solution.py:563
  33.5 5.2 %collective-permute-start.13 = (bf16[224,128]{1,0:T(8,128)(2,1)S(1)}, bf16[224,128]{1,0:T(8,128)(2,1)S(1)}, u32[]{:S(2)}, u32[]{:S(2)}) collective-permute-start(bf16[224,128]{1,0:T(8,128)(2,1)S(1)} %add_convert_fusion), channel_id=1, source_target_pairs={{0,24},{1,25},{2,26},{3,27},{4,28},{5,29},{6,30},{7,31},{8,16},{9,... | collective-permute-start | bytes 172040 | tf_op jit(solution)/shard_map/ppermute | solution.py:563
  35.3 4.6 %collective-permute-start.12 = (bf16[224,128]{1,0:T(8,128)(2,1)S(1)}, bf16[224,128]{1,0:T(8,128)(2,1)S(1)}, u32[]{:S(2)}, u32[]{:S(2)}) collective-permute-start(bf16[224,128]{1,0:T(8,128)(2,1)S(1)} %add_convert_fusion), channel_id=1, source_target_pairs={{0,17},{1,16},{2,19},{3,18},{4,21},{5,20},{6,23},{7,22},{8,25},{9,... | collective-permute-start | bytes 172040 | tf_op jit(solution)/shard_map/ppermute | solution.py:563
  35.3 4.7 %collective-permute-start.11 = (bf16[224,128]{1,0:T(8,128)(2,1)S(1)}, bf16[224,128]{1,0:T(8,128)(2,1)S(1)}, u32[]{:S(2)}, u32[]{:S(2)}) collective-permute-start(bf16[224,128]{1,0:T(8,128)(2,1)S(1)} %add_convert_fusion), channel_id=1, source_target_pairs={{0,9},{1,8},{2,11},{3,10},{4,13},{5,12},{6,15},{7,14},{8,1},{9,0},... | collective-permute-start | bytes 172040 | tf_op jit(solution)/shard_map/ppermute | solution.py:563
  36.8 3.6 %collective-permute-start.14 = (bf16[224,128]{1,0:T(8,128)(2,1)S(1)}, bf16[224,128]{1,0:T(8,128)(2,1)S(1)}, u32[]{:S(2)}, u32[]{:S(2)}) collective-permute-start(bf16[224,128]{1,0:T(8,128)(2,1)S(1)} %add_convert_fusion), channel_id=1, source_target_pairs={{0,1},{1,0},{2,3},{3,2},{4,5},{5,4},{6,7},{7,6},{8,9},{9,8},{10,11... | collective-permute-start | bytes 172040 | tf_op jit(solution)/shard_map/ppermute | solution.py:595
  38.7 1.8 %collective-permute-start.17 = (bf16[224,128]{1,0:T(8,128)(2,1)S(1)}, bf16[224,128]{1,0:T(8,128)(2,1)S(1)}, u32[]{:S(2)}, u32[]{:S(2)}) collective-permute-start(bf16[224,128]{1,0:T(8,128)(2,1)S(1)} %collective-permute-done.13), channel_id=1, source_target_pairs={{0,1},{1,0},{2,3},{3,2},{4,5},{5,4},{6,7},{7,6},{8,9},{9,8},{10,11... | collective-permute-start | bytes 172040 | tf_op jit(solution)/shard_map/ppermute | solution.py:595
  39.9 1.2 %collective-permute-start.16 = (bf16[224,128]{1,0:T(8,128)(2,1)S(1)}, bf16[224,128]{1,0:T(8,128)(2,1)S(1)}, u32[]{:S(2)}, u32[]{:S(2)}) collective-permute-start(bf16[224,128]{1,0:T(8,128)(2,1)S(1)} %collective-permute-done.12), channel_id=1, source_target_pairs={{0,1},{1,0},{2,3},{3,2},{4,5},{5,4},{6,7},{7,6},{8,9},{9,8},{10,11... | collective-permute-start | bytes 172040 | tf_op jit(solution)/shard_map/ppermute | solution.py:595
  40.0 1.3 %collective-permute-start.15 = (bf16[224,128]{1,0:T(8,128)(2,1)S(1)}, bf16[224,128]{1,0:T(8,128)(2,1)S(1)}, u32[]{:S(2)}, u32[]{:S(2)}) collective-permute-start(bf16[224,128]{1,0:T(8,128)(2,1)S(1)} %collective-permute-done.11), channel_id=1, source_target_pairs={{0,1},{1,0},{2,3},{3,2},{4,5},{5,4},{6,7},{7,6},{8,9},{9,8},{10,11... | collective-permute-start | bytes 172040 | tf_op jit(solution)/shard_map/ppermute | solution.py:595

commit v15 on v13

--- a/solution.py
+++ b/solution.py
@@ -560,7 +560,7 @@
     parts = (own + lax.ppermute(other, "lon", swap)).reshape(lats, block, c1)
     sent = [parts[far].astype(BF16) for far in range(1, lats)]
     *sent, ends = lax.optimization_barrier((*sent, ends))
-    got = [between_chips(sent[far - 1], far, 0) for far in reversed(range(1, lats))]
+    got = [between_chips(sent[far - 1], far, 0) for far in range(1, lats)]
     grad_inputs = pl.pallas_call(
         functools.partial(last_kernel, lats),
         out_shape=shape((rows, c0, cols), BF16),
@@ -583,7 +583,7 @@
     terms = [part] + [between_chips(part, 0, far) for far in range(1, depths)]
     terms = [term.astype(F32) for term in terms]
     while len(terms) > 1:
-        terms = [terms[k] + terms[k + 1] for k in range(0, len(terms), 2)]
+        terms = [terms[k + (k > 0)] + terms[k + (k == 0)] for k in range(0, len(terms), 2)]
     part = terms[0].astype(BF16)
     mine = jnp.stack([part] + [between_chips(part, far, 0) for far in range(1, lats)], 0)
     theirs = lax.ppermute(mine, "lon", swap)

time: 42.6 us -> 42.9 us (level)
  waiting for transfers between devices: 14.6 us -> 16 us
  starting transfers between devices: 17.2 us -> 16 us
    ppermute x9, waiting for transfers between devices: 8.66 us -> 10.1 us  [between_chips(): lax.ppermute(value, AREA, [(i * lons + j, (i ^ over_lat) * lons + (j ^ 2...]
    ppermute x9, starting transfers between devices: 10.7 us -> 9.53 us  [between_chips(): lax.ppermute(value, AREA, [(i * lons + j, (i ^ over_lat) * lons + (j ^ 2...]
  transfers between devices with their start and end apart: 15 -> 15, of which waited for: 11 -> 11; matrix products, arithmetic and copies ran while one was open for 0% -> 0% of each run, Pallas kernels for 15% -> 14%
where the time goes in v15:
time: 42.9 us; the launch traced here: 42.7 us
  starting transfers between devices  16 us (37%)
  waiting for transfers between devices  16 us (37%)
  Pallas kernels  9.56 us (22%)
  between operations  0.8 us (2%)
    ppermute x9, waiting for transfers between devices, between_chips(): lax.ppermute(value, AREA, [(i * lons + j, (i ^ over_lat) * lons + (j ^ 2...  10.1 us
    ppermute x9, starting transfers between devices, between_chips(): lax.ppermute(value, AREA, [(i * lons + j, (i ^ over_lat) * lons + (j ^ 2...  9.53 us
    ppermute x1, starting transfers between devices, body(): row_b = lax.ppermute(row_b, AREA, pairs)  4.1 us
    pallas_call x1, Pallas kernels, body(): pl.pallas_call(functools.partial(middle_kernel, lats), out_shape=(shape((...  2.4 us
    pallas_call x1, Pallas kernels, body(): pl.pallas_call(functools.partial(last_kernel, lats), out_shape=shape((row...  2.16 us
    ppermute x1, waiting for transfers between devices, body(): parts = (own + lax.ppermute(other, 'lon', swap)).reshape(lats, block, c1)  1.8 us
    ppermute x1, waiting for transfers between devices, body(): row_a = lax.ppermute(row_a, AREA, every)  1.49 us
    ppermute x1, waiting for transfers between devices, body(): theirs = lax.ppermute(mine, 'lon', swap)  1.37 us
  transfers between devices with their start and end apart: 15, of which 11 were waited for; matrix products, arithmetic and copies ran while one was open for 0% of the time, Pallas kernels for 14%

profile of v15, /device:TPU:0, one launch (start us, length us, event | category | flops | bytes accessed | tf_op | source)
XLA Modules:
  0.0 42.7 jit_solution(1444003523544599932)
XLA Ops:
  0.6 0.0 copy-start.3
  0.6 0.0 copy-start
  0.7 0.0 copy-start.2
  0.7 0.0 copy-start.1
  0.7 1.2 %shard_map.76 = (bf16[192,128]{1,0:T(8,128)(2,1)S(1)}, bf16[192,128]{1,0:T(8,128)(2,1)S(1)}, bf16[32,128]{1,0:T(8,128)(2,1)S(1)}, bf16[32,128]{1,0:T(8,128)(2,1)S(1)}, bf16[16,128,128]{2,1,0:T(8,128)(2,1)S(1)}) custom-call(bf16[16,128,128]{2,1,0:T(8,128)(2,1)} %pre_far.1, bf16[8,64,128]{2,1,0:T(8,128)(2,1)} %grad_out.1), custom_call_target="tpu_custom_call" | custom-call | flops 1000 | bytes 262144 | tf_op jit(solution)/shard_map/pallas_call | solution.py:432
  1.9 4.1 %collective-permute-start = (bf16[192,128]{1,0:T(8,128)(2,1)S(1)}, bf16[192,128]{1,0:T(8,128)(2,1)S(1)}, u32[]{:S(2)}, u32[]{:S(2)}) collective-permute-start(bf16[192,128]{1,0:T(8,128)(2,1)S(1)} %get-tuple-element.41), channel_id=1, source_target_pairs={{0,4},{1,5},{2,6},{3,7},{4,0},{5,1},{6,2},{7,3},{24,28},{25,29},{2... | collective-permute-start | bytes 147464 | tf_op jit(solution)/shard_map/ppermute | solution.py:456
  6.0 0.4 collective-permute-start.1
  6.4 0.1 pad.9.clone
  6.4 0.9 %shard_map.77 = (f32[16,64,256]{2,1,0:T(8,128)S(1)}, bf16[2,256,512]{2,1,0:T(8,128)(2,1)S(1)}, f32[2,16,128]{2,1,0:T(8,128)S(1)}) custom-call(bf16[16,128,128]{2,1,0:T(8,128)(2,1)S(1)} %get-tuple-element.43.pre), custom_call_target="tpu_custom_call" | custom-call | flops 15728640 | bytes 2097152 | tf_op jit(solution)/shard_map/pallas_call | solution.py:459
  7.4 0.0 copy-done
  7.4 0.0 copy-done.2
  7.4 0.0 copy-done.1
  7.4 0.7 %shard_map.78 = (bf16[128,1024]{1,0:T(8,128)(2,1)S(1)}, bf16[128,32]{1,0:T(8,128)(2,1)S(1)}, bf16[384,512]{1,0:T(8,128)(2,1)S(1)}, bf16[3,256,512]{2,1,0:T(8,128)(2,1)S(1)}) custom-call(bf16[16,64,128]{2,1,0:T(8,128)(2,1)S(1)} %bitcast.8, bf16[3,3,64,128]{3,2,1,0:T(8,128)(2,1)S(1)} %copy-done.2, bf16[3,3,128,128]{3,2,1,0:T(8,128)(2,1)S(1)} %copy-done), custom_call_target="tpu_custom_call" | custom-call | flops 67108864 | bytes 3145728 | tf_op jit(solution)/shard_map/pallas_call | solution.py:477
  8.1 0.4 %collective-permute-done.row_b = bf16[192,128]{1,0:T(8,128)(2,1)S(1)} collective-permute-done((bf16[192,128]{1,0:T(8,128)(2,1)S(1)}, bf16[192,128]{1,0:T(8,128)(2,1)S(1)}, u32[]{:S(2)}, u32[]{:S(2)}) %collective-permute-start) | collective-permute-done | bytes 49184 | tf_op jit(solution)/shard_map/ppermute | solution.py:456
  8.6 1.5 %collective-permute-done.1.row_a = bf16[192,128]{1,0:T(8,128)(2,1)S(1)} collective-permute-done((bf16[192,128]{1,0:T(8,128)(2,1)S(1)}, bf16[192,128]{1,0:T(8,128)(2,1)S(1)}, u32[]{:S(2)}, u32[]{:S(2)}) %collective-permute-start.1) | collective-permute-done | bytes 49184 | tf_op jit(solution)/shard_map/ppermute | solution.py:457
  10.1 0.1 maximum_maximum_fusion.1
  10.2 0.8 %collective-permute-start.3 = (bf16[32,128]{1,0:T(8,128)(2,1)S(1)}, bf16[32,128]{1,0:T(8,128)(2,1)S(1)}, u32[]{:S(2)}, u32[]{:S(2)}) collective-permute-start(bf16[32,128]{1,0:T(8,128)(2,1)S(1)} %get-tuple-element.94), channel_id=1, source_target_pairs={{0,7},{1,2},{2,1},{3,4},{4,3},{5,6},{6,5},{7,0},{8,15},{9,10},{10,... | collective-permute-start | bytes 24584 | tf_op jit(solution)/shard_map/ppermute | solution.py:502
  11.0 0.9 %collective-permute-start.2 = (bf16[32,128]{1,0:T(8,128)(2,1)S(1)}, bf16[32,128]{1,0:T(8,128)(2,1)S(1)}, u32[]{:S(2)}, u32[]{:S(2)}) collective-permute-start(bf16[32,128]{1,0:T(8,128)(2,1)S(1)} %get-tuple-element.95), channel_id=1, source_target_pairs={{0,1},{1,0},{2,3},{3,2},{4,5},{5,4},{6,7},{7,6},{8,9},{9,8},{10,11... | collective-permute-start | bytes 24584 | tf_op jit(solution)/shard_map/ppermute | solution.py:503
  11.9 0.0 copy-done.3
  11.9 2.4 %shard_map.79 = (bf16[19,64,512]{2,1,0:T(8,128)(2,1)S(1)}, f32[1792,128]{1,0:T(8,128)S(1)}, f32[2,32,128]{2,1,0:T(8,128)S(1)}, f32[2,32,128]{2,1,0:T(8,128)S(1)}, f32[2,16,128]{2,1,0:T(8,128)S(1)}) custom-call(bf16[8,64,128]{2,1,0:T(8,128)(2,1)S(1)} %copy-done.3, bf16[192,128]{1,0:T(8,128)(2,1)S(1)} %collective-permute-done.1.row_a, ...), custom_call_target="tpu_custom_call" | custom-call | flops 1509949440 | bytes 8388608 | tf_op jit(solution)/shard_map/pallas_call | solution.py:508
  14.3 0.8 %collective-permute-done.3.col_b = bf16[32,128]{1,0:T(8,128)(2,1)S(1)} collective-permute-done((bf16[32,128]{1,0:T(8,128)(2,1)S(1)}, bf16[32,128]{1,0:T(8,128)(2,1)S(1)}, u32[]{:S(2)}, u32[]{:S(2)}) %collective-permute-start.3) | collective-permute-done | bytes 8224 | tf_op jit(solution)/shard_map/ppermute | solution.py:502
  15.1 0.0 collective-permute-done.2.col_a
  15.1 1.2 %shard_map.80 = (bf16[4,32,128]{2,1,0:T(8,128)(2,1)S(1)}, f32[896,128]{1,0:T(8,128)S(1)}, f32[896,128]{1,0:T(8,128)S(1)}) custom-call(bf16[32,128]{1,0:T(8,128)(2,1)S(1)} %collective-permute-done.2.col_a, bf16[32,128]{1,0:T(8,128)(2,1)S(1)} %collective-permute-done.3.col_b, f32[2,16,128]{2,1,0:T(8,128)S(1)} %get-tuple-element.56.act_ends, ...), custom_call_target="tpu_custom_call" | custom-call | flops 268435456 | bytes 3145728 | tf_op jit(solution)/shard_map/pallas_call | solution.py:534
  16.3 0.1 collective-permute-start.4
  16.3 1.8 %collective-permute-done.4 = f32[896,128]{1,0:T(8,128)S(1)} collective-permute-done((f32[896,128]{1,0:T(8,128)S(1)}, f32[896,128]{1,0:T(8,128)S(1)}, u32[]{:S(2)}, u32[]{:S(2)}) %collective-permute-start.4) | collective-permute-done | bytes 458784 | tf_op jit(solution)/shard_map/ppermute | solution.py:560
  18.1 0.1 fusion.3
  18.2 0.2 collective-permute-start.5
  18.4 2.6 %collective-permute-start.6 = (bf16[224,128]{1,0:T(8,128)(2,1)S(1)}, bf16[224,128]{1,0:T(8,128)(2,1)S(1)}, u32[]{:S(2)}, u32[]{:S(2)}) collective-permute-start(bf16[224,128]{1,0:T(8,128)(2,1)S(1)} %get-tuple-element.66), channel_id=1, source_target_pairs={{0,17},{1,16},{2,19},{3,18},{4,21},{5,20},{6,23},{7,22},{8,25},{9,... | collective-permute-start | bytes 172040 | tf_op jit(solution)/shard_map/ppermute | solution.py:557
  21.0 0.5 %collective-permute-start.7 = (bf16[224,128]{1,0:T(8,128)(2,1)S(1)}, bf16[224,128]{1,0:T(8,128)(2,1)S(1)}, u32[]{:S(2)}, u32[]{:S(2)}) collective-permute-start(bf16[224,128]{1,0:T(8,128)(2,1)S(1)} %get-tuple-element.67), channel_id=1, source_target_pairs={{0,24},{1,25},{2,26},{3,27},{4,28},{5,29},{6,30},{7,31},{8,16},{9,... | collective-permute-start | bytes 172040 | tf_op jit(solution)/shard_map/ppermute | solution.py:557
  21.5 2.2 %shard_map.81 = bf16[16,64,128]{2,1,0:T(8,128)(2,1)} custom-call(bf16[19,64,512]{2,1,0:T(8,128)(2,1)S(1)} %get-tuple-element.68.part, bf16[4,32,128]{2,1,0:T(8,128)(2,1)S(1)} %get-tuple-element.69.ends, bf16[384,512]{1,0:T(8,128)(2,1)S(1)} %get-tuple-element.70.taps), custom_call_target="tpu_custom_call" | custom-call | flops 301989888 | bytes 3145728 | tf_op jit(solution)/shard_map/pallas_call | solution.py:564
  23.7 0.0 collective-permute-done.5
  23.7 0.4 collective-permute-done.6
  24.1 2.0 %collective-permute-done.7 = bf16[224,128]{1,0:T(8,128)(2,1)S(1)} collective-permute-done((bf16[224,128]{1,0:T(8,128)(2,1)S(1)}, bf16[224,128]{1,0:T(8,128)(2,1)S(1)}, u32[]{:S(2)}, u32[]{:S(2)}) %collective-permute-start.7) | collective-permute-done | bytes 57376 | tf_op jit(solution)/shard_map/ppermute | solution.py:557
  26.1 0.1 collective-permute-start.10
  26.2 1.6 %collective-permute-start.9 = (bf16[224,128]{1,0:T(8,128)(2,1)S(1)}, bf16[224,128]{1,0:T(8,128)(2,1)S(1)}, u32[]{:S(2)}, u32[]{:S(2)}) collective-permute-start(bf16[224,128]{1,0:T(8,128)(2,1)S(1)} %fusion.2), channel_id=1, source_target_pairs={{0,6},{1,7},{2,4},{3,5},{4,2},{5,3},{6,0},{7,1},{8,14},{9,15},{10,... | collective-permute-start | bytes 172040 | tf_op jit(solution)/shard_map/ppermute | solution.py:557
  27.8 1.4 %collective-permute-start.8 = (bf16[224,128]{1,0:T(8,128)(2,1)S(1)}, bf16[224,128]{1,0:T(8,128)(2,1)S(1)}, u32[]{:S(2)}, u32[]{:S(2)}) collective-permute-start(bf16[224,128]{1,0:T(8,128)(2,1)S(1)} %fusion.2), channel_id=1, source_target_pairs={{0,3},{1,2},{2,1},{3,0},{4,7},{5,6},{6,5},{7,4},{8,11},{9,10},{10,... | collective-permute-start | bytes 172040 | tf_op jit(solution)/shard_map/ppermute | solution.py:557
  29.1 3.9 %collective-permute-done.10 = bf16[224,128]{1,0:T(8,128)(2,1)S(1)} collective-permute-done((bf16[224,128]{1,0:T(8,128)(2,1)S(1)}, bf16[224,128]{1,0:T(8,128)(2,1)S(1)}, u32[]{:S(2)}, u32[]{:S(2)}) %collective-permute-start.10) | collective-permute-done | bytes 57376 | tf_op jit(solution)/shard_map/ppermute | solution.py:557
  33.1 0.0 collective-permute-done.9
  33.1 1.0 %collective-permute-done.8 = bf16[224,128]{1,0:T(8,128)(2,1)S(1)} collective-permute-done((bf16[224,128]{1,0:T(8,128)(2,1)S(1)}, bf16[224,128]{1,0:T(8,128)(2,1)S(1)}, u32[]{:S(2)}, u32[]{:S(2)}) %collective-permute-start.8) | collective-permute-done | bytes 57376 | tf_op jit(solution)/shard_map/ppermute | solution.py:557
  34.1 0.5 %collective-permute-start.13 = (bf16[224,128]{1,0:T(8,128)(2,1)S(1)}, bf16[224,128]{1,0:T(8,128)(2,1)S(1)}, u32[]{:S(2)}, u32[]{:S(2)}) collective-permute-start(bf16[224,128]{1,0:T(8,128)(2,1)S(1)} %add_convert_fusion), channel_id=1, source_target_pairs={{0,24},{1,25},{2,26},{3,27},{4,28},{5,29},{6,30},{7,31},{8,16},{9,... | collective-permute-start | bytes 172040 | tf_op jit(solution)/shard_map/ppermute | solution.py:557
  34.7 0.5 %collective-permute-start.12 = (bf16[224,128]{1,0:T(8,128)(2,1)S(1)}, bf16[224,128]{1,0:T(8,128)(2,1)S(1)}, u32[]{:S(2)}, u32[]{:S(2)}) collective-permute-start(bf16[224,128]{1,0:T(8,128)(2,1)S(1)} %add_convert_fusion), channel_id=1, source_target_pairs={{0,17},{1,16},{2,19},{3,18},{4,21},{5,20},{6,23},{7,22},{8,25},{9,... | collective-permute-start | bytes 172040 | tf_op jit(solution)/shard_map/ppermute | solution.py:557
  35.2 2.2 %collective-permute-start.11 = (bf16[224,128]{1,0:T(8,128)(2,1)S(1)}, bf16[224,128]{1,0:T(8,128)(2,1)S(1)}, u32[]{:S(2)}, u32[]{:S(2)}) collective-permute-start(bf16[224,128]{1,0:T(8,128)(2,1)S(1)} %add_convert_fusion), channel_id=1, source_target_pairs={{0,9},{1,8},{2,11},{3,10},{4,13},{5,12},{6,15},{7,14},{8,1},{9,0},... | collective-permute-start | bytes 172040 | tf_op jit(solution)/shard_map/ppermute | solution.py:557
  37.4 2.4 %collective-permute-done.13 = bf16[224,128]{1,0:T(8,128)(2,1)S(1)} collective-permute-done((bf16[224,128]{1,0:T(8,128)(2,1)S(1)}, bf16[224,128]{1,0:T(8,128)(2,1)S(1)}, u32[]{:S(2)}, u32[]{:S(2)}) %collective-permute-start.13) | collective-permute-done | bytes 57376 | tf_op jit(solution)/shard_map/ppermute | solution.py:557
  39.8 0.3 collective-permute-done.12
  40.1 0.0 collective-permute-done.11
  40.2 0.2 collective-permute-start.14
  40.3 1.4 %collective-permute-done.14.theirs = bf16[4,224,128]{2,1,0:T(8,128)(2,1)S(1)} collective-permute-done((bf16[4,224,128]{2,1,0:T(8,128)(2,1)S(1)}, bf16[4,224,128]{2,1,0:T(8,128)(2,1)S(1)}, u32[]{:S(2)}, u32[]{:S(2)}) %collective-permute-start.14) | collective-permute-done | bytes 229408 | tf_op jit(solution)/shard_map/ppermute | solution.py:589
  41.7 1.0 %shard_map.82 = (f32[576,128]{1,0:T(8,128)}, f32[1152,128]{1,0:T(8,128)}) custom-call(bf16[4,224,128]{2,1,0:T(8,128)(2,1)S(1)} %pad_maximum_fusion.mine, bf16[4,224,128]{2,1,0:T(8,128)(2,1)S(1)} %collective-permute-done.14.theirs), custom_call_target="tpu_custom_call" | custom-call | flops 1000 | bytes 1572864 | tf_op jit(solution)/shard_map/pallas_call | solution.py:591
  (10 shorter events, 0.2 us)
Async XLA Ops:
  0.6 11.3 %copy-start.3 = (bf16[8,64,128]{2,1,0:T(8,128)(2,1)S(1)}, bf16[8,64,128]{2,1,0:T(8,128)(2,1)}, u32[]{:S(2)}) copy-start(bf16[8,64,128]{2,1,0:T(8,128)(2,1)} %grad_out.1) | copy-start | bytes 393220
  0.6 6.7 %copy-start = (bf16[3,3,128,128]{3,2,1,0:T(8,128)(2,1)S(1)}, bf16[3,3,128,128]{3,2,1,0:T(8,128)(2,1)}, u32[]{:S(2)}) copy-start(bf16[3,3,128,128]{3,2,1,0:T(8,128)(2,1)} %w_second.1) | copy-start | bytes 884740
  0.7 6.7 %copy-start.2 = (bf16[3,3,64,128]{3,2,1,0:T(8,128)(2,1)S(1)}, bf16[3,3,64,128]{3,2,1,0:T(8,128)(2,1)}, u32[]{:S(2)}) copy-start(bf16[3,3,64,128]{3,2,1,0:T(8,128)(2,1)} %w_first.1) | copy-start | bytes 442372
  0.7 6.7 %copy-start.1 = (bf16[16,128,64]{1,2,0:T(8,128)(2,1)S(1)}, bf16[16,128,64]{1,2,0:T(8,128)(2,1)}, u32[]{:S(2)}) copy-start(bf16[16,128,64]{1,2,0:T(8,128)(2,1)} %param.5) | copy-start | bytes 786436
  1.9 6.7 %collective-permute-start = (bf16[192,128]{1,0:T(8,128)(2,1)S(1)}, bf16[192,128]{1,0:T(8,128)(2,1)S(1)}, u32[]{:S(2)}, u32[]{:S(2)}) collective-permute-start(bf16[192,128]{1,0:T(8,128)(2,1)S(1)} %get-tuple-element.41), channel_id=1, source_target_pairs={{0,4},{1,5},{2,6},{3,7},{4,0},{5,1},{6,2},{7,3},{24,28},{25,29},{2... | collective-permute-start | bytes 147464 | tf_op jit(solution)/shard_map/ppermute | solution.py:456
  6.0 4.1 %collective-permute-start.1 = (bf16[192,128]{1,0:T(8,128)(2,1)S(1)}, bf16[192,128]{1,0:T(8,128)(2,1)S(1)}, u32[]{:S(2)}, u32[]{:S(2)}) collective-permute-start(bf16[192,128]{1,0:T(8,128)(2,1)S(1)} %get-tuple-element.42), channel_id=1, source_target_pairs={{0,8},{1,9},{2,10},{3,11},{4,12},{5,13},{6,14},{7,15},{8,0},{9,1},... | collective-permute-start | bytes 147464 | tf_op jit(solution)/shard_map/ppermute | solution.py:457
  10.2 4.9 %collective-permute-start.3 = (bf16[32,128]{1,0:T(8,128)(2,1)S(1)}, bf16[32,128]{1,0:T(8,128)(2,1)S(1)}, u32[]{:S(2)}, u32[]{:S(2)}) collective-permute-start(bf16[32,128]{1,0:T(8,128)(2,1)S(1)} %get-tuple-element.94), channel_id=1, source_target_pairs={{0,7},{1,2},{2,1},{3,4},{4,3},{5,6},{6,5},{7,0},{8,15},{9,10},{10,... | collective-permute-start | bytes 24584 | tf_op jit(solution)/shard_map/ppermute | solution.py:502
  11.0 4.1 %collective-permute-start.2 = (bf16[32,128]{1,0:T(8,128)(2,1)S(1)}, bf16[32,128]{1,0:T(8,128)(2,1)S(1)}, u32[]{:S(2)}, u32[]{:S(2)}) collective-permute-start(bf16[32,128]{1,0:T(8,128)(2,1)S(1)} %get-tuple-element.95), channel_id=1, source_target_pairs={{0,1},{1,0},{2,3},{3,2},{4,5},{5,4},{6,7},{7,6},{8,9},{9,8},{10,11... | collective-permute-start | bytes 24584 | tf_op jit(solution)/shard_map/ppermute | solution.py:503
  16.3 1.9 %collective-permute-start.4 = (f32[896,128]{1,0:T(8,128)S(1)}, f32[896,128]{1,0:T(8,128)S(1)}, u32[]{:S(2)}, u32[]{:S(2)}) collective-permute-start(f32[896,128]{1,0:T(8,128)S(1)} %get-tuple-element.63), channel_id=1, source_target_pairs={{0,1},{1,0},{2,3},{3,2},{4,5},{5,4},{6,7},{7,6},{8,9},{9,8},{10,11... | collective-permute-start | bytes 1376264 | tf_op jit(solution)/shard_map/ppermute | solution.py:560
  18.2 5.4 %collective-permute-start.5 = (bf16[224,128]{1,0:T(8,128)(2,1)S(1)}, bf16[224,128]{1,0:T(8,128)(2,1)S(1)}, u32[]{:S(2)}, u32[]{:S(2)}) collective-permute-start(bf16[224,128]{1,0:T(8,128)(2,1)S(1)} %get-tuple-element.65), channel_id=1, source_target_pairs={{0,9},{1,8},{2,11},{3,10},{4,13},{5,12},{6,15},{7,14},{8,1},{9,0},... | collective-permute-start | bytes 172040 | tf_op jit(solution)/shard_map/ppermute | solution.py:557
  18.4 5.6 %collective-permute-start.6 = (bf16[224,128]{1,0:T(8,128)(2,1)S(1)}, bf16[224,128]{1,0:T(8,128)(2,1)S(1)}, u32[]{:S(2)}, u32[]{:S(2)}) collective-permute-start(bf16[224,128]{1,0:T(8,128)(2,1)S(1)} %get-tuple-element.66), channel_id=1, source_target_pairs={{0,17},{1,16},{2,19},{3,18},{4,21},{5,20},{6,23},{7,22},{8,25},{9,... | collective-permute-start | bytes 172040 | tf_op jit(solution)/shard_map/ppermute | solution.py:557
  21.0 5.1 %collective-permute-start.7 = (bf16[224,128]{1,0:T(8,128)(2,1)S(1)}, bf16[224,128]{1,0:T(8,128)(2,1)S(1)}, u32[]{:S(2)}, u32[]{:S(2)}) collective-permute-start(bf16[224,128]{1,0:T(8,128)(2,1)S(1)} %get-tuple-element.67), channel_id=1, source_target_pairs={{0,24},{1,25},{2,26},{3,27},{4,28},{5,29},{6,30},{7,31},{8,16},{9,... | collective-permute-start | bytes 172040 | tf_op jit(solution)/shard_map/ppermute | solution.py:557
  26.1 6.9 %collective-permute-start.10 = (bf16[224,128]{1,0:T(8,128)(2,1)S(1)}, bf16[224,128]{1,0:T(8,128)(2,1)S(1)}, u32[]{:S(2)}, u32[]{:S(2)}) collective-permute-start(bf16[224,128]{1,0:T(8,128)(2,1)S(1)} %fusion.2), channel_id=1, source_target_pairs={{0,5},{1,4},{2,7},{3,6},{4,1},{5,0},{6,3},{7,2},{8,13},{9,12},{10,... | collective-permute-start | bytes 172040 | tf_op jit(solution)/shard_map/ppermute | solution.py:557
  26.2 6.8 %collective-permute-start.9 = (bf16[224,128]{1,0:T(8,128)(2,1)S(1)}, bf16[224,128]{1,0:T(8,128)(2,1)S(1)}, u32[]{:S(2)}, u32[]{:S(2)}) collective-permute-start(bf16[224,128]{1,0:T(8,128)(2,1)S(1)} %fusion.2), channel_id=1, source_target_pairs={{0,6},{1,7},{2,4},{3,5},{4,2},{5,3},{6,0},{7,1},{8,14},{9,15},{10,... | collective-permute-start | bytes 172040 | tf_op jit(solution)/shard_map/ppermute | solution.py:557
  27.8 6.3 %collective-permute-start.8 = (bf16[224,128]{1,0:T(8,128)(2,1)S(1)}, bf16[224,128]{1,0:T(8,128)(2,1)S(1)}, u32[]{:S(2)}, u32[]{:S(2)}) collective-permute-start(bf16[224,128]{1,0:T(8,128)(2,1)S(1)} %fusion.2), channel_id=1, source_target_pairs={{0,3},{1,2},{2,1},{3,0},{4,7},{5,6},{6,5},{7,4},{8,11},{9,10},{10,... | collective-permute-start | bytes 172040 | tf_op jit(solution)/shard_map/ppermute | solution.py:557
  34.1 5.7 %collective-permute-start.13 = (bf16[224,128]{1,0:T(8,128)(2,1)S(1)}, bf16[224,128]{1,0:T(8,128)(2,1)S(1)}, u32[]{:S(2)}, u32[]{:S(2)}) collective-permute-start(bf16[224,128]{1,0:T(8,128)(2,1)S(1)} %add_convert_fusion), channel_id=1, source_target_pairs={{0,24},{1,25},{2,26},{3,27},{4,28},{5,29},{6,30},{7,31},{8,16},{9,... | collective-permute-start | bytes 172040 | tf_op jit(solution)/shard_map/ppermute | solution.py:557
  34.7 5.4 %collective-permute-start.12 = (bf16[224,128]{1,0:T(8,128)(2,1)S(1)}, bf16[224,128]{1,0:T(8,128)(2,1)S(1)}, u32[]{:S(2)}, u32[]{:S(2)}) collective-permute-start(bf16[224,128]{1,0:T(8,128)(2,1)S(1)} %add_convert_fusion), channel_id=1, source_target_pairs={{0,17},{1,16},{2,19},{3,18},{4,21},{5,20},{6,23},{7,22},{8,25},{9,... | collective-permute-start | bytes 172040 | tf_op jit(solution)/shard_map/ppermute | solution.py:557
  35.2 4.9 %collective-permute-start.11 = (bf16[224,128]{1,0:T(8,128)(2,1)S(1)}, bf16[224,128]{1,0:T(8,128)(2,1)S(1)}, u32[]{:S(2)}, u32[]{:S(2)}) collective-permute-start(bf16[224,128]{1,0:T(8,128)(2,1)S(1)} %add_convert_fusion), channel_id=1, source_target_pairs={{0,9},{1,8},{2,11},{3,10},{4,13},{5,12},{6,15},{7,14},{8,1},{9,0},... | collective-permute-start | bytes 172040 | tf_op jit(solution)/shard_map/ppermute | solution.py:557
  40.2 1.6 %collective-permute-start.14 = (bf16[4,224,128]{2,1,0:T(8,128)(2,1)S(1)}, bf16[4,224,128]{2,1,0:T(8,128)(2,1)S(1)}, u32[]{:S(2)}, u32[]{:S(2)}) collective-permute-start(bf16[4,224,128]{2,1,0:T(8,128)(2,1)S(1)} %pad_maximum_fusion.mine), channel_id=1, source_target_pairs={{0,1},{1,0},{2,3},{3,2},{4,5},{5,4},{6,7},{7,6},{8,9},{9,8},{10,11... | collective-permute-start | bytes 688136 | tf_op jit(solution)/shard_map/ppermute | solution.py:589

commit v16 on v15

--- a/solution.py
+++ b/solution.py
@@ -560,7 +560,7 @@
     parts = (own + lax.ppermute(other, "lon", swap)).reshape(lats, block, c1)
     sent = [parts[far].astype(BF16) for far in range(1, lats)]
     *sent, ends = lax.optimization_barrier((*sent, ends))
-    got = [between_chips(sent[far - 1], far, 0) for far in range(1, lats)]
+    got = [between_chips(sent[far - 1], far, 0) for far in reversed(range(1, lats))]
     grad_inputs = pl.pallas_call(
         functools.partial(last_kernel, lats),
         out_shape=shape((rows, c0, cols), BF16),

time: 42.9 us -> 42.2 us (0.984)
  waiting for transfers between devices: 16 us -> 15.3 us
    ppermute x9, waiting for transfers between devices: 10.1 us -> 9.42 us  [between_chips(): lax.ppermute(value, AREA, [(i * lons + j, (i ^ over_lat) * lons + (j ^ 2...]
  transfers between devices with their start and end apart: 15 -> 15, of which waited for: 11 -> 11; matrix products, arithmetic and copies ran while one was open for 0% -> 0% of each run, Pallas kernels for 14% -> 15%
where the time goes in v16:
time: 42.2 us; the launch traced here: 42 us
  starting transfers between devices  16 us (38%)
  waiting for transfers between devices  15.3 us (36%)
  Pallas kernels  9.56 us (23%)
  between operations  0.79 us (2%)
    ppermute x9, starting transfers between devices, between_chips(): lax.ppermute(value, AREA, [(i * lons + j, (i ^ over_lat) * lons + (j ^ 2...  9.54 us
    ppermute x9, waiting for transfers between devices, between_chips(): lax.ppermute(value, AREA, [(i * lons + j, (i ^ over_lat) * lons + (j ^ 2...  9.42 us
    ppermute x1, starting transfers between devices, body(): row_b = lax.ppermute(row_b, AREA, pairs)  4.1 us
    pallas_call x1, Pallas kernels, body(): pl.pallas_call(functools.partial(middle_kernel, lats), out_shape=(shape((...  2.4 us
    pallas_call x1, Pallas kernels, body(): pl.pallas_call(functools.partial(last_kernel, lats), out_shape=shape((row...  2.16 us
    ppermute x1, waiting for transfers between devices, body(): parts = (own + lax.ppermute(other, 'lon', swap)).reshape(lats, block, c1)  1.8 us
    ppermute x1, waiting for transfers between devices, body(): row_a = lax.ppermute(row_a, AREA, every)  1.49 us
    ppermute x1, waiting for transfers between devices, body(): theirs = lax.ppermute(mine, 'lon', swap)  1.38 us
  transfers between devices with their start and end apart: 15, of which 11 were waited for; matrix products, arithmetic and copies ran while one was open for 0% of the time, Pallas kernels for 15%

profile of v16, /device:TPU:0, one launch (start us, length us, event | category | flops | bytes accessed | tf_op | source)
XLA Modules:
  0.0 42.0 jit_solution(7693458741460852720)
XLA Ops:
  0.6 0.0 copy-start.3
  0.6 0.0 copy-start
  0.7 0.0 copy-start.2
  0.7 0.0 copy-start.1
  0.7 1.2 %shard_map.76 = (bf16[192,128]{1,0:T(8,128)(2,1)S(1)}, bf16[192,128]{1,0:T(8,128)(2,1)S(1)}, bf16[32,128]{1,0:T(8,128)(2,1)S(1)}, bf16[32,128]{1,0:T(8,128)(2,1)S(1)}, bf16[16,128,128]{2,1,0:T(8,128)(2,1)S(1)}) custom-call(bf16[16,128,128]{2,1,0:T(8,128)(2,1)} %pre_far.1, bf16[8,64,128]{2,1,0:T(8,128)(2,1)} %grad_out.1), custom_call_target="tpu_custom_call" | custom-call | flops 1000 | bytes 262144 | tf_op jit(solution)/shard_map/pallas_call | solution.py:432
  1.9 4.1 %collective-permute-start = (bf16[192,128]{1,0:T(8,128)(2,1)S(1)}, bf16[192,128]{1,0:T(8,128)(2,1)S(1)}, u32[]{:S(2)}, u32[]{:S(2)}) collective-permute-start(bf16[192,128]{1,0:T(8,128)(2,1)S(1)} %get-tuple-element.41), channel_id=1, source_target_pairs={{0,4},{1,5},{2,6},{3,7},{4,0},{5,1},{6,2},{7,3},{24,28},{25,29},{2... | collective-permute-start | bytes 147464 | tf_op jit(solution)/shard_map/ppermute | solution.py:456
  6.0 0.4 collective-permute-start.1
  6.4 0.1 pad.9.clone
  6.4 0.9 %shard_map.77 = (f32[16,64,256]{2,1,0:T(8,128)S(1)}, bf16[2,256,512]{2,1,0:T(8,128)(2,1)S(1)}, f32[2,16,128]{2,1,0:T(8,128)S(1)}) custom-call(bf16[16,128,128]{2,1,0:T(8,128)(2,1)S(1)} %get-tuple-element.43.pre), custom_call_target="tpu_custom_call" | custom-call | flops 15728640 | bytes 2097152 | tf_op jit(solution)/shard_map/pallas_call | solution.py:459
  7.4 0.0 copy-done
  7.4 0.0 copy-done.2
  7.4 0.0 copy-done.1
  7.4 0.7 %shard_map.78 = (bf16[128,1024]{1,0:T(8,128)(2,1)S(1)}, bf16[128,32]{1,0:T(8,128)(2,1)S(1)}, bf16[384,512]{1,0:T(8,128)(2,1)S(1)}, bf16[3,256,512]{2,1,0:T(8,128)(2,1)S(1)}) custom-call(bf16[16,64,128]{2,1,0:T(8,128)(2,1)S(1)} %bitcast.8, bf16[3,3,64,128]{3,2,1,0:T(8,128)(2,1)S(1)} %copy-done.2, bf16[3,3,128,128]{3,2,1,0:T(8,128)(2,1)S(1)} %copy-done), custom_call_target="tpu_custom_call" | custom-call | flops 67108864 | bytes 3145728 | tf_op jit(solution)/shard_map/pallas_call | solution.py:477
  8.1 0.4 %collective-permute-done.row_b = bf16[192,128]{1,0:T(8,128)(2,1)S(1)} collective-permute-done((bf16[192,128]{1,0:T(8,128)(2,1)S(1)}, bf16[192,128]{1,0:T(8,128)(2,1)S(1)}, u32[]{:S(2)}, u32[]{:S(2)}) %collective-permute-start) | collective-permute-done | bytes 49184 | tf_op jit(solution)/shard_map/ppermute | solution.py:456
  8.6 1.5 %collective-permute-done.1.row_a = bf16[192,128]{1,0:T(8,128)(2,1)S(1)} collective-permute-done((bf16[192,128]{1,0:T(8,128)(2,1)S(1)}, bf16[192,128]{1,0:T(8,128)(2,1)S(1)}, u32[]{:S(2)}, u32[]{:S(2)}) %collective-permute-start.1) | collective-permute-done | bytes 49184 | tf_op jit(solution)/shard_map/ppermute | solution.py:457
  10.1 0.1 maximum_maximum_fusion.1
  10.2 0.8 %collective-permute-start.3 = (bf16[32,128]{1,0:T(8,128)(2,1)S(1)}, bf16[32,128]{1,0:T(8,128)(2,1)S(1)}, u32[]{:S(2)}, u32[]{:S(2)}) collective-permute-start(bf16[32,128]{1,0:T(8,128)(2,1)S(1)} %get-tuple-element.94), channel_id=1, source_target_pairs={{0,7},{1,2},{2,1},{3,4},{4,3},{5,6},{6,5},{7,0},{8,15},{9,10},{10,... | collective-permute-start | bytes 24584 | tf_op jit(solution)/shard_map/ppermute | solution.py:502
  11.0 0.9 %collective-permute-start.2 = (bf16[32,128]{1,0:T(8,128)(2,1)S(1)}, bf16[32,128]{1,0:T(8,128)(2,1)S(1)}, u32[]{:S(2)}, u32[]{:S(2)}) collective-permute-start(bf16[32,128]{1,0:T(8,128)(2,1)S(1)} %get-tuple-element.95), channel_id=1, source_target_pairs={{0,1},{1,0},{2,3},{3,2},{4,5},{5,4},{6,7},{7,6},{8,9},{9,8},{10,11... | collective-permute-start | bytes 24584 | tf_op jit(solution)/shard_map/ppermute | solution.py:503
  11.9 0.0 copy-done.3
  11.9 2.4 %shard_map.79 = (bf16[19,64,512]{2,1,0:T(8,128)(2,1)S(1)}, f32[1792,128]{1,0:T(8,128)S(1)}, f32[2,32,128]{2,1,0:T(8,128)S(1)}, f32[2,32,128]{2,1,0:T(8,128)S(1)}, f32[2,16,128]{2,1,0:T(8,128)S(1)}) custom-call(bf16[8,64,128]{2,1,0:T(8,128)(2,1)S(1)} %copy-done.3, bf16[192,128]{1,0:T(8,128)(2,1)S(1)} %collective-permute-done.1.row_a, ...), custom_call_target="tpu_custom_call" | custom-call | flops 1509949440 | bytes 8388608 | tf_op jit(solution)/shard_map/pallas_call | solution.py:508
  14.3 0.8 %collective-permute-done.3.col_b = bf16[32,128]{1,0:T(8,128)(2,1)S(1)} collective-permute-done((bf16[32,128]{1,0:T(8,128)(2,1)S(1)}, bf16[32,128]{1,0:T(8,128)(2,1)S(1)}, u32[]{:S(2)}, u32[]{:S(2)}) %collective-permute-start.3) | collective-permute-done | bytes 8224 | tf_op jit(solution)/shard_map/ppermute | solution.py:502
  15.1 0.0 collective-permute-done.2.col_a
  15.1 1.2 %shard_map.80 = (bf16[4,32,128]{2,1,0:T(8,128)(2,1)S(1)}, f32[896,128]{1,0:T(8,128)S(1)}, f32[896,128]{1,0:T(8,128)S(1)}) custom-call(bf16[32,128]{1,0:T(8,128)(2,1)S(1)} %collective-permute-done.2.col_a, bf16[32,128]{1,0:T(8,128)(2,1)S(1)} %collective-permute-done.3.col_b, f32[2,16,128]{2,1,0:T(8,128)S(1)} %get-tuple-element.56.act_ends, ...), custom_call_target="tpu_custom_call" | custom-call | flops 268435456 | bytes 3145728 | tf_op jit(solution)/shard_map/pallas_call | solution.py:534
  16.3 0.1 collective-permute-start.4
  16.3 1.8 %collective-permute-done.4 = f32[896,128]{1,0:T(8,128)S(1)} collective-permute-done((f32[896,128]{1,0:T(8,128)S(1)}, f32[896,128]{1,0:T(8,128)S(1)}, u32[]{:S(2)}, u32[]{:S(2)}) %collective-permute-start.4) | collective-permute-done | bytes 458784 | tf_op jit(solution)/shard_map/ppermute | solution.py:560
  18.1 0.1 fusion.3
  18.2 2.5 %collective-permute-start.5 = (bf16[224,128]{1,0:T(8,128)(2,1)S(1)}, bf16[224,128]{1,0:T(8,128)(2,1)S(1)}, u32[]{:S(2)}, u32[]{:S(2)}) collective-permute-start(bf16[224,128]{1,0:T(8,128)(2,1)S(1)} %get-tuple-element.65), channel_id=1, source_target_pairs={{0,24},{1,25},{2,26},{3,27},{4,28},{5,29},{6,30},{7,31},{8,16},{9,... | collective-permute-start | bytes 172040 | tf_op jit(solution)/shard_map/ppermute | solution.py:557
  20.7 0.0 collective-permute-start.6
  20.8 0.8 %collective-permute-start.7 = (bf16[224,128]{1,0:T(8,128)(2,1)S(1)}, bf16[224,128]{1,0:T(8,128)(2,1)S(1)}, u32[]{:S(2)}, u32[]{:S(2)}) collective-permute-start(bf16[224,128]{1,0:T(8,128)(2,1)S(1)} %get-tuple-element.67), channel_id=1, source_target_pairs={{0,9},{1,8},{2,11},{3,10},{4,13},{5,12},{6,15},{7,14},{8,1},{9,0},... | collective-permute-start | bytes 172040 | tf_op jit(solution)/shard_map/ppermute | solution.py:557
  21.5 2.2 %shard_map.81 = bf16[16,64,128]{2,1,0:T(8,128)(2,1)} custom-call(bf16[19,64,512]{2,1,0:T(8,128)(2,1)S(1)} %get-tuple-element.68.part, bf16[4,32,128]{2,1,0:T(8,128)(2,1)S(1)} %get-tuple-element.69.ends, bf16[384,512]{1,0:T(8,128)(2,1)S(1)} %get-tuple-element.70.taps), custom_call_target="tpu_custom_call" | custom-call | flops 301989888 | bytes 3145728 | tf_op jit(solution)/shard_map/pallas_call | solution.py:564
  23.7 0.0 collective-permute-done.5
  23.7 1.3 %collective-permute-done.6 = bf16[224,128]{1,0:T(8,128)(2,1)S(1)} collective-permute-done((bf16[224,128]{1,0:T(8,128)(2,1)S(1)}, bf16[224,128]{1,0:T(8,128)(2,1)S(1)}, u32[]{:S(2)}, u32[]{:S(2)}) %collective-permute-start.6) | collective-permute-done | bytes 57376 | tf_op jit(solution)/shard_map/ppermute | solution.py:557
  24.9 0.0 collective-permute-done.7
  25.0 0.5 %collective-permute-start.10 = (bf16[224,128]{1,0:T(8,128)(2,1)S(1)}, bf16[224,128]{1,0:T(8,128)(2,1)S(1)}, u32[]{:S(2)}, u32[]{:S(2)}) collective-permute-start(bf16[224,128]{1,0:T(8,128)(2,1)S(1)} %fusion.2), channel_id=1, source_target_pairs={{0,5},{1,4},{2,7},{3,6},{4,1},{5,0},{6,3},{7,2},{8,13},{9,12},{10,... | collective-permute-start | bytes 172040 | tf_op jit(solution)/shard_map/ppermute | solution.py:557
  25.4 1.5 %collective-permute-start.9 = (bf16[224,128]{1,0:T(8,128)(2,1)S(1)}, bf16[224,128]{1,0:T(8,128)(2,1)S(1)}, u32[]{:S(2)}, u32[]{:S(2)}) collective-permute-start(bf16[224,128]{1,0:T(8,128)(2,1)S(1)} %fusion.2), channel_id=1, source_target_pairs={{0,6},{1,7},{2,4},{3,5},{4,2},{5,3},{6,0},{7,1},{8,14},{9,15},{10,... | collective-permute-start | bytes 172040 | tf_op jit(solution)/shard_map/ppermute | solution.py:557
  26.9 1.1 %collective-permute-start.8 = (bf16[224,128]{1,0:T(8,128)(2,1)S(1)}, bf16[224,128]{1,0:T(8,128)(2,1)S(1)}, u32[]{:S(2)}, u32[]{:S(2)}) collective-permute-start(bf16[224,128]{1,0:T(8,128)(2,1)S(1)} %fusion.2), channel_id=1, source_target_pairs={{0,3},{1,2},{2,1},{3,0},{4,7},{5,6},{6,5},{7,4},{8,11},{9,10},{10,... | collective-permute-start | bytes 172040 | tf_op jit(solution)/shard_map/ppermute | solution.py:557
  28.0 3.7 %collective-permute-done.10 = bf16[224,128]{1,0:T(8,128)(2,1)S(1)} collective-permute-done((bf16[224,128]{1,0:T(8,128)(2,1)S(1)}, bf16[224,128]{1,0:T(8,128)(2,1)S(1)}, u32[]{:S(2)}, u32[]{:S(2)}) %collective-permute-start.10) | collective-permute-done | bytes 57376 | tf_op jit(solution)/shard_map/ppermute | solution.py:557
  31.7 0.3 collective-permute-done.9
  32.0 1.1 %collective-permute-done.8 = bf16[224,128]{1,0:T(8,128)(2,1)S(1)} collective-permute-done((bf16[224,128]{1,0:T(8,128)(2,1)S(1)}, bf16[224,128]{1,0:T(8,128)(2,1)S(1)}, u32[]{:S(2)}, u32[]{:S(2)}) %collective-permute-start.8) | collective-permute-done | bytes 57376 | tf_op jit(solution)/shard_map/ppermute | solution.py:557
  33.1 1.8 %collective-permute-start.13 = (bf16[224,128]{1,0:T(8,128)(2,1)S(1)}, bf16[224,128]{1,0:T(8,128)(2,1)S(1)}, u32[]{:S(2)}, u32[]{:S(2)}) collective-permute-start(bf16[224,128]{1,0:T(8,128)(2,1)S(1)} %add_convert_fusion), channel_id=1, source_target_pairs={{0,24},{1,25},{2,26},{3,27},{4,28},{5,29},{6,30},{7,31},{8,16},{9,... | collective-permute-start | bytes 172040 | tf_op jit(solution)/shard_map/ppermute | solution.py:557
  34.8 0.2 collective-permute-start.12
  35.1 1.3 %collective-permute-start.11 = (bf16[224,128]{1,0:T(8,128)(2,1)S(1)}, bf16[224,128]{1,0:T(8,128)(2,1)S(1)}, u32[]{:S(2)}, u32[]{:S(2)}) collective-permute-start(bf16[224,128]{1,0:T(8,128)(2,1)S(1)} %add_convert_fusion), channel_id=1, source_target_pairs={{0,9},{1,8},{2,11},{3,10},{4,13},{5,12},{6,15},{7,14},{8,1},{9,0},... | collective-permute-start | bytes 172040 | tf_op jit(solution)/shard_map/ppermute | solution.py:557
  36.3 1.9 %collective-permute-done.13 = bf16[224,128]{1,0:T(8,128)(2,1)S(1)} collective-permute-done((bf16[224,128]{1,0:T(8,128)(2,1)S(1)}, bf16[224,128]{1,0:T(8,128)(2,1)S(1)}, u32[]{:S(2)}, u32[]{:S(2)}) %collective-permute-start.13) | collective-permute-done | bytes 57376 | tf_op jit(solution)/shard_map/ppermute | solution.py:557
  38.3 1.2 %collective-permute-done.12 = bf16[224,128]{1,0:T(8,128)(2,1)S(1)} collective-permute-done((bf16[224,128]{1,0:T(8,128)(2,1)S(1)}, bf16[224,128]{1,0:T(8,128)(2,1)S(1)}, u32[]{:S(2)}, u32[]{:S(2)}) %collective-permute-start.12) | collective-permute-done | bytes 57376 | tf_op jit(solution)/shard_map/ppermute | solution.py:557
  39.4 0.0 collective-permute-done.11
  39.5 0.2 collective-permute-start.14
  39.7 1.4 %collective-permute-done.14.theirs = bf16[4,224,128]{2,1,0:T(8,128)(2,1)S(1)} collective-permute-done((bf16[4,224,128]{2,1,0:T(8,128)(2,1)S(1)}, bf16[4,224,128]{2,1,0:T(8,128)(2,1)S(1)}, u32[]{:S(2)}, u32[]{:S(2)}) %collective-permute-start.14) | collective-permute-done | bytes 229408 | tf_op jit(solution)/shard_map/ppermute | solution.py:589
  41.0 1.0 %shard_map.82 = (f32[576,128]{1,0:T(8,128)}, f32[1152,128]{1,0:T(8,128)}) custom-call(bf16[4,224,128]{2,1,0:T(8,128)(2,1)S(1)} %pad_maximum_fusion.mine, bf16[4,224,128]{2,1,0:T(8,128)(2,1)S(1)} %collective-permute-done.14.theirs), custom_call_target="tpu_custom_call" | custom-call | flops 1000 | bytes 1572864 | tf_op jit(solution)/shard_map/pallas_call | solution.py:591
  (10 shorter events, 0.2 us)
Async XLA Ops:
  0.6 11.3 %copy-start.3 = (bf16[8,64,128]{2,1,0:T(8,128)(2,1)S(1)}, bf16[8,64,128]{2,1,0:T(8,128)(2,1)}, u32[]{:S(2)}) copy-start(bf16[8,64,128]{2,1,0:T(8,128)(2,1)} %grad_out.1) | copy-start | bytes 393220
  0.6 6.7 %copy-start = (bf16[3,3,128,128]{3,2,1,0:T(8,128)(2,1)S(1)}, bf16[3,3,128,128]{3,2,1,0:T(8,128)(2,1)}, u32[]{:S(2)}) copy-start(bf16[3,3,128,128]{3,2,1,0:T(8,128)(2,1)} %w_second.1) | copy-start | bytes 884740
  0.7 6.7 %copy-start.2 = (bf16[3,3,64,128]{3,2,1,0:T(8,128)(2,1)S(1)}, bf16[3,3,64,128]{3,2,1,0:T(8,128)(2,1)}, u32[]{:S(2)}) copy-start(bf16[3,3,64,128]{3,2,1,0:T(8,128)(2,1)} %w_first.1) | copy-start | bytes 442372
  0.7 6.7 %copy-start.1 = (bf16[16,128,64]{1,2,0:T(8,128)(2,1)S(1)}, bf16[16,128,64]{1,2,0:T(8,128)(2,1)}, u32[]{:S(2)}) copy-start(bf16[16,128,64]{1,2,0:T(8,128)(2,1)} %param.5) | copy-start | bytes 786436
  1.9 6.7 %collective-permute-start = (bf16[192,128]{1,0:T(8,128)(2,1)S(1)}, bf16[192,128]{1,0:T(8,128)(2,1)S(1)}, u32[]{:S(2)}, u32[]{:S(2)}) collective-permute-start(bf16[192,128]{1,0:T(8,128)(2,1)S(1)} %get-tuple-element.41), channel_id=1, source_target_pairs={{0,4},{1,5},{2,6},{3,7},{4,0},{5,1},{6,2},{7,3},{24,28},{25,29},{2... | collective-permute-start | bytes 147464 | tf_op jit(solution)/shard_map/ppermute | solution.py:456
  6.0 4.1 %collective-permute-start.1 = (bf16[192,128]{1,0:T(8,128)(2,1)S(1)}, bf16[192,128]{1,0:T(8,128)(2,1)S(1)}, u32[]{:S(2)}, u32[]{:S(2)}) collective-permute-start(bf16[192,128]{1,0:T(8,128)(2,1)S(1)} %get-tuple-element.42), channel_id=1, source_target_pairs={{0,8},{1,9},{2,10},{3,11},{4,12},{5,13},{6,14},{7,15},{8,0},{9,1},... | collective-permute-start | bytes 147464 | tf_op jit(solution)/shard_map/ppermute | solution.py:457
  10.2 4.9 %collective-permute-start.3 = (bf16[32,128]{1,0:T(8,128)(2,1)S(1)}, bf16[32,128]{1,0:T(8,128)(2,1)S(1)}, u32[]{:S(2)}, u32[]{:S(2)}) collective-permute-start(bf16[32,128]{1,0:T(8,128)(2,1)S(1)} %get-tuple-element.94), channel_id=1, source_target_pairs={{0,7},{1,2},{2,1},{3,4},{4,3},{5,6},{6,5},{7,0},{8,15},{9,10},{10,... | collective-permute-start | bytes 24584 | tf_op jit(solution)/shard_map/ppermute | solution.py:502
  11.0 4.1 %collective-permute-start.2 = (bf16[32,128]{1,0:T(8,128)(2,1)S(1)}, bf16[32,128]{1,0:T(8,128)(2,1)S(1)}, u32[]{:S(2)}, u32[]{:S(2)}) collective-permute-start(bf16[32,128]{1,0:T(8,128)(2,1)S(1)} %get-tuple-element.95), channel_id=1, source_target_pairs={{0,1},{1,0},{2,3},{3,2},{4,5},{5,4},{6,7},{7,6},{8,9},{9,8},{10,11... | collective-permute-start | bytes 24584 | tf_op jit(solution)/shard_map/ppermute | solution.py:503
  16.3 1.9 %collective-permute-start.4 = (f32[896,128]{1,0:T(8,128)S(1)}, f32[896,128]{1,0:T(8,128)S(1)}, u32[]{:S(2)}, u32[]{:S(2)}) collective-permute-start(f32[896,128]{1,0:T(8,128)S(1)} %get-tuple-element.63), channel_id=1, source_target_pairs={{0,1},{1,0},{2,3},{3,2},{4,5},{5,4},{6,7},{7,6},{8,9},{9,8},{10,11... | collective-permute-start | bytes 1376264 | tf_op jit(solution)/shard_map/ppermute | solution.py:560
  18.2 5.4 %collective-permute-start.5 = (bf16[224,128]{1,0:T(8,128)(2,1)S(1)}, bf16[224,128]{1,0:T(8,128)(2,1)S(1)}, u32[]{:S(2)}, u32[]{:S(2)}) collective-permute-start(bf16[224,128]{1,0:T(8,128)(2,1)S(1)} %get-tuple-element.65), channel_id=1, source_target_pairs={{0,24},{1,25},{2,26},{3,27},{4,28},{5,29},{6,30},{7,31},{8,16},{9,... | collective-permute-start | bytes 172040 | tf_op jit(solution)/shard_map/ppermute | solution.py:557
  20.7 4.2 %collective-permute-start.6 = (bf16[224,128]{1,0:T(8,128)(2,1)S(1)}, bf16[224,128]{1,0:T(8,128)(2,1)S(1)}, u32[]{:S(2)}, u32[]{:S(2)}) collective-permute-start(bf16[224,128]{1,0:T(8,128)(2,1)S(1)} %get-tuple-element.66), channel_id=1, source_target_pairs={{0,17},{1,16},{2,19},{3,18},{4,21},{5,20},{6,23},{7,22},{8,25},{9,... | collective-permute-start | bytes 172040 | tf_op jit(solution)/shard_map/ppermute | solution.py:557
  20.8 4.2 %collective-permute-start.7 = (bf16[224,128]{1,0:T(8,128)(2,1)S(1)}, bf16[224,128]{1,0:T(8,128)(2,1)S(1)}, u32[]{:S(2)}, u32[]{:S(2)}) collective-permute-start(bf16[224,128]{1,0:T(8,128)(2,1)S(1)} %get-tuple-element.67), channel_id=1, source_target_pairs={{0,9},{1,8},{2,11},{3,10},{4,13},{5,12},{6,15},{7,14},{8,1},{9,0},... | collective-permute-start | bytes 172040 | tf_op jit(solution)/shard_map/ppermute | solution.py:557
  25.0 6.7 %collective-permute-start.10 = (bf16[224,128]{1,0:T(8,128)(2,1)S(1)}, bf16[224,128]{1,0:T(8,128)(2,1)S(1)}, u32[]{:S(2)}, u32[]{:S(2)}) collective-permute-start(bf16[224,128]{1,0:T(8,128)(2,1)S(1)} %fusion.2), channel_id=1, source_target_pairs={{0,5},{1,4},{2,7},{3,6},{4,1},{5,0},{6,3},{7,2},{8,13},{9,12},{10,... | collective-permute-start | bytes 172040 | tf_op jit(solution)/shard_map/ppermute | solution.py:557
  25.4 6.5 %collective-permute-start.9 = (bf16[224,128]{1,0:T(8,128)(2,1)S(1)}, bf16[224,128]{1,0:T(8,128)(2,1)S(1)}, u32[]{:S(2)}, u32[]{:S(2)}) collective-permute-start(bf16[224,128]{1,0:T(8,128)(2,1)S(1)} %fusion.2), channel_id=1, source_target_pairs={{0,6},{1,7},{2,4},{3,5},{4,2},{5,3},{6,0},{7,1},{8,14},{9,15},{10,... | collective-permute-start | bytes 172040 | tf_op jit(solution)/shard_map/ppermute | solution.py:557
  26.9 6.1 %collective-permute-start.8 = (bf16[224,128]{1,0:T(8,128)(2,1)S(1)}, bf16[224,128]{1,0:T(8,128)(2,1)S(1)}, u32[]{:S(2)}, u32[]{:S(2)}) collective-permute-start(bf16[224,128]{1,0:T(8,128)(2,1)S(1)} %fusion.2), channel_id=1, source_target_pairs={{0,3},{1,2},{2,1},{3,0},{4,7},{5,6},{6,5},{7,4},{8,11},{9,10},{10,... | collective-permute-start | bytes 172040 | tf_op jit(solution)/shard_map/ppermute | solution.py:557
  33.1 5.2 %collective-permute-start.13 = (bf16[224,128]{1,0:T(8,128)(2,1)S(1)}, bf16[224,128]{1,0:T(8,128)(2,1)S(1)}, u32[]{:S(2)}, u32[]{:S(2)}) collective-permute-start(bf16[224,128]{1,0:T(8,128)(2,1)S(1)} %add_convert_fusion), channel_id=1, source_target_pairs={{0,24},{1,25},{2,26},{3,27},{4,28},{5,29},{6,30},{7,31},{8,16},{9,... | collective-permute-start | bytes 172040 | tf_op jit(solution)/shard_map/ppermute | solution.py:557
  34.8 4.6 %collective-permute-start.12 = (bf16[224,128]{1,0:T(8,128)(2,1)S(1)}, bf16[224,128]{1,0:T(8,128)(2,1)S(1)}, u32[]{:S(2)}, u32[]{:S(2)}) collective-permute-start(bf16[224,128]{1,0:T(8,128)(2,1)S(1)} %add_convert_fusion), channel_id=1, source_target_pairs={{0,17},{1,16},{2,19},{3,18},{4,21},{5,20},{6,23},{7,22},{8,25},{9,... | collective-permute-start | bytes 172040 | tf_op jit(solution)/shard_map/ppermute | solution.py:557
  35.1 4.4 %collective-permute-start.11 = (bf16[224,128]{1,0:T(8,128)(2,1)S(1)}, bf16[224,128]{1,0:T(8,128)(2,1)S(1)}, u32[]{:S(2)}, u32[]{:S(2)}) collective-permute-start(bf16[224,128]{1,0:T(8,128)(2,1)S(1)} %add_convert_fusion), channel_id=1, source_target_pairs={{0,9},{1,8},{2,11},{3,10},{4,13},{5,12},{6,15},{7,14},{8,1},{9,0},... | collective-permute-start | bytes 172040 | tf_op jit(solution)/shard_map/ppermute | solution.py:557
  39.5 1.6 %collective-permute-start.14 = (bf16[4,224,128]{2,1,0:T(8,128)(2,1)S(1)}, bf16[4,224,128]{2,1,0:T(8,128)(2,1)S(1)}, u32[]{:S(2)}, u32[]{:S(2)}) collective-permute-start(bf16[4,224,128]{2,1,0:T(8,128)(2,1)S(1)} %pad_maximum_fusion.mine), channel_id=1, source_target_pairs={{0,1},{1,0},{2,3},{3,2},{4,5},{5,4},{6,7},{7,6},{8,9},{9,8},{10,11... | collective-permute-start | bytes 688136 | tf_op jit(solution)/shard_map/ppermute | solution.py:589

commit v17 on v16

--- a/solution.py
+++ b/solution.py
@@ -448,7 +448,8 @@
         compiler_params=params(58),
         cost_estimate=pl.CostEstimate(flops=1000, bytes_accessed=1 << 18, transcendentals=0),
     )(pre_first, grad_out)
-    pairs = [(i * lons + j, i * lons + (j + lons // 2) % lons) for i in (0, lats - 1) for j in range(lons)]
+    pairs = [(j, (j + lons // 2) % lons) for j in range(lons)]
+    pairs += [((lats - 1) * lons + j, (lats - 1) * lons + (j ^ 1)) for j in range(lons)]
     for i in range(1, lats - 1, 2):
         for j in range(lons):
             pairs += [(i * lons + j, (i + 1) * lons + j), ((i + 1) * lons + j, i * lons + j)]

time: 42.2 us -> 41.8 us (level)
  transfers between devices with their start and end apart: 15 -> 15, of which waited for: 11 -> 12; matrix products, arithmetic and copies ran while one was open for 0% -> 0% of each run, Pallas kernels for 15% -> 15%
where the time goes in v17:
time: 41.8 us; the launch traced here: 41.7 us
  starting transfers between devices  16 us (38%)
  waiting for transfers between devices  14.9 us (36%)
  Pallas kernels  9.56 us (23%)
  between operations  0.79 us (2%)
    ppermute x9, starting transfers between devices, between_chips(): lax.ppermute(value, AREA, [(i * lons + j, (i ^ over_lat) * lons + (j ^ 2...  9.57 us
    ppermute x9, waiting for transfers between devices, between_chips(): lax.ppermute(value, AREA, [(i * lons + j, (i ^ over_lat) * lons + (j ^ 2...  9.01 us
    ppermute x1, starting transfers between devices, body(): row_b = lax.ppermute(row_b, AREA, pairs)  4.1 us
    pallas_call x1, Pallas kernels, body(): pl.pallas_call(functools.partial(middle_kernel, lats), out_shape=(shape((...  2.4 us
    pallas_call x1, Pallas kernels, body(): pl.pallas_call(functools.partial(last_kernel, lats), out_shape=shape((row...  2.16 us
    ppermute x1, waiting for transfers between devices, body(): parts = (own + lax.ppermute(other, 'lon', swap)).reshape(lats, block, c1)  1.8 us
    ppermute x1, waiting for transfers between devices, body(): row_a = lax.ppermute(row_a, AREA, every)  1.49 us
    ppermute x1, waiting for transfers between devices, body(): theirs = lax.ppermute(mine, 'lon', swap)  1.37 us
  transfers between devices with their start and end apart: 15, of which 12 were waited for; matrix products, arithmetic and copies ran while one was open for 0% of the time, Pallas kernels for 15%

profile of v17, /device:TPU:0, one launch (start us, length us, event | category | flops | bytes accessed | tf_op | source)
XLA Modules:
  0.0 41.7 jit_solution(2205093501397663801)
XLA Ops:
  0.6 0.0 copy-start.3
  0.6 0.0 copy-start
  0.7 0.0 copy-start.2
  0.7 0.0 copy-start.1
  0.7 1.2 %shard_map.76 = (bf16[192,128]{1,0:T(8,128)(2,1)S(1)}, bf16[192,128]{1,0:T(8,128)(2,1)S(1)}, bf16[32,128]{1,0:T(8,128)(2,1)S(1)}, bf16[32,128]{1,0:T(8,128)(2,1)S(1)}, bf16[16,128,128]{2,1,0:T(8,128)(2,1)S(1)}) custom-call(bf16[16,128,128]{2,1,0:T(8,128)(2,1)} %pre_far.1, bf16[8,64,128]{2,1,0:T(8,128)(2,1)} %grad_out.1), custom_call_target="tpu_custom_call" | custom-call | flops 1000 | bytes 262144 | tf_op jit(solution)/shard_map/pallas_call | solution.py:432
  1.9 4.1 %collective-permute-start = (bf16[192,128]{1,0:T(8,128)(2,1)S(1)}, bf16[192,128]{1,0:T(8,128)(2,1)S(1)}, u32[]{:S(2)}, u32[]{:S(2)}) collective-permute-start(bf16[192,128]{1,0:T(8,128)(2,1)S(1)} %get-tuple-element.41), channel_id=1, source_target_pairs={{0,4},{1,5},{2,6},{3,7},{4,0},{5,1},{6,2},{7,3},{24,25},{25,24},{2... | collective-permute-start | bytes 147464 | tf_op jit(solution)/shard_map/ppermute | solution.py:457
  6.0 0.4 collective-permute-start.1
  6.4 0.1 pad.9.clone
  6.4 0.9 %shard_map.77 = (f32[16,64,256]{2,1,0:T(8,128)S(1)}, bf16[2,256,512]{2,1,0:T(8,128)(2,1)S(1)}, f32[2,16,128]{2,1,0:T(8,128)S(1)}) custom-call(bf16[16,128,128]{2,1,0:T(8,128)(2,1)S(1)} %get-tuple-element.43.pre), custom_call_target="tpu_custom_call" | custom-call | flops 15728640 | bytes 2097152 | tf_op jit(solution)/shard_map/pallas_call | solution.py:460
  7.4 0.0 copy-done
  7.4 0.0 copy-done.2
  7.4 0.0 copy-done.1
  7.4 0.7 %shard_map.78 = (bf16[128,1024]{1,0:T(8,128)(2,1)S(1)}, bf16[128,32]{1,0:T(8,128)(2,1)S(1)}, bf16[384,512]{1,0:T(8,128)(2,1)S(1)}, bf16[3,256,512]{2,1,0:T(8,128)(2,1)S(1)}) custom-call(bf16[16,64,128]{2,1,0:T(8,128)(2,1)S(1)} %bitcast.8, bf16[3,3,64,128]{3,2,1,0:T(8,128)(2,1)S(1)} %copy-done.2, bf16[3,3,128,128]{3,2,1,0:T(8,128)(2,1)S(1)} %copy-done), custom_call_target="tpu_custom_call" | custom-call | flops 67108864 | bytes 3145728 | tf_op jit(solution)/shard_map/pallas_call | solution.py:478
  8.1 0.4 %collective-permute-done.row_b = bf16[192,128]{1,0:T(8,128)(2,1)S(1)} collective-permute-done((bf16[192,128]{1,0:T(8,128)(2,1)S(1)}, bf16[192,128]{1,0:T(8,128)(2,1)S(1)}, u32[]{:S(2)}, u32[]{:S(2)}) %collective-permute-start) | collective-permute-done | bytes 49184 | tf_op jit(solution)/shard_map/ppermute | solution.py:457
  8.6 1.5 %collective-permute-done.1.row_a = bf16[192,128]{1,0:T(8,128)(2,1)S(1)} collective-permute-done((bf16[192,128]{1,0:T(8,128)(2,1)S(1)}, bf16[192,128]{1,0:T(8,128)(2,1)S(1)}, u32[]{:S(2)}, u32[]{:S(2)}) %collective-permute-start.1) | collective-permute-done | bytes 49184 | tf_op jit(solution)/shard_map/ppermute | solution.py:458
  10.1 0.1 maximum_maximum_fusion.1
  10.2 0.8 %collective-permute-start.3 = (bf16[32,128]{1,0:T(8,128)(2,1)S(1)}, bf16[32,128]{1,0:T(8,128)(2,1)S(1)}, u32[]{:S(2)}, u32[]{:S(2)}) collective-permute-start(bf16[32,128]{1,0:T(8,128)(2,1)S(1)} %get-tuple-element.94), channel_id=1, source_target_pairs={{0,7},{1,2},{2,1},{3,4},{4,3},{5,6},{6,5},{7,0},{8,15},{9,10},{10,... | collective-permute-start | bytes 24584 | tf_op jit(solution)/shard_map/ppermute | solution.py:503
  11.0 0.9 %collective-permute-start.2 = (bf16[32,128]{1,0:T(8,128)(2,1)S(1)}, bf16[32,128]{1,0:T(8,128)(2,1)S(1)}, u32[]{:S(2)}, u32[]{:S(2)}) collective-permute-start(bf16[32,128]{1,0:T(8,128)(2,1)S(1)} %get-tuple-element.95), channel_id=1, source_target_pairs={{0,1},{1,0},{2,3},{3,2},{4,5},{5,4},{6,7},{7,6},{8,9},{9,8},{10,11... | collective-permute-start | bytes 24584 | tf_op jit(solution)/shard_map/ppermute | solution.py:504
  11.9 0.0 copy-done.3
  11.9 2.4 %shard_map.79 = (bf16[19,64,512]{2,1,0:T(8,128)(2,1)S(1)}, f32[1792,128]{1,0:T(8,128)S(1)}, f32[2,32,128]{2,1,0:T(8,128)S(1)}, f32[2,32,128]{2,1,0:T(8,128)S(1)}, f32[2,16,128]{2,1,0:T(8,128)S(1)}) custom-call(bf16[8,64,128]{2,1,0:T(8,128)(2,1)S(1)} %copy-done.3, bf16[192,128]{1,0:T(8,128)(2,1)S(1)} %collective-permute-done.1.row_a, ...), custom_call_target="tpu_custom_call" | custom-call | flops 1509949440 | bytes 8388608 | tf_op jit(solution)/shard_map/pallas_call | solution.py:509
  14.3 0.8 %collective-permute-done.3.col_b = bf16[32,128]{1,0:T(8,128)(2,1)S(1)} collective-permute-done((bf16[32,128]{1,0:T(8,128)(2,1)S(1)}, bf16[32,128]{1,0:T(8,128)(2,1)S(1)}, u32[]{:S(2)}, u32[]{:S(2)}) %collective-permute-start.3) | collective-permute-done | bytes 8224 | tf_op jit(solution)/shard_map/ppermute | solution.py:503
  15.1 0.0 collective-permute-done.2.col_a
  15.1 1.2 %shard_map.80 = (bf16[4,32,128]{2,1,0:T(8,128)(2,1)S(1)}, f32[896,128]{1,0:T(8,128)S(1)}, f32[896,128]{1,0:T(8,128)S(1)}) custom-call(bf16[32,128]{1,0:T(8,128)(2,1)S(1)} %collective-permute-done.2.col_a, bf16[32,128]{1,0:T(8,128)(2,1)S(1)} %collective-permute-done.3.col_b, f32[2,16,128]{2,1,0:T(8,128)S(1)} %get-tuple-element.56.act_ends, ...), custom_call_target="tpu_custom_call" | custom-call | flops 268435456 | bytes 3145728 | tf_op jit(solution)/shard_map/pallas_call | solution.py:535
  16.3 0.1 collective-permute-start.4
  16.3 1.8 %collective-permute-done.4 = f32[896,128]{1,0:T(8,128)S(1)} collective-permute-done((f32[896,128]{1,0:T(8,128)S(1)}, f32[896,128]{1,0:T(8,128)S(1)}, u32[]{:S(2)}, u32[]{:S(2)}) %collective-permute-start.4) | collective-permute-done | bytes 458784 | tf_op jit(solution)/shard_map/ppermute | solution.py:561
  18.1 0.1 fusion.3
  18.2 0.5 %collective-permute-start.5 = (bf16[224,128]{1,0:T(8,128)(2,1)S(1)}, bf16[224,128]{1,0:T(8,128)(2,1)S(1)}, u32[]{:S(2)}, u32[]{:S(2)}) collective-permute-start(bf16[224,128]{1,0:T(8,128)(2,1)S(1)} %get-tuple-element.65), channel_id=1, source_target_pairs={{0,24},{1,25},{2,26},{3,27},{4,28},{5,29},{6,30},{7,31},{8,16},{9,... | collective-permute-start | bytes 172040 | tf_op jit(solution)/shard_map/ppermute | solution.py:558
  18.8 0.9 %collective-permute-start.6 = (bf16[224,128]{1,0:T(8,128)(2,1)S(1)}, bf16[224,128]{1,0:T(8,128)(2,1)S(1)}, u32[]{:S(2)}, u32[]{:S(2)}) collective-permute-start(bf16[224,128]{1,0:T(8,128)(2,1)S(1)} %get-tuple-element.66), channel_id=1, source_target_pairs={{0,17},{1,16},{2,19},{3,18},{4,21},{5,20},{6,23},{7,22},{8,25},{9,... | collective-permute-start | bytes 172040 | tf_op jit(solution)/shard_map/ppermute | solution.py:558
  19.6 1.9 %collective-permute-start.7 = (bf16[224,128]{1,0:T(8,128)(2,1)S(1)}, bf16[224,128]{1,0:T(8,128)(2,1)S(1)}, u32[]{:S(2)}, u32[]{:S(2)}) collective-permute-start(bf16[224,128]{1,0:T(8,128)(2,1)S(1)} %get-tuple-element.67), channel_id=1, source_target_pairs={{0,9},{1,8},{2,11},{3,10},{4,13},{5,12},{6,15},{7,14},{8,1},{9,0},... | collective-permute-start | bytes 172040 | tf_op jit(solution)/shard_map/ppermute | solution.py:558
  21.5 2.2 %shard_map.81 = bf16[16,64,128]{2,1,0:T(8,128)(2,1)} custom-call(bf16[19,64,512]{2,1,0:T(8,128)(2,1)S(1)} %get-tuple-element.68.part, bf16[4,32,128]{2,1,0:T(8,128)(2,1)S(1)} %get-tuple-element.69.ends, bf16[384,512]{1,0:T(8,128)(2,1)S(1)} %get-tuple-element.70.taps), custom_call_target="tpu_custom_call" | custom-call | flops 301989888 | bytes 3145728 | tf_op jit(solution)/shard_map/pallas_call | solution.py:565
  23.7 0.3 collective-permute-done.5
  23.9 0.1 collective-permute-done.6
  24.0 0.0 collective-permute-done.7
  24.1 1.3 %collective-permute-start.10 = (bf16[224,128]{1,0:T(8,128)(2,1)S(1)}, bf16[224,128]{1,0:T(8,128)(2,1)S(1)}, u32[]{:S(2)}, u32[]{:S(2)}) collective-permute-start(bf16[224,128]{1,0:T(8,128)(2,1)S(1)} %fusion.2), channel_id=1, source_target_pairs={{0,5},{1,4},{2,7},{3,6},{4,1},{5,0},{6,3},{7,2},{8,13},{9,12},{10,... | collective-permute-start | bytes 172040 | tf_op jit(solution)/shard_map/ppermute | solution.py:558
  25.4 1.3 %collective-permute-start.9 = (bf16[224,128]{1,0:T(8,128)(2,1)S(1)}, bf16[224,128]{1,0:T(8,128)(2,1)S(1)}, u32[]{:S(2)}, u32[]{:S(2)}) collective-permute-start(bf16[224,128]{1,0:T(8,128)(2,1)S(1)} %fusion.2), channel_id=1, source_target_pairs={{0,6},{1,7},{2,4},{3,5},{4,2},{5,3},{6,0},{7,1},{8,14},{9,15},{10,... | collective-permute-start | bytes 172040 | tf_op jit(solution)/shard_map/ppermute | solution.py:558
  26.8 0.3 collective-permute-start.8
  27.1 4.0 %collective-permute-done.10 = bf16[224,128]{1,0:T(8,128)(2,1)S(1)} collective-permute-done((bf16[224,128]{1,0:T(8,128)(2,1)S(1)}, bf16[224,128]{1,0:T(8,128)(2,1)S(1)}, u32[]{:S(2)}, u32[]{:S(2)}) %collective-permute-start.10) | collective-permute-done | bytes 57376 | tf_op jit(solution)/shard_map/ppermute | solution.py:558
  31.1 0.8 %collective-permute-done.9 = bf16[224,128]{1,0:T(8,128)(2,1)S(1)} collective-permute-done((bf16[224,128]{1,0:T(8,128)(2,1)S(1)}, bf16[224,128]{1,0:T(8,128)(2,1)S(1)}, u32[]{:S(2)}, u32[]{:S(2)}) %collective-permute-start.9) | collective-permute-done | bytes 57376 | tf_op jit(solution)/shard_map/ppermute | solution.py:558
  31.8 0.9 %collective-permute-done.8 = bf16[224,128]{1,0:T(8,128)(2,1)S(1)} collective-permute-done((bf16[224,128]{1,0:T(8,128)(2,1)S(1)}, bf16[224,128]{1,0:T(8,128)(2,1)S(1)}, u32[]{:S(2)}, u32[]{:S(2)}) %collective-permute-start.8) | collective-permute-done | bytes 57376 | tf_op jit(solution)/shard_map/ppermute | solution.py:558
  32.8 1.5 %collective-permute-start.13 = (bf16[224,128]{1,0:T(8,128)(2,1)S(1)}, bf16[224,128]{1,0:T(8,128)(2,1)S(1)}, u32[]{:S(2)}, u32[]{:S(2)}) collective-permute-start(bf16[224,128]{1,0:T(8,128)(2,1)S(1)} %add_convert_fusion), channel_id=1, source_target_pairs={{0,24},{1,25},{2,26},{3,27},{4,28},{5,29},{6,30},{7,31},{8,16},{9,... | collective-permute-start | bytes 172040 | tf_op jit(solution)/shard_map/ppermute | solution.py:558
  34.2 0.4 collective-permute-start.12
  34.6 1.4 %collective-permute-start.11 = (bf16[224,128]{1,0:T(8,128)(2,1)S(1)}, bf16[224,128]{1,0:T(8,128)(2,1)S(1)}, u32[]{:S(2)}, u32[]{:S(2)}) collective-permute-start(bf16[224,128]{1,0:T(8,128)(2,1)S(1)} %add_convert_fusion), channel_id=1, source_target_pairs={{0,9},{1,8},{2,11},{3,10},{4,13},{5,12},{6,15},{7,14},{8,1},{9,0},... | collective-permute-start | bytes 172040 | tf_op jit(solution)/shard_map/ppermute | solution.py:558
  36.0 2.0 %collective-permute-done.13 = bf16[224,128]{1,0:T(8,128)(2,1)S(1)} collective-permute-done((bf16[224,128]{1,0:T(8,128)(2,1)S(1)}, bf16[224,128]{1,0:T(8,128)(2,1)S(1)}, u32[]{:S(2)}, u32[]{:S(2)}) %collective-permute-start.13) | collective-permute-done | bytes 57376 | tf_op jit(solution)/shard_map/ppermute | solution.py:558
  38.0 1.0 %collective-permute-done.12 = bf16[224,128]{1,0:T(8,128)(2,1)S(1)} collective-permute-done((bf16[224,128]{1,0:T(8,128)(2,1)S(1)}, bf16[224,128]{1,0:T(8,128)(2,1)S(1)}, u32[]{:S(2)}, u32[]{:S(2)}) %collective-permute-start.12) | collective-permute-done | bytes 57376 | tf_op jit(solution)/shard_map/ppermute | solution.py:558
  39.1 0.0 collective-permute-done.11
  39.1 0.2 collective-permute-start.14
  39.3 1.4 %collective-permute-done.14.theirs = bf16[4,224,128]{2,1,0:T(8,128)(2,1)S(1)} collective-permute-done((bf16[4,224,128]{2,1,0:T(8,128)(2,1)S(1)}, bf16[4,224,128]{2,1,0:T(8,128)(2,1)S(1)}, u32[]{:S(2)}, u32[]{:S(2)}) %collective-permute-start.14) | collective-permute-done | bytes 229408 | tf_op jit(solution)/shard_map/ppermute | solution.py:590
  40.7 1.0 %shard_map.82 = (f32[576,128]{1,0:T(8,128)}, f32[1152,128]{1,0:T(8,128)}) custom-call(bf16[4,224,128]{2,1,0:T(8,128)(2,1)S(1)} %pad_maximum_fusion.mine, bf16[4,224,128]{2,1,0:T(8,128)(2,1)S(1)} %collective-permute-done.14.theirs), custom_call_target="tpu_custom_call" | custom-call | flops 1000 | bytes 1572864 | tf_op jit(solution)/shard_map/pallas_call | solution.py:592
  (10 shorter events, 0.2 us)
Async XLA Ops:
  0.6 11.3 %copy-start.3 = (bf16[8,64,128]{2,1,0:T(8,128)(2,1)S(1)}, bf16[8,64,128]{2,1,0:T(8,128)(2,1)}, u32[]{:S(2)}) copy-start(bf16[8,64,128]{2,1,0:T(8,128)(2,1)} %grad_out.1) | copy-start | bytes 393220
  0.6 6.7 %copy-start = (bf16[3,3,128,128]{3,2,1,0:T(8,128)(2,1)S(1)}, bf16[3,3,128,128]{3,2,1,0:T(8,128)(2,1)}, u32[]{:S(2)}) copy-start(bf16[3,3,128,128]{3,2,1,0:T(8,128)(2,1)} %w_second.1) | copy-start | bytes 884740
  0.7 6.7 %copy-start.2 = (bf16[3,3,64,128]{3,2,1,0:T(8,128)(2,1)S(1)}, bf16[3,3,64,128]{3,2,1,0:T(8,128)(2,1)}, u32[]{:S(2)}) copy-start(bf16[3,3,64,128]{3,2,1,0:T(8,128)(2,1)} %w_first.1) | copy-start | bytes 442372
  0.7 6.7 %copy-start.1 = (bf16[16,128,64]{1,2,0:T(8,128)(2,1)S(1)}, bf16[16,128,64]{1,2,0:T(8,128)(2,1)}, u32[]{:S(2)}) copy-start(bf16[16,128,64]{1,2,0:T(8,128)(2,1)} %param.5) | copy-start | bytes 786436
  1.9 6.7 %collective-permute-start = (bf16[192,128]{1,0:T(8,128)(2,1)S(1)}, bf16[192,128]{1,0:T(8,128)(2,1)S(1)}, u32[]{:S(2)}, u32[]{:S(2)}) collective-permute-start(bf16[192,128]{1,0:T(8,128)(2,1)S(1)} %get-tuple-element.41), channel_id=1, source_target_pairs={{0,4},{1,5},{2,6},{3,7},{4,0},{5,1},{6,2},{7,3},{24,25},{25,24},{2... | collective-permute-start | bytes 147464 | tf_op jit(solution)/shard_map/ppermute | solution.py:457
  6.0 4.1 %collective-permute-start.1 = (bf16[192,128]{1,0:T(8,128)(2,1)S(1)}, bf16[192,128]{1,0:T(8,128)(2,1)S(1)}, u32[]{:S(2)}, u32[]{:S(2)}) collective-permute-start(bf16[192,128]{1,0:T(8,128)(2,1)S(1)} %get-tuple-element.42), channel_id=1, source_target_pairs={{0,8},{1,9},{2,10},{3,11},{4,12},{5,13},{6,14},{7,15},{8,0},{9,1},... | collective-permute-start | bytes 147464 | tf_op jit(solution)/shard_map/ppermute | solution.py:458
  10.2 4.9 %collective-permute-start.3 = (bf16[32,128]{1,0:T(8,128)(2,1)S(1)}, bf16[32,128]{1,0:T(8,128)(2,1)S(1)}, u32[]{:S(2)}, u32[]{:S(2)}) collective-permute-start(bf16[32,128]{1,0:T(8,128)(2,1)S(1)} %get-tuple-element.94), channel_id=1, source_target_pairs={{0,7},{1,2},{2,1},{3,4},{4,3},{5,6},{6,5},{7,0},{8,15},{9,10},{10,... | collective-permute-start | bytes 24584 | tf_op jit(solution)/shard_map/ppermute | solution.py:503
  11.0 4.1 %collective-permute-start.2 = (bf16[32,128]{1,0:T(8,128)(2,1)S(1)}, bf16[32,128]{1,0:T(8,128)(2,1)S(1)}, u32[]{:S(2)}, u32[]{:S(2)}) collective-permute-start(bf16[32,128]{1,0:T(8,128)(2,1)S(1)} %get-tuple-element.95), channel_id=1, source_target_pairs={{0,1},{1,0},{2,3},{3,2},{4,5},{5,4},{6,7},{7,6},{8,9},{9,8},{10,11... | collective-permute-start | bytes 24584 | tf_op jit(solution)/shard_map/ppermute | solution.py:504
  16.3 1.9 %collective-permute-start.4 = (f32[896,128]{1,0:T(8,128)S(1)}, f32[896,128]{1,0:T(8,128)S(1)}, u32[]{:S(2)}, u32[]{:S(2)}) collective-permute-start(f32[896,128]{1,0:T(8,128)S(1)} %get-tuple-element.63), channel_id=1, source_target_pairs={{0,1},{1,0},{2,3},{3,2},{4,5},{5,4},{6,7},{7,6},{8,9},{9,8},{10,11... | collective-permute-start | bytes 1376264 | tf_op jit(solution)/shard_map/ppermute | solution.py:561
  18.2 5.7 %collective-permute-start.5 = (bf16[224,128]{1,0:T(8,128)(2,1)S(1)}, bf16[224,128]{1,0:T(8,128)(2,1)S(1)}, u32[]{:S(2)}, u32[]{:S(2)}) collective-permute-start(bf16[224,128]{1,0:T(8,128)(2,1)S(1)} %get-tuple-element.65), channel_id=1, source_target_pairs={{0,24},{1,25},{2,26},{3,27},{4,28},{5,29},{6,30},{7,31},{8,16},{9,... | collective-permute-start | bytes 172040 | tf_op jit(solution)/shard_map/ppermute | solution.py:558
  18.8 5.3 %collective-permute-start.6 = (bf16[224,128]{1,0:T(8,128)(2,1)S(1)}, bf16[224,128]{1,0:T(8,128)(2,1)S(1)}, u32[]{:S(2)}, u32[]{:S(2)}) collective-permute-start(bf16[224,128]{1,0:T(8,128)(2,1)S(1)} %get-tuple-element.66), channel_id=1, source_target_pairs={{0,17},{1,16},{2,19},{3,18},{4,21},{5,20},{6,23},{7,22},{8,25},{9,... | collective-permute-start | bytes 172040 | tf_op jit(solution)/shard_map/ppermute | solution.py:558
  19.6 4.4 %collective-permute-start.7 = (bf16[224,128]{1,0:T(8,128)(2,1)S(1)}, bf16[224,128]{1,0:T(8,128)(2,1)S(1)}, u32[]{:S(2)}, u32[]{:S(2)}) collective-permute-start(bf16[224,128]{1,0:T(8,128)(2,1)S(1)} %get-tuple-element.67), channel_id=1, source_target_pairs={{0,9},{1,8},{2,11},{3,10},{4,13},{5,12},{6,15},{7,14},{8,1},{9,0},... | collective-permute-start | bytes 172040 | tf_op jit(solution)/shard_map/ppermute | solution.py:558
  24.1 7.0 %collective-permute-start.10 = (bf16[224,128]{1,0:T(8,128)(2,1)S(1)}, bf16[224,128]{1,0:T(8,128)(2,1)S(1)}, u32[]{:S(2)}, u32[]{:S(2)}) collective-permute-start(bf16[224,128]{1,0:T(8,128)(2,1)S(1)} %fusion.2), channel_id=1, source_target_pairs={{0,5},{1,4},{2,7},{3,6},{4,1},{5,0},{6,3},{7,2},{8,13},{9,12},{10,... | collective-permute-start | bytes 172040 | tf_op jit(solution)/shard_map/ppermute | solution.py:558
  25.4 6.4 %collective-permute-start.9 = (bf16[224,128]{1,0:T(8,128)(2,1)S(1)}, bf16[224,128]{1,0:T(8,128)(2,1)S(1)}, u32[]{:S(2)}, u32[]{:S(2)}) collective-permute-start(bf16[224,128]{1,0:T(8,128)(2,1)S(1)} %fusion.2), channel_id=1, source_target_pairs={{0,6},{1,7},{2,4},{3,5},{4,2},{5,3},{6,0},{7,1},{8,14},{9,15},{10,... | collective-permute-start | bytes 172040 | tf_op jit(solution)/shard_map/ppermute | solution.py:558
  26.8 6.0 %collective-permute-start.8 = (bf16[224,128]{1,0:T(8,128)(2,1)S(1)}, bf16[224,128]{1,0:T(8,128)(2,1)S(1)}, u32[]{:S(2)}, u32[]{:S(2)}) collective-permute-start(bf16[224,128]{1,0:T(8,128)(2,1)S(1)} %fusion.2), channel_id=1, source_target_pairs={{0,3},{1,2},{2,1},{3,0},{4,7},{5,6},{6,5},{7,4},{8,11},{9,10},{10,... | collective-permute-start | bytes 172040 | tf_op jit(solution)/shard_map/ppermute | solution.py:558
  32.8 5.2 %collective-permute-start.13 = (bf16[224,128]{1,0:T(8,128)(2,1)S(1)}, bf16[224,128]{1,0:T(8,128)(2,1)S(1)}, u32[]{:S(2)}, u32[]{:S(2)}) collective-permute-start(bf16[224,128]{1,0:T(8,128)(2,1)S(1)} %add_convert_fusion), channel_id=1, source_target_pairs={{0,24},{1,25},{2,26},{3,27},{4,28},{5,29},{6,30},{7,31},{8,16},{9,... | collective-permute-start | bytes 172040 | tf_op jit(solution)/shard_map/ppermute | solution.py:558
  34.2 4.8 %collective-permute-start.12 = (bf16[224,128]{1,0:T(8,128)(2,1)S(1)}, bf16[224,128]{1,0:T(8,128)(2,1)S(1)}, u32[]{:S(2)}, u32[]{:S(2)}) collective-permute-start(bf16[224,128]{1,0:T(8,128)(2,1)S(1)} %add_convert_fusion), channel_id=1, source_target_pairs={{0,17},{1,16},{2,19},{3,18},{4,21},{5,20},{6,23},{7,22},{8,25},{9,... | collective-permute-start | bytes 172040 | tf_op jit(solution)/shard_map/ppermute | solution.py:558
  34.6 4.4 %collective-permute-start.11 = (bf16[224,128]{1,0:T(8,128)(2,1)S(1)}, bf16[224,128]{1,0:T(8,128)(2,1)S(1)}, u32[]{:S(2)}, u32[]{:S(2)}) collective-permute-start(bf16[224,128]{1,0:T(8,128)(2,1)S(1)} %add_convert_fusion), channel_id=1, source_target_pairs={{0,9},{1,8},{2,11},{3,10},{4,13},{5,12},{6,15},{7,14},{8,1},{9,0},... | collective-permute-start | bytes 172040 | tf_op jit(solution)/shard_map/ppermute | solution.py:558
  39.1 1.6 %collective-permute-start.14 = (bf16[4,224,128]{2,1,0:T(8,128)(2,1)S(1)}, bf16[4,224,128]{2,1,0:T(8,128)(2,1)S(1)}, u32[]{:S(2)}, u32[]{:S(2)}) collective-permute-start(bf16[4,224,128]{2,1,0:T(8,128)(2,1)S(1)} %pad_maximum_fusion.mine), channel_id=1, source_target_pairs={{0,1},{1,0},{2,3},{3,2},{4,5},{5,4},{6,7},{7,6},{8,9},{9,8},{10,11... | collective-permute-start | bytes 688136 | tf_op jit(solution)/shard_map/ppermute | solution.py:590

commit v18 on v17

--- a/solution.py
+++ b/solution.py
@@ -98,6 +98,7 @@
     rows, c0, cols = fields.shape
     c1 = w_first.shape[3]
     half = cols // 2
+    first = lax.axis_index("lat") == 0
     col = lax.broadcasted_iota(jnp.int32, (cols, 2 * cols), 0)
     lane = lax.broadcasted_iota(jnp.int32, (cols, 2 * cols), 1)
     turn = lane // cols
@@ -106,12 +107,22 @@
     order = one_at(col == 2 * (lane % half) + parity)
     turned[...] = dot(fields[...].reshape(rows * c0, cols), order).astype(BF16).reshape(rows, c0, 2 * cols)
     low = lax.broadcasted_iota(jnp.int32, (c0, cols), 1) < half
-    for q in range(rows // 2):
-        fields_t[:c0, q * cols:(q + 1) * cols] = jnp.where(low, turned[2 * q, :, :cols], turned[2 * q + 1, :, cols:])
-        fields_t[c0:, q * cols:(q + 1) * cols] = jnp.where(low, turned[2 * q, :, cols:], turned[2 * q + 1, :, :cols])
-    cell = lax.broadcasted_iota(jnp.int32, (rows * half, 2 * rows), 0)
-    n = lax.broadcasted_iota(jnp.int32, (rows * half, 2 * rows), 1)
-    pick = one_at(cell == (n % rows) * half + (n // rows) * (half - 1))
+    none = jnp.zeros((c0, cols), BF16)
+    for a in range(3):
+        for q in range(rows // 2 + 1):
+            for pc in range(2):
+                near, away = (slice(0, cols), slice(cols, 2 * cols)) if pc == 0 else (slice(cols, 2 * cols), slice(0, cols))
+                left, right = 2 * q - 2 + a, 2 * q - 1 + a
+                one = turned[left, :, near] if 0 <= left < rows else none
+                two = turned[right, :, away] if 0 <= right < rows else none
+                if q == 0 and a != 1:
+                    one = jnp.where(first == (a == 0), turned[0, :, near], none)
+                start = (2 * a + pc) * c0
+                fields_t[start:start + c0, q * cols:(q + 1) * cols] = jnp.where(low, one, two)
+    reach = field_ends.shape[1] // 2
+    cell = lax.broadcasted_iota(jnp.int32, ((rows + 2) * half, 2 * reach), 0)
+    n = lax.broadcasted_iota(jnp.int32, ((rows + 2) * half, 2 * reach), 1)
+    pick = one_at(cell == (n % reach) * half + (n // reach) * (half - 1))
     field_ends[...] = dot(fields_t[...], pick).astype(BF16)
     taps_second[...] = jnp.zeros_like(taps_second)
     taps_first[...] = jnp.zeros_like(taps_first)
@@ -129,14 +140,14 @@
 
 def middle_kernel(lats, grad_out, row_a, row_b, slope, act_t, fields_t, taps,
                   spread, keep, raw_ends, slope_ends, out_ends,
-                  grid, wide, prods, ends, line, sums, corner):
+                  grid, wide, prods, line, sums, corner):
     _, first, last, even, _ = position(lats)
     top = jnp.where(even, row_b[...], row_a[...])
     bottom = jnp.where(even, row_a[...], row_b[...])
     rows, half, c2 = slope.shape
     c1 = c2 // 2
     pooled = rows // 2
-    c0 = fields_t.shape[0] // 2
+    c0 = fields_t.shape[0] // 6
     cells = pooled * half
     raw_ends[...] = jnp.zeros_like(raw_ends)
     slope_ends[...] = jnp.zeros_like(slope_ends)
@@ -156,14 +167,10 @@
         wide[i, :, 2 * c1:3 * c1] = jnp.where(at == half - 1, 0.0, pltpu.roll(here, half - 1, 0)).astype(BF16)
         wide[i, :, 3 * c1:] = here.astype(BF16)
 
-    flat = wide[1:pooled + 1].reshape(cells, 4 * c1)
-    for a in range(3):
-        prods[a] = dot_nt(flat, taps[a]).reshape(pooled, half, c2)
-    fold = jnp.where(first, taps[0], taps[2])
-    ends[0] = dot_nt(wide[0], fold)
-    ends[1] = dot_nt(wide[0], taps[1])
-    ends[2] = dot_nt(wide[pooled + 1], taps[0])
-    ends[3] = dot_nt(wide[pooled + 1], taps[1])
+    flat = wide[...].reshape((pooled + 2) * half, 4 * c1)
+    for a in range(3):
+        prods[a] = dot_nt(flat, taps[a]).reshape(pooled + 2, half, c2)
+    fold = jnp.where(first, prods[0, 0], prods[2, 0])
 
     def place(r, total, incline):
         inner = total * incline
@@ -182,19 +189,18 @@
         both = [line[pl.ds(pc, half, stride=2), :] for pc in range(2)]
         return jnp.concatenate([slope_of(v, cdf_of(v)) for v in both], axis=1)
 
-    place(0, ends[0] + ends[1] + prods[0, 0], halo_slope(top))
-    place(1, ends[0] + prods[1, 0] + prods[0, 0], slope[0])
+    place(0, fold + prods[1, 0] + prods[0, 1], halo_slope(top))
+    place(1, fold + prods[1, 1] + prods[0, 1], slope[0])
 
     def pair(i, carry):
-        middle = prods[2, i] + prods[1, i]
-        place(2 * i + 2, middle + prods[0, i + 1], slope[2 * i + 1])
-        place(2 * i + 3, prods[2, i] + prods[1, i + 1] + prods[0, i + 1], slope[2 * i + 2])
+        place(2 * i, prods[2, i] + prods[1, i] + prods[0, i + 1], slope[2 * i - 1])
+        place(2 * i + 1, prods[2, i] + prods[1, i + 1] + prods[0, i + 1], slope[2 * i])
         return carry
 
-    lax.fori_loop(0, pooled - 1, pair, 0)
-    final = prods[2, pooled - 1]
-    place(rows, final + prods[1, pooled - 1] + ends[2], slope[rows - 1])
-    place(rows + 1, (final + ends[3] + ends[2]) * outside, halo_slope(bottom))
+    lax.fori_loop(1, pooled, pair, 0)
+    final, below = prods[2, pooled], prods[0, pooled + 1]
+    place(rows, final + prods[1, pooled] + below, slope[rows - 1])
+    place(rows + 1, (final + prods[1, pooled + 1] + below) * outside, halo_slope(bottom))
 
     is_first = jnp.where(first, 1.0, 0.0).astype(BF16)
     not_first = jnp.where(first, 0.0, 1.0).astype(BF16)
@@ -229,18 +235,11 @@
             for part in range(per_tap):
                 put((3 * a + b) * per_tap + part, total[part * unit:(part + 1) * unit])
 
-    head = spread[0]
-    spread[0] = head * not_first
-    spread[rows + 2] = head * is_first
-    folded = dot(fields_t[:, :half], spread[rows + 2])
-    for a in range(3):
-        around = spread[2 - a:2 - a + rows].reshape(rows * half, 4 * c1)
-        got = dot(fields_t[...], around)
-        if a == 0:
-            got = got + folded
+    got = dot(fields_t[...], spread[...].reshape((rows + 2) * half, 4 * c1))
+    for a in range(3):
         for b in range(3):
-            even = got[:c0, (2 - b) * c1:(3 - b) * c1]
-            odd = got[c0:, (3 - b) * c1:(4 - b) * c1]
+            even = got[2 * a * c0:(2 * a + 1) * c0, (2 - b) * c1:(3 - b) * c1]
+            odd = got[(2 * a + 1) * c0:(2 * a + 2) * c0, (3 - b) * c1:(4 - b) * c1]
             put(9 * per_tap + 3 * a + b, even + odd)
     if keep.shape[0] > count * unit:
         keep[count * unit:] = jnp.zeros((keep.shape[0] - count * unit, c1), F32)
@@ -252,7 +251,7 @@
     c1 = act_ends.shape[2]
     rows = act_ends.shape[1]
     pooled = rows // 2
-    c0 = field_ends.shape[0] // 2
+    c0 = field_ends.shape[0] // 6
     span, size = raw_ends.shape[1], col_a.shape[0]
     got_a, got_b = col_a[...].astype(F32), col_b[...].astype(F32)
     message = jnp.concatenate([jnp.where(core == 0, got_b, got_a), jnp.where(core == 0, got_a, got_b)], 1)
@@ -277,34 +276,37 @@
     saved = dot(one_at(jnp.logical_and(k == place, n < rows + 2)), message)
     incline = slope_of(saved, cdf_of(saved))
 
-    head = lax.broadcasted_iota(jnp.int32, (span, 2 * c1), 0) < 2
-    turned = jnp.logical_and(head, first)
+    row = lax.broadcasted_iota(jnp.int32, (span, 2 * c1), 0)
+    turned = jnp.logical_and(row < 2, first)
+    sides, inner = ([x[a * span:(a + 1) * span] for a in range(3)] for x in (beside, within))
+    over, over_inner = (jnp.where(turned, x[2], 0.0) for x in (sides, inner))
+    sides[2], inner[2] = (jnp.where(turned, 0.0, x[2]) for x in (sides, inner))
+    rights = sides + [over]
     lhs[...] = jnp.zeros_like(lhs)
-    rights = []
-    for a in range(4):
-        sides, inner = (x[min(a, 2) * span:(min(a, 2) + 1) * span] for x in (beside, within))
-        if a == 2:
-            sides, inner = jnp.where(turned, 0.0, sides), jnp.where(turned, 0.0, inner)
-        if a == 3:
-            sides, inner = jnp.where(turned, sides, 0.0), jnp.where(turned, inner, 0.0)
-        rights.append(sides)
-        sides, inner = sides.astype(BF16), inner.astype(BF16)
-        left, right = sides[:, :c1], sides[:, c1:]
+    for a in range(3):
+        one, two = sides[a], inner[a]
+        if a == 0:
+            one, two = one + pltpu.roll(over, span - 8, 0), two + pltpu.roll(over_inner, span - 8, 0)
+        one, two = one.astype(BF16), two.astype(BF16)
+        left, right = one[:, :c1], one[:, c1:]
         lhs[a, :span, c1:2 * c1] = left
-        lhs[a, :span, 2 * c1:3 * c1] = inner[:, :c1]
+        lhs[a, :span, 2 * c1:3 * c1] = two[:, :c1]
         lhs[a, :span, 3 * c1:] = left
         lhs[a, span:2 * span, :c1] = left
-        lhs[a, 2 * span:3 * span, :c1] = inner[:, c1:]
+        lhs[a, 2 * span:3 * span, :c1] = two[:, c1:]
         lhs[a, 2 * span:3 * span, c1:2 * c1] = right
         lhs[a, 2 * span:3 * span, 3 * c1:] = right
         lhs[a, 3 * span:, 2 * c1:3 * c1] = right
-    found = dot_nt(lhs[0], taps[0]) + dot_nt(lhs[1], taps[1]) + dot_nt(lhs[2], taps[2]) + dot_nt(lhs[3], taps[0])
+    found = dot_nt(lhs[0], taps[0]) + dot_nt(lhs[1], taps[1]) + dot_nt(lhs[2], taps[2])
+    head = lax.broadcasted_iota(jnp.int32, (span, 2 * c1), 0) < 2
+    found = [found[k * span:(k + 1) * span] for k in range(4)]
+    found = [x + jnp.where(head, pltpu.roll(x, 8, 0), 0.0) for x in found]
     row = lax.broadcasted_iota(jnp.int32, (span, c1), 0)
     inside = jnp.where(jnp.logical_or(row > rows + 1, jnp.logical_and(row == rows + 1, last)), 0.0, 1.0)
-    values[0] = found[:span, c1:] * incline[:, :c1] * inside
-    values[1] = (raw_ends[0] + found[span:2 * span, :c1]) * slope_ends[0] * inside
-    values[2] = (raw_ends[1] + found[3 * span:, c1:]) * slope_ends[1] * inside
-    values[3] = found[2 * span:3 * span, :c1] * incline[:, c1:] * inside
+    values[0] = found[0][:, c1:] * incline[:, :c1] * inside
+    values[1] = (raw_ends[0] + found[1][:, :c1]) * slope_ends[0] * inside
+    values[2] = (raw_ends[1] + found[3][:, c1:]) * slope_ends[1] * inside
+    values[3] = found[2][:, :c1] * incline[:, c1:] * inside
     ends[...] = values[...].astype(BF16)
 
     total[...] = keep[...]
@@ -319,23 +321,13 @@
             low = (3 * a + b) * c1
             total[low:low + c1] = total[low:low + c1] + term
     right_hand[...] = jnp.zeros_like(right_hand)
-    top = lax.broadcasted_iota(jnp.int32, (rows, c1), 0) == 0
-    over = jnp.logical_and(top, first)
-    for a in range(4):
-        for j in range(4):
-            value = values[j, 2 - min(a, 2):2 - min(a, 2) + rows]
-            if a == 2:
-                value = jnp.where(over, 0.0, value)
-            if a == 3:
-                value = jnp.where(over, value, 0.0)
-            right_hand[a, j // 2 * rows:(j // 2 + 1) * rows, j * c1:(j + 1) * c1] = value.astype(BF16)
-    for a in range(3):
-        got = dot(field_ends[...], right_hand[a])
-        if a == 0:
-            got = got + dot(field_ends[...], right_hand[3])
+    for j in range(4):
+        right_hand[j // 2 * span:(j // 2 + 1) * span, j * c1:(j + 1) * c1] = ends[j]
+    got = dot(field_ends[...], right_hand[...])
+    for a in range(3):
         for b in range(3):
-            even = got[:c0, (2 - b) * c1:(3 - b) * c1]
-            odd = got[c0:, (3 - b) * c1:(4 - b) * c1]
+            even = got[2 * a * c0:(2 * a + 1) * c0, (2 - b) * c1:(3 - b) * c1]
+            odd = got[(2 * a + 1) * c0:(2 * a + 2) * c0, (3 - b) * c1:(4 - b) * c1]
             low = 9 * c1 + (3 * a + b) * c0
             total[low:low + c0] = total[low:low + c0] + even + odd
 
@@ -354,7 +346,8 @@
     c2 = 2 * c0
     depth = spread.shape[2]
     first = position(lats)[1]
-    spread[...] = part[...]
+    spread[:rows + 2] = part[...]
+    spread[rows + 2] = part[0]
     c1 = depth // 4
     for j in range(4):
         values[:, j * c1:(j + 1) * c1] = ends[j].astype(F32)
@@ -364,10 +357,10 @@
         for side, (low, spot) in enumerate(((0, 0), (half - 16, 15))):
             lanes = slice(2 * side * c1, 2 * (side + 1) * c1)
             new = values[n:n + 1, lanes]
-            if n == 0:
-                new = jnp.where(first == (r != 0), new, 0.0)
             tile = spread[r, low:low + 16, lanes].astype(F32)
             spread[r, low:low + 16, lanes] = jnp.where(at == spot, new, tile).astype(BF16)
+    spread[0] = spread[0] * one_at(~first)
+    spread[rows + 2] = spread[rows + 2] * one_at(first)
     result = dot_nt(taps[:c2], spread[2:rows + 2].reshape(rows * half, depth))
     for a in (1, 2):
         result = result + dot_nt(taps[a * c2:(a + 1) * c2],
@@ -429,6 +422,7 @@
     even = lax.rem(band, 2) == 0
 
     edge = -(-(rows + pooled + 4) // 16) * 16
+    reach = -(-(rows + 10) // 16) * 16
     row_a, row_b, col_a, col_b, held_pre = pl.pallas_call(
         functools.partial(pack_kernel, lats),
         out_shape=(
@@ -478,8 +472,8 @@
     fields_t, field_ends, taps_first, taps_second = pl.pallas_call(
         layout_kernel,
         out_shape=(
-            shape((2 * c0, rows * half), BF16),
-            shape((2 * c0, 2 * rows), BF16),
+            shape((6 * c0, (rows + 2) * half), BF16),
+            shape((6 * c0, 2 * reach), BF16),
             shape((6 * c0, 4 * c1), BF16),
             shape((3, 2 * c1, 4 * c1), BF16),
         ),
@@ -505,11 +499,10 @@
 
     block = -(-9 * (c1 + c0) // (32 * lats)) * 16
     held = lats * block
-    reach = -(-(rows + 2) // 16) * 16
     spread, keep, raw_ends, slope_ends, out_ends = pl.pallas_call(
         functools.partial(middle_kernel, lats),
         out_shape=(
-            shape((rows + 3, half, 4 * c1), BF16),
+            shape((rows + 2, half, 4 * c1), BF16),
             shape((2 * held, c1), F32),
             shape((2, reach, c1), F32),
             shape((2, reach, c1), F32),
@@ -520,8 +513,7 @@
         scratch_shapes=[
             pltpu.VMEM((pooled + 2, half, c1), F32),
             pltpu.VMEM((pooled + 2, half, 4 * c1), BF16),
-            pltpu.VMEM((3, pooled, half, 2 * c1), F32),
-            pltpu.VMEM((4, half, 2 * c1), F32),
+            pltpu.VMEM((3, pooled + 2, half, 2 * c1), F32),
             pltpu.VMEM((cols, c1), F32),
             pltpu.VMEM((4, 2 * c1, 3 * c1), F32),
             pltpu.VMEM((2 * c1, 3 * c1), F32),
@@ -542,9 +534,9 @@
         in_specs=vmem(9),
         out_specs=tuple(vmem(3)),
         scratch_shapes=[
-            pltpu.VMEM((4, 4 * reach, 4 * c1), BF16),
+            pltpu.VMEM((3, 4 * reach, 4 * c1), BF16),
             pltpu.VMEM((4, reach, c1), F32),
-            pltpu.VMEM((4, 2 * rows, 4 * c1), BF16),
+            pltpu.VMEM((2 * reach, 4 * c1), BF16),
             pltpu.VMEM((2 * held, c1), F32),
         ],
         compiler_params=params(16),

time: 41.8 us -> 41.8 us (level)
  transfers between devices with their start and end apart: 15 -> 15, of which waited for: 12 -> 12; matrix products, arithmetic and copies ran while one was open for 0% -> 0% of each run, Pallas kernels for 15% -> 16%
where the time goes in v18:
time: 41.8 us; the launch traced here: 41.7 us
  starting transfers between devices  16 us (38%)
  waiting for transfers between devices  14.6 us (35%)
  Pallas kernels  9.85 us (24%)
  between operations  0.79 us (2%)
    ppermute x9, starting transfers between devices, between_chips(): lax.ppermute(value, AREA, [(i * lons + j, (i ^ over_lat) * lons + (j ^ 2...  9.57 us
    ppermute x9, waiting for transfers between devices, between_chips(): lax.ppermute(value, AREA, [(i * lons + j, (i ^ over_lat) * lons + (j ^ 2...  9.16 us
    ppermute x1, starting transfers between devices, body(): row_b = lax.ppermute(row_b, AREA, pairs)  4.1 us
    pallas_call x1, Pallas kernels, body(): pl.pallas_call(functools.partial(middle_kernel, lats), out_shape=(shape((...  2.61 us
    pallas_call x1, Pallas kernels, body(): pl.pallas_call(functools.partial(last_kernel, lats), out_shape=shape((row...  2.16 us
    ppermute x1, waiting for transfers between devices, body(): parts = (own + lax.ppermute(other, 'lon', swap)).reshape(lats, block, c1)  1.8 us
    ppermute x1, waiting for transfers between devices, body(): row_a = lax.ppermute(row_a, AREA, every)  1.49 us
    ppermute x1, waiting for transfers between devices, body(): theirs = lax.ppermute(mine, 'lon', swap)  1.37 us
  transfers between devices with their start and end apart: 15, of which 12 were waited for; matrix products, arithmetic and copies ran while one was open for 0% of the time, Pallas kernels for 16%

profile of v18, /device:TPU:0, one launch (start us, length us, event | category | flops | bytes accessed | tf_op | source)
XLA Modules:
  0.0 41.7 jit_solution(5029135233106490794)
XLA Ops:
  0.6 0.0 copy-start
  0.6 0.0 copy-start.2
  0.7 0.0 copy-start.1
  0.7 1.2 %shard_map.76 = (bf16[192,128]{1,0:T(8,128)(2,1)S(1)}, bf16[192,128]{1,0:T(8,128)(2,1)S(1)}, bf16[32,128]{1,0:T(8,128)(2,1)S(1)}, bf16[32,128]{1,0:T(8,128)(2,1)S(1)}, bf16[16,128,128]{2,1,0:T(8,128)(2,1)S(1)}) custom-call(bf16[16,128,128]{2,1,0:T(8,128)(2,1)} %pre_far.1, bf16[8,64,128]{2,1,0:T(8,128)(2,1)} %grad_out.1), custom_call_target="tpu_custom_call" | custom-call | flops 1000 | bytes 262144 | tf_op jit(solution)/shard_map/pallas_call | solution.py:426
  1.8 0.0 copy-start.3
  1.9 4.1 %collective-permute-start = (bf16[192,128]{1,0:T(8,128)(2,1)S(1)}, bf16[192,128]{1,0:T(8,128)(2,1)S(1)}, u32[]{:S(2)}, u32[]{:S(2)}) collective-permute-start(bf16[192,128]{1,0:T(8,128)(2,1)S(1)} %get-tuple-element.41), channel_id=1, source_target_pairs={{0,4},{1,5},{2,6},{3,7},{4,0},{5,1},{6,2},{7,3},{24,25},{25,24},{2... | collective-permute-start | bytes 147464 | tf_op jit(solution)/shard_map/ppermute | solution.py:451
  6.0 0.4 collective-permute-start.1
  6.4 0.1 pad.9.clone
  6.4 0.9 %shard_map.77 = (f32[16,64,256]{2,1,0:T(8,128)S(1)}, bf16[2,256,512]{2,1,0:T(8,128)(2,1)S(1)}, f32[2,16,128]{2,1,0:T(8,128)S(1)}) custom-call(bf16[16,128,128]{2,1,0:T(8,128)(2,1)S(1)} %get-tuple-element.43.pre), custom_call_target="tpu_custom_call" | custom-call | flops 15728640 | bytes 2097152 | tf_op jit(solution)/shard_map/pallas_call | solution.py:454
  7.4 0.0 copy-done
  7.4 0.0 copy-done.2
  7.4 0.0 copy-done.1
  7.4 0.9 %shard_map.78 = (bf16[384,1152]{1,0:T(8,128)(2,1)S(1)}, bf16[384,64]{1,0:T(8,128)(2,1)S(1)}, bf16[384,512]{1,0:T(8,128)(2,1)S(1)}, bf16[3,256,512]{2,1,0:T(8,128)(2,1)S(1)}) custom-call(bf16[16,64,128]{2,1,0:T(8,128)(2,1)S(1)} %bitcast.8, bf16[3,3,64,128]{3,2,1,0:T(8,128)(2,1)S(1)} %copy-done.2, bf16[3,3,128,128]{3,2,1,0:T(8,128)(2,1)S(1)} %copy-done), custom_call_target="tpu_custom_call" | custom-call | flops 67108864 | bytes 3145728 | tf_op jit(solution)/shard_map/pallas_call | solution.py:472
  8.3 0.2 collective-permute-done.row_b
  8.5 1.5 %collective-permute-done.1.row_a = bf16[192,128]{1,0:T(8,128)(2,1)S(1)} collective-permute-done((bf16[192,128]{1,0:T(8,128)(2,1)S(1)}, bf16[192,128]{1,0:T(8,128)(2,1)S(1)}, u32[]{:S(2)}, u32[]{:S(2)}) %collective-permute-start.1) | collective-permute-done | bytes 49184 | tf_op jit(solution)/shard_map/ppermute | solution.py:452
  10.1 0.1 maximum_maximum_fusion.1
  10.2 0.8 %collective-permute-start.3 = (bf16[32,128]{1,0:T(8,128)(2,1)S(1)}, bf16[32,128]{1,0:T(8,128)(2,1)S(1)}, u32[]{:S(2)}, u32[]{:S(2)}) collective-permute-start(bf16[32,128]{1,0:T(8,128)(2,1)S(1)} %get-tuple-element.94), channel_id=1, source_target_pairs={{0,7},{1,2},{2,1},{3,4},{4,3},{5,6},{6,5},{7,0},{8,15},{9,10},{10,... | collective-permute-start | bytes 24584 | tf_op jit(solution)/shard_map/ppermute | solution.py:497
  11.0 0.9 %collective-permute-start.2 = (bf16[32,128]{1,0:T(8,128)(2,1)S(1)}, bf16[32,128]{1,0:T(8,128)(2,1)S(1)}, u32[]{:S(2)}, u32[]{:S(2)}) collective-permute-start(bf16[32,128]{1,0:T(8,128)(2,1)S(1)} %get-tuple-element.95), channel_id=1, source_target_pairs={{0,1},{1,0},{2,3},{3,2},{4,5},{5,4},{6,7},{7,6},{8,9},{9,8},{10,11... | collective-permute-start | bytes 24584 | tf_op jit(solution)/shard_map/ppermute | solution.py:498
  11.9 0.0 copy-done.3
  11.9 2.6 %shard_map.79 = (bf16[18,64,512]{2,1,0:T(8,128)(2,1)S(1)}, f32[1792,128]{1,0:T(8,128)S(1)}, f32[2,32,128]{2,1,0:T(8,128)S(1)}, f32[2,32,128]{2,1,0:T(8,128)S(1)}, f32[2,16,128]{2,1,0:T(8,128)S(1)}) custom-call(bf16[8,64,128]{2,1,0:T(8,128)(2,1)S(1)} %copy-done.3, bf16[192,128]{1,0:T(8,128)(2,1)S(1)} %collective-permute-done.1.row_a, ...), custom_call_target="tpu_custom_call" | custom-call | flops 1509949440 | bytes 8388608 | tf_op jit(solution)/shard_map/pallas_call | solution.py:502
  14.5 0.6 %collective-permute-done.3.col_b = bf16[32,128]{1,0:T(8,128)(2,1)S(1)} collective-permute-done((bf16[32,128]{1,0:T(8,128)(2,1)S(1)}, bf16[32,128]{1,0:T(8,128)(2,1)S(1)}, u32[]{:S(2)}, u32[]{:S(2)}) %collective-permute-start.3) | collective-permute-done | bytes 8224 | tf_op jit(solution)/shard_map/ppermute | solution.py:497
  15.1 0.0 collective-permute-done.2.col_a
  15.1 1.1 %shard_map.80 = (bf16[4,32,128]{2,1,0:T(8,128)(2,1)S(1)}, f32[896,128]{1,0:T(8,128)S(1)}, f32[896,128]{1,0:T(8,128)S(1)}) custom-call(bf16[32,128]{1,0:T(8,128)(2,1)S(1)} %collective-permute-done.2.col_a, bf16[32,128]{1,0:T(8,128)(2,1)S(1)} %collective-permute-done.3.col_b, f32[2,16,128]{2,1,0:T(8,128)S(1)} %get-tuple-element.56.act_ends, ...), custom_call_target="tpu_custom_call" | custom-call | flops 268435456 | bytes 3145728 | tf_op jit(solution)/shard_map/pallas_call | solution.py:527
  16.1 0.1 collective-permute-start.4
  16.2 1.8 %collective-permute-done.4 = f32[896,128]{1,0:T(8,128)S(1)} collective-permute-done((f32[896,128]{1,0:T(8,128)S(1)}, f32[896,128]{1,0:T(8,128)S(1)}, u32[]{:S(2)}, u32[]{:S(2)}) %collective-permute-start.4) | collective-permute-done | bytes 458784 | tf_op jit(solution)/shard_map/ppermute | solution.py:553
  18.0 0.1 fusion.3
  18.1 0.7 %collective-permute-start.5 = (bf16[224,128]{1,0:T(8,128)(2,1)S(1)}, bf16[224,128]{1,0:T(8,128)(2,1)S(1)}, u32[]{:S(2)}, u32[]{:S(2)}) collective-permute-start(bf16[224,128]{1,0:T(8,128)(2,1)S(1)} %get-tuple-element.65), channel_id=1, source_target_pairs={{0,24},{1,25},{2,26},{3,27},{4,28},{5,29},{6,30},{7,31},{8,16},{9,... | collective-permute-start | bytes 172040 | tf_op jit(solution)/shard_map/ppermute | solution.py:550
  18.8 0.7 %collective-permute-start.6 = (bf16[224,128]{1,0:T(8,128)(2,1)S(1)}, bf16[224,128]{1,0:T(8,128)(2,1)S(1)}, u32[]{:S(2)}, u32[]{:S(2)}) collective-permute-start(bf16[224,128]{1,0:T(8,128)(2,1)S(1)} %get-tuple-element.66), channel_id=1, source_target_pairs={{0,17},{1,16},{2,19},{3,18},{4,21},{5,20},{6,23},{7,22},{8,25},{9,... | collective-permute-start | bytes 172040 | tf_op jit(solution)/shard_map/ppermute | solution.py:550
  19.5 1.9 %collective-permute-start.7 = (bf16[224,128]{1,0:T(8,128)(2,1)S(1)}, bf16[224,128]{1,0:T(8,128)(2,1)S(1)}, u32[]{:S(2)}, u32[]{:S(2)}) collective-permute-start(bf16[224,128]{1,0:T(8,128)(2,1)S(1)} %get-tuple-element.67), channel_id=1, source_target_pairs={{0,9},{1,8},{2,11},{3,10},{4,13},{5,12},{6,15},{7,14},{8,1},{9,0},... | collective-permute-start | bytes 172040 | tf_op jit(solution)/shard_map/ppermute | solution.py:550
  21.4 2.2 %shard_map.81 = bf16[16,64,128]{2,1,0:T(8,128)(2,1)} custom-call(bf16[18,64,512]{2,1,0:T(8,128)(2,1)S(1)} %get-tuple-element.68.part, bf16[4,32,128]{2,1,0:T(8,128)(2,1)S(1)} %get-tuple-element.69.ends, bf16[384,512]{1,0:T(8,128)(2,1)S(1)} %get-tuple-element.70.taps), custom_call_target="tpu_custom_call" | custom-call | flops 301989888 | bytes 3145728 | tf_op jit(solution)/shard_map/pallas_call | solution.py:557
  23.5 0.1 collective-permute-done.5
  23.6 0.4 %collective-permute-done.6 = bf16[224,128]{1,0:T(8,128)(2,1)S(1)} collective-permute-done((bf16[224,128]{1,0:T(8,128)(2,1)S(1)}, bf16[224,128]{1,0:T(8,128)(2,1)S(1)}, u32[]{:S(2)}, u32[]{:S(2)}) %collective-permute-start.6) | collective-permute-done | bytes 57376 | tf_op jit(solution)/shard_map/ppermute | solution.py:550
  24.1 0.0 collective-permute-done.7
  24.1 1.4 %collective-permute-start.10 = (bf16[224,128]{1,0:T(8,128)(2,1)S(1)}, bf16[224,128]{1,0:T(8,128)(2,1)S(1)}, u32[]{:S(2)}, u32[]{:S(2)}) collective-permute-start(bf16[224,128]{1,0:T(8,128)(2,1)S(1)} %fusion.2), channel_id=1, source_target_pairs={{0,5},{1,4},{2,7},{3,6},{4,1},{5,0},{6,3},{7,2},{8,13},{9,12},{10,... | collective-permute-start | bytes 172040 | tf_op jit(solution)/shard_map/ppermute | solution.py:550
  25.5 1.4 %collective-permute-start.9 = (bf16[224,128]{1,0:T(8,128)(2,1)S(1)}, bf16[224,128]{1,0:T(8,128)(2,1)S(1)}, u32[]{:S(2)}, u32[]{:S(2)}) collective-permute-start(bf16[224,128]{1,0:T(8,128)(2,1)S(1)} %fusion.2), channel_id=1, source_target_pairs={{0,6},{1,7},{2,4},{3,5},{4,2},{5,3},{6,0},{7,1},{8,14},{9,15},{10,... | collective-permute-start | bytes 172040 | tf_op jit(solution)/shard_map/ppermute | solution.py:550
  26.9 0.3 collective-permute-start.8
  27.1 3.9 %collective-permute-done.10 = bf16[224,128]{1,0:T(8,128)(2,1)S(1)} collective-permute-done((bf16[224,128]{1,0:T(8,128)(2,1)S(1)}, bf16[224,128]{1,0:T(8,128)(2,1)S(1)}, u32[]{:S(2)}, u32[]{:S(2)}) %collective-permute-start.10) | collective-permute-done | bytes 57376 | tf_op jit(solution)/shard_map/ppermute | solution.py:550
  31.1 0.9 %collective-permute-done.9 = bf16[224,128]{1,0:T(8,128)(2,1)S(1)} collective-permute-done((bf16[224,128]{1,0:T(8,128)(2,1)S(1)}, bf16[224,128]{1,0:T(8,128)(2,1)S(1)}, u32[]{:S(2)}, u32[]{:S(2)}) %collective-permute-start.9) | collective-permute-done | bytes 57376 | tf_op jit(solution)/shard_map/ppermute | solution.py:550
  31.9 0.9 %collective-permute-done.8 = bf16[224,128]{1,0:T(8,128)(2,1)S(1)} collective-permute-done((bf16[224,128]{1,0:T(8,128)(2,1)S(1)}, bf16[224,128]{1,0:T(8,128)(2,1)S(1)}, u32[]{:S(2)}, u32[]{:S(2)}) %collective-permute-start.8) | collective-permute-done | bytes 57376 | tf_op jit(solution)/shard_map/ppermute | solution.py:550
  32.8 1.5 %collective-permute-start.13 = (bf16[224,128]{1,0:T(8,128)(2,1)S(1)}, bf16[224,128]{1,0:T(8,128)(2,1)S(1)}, u32[]{:S(2)}, u32[]{:S(2)}) collective-permute-start(bf16[224,128]{1,0:T(8,128)(2,1)S(1)} %add_convert_fusion), channel_id=1, source_target_pairs={{0,24},{1,25},{2,26},{3,27},{4,28},{5,29},{6,30},{7,31},{8,16},{9,... | collective-permute-start | bytes 172040 | tf_op jit(solution)/shard_map/ppermute | solution.py:550
  34.3 0.4 %collective-permute-start.12 = (bf16[224,128]{1,0:T(8,128)(2,1)S(1)}, bf16[224,128]{1,0:T(8,128)(2,1)S(1)}, u32[]{:S(2)}, u32[]{:S(2)}) collective-permute-start(bf16[224,128]{1,0:T(8,128)(2,1)S(1)} %add_convert_fusion), channel_id=1, source_target_pairs={{0,17},{1,16},{2,19},{3,18},{4,21},{5,20},{6,23},{7,22},{8,25},{9,... | collective-permute-start | bytes 172040 | tf_op jit(solution)/shard_map/ppermute | solution.py:550
  34.7 1.4 %collective-permute-start.11 = (bf16[224,128]{1,0:T(8,128)(2,1)S(1)}, bf16[224,128]{1,0:T(8,128)(2,1)S(1)}, u32[]{:S(2)}, u32[]{:S(2)}) collective-permute-start(bf16[224,128]{1,0:T(8,128)(2,1)S(1)} %add_convert_fusion), channel_id=1, source_target_pairs={{0,9},{1,8},{2,11},{3,10},{4,13},{5,12},{6,15},{7,14},{8,1},{9,0},... | collective-permute-start | bytes 172040 | tf_op jit(solution)/shard_map/ppermute | solution.py:550
  36.1 2.0 %collective-permute-done.13 = bf16[224,128]{1,0:T(8,128)(2,1)S(1)} collective-permute-done((bf16[224,128]{1,0:T(8,128)(2,1)S(1)}, bf16[224,128]{1,0:T(8,128)(2,1)S(1)}, u32[]{:S(2)}, u32[]{:S(2)}) %collective-permute-start.13) | collective-permute-done | bytes 57376 | tf_op jit(solution)/shard_map/ppermute | solution.py:550
  38.1 1.0 %collective-permute-done.12 = bf16[224,128]{1,0:T(8,128)(2,1)S(1)} collective-permute-done((bf16[224,128]{1,0:T(8,128)(2,1)S(1)}, bf16[224,128]{1,0:T(8,128)(2,1)S(1)}, u32[]{:S(2)}, u32[]{:S(2)}) %collective-permute-start.12) | collective-permute-done | bytes 57376 | tf_op jit(solution)/shard_map/ppermute | solution.py:550
  39.1 0.0 collective-permute-done.11
  39.1 0.2 collective-permute-start.14
  39.3 1.4 %collective-permute-done.14.theirs = bf16[4,224,128]{2,1,0:T(8,128)(2,1)S(1)} collective-permute-done((bf16[4,224,128]{2,1,0:T(8,128)(2,1)S(1)}, bf16[4,224,128]{2,1,0:T(8,128)(2,1)S(1)}, u32[]{:S(2)}, u32[]{:S(2)}) %collective-permute-start.14) | collective-permute-done | bytes 229408 | tf_op jit(solution)/shard_map/ppermute | solution.py:582
  40.7 1.0 %shard_map.82 = (f32[576,128]{1,0:T(8,128)}, f32[1152,128]{1,0:T(8,128)}) custom-call(bf16[4,224,128]{2,1,0:T(8,128)(2,1)S(1)} %pad_maximum_fusion.mine, bf16[4,224,128]{2,1,0:T(8,128)(2,1)S(1)} %collective-permute-done.14.theirs), custom_call_target="tpu_custom_call" | custom-call | flops 1000 | bytes 1572864 | tf_op jit(solution)/shard_map/pallas_call | solution.py:584
  (10 shorter events, 0.2 us)
Async XLA Ops:
  0.6 6.8 %copy-start = (bf16[3,3,128,128]{3,2,1,0:T(8,128)(2,1)S(1)}, bf16[3,3,128,128]{3,2,1,0:T(8,128)(2,1)}, u32[]{:S(2)}) copy-start(bf16[3,3,128,128]{3,2,1,0:T(8,128)(2,1)} %w_second.1) | copy-start | bytes 884740
  0.6 6.8 %copy-start.2 = (bf16[3,3,64,128]{3,2,1,0:T(8,128)(2,1)S(1)}, bf16[3,3,64,128]{3,2,1,0:T(8,128)(2,1)}, u32[]{:S(2)}) copy-start(bf16[3,3,64,128]{3,2,1,0:T(8,128)(2,1)} %w_first.1) | copy-start | bytes 442372
  0.7 6.8 %copy-start.1 = (bf16[16,128,64]{1,2,0:T(8,128)(2,1)S(1)}, bf16[16,128,64]{1,2,0:T(8,128)(2,1)}, u32[]{:S(2)}) copy-start(bf16[16,128,64]{1,2,0:T(8,128)(2,1)} %param.5) | copy-start | bytes 786436
  1.8 10.0 %copy-start.3 = (bf16[8,64,128]{2,1,0:T(8,128)(2,1)S(1)}, bf16[8,64,128]{2,1,0:T(8,128)(2,1)}, u32[]{:S(2)}) copy-start(bf16[8,64,128]{2,1,0:T(8,128)(2,1)} %grad_out.1) | copy-start | bytes 393220
  1.9 6.7 %collective-permute-start = (bf16[192,128]{1,0:T(8,128)(2,1)S(1)}, bf16[192,128]{1,0:T(8,128)(2,1)S(1)}, u32[]{:S(2)}, u32[]{:S(2)}) collective-permute-start(bf16[192,128]{1,0:T(8,128)(2,1)S(1)} %get-tuple-element.41), channel_id=1, source_target_pairs={{0,4},{1,5},{2,6},{3,7},{4,0},{5,1},{6,2},{7,3},{24,25},{25,24},{2... | collective-permute-start | bytes 147464 | tf_op jit(solution)/shard_map/ppermute | solution.py:451
  6.0 4.1 %collective-permute-start.1 = (bf16[192,128]{1,0:T(8,128)(2,1)S(1)}, bf16[192,128]{1,0:T(8,128)(2,1)S(1)}, u32[]{:S(2)}, u32[]{:S(2)}) collective-permute-start(bf16[192,128]{1,0:T(8,128)(2,1)S(1)} %get-tuple-element.42), channel_id=1, source_target_pairs={{0,8},{1,9},{2,10},{3,11},{4,12},{5,13},{6,14},{7,15},{8,0},{9,1},... | collective-permute-start | bytes 147464 | tf_op jit(solution)/shard_map/ppermute | solution.py:452
  10.2 4.9 %collective-permute-start.3 = (bf16[32,128]{1,0:T(8,128)(2,1)S(1)}, bf16[32,128]{1,0:T(8,128)(2,1)S(1)}, u32[]{:S(2)}, u32[]{:S(2)}) collective-permute-start(bf16[32,128]{1,0:T(8,128)(2,1)S(1)} %get-tuple-element.94), channel_id=1, source_target_pairs={{0,7},{1,2},{2,1},{3,4},{4,3},{5,6},{6,5},{7,0},{8,15},{9,10},{10,... | collective-permute-start | bytes 24584 | tf_op jit(solution)/shard_map/ppermute | solution.py:497
  11.0 4.1 %collective-permute-start.2 = (bf16[32,128]{1,0:T(8,128)(2,1)S(1)}, bf16[32,128]{1,0:T(8,128)(2,1)S(1)}, u32[]{:S(2)}, u32[]{:S(2)}) collective-permute-start(bf16[32,128]{1,0:T(8,128)(2,1)S(1)} %get-tuple-element.95), channel_id=1, source_target_pairs={{0,1},{1,0},{2,3},{3,2},{4,5},{5,4},{6,7},{7,6},{8,9},{9,8},{10,11... | collective-permute-start | bytes 24584 | tf_op jit(solution)/shard_map/ppermute | solution.py:498
  16.1 1.9 %collective-permute-start.4 = (f32[896,128]{1,0:T(8,128)S(1)}, f32[896,128]{1,0:T(8,128)S(1)}, u32[]{:S(2)}, u32[]{:S(2)}) collective-permute-start(f32[896,128]{1,0:T(8,128)S(1)} %get-tuple-element.63), channel_id=1, source_target_pairs={{0,1},{1,0},{2,3},{3,2},{4,5},{5,4},{6,7},{7,6},{8,9},{9,8},{10,11... | collective-permute-start | bytes 1376264 | tf_op jit(solution)/shard_map/ppermute | solution.py:553
  18.1 5.5 %collective-permute-start.5 = (bf16[224,128]{1,0:T(8,128)(2,1)S(1)}, bf16[224,128]{1,0:T(8,128)(2,1)S(1)}, u32[]{:S(2)}, u32[]{:S(2)}) collective-permute-start(bf16[224,128]{1,0:T(8,128)(2,1)S(1)} %get-tuple-element.65), channel_id=1, source_target_pairs={{0,24},{1,25},{2,26},{3,27},{4,28},{5,29},{6,30},{7,31},{8,16},{9,... | collective-permute-start | bytes 172040 | tf_op jit(solution)/shard_map/ppermute | solution.py:550
  18.8 5.3 %collective-permute-start.6 = (bf16[224,128]{1,0:T(8,128)(2,1)S(1)}, bf16[224,128]{1,0:T(8,128)(2,1)S(1)}, u32[]{:S(2)}, u32[]{:S(2)}) collective-permute-start(bf16[224,128]{1,0:T(8,128)(2,1)S(1)} %get-tuple-element.66), channel_id=1, source_target_pairs={{0,17},{1,16},{2,19},{3,18},{4,21},{5,20},{6,23},{7,22},{8,25},{9,... | collective-permute-start | bytes 172040 | tf_op jit(solution)/shard_map/ppermute | solution.py:550
  19.5 4.6 %collective-permute-start.7 = (bf16[224,128]{1,0:T(8,128)(2,1)S(1)}, bf16[224,128]{1,0:T(8,128)(2,1)S(1)}, u32[]{:S(2)}, u32[]{:S(2)}) collective-permute-start(bf16[224,128]{1,0:T(8,128)(2,1)S(1)} %get-tuple-element.67), channel_id=1, source_target_pairs={{0,9},{1,8},{2,11},{3,10},{4,13},{5,12},{6,15},{7,14},{8,1},{9,0},... | collective-permute-start | bytes 172040 | tf_op jit(solution)/shard_map/ppermute | solution.py:550
  24.1 7.0 %collective-permute-start.10 = (bf16[224,128]{1,0:T(8,128)(2,1)S(1)}, bf16[224,128]{1,0:T(8,128)(2,1)S(1)}, u32[]{:S(2)}, u32[]{:S(2)}) collective-permute-start(bf16[224,128]{1,0:T(8,128)(2,1)S(1)} %fusion.2), channel_id=1, source_target_pairs={{0,5},{1,4},{2,7},{3,6},{4,1},{5,0},{6,3},{7,2},{8,13},{9,12},{10,... | collective-permute-start | bytes 172040 | tf_op jit(solution)/shard_map/ppermute | solution.py:550
  25.5 6.4 %collective-permute-start.9 = (bf16[224,128]{1,0:T(8,128)(2,1)S(1)}, bf16[224,128]{1,0:T(8,128)(2,1)S(1)}, u32[]{:S(2)}, u32[]{:S(2)}) collective-permute-start(bf16[224,128]{1,0:T(8,128)(2,1)S(1)} %fusion.2), channel_id=1, source_target_pairs={{0,6},{1,7},{2,4},{3,5},{4,2},{5,3},{6,0},{7,1},{8,14},{9,15},{10,... | collective-permute-start | bytes 172040 | tf_op jit(solution)/shard_map/ppermute | solution.py:550
  26.9 5.9 %collective-permute-start.8 = (bf16[224,128]{1,0:T(8,128)(2,1)S(1)}, bf16[224,128]{1,0:T(8,128)(2,1)S(1)}, u32[]{:S(2)}, u32[]{:S(2)}) collective-permute-start(bf16[224,128]{1,0:T(8,128)(2,1)S(1)} %fusion.2), channel_id=1, source_target_pairs={{0,3},{1,2},{2,1},{3,0},{4,7},{5,6},{6,5},{7,4},{8,11},{9,10},{10,... | collective-permute-start | bytes 172040 | tf_op jit(solution)/shard_map/ppermute | solution.py:550
  32.8 5.2 %collective-permute-start.13 = (bf16[224,128]{1,0:T(8,128)(2,1)S(1)}, bf16[224,128]{1,0:T(8,128)(2,1)S(1)}, u32[]{:S(2)}, u32[]{:S(2)}) collective-permute-start(bf16[224,128]{1,0:T(8,128)(2,1)S(1)} %add_convert_fusion), channel_id=1, source_target_pairs={{0,24},{1,25},{2,26},{3,27},{4,28},{5,29},{6,30},{7,31},{8,16},{9,... | collective-permute-start | bytes 172040 | tf_op jit(solution)/shard_map/ppermute | solution.py:550
  34.3 4.8 %collective-permute-start.12 = (bf16[224,128]{1,0:T(8,128)(2,1)S(1)}, bf16[224,128]{1,0:T(8,128)(2,1)S(1)}, u32[]{:S(2)}, u32[]{:S(2)}) collective-permute-start(bf16[224,128]{1,0:T(8,128)(2,1)S(1)} %add_convert_fusion), channel_id=1, source_target_pairs={{0,17},{1,16},{2,19},{3,18},{4,21},{5,20},{6,23},{7,22},{8,25},{9,... | collective-permute-start | bytes 172040 | tf_op jit(solution)/shard_map/ppermute | solution.py:550
  34.7 4.4 %collective-permute-start.11 = (bf16[224,128]{1,0:T(8,128)(2,1)S(1)}, bf16[224,128]{1,0:T(8,128)(2,1)S(1)}, u32[]{:S(2)}, u32[]{:S(2)}) collective-permute-start(bf16[224,128]{1,0:T(8,128)(2,1)S(1)} %add_convert_fusion), channel_id=1, source_target_pairs={{0,9},{1,8},{2,11},{3,10},{4,13},{5,12},{6,15},{7,14},{8,1},{9,0},... | collective-permute-start | bytes 172040 | tf_op jit(solution)/shard_map/ppermute | solution.py:550
  39.1 1.6 %collective-permute-start.14 = (bf16[4,224,128]{2,1,0:T(8,128)(2,1)S(1)}, bf16[4,224,128]{2,1,0:T(8,128)(2,1)S(1)}, u32[]{:S(2)}, u32[]{:S(2)}) collective-permute-start(bf16[4,224,128]{2,1,0:T(8,128)(2,1)S(1)} %pad_maximum_fusion.mine), channel_id=1, source_target_pairs={{0,1},{1,0},{2,3},{3,2},{4,5},{5,4},{6,7},{7,6},{8,9},{9,8},{10,11... | collective-permute-start | bytes 688136 | tf_op jit(solution)/shard_map/ppermute | solution.py:582

commit v19 on v17

--- a/solution.py
+++ b/solution.py
@@ -247,7 +247,8 @@
 
 
 def columns_kernel(lats, col_a, col_b, act_ends, field_ends, taps, keep, raw_ends, slope_ends, out_ends,
-                   ends, own, other, lhs, values, right_hand, total):
+                   ends, *rest):
+    own, other, (lhs, values, right_hand, total) = rest[:lats], rest[lats:2 * lats], rest[2 * lats:]
     band, first, last, _, core = position(lats)
     c1 = act_ends.shape[2]
     rows = act_ends.shape[1]
@@ -339,13 +340,12 @@
             low = 9 * c1 + (3 * a + b) * c0
             total[low:low + c0] = total[low:low + c0] + even + odd
 
-    held = own.shape[0]
-    block = held // lats
+    block = own[0].shape[0]
     mine = half_held()
-    for target, half_of in ((own, mine), (other, 1 - mine)):
+    for targets, half_of in ((own, mine), (other, 1 - mine)):
         for far in range(lats):
-            start = half_of * held + (band ^ far) * block
-            target[far * block:(far + 1) * block] = total[pl.ds(pl.multiple_of(start, block), block), :]
+            start = (half_of * lats + (band ^ far)) * block
+            targets[far][...] = total[pl.ds(pl.multiple_of(start, block), block), :]
 
 
 def last_kernel(lats, part, ends, taps, out, spread, values, total, turned):
@@ -532,15 +532,13 @@
     )(grad_out, row_a, row_b, slope, act_t, fields_t, taps_second)
     col_a, col_b, keep = lax.optimization_barrier((col_a, col_b, keep))
 
-    ends, own, other = pl.pallas_call(
+    ends, *halves = pl.pallas_call(
         functools.partial(columns_kernel, lats),
         out_shape=(
             shape((4, reach, c1), BF16),
-            shape((held, c1), F32),
-            shape((held, c1), F32),
-        ),
+        ) + (shape((block, c1), F32),) * (2 * lats),
         in_specs=vmem(9),
-        out_specs=tuple(vmem(3)),
+        out_specs=tuple(vmem(2 * lats + 1)),
         scratch_shapes=[
             pltpu.VMEM((4, 4 * reach, 4 * c1), BF16),
             pltpu.VMEM((4, reach, c1), F32),
@@ -558,10 +556,10 @@
         return lax.ppermute(value, AREA, [
             (i * lons + j, (i ^ over_lat) * lons + (j ^ (2 * over_lon) ^ turn)) for i in range(lats) for j in range(lons)])
 
-    parts = (own + lax.ppermute(other, "lon", swap)).reshape(lats, block, c1)
-    sent = [parts[far].astype(BF16) for far in range(1, lats)]
-    *sent, ends = lax.optimization_barrier((*sent, ends))
-    got = [between_chips(sent[far - 1], far, 0) for far in reversed(range(1, lats))]
+    own, other = halves[:lats], halves[lats:]
+    other = {far: lax.ppermute(other[far], "lon", swap) for far in reversed(range(lats))}
+    parts = [own[far] + other[far] for far in range(lats)]
+    got = [between_chips(parts[far].astype(BF16), far, 0) for far in reversed(range(1, lats))]
     grad_inputs = pl.pallas_call(
         functools.partial(last_kernel, lats),
         out_shape=shape((rows, c0, cols), BF16),

time: 41.8 us -> 41.4 us (level)
  waiting for transfers between devices: 14.9 us -> 13.3 us
  starting transfers between devices: 16 us -> 17.2 us
    ppermute x1 -> x4, waiting for transfers between devices: 1.8 us -> 0.31 us  [body(): lax.ppermute(other[far], 'lon', swap)]
    ppermute x1 -> x4, starting transfers between devices: 0.07 us -> 1.08 us  [body(): lax.ppermute(other[far], 'lon', swap)]
  transfers between devices with their start and end apart: 15 -> 18, of which waited for: 12 -> 11; matrix products, arithmetic and copies ran while one was open for 0% -> 0% of each run, Pallas kernels for 15% -> 15%
where the time goes in v19:
time: 41.4 us; the launch traced here: 41.2 us
  starting transfers between devices  17.2 us (42%)
  waiting for transfers between devices  13.3 us (32%)
  Pallas kernels  9.57 us (23%)
  between operations  0.8 us (2%)
    ppermute x9, starting transfers between devices, between_chips(): lax.ppermute(value, AREA, [(i * lons + j, (i ^ over_lat) * lons + (j ^ 2...  9.71 us
    ppermute x9, waiting for transfers between devices, between_chips(): lax.ppermute(value, AREA, [(i * lons + j, (i ^ over_lat) * lons + (j ^ 2...  8.92 us
    ppermute x1, starting transfers between devices, body(): row_b = lax.ppermute(row_b, AREA, pairs)  4.1 us
    pallas_call x1, Pallas kernels, body(): pl.pallas_call(functools.partial(middle_kernel, lats), out_shape=(shape((...  2.4 us
    pallas_call x1, Pallas kernels, body(): pl.pallas_call(functools.partial(last_kernel, lats), out_shape=shape((row...  2.16 us
    ppermute x1, waiting for transfers between devices, body(): row_a = lax.ppermute(row_a, AREA, every)  1.49 us
    ppermute x1, waiting for transfers between devices, body(): theirs = lax.ppermute(mine, 'lon', swap)  1.38 us
    pallas_call x1, Pallas kernels, body(): pl.pallas_call(functools.partial(columns_kernel, lats), out_shape=(shape(...  1.19 us
  transfers between devices with their start and end apart: 18, of which 11 were waited for; matrix products, arithmetic and copies ran while one was open for 0% of the time, Pallas kernels for 15%

profile of v19, /device:TPU:0, one launch (start us, length us, event | category | flops | bytes accessed | tf_op | source)
XLA Modules:
  0.0 41.2 jit_solution(341771555091831692)
XLA Ops:
  0.6 0.0 copy-start.3
  0.6 0.0 copy-start
  0.7 0.0 copy-start.2
  0.7 0.0 copy-start.1
  0.7 1.2 %shard_map.76 = (bf16[192,128]{1,0:T(8,128)(2,1)S(1)}, bf16[192,128]{1,0:T(8,128)(2,1)S(1)}, bf16[32,128]{1,0:T(8,128)(2,1)S(1)}, bf16[32,128]{1,0:T(8,128)(2,1)S(1)}, bf16[16,128,128]{2,1,0:T(8,128)(2,1)S(1)}) custom-call(bf16[16,128,128]{2,1,0:T(8,128)(2,1)} %pre_far.1, bf16[8,64,128]{2,1,0:T(8,128)(2,1)} %grad_out.1), custom_call_target="tpu_custom_call" | custom-call | flops 1000 | bytes 262144 | tf_op jit(solution)/shard_map/pallas_call | solution.py:432
  1.9 4.1 %collective-permute-start = (bf16[192,128]{1,0:T(8,128)(2,1)S(1)}, bf16[192,128]{1,0:T(8,128)(2,1)S(1)}, u32[]{:S(2)}, u32[]{:S(2)}) collective-permute-start(bf16[192,128]{1,0:T(8,128)(2,1)S(1)} %get-tuple-element.43), channel_id=1, source_target_pairs={{0,4},{1,5},{2,6},{3,7},{4,0},{5,1},{6,2},{7,3},{24,25},{25,24},{2... | collective-permute-start | bytes 147464 | tf_op jit(solution)/shard_map/ppermute | solution.py:457
  6.0 0.4 collective-permute-start.1
  6.4 0.1 pad.9.clone
  6.4 0.9 %shard_map.77 = (f32[16,64,256]{2,1,0:T(8,128)S(1)}, bf16[2,256,512]{2,1,0:T(8,128)(2,1)S(1)}, f32[2,16,128]{2,1,0:T(8,128)S(1)}) custom-call(bf16[16,128,128]{2,1,0:T(8,128)(2,1)S(1)} %get-tuple-element.45.pre), custom_call_target="tpu_custom_call" | custom-call | flops 15728640 | bytes 2097152 | tf_op jit(solution)/shard_map/pallas_call | solution.py:460
  7.4 0.0 copy-done
  7.4 0.0 copy-done.2
  7.4 0.0 copy-done.1
  7.4 0.7 %shard_map.78 = (bf16[128,1024]{1,0:T(8,128)(2,1)S(1)}, bf16[128,32]{1,0:T(8,128)(2,1)S(1)}, bf16[384,512]{1,0:T(8,128)(2,1)S(1)}, bf16[3,256,512]{2,1,0:T(8,128)(2,1)S(1)}) custom-call(bf16[16,64,128]{2,1,0:T(8,128)(2,1)S(1)} %bitcast.8, bf16[3,3,64,128]{3,2,1,0:T(8,128)(2,1)S(1)} %copy-done.2, bf16[3,3,128,128]{3,2,1,0:T(8,128)(2,1)S(1)} %copy-done), custom_call_target="tpu_custom_call" | custom-call | flops 67108864 | bytes 3145728 | tf_op jit(solution)/shard_map/pallas_call | solution.py:478
  8.1 0.4 %collective-permute-done.row_b = bf16[192,128]{1,0:T(8,128)(2,1)S(1)} collective-permute-done((bf16[192,128]{1,0:T(8,128)(2,1)S(1)}, bf16[192,128]{1,0:T(8,128)(2,1)S(1)}, u32[]{:S(2)}, u32[]{:S(2)}) %collective-permute-start) | collective-permute-done | bytes 49184 | tf_op jit(solution)/shard_map/ppermute | solution.py:457
  8.6 1.5 %collective-permute-done.1.row_a = bf16[192,128]{1,0:T(8,128)(2,1)S(1)} collective-permute-done((bf16[192,128]{1,0:T(8,128)(2,1)S(1)}, bf16[192,128]{1,0:T(8,128)(2,1)S(1)}, u32[]{:S(2)}, u32[]{:S(2)}) %collective-permute-start.1) | collective-permute-done | bytes 49184 | tf_op jit(solution)/shard_map/ppermute | solution.py:458
  10.1 0.1 maximum_maximum_fusion.1
  10.2 0.8 %collective-permute-start.3 = (bf16[32,128]{1,0:T(8,128)(2,1)S(1)}, bf16[32,128]{1,0:T(8,128)(2,1)S(1)}, u32[]{:S(2)}, u32[]{:S(2)}) collective-permute-start(bf16[32,128]{1,0:T(8,128)(2,1)S(1)} %get-tuple-element.93), channel_id=1, source_target_pairs={{0,7},{1,2},{2,1},{3,4},{4,3},{5,6},{6,5},{7,0},{8,15},{9,10},{10,... | collective-permute-start | bytes 24584 | tf_op jit(solution)/shard_map/ppermute | solution.py:503
  11.0 0.9 %collective-permute-start.2 = (bf16[32,128]{1,0:T(8,128)(2,1)S(1)}, bf16[32,128]{1,0:T(8,128)(2,1)S(1)}, u32[]{:S(2)}, u32[]{:S(2)}) collective-permute-start(bf16[32,128]{1,0:T(8,128)(2,1)S(1)} %get-tuple-element.94), channel_id=1, source_target_pairs={{0,1},{1,0},{2,3},{3,2},{4,5},{5,4},{6,7},{7,6},{8,9},{9,8},{10,11... | collective-permute-start | bytes 24584 | tf_op jit(solution)/shard_map/ppermute | solution.py:504
  11.9 0.0 copy-done.3
  11.9 2.4 %shard_map.79 = (bf16[19,64,512]{2,1,0:T(8,128)(2,1)S(1)}, f32[1792,128]{1,0:T(8,128)S(1)}, f32[2,32,128]{2,1,0:T(8,128)S(1)}, f32[2,32,128]{2,1,0:T(8,128)S(1)}, f32[2,16,128]{2,1,0:T(8,128)S(1)}) custom-call(bf16[8,64,128]{2,1,0:T(8,128)(2,1)S(1)} %copy-done.3, bf16[192,128]{1,0:T(8,128)(2,1)S(1)} %collective-permute-done.1.row_a, ...), custom_call_target="tpu_custom_call" | custom-call | flops 1509949440 | bytes 8388608 | tf_op jit(solution)/shard_map/pallas_call | solution.py:509
  14.3 0.8 %collective-permute-done.3.col_b = bf16[32,128]{1,0:T(8,128)(2,1)S(1)} collective-permute-done((bf16[32,128]{1,0:T(8,128)(2,1)S(1)}, bf16[32,128]{1,0:T(8,128)(2,1)S(1)}, u32[]{:S(2)}, u32[]{:S(2)}) %collective-permute-start.3) | collective-permute-done | bytes 8224 | tf_op jit(solution)/shard_map/ppermute | solution.py:503
  15.1 0.0 collective-permute-done.2.col_a
  15.1 1.2 %shard_map.80 = (bf16[4,32,128]{2,1,0:T(8,128)(2,1)S(1)}, f32[224,128]{1,0:T(8,128)S(1)}, f32[224,128]{1,0:T(8,128)S(1)}, f32[224,128]{1,0:T(8,128)S(1)}, f32[22...) custom-call(bf16[32,128]{1,0:T(8,128)(2,1)S(1)} %collective-permute-, ...), custom_call_target="tpu_custom_call" | custom-call | flops 268435456 | bytes 3145728 | tf_op jit(solution)/shard_map/pallas_call | solution.py:535
  16.3 0.1 collective-permute-start.4
  16.4 0.5 %collective-permute-start.6 = (f32[224,128]{1,0:T(8,128)S(1)}, f32[224,128]{1,0:T(8,128)S(1)}, u32[]{:S(2)}, u32[]{:S(2)}) collective-permute-start(f32[224,128]{1,0:T(8,128)S(1)} %get-tuple-element.67), channel_id=1, source_target_pairs={{0,1},{1,0},{2,3},{3,2},{4,5},{5,4},{6,7},{7,6},{8,9},{9,8},{10,11... | collective-permute-start | bytes 344072 | tf_op jit(solution)/shard_map/ppermute | solution.py:560
  16.9 0.1 collective-permute-start.8
  16.9 0.4 %collective-permute-start.10 = (f32[224,128]{1,0:T(8,128)S(1)}, f32[224,128]{1,0:T(8,128)S(1)}, u32[]{:S(2)}, u32[]{:S(2)}) collective-permute-start(f32[224,128]{1,0:T(8,128)S(1)} %get-tuple-element.75), channel_id=1, source_target_pairs={{0,1},{1,0},{2,3},{3,2},{4,5},{5,4},{6,7},{7,6},{8,9},{9,8},{10,11... | collective-permute-start | bytes 344072 | tf_op jit(solution)/shard_map/ppermute | solution.py:560
  17.4 0.3 collective-permute-done.4
  17.7 0.5 %collective-permute-start.5 = (bf16[224,128]{1,0:T(8,128)(2,1)S(1)}, bf16[224,128]{1,0:T(8,128)(2,1)S(1)}, u32[]{:S(2)}, u32[]{:S(2)}) collective-permute-start(bf16[224,128]{1,0:T(8,128)(2,1)S(1)} %add_convert_fusion.4), channel_id=1, source_target_pairs={{0,24},{1,25},{2,26},{3,27},{4,28},{5,29},{6,30},{7,31},{8,16},{9,... | collective-permute-start | bytes 172040 | tf_op jit(solution)/shard_map/ppermute | solution.py:556
  18.2 0.0 collective-permute-done.6
  18.2 0.9 %collective-permute-start.7 = (bf16[224,128]{1,0:T(8,128)(2,1)S(1)}, bf16[224,128]{1,0:T(8,128)(2,1)S(1)}, u32[]{:S(2)}, u32[]{:S(2)}) collective-permute-start(bf16[224,128]{1,0:T(8,128)(2,1)S(1)} %add_convert_fusion.3), channel_id=1, source_target_pairs={{0,17},{1,16},{2,19},{3,18},{4,21},{5,20},{6,23},{7,22},{8,25},{9,... | collective-permute-start | bytes 172040 | tf_op jit(solution)/shard_map/ppermute | solution.py:556
  19.2 0.0 collective-permute-done.8
  19.2 1.9 %collective-permute-start.9 = (bf16[224,128]{1,0:T(8,128)(2,1)S(1)}, bf16[224,128]{1,0:T(8,128)(2,1)S(1)}, u32[]{:S(2)}, u32[]{:S(2)}) collective-permute-start(bf16[224,128]{1,0:T(8,128)(2,1)S(1)} %add_convert_fusion.2), channel_id=1, source_target_pairs={{0,9},{1,8},{2,11},{3,10},{4,13},{5,12},{6,15},{7,14},{8,1},{9,0},... | collective-permute-start | bytes 172040 | tf_op jit(solution)/shard_map/ppermute | solution.py:556
  21.1 2.2 %shard_map.81 = bf16[16,64,128]{2,1,0:T(8,128)(2,1)} custom-call(bf16[19,64,512]{2,1,0:T(8,128)(2,1)S(1)} %get-tuple-element.70.part, bf16[4,32,128]{2,1,0:T(8,128)(2,1)S(1)} %get-tuple-element.71.ends, bf16[384,512]{1,0:T(8,128)(2,1)S(1)} %get-tuple-element.72.taps), custom_call_target="tpu_custom_call" | custom-call | flops 301989888 | bytes 3145728 | tf_op jit(solution)/shard_map/pallas_call | solution.py:563
  23.3 0.0 collective-permute-done.5
  23.3 0.3 collective-permute-done.7
  23.6 0.0 collective-permute-done.9
  23.6 0.0 collective-permute-done.10
  23.6 1.4 %collective-permute-start.13 = (bf16[224,128]{1,0:T(8,128)(2,1)S(1)}, bf16[224,128]{1,0:T(8,128)(2,1)S(1)}, u32[]{:S(2)}, u32[]{:S(2)}) collective-permute-start(bf16[224,128]{1,0:T(8,128)(2,1)S(1)} %add_convert_fusion.1), channel_id=1, source_target_pairs={{0,5},{1,4},{2,7},{3,6},{4,1},{5,0},{6,3},{7,2},{8,13},{9,12},{10,... | collective-permute-start | bytes 172040 | tf_op jit(solution)/shard_map/ppermute | solution.py:556
  25.1 1.4 %collective-permute-start.12 = (bf16[224,128]{1,0:T(8,128)(2,1)S(1)}, bf16[224,128]{1,0:T(8,128)(2,1)S(1)}, u32[]{:S(2)}, u32[]{:S(2)}) collective-permute-start(bf16[224,128]{1,0:T(8,128)(2,1)S(1)} %add_convert_fusion.1), channel_id=1, source_target_pairs={{0,6},{1,7},{2,4},{3,5},{4,2},{5,3},{6,0},{7,1},{8,14},{9,15},{10,... | collective-permute-start | bytes 172040 | tf_op jit(solution)/shard_map/ppermute | solution.py:556
  26.4 0.3 collective-permute-start.11
  26.7 3.8 %collective-permute-done.13 = bf16[224,128]{1,0:T(8,128)(2,1)S(1)} collective-permute-done((bf16[224,128]{1,0:T(8,128)(2,1)S(1)}, bf16[224,128]{1,0:T(8,128)(2,1)S(1)}, u32[]{:S(2)}, u32[]{:S(2)}) %collective-permute-start.13) | collective-permute-done | bytes 57376 | tf_op jit(solution)/shard_map/ppermute | solution.py:556
  30.4 0.9 %collective-permute-done.12 = bf16[224,128]{1,0:T(8,128)(2,1)S(1)} collective-permute-done((bf16[224,128]{1,0:T(8,128)(2,1)S(1)}, bf16[224,128]{1,0:T(8,128)(2,1)S(1)}, u32[]{:S(2)}, u32[]{:S(2)}) %collective-permute-start.12) | collective-permute-done | bytes 57376 | tf_op jit(solution)/shard_map/ppermute | solution.py:556
  31.3 0.9 %collective-permute-done.11 = bf16[224,128]{1,0:T(8,128)(2,1)S(1)} collective-permute-done((bf16[224,128]{1,0:T(8,128)(2,1)S(1)}, bf16[224,128]{1,0:T(8,128)(2,1)S(1)}, u32[]{:S(2)}, u32[]{:S(2)}) %collective-permute-start.11) | collective-permute-done | bytes 57376 | tf_op jit(solution)/shard_map/ppermute | solution.py:556
  32.2 1.6 %collective-permute-start.16 = (bf16[224,128]{1,0:T(8,128)(2,1)S(1)}, bf16[224,128]{1,0:T(8,128)(2,1)S(1)}, u32[]{:S(2)}, u32[]{:S(2)}) collective-permute-start(bf16[224,128]{1,0:T(8,128)(2,1)S(1)} %add_convert_fusion), channel_id=1, source_target_pairs={{0,24},{1,25},{2,26},{3,27},{4,28},{5,29},{6,30},{7,31},{8,16},{9,... | collective-permute-start | bytes 172040 | tf_op jit(solution)/shard_map/ppermute | solution.py:556
  33.8 0.5 %collective-permute-start.15 = (bf16[224,128]{1,0:T(8,128)(2,1)S(1)}, bf16[224,128]{1,0:T(8,128)(2,1)S(1)}, u32[]{:S(2)}, u32[]{:S(2)}) collective-permute-start(bf16[224,128]{1,0:T(8,128)(2,1)S(1)} %add_convert_fusion), channel_id=1, source_target_pairs={{0,17},{1,16},{2,19},{3,18},{4,21},{5,20},{6,23},{7,22},{8,25},{9,... | collective-permute-start | bytes 172040 | tf_op jit(solution)/shard_map/ppermute | solution.py:556
  34.3 1.2 %collective-permute-start.14 = (bf16[224,128]{1,0:T(8,128)(2,1)S(1)}, bf16[224,128]{1,0:T(8,128)(2,1)S(1)}, u32[]{:S(2)}, u32[]{:S(2)}) collective-permute-start(bf16[224,128]{1,0:T(8,128)(2,1)S(1)} %add_convert_fusion), channel_id=1, source_target_pairs={{0,9},{1,8},{2,11},{3,10},{4,13},{5,12},{6,15},{7,14},{8,1},{9,0},... | collective-permute-start | bytes 172040 | tf_op jit(solution)/shard_map/ppermute | solution.py:556
  35.5 1.9 %collective-permute-done.16 = bf16[224,128]{1,0:T(8,128)(2,1)S(1)} collective-permute-done((bf16[224,128]{1,0:T(8,128)(2,1)S(1)}, bf16[224,128]{1,0:T(8,128)(2,1)S(1)}, u32[]{:S(2)}, u32[]{:S(2)}) %collective-permute-start.16) | collective-permute-done | bytes 57376 | tf_op jit(solution)/shard_map/ppermute | solution.py:556
  37.4 1.2 %collective-permute-done.15 = bf16[224,128]{1,0:T(8,128)(2,1)S(1)} collective-permute-done((bf16[224,128]{1,0:T(8,128)(2,1)S(1)}, bf16[224,128]{1,0:T(8,128)(2,1)S(1)}, u32[]{:S(2)}, u32[]{:S(2)}) %collective-permute-start.15) | collective-permute-done | bytes 57376 | tf_op jit(solution)/shard_map/ppermute | solution.py:556
  38.6 0.0 collective-permute-done.14
  38.6 0.2 collective-permute-start.17
  38.8 1.4 %collective-permute-done.17.theirs = bf16[4,224,128]{2,1,0:T(8,128)(2,1)S(1)} collective-permute-done((bf16[4,224,128]{2,1,0:T(8,128)(2,1)S(1)}, bf16[4,224,128]{2,1,0:T(8,128)(2,1)S(1)}, u32[]{:S(2)}, u32[]{:S(2)}) %collective-permute-start.17) | collective-permute-done | bytes 229408 | tf_op jit(solution)/shard_map/ppermute | solution.py:588
  40.2 1.0 %shard_map.82 = (f32[576,128]{1,0:T(8,128)}, f32[1152,128]{1,0:T(8,128)}) custom-call(bf16[4,224,128]{2,1,0:T(8,128)(2,1)S(1)} %pad_maximum_fusion.mine, bf16[4,224,128]{2,1,0:T(8,128)(2,1)S(1)} %collective-permute-done.17.theirs), custom_call_target="tpu_custom_call" | custom-call | flops 1000 | bytes 1572864 | tf_op jit(solution)/shard_map/pallas_call | solution.py:590
  (12 shorter events, 0.2 us)
Async XLA Ops:
  0.6 11.3 %copy-start.3 = (bf16[8,64,128]{2,1,0:T(8,128)(2,1)S(1)}, bf16[8,64,128]{2,1,0:T(8,128)(2,1)}, u32[]{:S(2)}) copy-start(bf16[8,64,128]{2,1,0:T(8,128)(2,1)} %grad_out.1) | copy-start | bytes 393220
  0.6 6.7 %copy-start = (bf16[3,3,128,128]{3,2,1,0:T(8,128)(2,1)S(1)}, bf16[3,3,128,128]{3,2,1,0:T(8,128)(2,1)}, u32[]{:S(2)}) copy-start(bf16[3,3,128,128]{3,2,1,0:T(8,128)(2,1)} %w_second.1) | copy-start | bytes 884740
  0.7 6.7 %copy-start.2 = (bf16[3,3,64,128]{3,2,1,0:T(8,128)(2,1)S(1)}, bf16[3,3,64,128]{3,2,1,0:T(8,128)(2,1)}, u32[]{:S(2)}) copy-start(bf16[3,3,64,128]{3,2,1,0:T(8,128)(2,1)} %w_first.1) | copy-start | bytes 442372
  0.7 6.7 %copy-start.1 = (bf16[16,128,64]{1,2,0:T(8,128)(2,1)S(1)}, bf16[16,128,64]{1,2,0:T(8,128)(2,1)}, u32[]{:S(2)}) copy-start(bf16[16,128,64]{1,2,0:T(8,128)(2,1)} %param.5) | copy-start | bytes 786436
  1.9 6.7 %collective-permute-start = (bf16[192,128]{1,0:T(8,128)(2,1)S(1)}, bf16[192,128]{1,0:T(8,128)(2,1)S(1)}, u32[]{:S(2)}, u32[]{:S(2)}) collective-permute-start(bf16[192,128]{1,0:T(8,128)(2,1)S(1)} %get-tuple-element.43), channel_id=1, source_target_pairs={{0,4},{1,5},{2,6},{3,7},{4,0},{5,1},{6,2},{7,3},{24,25},{25,24},{2... | collective-permute-start | bytes 147464 | tf_op jit(solution)/shard_map/ppermute | solution.py:457
  6.0 4.1 %collective-permute-start.1 = (bf16[192,128]{1,0:T(8,128)(2,1)S(1)}, bf16[192,128]{1,0:T(8,128)(2,1)S(1)}, u32[]{:S(2)}, u32[]{:S(2)}) collective-permute-start(bf16[192,128]{1,0:T(8,128)(2,1)S(1)} %get-tuple-element.44), channel_id=1, source_target_pairs={{0,8},{1,9},{2,10},{3,11},{4,12},{5,13},{6,14},{7,15},{8,0},{9,1},... | collective-permute-start | bytes 147464 | tf_op jit(solution)/shard_map/ppermute | solution.py:458
  10.2 4.9 %collective-permute-start.3 = (bf16[32,128]{1,0:T(8,128)(2,1)S(1)}, bf16[32,128]{1,0:T(8,128)(2,1)S(1)}, u32[]{:S(2)}, u32[]{:S(2)}) collective-permute-start(bf16[32,128]{1,0:T(8,128)(2,1)S(1)} %get-tuple-element.93), channel_id=1, source_target_pairs={{0,7},{1,2},{2,1},{3,4},{4,3},{5,6},{6,5},{7,0},{8,15},{9,10},{10,... | collective-permute-start | bytes 24584 | tf_op jit(solution)/shard_map/ppermute | solution.py:503
  11.0 4.1 %collective-permute-start.2 = (bf16[32,128]{1,0:T(8,128)(2,1)S(1)}, bf16[32,128]{1,0:T(8,128)(2,1)S(1)}, u32[]{:S(2)}, u32[]{:S(2)}) collective-permute-start(bf16[32,128]{1,0:T(8,128)(2,1)S(1)} %get-tuple-element.94), channel_id=1, source_target_pairs={{0,1},{1,0},{2,3},{3,2},{4,5},{5,4},{6,7},{7,6},{8,9},{9,8},{10,11... | collective-permute-start | bytes 24584 | tf_op jit(solution)/shard_map/ppermute | solution.py:504
  16.3 1.4 %collective-permute-start.4 = (f32[224,128]{1,0:T(8,128)S(1)}, f32[224,128]{1,0:T(8,128)S(1)}, u32[]{:S(2)}, u32[]{:S(2)}) collective-permute-start(f32[224,128]{1,0:T(8,128)S(1)} %get-tuple-element.65), channel_id=1, source_target_pairs={{0,1},{1,0},{2,3},{3,2},{4,5},{5,4},{6,7},{7,6},{8,9},{9,8},{10,11... | collective-permute-start | bytes 344072 | tf_op jit(solution)/shard_map/ppermute | solution.py:560
  16.4 1.9 %collective-permute-start.6 = (f32[224,128]{1,0:T(8,128)S(1)}, f32[224,128]{1,0:T(8,128)S(1)}, u32[]{:S(2)}, u32[]{:S(2)}) collective-permute-start(f32[224,128]{1,0:T(8,128)S(1)} %get-tuple-element.67), channel_id=1, source_target_pairs={{0,1},{1,0},{2,3},{3,2},{4,5},{5,4},{6,7},{7,6},{8,9},{9,8},{10,11... | collective-permute-start | bytes 344072 | tf_op jit(solution)/shard_map/ppermute | solution.py:560
  16.9 2.3 %collective-permute-start.8 = (f32[224,128]{1,0:T(8,128)S(1)}, f32[224,128]{1,0:T(8,128)S(1)}, u32[]{:S(2)}, u32[]{:S(2)}) collective-permute-start(f32[224,128]{1,0:T(8,128)S(1)} %get-tuple-element.69), channel_id=1, source_target_pairs={{0,1},{1,0},{2,3},{3,2},{4,5},{5,4},{6,7},{7,6},{8,9},{9,8},{10,11... | collective-permute-start | bytes 344072 | tf_op jit(solution)/shard_map/ppermute | solution.py:560
  16.9 6.7 %collective-permute-start.10 = (f32[224,128]{1,0:T(8,128)S(1)}, f32[224,128]{1,0:T(8,128)S(1)}, u32[]{:S(2)}, u32[]{:S(2)}) collective-permute-start(f32[224,128]{1,0:T(8,128)S(1)} %get-tuple-element.75), channel_id=1, source_target_pairs={{0,1},{1,0},{2,3},{3,2},{4,5},{5,4},{6,7},{7,6},{8,9},{9,8},{10,11... | collective-permute-start | bytes 344072 | tf_op jit(solution)/shard_map/ppermute | solution.py:560
  17.7 5.6 %collective-permute-start.5 = (bf16[224,128]{1,0:T(8,128)(2,1)S(1)}, bf16[224,128]{1,0:T(8,128)(2,1)S(1)}, u32[]{:S(2)}, u32[]{:S(2)}) collective-permute-start(bf16[224,128]{1,0:T(8,128)(2,1)S(1)} %add_convert_fusion.4), channel_id=1, source_target_pairs={{0,24},{1,25},{2,26},{3,27},{4,28},{5,29},{6,30},{7,31},{8,16},{9,... | collective-permute-start | bytes 172040 | tf_op jit(solution)/shard_map/ppermute | solution.py:556
  18.2 5.3 %collective-permute-start.7 = (bf16[224,128]{1,0:T(8,128)(2,1)S(1)}, bf16[224,128]{1,0:T(8,128)(2,1)S(1)}, u32[]{:S(2)}, u32[]{:S(2)}) collective-permute-start(bf16[224,128]{1,0:T(8,128)(2,1)S(1)} %add_convert_fusion.3), channel_id=1, source_target_pairs={{0,17},{1,16},{2,19},{3,18},{4,21},{5,20},{6,23},{7,22},{8,25},{9,... | collective-permute-start | bytes 172040 | tf_op jit(solution)/shard_map/ppermute | solution.py:556
  19.2 4.4 %collective-permute-start.9 = (bf16[224,128]{1,0:T(8,128)(2,1)S(1)}, bf16[224,128]{1,0:T(8,128)(2,1)S(1)}, u32[]{:S(2)}, u32[]{:S(2)}) collective-permute-start(bf16[224,128]{1,0:T(8,128)(2,1)S(1)} %add_convert_fusion.2), channel_id=1, source_target_pairs={{0,9},{1,8},{2,11},{3,10},{4,13},{5,12},{6,15},{7,14},{8,1},{9,0},... | collective-permute-start | bytes 172040 | tf_op jit(solution)/shard_map/ppermute | solution.py:556
  23.6 6.8 %collective-permute-start.13 = (bf16[224,128]{1,0:T(8,128)(2,1)S(1)}, bf16[224,128]{1,0:T(8,128)(2,1)S(1)}, u32[]{:S(2)}, u32[]{:S(2)}) collective-permute-start(bf16[224,128]{1,0:T(8,128)(2,1)S(1)} %add_convert_fusion.1), channel_id=1, source_target_pairs={{0,5},{1,4},{2,7},{3,6},{4,1},{5,0},{6,3},{7,2},{8,13},{9,12},{10,... | collective-permute-start | bytes 172040 | tf_op jit(solution)/shard_map/ppermute | solution.py:556
  25.1 6.2 %collective-permute-start.12 = (bf16[224,128]{1,0:T(8,128)(2,1)S(1)}, bf16[224,128]{1,0:T(8,128)(2,1)S(1)}, u32[]{:S(2)}, u32[]{:S(2)}) collective-permute-start(bf16[224,128]{1,0:T(8,128)(2,1)S(1)} %add_convert_fusion.1), channel_id=1, source_target_pairs={{0,6},{1,7},{2,4},{3,5},{4,2},{5,3},{6,0},{7,1},{8,14},{9,15},{10,... | collective-permute-start | bytes 172040 | tf_op jit(solution)/shard_map/ppermute | solution.py:556
  26.4 5.8 %collective-permute-start.11 = (bf16[224,128]{1,0:T(8,128)(2,1)S(1)}, bf16[224,128]{1,0:T(8,128)(2,1)S(1)}, u32[]{:S(2)}, u32[]{:S(2)}) collective-permute-start(bf16[224,128]{1,0:T(8,128)(2,1)S(1)} %add_convert_fusion.1), channel_id=1, source_target_pairs={{0,3},{1,2},{2,1},{3,0},{4,7},{5,6},{6,5},{7,4},{8,11},{9,10},{10,... | collective-permute-start | bytes 172040 | tf_op jit(solution)/shard_map/ppermute | solution.py:556
  32.2 5.2 %collective-permute-start.16 = (bf16[224,128]{1,0:T(8,128)(2,1)S(1)}, bf16[224,128]{1,0:T(8,128)(2,1)S(1)}, u32[]{:S(2)}, u32[]{:S(2)}) collective-permute-start(bf16[224,128]{1,0:T(8,128)(2,1)S(1)} %add_convert_fusion), channel_id=1, source_target_pairs={{0,24},{1,25},{2,26},{3,27},{4,28},{5,29},{6,30},{7,31},{8,16},{9,... | collective-permute-start | bytes 172040 | tf_op jit(solution)/shard_map/ppermute | solution.py:556
  33.8 4.8 %collective-permute-start.15 = (bf16[224,128]{1,0:T(8,128)(2,1)S(1)}, bf16[224,128]{1,0:T(8,128)(2,1)S(1)}, u32[]{:S(2)}, u32[]{:S(2)}) collective-permute-start(bf16[224,128]{1,0:T(8,128)(2,1)S(1)} %add_convert_fusion), channel_id=1, source_target_pairs={{0,17},{1,16},{2,19},{3,18},{4,21},{5,20},{6,23},{7,22},{8,25},{9,... | collective-permute-start | bytes 172040 | tf_op jit(solution)/shard_map/ppermute | solution.py:556
  34.3 4.3 %collective-permute-start.14 = (bf16[224,128]{1,0:T(8,128)(2,1)S(1)}, bf16[224,128]{1,0:T(8,128)(2,1)S(1)}, u32[]{:S(2)}, u32[]{:S(2)}) collective-permute-start(bf16[224,128]{1,0:T(8,128)(2,1)S(1)} %add_convert_fusion), channel_id=1, source_target_pairs={{0,9},{1,8},{2,11},{3,10},{4,13},{5,12},{6,15},{7,14},{8,1},{9,0},... | collective-permute-start | bytes 172040 | tf_op jit(solution)/shard_map/ppermute | solution.py:556
  38.6 1.6 %collective-permute-start.17 = (bf16[4,224,128]{2,1,0:T(8,128)(2,1)S(1)}, bf16[4,224,128]{2,1,0:T(8,128)(2,1)S(1)}, u32[]{:S(2)}, u32[]{:S(2)}) collective-permute-start(bf16[4,224,128]{2,1,0:T(8,128)(2,1)S(1)} %pad_maximum_fusion.mine), channel_id=1, source_target_pairs={{0,1},{1,0},{2,3},{3,2},{4,5},{5,4},{6,7},{7,6},{8,9},{9,8},{10,11... | collective-permute-start | bytes 688136 | tf_op jit(solution)/shard_map/ppermute | solution.py:588

commit v20 on v19

--- a/solution.py
+++ b/solution.py
@@ -395,11 +395,12 @@
     for h in range(2):
         for i in range(lats):
             at = (h * lats + i) * rows
+            here, there = (x[i ^ band].astype(F32) for x in (mine, theirs))
+            value = jnp.where(held == h, here, there)
             for out, base, end in ((out_second, 0, size), (out_first, size, total)):
                 low, high = max(at, base), min(at + rows, end)
                 if low < high:
-                    here, there = (x[i ^ band, low - at:high - at] for x in (mine, theirs))
-                    out[low - base:high - base] = jnp.where(held == h, here, there).astype(F32)
+                    out[low - base:high - base] = value[low - at:high - at]
 
 
 def vmem(count):
@@ -503,7 +504,7 @@
     col_b = lax.ppermute(col_b, "lon", [(i, (i + 2 * (i % 2) - 1) % lons) for i in range(lons)])
     col_a = lax.ppermute(col_a, "lon", [(i, i ^ 1) for i in range(lons)])
 
-    block = -(-9 * (c1 + c0) // (32 * lats)) * 16
+    block = -(-9 * (c1 + c0) // (16 * lats)) * 8
     held = lats * block
     reach = -(-(rows + 2) // 16) * 16
     spread, keep, raw_ends, slope_ends, out_ends = pl.pallas_call(

time: 41.4 us -> 41 us (level)
  no operation moved by 1% of the time
where the time goes in v20:
time: 41 us; the launch traced here: 40.9 us
  starting transfers between devices  17.2 us (42%)
  waiting for transfers between devices  13 us (32%)
  Pallas kernels  9.53 us (23%)
  between operations  0.79 us (2%)
    ppermute x9, starting transfers between devices, between_chips(): lax.ppermute(value, AREA, [(i * lons + j, (i ^ over_lat) * lons + (j ^ 2...  9.71 us
    ppermute x9, waiting for transfers between devices, between_chips(): lax.ppermute(value, AREA, [(i * lons + j, (i ^ over_lat) * lons + (j ^ 2...  8.61 us
    ppermute x1, starting transfers between devices, body(): row_b = lax.ppermute(row_b, AREA, pairs)  4.1 us
    pallas_call x1, Pallas kernels, body(): pl.pallas_call(functools.partial(middle_kernel, lats), out_shape=(shape((...  2.4 us
    pallas_call x1, Pallas kernels, body(): pl.pallas_call(functools.partial(last_kernel, lats), out_shape=shape((row...  2.16 us
    ppermute x1, waiting for transfers between devices, body(): row_a = lax.ppermute(row_a, AREA, every)  1.49 us
    ppermute x1, waiting for transfers between devices, body(): theirs = lax.ppermute(mine, 'lon', swap)  1.37 us
    pallas_call x1, Pallas kernels, body(): pl.pallas_call(functools.partial(columns_kernel, lats), out_shape=(shape(...  1.19 us
  transfers between devices with their start and end apart: 18, of which 11 were waited for; matrix products, arithmetic and copies ran while one was open for 0% of the time, Pallas kernels for 15%

profile of v20, /device:TPU:0, one launch (start us, length us, event | category | flops | bytes accessed | tf_op | source)
XLA Modules:
  0.0 40.9 jit_solution(5716057129399168312)
XLA Ops:
  0.6 0.0 copy-start.3
  0.6 0.0 copy-start
  0.7 0.0 copy-start.2
  0.7 0.0 copy-start.1
  0.7 1.2 %shard_map.76 = (bf16[192,128]{1,0:T(8,128)(2,1)S(1)}, bf16[192,128]{1,0:T(8,128)(2,1)S(1)}, bf16[32,128]{1,0:T(8,128)(2,1)S(1)}, bf16[32,128]{1,0:T(8,128)(2,1)S(1)}, bf16[16,128,128]{2,1,0:T(8,128)(2,1)S(1)}) custom-call(bf16[16,128,128]{2,1,0:T(8,128)(2,1)} %pre_far.1, bf16[8,64,128]{2,1,0:T(8,128)(2,1)} %grad_out.1), custom_call_target="tpu_custom_call" | custom-call | flops 1000 | bytes 262144 | tf_op jit(solution)/shard_map/pallas_call | solution.py:433
  1.9 4.1 %collective-permute-start = (bf16[192,128]{1,0:T(8,128)(2,1)S(1)}, bf16[192,128]{1,0:T(8,128)(2,1)S(1)}, u32[]{:S(2)}, u32[]{:S(2)}) collective-permute-start(bf16[192,128]{1,0:T(8,128)(2,1)S(1)} %get-tuple-element.43), channel_id=1, source_target_pairs={{0,4},{1,5},{2,6},{3,7},{4,0},{5,1},{6,2},{7,3},{24,25},{25,24},{2... | collective-permute-start | bytes 147464 | tf_op jit(solution)/shard_map/ppermute | solution.py:458
  6.0 0.4 collective-permute-start.1
  6.4 0.1 pad.9.clone
  6.4 0.9 %shard_map.77 = (f32[16,64,256]{2,1,0:T(8,128)S(1)}, bf16[2,256,512]{2,1,0:T(8,128)(2,1)S(1)}, f32[2,16,128]{2,1,0:T(8,128)S(1)}) custom-call(bf16[16,128,128]{2,1,0:T(8,128)(2,1)S(1)} %get-tuple-element.45.pre), custom_call_target="tpu_custom_call" | custom-call | flops 15728640 | bytes 2097152 | tf_op jit(solution)/shard_map/pallas_call | solution.py:461
  7.4 0.0 copy-done
  7.4 0.0 copy-done.2
  7.4 0.0 copy-done.1
  7.4 0.7 %shard_map.78 = (bf16[128,1024]{1,0:T(8,128)(2,1)S(1)}, bf16[128,32]{1,0:T(8,128)(2,1)S(1)}, bf16[384,512]{1,0:T(8,128)(2,1)S(1)}, bf16[3,256,512]{2,1,0:T(8,128)(2,1)S(1)}) custom-call(bf16[16,64,128]{2,1,0:T(8,128)(2,1)S(1)} %bitcast.8, bf16[3,3,64,128]{3,2,1,0:T(8,128)(2,1)S(1)} %copy-done.2, bf16[3,3,128,128]{3,2,1,0:T(8,128)(2,1)S(1)} %copy-done), custom_call_target="tpu_custom_call" | custom-call | flops 67108864 | bytes 3145728 | tf_op jit(solution)/shard_map/pallas_call | solution.py:479
  8.1 0.4 %collective-permute-done.row_b = bf16[192,128]{1,0:T(8,128)(2,1)S(1)} collective-permute-done((bf16[192,128]{1,0:T(8,128)(2,1)S(1)}, bf16[192,128]{1,0:T(8,128)(2,1)S(1)}, u32[]{:S(2)}, u32[]{:S(2)}) %collective-permute-start) | collective-permute-done | bytes 49184 | tf_op jit(solution)/shard_map/ppermute | solution.py:458
  8.6 1.5 %collective-permute-done.1.row_a = bf16[192,128]{1,0:T(8,128)(2,1)S(1)} collective-permute-done((bf16[192,128]{1,0:T(8,128)(2,1)S(1)}, bf16[192,128]{1,0:T(8,128)(2,1)S(1)}, u32[]{:S(2)}, u32[]{:S(2)}) %collective-permute-start.1) | collective-permute-done | bytes 49184 | tf_op jit(solution)/shard_map/ppermute | solution.py:459
  10.1 0.1 maximum_maximum_fusion.1
  10.2 0.8 %collective-permute-start.3 = (bf16[32,128]{1,0:T(8,128)(2,1)S(1)}, bf16[32,128]{1,0:T(8,128)(2,1)S(1)}, u32[]{:S(2)}, u32[]{:S(2)}) collective-permute-start(bf16[32,128]{1,0:T(8,128)(2,1)S(1)} %get-tuple-element.93), channel_id=1, source_target_pairs={{0,7},{1,2},{2,1},{3,4},{4,3},{5,6},{6,5},{7,0},{8,15},{9,10},{10,... | collective-permute-start | bytes 24584 | tf_op jit(solution)/shard_map/ppermute | solution.py:504
  11.0 0.9 %collective-permute-start.2 = (bf16[32,128]{1,0:T(8,128)(2,1)S(1)}, bf16[32,128]{1,0:T(8,128)(2,1)S(1)}, u32[]{:S(2)}, u32[]{:S(2)}) collective-permute-start(bf16[32,128]{1,0:T(8,128)(2,1)S(1)} %get-tuple-element.94), channel_id=1, source_target_pairs={{0,1},{1,0},{2,3},{3,2},{4,5},{5,4},{6,7},{7,6},{8,9},{9,8},{10,11... | collective-permute-start | bytes 24584 | tf_op jit(solution)/shard_map/ppermute | solution.py:505
  11.9 0.0 copy-done.3
  11.9 2.4 %shard_map.79 = (bf16[19,64,512]{2,1,0:T(8,128)(2,1)S(1)}, f32[1728,128]{1,0:T(8,128)S(1)}, f32[2,32,128]{2,1,0:T(8,128)S(1)}, f32[2,32,128]{2,1,0:T(8,128)S(1)}, f32[2,16,128]{2,1,0:T(8,128)S(1)}) custom-call(bf16[8,64,128]{2,1,0:T(8,128)(2,1)S(1)} %copy-done.3, bf16[192,128]{1,0:T(8,128)(2,1)S(1)} %collective-permute-done.1.row_a, ...), custom_call_target="tpu_custom_call" | custom-call | flops 1509949440 | bytes 8388608 | tf_op jit(solution)/shard_map/pallas_call | solution.py:510
  14.3 0.8 %collective-permute-done.3.col_b = bf16[32,128]{1,0:T(8,128)(2,1)S(1)} collective-permute-done((bf16[32,128]{1,0:T(8,128)(2,1)S(1)}, bf16[32,128]{1,0:T(8,128)(2,1)S(1)}, u32[]{:S(2)}, u32[]{:S(2)}) %collective-permute-start.3) | collective-permute-done | bytes 8224 | tf_op jit(solution)/shard_map/ppermute | solution.py:504
  15.1 0.0 collective-permute-done.2.col_a
  15.1 1.2 %shard_map.80 = (bf16[4,32,128]{2,1,0:T(8,128)(2,1)S(1)}, f32[216,128]{1,0:T(8,128)S(1)}, f32[216,128]{1,0:T(8,128)S(1)}, f32[216,128]{1,0:T(8,128)S(1)}, f32[21...) custom-call(bf16[32,128]{1,0:T(8,128)(2,1)S(1)} %collective-permute-, ...), custom_call_target="tpu_custom_call" | custom-call | flops 268435456 | bytes 3145728 | tf_op jit(solution)/shard_map/pallas_call | solution.py:536
  16.3 0.1 collective-permute-start.4
  16.4 0.5 %collective-permute-start.6 = (f32[216,128]{1,0:T(8,128)S(1)}, f32[216,128]{1,0:T(8,128)S(1)}, u32[]{:S(2)}, u32[]{:S(2)}) collective-permute-start(f32[216,128]{1,0:T(8,128)S(1)} %get-tuple-element.67), channel_id=1, source_target_pairs={{0,1},{1,0},{2,3},{3,2},{4,5},{5,4},{6,7},{7,6},{8,9},{9,8},{10,11... | collective-permute-start | bytes 331784 | tf_op jit(solution)/shard_map/ppermute | solution.py:561
  16.8 0.1 collective-permute-start.8
  16.9 0.4 %collective-permute-start.10 = (f32[216,128]{1,0:T(8,128)S(1)}, f32[216,128]{1,0:T(8,128)S(1)}, u32[]{:S(2)}, u32[]{:S(2)}) collective-permute-start(f32[216,128]{1,0:T(8,128)S(1)} %get-tuple-element.75), channel_id=1, source_target_pairs={{0,1},{1,0},{2,3},{3,2},{4,5},{5,4},{6,7},{7,6},{8,9},{9,8},{10,11... | collective-permute-start | bytes 331784 | tf_op jit(solution)/shard_map/ppermute | solution.py:561
  17.4 0.3 collective-permute-done.4
  17.7 0.5 %collective-permute-start.5 = (bf16[216,128]{1,0:T(8,128)(2,1)S(1)}, bf16[216,128]{1,0:T(8,128)(2,1)S(1)}, u32[]{:S(2)}, u32[]{:S(2)}) collective-permute-start(bf16[216,128]{1,0:T(8,128)(2,1)S(1)} %add_convert_fusion.4), channel_id=1, source_target_pairs={{0,24},{1,25},{2,26},{3,27},{4,28},{5,29},{6,30},{7,31},{8,16},{9,... | collective-permute-start | bytes 165896 | tf_op jit(solution)/shard_map/ppermute | solution.py:557
  18.2 0.0 collective-permute-done.6
  18.2 0.9 %collective-permute-start.7 = (bf16[216,128]{1,0:T(8,128)(2,1)S(1)}, bf16[216,128]{1,0:T(8,128)(2,1)S(1)}, u32[]{:S(2)}, u32[]{:S(2)}) collective-permute-start(bf16[216,128]{1,0:T(8,128)(2,1)S(1)} %add_convert_fusion.3), channel_id=1, source_target_pairs={{0,17},{1,16},{2,19},{3,18},{4,21},{5,20},{6,23},{7,22},{8,25},{9,... | collective-permute-start | bytes 165896 | tf_op jit(solution)/shard_map/ppermute | solution.py:557
  19.2 0.0 collective-permute-done.8
  19.2 1.9 %collective-permute-start.9 = (bf16[216,128]{1,0:T(8,128)(2,1)S(1)}, bf16[216,128]{1,0:T(8,128)(2,1)S(1)}, u32[]{:S(2)}, u32[]{:S(2)}) collective-permute-start(bf16[216,128]{1,0:T(8,128)(2,1)S(1)} %add_convert_fusion.2), channel_id=1, source_target_pairs={{0,9},{1,8},{2,11},{3,10},{4,13},{5,12},{6,15},{7,14},{8,1},{9,0},... | collective-permute-start | bytes 165896 | tf_op jit(solution)/shard_map/ppermute | solution.py:557
  21.1 2.2 %shard_map.81 = bf16[16,64,128]{2,1,0:T(8,128)(2,1)} custom-call(bf16[19,64,512]{2,1,0:T(8,128)(2,1)S(1)} %get-tuple-element.70.part, bf16[4,32,128]{2,1,0:T(8,128)(2,1)S(1)} %get-tuple-element.71.ends, bf16[384,512]{1,0:T(8,128)(2,1)S(1)} %get-tuple-element.72.taps), custom_call_target="tpu_custom_call" | custom-call | flops 301989888 | bytes 3145728 | tf_op jit(solution)/shard_map/pallas_call | solution.py:564
  23.3 0.0 collective-permute-done.5
  23.3 0.2 collective-permute-done.7
  23.5 0.0 collective-permute-done.9
  23.5 0.0 collective-permute-done.10
  23.6 1.5 %collective-permute-start.13 = (bf16[216,128]{1,0:T(8,128)(2,1)S(1)}, bf16[216,128]{1,0:T(8,128)(2,1)S(1)}, u32[]{:S(2)}, u32[]{:S(2)}) collective-permute-start(bf16[216,128]{1,0:T(8,128)(2,1)S(1)} %add_convert_fusion.1), channel_id=1, source_target_pairs={{0,5},{1,4},{2,7},{3,6},{4,1},{5,0},{6,3},{7,2},{8,13},{9,12},{10,... | collective-permute-start | bytes 165896 | tf_op jit(solution)/shard_map/ppermute | solution.py:557
  25.0 1.4 %collective-permute-start.12 = (bf16[216,128]{1,0:T(8,128)(2,1)S(1)}, bf16[216,128]{1,0:T(8,128)(2,1)S(1)}, u32[]{:S(2)}, u32[]{:S(2)}) collective-permute-start(bf16[216,128]{1,0:T(8,128)(2,1)S(1)} %add_convert_fusion.1), channel_id=1, source_target_pairs={{0,6},{1,7},{2,4},{3,5},{4,2},{5,3},{6,0},{7,1},{8,14},{9,15},{10,... | collective-permute-start | bytes 165896 | tf_op jit(solution)/shard_map/ppermute | solution.py:557
  26.4 0.2 collective-permute-start.11
  26.6 3.7 %collective-permute-done.13 = bf16[216,128]{1,0:T(8,128)(2,1)S(1)} collective-permute-done((bf16[216,128]{1,0:T(8,128)(2,1)S(1)}, bf16[216,128]{1,0:T(8,128)(2,1)S(1)}, u32[]{:S(2)}, u32[]{:S(2)}) %collective-permute-start.13) | collective-permute-done | bytes 55328 | tf_op jit(solution)/shard_map/ppermute | solution.py:557
  30.2 0.9 %collective-permute-done.12 = bf16[216,128]{1,0:T(8,128)(2,1)S(1)} collective-permute-done((bf16[216,128]{1,0:T(8,128)(2,1)S(1)}, bf16[216,128]{1,0:T(8,128)(2,1)S(1)}, u32[]{:S(2)}, u32[]{:S(2)}) %collective-permute-start.12) | collective-permute-done | bytes 55328 | tf_op jit(solution)/shard_map/ppermute | solution.py:557
  31.2 0.8 %collective-permute-done.11 = bf16[216,128]{1,0:T(8,128)(2,1)S(1)} collective-permute-done((bf16[216,128]{1,0:T(8,128)(2,1)S(1)}, bf16[216,128]{1,0:T(8,128)(2,1)S(1)}, u32[]{:S(2)}, u32[]{:S(2)}) %collective-permute-start.11) | collective-permute-done | bytes 55328 | tf_op jit(solution)/shard_map/ppermute | solution.py:557
  32.0 1.6 %collective-permute-start.16 = (bf16[216,128]{1,0:T(8,128)(2,1)S(1)}, bf16[216,128]{1,0:T(8,128)(2,1)S(1)}, u32[]{:S(2)}, u32[]{:S(2)}) collective-permute-start(bf16[216,128]{1,0:T(8,128)(2,1)S(1)} %add_convert_fusion), channel_id=1, source_target_pairs={{0,24},{1,25},{2,26},{3,27},{4,28},{5,29},{6,30},{7,31},{8,16},{9,... | collective-permute-start | bytes 165896 | tf_op jit(solution)/shard_map/ppermute | solution.py:557
  33.6 0.6 %collective-permute-start.15 = (bf16[216,128]{1,0:T(8,128)(2,1)S(1)}, bf16[216,128]{1,0:T(8,128)(2,1)S(1)}, u32[]{:S(2)}, u32[]{:S(2)}) collective-permute-start(bf16[216,128]{1,0:T(8,128)(2,1)S(1)} %add_convert_fusion), channel_id=1, source_target_pairs={{0,17},{1,16},{2,19},{3,18},{4,21},{5,20},{6,23},{7,22},{8,25},{9,... | collective-permute-start | bytes 165896 | tf_op jit(solution)/shard_map/ppermute | solution.py:557
  34.1 1.1 %collective-permute-start.14 = (bf16[216,128]{1,0:T(8,128)(2,1)S(1)}, bf16[216,128]{1,0:T(8,128)(2,1)S(1)}, u32[]{:S(2)}, u32[]{:S(2)}) collective-permute-start(bf16[216,128]{1,0:T(8,128)(2,1)S(1)} %add_convert_fusion), channel_id=1, source_target_pairs={{0,9},{1,8},{2,11},{3,10},{4,13},{5,12},{6,15},{7,14},{8,1},{9,0},... | collective-permute-start | bytes 165896 | tf_op jit(solution)/shard_map/ppermute | solution.py:557
  35.3 1.9 %collective-permute-done.16 = bf16[216,128]{1,0:T(8,128)(2,1)S(1)} collective-permute-done((bf16[216,128]{1,0:T(8,128)(2,1)S(1)}, bf16[216,128]{1,0:T(8,128)(2,1)S(1)}, u32[]{:S(2)}, u32[]{:S(2)}) %collective-permute-start.16) | collective-permute-done | bytes 55328 | tf_op jit(solution)/shard_map/ppermute | solution.py:557
  37.2 1.1 %collective-permute-done.15 = bf16[216,128]{1,0:T(8,128)(2,1)S(1)} collective-permute-done((bf16[216,128]{1,0:T(8,128)(2,1)S(1)}, bf16[216,128]{1,0:T(8,128)(2,1)S(1)}, u32[]{:S(2)}, u32[]{:S(2)}) %collective-permute-start.15) | collective-permute-done | bytes 55328 | tf_op jit(solution)/shard_map/ppermute | solution.py:557
  38.3 0.0 collective-permute-done.14
  38.3 0.2 collective-permute-start.17
  38.5 1.4 %collective-permute-done.17.theirs = bf16[4,216,128]{2,1,0:T(8,128)(2,1)S(1)} collective-permute-done((bf16[4,216,128]{2,1,0:T(8,128)(2,1)S(1)}, bf16[4,216,128]{2,1,0:T(8,128)(2,1)S(1)}, u32[]{:S(2)}, u32[]{:S(2)}) %collective-permute-start.17) | collective-permute-done | bytes 221216 | tf_op jit(solution)/shard_map/ppermute | solution.py:589
  39.9 1.0 %shard_map.82 = (f32[576,128]{1,0:T(8,128)}, f32[1152,128]{1,0:T(8,128)}) custom-call(bf16[4,216,128]{2,1,0:T(8,128)(2,1)S(1)} %pad_maximum_fusion.mine, bf16[4,216,128]{2,1,0:T(8,128)(2,1)S(1)} %collective-permute-done.17.theirs), custom_call_target="tpu_custom_call" | custom-call | flops 1000 | bytes 1572864 | tf_op jit(solution)/shard_map/pallas_call | solution.py:591
  (12 shorter events, 0.2 us)
Async XLA Ops:
  0.6 11.3 %copy-start.3 = (bf16[8,64,128]{2,1,0:T(8,128)(2,1)S(1)}, bf16[8,64,128]{2,1,0:T(8,128)(2,1)}, u32[]{:S(2)}) copy-start(bf16[8,64,128]{2,1,0:T(8,128)(2,1)} %grad_out.1) | copy-start | bytes 393220
  0.6 6.7 %copy-start = (bf16[3,3,128,128]{3,2,1,0:T(8,128)(2,1)S(1)}, bf16[3,3,128,128]{3,2,1,0:T(8,128)(2,1)}, u32[]{:S(2)}) copy-start(bf16[3,3,128,128]{3,2,1,0:T(8,128)(2,1)} %w_second.1) | copy-start | bytes 884740
  0.7 6.7 %copy-start.2 = (bf16[3,3,64,128]{3,2,1,0:T(8,128)(2,1)S(1)}, bf16[3,3,64,128]{3,2,1,0:T(8,128)(2,1)}, u32[]{:S(2)}) copy-start(bf16[3,3,64,128]{3,2,1,0:T(8,128)(2,1)} %w_first.1) | copy-start | bytes 442372
  0.7 6.7 %copy-start.1 = (bf16[16,128,64]{1,2,0:T(8,128)(2,1)S(1)}, bf16[16,128,64]{1,2,0:T(8,128)(2,1)}, u32[]{:S(2)}) copy-start(bf16[16,128,64]{1,2,0:T(8,128)(2,1)} %param.5) | copy-start | bytes 786436
  1.9 6.7 %collective-permute-start = (bf16[192,128]{1,0:T(8,128)(2,1)S(1)}, bf16[192,128]{1,0:T(8,128)(2,1)S(1)}, u32[]{:S(2)}, u32[]{:S(2)}) collective-permute-start(bf16[192,128]{1,0:T(8,128)(2,1)S(1)} %get-tuple-element.43), channel_id=1, source_target_pairs={{0,4},{1,5},{2,6},{3,7},{4,0},{5,1},{6,2},{7,3},{24,25},{25,24},{2... | collective-permute-start | bytes 147464 | tf_op jit(solution)/shard_map/ppermute | solution.py:458
  6.0 4.1 %collective-permute-start.1 = (bf16[192,128]{1,0:T(8,128)(2,1)S(1)}, bf16[192,128]{1,0:T(8,128)(2,1)S(1)}, u32[]{:S(2)}, u32[]{:S(2)}) collective-permute-start(bf16[192,128]{1,0:T(8,128)(2,1)S(1)} %get-tuple-element.44), channel_id=1, source_target_pairs={{0,8},{1,9},{2,10},{3,11},{4,12},{5,13},{6,14},{7,15},{8,0},{9,1},... | collective-permute-start | bytes 147464 | tf_op jit(solution)/shard_map/ppermute | solution.py:459
  10.2 4.9 %collective-permute-start.3 = (bf16[32,128]{1,0:T(8,128)(2,1)S(1)}, bf16[32,128]{1,0:T(8,128)(2,1)S(1)}, u32[]{:S(2)}, u32[]{:S(2)}) collective-permute-start(bf16[32,128]{1,0:T(8,128)(2,1)S(1)} %get-tuple-element.93), channel_id=1, source_target_pairs={{0,7},{1,2},{2,1},{3,4},{4,3},{5,6},{6,5},{7,0},{8,15},{9,10},{10,... | collective-permute-start | bytes 24584 | tf_op jit(solution)/shard_map/ppermute | solution.py:504
  11.0 4.1 %collective-permute-start.2 = (bf16[32,128]{1,0:T(8,128)(2,1)S(1)}, bf16[32,128]{1,0:T(8,128)(2,1)S(1)}, u32[]{:S(2)}, u32[]{:S(2)}) collective-permute-start(bf16[32,128]{1,0:T(8,128)(2,1)S(1)} %get-tuple-element.94), channel_id=1, source_target_pairs={{0,1},{1,0},{2,3},{3,2},{4,5},{5,4},{6,7},{7,6},{8,9},{9,8},{10,11... | collective-permute-start | bytes 24584 | tf_op jit(solution)/shard_map/ppermute | solution.py:505
  16.3 1.4 %collective-permute-start.4 = (f32[216,128]{1,0:T(8,128)S(1)}, f32[216,128]{1,0:T(8,128)S(1)}, u32[]{:S(2)}, u32[]{:S(2)}) collective-permute-start(f32[216,128]{1,0:T(8,128)S(1)} %get-tuple-element.65), channel_id=1, source_target_pairs={{0,1},{1,0},{2,3},{3,2},{4,5},{5,4},{6,7},{7,6},{8,9},{9,8},{10,11... | collective-permute-start | bytes 331784 | tf_op jit(solution)/shard_map/ppermute | solution.py:561
  16.4 1.9 %collective-permute-start.6 = (f32[216,128]{1,0:T(8,128)S(1)}, f32[216,128]{1,0:T(8,128)S(1)}, u32[]{:S(2)}, u32[]{:S(2)}) collective-permute-start(f32[216,128]{1,0:T(8,128)S(1)} %get-tuple-element.67), channel_id=1, source_target_pairs={{0,1},{1,0},{2,3},{3,2},{4,5},{5,4},{6,7},{7,6},{8,9},{9,8},{10,11... | collective-permute-start | bytes 331784 | tf_op jit(solution)/shard_map/ppermute | solution.py:561
  16.8 2.3 %collective-permute-start.8 = (f32[216,128]{1,0:T(8,128)S(1)}, f32[216,128]{1,0:T(8,128)S(1)}, u32[]{:S(2)}, u32[]{:S(2)}) collective-permute-start(f32[216,128]{1,0:T(8,128)S(1)} %get-tuple-element.69), channel_id=1, source_target_pairs={{0,1},{1,0},{2,3},{3,2},{4,5},{5,4},{6,7},{7,6},{8,9},{9,8},{10,11... | collective-permute-start | bytes 331784 | tf_op jit(solution)/shard_map/ppermute | solution.py:561
  16.9 6.6 %collective-permute-start.10 = (f32[216,128]{1,0:T(8,128)S(1)}, f32[216,128]{1,0:T(8,128)S(1)}, u32[]{:S(2)}, u32[]{:S(2)}) collective-permute-start(f32[216,128]{1,0:T(8,128)S(1)} %get-tuple-element.75), channel_id=1, source_target_pairs={{0,1},{1,0},{2,3},{3,2},{4,5},{5,4},{6,7},{7,6},{8,9},{9,8},{10,11... | collective-permute-start | bytes 331784 | tf_op jit(solution)/shard_map/ppermute | solution.py:561
  17.7 5.6 %collective-permute-start.5 = (bf16[216,128]{1,0:T(8,128)(2,1)S(1)}, bf16[216,128]{1,0:T(8,128)(2,1)S(1)}, u32[]{:S(2)}, u32[]{:S(2)}) collective-permute-start(bf16[216,128]{1,0:T(8,128)(2,1)S(1)} %add_convert_fusion.4), channel_id=1, source_target_pairs={{0,24},{1,25},{2,26},{3,27},{4,28},{5,29},{6,30},{7,31},{8,16},{9,... | collective-permute-start | bytes 165896 | tf_op jit(solution)/shard_map/ppermute | solution.py:557
  18.2 5.3 %collective-permute-start.7 = (bf16[216,128]{1,0:T(8,128)(2,1)S(1)}, bf16[216,128]{1,0:T(8,128)(2,1)S(1)}, u32[]{:S(2)}, u32[]{:S(2)}) collective-permute-start(bf16[216,128]{1,0:T(8,128)(2,1)S(1)} %add_convert_fusion.3), channel_id=1, source_target_pairs={{0,17},{1,16},{2,19},{3,18},{4,21},{5,20},{6,23},{7,22},{8,25},{9,... | collective-permute-start | bytes 165896 | tf_op jit(solution)/shard_map/ppermute | solution.py:557
  19.2 4.3 %collective-permute-start.9 = (bf16[216,128]{1,0:T(8,128)(2,1)S(1)}, bf16[216,128]{1,0:T(8,128)(2,1)S(1)}, u32[]{:S(2)}, u32[]{:S(2)}) collective-permute-start(bf16[216,128]{1,0:T(8,128)(2,1)S(1)} %add_convert_fusion.2), channel_id=1, source_target_pairs={{0,9},{1,8},{2,11},{3,10},{4,13},{5,12},{6,15},{7,14},{8,1},{9,0},... | collective-permute-start | bytes 165896 | tf_op jit(solution)/shard_map/ppermute | solution.py:557
  23.6 6.7 %collective-permute-start.13 = (bf16[216,128]{1,0:T(8,128)(2,1)S(1)}, bf16[216,128]{1,0:T(8,128)(2,1)S(1)}, u32[]{:S(2)}, u32[]{:S(2)}) collective-permute-start(bf16[216,128]{1,0:T(8,128)(2,1)S(1)} %add_convert_fusion.1), channel_id=1, source_target_pairs={{0,5},{1,4},{2,7},{3,6},{4,1},{5,0},{6,3},{7,2},{8,13},{9,12},{10,... | collective-permute-start | bytes 165896 | tf_op jit(solution)/shard_map/ppermute | solution.py:557
  25.0 6.1 %collective-permute-start.12 = (bf16[216,128]{1,0:T(8,128)(2,1)S(1)}, bf16[216,128]{1,0:T(8,128)(2,1)S(1)}, u32[]{:S(2)}, u32[]{:S(2)}) collective-permute-start(bf16[216,128]{1,0:T(8,128)(2,1)S(1)} %add_convert_fusion.1), channel_id=1, source_target_pairs={{0,6},{1,7},{2,4},{3,5},{4,2},{5,3},{6,0},{7,1},{8,14},{9,15},{10,... | collective-permute-start | bytes 165896 | tf_op jit(solution)/shard_map/ppermute | solution.py:557
  26.4 5.6 %collective-permute-start.11 = (bf16[216,128]{1,0:T(8,128)(2,1)S(1)}, bf16[216,128]{1,0:T(8,128)(2,1)S(1)}, u32[]{:S(2)}, u32[]{:S(2)}) collective-permute-start(bf16[216,128]{1,0:T(8,128)(2,1)S(1)} %add_convert_fusion.1), channel_id=1, source_target_pairs={{0,3},{1,2},{2,1},{3,0},{4,7},{5,6},{6,5},{7,4},{8,11},{9,10},{10,... | collective-permute-start | bytes 165896 | tf_op jit(solution)/shard_map/ppermute | solution.py:557
  32.0 5.2 %collective-permute-start.16 = (bf16[216,128]{1,0:T(8,128)(2,1)S(1)}, bf16[216,128]{1,0:T(8,128)(2,1)S(1)}, u32[]{:S(2)}, u32[]{:S(2)}) collective-permute-start(bf16[216,128]{1,0:T(8,128)(2,1)S(1)} %add_convert_fusion), channel_id=1, source_target_pairs={{0,24},{1,25},{2,26},{3,27},{4,28},{5,29},{6,30},{7,31},{8,16},{9,... | collective-permute-start | bytes 165896 | tf_op jit(solution)/shard_map/ppermute | solution.py:557
  33.6 4.7 %collective-permute-start.15 = (bf16[216,128]{1,0:T(8,128)(2,1)S(1)}, bf16[216,128]{1,0:T(8,128)(2,1)S(1)}, u32[]{:S(2)}, u32[]{:S(2)}) collective-permute-start(bf16[216,128]{1,0:T(8,128)(2,1)S(1)} %add_convert_fusion), channel_id=1, source_target_pairs={{0,17},{1,16},{2,19},{3,18},{4,21},{5,20},{6,23},{7,22},{8,25},{9,... | collective-permute-start | bytes 165896 | tf_op jit(solution)/shard_map/ppermute | solution.py:557
  34.1 4.2 %collective-permute-start.14 = (bf16[216,128]{1,0:T(8,128)(2,1)S(1)}, bf16[216,128]{1,0:T(8,128)(2,1)S(1)}, u32[]{:S(2)}, u32[]{:S(2)}) collective-permute-start(bf16[216,128]{1,0:T(8,128)(2,1)S(1)} %add_convert_fusion), channel_id=1, source_target_pairs={{0,9},{1,8},{2,11},{3,10},{4,13},{5,12},{6,15},{7,14},{8,1},{9,0},... | collective-permute-start | bytes 165896 | tf_op jit(solution)/shard_map/ppermute | solution.py:557
  38.3 1.5 %collective-permute-start.17 = (bf16[4,216,128]{2,1,0:T(8,128)(2,1)S(1)}, bf16[4,216,128]{2,1,0:T(8,128)(2,1)S(1)}, u32[]{:S(2)}, u32[]{:S(2)}) collective-permute-start(bf16[4,216,128]{2,1,0:T(8,128)(2,1)S(1)} %pad_maximum_fusion.mine), channel_id=1, source_target_pairs={{0,1},{1,0},{2,3},{3,2},{4,5},{5,4},{6,7},{7,6},{8,9},{9,8},{10,11... | collective-permute-start | bytes 663560 | tf_op jit(solution)/shard_map/ppermute | solution.py:589

commit v21 on v20

--- a/solution.py
+++ b/solution.py
@@ -56,7 +56,8 @@
     rows, cols, c1 = pre.shape
     pooled, half = grad_out.shape[:2]
     _, _, _, even, core = position(lats)
-    for message, low in ((row_a, ~even), (row_b, even)):
+    up = jnp.logical_xor(even, core == 1)
+    for message, low in ((row_a, up), (row_b, ~up)):
         message[:cols] = pre[jnp.where(low, 0, rows - 1)]
         message[cols:] = grad_out[jnp.where(low, 0, pooled - 1)]
     hold[:, rows + pooled:] = jnp.zeros((2, hold.shape[1] - rows - pooled, c1), F32)
@@ -130,9 +131,10 @@
 def middle_kernel(lats, grad_out, row_a, row_b, slope, act_t, fields_t, taps,
                   spread, keep, raw_ends, slope_ends, out_ends,
                   grid, wide, prods, ends, line, sums, corner):
-    _, first, last, even, _ = position(lats)
-    top = jnp.where(even, row_b[...], row_a[...])
-    bottom = jnp.where(even, row_a[...], row_b[...])
+    _, first, last, even, core = position(lats)
+    up = jnp.logical_xor(even, core == 1)
+    top = jnp.where(up, row_a[...], row_b[...])
+    bottom = jnp.where(up, row_b[...], row_a[...])
     rows, half, c2 = slope.shape
     c1 = c2 // 2
     pooled = rows // 2
@@ -449,14 +451,22 @@
         compiler_params=params(58),
         cost_estimate=pl.CostEstimate(flops=1000, bytes_accessed=1 << 18, transcendentals=0),
     )(pre_first, grad_out)
-    pairs = [(j, (j + lons // 2) % lons) for j in range(lons)]
-    pairs += [((lats - 1) * lons + j, (lats - 1) * lons + (j ^ 1)) for j in range(lons)]
-    for i in range(1, lats - 1, 2):
-        for j in range(lons):
-            pairs += [(i * lons + j, (i + 1) * lons + j), ((i + 1) * lons + j, i * lons + j)]
-    every = [(i * lons + j, (i ^ 1) * lons + j) for i in range(lats) for j in range(lons)]
-    row_b = lax.ppermute(row_b, AREA, pairs)
-    row_a = lax.ppermute(row_a, AREA, every)
+    def partner(i, j, near):
+        if near:
+            return (i ^ 1) * lons + j
+        if i == 0:
+            return (j + lons // 2) % lons
+        if i == lats - 1:
+            return i * lons + (j ^ 2)
+        return (i + 1 if i % 2 else i - 1) * lons + j
+
+    def rows_round(value, near):
+        return lax.ppermute(value, AREA, [
+            (i * lons + j, partner(i, j, near[j % 2])) for i in range(lats) for j in range(lons)])
+
+    up = jnp.logical_xor(even, core == 1)
+    row_a = rows_round(row_a, (False, True))
+    row_b = rows_round(row_b, (True, False))
 
     slope, act_t, act_ends = pl.pallas_call(
         local_kernel,
@@ -490,11 +500,11 @@
         compiler_params=params(16),
         cost_estimate=pl.CostEstimate(flops=4 * rows * cols * c0 * cols, bytes_accessed=3 << 20, transcendentals=0),
     )(jnp.transpose(inputs, (0, 2, 1)), w_first, w_second)
-    row_b, row_a, slope, fields_t = lax.optimization_barrier((row_b, row_a, slope, fields_t))
+    row_a, row_b, slope, fields_t = lax.optimization_barrier((row_a, row_b, slope, fields_t))
 
     def corners(at):
         places = (at * (cols - 1), cols + at * (half - 1))
-        above, below = (jnp.where(even, one, two) for one, two in ((row_b, row_a), (row_a, row_b)))
+        above, below = (jnp.where(up, one, two) for one, two in ((row_a, row_b), (row_b, row_a)))
         return jnp.concatenate([part[p:p + 1] for p in places for part in (above, below)], 0)
 
     low, high = corners(0), corners(1)

time: 41 us -> 41.5 us (1.012)
  starting transfers between devices: 17.2 us -> 19 us
  waiting for transfers between devices: 13 us -> 11.7 us
    ppermute x1, starting transfers between devices: 0.79 us -> 3.1 us  [body(): lax.ppermute(col_b, 'lon', [(i, (i + 2 * (i % 2) - 1) % lons) for i in ra...]
    ppermute x1, starting transfers between devices: 0.91 us -> 0.01 us  [body(): col_a = lax.ppermute(col_a, 'lon', [(i, i ^ 1) for i in range(lons)])]
    ppermute x1, waiting for transfers between devices: 0.78 us -> 0.01 us  [body(): lax.ppermute(col_b, 'lon', [(i, (i + 2 * (i % 2) - 1) % lons) for i in ra...]
  transfers between devices with their start and end apart: 18 -> 18, of which waited for: 11 -> 10; matrix products, arithmetic and copies ran while one was open for 0% -> 0% of each run, Pallas kernels for 15% -> 15%
where the time goes in v21:
time: 41.5 us; the launch traced here: 41.4 us
  starting transfers between devices  19 us (46%)
  waiting for transfers between devices  11.7 us (28%)
  Pallas kernels  9.53 us (23%)
  between operations  0.81 us (2%)
    ppermute x9, starting transfers between devices, between_chips(): lax.ppermute(value, AREA, [(i * lons + j, (i ^ over_lat) * lons + (j ^ 2...  9.7 us
    ppermute x9, waiting for transfers between devices, between_chips(): lax.ppermute(value, AREA, [(i * lons + j, (i ^ over_lat) * lons + (j ^ 2...  8.25 us
    ppermute x2, starting transfers between devices, rows_round(): lax.ppermute(value, AREA, [(i * lons + j, partner(i, j, near[j % 2])) for...  4.49 us
    ppermute x1, starting transfers between devices, body(): lax.ppermute(col_b, 'lon', [(i, (i + 2 * (i % 2) - 1) % lons) for i in ra...  3.1 us
    pallas_call x1, Pallas kernels, body(): pl.pallas_call(functools.partial(middle_kernel, lats), out_shape=(shape((...  2.38 us
    pallas_call x1, Pallas kernels, body(): pl.pallas_call(functools.partial(last_kernel, lats), out_shape=shape((row...  2.15 us
    ppermute x2, waiting for transfers between devices, rows_round(): lax.ppermute(value, AREA, [(i * lons + j, partner(i, j, near[j % 2])) for...  1.93 us
    pallas_call x1, Pallas kernels, body(): pl.pallas_call(functools.partial(columns_kernel, lats), out_shape=(shape(...  1.2 us
  transfers between devices with their start and end apart: 18, of which 10 were waited for; matrix products, arithmetic and copies ran while one was open for 0% of the time, Pallas kernels for 15%

profile of v21, /device:TPU:0, one launch (start us, length us, event | category | flops | bytes accessed | tf_op | source)
XLA Modules:
  0.0 41.4 jit_solution(11479691605253057307)
XLA Ops:
  0.6 0.0 copy-start.3
  0.6 0.0 copy-start
  0.7 0.0 copy-start.2
  0.7 0.0 copy-start.1
  0.7 1.2 %shard_map.76 = (bf16[192,128]{1,0:T(8,128)(2,1)S(1)}, bf16[192,128]{1,0:T(8,128)(2,1)S(1)}, bf16[32,128]{1,0:T(8,128)(2,1)S(1)}, bf16[32,128]{1,0:T(8,128)(2,1)S(1)}, bf16[16,128,128]{2,1,0:T(8,128)(2,1)S(1)}) custom-call(bf16[16,128,128]{2,1,0:T(8,128)(2,1)} %pre_far.1, bf16[8,64,128]{2,1,0:T(8,128)(2,1)} %grad_out.1), custom_call_target="tpu_custom_call" | custom-call | flops 1000 | bytes 262144 | tf_op jit(solution)/shard_map/pallas_call | solution.py:435
  1.9 4.1 %collective-permute-start = (bf16[192,128]{1,0:T(8,128)(2,1)S(1)}, bf16[192,128]{1,0:T(8,128)(2,1)S(1)}, u32[]{:S(2)}, u32[]{:S(2)}) collective-permute-start(bf16[192,128]{1,0:T(8,128)(2,1)S(1)} %get-tuple-element.43), channel_id=1, source_target_pairs={{0,4},{1,9},{2,6},{3,11},{4,0},{5,13},{6,2},{7,15},{8,16},{9,1},{1... | collective-permute-start | bytes 147464 | tf_op jit(solution)/shard_map/ppermute | solution.py:464
  6.0 0.4 collective-permute-start.1
  6.4 0.1 pad.9.clone
  6.4 0.9 %shard_map.77 = (f32[16,64,256]{2,1,0:T(8,128)S(1)}, bf16[2,256,512]{2,1,0:T(8,128)(2,1)S(1)}, f32[2,16,128]{2,1,0:T(8,128)S(1)}) custom-call(bf16[16,128,128]{2,1,0:T(8,128)(2,1)S(1)} %get-tuple-element.45.pre), custom_call_target="tpu_custom_call" | custom-call | flops 15728640 | bytes 2097152 | tf_op jit(solution)/shard_map/pallas_call | solution.py:471
  7.4 0.0 copy-done
  7.4 0.0 copy-done.2
  7.4 0.0 copy-done.1
  7.4 0.7 %shard_map.78 = (bf16[128,1024]{1,0:T(8,128)(2,1)S(1)}, bf16[128,32]{1,0:T(8,128)(2,1)S(1)}, bf16[384,512]{1,0:T(8,128)(2,1)S(1)}, bf16[3,256,512]{2,1,0:T(8,128)(2,1)S(1)}) custom-call(bf16[16,64,128]{2,1,0:T(8,128)(2,1)S(1)} %bitcast.8, bf16[3,3,64,128]{3,2,1,0:T(8,128)(2,1)S(1)} %copy-done.2, bf16[3,3,128,128]{3,2,1,0:T(8,128)(2,1)S(1)} %copy-done), custom_call_target="tpu_custom_call" | custom-call | flops 67108864 | bytes 3145728 | tf_op jit(solution)/shard_map/pallas_call | solution.py:489
  8.1 0.1 collective-permute-done.row_a
  8.2 1.8 %collective-permute-done.1.row_b = bf16[192,128]{1,0:T(8,128)(2,1)S(1)} collective-permute-done((bf16[192,128]{1,0:T(8,128)(2,1)S(1)}, bf16[192,128]{1,0:T(8,128)(2,1)S(1)}, u32[]{:S(2)}, u32[]{:S(2)}) %collective-permute-start.1) | collective-permute-done | bytes 49184 | tf_op jit(solution)/shard_map/ppermute | solution.py:464
  10.1 0.1 maximum_maximum_fusion.1
  10.2 3.1 %collective-permute-start.3 = (bf16[32,128]{1,0:T(8,128)(2,1)S(1)}, bf16[32,128]{1,0:T(8,128)(2,1)S(1)}, u32[]{:S(2)}, u32[]{:S(2)}) collective-permute-start(bf16[32,128]{1,0:T(8,128)(2,1)S(1)} %get-tuple-element.93), channel_id=1, source_target_pairs={{0,7},{1,2},{2,1},{3,4},{4,3},{5,6},{6,5},{7,0},{8,15},{9,10},{10,... | collective-permute-start | bytes 24584 | tf_op jit(solution)/shard_map/ppermute | solution.py:514
  13.3 0.0 collective-permute-start.2
  13.3 0.0 copy-done.3
  13.3 2.4 %shard_map.79 = (bf16[19,64,512]{2,1,0:T(8,128)(2,1)S(1)}, f32[1728,128]{1,0:T(8,128)S(1)}, f32[2,32,128]{2,1,0:T(8,128)S(1)}, f32[2,32,128]{2,1,0:T(8,128)S(1)}, f32[2,16,128]{2,1,0:T(8,128)S(1)}) custom-call(bf16[8,64,128]{2,1,0:T(8,128)(2,1)S(1)} %copy-done.3, bf16[192,128]{1,0:T(8,128)(2,1)S(1)} %collective-permute-done.row_a, ...), custom_call_target="tpu_custom_call" | custom-call | flops 1509949440 | bytes 8388608 | tf_op jit(solution)/shard_map/pallas_call | solution.py:520
  15.7 0.0 collective-permute-done.3.col_b
  15.7 0.0 collective-permute-done.2.col_a
  15.7 1.2 %shard_map.80 = (bf16[4,32,128]{2,1,0:T(8,128)(2,1)S(1)}, f32[216,128]{1,0:T(8,128)S(1)}, f32[216,128]{1,0:T(8,128)S(1)}, f32[216,128]{1,0:T(8,128)S(1)}, f32[21...) custom-call(bf16[32,128]{1,0:T(8,128)(2,1)S(1)} %collective-permute-, ...), custom_call_target="tpu_custom_call" | custom-call | flops 268435456 | bytes 3145728 | tf_op jit(solution)/shard_map/pallas_call | solution.py:546
  16.9 0.6 %collective-permute-start.4 = (f32[216,128]{1,0:T(8,128)S(1)}, f32[216,128]{1,0:T(8,128)S(1)}, u32[]{:S(2)}, u32[]{:S(2)}) collective-permute-start(f32[216,128]{1,0:T(8,128)S(1)} %get-tuple-element.65), channel_id=1, source_target_pairs={{0,1},{1,0},{2,3},{3,2},{4,5},{5,4},{6,7},{7,6},{8,9},{9,8},{10,11... | collective-permute-start | bytes 331784 | tf_op jit(solution)/shard_map/ppermute | solution.py:571
  17.5 0.1 collective-permute-start.6
  17.6 0.4 %collective-permute-start.8 = (f32[216,128]{1,0:T(8,128)S(1)}, f32[216,128]{1,0:T(8,128)S(1)}, u32[]{:S(2)}, u32[]{:S(2)}) collective-permute-start(f32[216,128]{1,0:T(8,128)S(1)} %get-tuple-element.69), channel_id=1, source_target_pairs={{0,1},{1,0},{2,3},{3,2},{4,5},{5,4},{6,7},{7,6},{8,9},{9,8},{10,11... | collective-permute-start | bytes 331784 | tf_op jit(solution)/shard_map/ppermute | solution.py:571
  18.0 0.1 collective-permute-start.10
  18.1 0.4 collective-permute-done.4
  18.5 0.7 %collective-permute-start.5 = (bf16[216,128]{1,0:T(8,128)(2,1)S(1)}, bf16[216,128]{1,0:T(8,128)(2,1)S(1)}, u32[]{:S(2)}, u32[]{:S(2)}) collective-permute-start(bf16[216,128]{1,0:T(8,128)(2,1)S(1)} %add_convert_fusion.4), channel_id=1, source_target_pairs={{0,24},{1,25},{2,26},{3,27},{4,28},{5,29},{6,30},{7,31},{8,16},{9,... | collective-permute-start | bytes 165896 | tf_op jit(solution)/shard_map/ppermute | solution.py:567
  19.2 0.0 collective-permute-done.6
  19.2 0.1 collective-permute-start.7
  19.3 0.0 collective-permute-done.8
  19.3 2.6 %collective-permute-start.9 = (bf16[216,128]{1,0:T(8,128)(2,1)S(1)}, bf16[216,128]{1,0:T(8,128)(2,1)S(1)}, u32[]{:S(2)}, u32[]{:S(2)}) collective-permute-start(bf16[216,128]{1,0:T(8,128)(2,1)S(1)} %add_convert_fusion.2), channel_id=1, source_target_pairs={{0,9},{1,8},{2,11},{3,10},{4,13},{5,12},{6,15},{7,14},{8,1},{9,0},... | collective-permute-start | bytes 165896 | tf_op jit(solution)/shard_map/ppermute | solution.py:567
  21.9 2.2 %shard_map.81 = bf16[16,64,128]{2,1,0:T(8,128)(2,1)} custom-call(bf16[19,64,512]{2,1,0:T(8,128)(2,1)S(1)} %get-tuple-element.70.part, bf16[4,32,128]{2,1,0:T(8,128)(2,1)S(1)} %get-tuple-element.71.ends, bf16[384,512]{1,0:T(8,128)(2,1)S(1)} %get-tuple-element.72.taps), custom_call_target="tpu_custom_call" | custom-call | flops 301989888 | bytes 3145728 | tf_op jit(solution)/shard_map/pallas_call | solution.py:574
  24.1 0.0 collective-permute-done.5
  24.1 0.5 %collective-permute-done.7 = bf16[216,128]{1,0:T(8,128)(2,1)S(1)} collective-permute-done((bf16[216,128]{1,0:T(8,128)(2,1)S(1)}, bf16[216,128]{1,0:T(8,128)(2,1)S(1)}, u32[]{:S(2)}, u32[]{:S(2)}) %collective-permute-start.7) | collective-permute-done | bytes 55328 | tf_op jit(solution)/shard_map/ppermute | solution.py:567
  24.6 0.0 collective-permute-done.9
  24.6 0.0 collective-permute-done.10
  24.6 0.6 %collective-permute-start.13 = (bf16[216,128]{1,0:T(8,128)(2,1)S(1)}, bf16[216,128]{1,0:T(8,128)(2,1)S(1)}, u32[]{:S(2)}, u32[]{:S(2)}) collective-permute-start(bf16[216,128]{1,0:T(8,128)(2,1)S(1)} %add_convert_fusion.1), channel_id=1, source_target_pairs={{0,5},{1,4},{2,7},{3,6},{4,1},{5,0},{6,3},{7,2},{8,13},{9,12},{10,... | collective-permute-start | bytes 165896 | tf_op jit(solution)/shard_map/ppermute | solution.py:567
  25.2 1.5 %collective-permute-start.12 = (bf16[216,128]{1,0:T(8,128)(2,1)S(1)}, bf16[216,128]{1,0:T(8,128)(2,1)S(1)}, u32[]{:S(2)}, u32[]{:S(2)}) collective-permute-start(bf16[216,128]{1,0:T(8,128)(2,1)S(1)} %add_convert_fusion.1), channel_id=1, source_target_pairs={{0,6},{1,7},{2,4},{3,5},{4,2},{5,3},{6,0},{7,1},{8,14},{9,15},{10,... | collective-permute-start | bytes 165896 | tf_op jit(solution)/shard_map/ppermute | solution.py:567
  26.7 1.0 %collective-permute-start.11 = (bf16[216,128]{1,0:T(8,128)(2,1)S(1)}, bf16[216,128]{1,0:T(8,128)(2,1)S(1)}, u32[]{:S(2)}, u32[]{:S(2)}) collective-permute-start(bf16[216,128]{1,0:T(8,128)(2,1)S(1)} %add_convert_fusion.1), channel_id=1, source_target_pairs={{0,3},{1,2},{2,1},{3,0},{4,7},{5,6},{6,5},{7,4},{8,11},{9,10},{10,... | collective-permute-start | bytes 165896 | tf_op jit(solution)/shard_map/ppermute | solution.py:567
  27.7 2.4 %collective-permute-done.13 = bf16[216,128]{1,0:T(8,128)(2,1)S(1)} collective-permute-done((bf16[216,128]{1,0:T(8,128)(2,1)S(1)}, bf16[216,128]{1,0:T(8,128)(2,1)S(1)}, u32[]{:S(2)}, u32[]{:S(2)}) %collective-permute-start.13) | collective-permute-done | bytes 55328 | tf_op jit(solution)/shard_map/ppermute | solution.py:567
  30.0 1.6 %collective-permute-done.12 = bf16[216,128]{1,0:T(8,128)(2,1)S(1)} collective-permute-done((bf16[216,128]{1,0:T(8,128)(2,1)S(1)}, bf16[216,128]{1,0:T(8,128)(2,1)S(1)}, u32[]{:S(2)}, u32[]{:S(2)}) %collective-permute-start.12) | collective-permute-done | bytes 55328 | tf_op jit(solution)/shard_map/ppermute | solution.py:567
  31.6 0.8 %collective-permute-done.11 = bf16[216,128]{1,0:T(8,128)(2,1)S(1)} collective-permute-done((bf16[216,128]{1,0:T(8,128)(2,1)S(1)}, bf16[216,128]{1,0:T(8,128)(2,1)S(1)}, u32[]{:S(2)}, u32[]{:S(2)}) %collective-permute-start.11) | collective-permute-done | bytes 55328 | tf_op jit(solution)/shard_map/ppermute | solution.py:567
  32.4 1.8 %collective-permute-start.16 = (bf16[216,128]{1,0:T(8,128)(2,1)S(1)}, bf16[216,128]{1,0:T(8,128)(2,1)S(1)}, u32[]{:S(2)}, u32[]{:S(2)}) collective-permute-start(bf16[216,128]{1,0:T(8,128)(2,1)S(1)} %add_convert_fusion), channel_id=1, source_target_pairs={{0,24},{1,25},{2,26},{3,27},{4,28},{5,29},{6,30},{7,31},{8,16},{9,... | collective-permute-start | bytes 165896 | tf_op jit(solution)/shard_map/ppermute | solution.py:567
  34.3 0.7 %collective-permute-start.15 = (bf16[216,128]{1,0:T(8,128)(2,1)S(1)}, bf16[216,128]{1,0:T(8,128)(2,1)S(1)}, u32[]{:S(2)}, u32[]{:S(2)}) collective-permute-start(bf16[216,128]{1,0:T(8,128)(2,1)S(1)} %add_convert_fusion), channel_id=1, source_target_pairs={{0,17},{1,16},{2,19},{3,18},{4,21},{5,20},{6,23},{7,22},{8,25},{9,... | collective-permute-start | bytes 165896 | tf_op jit(solution)/shard_map/ppermute | solution.py:567
  34.9 0.8 %collective-permute-start.14 = (bf16[216,128]{1,0:T(8,128)(2,1)S(1)}, bf16[216,128]{1,0:T(8,128)(2,1)S(1)}, u32[]{:S(2)}, u32[]{:S(2)}) collective-permute-start(bf16[216,128]{1,0:T(8,128)(2,1)S(1)} %add_convert_fusion), channel_id=1, source_target_pairs={{0,9},{1,8},{2,11},{3,10},{4,13},{5,12},{6,15},{7,14},{8,1},{9,0},... | collective-permute-start | bytes 165896 | tf_op jit(solution)/shard_map/ppermute | solution.py:567
  35.7 1.9 %collective-permute-done.16 = bf16[216,128]{1,0:T(8,128)(2,1)S(1)} collective-permute-done((bf16[216,128]{1,0:T(8,128)(2,1)S(1)}, bf16[216,128]{1,0:T(8,128)(2,1)S(1)}, u32[]{:S(2)}, u32[]{:S(2)}) %collective-permute-start.16) | collective-permute-done | bytes 55328 | tf_op jit(solution)/shard_map/ppermute | solution.py:567
  37.6 1.2 %collective-permute-done.15 = bf16[216,128]{1,0:T(8,128)(2,1)S(1)} collective-permute-done((bf16[216,128]{1,0:T(8,128)(2,1)S(1)}, bf16[216,128]{1,0:T(8,128)(2,1)S(1)}, u32[]{:S(2)}, u32[]{:S(2)}) %collective-permute-start.15) | collective-permute-done | bytes 55328 | tf_op jit(solution)/shard_map/ppermute | solution.py:567
  38.7 0.0 collective-permute-done.14
  38.8 0.5 %collective-permute-start.17 = (bf16[4,216,128]{2,1,0:T(8,128)(2,1)S(1)}, bf16[4,216,128]{2,1,0:T(8,128)(2,1)S(1)}, u32[]{:S(2)}, u32[]{:S(2)}) collective-permute-start(bf16[4,216,128]{2,1,0:T(8,128)(2,1)S(1)} %pad_maximum_fusion.mine), channel_id=1, source_target_pairs={{0,1},{1,0},{2,3},{3,2},{4,5},{5,4},{6,7},{7,6},{8,9},{9,8},{10,11... | collective-permute-start | bytes 663560 | tf_op jit(solution)/shard_map/ppermute | solution.py:599
  39.3 1.1 %collective-permute-done.17.theirs = bf16[4,216,128]{2,1,0:T(8,128)(2,1)S(1)} collective-permute-done((bf16[4,216,128]{2,1,0:T(8,128)(2,1)S(1)}, bf16[4,216,128]{2,1,0:T(8,128)(2,1)S(1)}, u32[]{:S(2)}, u32[]{:S(2)}) %collective-permute-start.17) | collective-permute-done | bytes 221216 | tf_op jit(solution)/shard_map/ppermute | solution.py:599
  40.4 1.0 %shard_map.82 = (f32[576,128]{1,0:T(8,128)}, f32[1152,128]{1,0:T(8,128)}) custom-call(bf16[4,216,128]{2,1,0:T(8,128)(2,1)S(1)} %pad_maximum_fusion.mine, bf16[4,216,128]{2,1,0:T(8,128)(2,1)S(1)} %collective-permute-done.17.theirs), custom_call_target="tpu_custom_call" | custom-call | flops 1000 | bytes 1572864 | tf_op jit(solution)/shard_map/pallas_call | solution.py:601
  (12 shorter events, 0.2 us)
Async XLA Ops:
  0.6 12.7 %copy-start.3 = (bf16[8,64,128]{2,1,0:T(8,128)(2,1)S(1)}, bf16[8,64,128]{2,1,0:T(8,128)(2,1)}, u32[]{:S(2)}) copy-start(bf16[8,64,128]{2,1,0:T(8,128)(2,1)} %grad_out.1) | copy-start | bytes 393220
  0.6 6.8 %copy-start = (bf16[3,3,128,128]{3,2,1,0:T(8,128)(2,1)S(1)}, bf16[3,3,128,128]{3,2,1,0:T(8,128)(2,1)}, u32[]{:S(2)}) copy-start(bf16[3,3,128,128]{3,2,1,0:T(8,128)(2,1)} %w_second.1) | copy-start | bytes 884740
  0.7 6.8 %copy-start.2 = (bf16[3,3,64,128]{3,2,1,0:T(8,128)(2,1)S(1)}, bf16[3,3,64,128]{3,2,1,0:T(8,128)(2,1)}, u32[]{:S(2)}) copy-start(bf16[3,3,64,128]{3,2,1,0:T(8,128)(2,1)} %w_first.1) | copy-start | bytes 442372
  0.7 6.8 %copy-start.1 = (bf16[16,128,64]{1,2,0:T(8,128)(2,1)S(1)}, bf16[16,128,64]{1,2,0:T(8,128)(2,1)}, u32[]{:S(2)}) copy-start(bf16[16,128,64]{1,2,0:T(8,128)(2,1)} %param.5) | copy-start | bytes 786436
  1.9 6.4 %collective-permute-start = (bf16[192,128]{1,0:T(8,128)(2,1)S(1)}, bf16[192,128]{1,0:T(8,128)(2,1)S(1)}, u32[]{:S(2)}, u32[]{:S(2)}) collective-permute-start(bf16[192,128]{1,0:T(8,128)(2,1)S(1)} %get-tuple-element.43), channel_id=1, source_target_pairs={{0,4},{1,9},{2,6},{3,11},{4,0},{5,13},{6,2},{7,15},{8,16},{9,1},{1... | collective-permute-start | bytes 147464 | tf_op jit(solution)/shard_map/ppermute | solution.py:464
  6.0 4.1 %collective-permute-start.1 = (bf16[192,128]{1,0:T(8,128)(2,1)S(1)}, bf16[192,128]{1,0:T(8,128)(2,1)S(1)}, u32[]{:S(2)}, u32[]{:S(2)}) collective-permute-start(bf16[192,128]{1,0:T(8,128)(2,1)S(1)} %get-tuple-element.44), channel_id=1, source_target_pairs={{0,8},{1,5},{2,10},{3,7},{4,12},{5,1},{6,14},{7,3},{8,0},{9,17},{1... | collective-permute-start | bytes 147464 | tf_op jit(solution)/shard_map/ppermute | solution.py:464
  10.2 5.5 %collective-permute-start.3 = (bf16[32,128]{1,0:T(8,128)(2,1)S(1)}, bf16[32,128]{1,0:T(8,128)(2,1)S(1)}, u32[]{:S(2)}, u32[]{:S(2)}) collective-permute-start(bf16[32,128]{1,0:T(8,128)(2,1)S(1)} %get-tuple-element.93), channel_id=1, source_target_pairs={{0,7},{1,2},{2,1},{3,4},{4,3},{5,6},{6,5},{7,0},{8,15},{9,10},{10,... | collective-permute-start | bytes 24584 | tf_op jit(solution)/shard_map/ppermute | solution.py:514
  13.3 2.4 %collective-permute-start.2 = (bf16[32,128]{1,0:T(8,128)(2,1)S(1)}, bf16[32,128]{1,0:T(8,128)(2,1)S(1)}, u32[]{:S(2)}, u32[]{:S(2)}) collective-permute-start(bf16[32,128]{1,0:T(8,128)(2,1)S(1)} %get-tuple-element.94), channel_id=1, source_target_pairs={{0,1},{1,0},{2,3},{3,2},{4,5},{5,4},{6,7},{7,6},{8,9},{9,8},{10,11... | collective-permute-start | bytes 24584 | tf_op jit(solution)/shard_map/ppermute | solution.py:515
  16.9 1.5 %collective-permute-start.4 = (f32[216,128]{1,0:T(8,128)S(1)}, f32[216,128]{1,0:T(8,128)S(1)}, u32[]{:S(2)}, u32[]{:S(2)}) collective-permute-start(f32[216,128]{1,0:T(8,128)S(1)} %get-tuple-element.65), channel_id=1, source_target_pairs={{0,1},{1,0},{2,3},{3,2},{4,5},{5,4},{6,7},{7,6},{8,9},{9,8},{10,11... | collective-permute-start | bytes 331784 | tf_op jit(solution)/shard_map/ppermute | solution.py:571
  17.5 1.7 %collective-permute-start.6 = (f32[216,128]{1,0:T(8,128)S(1)}, f32[216,128]{1,0:T(8,128)S(1)}, u32[]{:S(2)}, u32[]{:S(2)}) collective-permute-start(f32[216,128]{1,0:T(8,128)S(1)} %get-tuple-element.67), channel_id=1, source_target_pairs={{0,1},{1,0},{2,3},{3,2},{4,5},{5,4},{6,7},{7,6},{8,9},{9,8},{10,11... | collective-permute-start | bytes 331784 | tf_op jit(solution)/shard_map/ppermute | solution.py:571
  17.6 1.7 %collective-permute-start.8 = (f32[216,128]{1,0:T(8,128)S(1)}, f32[216,128]{1,0:T(8,128)S(1)}, u32[]{:S(2)}, u32[]{:S(2)}) collective-permute-start(f32[216,128]{1,0:T(8,128)S(1)} %get-tuple-element.69), channel_id=1, source_target_pairs={{0,1},{1,0},{2,3},{3,2},{4,5},{5,4},{6,7},{7,6},{8,9},{9,8},{10,11... | collective-permute-start | bytes 331784 | tf_op jit(solution)/shard_map/ppermute | solution.py:571
  18.0 6.6 %collective-permute-start.10 = (f32[216,128]{1,0:T(8,128)S(1)}, f32[216,128]{1,0:T(8,128)S(1)}, u32[]{:S(2)}, u32[]{:S(2)}) collective-permute-start(f32[216,128]{1,0:T(8,128)S(1)} %get-tuple-element.75), channel_id=1, source_target_pairs={{0,1},{1,0},{2,3},{3,2},{4,5},{5,4},{6,7},{7,6},{8,9},{9,8},{10,11... | collective-permute-start | bytes 331784 | tf_op jit(solution)/shard_map/ppermute | solution.py:571
  18.5 5.6 %collective-permute-start.5 = (bf16[216,128]{1,0:T(8,128)(2,1)S(1)}, bf16[216,128]{1,0:T(8,128)(2,1)S(1)}, u32[]{:S(2)}, u32[]{:S(2)}) collective-permute-start(bf16[216,128]{1,0:T(8,128)(2,1)S(1)} %add_convert_fusion.4), channel_id=1, source_target_pairs={{0,24},{1,25},{2,26},{3,27},{4,28},{5,29},{6,30},{7,31},{8,16},{9,... | collective-permute-start | bytes 165896 | tf_op jit(solution)/shard_map/ppermute | solution.py:567
  19.2 5.4 %collective-permute-start.7 = (bf16[216,128]{1,0:T(8,128)(2,1)S(1)}, bf16[216,128]{1,0:T(8,128)(2,1)S(1)}, u32[]{:S(2)}, u32[]{:S(2)}) collective-permute-start(bf16[216,128]{1,0:T(8,128)(2,1)S(1)} %add_convert_fusion.3), channel_id=1, source_target_pairs={{0,17},{1,16},{2,19},{3,18},{4,21},{5,20},{6,23},{7,22},{8,25},{9,... | collective-permute-start | bytes 165896 | tf_op jit(solution)/shard_map/ppermute | solution.py:567
  19.3 5.3 %collective-permute-start.9 = (bf16[216,128]{1,0:T(8,128)(2,1)S(1)}, bf16[216,128]{1,0:T(8,128)(2,1)S(1)}, u32[]{:S(2)}, u32[]{:S(2)}) collective-permute-start(bf16[216,128]{1,0:T(8,128)(2,1)S(1)} %add_convert_fusion.2), channel_id=1, source_target_pairs={{0,9},{1,8},{2,11},{3,10},{4,13},{5,12},{6,15},{7,14},{8,1},{9,0},... | collective-permute-start | bytes 165896 | tf_op jit(solution)/shard_map/ppermute | solution.py:567
  24.6 5.4 %collective-permute-start.13 = (bf16[216,128]{1,0:T(8,128)(2,1)S(1)}, bf16[216,128]{1,0:T(8,128)(2,1)S(1)}, u32[]{:S(2)}, u32[]{:S(2)}) collective-permute-start(bf16[216,128]{1,0:T(8,128)(2,1)S(1)} %add_convert_fusion.1), channel_id=1, source_target_pairs={{0,5},{1,4},{2,7},{3,6},{4,1},{5,0},{6,3},{7,2},{8,13},{9,12},{10,... | collective-permute-start | bytes 165896 | tf_op jit(solution)/shard_map/ppermute | solution.py:567
  25.2 6.4 %collective-permute-start.12 = (bf16[216,128]{1,0:T(8,128)(2,1)S(1)}, bf16[216,128]{1,0:T(8,128)(2,1)S(1)}, u32[]{:S(2)}, u32[]{:S(2)}) collective-permute-start(bf16[216,128]{1,0:T(8,128)(2,1)S(1)} %add_convert_fusion.1), channel_id=1, source_target_pairs={{0,6},{1,7},{2,4},{3,5},{4,2},{5,3},{6,0},{7,1},{8,14},{9,15},{10,... | collective-permute-start | bytes 165896 | tf_op jit(solution)/shard_map/ppermute | solution.py:567
  26.7 5.7 %collective-permute-start.11 = (bf16[216,128]{1,0:T(8,128)(2,1)S(1)}, bf16[216,128]{1,0:T(8,128)(2,1)S(1)}, u32[]{:S(2)}, u32[]{:S(2)}) collective-permute-start(bf16[216,128]{1,0:T(8,128)(2,1)S(1)} %add_convert_fusion.1), channel_id=1, source_target_pairs={{0,3},{1,2},{2,1},{3,0},{4,7},{5,6},{6,5},{7,4},{8,11},{9,10},{10,... | collective-permute-start | bytes 165896 | tf_op jit(solution)/shard_map/ppermute | solution.py:567
  32.4 5.1 %collective-permute-start.16 = (bf16[216,128]{1,0:T(8,128)(2,1)S(1)}, bf16[216,128]{1,0:T(8,128)(2,1)S(1)}, u32[]{:S(2)}, u32[]{:S(2)}) collective-permute-start(bf16[216,128]{1,0:T(8,128)(2,1)S(1)} %add_convert_fusion), channel_id=1, source_target_pairs={{0,24},{1,25},{2,26},{3,27},{4,28},{5,29},{6,30},{7,31},{8,16},{9,... | collective-permute-start | bytes 165896 | tf_op jit(solution)/shard_map/ppermute | solution.py:567
  34.3 4.5 %collective-permute-start.15 = (bf16[216,128]{1,0:T(8,128)(2,1)S(1)}, bf16[216,128]{1,0:T(8,128)(2,1)S(1)}, u32[]{:S(2)}, u32[]{:S(2)}) collective-permute-start(bf16[216,128]{1,0:T(8,128)(2,1)S(1)} %add_convert_fusion), channel_id=1, source_target_pairs={{0,17},{1,16},{2,19},{3,18},{4,21},{5,20},{6,23},{7,22},{8,25},{9,... | collective-permute-start | bytes 165896 | tf_op jit(solution)/shard_map/ppermute | solution.py:567
  34.9 3.8 %collective-permute-start.14 = (bf16[216,128]{1,0:T(8,128)(2,1)S(1)}, bf16[216,128]{1,0:T(8,128)(2,1)S(1)}, u32[]{:S(2)}, u32[]{:S(2)}) collective-permute-start(bf16[216,128]{1,0:T(8,128)(2,1)S(1)} %add_convert_fusion), channel_id=1, source_target_pairs={{0,9},{1,8},{2,11},{3,10},{4,13},{5,12},{6,15},{7,14},{8,1},{9,0},... | collective-permute-start | bytes 165896 | tf_op jit(solution)/shard_map/ppermute | solution.py:567
  38.8 1.6 %collective-permute-start.17 = (bf16[4,216,128]{2,1,0:T(8,128)(2,1)S(1)}, bf16[4,216,128]{2,1,0:T(8,128)(2,1)S(1)}, u32[]{:S(2)}, u32[]{:S(2)}) collective-permute-start(bf16[4,216,128]{2,1,0:T(8,128)(2,1)S(1)} %pad_maximum_fusion.mine), channel_id=1, source_target_pairs={{0,1},{1,0},{2,3},{3,2},{4,5},{5,4},{6,7},{7,6},{8,9},{9,8},{10,11... | collective-permute-start | bytes 663560 | tf_op jit(solution)/shard_map/ppermute | solution.py:599

commit v22 on v20

--- a/solution.py
+++ b/solution.py
@@ -129,7 +129,7 @@
 
 def middle_kernel(lats, grad_out, row_a, row_b, slope, act_t, fields_t, taps,
                   spread, keep, raw_ends, slope_ends, out_ends,
-                  grid, wide, prods, ends, line, sums, corner):
+                  grid, wide, prods, line, sums, corner):
     _, first, last, even, _ = position(lats)
     top = jnp.where(even, row_b[...], row_a[...])
     bottom = jnp.where(even, row_a[...], row_b[...])
@@ -156,14 +156,10 @@
         wide[i, :, 2 * c1:3 * c1] = jnp.where(at == half - 1, 0.0, pltpu.roll(here, half - 1, 0)).astype(BF16)
         wide[i, :, 3 * c1:] = here.astype(BF16)
 
-    flat = wide[1:pooled + 1].reshape(cells, 4 * c1)
+    flat = wide[...].reshape((pooled + 2) * half, 4 * c1)
     for a in range(3):
-        prods[a] = dot_nt(flat, taps[a]).reshape(pooled, half, c2)
-    fold = jnp.where(first, taps[0], taps[2])
-    ends[0] = dot_nt(wide[0], fold)
-    ends[1] = dot_nt(wide[0], taps[1])
-    ends[2] = dot_nt(wide[pooled + 1], taps[0])
-    ends[3] = dot_nt(wide[pooled + 1], taps[1])
+        prods[a] = dot_nt(flat, taps[a]).reshape(pooled + 2, half, c2)
+    fold = jnp.where(first, prods[0, 0], prods[2, 0])
 
     def place(r, total, incline):
         inner = total * incline
@@ -182,19 +178,18 @@
         both = [line[pl.ds(pc, half, stride=2), :] for pc in range(2)]
         return jnp.concatenate([slope_of(v, cdf_of(v)) for v in both], axis=1)
 
-    place(0, ends[0] + ends[1] + prods[0, 0], halo_slope(top))
-    place(1, ends[0] + prods[1, 0] + prods[0, 0], slope[0])
+    place(0, fold + prods[1, 0] + prods[0, 1], halo_slope(top))
+    place(1, fold + prods[1, 1] + prods[0, 1], slope[0])
 
     def pair(i, carry):
-        middle = prods[2, i] + prods[1, i]
-        place(2 * i + 2, middle + prods[0, i + 1], slope[2 * i + 1])
-        place(2 * i + 3, prods[2, i] + prods[1, i + 1] + prods[0, i + 1], slope[2 * i + 2])
+        place(2 * i, prods[2, i] + prods[1, i] + prods[0, i + 1], slope[2 * i - 1])
+        place(2 * i + 1, prods[2, i] + prods[1, i + 1] + prods[0, i + 1], slope[2 * i])
         return carry
 
-    lax.fori_loop(0, pooled - 1, pair, 0)
-    final = prods[2, pooled - 1]
-    place(rows, final + prods[1, pooled - 1] + ends[2], slope[rows - 1])
-    place(rows + 1, (final + ends[3] + ends[2]) * outside, halo_slope(bottom))
+    lax.fori_loop(1, pooled, pair, 0)
+    final, below = prods[2, pooled], prods[0, pooled + 1]
+    place(rows, final + prods[1, pooled] + below, slope[rows - 1])
+    place(rows + 1, (final + prods[1, pooled + 1] + below) * outside, halo_slope(bottom))
 
     is_first = jnp.where(first, 1.0, 0.0).astype(BF16)
     not_first = jnp.where(first, 0.0, 1.0).astype(BF16)
@@ -521,8 +516,7 @@
         scratch_shapes=[
             pltpu.VMEM((pooled + 2, half, c1), F32),
             pltpu.VMEM((pooled + 2, half, 4 * c1), BF16),
-            pltpu.VMEM((3, pooled, half, 2 * c1), F32),
-            pltpu.VMEM((4, half, 2 * c1), F32),
+            pltpu.VMEM((3, pooled + 2, half, 2 * c1), F32),
             pltpu.VMEM((cols, c1), F32),
             pltpu.VMEM((4, 2 * c1, 3 * c1), F32),
             pltpu.VMEM((2 * c1, 3 * c1), F32),

time: 41 us -> 41.1 us (level)
  transfers between devices with their start and end apart: 18 -> 18, of which waited for: 11 -> 11; matrix products, arithmetic and copies ran while one was open for 0% -> 0% of each run, Pallas kernels for 15% -> 16%
where the time goes in v22:
time: 41.1 us; the launch traced here: 40.9 us
  starting transfers between devices  17.2 us (42%)
  waiting for transfers between devices  12.9 us (31%)
  Pallas kernels  9.69 us (24%)
  between operations  0.79 us (2%)
    ppermute x9, starting transfers between devices, between_chips(): lax.ppermute(value, AREA, [(i * lons + j, (i ^ over_lat) * lons + (j ^ 2...  9.71 us
    ppermute x9, waiting for transfers between devices, between_chips(): lax.ppermute(value, AREA, [(i * lons + j, (i ^ over_lat) * lons + (j ^ 2...  8.71 us
    ppermute x1, starting transfers between devices, body(): row_b = lax.ppermute(row_b, AREA, pairs)  4.1 us
    pallas_call x1, Pallas kernels, body(): pl.pallas_call(functools.partial(middle_kernel, lats), out_shape=(shape((...  2.55 us
    pallas_call x1, Pallas kernels, body(): pl.pallas_call(functools.partial(last_kernel, lats), out_shape=shape((row...  2.16 us
    ppermute x1, waiting for transfers between devices, body(): row_a = lax.ppermute(row_a, AREA, every)  1.49 us
    ppermute x1, waiting for transfers between devices, body(): theirs = lax.ppermute(mine, 'lon', swap)  1.37 us
    pallas_call x1, Pallas kernels, body(): pl.pallas_call(functools.partial(columns_kernel, lats), out_shape=(shape(...  1.19 us
  transfers between devices with their start and end apart: 18, of which 11 were waited for; matrix products, arithmetic and copies ran while one was open for 0% of the time, Pallas kernels for 16%

profile of v22, /device:TPU:0, one launch (start us, length us, event | category | flops | bytes accessed | tf_op | source)
XLA Modules:
  0.0 40.9 jit_solution(15445666212642326136)
XLA Ops:
  0.6 0.0 copy-start.3
  0.6 0.0 copy-start
  0.7 0.0 copy-start.2
  0.7 0.0 copy-start.1
  0.7 1.2 %shard_map.76 = (bf16[192,128]{1,0:T(8,128)(2,1)S(1)}, bf16[192,128]{1,0:T(8,128)(2,1)S(1)}, bf16[32,128]{1,0:T(8,128)(2,1)S(1)}, bf16[32,128]{1,0:T(8,128)(2,1)S(1)}, bf16[16,128,128]{2,1,0:T(8,128)(2,1)S(1)}) custom-call(bf16[16,128,128]{2,1,0:T(8,128)(2,1)} %pre_far.1, bf16[8,64,128]{2,1,0:T(8,128)(2,1)} %grad_out.1), custom_call_target="tpu_custom_call" | custom-call | flops 1000 | bytes 262144 | tf_op jit(solution)/shard_map/pallas_call | solution.py:428
  1.9 4.1 %collective-permute-start = (bf16[192,128]{1,0:T(8,128)(2,1)S(1)}, bf16[192,128]{1,0:T(8,128)(2,1)S(1)}, u32[]{:S(2)}, u32[]{:S(2)}) collective-permute-start(bf16[192,128]{1,0:T(8,128)(2,1)S(1)} %get-tuple-element.43), channel_id=1, source_target_pairs={{0,4},{1,5},{2,6},{3,7},{4,0},{5,1},{6,2},{7,3},{24,25},{25,24},{2... | collective-permute-start | bytes 147464 | tf_op jit(solution)/shard_map/ppermute | solution.py:453
  6.0 0.4 collective-permute-start.1
  6.4 0.1 pad.9.clone
  6.4 0.9 %shard_map.77 = (f32[16,64,256]{2,1,0:T(8,128)S(1)}, bf16[2,256,512]{2,1,0:T(8,128)(2,1)S(1)}, f32[2,16,128]{2,1,0:T(8,128)S(1)}) custom-call(bf16[16,128,128]{2,1,0:T(8,128)(2,1)S(1)} %get-tuple-element.45.pre), custom_call_target="tpu_custom_call" | custom-call | flops 15728640 | bytes 2097152 | tf_op jit(solution)/shard_map/pallas_call | solution.py:456
  7.4 0.0 copy-done
  7.4 0.0 copy-done.2
  7.4 0.0 copy-done.1
  7.4 0.7 %shard_map.78 = (bf16[128,1024]{1,0:T(8,128)(2,1)S(1)}, bf16[128,32]{1,0:T(8,128)(2,1)S(1)}, bf16[384,512]{1,0:T(8,128)(2,1)S(1)}, bf16[3,256,512]{2,1,0:T(8,128)(2,1)S(1)}) custom-call(bf16[16,64,128]{2,1,0:T(8,128)(2,1)S(1)} %bitcast.8, bf16[3,3,64,128]{3,2,1,0:T(8,128)(2,1)S(1)} %copy-done.2, bf16[3,3,128,128]{3,2,1,0:T(8,128)(2,1)S(1)} %copy-done), custom_call_target="tpu_custom_call" | custom-call | flops 67108864 | bytes 3145728 | tf_op jit(solution)/shard_map/pallas_call | solution.py:474
  8.1 0.4 %collective-permute-done.row_b = bf16[192,128]{1,0:T(8,128)(2,1)S(1)} collective-permute-done((bf16[192,128]{1,0:T(8,128)(2,1)S(1)}, bf16[192,128]{1,0:T(8,128)(2,1)S(1)}, u32[]{:S(2)}, u32[]{:S(2)}) %collective-permute-start) | collective-permute-done | bytes 49184 | tf_op jit(solution)/shard_map/ppermute | solution.py:453
  8.6 1.5 %collective-permute-done.1.row_a = bf16[192,128]{1,0:T(8,128)(2,1)S(1)} collective-permute-done((bf16[192,128]{1,0:T(8,128)(2,1)S(1)}, bf16[192,128]{1,0:T(8,128)(2,1)S(1)}, u32[]{:S(2)}, u32[]{:S(2)}) %collective-permute-start.1) | collective-permute-done | bytes 49184 | tf_op jit(solution)/shard_map/ppermute | solution.py:454
  10.1 0.1 maximum_maximum_fusion.1
  10.2 0.8 %collective-permute-start.3 = (bf16[32,128]{1,0:T(8,128)(2,1)S(1)}, bf16[32,128]{1,0:T(8,128)(2,1)S(1)}, u32[]{:S(2)}, u32[]{:S(2)}) collective-permute-start(bf16[32,128]{1,0:T(8,128)(2,1)S(1)} %get-tuple-element.93), channel_id=1, source_target_pairs={{0,7},{1,2},{2,1},{3,4},{4,3},{5,6},{6,5},{7,0},{8,15},{9,10},{10,... | collective-permute-start | bytes 24584 | tf_op jit(solution)/shard_map/ppermute | solution.py:499
  11.0 0.9 %collective-permute-start.2 = (bf16[32,128]{1,0:T(8,128)(2,1)S(1)}, bf16[32,128]{1,0:T(8,128)(2,1)S(1)}, u32[]{:S(2)}, u32[]{:S(2)}) collective-permute-start(bf16[32,128]{1,0:T(8,128)(2,1)S(1)} %get-tuple-element.94), channel_id=1, source_target_pairs={{0,1},{1,0},{2,3},{3,2},{4,5},{5,4},{6,7},{7,6},{8,9},{9,8},{10,11... | collective-permute-start | bytes 24584 | tf_op jit(solution)/shard_map/ppermute | solution.py:500
  11.9 0.0 copy-done.3
  11.9 2.6 %shard_map.79 = (bf16[19,64,512]{2,1,0:T(8,128)(2,1)S(1)}, f32[1728,128]{1,0:T(8,128)S(1)}, f32[2,32,128]{2,1,0:T(8,128)S(1)}, f32[2,32,128]{2,1,0:T(8,128)S(1)}, f32[2,16,128]{2,1,0:T(8,128)S(1)}) custom-call(bf16[8,64,128]{2,1,0:T(8,128)(2,1)S(1)} %copy-done.3, bf16[192,128]{1,0:T(8,128)(2,1)S(1)} %collective-permute-done.1.row_a, ...), custom_call_target="tpu_custom_call" | custom-call | flops 1509949440 | bytes 8388608 | tf_op jit(solution)/shard_map/pallas_call | solution.py:505
  14.5 0.6 %collective-permute-done.3.col_b = bf16[32,128]{1,0:T(8,128)(2,1)S(1)} collective-permute-done((bf16[32,128]{1,0:T(8,128)(2,1)S(1)}, bf16[32,128]{1,0:T(8,128)(2,1)S(1)}, u32[]{:S(2)}, u32[]{:S(2)}) %collective-permute-start.3) | collective-permute-done | bytes 8224 | tf_op jit(solution)/shard_map/ppermute | solution.py:499
  15.1 0.0 collective-permute-done.2.col_a
  15.1 1.2 %shard_map.80 = (bf16[4,32,128]{2,1,0:T(8,128)(2,1)S(1)}, f32[216,128]{1,0:T(8,128)S(1)}, f32[216,128]{1,0:T(8,128)S(1)}, f32[216,128]{1,0:T(8,128)S(1)}, f32[21...) custom-call(bf16[32,128]{1,0:T(8,128)(2,1)S(1)} %collective-permute-, ...), custom_call_target="tpu_custom_call" | custom-call | flops 268435456 | bytes 3145728 | tf_op jit(solution)/shard_map/pallas_call | solution.py:530
  16.3 0.1 collective-permute-start.4
  16.4 0.5 %collective-permute-start.6 = (f32[216,128]{1,0:T(8,128)S(1)}, f32[216,128]{1,0:T(8,128)S(1)}, u32[]{:S(2)}, u32[]{:S(2)}) collective-permute-start(f32[216,128]{1,0:T(8,128)S(1)} %get-tuple-element.67), channel_id=1, source_target_pairs={{0,1},{1,0},{2,3},{3,2},{4,5},{5,4},{6,7},{7,6},{8,9},{9,8},{10,11... | collective-permute-start | bytes 331784 | tf_op jit(solution)/shard_map/ppermute | solution.py:555
  16.8 0.1 collective-permute-start.8
  16.9 0.4 %collective-permute-start.10 = (f32[216,128]{1,0:T(8,128)S(1)}, f32[216,128]{1,0:T(8,128)S(1)}, u32[]{:S(2)}, u32[]{:S(2)}) collective-permute-start(f32[216,128]{1,0:T(8,128)S(1)} %get-tuple-element.75), channel_id=1, source_target_pairs={{0,1},{1,0},{2,3},{3,2},{4,5},{5,4},{6,7},{7,6},{8,9},{9,8},{10,11... | collective-permute-start | bytes 331784 | tf_op jit(solution)/shard_map/ppermute | solution.py:555
  17.4 0.3 collective-permute-done.4
  17.7 0.6 %collective-permute-start.5 = (bf16[216,128]{1,0:T(8,128)(2,1)S(1)}, bf16[216,128]{1,0:T(8,128)(2,1)S(1)}, u32[]{:S(2)}, u32[]{:S(2)}) collective-permute-start(bf16[216,128]{1,0:T(8,128)(2,1)S(1)} %add_convert_fusion.4), channel_id=1, source_target_pairs={{0,24},{1,25},{2,26},{3,27},{4,28},{5,29},{6,30},{7,31},{8,16},{9,... | collective-permute-start | bytes 165896 | tf_op jit(solution)/shard_map/ppermute | solution.py:551
  18.3 0.0 collective-permute-done.6
  18.3 0.8 %collective-permute-start.7 = (bf16[216,128]{1,0:T(8,128)(2,1)S(1)}, bf16[216,128]{1,0:T(8,128)(2,1)S(1)}, u32[]{:S(2)}, u32[]{:S(2)}) collective-permute-start(bf16[216,128]{1,0:T(8,128)(2,1)S(1)} %add_convert_fusion.3), channel_id=1, source_target_pairs={{0,17},{1,16},{2,19},{3,18},{4,21},{5,20},{6,23},{7,22},{8,25},{9,... | collective-permute-start | bytes 165896 | tf_op jit(solution)/shard_map/ppermute | solution.py:551
  19.2 0.0 collective-permute-done.8
  19.2 1.9 %collective-permute-start.9 = (bf16[216,128]{1,0:T(8,128)(2,1)S(1)}, bf16[216,128]{1,0:T(8,128)(2,1)S(1)}, u32[]{:S(2)}, u32[]{:S(2)}) collective-permute-start(bf16[216,128]{1,0:T(8,128)(2,1)S(1)} %add_convert_fusion.2), channel_id=1, source_target_pairs={{0,9},{1,8},{2,11},{3,10},{4,13},{5,12},{6,15},{7,14},{8,1},{9,0},... | collective-permute-start | bytes 165896 | tf_op jit(solution)/shard_map/ppermute | solution.py:551
  21.1 2.2 %shard_map.81 = bf16[16,64,128]{2,1,0:T(8,128)(2,1)} custom-call(bf16[19,64,512]{2,1,0:T(8,128)(2,1)S(1)} %get-tuple-element.70.part, bf16[4,32,128]{2,1,0:T(8,128)(2,1)S(1)} %get-tuple-element.71.ends, bf16[384,512]{1,0:T(8,128)(2,1)S(1)} %get-tuple-element.72.taps), custom_call_target="tpu_custom_call" | custom-call | flops 301989888 | bytes 3145728 | tf_op jit(solution)/shard_map/pallas_call | solution.py:558
  23.3 0.0 collective-permute-done.5
  23.3 0.3 collective-permute-done.7
  23.6 0.0 collective-permute-done.9
  23.6 0.0 collective-permute-done.10
  23.7 1.5 %collective-permute-start.13 = (bf16[216,128]{1,0:T(8,128)(2,1)S(1)}, bf16[216,128]{1,0:T(8,128)(2,1)S(1)}, u32[]{:S(2)}, u32[]{:S(2)}) collective-permute-start(bf16[216,128]{1,0:T(8,128)(2,1)S(1)} %add_convert_fusion.1), channel_id=1, source_target_pairs={{0,5},{1,4},{2,7},{3,6},{4,1},{5,0},{6,3},{7,2},{8,13},{9,12},{10,... | collective-permute-start | bytes 165896 | tf_op jit(solution)/shard_map/ppermute | solution.py:551
  25.2 1.3 %collective-permute-start.12 = (bf16[216,128]{1,0:T(8,128)(2,1)S(1)}, bf16[216,128]{1,0:T(8,128)(2,1)S(1)}, u32[]{:S(2)}, u32[]{:S(2)}) collective-permute-start(bf16[216,128]{1,0:T(8,128)(2,1)S(1)} %add_convert_fusion.1), channel_id=1, source_target_pairs={{0,6},{1,7},{2,4},{3,5},{4,2},{5,3},{6,0},{7,1},{8,14},{9,15},{10,... | collective-permute-start | bytes 165896 | tf_op jit(solution)/shard_map/ppermute | solution.py:551
  26.5 0.2 collective-permute-start.11
  26.7 3.6 %collective-permute-done.13 = bf16[216,128]{1,0:T(8,128)(2,1)S(1)} collective-permute-done((bf16[216,128]{1,0:T(8,128)(2,1)S(1)}, bf16[216,128]{1,0:T(8,128)(2,1)S(1)}, u32[]{:S(2)}, u32[]{:S(2)}) %collective-permute-start.13) | collective-permute-done | bytes 55328 | tf_op jit(solution)/shard_map/ppermute | solution.py:551
  30.3 1.0 %collective-permute-done.12 = bf16[216,128]{1,0:T(8,128)(2,1)S(1)} collective-permute-done((bf16[216,128]{1,0:T(8,128)(2,1)S(1)}, bf16[216,128]{1,0:T(8,128)(2,1)S(1)}, u32[]{:S(2)}, u32[]{:S(2)}) %collective-permute-start.12) | collective-permute-done | bytes 55328 | tf_op jit(solution)/shard_map/ppermute | solution.py:551
  31.3 0.7 %collective-permute-done.11 = bf16[216,128]{1,0:T(8,128)(2,1)S(1)} collective-permute-done((bf16[216,128]{1,0:T(8,128)(2,1)S(1)}, bf16[216,128]{1,0:T(8,128)(2,1)S(1)}, u32[]{:S(2)}, u32[]{:S(2)}) %collective-permute-start.11) | collective-permute-done | bytes 55328 | tf_op jit(solution)/shard_map/ppermute | solution.py:551
  32.1 1.6 %collective-permute-start.16 = (bf16[216,128]{1,0:T(8,128)(2,1)S(1)}, bf16[216,128]{1,0:T(8,128)(2,1)S(1)}, u32[]{:S(2)}, u32[]{:S(2)}) collective-permute-start(bf16[216,128]{1,0:T(8,128)(2,1)S(1)} %add_convert_fusion), channel_id=1, source_target_pairs={{0,24},{1,25},{2,26},{3,27},{4,28},{5,29},{6,30},{7,31},{8,16},{9,... | collective-permute-start | bytes 165896 | tf_op jit(solution)/shard_map/ppermute | solution.py:551
  33.6 0.5 %collective-permute-start.15 = (bf16[216,128]{1,0:T(8,128)(2,1)S(1)}, bf16[216,128]{1,0:T(8,128)(2,1)S(1)}, u32[]{:S(2)}, u32[]{:S(2)}) collective-permute-start(bf16[216,128]{1,0:T(8,128)(2,1)S(1)} %add_convert_fusion), channel_id=1, source_target_pairs={{0,17},{1,16},{2,19},{3,18},{4,21},{5,20},{6,23},{7,22},{8,25},{9,... | collective-permute-start | bytes 165896 | tf_op jit(solution)/shard_map/ppermute | solution.py:551
  34.1 1.2 %collective-permute-start.14 = (bf16[216,128]{1,0:T(8,128)(2,1)S(1)}, bf16[216,128]{1,0:T(8,128)(2,1)S(1)}, u32[]{:S(2)}, u32[]{:S(2)}) collective-permute-start(bf16[216,128]{1,0:T(8,128)(2,1)S(1)} %add_convert_fusion), channel_id=1, source_target_pairs={{0,9},{1,8},{2,11},{3,10},{4,13},{5,12},{6,15},{7,14},{8,1},{9,0},... | collective-permute-start | bytes 165896 | tf_op jit(solution)/shard_map/ppermute | solution.py:551
  35.4 1.9 %collective-permute-done.16 = bf16[216,128]{1,0:T(8,128)(2,1)S(1)} collective-permute-done((bf16[216,128]{1,0:T(8,128)(2,1)S(1)}, bf16[216,128]{1,0:T(8,128)(2,1)S(1)}, u32[]{:S(2)}, u32[]{:S(2)}) %collective-permute-start.16) | collective-permute-done | bytes 55328 | tf_op jit(solution)/shard_map/ppermute | solution.py:551
  37.3 1.1 %collective-permute-done.15 = bf16[216,128]{1,0:T(8,128)(2,1)S(1)} collective-permute-done((bf16[216,128]{1,0:T(8,128)(2,1)S(1)}, bf16[216,128]{1,0:T(8,128)(2,1)S(1)}, u32[]{:S(2)}, u32[]{:S(2)}) %collective-permute-start.15) | collective-permute-done | bytes 55328 | tf_op jit(solution)/shard_map/ppermute | solution.py:551
  38.4 0.0 collective-permute-done.14
  38.4 0.2 collective-permute-start.17
  38.6 1.4 %collective-permute-done.17.theirs = bf16[4,216,128]{2,1,0:T(8,128)(2,1)S(1)} collective-permute-done((bf16[4,216,128]{2,1,0:T(8,128)(2,1)S(1)}, bf16[4,216,128]{2,1,0:T(8,128)(2,1)S(1)}, u32[]{:S(2)}, u32[]{:S(2)}) %collective-permute-start.17) | collective-permute-done | bytes 221216 | tf_op jit(solution)/shard_map/ppermute | solution.py:583
  40.0 1.0 %shard_map.82 = (f32[576,128]{1,0:T(8,128)}, f32[1152,128]{1,0:T(8,128)}) custom-call(bf16[4,216,128]{2,1,0:T(8,128)(2,1)S(1)} %pad_maximum_fusion.mine, bf16[4,216,128]{2,1,0:T(8,128)(2,1)S(1)} %collective-permute-done.17.theirs), custom_call_target="tpu_custom_call" | custom-call | flops 1000 | bytes 1572864 | tf_op jit(solution)/shard_map/pallas_call | solution.py:585
  (12 shorter events, 0.2 us)
Async XLA Ops:
  0.6 11.3 %copy-start.3 = (bf16[8,64,128]{2,1,0:T(8,128)(2,1)S(1)}, bf16[8,64,128]{2,1,0:T(8,128)(2,1)}, u32[]{:S(2)}) copy-start(bf16[8,64,128]{2,1,0:T(8,128)(2,1)} %grad_out.1) | copy-start | bytes 393220
  0.6 6.7 %copy-start = (bf16[3,3,128,128]{3,2,1,0:T(8,128)(2,1)S(1)}, bf16[3,3,128,128]{3,2,1,0:T(8,128)(2,1)}, u32[]{:S(2)}) copy-start(bf16[3,3,128,128]{3,2,1,0:T(8,128)(2,1)} %w_second.1) | copy-start | bytes 884740
  0.7 6.7 %copy-start.2 = (bf16[3,3,64,128]{3,2,1,0:T(8,128)(2,1)S(1)}, bf16[3,3,64,128]{3,2,1,0:T(8,128)(2,1)}, u32[]{:S(2)}) copy-start(bf16[3,3,64,128]{3,2,1,0:T(8,128)(2,1)} %w_first.1) | copy-start | bytes 442372
  0.7 6.7 %copy-start.1 = (bf16[16,128,64]{1,2,0:T(8,128)(2,1)S(1)}, bf16[16,128,64]{1,2,0:T(8,128)(2,1)}, u32[]{:S(2)}) copy-start(bf16[16,128,64]{1,2,0:T(8,128)(2,1)} %param.5) | copy-start | bytes 786436
  1.9 6.7 %collective-permute-start = (bf16[192,128]{1,0:T(8,128)(2,1)S(1)}, bf16[192,128]{1,0:T(8,128)(2,1)S(1)}, u32[]{:S(2)}, u32[]{:S(2)}) collective-permute-start(bf16[192,128]{1,0:T(8,128)(2,1)S(1)} %get-tuple-element.43), channel_id=1, source_target_pairs={{0,4},{1,5},{2,6},{3,7},{4,0},{5,1},{6,2},{7,3},{24,25},{25,24},{2... | collective-permute-start | bytes 147464 | tf_op jit(solution)/shard_map/ppermute | solution.py:453
  6.0 4.1 %collective-permute-start.1 = (bf16[192,128]{1,0:T(8,128)(2,1)S(1)}, bf16[192,128]{1,0:T(8,128)(2,1)S(1)}, u32[]{:S(2)}, u32[]{:S(2)}) collective-permute-start(bf16[192,128]{1,0:T(8,128)(2,1)S(1)} %get-tuple-element.44), channel_id=1, source_target_pairs={{0,8},{1,9},{2,10},{3,11},{4,12},{5,13},{6,14},{7,15},{8,0},{9,1},... | collective-permute-start | bytes 147464 | tf_op jit(solution)/shard_map/ppermute | solution.py:454
  10.2 4.9 %collective-permute-start.3 = (bf16[32,128]{1,0:T(8,128)(2,1)S(1)}, bf16[32,128]{1,0:T(8,128)(2,1)S(1)}, u32[]{:S(2)}, u32[]{:S(2)}) collective-permute-start(bf16[32,128]{1,0:T(8,128)(2,1)S(1)} %get-tuple-element.93), channel_id=1, source_target_pairs={{0,7},{1,2},{2,1},{3,4},{4,3},{5,6},{6,5},{7,0},{8,15},{9,10},{10,... | collective-permute-start | bytes 24584 | tf_op jit(solution)/shard_map/ppermute | solution.py:499
  11.0 4.1 %collective-permute-start.2 = (bf16[32,128]{1,0:T(8,128)(2,1)S(1)}, bf16[32,128]{1,0:T(8,128)(2,1)S(1)}, u32[]{:S(2)}, u32[]{:S(2)}) collective-permute-start(bf16[32,128]{1,0:T(8,128)(2,1)S(1)} %get-tuple-element.94), channel_id=1, source_target_pairs={{0,1},{1,0},{2,3},{3,2},{4,5},{5,4},{6,7},{7,6},{8,9},{9,8},{10,11... | collective-permute-start | bytes 24584 | tf_op jit(solution)/shard_map/ppermute | solution.py:500
  16.3 1.4 %collective-permute-start.4 = (f32[216,128]{1,0:T(8,128)S(1)}, f32[216,128]{1,0:T(8,128)S(1)}, u32[]{:S(2)}, u32[]{:S(2)}) collective-permute-start(f32[216,128]{1,0:T(8,128)S(1)} %get-tuple-element.65), channel_id=1, source_target_pairs={{0,1},{1,0},{2,3},{3,2},{4,5},{5,4},{6,7},{7,6},{8,9},{9,8},{10,11... | collective-permute-start | bytes 331784 | tf_op jit(solution)/shard_map/ppermute | solution.py:555
  16.4 1.9 %collective-permute-start.6 = (f32[216,128]{1,0:T(8,128)S(1)}, f32[216,128]{1,0:T(8,128)S(1)}, u32[]{:S(2)}, u32[]{:S(2)}) collective-permute-start(f32[216,128]{1,0:T(8,128)S(1)} %get-tuple-element.67), channel_id=1, source_target_pairs={{0,1},{1,0},{2,3},{3,2},{4,5},{5,4},{6,7},{7,6},{8,9},{9,8},{10,11... | collective-permute-start | bytes 331784 | tf_op jit(solution)/shard_map/ppermute | solution.py:555
  16.8 2.3 %collective-permute-start.8 = (f32[216,128]{1,0:T(8,128)S(1)}, f32[216,128]{1,0:T(8,128)S(1)}, u32[]{:S(2)}, u32[]{:S(2)}) collective-permute-start(f32[216,128]{1,0:T(8,128)S(1)} %get-tuple-element.69), channel_id=1, source_target_pairs={{0,1},{1,0},{2,3},{3,2},{4,5},{5,4},{6,7},{7,6},{8,9},{9,8},{10,11... | collective-permute-start | bytes 331784 | tf_op jit(solution)/shard_map/ppermute | solution.py:555
  16.9 6.7 %collective-permute-start.10 = (f32[216,128]{1,0:T(8,128)S(1)}, f32[216,128]{1,0:T(8,128)S(1)}, u32[]{:S(2)}, u32[]{:S(2)}) collective-permute-start(f32[216,128]{1,0:T(8,128)S(1)} %get-tuple-element.75), channel_id=1, source_target_pairs={{0,1},{1,0},{2,3},{3,2},{4,5},{5,4},{6,7},{7,6},{8,9},{9,8},{10,11... | collective-permute-start | bytes 331784 | tf_op jit(solution)/shard_map/ppermute | solution.py:555
  17.7 5.6 %collective-permute-start.5 = (bf16[216,128]{1,0:T(8,128)(2,1)S(1)}, bf16[216,128]{1,0:T(8,128)(2,1)S(1)}, u32[]{:S(2)}, u32[]{:S(2)}) collective-permute-start(bf16[216,128]{1,0:T(8,128)(2,1)S(1)} %add_convert_fusion.4), channel_id=1, source_target_pairs={{0,24},{1,25},{2,26},{3,27},{4,28},{5,29},{6,30},{7,31},{8,16},{9,... | collective-permute-start | bytes 165896 | tf_op jit(solution)/shard_map/ppermute | solution.py:551
  18.3 5.3 %collective-permute-start.7 = (bf16[216,128]{1,0:T(8,128)(2,1)S(1)}, bf16[216,128]{1,0:T(8,128)(2,1)S(1)}, u32[]{:S(2)}, u32[]{:S(2)}) collective-permute-start(bf16[216,128]{1,0:T(8,128)(2,1)S(1)} %add_convert_fusion.3), channel_id=1, source_target_pairs={{0,17},{1,16},{2,19},{3,18},{4,21},{5,20},{6,23},{7,22},{8,25},{9,... | collective-permute-start | bytes 165896 | tf_op jit(solution)/shard_map/ppermute | solution.py:551
  19.2 4.4 %collective-permute-start.9 = (bf16[216,128]{1,0:T(8,128)(2,1)S(1)}, bf16[216,128]{1,0:T(8,128)(2,1)S(1)}, u32[]{:S(2)}, u32[]{:S(2)}) collective-permute-start(bf16[216,128]{1,0:T(8,128)(2,1)S(1)} %add_convert_fusion.2), channel_id=1, source_target_pairs={{0,9},{1,8},{2,11},{3,10},{4,13},{5,12},{6,15},{7,14},{8,1},{9,0},... | collective-permute-start | bytes 165896 | tf_op jit(solution)/shard_map/ppermute | solution.py:551
  23.7 6.7 %collective-permute-start.13 = (bf16[216,128]{1,0:T(8,128)(2,1)S(1)}, bf16[216,128]{1,0:T(8,128)(2,1)S(1)}, u32[]{:S(2)}, u32[]{:S(2)}) collective-permute-start(bf16[216,128]{1,0:T(8,128)(2,1)S(1)} %add_convert_fusion.1), channel_id=1, source_target_pairs={{0,5},{1,4},{2,7},{3,6},{4,1},{5,0},{6,3},{7,2},{8,13},{9,12},{10,... | collective-permute-start | bytes 165896 | tf_op jit(solution)/shard_map/ppermute | solution.py:551
  25.2 6.1 %collective-permute-start.12 = (bf16[216,128]{1,0:T(8,128)(2,1)S(1)}, bf16[216,128]{1,0:T(8,128)(2,1)S(1)}, u32[]{:S(2)}, u32[]{:S(2)}) collective-permute-start(bf16[216,128]{1,0:T(8,128)(2,1)S(1)} %add_convert_fusion.1), channel_id=1, source_target_pairs={{0,6},{1,7},{2,4},{3,5},{4,2},{5,3},{6,0},{7,1},{8,14},{9,15},{10,... | collective-permute-start | bytes 165896 | tf_op jit(solution)/shard_map/ppermute | solution.py:551
  26.5 5.5 %collective-permute-start.11 = (bf16[216,128]{1,0:T(8,128)(2,1)S(1)}, bf16[216,128]{1,0:T(8,128)(2,1)S(1)}, u32[]{:S(2)}, u32[]{:S(2)}) collective-permute-start(bf16[216,128]{1,0:T(8,128)(2,1)S(1)} %add_convert_fusion.1), channel_id=1, source_target_pairs={{0,3},{1,2},{2,1},{3,0},{4,7},{5,6},{6,5},{7,4},{8,11},{9,10},{10,... | collective-permute-start | bytes 165896 | tf_op jit(solution)/shard_map/ppermute | solution.py:551
  32.1 5.2 %collective-permute-start.16 = (bf16[216,128]{1,0:T(8,128)(2,1)S(1)}, bf16[216,128]{1,0:T(8,128)(2,1)S(1)}, u32[]{:S(2)}, u32[]{:S(2)}) collective-permute-start(bf16[216,128]{1,0:T(8,128)(2,1)S(1)} %add_convert_fusion), channel_id=1, source_target_pairs={{0,24},{1,25},{2,26},{3,27},{4,28},{5,29},{6,30},{7,31},{8,16},{9,... | collective-permute-start | bytes 165896 | tf_op jit(solution)/shard_map/ppermute | solution.py:551
  33.6 4.7 %collective-permute-start.15 = (bf16[216,128]{1,0:T(8,128)(2,1)S(1)}, bf16[216,128]{1,0:T(8,128)(2,1)S(1)}, u32[]{:S(2)}, u32[]{:S(2)}) collective-permute-start(bf16[216,128]{1,0:T(8,128)(2,1)S(1)} %add_convert_fusion), channel_id=1, source_target_pairs={{0,17},{1,16},{2,19},{3,18},{4,21},{5,20},{6,23},{7,22},{8,25},{9,... | collective-permute-start | bytes 165896 | tf_op jit(solution)/shard_map/ppermute | solution.py:551
  34.1 4.3 %collective-permute-start.14 = (bf16[216,128]{1,0:T(8,128)(2,1)S(1)}, bf16[216,128]{1,0:T(8,128)(2,1)S(1)}, u32[]{:S(2)}, u32[]{:S(2)}) collective-permute-start(bf16[216,128]{1,0:T(8,128)(2,1)S(1)} %add_convert_fusion), channel_id=1, source_target_pairs={{0,9},{1,8},{2,11},{3,10},{4,13},{5,12},{6,15},{7,14},{8,1},{9,0},... | collective-permute-start | bytes 165896 | tf_op jit(solution)/shard_map/ppermute | solution.py:551
  38.4 1.5 %collective-permute-start.17 = (bf16[4,216,128]{2,1,0:T(8,128)(2,1)S(1)}, bf16[4,216,128]{2,1,0:T(8,128)(2,1)S(1)}, u32[]{:S(2)}, u32[]{:S(2)}) collective-permute-start(bf16[4,216,128]{2,1,0:T(8,128)(2,1)S(1)} %pad_maximum_fusion.mine), channel_id=1, source_target_pairs={{0,1},{1,0},{2,3},{3,2},{4,5},{5,4},{6,7},{7,6},{8,9},{9,8},{10,11... | collective-permute-start | bytes 663560 | tf_op jit(solution)/shard_map/ppermute | solution.py:583

commit v23 on v20

--- a/solution.py
+++ b/solution.py
@@ -558,9 +558,11 @@
             (i * lons + j, (i ^ over_lat) * lons + (j ^ (2 * over_lon) ^ turn)) for i in range(lats) for j in range(lons)])
 
     own, other = halves[:lats], halves[lats:]
-    other = {far: lax.ppermute(other[far], "lon", swap) for far in reversed(range(lats))}
-    parts = [own[far] + other[far] for far in range(lats)]
-    got = [between_chips(parts[far].astype(BF16), far, 0) for far in reversed(range(1, lats))]
+    swapped = {far: lax.ppermute(other[far], "lon", swap) for far in reversed(range(1, lats))}
+    sent = {far: (own[far] + swapped[far]).astype(BF16) for far in reversed(range(1, lats))}
+    sent[lats - 1], late = lax.optimization_barrier((sent[lats - 1], other[0]))
+    got = [between_chips(sent[far], far, 0) for far in reversed(range(1, lats))]
+    parts = [own[0] + lax.ppermute(late, "lon", swap)]
     grad_inputs = pl.pallas_call(
         functools.partial(last_kernel, lats),
         out_shape=shape((rows, c0, cols), BF16),

time: 41 us -> 41.4 us (level)
  waiting for transfers between devices: 13 us -> 13.8 us
  starting transfers between devices: 17.2 us -> 16.7 us
    ppermute x4 -> x3, starting transfers between devices: 1.08 us -> 0.65 us  [body(): lax.ppermute(other[far], 'lon', swap)]
    ppermute x4 -> x3, waiting for transfers between devices: 0.3 us -> 0.73 us  [body(): lax.ppermute(other[far], 'lon', swap)]
  transfers between devices with their start and end apart: 18 -> 18, of which waited for: 11 -> 12; matrix products, arithmetic and copies ran while one was open for 0% -> 0% of each run, Pallas kernels for 15% -> 15%
where the time goes in v23:
time: 41.4 us; the launch traced here: 41.3 us
  starting transfers between devices  16.7 us (40%)
  waiting for transfers between devices  13.8 us (33%)
  Pallas kernels  9.54 us (23%)
  between operations  0.79 us (2%)
    ppermute x9, starting transfers between devices, between_chips(): lax.ppermute(value, AREA, [(i * lons + j, (i ^ over_lat) * lons + (j ^ 2...  9.71 us
    ppermute x9, waiting for transfers between devices, between_chips(): lax.ppermute(value, AREA, [(i * lons + j, (i ^ over_lat) * lons + (j ^ 2...  9.02 us
    ppermute x1, starting transfers between devices, body(): row_b = lax.ppermute(row_b, AREA, pairs)  4.1 us
    pallas_call x1, Pallas kernels, body(): pl.pallas_call(functools.partial(middle_kernel, lats), out_shape=(shape((...  2.4 us
    pallas_call x1, Pallas kernels, body(): pl.pallas_call(functools.partial(last_kernel, lats), out_shape=shape((row...  2.16 us
    ppermute x1, waiting for transfers between devices, body(): row_a = lax.ppermute(row_a, AREA, every)  1.49 us
    ppermute x1, waiting for transfers between devices, body(): theirs = lax.ppermute(mine, 'lon', swap)  1.36 us
    pallas_call x1, Pallas kernels, body(): pl.pallas_call(functools.partial(columns_kernel, lats), out_shape=(shape(...  1.19 us
  transfers between devices with their start and end apart: 18, of which 12 were waited for; matrix products, arithmetic and copies ran while one was open for 0% of the time, Pallas kernels for 15%

profile of v23, /device:TPU:0, one launch (start us, length us, event | category | flops | bytes accessed | tf_op | source)
XLA Modules:
  0.0 41.3 jit_solution(9679315434333572125)
XLA Ops:
  0.6 0.0 copy-start.3
  0.6 0.0 copy-start
  0.7 0.0 copy-start.2
  0.7 0.0 copy-start.1
  0.7 1.2 %shard_map.76 = (bf16[192,128]{1,0:T(8,128)(2,1)S(1)}, bf16[192,128]{1,0:T(8,128)(2,1)S(1)}, bf16[32,128]{1,0:T(8,128)(2,1)S(1)}, bf16[32,128]{1,0:T(8,128)(2,1)S(1)}, bf16[16,128,128]{2,1,0:T(8,128)(2,1)S(1)}) custom-call(bf16[16,128,128]{2,1,0:T(8,128)(2,1)} %pre_far.1, bf16[8,64,128]{2,1,0:T(8,128)(2,1)} %grad_out.1), custom_call_target="tpu_custom_call" | custom-call | flops 1000 | bytes 262144 | tf_op jit(solution)/shard_map/pallas_call | solution.py:433
  1.9 4.1 %collective-permute-start = (bf16[192,128]{1,0:T(8,128)(2,1)S(1)}, bf16[192,128]{1,0:T(8,128)(2,1)S(1)}, u32[]{:S(2)}, u32[]{:S(2)}) collective-permute-start(bf16[192,128]{1,0:T(8,128)(2,1)S(1)} %get-tuple-element.45), channel_id=1, source_target_pairs={{0,4},{1,5},{2,6},{3,7},{4,0},{5,1},{6,2},{7,3},{24,25},{25,24},{2... | collective-permute-start | bytes 147464 | tf_op jit(solution)/shard_map/ppermute | solution.py:458
  6.0 0.4 collective-permute-start.1
  6.4 0.1 pad.9.clone
  6.4 0.9 %shard_map.77 = (f32[16,64,256]{2,1,0:T(8,128)S(1)}, bf16[2,256,512]{2,1,0:T(8,128)(2,1)S(1)}, f32[2,16,128]{2,1,0:T(8,128)S(1)}) custom-call(bf16[16,128,128]{2,1,0:T(8,128)(2,1)S(1)} %get-tuple-element.47.pre), custom_call_target="tpu_custom_call" | custom-call | flops 15728640 | bytes 2097152 | tf_op jit(solution)/shard_map/pallas_call | solution.py:461
  7.4 0.0 copy-done
  7.4 0.0 copy-done.2
  7.4 0.0 copy-done.1
  7.4 0.7 %shard_map.78 = (bf16[128,1024]{1,0:T(8,128)(2,1)S(1)}, bf16[128,32]{1,0:T(8,128)(2,1)S(1)}, bf16[384,512]{1,0:T(8,128)(2,1)S(1)}, bf16[3,256,512]{2,1,0:T(8,128)(2,1)S(1)}) custom-call(bf16[16,64,128]{2,1,0:T(8,128)(2,1)S(1)} %bitcast.8, bf16[3,3,64,128]{3,2,1,0:T(8,128)(2,1)S(1)} %copy-done.2, bf16[3,3,128,128]{3,2,1,0:T(8,128)(2,1)S(1)} %copy-done), custom_call_target="tpu_custom_call" | custom-call | flops 67108864 | bytes 3145728 | tf_op jit(solution)/shard_map/pallas_call | solution.py:479
  8.1 0.4 %collective-permute-done.row_b = bf16[192,128]{1,0:T(8,128)(2,1)S(1)} collective-permute-done((bf16[192,128]{1,0:T(8,128)(2,1)S(1)}, bf16[192,128]{1,0:T(8,128)(2,1)S(1)}, u32[]{:S(2)}, u32[]{:S(2)}) %collective-permute-start) | collective-permute-done | bytes 49184 | tf_op jit(solution)/shard_map/ppermute | solution.py:458
  8.6 1.5 %collective-permute-done.1.row_a = bf16[192,128]{1,0:T(8,128)(2,1)S(1)} collective-permute-done((bf16[192,128]{1,0:T(8,128)(2,1)S(1)}, bf16[192,128]{1,0:T(8,128)(2,1)S(1)}, u32[]{:S(2)}, u32[]{:S(2)}) %collective-permute-start.1) | collective-permute-done | bytes 49184 | tf_op jit(solution)/shard_map/ppermute | solution.py:459
  10.1 0.1 maximum_maximum_fusion.1
  10.2 0.8 %collective-permute-start.3 = (bf16[32,128]{1,0:T(8,128)(2,1)S(1)}, bf16[32,128]{1,0:T(8,128)(2,1)S(1)}, u32[]{:S(2)}, u32[]{:S(2)}) collective-permute-start(bf16[32,128]{1,0:T(8,128)(2,1)S(1)} %get-tuple-element.97), channel_id=1, source_target_pairs={{0,7},{1,2},{2,1},{3,4},{4,3},{5,6},{6,5},{7,0},{8,15},{9,10},{10,... | collective-permute-start | bytes 24584 | tf_op jit(solution)/shard_map/ppermute | solution.py:504
  11.0 0.9 %collective-permute-start.2 = (bf16[32,128]{1,0:T(8,128)(2,1)S(1)}, bf16[32,128]{1,0:T(8,128)(2,1)S(1)}, u32[]{:S(2)}, u32[]{:S(2)}) collective-permute-start(bf16[32,128]{1,0:T(8,128)(2,1)S(1)} %get-tuple-element.98), channel_id=1, source_target_pairs={{0,1},{1,0},{2,3},{3,2},{4,5},{5,4},{6,7},{7,6},{8,9},{9,8},{10,11... | collective-permute-start | bytes 24584 | tf_op jit(solution)/shard_map/ppermute | solution.py:505
  11.9 0.0 copy-done.3
  11.9 2.4 %shard_map.79 = (bf16[19,64,512]{2,1,0:T(8,128)(2,1)S(1)}, f32[1728,128]{1,0:T(8,128)S(1)}, f32[2,32,128]{2,1,0:T(8,128)S(1)}, f32[2,32,128]{2,1,0:T(8,128)S(1)}, f32[2,16,128]{2,1,0:T(8,128)S(1)}) custom-call(bf16[8,64,128]{2,1,0:T(8,128)(2,1)S(1)} %copy-done.3, bf16[192,128]{1,0:T(8,128)(2,1)S(1)} %collective-permute-done.1.row_a, ...), custom_call_target="tpu_custom_call" | custom-call | flops 1509949440 | bytes 8388608 | tf_op jit(solution)/shard_map/pallas_call | solution.py:510
  14.3 0.8 %collective-permute-done.3.col_b = bf16[32,128]{1,0:T(8,128)(2,1)S(1)} collective-permute-done((bf16[32,128]{1,0:T(8,128)(2,1)S(1)}, bf16[32,128]{1,0:T(8,128)(2,1)S(1)}, u32[]{:S(2)}, u32[]{:S(2)}) %collective-permute-start.3) | collective-permute-done | bytes 8224 | tf_op jit(solution)/shard_map/ppermute | solution.py:504
  15.1 0.0 collective-permute-done.2.col_a
  15.1 1.2 %shard_map.80 = (bf16[4,32,128]{2,1,0:T(8,128)(2,1)S(1)}, f32[216,128]{1,0:T(8,128)S(1)}, f32[216,128]{1,0:T(8,128)S(1)}, f32[216,128]{1,0:T(8,128)S(1)}, f32[21...) custom-call(bf16[32,128]{1,0:T(8,128)(2,1)S(1)} %collective-permute-, ...), custom_call_target="tpu_custom_call" | custom-call | flops 268435456 | bytes 3145728 | tf_op jit(solution)/shard_map/pallas_call | solution.py:536
  16.3 0.1 collective-permute-start.4
  16.4 0.5 %collective-permute-start.6 = (f32[216,128]{1,0:T(8,128)S(1)}, f32[216,128]{1,0:T(8,128)S(1)}, u32[]{:S(2)}, u32[]{:S(2)}) collective-permute-start(f32[216,128]{1,0:T(8,128)S(1)} %get-tuple-element.71), channel_id=1, source_target_pairs={{0,1},{1,0},{2,3},{3,2},{4,5},{5,4},{6,7},{7,6},{8,9},{9,8},{10,11... | collective-permute-start | bytes 331784 | tf_op jit(solution)/shard_map/ppermute | solution.py:561
  16.8 0.1 collective-permute-start.8
  16.9 0.7 %collective-permute-done.4 = f32[216,128]{1,0:T(8,128)S(1)} collective-permute-done((f32[216,128]{1,0:T(8,128)S(1)}, f32[216,128]{1,0:T(8,128)S(1)}, u32[]{:S(2)}, u32[]{:S(2)}) %collective-permute-start.4) | collective-permute-done | bytes 110624 | tf_op jit(solution)/shard_map/ppermute | solution.py:561
  17.7 0.5 %collective-permute-start.5 = (bf16[216,128]{1,0:T(8,128)(2,1)S(1)}, bf16[216,128]{1,0:T(8,128)(2,1)S(1)}, u32[]{:S(2)}, u32[]{:S(2)}) collective-permute-start(bf16[216,128]{1,0:T(8,128)(2,1)S(1)} %add_convert_fusion.4), channel_id=1, source_target_pairs={{0,24},{1,25},{2,26},{3,27},{4,28},{5,29},{6,30},{7,31},{8,16},{9,... | collective-permute-start | bytes 165896 | tf_op jit(solution)/shard_map/ppermute | solution.py:557
  18.2 0.0 collective-permute-start.10
  18.2 0.0 collective-permute-done.6
  18.2 1.6 %collective-permute-start.7 = (bf16[216,128]{1,0:T(8,128)(2,1)S(1)}, bf16[216,128]{1,0:T(8,128)(2,1)S(1)}, u32[]{:S(2)}, u32[]{:S(2)}) collective-permute-start(bf16[216,128]{1,0:T(8,128)(2,1)S(1)} %add_convert_fusion.3), channel_id=1, source_target_pairs={{0,17},{1,16},{2,19},{3,18},{4,21},{5,20},{6,23},{7,22},{8,25},{9,... | collective-permute-start | bytes 165896 | tf_op jit(solution)/shard_map/ppermute | solution.py:557
  19.8 0.0 collective-permute-done.8
  19.8 1.3 %collective-permute-start.9 = (bf16[216,128]{1,0:T(8,128)(2,1)S(1)}, bf16[216,128]{1,0:T(8,128)(2,1)S(1)}, u32[]{:S(2)}, u32[]{:S(2)}) collective-permute-start(bf16[216,128]{1,0:T(8,128)(2,1)S(1)} %add_convert_fusion.2), channel_id=1, source_target_pairs={{0,9},{1,8},{2,11},{3,10},{4,13},{5,12},{6,15},{7,14},{8,1},{9,0},... | collective-permute-start | bytes 165896 | tf_op jit(solution)/shard_map/ppermute | solution.py:557
  21.1 2.2 %shard_map.81 = bf16[16,64,128]{2,1,0:T(8,128)(2,1)} custom-call(bf16[19,64,512]{2,1,0:T(8,128)(2,1)S(1)} %get-tuple-element.74.part, bf16[4,32,128]{2,1,0:T(8,128)(2,1)S(1)} %get-tuple-element.75.ends, bf16[384,512]{1,0:T(8,128)(2,1)S(1)} %get-tuple-element.76.taps), custom_call_target="tpu_custom_call" | custom-call | flops 301989888 | bytes 3145728 | tf_op jit(solution)/shard_map/pallas_call | solution.py:566
  23.3 0.0 collective-permute-done.5
  23.3 0.2 collective-permute-done.7
  23.5 0.4 collective-permute-done.9
  23.9 0.0 collective-permute-done.10
  23.9 1.6 %collective-permute-start.13 = (bf16[216,128]{1,0:T(8,128)(2,1)S(1)}, bf16[216,128]{1,0:T(8,128)(2,1)S(1)}, u32[]{:S(2)}, u32[]{:S(2)}) collective-permute-start(bf16[216,128]{1,0:T(8,128)(2,1)S(1)} %add_convert_fusion.1), channel_id=1, source_target_pairs={{0,5},{1,4},{2,7},{3,6},{4,1},{5,0},{6,3},{7,2},{8,13},{9,12},{10,... | collective-permute-start | bytes 165896 | tf_op jit(solution)/shard_map/ppermute | solution.py:557
  25.5 1.4 %collective-permute-start.12 = (bf16[216,128]{1,0:T(8,128)(2,1)S(1)}, bf16[216,128]{1,0:T(8,128)(2,1)S(1)}, u32[]{:S(2)}, u32[]{:S(2)}) collective-permute-start(bf16[216,128]{1,0:T(8,128)(2,1)S(1)} %add_convert_fusion.1), channel_id=1, source_target_pairs={{0,6},{1,7},{2,4},{3,5},{4,2},{5,3},{6,0},{7,1},{8,14},{9,15},{10,... | collective-permute-start | bytes 165896 | tf_op jit(solution)/shard_map/ppermute | solution.py:557
  26.9 0.0 collective-permute-start.11
  26.9 3.0 %collective-permute-done.13 = bf16[216,128]{1,0:T(8,128)(2,1)S(1)} collective-permute-done((bf16[216,128]{1,0:T(8,128)(2,1)S(1)}, bf16[216,128]{1,0:T(8,128)(2,1)S(1)}, u32[]{:S(2)}, u32[]{:S(2)}) %collective-permute-start.13) | collective-permute-done | bytes 55328 | tf_op jit(solution)/shard_map/ppermute | solution.py:557
  30.0 2.1 %collective-permute-done.12 = bf16[216,128]{1,0:T(8,128)(2,1)S(1)} collective-permute-done((bf16[216,128]{1,0:T(8,128)(2,1)S(1)}, bf16[216,128]{1,0:T(8,128)(2,1)S(1)}, u32[]{:S(2)}, u32[]{:S(2)}) %collective-permute-start.12) | collective-permute-done | bytes 55328 | tf_op jit(solution)/shard_map/ppermute | solution.py:557
  32.0 0.4 %collective-permute-done.11 = bf16[216,128]{1,0:T(8,128)(2,1)S(1)} collective-permute-done((bf16[216,128]{1,0:T(8,128)(2,1)S(1)}, bf16[216,128]{1,0:T(8,128)(2,1)S(1)}, u32[]{:S(2)}, u32[]{:S(2)}) %collective-permute-start.11) | collective-permute-done | bytes 55328 | tf_op jit(solution)/shard_map/ppermute | solution.py:557
  32.5 1.4 %collective-permute-start.16 = (bf16[216,128]{1,0:T(8,128)(2,1)S(1)}, bf16[216,128]{1,0:T(8,128)(2,1)S(1)}, u32[]{:S(2)}, u32[]{:S(2)}) collective-permute-start(bf16[216,128]{1,0:T(8,128)(2,1)S(1)} %add_convert_fusion), channel_id=1, source_target_pairs={{0,24},{1,25},{2,26},{3,27},{4,28},{5,29},{6,30},{7,31},{8,16},{9,... | collective-permute-start | bytes 165896 | tf_op jit(solution)/shard_map/ppermute | solution.py:557
  34.0 0.5 %collective-permute-start.15 = (bf16[216,128]{1,0:T(8,128)(2,1)S(1)}, bf16[216,128]{1,0:T(8,128)(2,1)S(1)}, u32[]{:S(2)}, u32[]{:S(2)}) collective-permute-start(bf16[216,128]{1,0:T(8,128)(2,1)S(1)} %add_convert_fusion), channel_id=1, source_target_pairs={{0,17},{1,16},{2,19},{3,18},{4,21},{5,20},{6,23},{7,22},{8,25},{9,... | collective-permute-start | bytes 165896 | tf_op jit(solution)/shard_map/ppermute | solution.py:557
  34.4 1.3 %collective-permute-start.14 = (bf16[216,128]{1,0:T(8,128)(2,1)S(1)}, bf16[216,128]{1,0:T(8,128)(2,1)S(1)}, u32[]{:S(2)}, u32[]{:S(2)}) collective-permute-start(bf16[216,128]{1,0:T(8,128)(2,1)S(1)} %add_convert_fusion), channel_id=1, source_target_pairs={{0,9},{1,8},{2,11},{3,10},{4,13},{5,12},{6,15},{7,14},{8,1},{9,0},... | collective-permute-start | bytes 165896 | tf_op jit(solution)/shard_map/ppermute | solution.py:557
  35.8 2.0 %collective-permute-done.16 = bf16[216,128]{1,0:T(8,128)(2,1)S(1)} collective-permute-done((bf16[216,128]{1,0:T(8,128)(2,1)S(1)}, bf16[216,128]{1,0:T(8,128)(2,1)S(1)}, u32[]{:S(2)}, u32[]{:S(2)}) %collective-permute-start.16) | collective-permute-done | bytes 55328 | tf_op jit(solution)/shard_map/ppermute | solution.py:557
  37.7 1.0 %collective-permute-done.15 = bf16[216,128]{1,0:T(8,128)(2,1)S(1)} collective-permute-done((bf16[216,128]{1,0:T(8,128)(2,1)S(1)}, bf16[216,128]{1,0:T(8,128)(2,1)S(1)}, u32[]{:S(2)}, u32[]{:S(2)}) %collective-permute-start.15) | collective-permute-done | bytes 55328 | tf_op jit(solution)/shard_map/ppermute | solution.py:557
  38.7 0.0 collective-permute-done.14
  38.7 0.2 collective-permute-start.17
  38.9 1.4 %collective-permute-done.17.theirs = bf16[4,216,128]{2,1,0:T(8,128)(2,1)S(1)} collective-permute-done((bf16[4,216,128]{2,1,0:T(8,128)(2,1)S(1)}, bf16[4,216,128]{2,1,0:T(8,128)(2,1)S(1)}, u32[]{:S(2)}, u32[]{:S(2)}) %collective-permute-start.17) | collective-permute-done | bytes 221216 | tf_op jit(solution)/shard_map/ppermute | solution.py:591
  40.3 1.0 %shard_map.82 = (f32[576,128]{1,0:T(8,128)}, f32[1152,128]{1,0:T(8,128)}) custom-call(bf16[4,216,128]{2,1,0:T(8,128)(2,1)S(1)} %pad_maximum_fusion.mine, bf16[4,216,128]{2,1,0:T(8,128)(2,1)S(1)} %collective-permute-done.17.theirs), custom_call_target="tpu_custom_call" | custom-call | flops 1000 | bytes 1572864 | tf_op jit(solution)/shard_map/pallas_call | solution.py:593
  (12 shorter events, 0.2 us)
Async XLA Ops:
  0.6 11.3 %copy-start.3 = (bf16[8,64,128]{2,1,0:T(8,128)(2,1)S(1)}, bf16[8,64,128]{2,1,0:T(8,128)(2,1)}, u32[]{:S(2)}) copy-start(bf16[8,64,128]{2,1,0:T(8,128)(2,1)} %grad_out.1) | copy-start | bytes 393220
  0.6 6.7 %copy-start = (bf16[3,3,128,128]{3,2,1,0:T(8,128)(2,1)S(1)}, bf16[3,3,128,128]{3,2,1,0:T(8,128)(2,1)}, u32[]{:S(2)}) copy-start(bf16[3,3,128,128]{3,2,1,0:T(8,128)(2,1)} %w_second.1) | copy-start | bytes 884740
  0.7 6.7 %copy-start.2 = (bf16[3,3,64,128]{3,2,1,0:T(8,128)(2,1)S(1)}, bf16[3,3,64,128]{3,2,1,0:T(8,128)(2,1)}, u32[]{:S(2)}) copy-start(bf16[3,3,64,128]{3,2,1,0:T(8,128)(2,1)} %w_first.1) | copy-start | bytes 442372
  0.7 6.7 %copy-start.1 = (bf16[16,128,64]{1,2,0:T(8,128)(2,1)S(1)}, bf16[16,128,64]{1,2,0:T(8,128)(2,1)}, u32[]{:S(2)}) copy-start(bf16[16,128,64]{1,2,0:T(8,128)(2,1)} %param.5) | copy-start | bytes 786436
  1.9 6.7 %collective-permute-start = (bf16[192,128]{1,0:T(8,128)(2,1)S(1)}, bf16[192,128]{1,0:T(8,128)(2,1)S(1)}, u32[]{:S(2)}, u32[]{:S(2)}) collective-permute-start(bf16[192,128]{1,0:T(8,128)(2,1)S(1)} %get-tuple-element.45), channel_id=1, source_target_pairs={{0,4},{1,5},{2,6},{3,7},{4,0},{5,1},{6,2},{7,3},{24,25},{25,24},{2... | collective-permute-start | bytes 147464 | tf_op jit(solution)/shard_map/ppermute | solution.py:458
  6.0 4.1 %collective-permute-start.1 = (bf16[192,128]{1,0:T(8,128)(2,1)S(1)}, bf16[192,128]{1,0:T(8,128)(2,1)S(1)}, u32[]{:S(2)}, u32[]{:S(2)}) collective-permute-start(bf16[192,128]{1,0:T(8,128)(2,1)S(1)} %get-tuple-element.46), channel_id=1, source_target_pairs={{0,8},{1,9},{2,10},{3,11},{4,12},{5,13},{6,14},{7,15},{8,0},{9,1},... | collective-permute-start | bytes 147464 | tf_op jit(solution)/shard_map/ppermute | solution.py:459
  10.2 4.9 %collective-permute-start.3 = (bf16[32,128]{1,0:T(8,128)(2,1)S(1)}, bf16[32,128]{1,0:T(8,128)(2,1)S(1)}, u32[]{:S(2)}, u32[]{:S(2)}) collective-permute-start(bf16[32,128]{1,0:T(8,128)(2,1)S(1)} %get-tuple-element.97), channel_id=1, source_target_pairs={{0,7},{1,2},{2,1},{3,4},{4,3},{5,6},{6,5},{7,0},{8,15},{9,10},{10,... | collective-permute-start | bytes 24584 | tf_op jit(solution)/shard_map/ppermute | solution.py:504
  11.0 4.1 %collective-permute-start.2 = (bf16[32,128]{1,0:T(8,128)(2,1)S(1)}, bf16[32,128]{1,0:T(8,128)(2,1)S(1)}, u32[]{:S(2)}, u32[]{:S(2)}) collective-permute-start(bf16[32,128]{1,0:T(8,128)(2,1)S(1)} %get-tuple-element.98), channel_id=1, source_target_pairs={{0,1},{1,0},{2,3},{3,2},{4,5},{5,4},{6,7},{7,6},{8,9},{9,8},{10,11... | collective-permute-start | bytes 24584 | tf_op jit(solution)/shard_map/ppermute | solution.py:505
  16.3 1.4 %collective-permute-start.4 = (f32[216,128]{1,0:T(8,128)S(1)}, f32[216,128]{1,0:T(8,128)S(1)}, u32[]{:S(2)}, u32[]{:S(2)}) collective-permute-start(f32[216,128]{1,0:T(8,128)S(1)} %get-tuple-element.67), channel_id=1, source_target_pairs={{0,1},{1,0},{2,3},{3,2},{4,5},{5,4},{6,7},{7,6},{8,9},{9,8},{10,11... | collective-permute-start | bytes 331784 | tf_op jit(solution)/shard_map/ppermute | solution.py:561
  16.4 1.9 %collective-permute-start.6 = (f32[216,128]{1,0:T(8,128)S(1)}, f32[216,128]{1,0:T(8,128)S(1)}, u32[]{:S(2)}, u32[]{:S(2)}) collective-permute-start(f32[216,128]{1,0:T(8,128)S(1)} %get-tuple-element.71), channel_id=1, source_target_pairs={{0,1},{1,0},{2,3},{3,2},{4,5},{5,4},{6,7},{7,6},{8,9},{9,8},{10,11... | collective-permute-start | bytes 331784 | tf_op jit(solution)/shard_map/ppermute | solution.py:561
  16.8 3.0 %collective-permute-start.8 = (f32[216,128]{1,0:T(8,128)S(1)}, f32[216,128]{1,0:T(8,128)S(1)}, u32[]{:S(2)}, u32[]{:S(2)}) collective-permute-start(f32[216,128]{1,0:T(8,128)S(1)} %get-tuple-element.73), channel_id=1, source_target_pairs={{0,1},{1,0},{2,3},{3,2},{4,5},{5,4},{6,7},{7,6},{8,9},{9,8},{10,11... | collective-permute-start | bytes 331784 | tf_op jit(solution)/shard_map/ppermute | solution.py:561
  17.7 5.6 %collective-permute-start.5 = (bf16[216,128]{1,0:T(8,128)(2,1)S(1)}, bf16[216,128]{1,0:T(8,128)(2,1)S(1)}, u32[]{:S(2)}, u32[]{:S(2)}) collective-permute-start(bf16[216,128]{1,0:T(8,128)(2,1)S(1)} %add_convert_fusion.4), channel_id=1, source_target_pairs={{0,24},{1,25},{2,26},{3,27},{4,28},{5,29},{6,30},{7,31},{8,16},{9,... | collective-permute-start | bytes 165896 | tf_op jit(solution)/shard_map/ppermute | solution.py:557
  18.2 5.7 %collective-permute-start.10 = (f32[216,128]{1,0:T(8,128)S(1)}, f32[216,128]{1,0:T(8,128)S(1)}, u32[]{:S(2)}, u32[]{:S(2)}) collective-permute-start(f32[216,128]{1,0:T(8,128)S(1)} %get-tuple-element.79), channel_id=1, source_target_pairs={{0,1},{1,0},{2,3},{3,2},{4,5},{5,4},{6,7},{7,6},{8,9},{9,8},{10,11... | collective-permute-start | bytes 331784 | tf_op jit(solution)/shard_map/ppermute | solution.py:565
  18.2 5.2 %collective-permute-start.7 = (bf16[216,128]{1,0:T(8,128)(2,1)S(1)}, bf16[216,128]{1,0:T(8,128)(2,1)S(1)}, u32[]{:S(2)}, u32[]{:S(2)}) collective-permute-start(bf16[216,128]{1,0:T(8,128)(2,1)S(1)} %add_convert_fusion.3), channel_id=1, source_target_pairs={{0,17},{1,16},{2,19},{3,18},{4,21},{5,20},{6,23},{7,22},{8,25},{9,... | collective-permute-start | bytes 165896 | tf_op jit(solution)/shard_map/ppermute | solution.py:557
  19.8 4.0 %collective-permute-start.9 = (bf16[216,128]{1,0:T(8,128)(2,1)S(1)}, bf16[216,128]{1,0:T(8,128)(2,1)S(1)}, u32[]{:S(2)}, u32[]{:S(2)}) collective-permute-start(bf16[216,128]{1,0:T(8,128)(2,1)S(1)} %add_convert_fusion.2), channel_id=1, source_target_pairs={{0,9},{1,8},{2,11},{3,10},{4,13},{5,12},{6,15},{7,14},{8,1},{9,0},... | collective-permute-start | bytes 165896 | tf_op jit(solution)/shard_map/ppermute | solution.py:557
  23.9 6.0 %collective-permute-start.13 = (bf16[216,128]{1,0:T(8,128)(2,1)S(1)}, bf16[216,128]{1,0:T(8,128)(2,1)S(1)}, u32[]{:S(2)}, u32[]{:S(2)}) collective-permute-start(bf16[216,128]{1,0:T(8,128)(2,1)S(1)} %add_convert_fusion.1), channel_id=1, source_target_pairs={{0,5},{1,4},{2,7},{3,6},{4,1},{5,0},{6,3},{7,2},{8,13},{9,12},{10,... | collective-permute-start | bytes 165896 | tf_op jit(solution)/shard_map/ppermute | solution.py:557
  25.5 6.5 %collective-permute-start.12 = (bf16[216,128]{1,0:T(8,128)(2,1)S(1)}, bf16[216,128]{1,0:T(8,128)(2,1)S(1)}, u32[]{:S(2)}, u32[]{:S(2)}) collective-permute-start(bf16[216,128]{1,0:T(8,128)(2,1)S(1)} %add_convert_fusion.1), channel_id=1, source_target_pairs={{0,6},{1,7},{2,4},{3,5},{4,2},{5,3},{6,0},{7,1},{8,14},{9,15},{10,... | collective-permute-start | bytes 165896 | tf_op jit(solution)/shard_map/ppermute | solution.py:557
  26.9 5.6 %collective-permute-start.11 = (bf16[216,128]{1,0:T(8,128)(2,1)S(1)}, bf16[216,128]{1,0:T(8,128)(2,1)S(1)}, u32[]{:S(2)}, u32[]{:S(2)}) collective-permute-start(bf16[216,128]{1,0:T(8,128)(2,1)S(1)} %add_convert_fusion.1), channel_id=1, source_target_pairs={{0,3},{1,2},{2,1},{3,0},{4,7},{5,6},{6,5},{7,4},{8,11},{9,10},{10,... | collective-permute-start | bytes 165896 | tf_op jit(solution)/shard_map/ppermute | solution.py:557
  32.5 5.2 %collective-permute-start.16 = (bf16[216,128]{1,0:T(8,128)(2,1)S(1)}, bf16[216,128]{1,0:T(8,128)(2,1)S(1)}, u32[]{:S(2)}, u32[]{:S(2)}) collective-permute-start(bf16[216,128]{1,0:T(8,128)(2,1)S(1)} %add_convert_fusion), channel_id=1, source_target_pairs={{0,24},{1,25},{2,26},{3,27},{4,28},{5,29},{6,30},{7,31},{8,16},{9,... | collective-permute-start | bytes 165896 | tf_op jit(solution)/shard_map/ppermute | solution.py:557
  34.0 4.7 %collective-permute-start.15 = (bf16[216,128]{1,0:T(8,128)(2,1)S(1)}, bf16[216,128]{1,0:T(8,128)(2,1)S(1)}, u32[]{:S(2)}, u32[]{:S(2)}) collective-permute-start(bf16[216,128]{1,0:T(8,128)(2,1)S(1)} %add_convert_fusion), channel_id=1, source_target_pairs={{0,17},{1,16},{2,19},{3,18},{4,21},{5,20},{6,23},{7,22},{8,25},{9,... | collective-permute-start | bytes 165896 | tf_op jit(solution)/shard_map/ppermute | solution.py:557
  34.4 4.3 %collective-permute-start.14 = (bf16[216,128]{1,0:T(8,128)(2,1)S(1)}, bf16[216,128]{1,0:T(8,128)(2,1)S(1)}, u32[]{:S(2)}, u32[]{:S(2)}) collective-permute-start(bf16[216,128]{1,0:T(8,128)(2,1)S(1)} %add_convert_fusion), channel_id=1, source_target_pairs={{0,9},{1,8},{2,11},{3,10},{4,13},{5,12},{6,15},{7,14},{8,1},{9,0},... | collective-permute-start | bytes 165896 | tf_op jit(solution)/shard_map/ppermute | solution.py:557
  38.7 1.5 %collective-permute-start.17 = (bf16[4,216,128]{2,1,0:T(8,128)(2,1)S(1)}, bf16[4,216,128]{2,1,0:T(8,128)(2,1)S(1)}, u32[]{:S(2)}, u32[]{:S(2)}) collective-permute-start(bf16[4,216,128]{2,1,0:T(8,128)(2,1)S(1)} %pad_maximum_fusion.mine), channel_id=1, source_target_pairs={{0,1},{1,0},{2,3},{3,2},{4,5},{5,4},{6,7},{7,6},{8,9},{9,8},{10,11... | collective-permute-start | bytes 663560 | tf_op jit(solution)/shard_map/ppermute | solution.py:591

commit v24 on v20

--- a/solution.py
+++ b/solution.py
@@ -583,7 +583,7 @@
     terms = [part] + [between_chips(part, 0, far) for far in range(1, depths)]
     terms = [term.astype(F32) for term in terms]
     while len(terms) > 1:
-        terms = [terms[k + (k > 0)] + terms[k + (k == 0)] for k in range(0, len(terms), 2)]
+        terms = [terms[k] + terms[k + 1] for k in range(0, len(terms), 2)]
     part = terms[0].astype(BF16)
     mine = jnp.stack([part] + [between_chips(part, far, 0) for far in range(1, lats)], 0)
     theirs = lax.ppermute(mine, "lon", swap)

time: 41 us -> 40.9 us (level)
  waiting for transfers between devices: 13 us -> 11.6 us
  starting transfers between devices: 17.2 us -> 18.4 us
    ppermute x9, waiting for transfers between devices: 8.61 us -> 7.33 us  [between_chips(): lax.ppermute(value, AREA, [(i * lons + j, (i ^ over_lat) * lons + (j ^ 2...]
    ppermute x9, starting transfers between devices: 9.71 us -> 10.9 us  [between_chips(): lax.ppermute(value, AREA, [(i * lons + j, (i ^ over_lat) * lons + (j ^ 2...]
where the time goes in v24:
time: 40.9 us; the launch traced here: 40.7 us
  starting transfers between devices  18.4 us (45%)
  waiting for transfers between devices  11.6 us (28%)
  Pallas kernels  9.53 us (23%)
  between operations  0.79 us (2%)
    ppermute x9, starting transfers between devices, between_chips(): lax.ppermute(value, AREA, [(i * lons + j, (i ^ over_lat) * lons + (j ^ 2...  10.9 us
    ppermute x9, waiting for transfers between devices, between_chips(): lax.ppermute(value, AREA, [(i * lons + j, (i ^ over_lat) * lons + (j ^ 2...  7.33 us
    ppermute x1, starting transfers between devices, body(): row_b = lax.ppermute(row_b, AREA, pairs)  4.1 us
    pallas_call x1, Pallas kernels, body(): pl.pallas_call(functools.partial(middle_kernel, lats), out_shape=(shape((...  2.4 us
    pallas_call x1, Pallas kernels, body(): pl.pallas_call(functools.partial(last_kernel, lats), out_shape=shape((row...  2.16 us
    ppermute x1, waiting for transfers between devices, body(): row_a = lax.ppermute(row_a, AREA, every)  1.49 us
    ppermute x1, waiting for transfers between devices, body(): theirs = lax.ppermute(mine, 'lon', swap)  1.23 us
    pallas_call x1, Pallas kernels, body(): pl.pallas_call(functools.partial(columns_kernel, lats), out_shape=(shape(...  1.19 us
  transfers between devices with their start and end apart: 18, of which 11 were waited for; matrix products, arithmetic and copies ran while one was open for 0% of the time, Pallas kernels for 15%

profile of v24, /device:TPU:0, one launch (start us, length us, event | category | flops | bytes accessed | tf_op | source)
XLA Modules:
  0.0 40.7 jit_solution(14755417884985764829)
XLA Ops:
  0.6 0.0 copy-start.3
  0.6 0.0 copy-start
  0.7 0.0 copy-start.2
  0.7 0.0 copy-start.1
  0.7 1.2 %shard_map.76 = (bf16[192,128]{1,0:T(8,128)(2,1)S(1)}, bf16[192,128]{1,0:T(8,128)(2,1)S(1)}, bf16[32,128]{1,0:T(8,128)(2,1)S(1)}, bf16[32,128]{1,0:T(8,128)(2,1)S(1)}, bf16[16,128,128]{2,1,0:T(8,128)(2,1)S(1)}) custom-call(bf16[16,128,128]{2,1,0:T(8,128)(2,1)} %pre_far.1, bf16[8,64,128]{2,1,0:T(8,128)(2,1)} %grad_out.1), custom_call_target="tpu_custom_call" | custom-call | flops 1000 | bytes 262144 | tf_op jit(solution)/shard_map/pallas_call | solution.py:433
  1.9 4.1 %collective-permute-start = (bf16[192,128]{1,0:T(8,128)(2,1)S(1)}, bf16[192,128]{1,0:T(8,128)(2,1)S(1)}, u32[]{:S(2)}, u32[]{:S(2)}) collective-permute-start(bf16[192,128]{1,0:T(8,128)(2,1)S(1)} %get-tuple-element.43), channel_id=1, source_target_pairs={{0,4},{1,5},{2,6},{3,7},{4,0},{5,1},{6,2},{7,3},{24,25},{25,24},{2... | collective-permute-start | bytes 147464 | tf_op jit(solution)/shard_map/ppermute | solution.py:458
  6.0 0.4 collective-permute-start.1
  6.4 0.1 pad.9.clone
  6.4 0.9 %shard_map.77 = (f32[16,64,256]{2,1,0:T(8,128)S(1)}, bf16[2,256,512]{2,1,0:T(8,128)(2,1)S(1)}, f32[2,16,128]{2,1,0:T(8,128)S(1)}) custom-call(bf16[16,128,128]{2,1,0:T(8,128)(2,1)S(1)} %get-tuple-element.45.pre), custom_call_target="tpu_custom_call" | custom-call | flops 15728640 | bytes 2097152 | tf_op jit(solution)/shard_map/pallas_call | solution.py:461
  7.4 0.0 copy-done
  7.4 0.0 copy-done.2
  7.4 0.0 copy-done.1
  7.4 0.7 %shard_map.78 = (bf16[128,1024]{1,0:T(8,128)(2,1)S(1)}, bf16[128,32]{1,0:T(8,128)(2,1)S(1)}, bf16[384,512]{1,0:T(8,128)(2,1)S(1)}, bf16[3,256,512]{2,1,0:T(8,128)(2,1)S(1)}) custom-call(bf16[16,64,128]{2,1,0:T(8,128)(2,1)S(1)} %bitcast.8, bf16[3,3,64,128]{3,2,1,0:T(8,128)(2,1)S(1)} %copy-done.2, bf16[3,3,128,128]{3,2,1,0:T(8,128)(2,1)S(1)} %copy-done), custom_call_target="tpu_custom_call" | custom-call | flops 67108864 | bytes 3145728 | tf_op jit(solution)/shard_map/pallas_call | solution.py:479
  8.1 0.4 %collective-permute-done.row_b = bf16[192,128]{1,0:T(8,128)(2,1)S(1)} collective-permute-done((bf16[192,128]{1,0:T(8,128)(2,1)S(1)}, bf16[192,128]{1,0:T(8,128)(2,1)S(1)}, u32[]{:S(2)}, u32[]{:S(2)}) %collective-permute-start) | collective-permute-done | bytes 49184 | tf_op jit(solution)/shard_map/ppermute | solution.py:458
  8.6 1.5 %collective-permute-done.1.row_a = bf16[192,128]{1,0:T(8,128)(2,1)S(1)} collective-permute-done((bf16[192,128]{1,0:T(8,128)(2,1)S(1)}, bf16[192,128]{1,0:T(8,128)(2,1)S(1)}, u32[]{:S(2)}, u32[]{:S(2)}) %collective-permute-start.1) | collective-permute-done | bytes 49184 | tf_op jit(solution)/shard_map/ppermute | solution.py:459
  10.1 0.1 maximum_maximum_fusion.1
  10.2 0.8 %collective-permute-start.3 = (bf16[32,128]{1,0:T(8,128)(2,1)S(1)}, bf16[32,128]{1,0:T(8,128)(2,1)S(1)}, u32[]{:S(2)}, u32[]{:S(2)}) collective-permute-start(bf16[32,128]{1,0:T(8,128)(2,1)S(1)} %get-tuple-element.93), channel_id=1, source_target_pairs={{0,7},{1,2},{2,1},{3,4},{4,3},{5,6},{6,5},{7,0},{8,15},{9,10},{10,... | collective-permute-start | bytes 24584 | tf_op jit(solution)/shard_map/ppermute | solution.py:504
  11.0 0.9 %collective-permute-start.2 = (bf16[32,128]{1,0:T(8,128)(2,1)S(1)}, bf16[32,128]{1,0:T(8,128)(2,1)S(1)}, u32[]{:S(2)}, u32[]{:S(2)}) collective-permute-start(bf16[32,128]{1,0:T(8,128)(2,1)S(1)} %get-tuple-element.94), channel_id=1, source_target_pairs={{0,1},{1,0},{2,3},{3,2},{4,5},{5,4},{6,7},{7,6},{8,9},{9,8},{10,11... | collective-permute-start | bytes 24584 | tf_op jit(solution)/shard_map/ppermute | solution.py:505
  11.9 0.0 copy-done.3
  11.9 2.4 %shard_map.79 = (bf16[19,64,512]{2,1,0:T(8,128)(2,1)S(1)}, f32[1728,128]{1,0:T(8,128)S(1)}, f32[2,32,128]{2,1,0:T(8,128)S(1)}, f32[2,32,128]{2,1,0:T(8,128)S(1)}, f32[2,16,128]{2,1,0:T(8,128)S(1)}) custom-call(bf16[8,64,128]{2,1,0:T(8,128)(2,1)S(1)} %copy-done.3, bf16[192,128]{1,0:T(8,128)(2,1)S(1)} %collective-permute-done.1.row_a, ...), custom_call_target="tpu_custom_call" | custom-call | flops 1509949440 | bytes 8388608 | tf_op jit(solution)/shard_map/pallas_call | solution.py:510
  14.3 0.8 %collective-permute-done.3.col_b = bf16[32,128]{1,0:T(8,128)(2,1)S(1)} collective-permute-done((bf16[32,128]{1,0:T(8,128)(2,1)S(1)}, bf16[32,128]{1,0:T(8,128)(2,1)S(1)}, u32[]{:S(2)}, u32[]{:S(2)}) %collective-permute-start.3) | collective-permute-done | bytes 8224 | tf_op jit(solution)/shard_map/ppermute | solution.py:504
  15.1 0.0 collective-permute-done.2.col_a
  15.1 1.2 %shard_map.80 = (bf16[4,32,128]{2,1,0:T(8,128)(2,1)S(1)}, f32[216,128]{1,0:T(8,128)S(1)}, f32[216,128]{1,0:T(8,128)S(1)}, f32[216,128]{1,0:T(8,128)S(1)}, f32[21...) custom-call(bf16[32,128]{1,0:T(8,128)(2,1)S(1)} %collective-permute-, ...), custom_call_target="tpu_custom_call" | custom-call | flops 268435456 | bytes 3145728 | tf_op jit(solution)/shard_map/pallas_call | solution.py:536
  16.3 0.1 collective-permute-start.4
  16.4 0.5 %collective-permute-start.6 = (f32[216,128]{1,0:T(8,128)S(1)}, f32[216,128]{1,0:T(8,128)S(1)}, u32[]{:S(2)}, u32[]{:S(2)}) collective-permute-start(f32[216,128]{1,0:T(8,128)S(1)} %get-tuple-element.67), channel_id=1, source_target_pairs={{0,1},{1,0},{2,3},{3,2},{4,5},{5,4},{6,7},{7,6},{8,9},{9,8},{10,11... | collective-permute-start | bytes 331784 | tf_op jit(solution)/shard_map/ppermute | solution.py:561
  16.8 0.1 collective-permute-start.8
  16.9 0.4 %collective-permute-start.10 = (f32[216,128]{1,0:T(8,128)S(1)}, f32[216,128]{1,0:T(8,128)S(1)}, u32[]{:S(2)}, u32[]{:S(2)}) collective-permute-start(f32[216,128]{1,0:T(8,128)S(1)} %get-tuple-element.75), channel_id=1, source_target_pairs={{0,1},{1,0},{2,3},{3,2},{4,5},{5,4},{6,7},{7,6},{8,9},{9,8},{10,11... | collective-permute-start | bytes 331784 | tf_op jit(solution)/shard_map/ppermute | solution.py:561
  17.4 0.3 collective-permute-done.4
  17.7 0.5 %collective-permute-start.5 = (bf16[216,128]{1,0:T(8,128)(2,1)S(1)}, bf16[216,128]{1,0:T(8,128)(2,1)S(1)}, u32[]{:S(2)}, u32[]{:S(2)}) collective-permute-start(bf16[216,128]{1,0:T(8,128)(2,1)S(1)} %add_convert_fusion.4), channel_id=1, source_target_pairs={{0,24},{1,25},{2,26},{3,27},{4,28},{5,29},{6,30},{7,31},{8,16},{9,... | collective-permute-start | bytes 165896 | tf_op jit(solution)/shard_map/ppermute | solution.py:557
  18.2 0.0 collective-permute-done.6
  18.2 0.9 %collective-permute-start.7 = (bf16[216,128]{1,0:T(8,128)(2,1)S(1)}, bf16[216,128]{1,0:T(8,128)(2,1)S(1)}, u32[]{:S(2)}, u32[]{:S(2)}) collective-permute-start(bf16[216,128]{1,0:T(8,128)(2,1)S(1)} %add_convert_fusion.3), channel_id=1, source_target_pairs={{0,17},{1,16},{2,19},{3,18},{4,21},{5,20},{6,23},{7,22},{8,25},{9,... | collective-permute-start | bytes 165896 | tf_op jit(solution)/shard_map/ppermute | solution.py:557
  19.2 0.0 collective-permute-done.8
  19.2 1.9 %collective-permute-start.9 = (bf16[216,128]{1,0:T(8,128)(2,1)S(1)}, bf16[216,128]{1,0:T(8,128)(2,1)S(1)}, u32[]{:S(2)}, u32[]{:S(2)}) collective-permute-start(bf16[216,128]{1,0:T(8,128)(2,1)S(1)} %add_convert_fusion.2), channel_id=1, source_target_pairs={{0,9},{1,8},{2,11},{3,10},{4,13},{5,12},{6,15},{7,14},{8,1},{9,0},... | collective-permute-start | bytes 165896 | tf_op jit(solution)/shard_map/ppermute | solution.py:557
  21.1 2.2 %shard_map.81 = bf16[16,64,128]{2,1,0:T(8,128)(2,1)} custom-call(bf16[19,64,512]{2,1,0:T(8,128)(2,1)S(1)} %get-tuple-element.70.part, bf16[4,32,128]{2,1,0:T(8,128)(2,1)S(1)} %get-tuple-element.71.ends, bf16[384,512]{1,0:T(8,128)(2,1)S(1)} %get-tuple-element.72.taps), custom_call_target="tpu_custom_call" | custom-call | flops 301989888 | bytes 3145728 | tf_op jit(solution)/shard_map/pallas_call | solution.py:564
  23.3 0.0 collective-permute-done.5
  23.3 0.2 collective-permute-done.7
  23.5 0.0 collective-permute-done.9
  23.5 0.0 collective-permute-done.10
  23.6 1.6 %collective-permute-start.13 = (bf16[216,128]{1,0:T(8,128)(2,1)S(1)}, bf16[216,128]{1,0:T(8,128)(2,1)S(1)}, u32[]{:S(2)}, u32[]{:S(2)}) collective-permute-start(bf16[216,128]{1,0:T(8,128)(2,1)S(1)} %add_convert_fusion.1), channel_id=1, source_target_pairs={{0,6},{1,7},{2,4},{3,5},{4,2},{5,3},{6,0},{7,1},{8,14},{9,15},{10,... | collective-permute-start | bytes 165896 | tf_op jit(solution)/shard_map/ppermute | solution.py:557
  25.2 0.0 collective-permute-start.12
  25.2 2.5 %collective-permute-start.11 = (bf16[216,128]{1,0:T(8,128)(2,1)S(1)}, bf16[216,128]{1,0:T(8,128)(2,1)S(1)}, u32[]{:S(2)}, u32[]{:S(2)}) collective-permute-start(bf16[216,128]{1,0:T(8,128)(2,1)S(1)} %add_convert_fusion.1), channel_id=1, source_target_pairs={{0,3},{1,2},{2,1},{3,0},{4,7},{5,6},{6,5},{7,4},{8,11},{9,10},{10,... | collective-permute-start | bytes 165896 | tf_op jit(solution)/shard_map/ppermute | solution.py:557
  27.7 2.3 %collective-permute-done.13 = bf16[216,128]{1,0:T(8,128)(2,1)S(1)} collective-permute-done((bf16[216,128]{1,0:T(8,128)(2,1)S(1)}, bf16[216,128]{1,0:T(8,128)(2,1)S(1)}, u32[]{:S(2)}, u32[]{:S(2)}) %collective-permute-start.13) | collective-permute-done | bytes 55328 | tf_op jit(solution)/shard_map/ppermute | solution.py:557
  30.0 1.7 %collective-permute-done.12 = bf16[216,128]{1,0:T(8,128)(2,1)S(1)} collective-permute-done((bf16[216,128]{1,0:T(8,128)(2,1)S(1)}, bf16[216,128]{1,0:T(8,128)(2,1)S(1)}, u32[]{:S(2)}, u32[]{:S(2)}) %collective-permute-start.12) | collective-permute-done | bytes 55328 | tf_op jit(solution)/shard_map/ppermute | solution.py:557
  31.7 0.2 collective-permute-done.11
  32.0 1.4 %collective-permute-start.16 = (bf16[216,128]{1,0:T(8,128)(2,1)S(1)}, bf16[216,128]{1,0:T(8,128)(2,1)S(1)}, u32[]{:S(2)}, u32[]{:S(2)}) collective-permute-start(bf16[216,128]{1,0:T(8,128)(2,1)S(1)} %add_convert_fusion), channel_id=1, source_target_pairs={{0,24},{1,25},{2,26},{3,27},{4,28},{5,29},{6,30},{7,31},{8,16},{9,... | collective-permute-start | bytes 165896 | tf_op jit(solution)/shard_map/ppermute | solution.py:557
  33.4 0.7 %collective-permute-start.15 = (bf16[216,128]{1,0:T(8,128)(2,1)S(1)}, bf16[216,128]{1,0:T(8,128)(2,1)S(1)}, u32[]{:S(2)}, u32[]{:S(2)}) collective-permute-start(bf16[216,128]{1,0:T(8,128)(2,1)S(1)} %add_convert_fusion), channel_id=1, source_target_pairs={{0,17},{1,16},{2,19},{3,18},{4,21},{5,20},{6,23},{7,22},{8,25},{9,... | collective-permute-start | bytes 165896 | tf_op jit(solution)/shard_map/ppermute | solution.py:557
  34.1 1.1 %collective-permute-start.14 = (bf16[216,128]{1,0:T(8,128)(2,1)S(1)}, bf16[216,128]{1,0:T(8,128)(2,1)S(1)}, u32[]{:S(2)}, u32[]{:S(2)}) collective-permute-start(bf16[216,128]{1,0:T(8,128)(2,1)S(1)} %add_convert_fusion), channel_id=1, source_target_pairs={{0,9},{1,8},{2,11},{3,10},{4,13},{5,12},{6,15},{7,14},{8,1},{9,0},... | collective-permute-start | bytes 165896 | tf_op jit(solution)/shard_map/ppermute | solution.py:557
  35.2 2.0 %collective-permute-done.16 = bf16[216,128]{1,0:T(8,128)(2,1)S(1)} collective-permute-done((bf16[216,128]{1,0:T(8,128)(2,1)S(1)}, bf16[216,128]{1,0:T(8,128)(2,1)S(1)}, u32[]{:S(2)}, u32[]{:S(2)}) %collective-permute-start.16) | collective-permute-done | bytes 55328 | tf_op jit(solution)/shard_map/ppermute | solution.py:557
  37.2 1.0 %collective-permute-done.15 = bf16[216,128]{1,0:T(8,128)(2,1)S(1)} collective-permute-done((bf16[216,128]{1,0:T(8,128)(2,1)S(1)}, bf16[216,128]{1,0:T(8,128)(2,1)S(1)}, u32[]{:S(2)}, u32[]{:S(2)}) %collective-permute-start.15) | collective-permute-done | bytes 55328 | tf_op jit(solution)/shard_map/ppermute | solution.py:557
  38.2 0.0 collective-permute-done.14
  38.2 0.3 collective-permute-start.17
  38.5 1.2 %collective-permute-done.17.theirs = bf16[4,216,128]{2,1,0:T(8,128)(2,1)S(1)} collective-permute-done((bf16[4,216,128]{2,1,0:T(8,128)(2,1)S(1)}, bf16[4,216,128]{2,1,0:T(8,128)(2,1)S(1)}, u32[]{:S(2)}, u32[]{:S(2)}) %collective-permute-start.17) | collective-permute-done | bytes 221216 | tf_op jit(solution)/shard_map/ppermute | solution.py:589
  39.7 1.0 %shard_map.82 = (f32[576,128]{1,0:T(8,128)}, f32[1152,128]{1,0:T(8,128)}) custom-call(bf16[4,216,128]{2,1,0:T(8,128)(2,1)S(1)} %pad_maximum_fusion.mine, bf16[4,216,128]{2,1,0:T(8,128)(2,1)S(1)} %collective-permute-done.17.theirs), custom_call_target="tpu_custom_call" | custom-call | flops 1000 | bytes 1572864 | tf_op jit(solution)/shard_map/pallas_call | solution.py:591
  (12 shorter events, 0.2 us)
Async XLA Ops:
  0.6 11.3 %copy-start.3 = (bf16[8,64,128]{2,1,0:T(8,128)(2,1)S(1)}, bf16[8,64,128]{2,1,0:T(8,128)(2,1)}, u32[]{:S(2)}) copy-start(bf16[8,64,128]{2,1,0:T(8,128)(2,1)} %grad_out.1) | copy-start | bytes 393220
  0.6 6.7 %copy-start = (bf16[3,3,128,128]{3,2,1,0:T(8,128)(2,1)S(1)}, bf16[3,3,128,128]{3,2,1,0:T(8,128)(2,1)}, u32[]{:S(2)}) copy-start(bf16[3,3,128,128]{3,2,1,0:T(8,128)(2,1)} %w_second.1) | copy-start | bytes 884740
  0.7 6.7 %copy-start.2 = (bf16[3,3,64,128]{3,2,1,0:T(8,128)(2,1)S(1)}, bf16[3,3,64,128]{3,2,1,0:T(8,128)(2,1)}, u32[]{:S(2)}) copy-start(bf16[3,3,64,128]{3,2,1,0:T(8,128)(2,1)} %w_first.1) | copy-start | bytes 442372
  0.7 6.7 %copy-start.1 = (bf16[16,128,64]{1,2,0:T(8,128)(2,1)S(1)}, bf16[16,128,64]{1,2,0:T(8,128)(2,1)}, u32[]{:S(2)}) copy-start(bf16[16,128,64]{1,2,0:T(8,128)(2,1)} %param.5) | copy-start | bytes 786436
  1.9 6.7 %collective-permute-start = (bf16[192,128]{1,0:T(8,128)(2,1)S(1)}, bf16[192,128]{1,0:T(8,128)(2,1)S(1)}, u32[]{:S(2)}, u32[]{:S(2)}) collective-permute-start(bf16[192,128]{1,0:T(8,128)(2,1)S(1)} %get-tuple-element.43), channel_id=1, source_target_pairs={{0,4},{1,5},{2,6},{3,7},{4,0},{5,1},{6,2},{7,3},{24,25},{25,24},{2... | collective-permute-start | bytes 147464 | tf_op jit(solution)/shard_map/ppermute | solution.py:458
  6.0 4.1 %collective-permute-start.1 = (bf16[192,128]{1,0:T(8,128)(2,1)S(1)}, bf16[192,128]{1,0:T(8,128)(2,1)S(1)}, u32[]{:S(2)}, u32[]{:S(2)}) collective-permute-start(bf16[192,128]{1,0:T(8,128)(2,1)S(1)} %get-tuple-element.44), channel_id=1, source_target_pairs={{0,8},{1,9},{2,10},{3,11},{4,12},{5,13},{6,14},{7,15},{8,0},{9,1},... | collective-permute-start | bytes 147464 | tf_op jit(solution)/shard_map/ppermute | solution.py:459
  10.2 4.9 %collective-permute-start.3 = (bf16[32,128]{1,0:T(8,128)(2,1)S(1)}, bf16[32,128]{1,0:T(8,128)(2,1)S(1)}, u32[]{:S(2)}, u32[]{:S(2)}) collective-permute-start(bf16[32,128]{1,0:T(8,128)(2,1)S(1)} %get-tuple-element.93), channel_id=1, source_target_pairs={{0,7},{1,2},{2,1},{3,4},{4,3},{5,6},{6,5},{7,0},{8,15},{9,10},{10,... | collective-permute-start | bytes 24584 | tf_op jit(solution)/shard_map/ppermute | solution.py:504
  11.0 4.1 %collective-permute-start.2 = (bf16[32,128]{1,0:T(8,128)(2,1)S(1)}, bf16[32,128]{1,0:T(8,128)(2,1)S(1)}, u32[]{:S(2)}, u32[]{:S(2)}) collective-permute-start(bf16[32,128]{1,0:T(8,128)(2,1)S(1)} %get-tuple-element.94), channel_id=1, source_target_pairs={{0,1},{1,0},{2,3},{3,2},{4,5},{5,4},{6,7},{7,6},{8,9},{9,8},{10,11... | collective-permute-start | bytes 24584 | tf_op jit(solution)/shard_map/ppermute | solution.py:505
  16.3 1.4 %collective-permute-start.4 = (f32[216,128]{1,0:T(8,128)S(1)}, f32[216,128]{1,0:T(8,128)S(1)}, u32[]{:S(2)}, u32[]{:S(2)}) collective-permute-start(f32[216,128]{1,0:T(8,128)S(1)} %get-tuple-element.65), channel_id=1, source_target_pairs={{0,1},{1,0},{2,3},{3,2},{4,5},{5,4},{6,7},{7,6},{8,9},{9,8},{10,11... | collective-permute-start | bytes 331784 | tf_op jit(solution)/shard_map/ppermute | solution.py:561
  16.4 1.9 %collective-permute-start.6 = (f32[216,128]{1,0:T(8,128)S(1)}, f32[216,128]{1,0:T(8,128)S(1)}, u32[]{:S(2)}, u32[]{:S(2)}) collective-permute-start(f32[216,128]{1,0:T(8,128)S(1)} %get-tuple-element.67), channel_id=1, source_target_pairs={{0,1},{1,0},{2,3},{3,2},{4,5},{5,4},{6,7},{7,6},{8,9},{9,8},{10,11... | collective-permute-start | bytes 331784 | tf_op jit(solution)/shard_map/ppermute | solution.py:561
  16.8 2.3 %collective-permute-start.8 = (f32[216,128]{1,0:T(8,128)S(1)}, f32[216,128]{1,0:T(8,128)S(1)}, u32[]{:S(2)}, u32[]{:S(2)}) collective-permute-start(f32[216,128]{1,0:T(8,128)S(1)} %get-tuple-element.69), channel_id=1, source_target_pairs={{0,1},{1,0},{2,3},{3,2},{4,5},{5,4},{6,7},{7,6},{8,9},{9,8},{10,11... | collective-permute-start | bytes 331784 | tf_op jit(solution)/shard_map/ppermute | solution.py:561
  16.9 6.6 %collective-permute-start.10 = (f32[216,128]{1,0:T(8,128)S(1)}, f32[216,128]{1,0:T(8,128)S(1)}, u32[]{:S(2)}, u32[]{:S(2)}) collective-permute-start(f32[216,128]{1,0:T(8,128)S(1)} %get-tuple-element.75), channel_id=1, source_target_pairs={{0,1},{1,0},{2,3},{3,2},{4,5},{5,4},{6,7},{7,6},{8,9},{9,8},{10,11... | collective-permute-start | bytes 331784 | tf_op jit(solution)/shard_map/ppermute | solution.py:561
  17.7 5.6 %collective-permute-start.5 = (bf16[216,128]{1,0:T(8,128)(2,1)S(1)}, bf16[216,128]{1,0:T(8,128)(2,1)S(1)}, u32[]{:S(2)}, u32[]{:S(2)}) collective-permute-start(bf16[216,128]{1,0:T(8,128)(2,1)S(1)} %add_convert_fusion.4), channel_id=1, source_target_pairs={{0,24},{1,25},{2,26},{3,27},{4,28},{5,29},{6,30},{7,31},{8,16},{9,... | collective-permute-start | bytes 165896 | tf_op jit(solution)/shard_map/ppermute | solution.py:557
  18.2 5.3 %collective-permute-start.7 = (bf16[216,128]{1,0:T(8,128)(2,1)S(1)}, bf16[216,128]{1,0:T(8,128)(2,1)S(1)}, u32[]{:S(2)}, u32[]{:S(2)}) collective-permute-start(bf16[216,128]{1,0:T(8,128)(2,1)S(1)} %add_convert_fusion.3), channel_id=1, source_target_pairs={{0,17},{1,16},{2,19},{3,18},{4,21},{5,20},{6,23},{7,22},{8,25},{9,... | collective-permute-start | bytes 165896 | tf_op jit(solution)/shard_map/ppermute | solution.py:557
  19.2 4.3 %collective-permute-start.9 = (bf16[216,128]{1,0:T(8,128)(2,1)S(1)}, bf16[216,128]{1,0:T(8,128)(2,1)S(1)}, u32[]{:S(2)}, u32[]{:S(2)}) collective-permute-start(bf16[216,128]{1,0:T(8,128)(2,1)S(1)} %add_convert_fusion.2), channel_id=1, source_target_pairs={{0,9},{1,8},{2,11},{3,10},{4,13},{5,12},{6,15},{7,14},{8,1},{9,0},... | collective-permute-start | bytes 165896 | tf_op jit(solution)/shard_map/ppermute | solution.py:557
  23.6 6.5 %collective-permute-start.13 = (bf16[216,128]{1,0:T(8,128)(2,1)S(1)}, bf16[216,128]{1,0:T(8,128)(2,1)S(1)}, u32[]{:S(2)}, u32[]{:S(2)}) collective-permute-start(bf16[216,128]{1,0:T(8,128)(2,1)S(1)} %add_convert_fusion.1), channel_id=1, source_target_pairs={{0,6},{1,7},{2,4},{3,5},{4,2},{5,3},{6,0},{7,1},{8,14},{9,15},{10,... | collective-permute-start | bytes 165896 | tf_op jit(solution)/shard_map/ppermute | solution.py:557
  25.2 6.5 %collective-permute-start.12 = (bf16[216,128]{1,0:T(8,128)(2,1)S(1)}, bf16[216,128]{1,0:T(8,128)(2,1)S(1)}, u32[]{:S(2)}, u32[]{:S(2)}) collective-permute-start(bf16[216,128]{1,0:T(8,128)(2,1)S(1)} %add_convert_fusion.1), channel_id=1, source_target_pairs={{0,5},{1,4},{2,7},{3,6},{4,1},{5,0},{6,3},{7,2},{8,13},{9,12},{10,... | collective-permute-start | bytes 165896 | tf_op jit(solution)/shard_map/ppermute | solution.py:557
  25.2 6.7 %collective-permute-start.11 = (bf16[216,128]{1,0:T(8,128)(2,1)S(1)}, bf16[216,128]{1,0:T(8,128)(2,1)S(1)}, u32[]{:S(2)}, u32[]{:S(2)}) collective-permute-start(bf16[216,128]{1,0:T(8,128)(2,1)S(1)} %add_convert_fusion.1), channel_id=1, source_target_pairs={{0,3},{1,2},{2,1},{3,0},{4,7},{5,6},{6,5},{7,4},{8,11},{9,10},{10,... | collective-permute-start | bytes 165896 | tf_op jit(solution)/shard_map/ppermute | solution.py:557
  32.0 5.2 %collective-permute-start.16 = (bf16[216,128]{1,0:T(8,128)(2,1)S(1)}, bf16[216,128]{1,0:T(8,128)(2,1)S(1)}, u32[]{:S(2)}, u32[]{:S(2)}) collective-permute-start(bf16[216,128]{1,0:T(8,128)(2,1)S(1)} %add_convert_fusion), channel_id=1, source_target_pairs={{0,24},{1,25},{2,26},{3,27},{4,28},{5,29},{6,30},{7,31},{8,16},{9,... | collective-permute-start | bytes 165896 | tf_op jit(solution)/shard_map/ppermute | solution.py:557
  33.4 4.7 %collective-permute-start.15 = (bf16[216,128]{1,0:T(8,128)(2,1)S(1)}, bf16[216,128]{1,0:T(8,128)(2,1)S(1)}, u32[]{:S(2)}, u32[]{:S(2)}) collective-permute-start(bf16[216,128]{1,0:T(8,128)(2,1)S(1)} %add_convert_fusion), channel_id=1, source_target_pairs={{0,17},{1,16},{2,19},{3,18},{4,21},{5,20},{6,23},{7,22},{8,25},{9,... | collective-permute-start | bytes 165896 | tf_op jit(solution)/shard_map/ppermute | solution.py:557
  34.1 4.0 %collective-permute-start.14 = (bf16[216,128]{1,0:T(8,128)(2,1)S(1)}, bf16[216,128]{1,0:T(8,128)(2,1)S(1)}, u32[]{:S(2)}, u32[]{:S(2)}) collective-permute-start(bf16[216,128]{1,0:T(8,128)(2,1)S(1)} %add_convert_fusion), channel_id=1, source_target_pairs={{0,9},{1,8},{2,11},{3,10},{4,13},{5,12},{6,15},{7,14},{8,1},{9,0},... | collective-permute-start | bytes 165896 | tf_op jit(solution)/shard_map/ppermute | solution.py:557
  38.2 1.5 %collective-permute-start.17 = (bf16[4,216,128]{2,1,0:T(8,128)(2,1)S(1)}, bf16[4,216,128]{2,1,0:T(8,128)(2,1)S(1)}, u32[]{:S(2)}, u32[]{:S(2)}) collective-permute-start(bf16[4,216,128]{2,1,0:T(8,128)(2,1)S(1)} %pad_maximum_fusion.mine), channel_id=1, source_target_pairs={{0,1},{1,0},{2,3},{3,2},{4,5},{5,4},{6,7},{7,6},{8,9},{9,8},{10,11... | collective-permute-start | bytes 663560 | tf_op jit(solution)/shard_map/ppermute | solution.py:589
